TPU v7x, 32 devices: a whole 2x2x4 slice. The times are simulated.
32 devices in a mesh: ctx: 8 (over z, y), head: 4 (over x, core).
Axes of the slice: x: 2, y: 2, z: 4, core: 2. Of those that a mesh axis runs over, the one named last changes fastest.
Arguments:
- queries: bfloat16 [2048, 2048], P('ctx', 'head'), may hold values from -6 to 6
- keys: bfloat16 [2048, 2048], P('ctx', 'head'), may hold values from -6 to 6
- values: bfloat16 [2048, 2048], P('ctx', 'head'), may hold values from -6 to 6
- directions: bfloat16 [2048, 2048], P('ctx', 'head'), may hold values from -6 to 6
- rates: float32 [16, 2048], P('head', 'ctx'), may hold values from 0.004 to 1.996
- selected: int32 [16, 4], P('ctx'), may hold values from 0 to 15, as said below
- out_weight: bfloat16 [2048, 2048], P('head'), may hold values from -0.1875 to 0.1875
Outputs:
- projected: bfloat16 [2048, 2048], P('ctx', 'head')
Inputs may be any that keep to these rules, and one draw needn't show every extreme that they name: `selected`: row c lists query block c's key blocks: entry 0 is c itself; the others lie from max(c - 14, 0) to c - 1 (or are 0 when c is 0), may repeat, and the farthest distance 7 * 2 is reached in every draw.
All inputs are finite; a program needn't handle non-finite values.
Results may differ from a plain program's by a relative error of at most 0.022.
Values may be sent and summed in bfloat16 or wider, within the bound.
No kernel may reach another device: no remote copies, remote signals or barrier semaphores. Data moves between devices by JAX's collectives and lax.ppermute only.
A program may use at most 64 MiB of HBM per device.

v0:
```python
import jax
import jax.numpy as jnp
from jax import lax
from jax.sharding import PartitionSpec as P

HEAD_DIM = 128
BLOCK = 128
LOOK = 7


def shifted(value, axis, by):
    count = lax.axis_size(axis)
    pairs = [(i, i + by) for i in range(count) if 0 <= i + by < count]
    return lax.ppermute(value, axis, pairs)


def product(left, right):
    return jnp.matmul(left, right, precision=lax.Precision.HIGHEST)


def flip_last(array):
    return jnp.swapaxes(array, -1, -2)


def block_terms(query_part, key_part, direction_part, rate_part):
    block_width = query_part.shape[-2]
    head_width = query_part.shape[-1]
    unit_vectors = direction_part * lax.rsqrt(
        jnp.sum(direction_part * direction_part, -1, keepdims=True) + 1e-06
    )
    positions = jnp.arange(block_width)
    strict_below = (positions[:, None] > positions[None, :]).astype(jnp.float32)
    at_or_below = (positions[:, None] >= positions[None, :]).astype(jnp.float32)
    identity = jnp.eye(block_width, dtype=jnp.float32)
    head_identity = jnp.eye(head_width, dtype=jnp.float32)
    gram_matrix = product(unit_vectors, flip_last(unit_vectors))
    lower_matrix = identity + rate_part[..., :, None] * gram_matrix * strict_below
    mixing = lax.linalg.triangular_solve(
        lower_matrix, rate_part[..., :, None] * identity, left_side=True, lower=True
    )
    query_proj = product(query_part, flip_last(unit_vectors)) * at_or_below
    key_proj = product(unit_vectors, flip_last(key_part)) * strict_below
    query_mix = product(query_proj, mixing)
    q_start = query_part - product(query_mix, unit_vectors)
    k_end = key_part - product(flip_last(product(mixing, key_proj)), unit_vectors)
    inner_scores = product(query_part, flip_last(key_part)) - product(query_mix, key_proj)
    block_maps = head_identity - product(product(flip_last(unit_vectors), mixing), unit_vectors)
    return (q_start, k_end, inner_scores, block_maps)


def body(queries, keys, values, directions, rates, selected, out_weight):
    local_tokens = queries.shape[0]
    heads_here = queries.shape[1] // HEAD_DIM
    blocks_here = local_tokens // BLOCK
    score_scale = HEAD_DIM ** (-0.5)

    def blocked(array):
        return array.reshape(blocks_here, BLOCK, heads_here, HEAD_DIM).transpose(0, 2, 1, 3)

    value_blocks = blocked(values)
    rate_blocks = rates.reshape(heads_here, blocks_here, BLOCK).transpose(1, 0, 2)
    q_start, k_end, inner_scores, block_maps = block_terms(
        blocked(queries).astype(jnp.float32),
        blocked(keys).astype(jnp.float32),
        blocked(directions).astype(jnp.float32),
        rate_blocks,
    )
    device = lax.axis_index("ctx")
    first_block = device * blocks_here
    positions = jnp.arange(BLOCK)
    causal = (positions[:, None] >= positions[None, :])[None]
    device_map = jnp.broadcast_to(
        jnp.eye(HEAD_DIM, dtype=jnp.float32), (heads_here, HEAD_DIM, HEAD_DIM)
    )
    tail_list = [None] * blocks_here
    for block_index in reversed(range(blocks_here)):
        tail_list[block_index] = product(k_end[block_index], flip_last(device_map))
        device_map = product(device_map, block_maps[block_index])
    key_tail = jnp.stack(tail_list)
    pieces = []
    front_list = []
    for query_block in range(blocks_here):
        listed = selected[query_block]
        entries = [
            (
                inner_scores[query_block] * score_scale,
                causal & jnp.any(listed == first_block + query_block),
                value_blocks[query_block],
            )
        ]
        moving = q_start[query_block]
        for earlier in reversed(range(query_block)):
            hit = jnp.any(listed == first_block + earlier)
            entries.append(
                (
                    product(moving, flip_last(k_end[earlier])) * score_scale,
                    jnp.broadcast_to(hit, (1, BLOCK, BLOCK)),
                    value_blocks[earlier],
                )
            )
            moving = product(moving, block_maps[earlier])
        pieces.append(entries)
        front_list.append(moving)
    query_front = jnp.stack(front_list)

    def score_rows(front, arrived_keys):
        front_rows = front.transpose(1, 0, 2, 3).reshape(heads_here, blocks_here * BLOCK, HEAD_DIM)
        key_rows = arrived_keys.transpose(1, 0, 2, 3).reshape(
            heads_here, blocks_here * BLOCK, HEAD_DIM
        )
        raw = product(front_rows, flip_last(key_rows)) * score_scale
        return raw.reshape(heads_here, blocks_here, BLOCK, blocks_here * BLOCK).transpose(
            1, 0, 2, 3
        )

    def collect(offset, front, arrived_keys, arrived_values):
        source_ids = (device - offset) * blocks_here + jnp.arange(blocks_here)
        hit = jnp.any(selected[:, :, None] == source_ids[None, None, :], axis=1)
        remote_scores = score_rows(front, arrived_keys)
        value_rows = arrived_values.transpose(1, 0, 2, 3).reshape(
            heads_here, blocks_here * BLOCK, HEAD_DIM
        )
        for query_block in range(blocks_here):
            allowed = jnp.repeat(hit[query_block], BLOCK)[None, None, :]
            pieces[query_block].append((remote_scores[query_block], allowed, value_rows))

    carried_keys = key_tail
    carried_values = value_blocks
    for offset in range(1, LOOK + 1):
        arrived_keys = shifted(carried_keys.astype(jnp.bfloat16), "ctx", 1).astype(
            carried_keys.dtype
        )
        arrived_values = shifted(carried_values, "ctx", 1)
        collect(offset, query_front, arrived_keys, arrived_values)
        if offset < LOOK:
            carried_keys = product(arrived_keys, flip_last(device_map)[None])
            carried_values = arrived_values
    outputs = []
    for query_block in range(blocks_here):
        entries = pieces[query_block]
        highest = None
        for scores, allowed, value_rows in entries:
            local_max = jnp.max(jnp.where(allowed, scores, -1e30), -1, keepdims=True)
            highest = local_max if highest is None else jnp.maximum(highest, local_max)
        expo_list = [
            jnp.exp(jnp.where(allowed, scores - highest, -1e30))
            for scores, allowed, value_rows in entries
        ]
        denominator = expo_list[0].sum(-1, keepdims=True)
        for expos in expo_list[1:]:
            denominator = denominator + expos.sum(-1, keepdims=True)
        blended = jnp.zeros((heads_here, BLOCK, HEAD_DIM), jnp.float32)
        for expos, entry in zip(expo_list, entries):
            weights = (expos / denominator).astype(jnp.bfloat16)
            blended = blended + jnp.einsum(
                "hqk,hke->hqe", weights, entry[2], preferred_element_type=jnp.float32
            )
        outputs.append(blended.astype(jnp.bfloat16))
    attended = jnp.stack(outputs)
    attended_flat = attended.transpose(0, 2, 1, 3).reshape(local_tokens, heads_here * HEAD_DIM)
    partial_value = jnp.dot(attended_flat, out_weight, preferred_element_type=jnp.float32).astype(
        jnp.bfloat16
    )
    summed = lax.psum_scatter(partial_value, "head", scatter_dimension=1, tiled=True).astype(
        jnp.float32
    )
    return summed.astype(jnp.bfloat16)


def solution(mesh):
    in_specs = (
        P("ctx", "head"),
        P("ctx", "head"),
        P("ctx", "head"),
        P("ctx", "head"),
        P("head", "ctx"),
        P("ctx", None),
        P("head", None),
    )
    out_specs = P("ctx", "head")
    return jax.shard_map(body, mesh=mesh, in_specs=in_specs, out_specs=out_specs, check_vma=False)
```

profile of v0, /device:TPU:0, one launch (start us, length us, event | category | flops | bytes accessed | tf_op | source)
XLA Modules:
  0.0 245.5 jit_solution(2674472143775322996)
XLA Ops:
  9.6 2.1 fusion.3
  11.6 79.2 %custom-call.3 = f32[2,4,1,128,128]{3,4,2,1,0:T(8,128)} custom-call(f32[2,4,1,128,128]{4,3,2,1,0:T(8,128)S(1)} %fusion.3), custom_call_target="InvertDiagBlocksLowerTriangular" | custom-call | tf_op jit(solution)/shard_map/triangular_solve | solution.py:38
  90.9 2.2 fusion.17
  100.0 5.6 %collective-permute-start = (bf16[2,4,128,128]{3,2,1,0:T(8,128)(2,1)}, bf16[2,4,128,128]{3,2,1,0:T(8,128)(2,1)}, u32[]{:S(2)}, u32[]{:S(2)}) collective-permute-start(bf16[2,4,128,128]{3,2,1,0:T(8,128)(2,1)} %pad_maximum_fusion), channel_id=1, source_target_pairs={{0,4},{4,8},{8,12},{12,16},{16,20},{20,24},{24,28},{1,5},{5,9},{9,... | collective-permute-start | bytes 786440 | tf_op jit(solution)/shard_map/ppermute | solution.py:14
  105.5 1.7 reshape.360
  107.2 1.7 copy.147
  109.0 3.4 %collective-permute-start.7 = (bf16[2,4,128,128]{3,2,1,0:T(8,128)(2,1)}, bf16[2,4,128,128]{3,2,1,0:T(8,128)(2,1)}, u32[]{:S(2)}, u32[]{:S(2)}) collective-permute-start(bf16[2,4,128,128]{3,2,1,0:T(8,128)(2,1)} %bitcast.449), channel_id=1, source_target_pairs={{0,4},{4,8},{8,12},{12,16},{16,20},{20,24},{24,28},{1,5},{5,9},{9,... | collective-permute-start | bytes 786440 | tf_op jit(solution)/shard_map/ppermute | solution.py:14
  112.4 1.7 reshape.342
  114.1 2.1 fusion.41
  130.4 2.9 %collective-permute-start.1 = (bf16[2,4,128,128]{3,2,0,1:T(8,128)(2,1)S(1)}, bf16[2,4,128,128]{3,2,0,1:T(8,128)(2,1)S(1)}, u32[]{:S(2)}, u32[]{:S(2)}) collective-permute-start(bf16[2,4,128,128]{3,2,0,1:T(8,128)(2,1)S(1)} %fusion.5), channel_id=1, source_target_pairs={{0,4},{4,8},{8,12},{12,16},{16,20},{20,24},{24,28},{1,5},{5,9},{9,... | collective-permute-start | bytes 786440 | tf_op jit(solution)/shard_map/ppermute | solution.py:14
  136.0 3.4 %collective-permute-start.8 = (bf16[2,4,128,128]{3,2,1,0:T(8,128)(2,1)}, bf16[2,4,128,128]{3,2,1,0:T(8,128)(2,1)S(1)}, u32[]{:S(2)}, u32[]{:S(2)}) collective-permute-start(bf16[2,4,128,128]{3,2,1,0:T(8,128)(2,1)} %collective-permute-done.7), channel_id=1, source_target_pairs={{0,4},{4,8},{8,12},{12,16},{16,20},{20,24},{24,28},{1,5},{5,9},{9,... | collective-permute-start | bytes 786440 | tf_op jit(solution)/shard_map/ppermute | solution.py:14
  140.1 3.4 %collective-permute-start.2 = (bf16[2,4,128,128]{3,2,0,1:T(8,128)(2,1)S(1)}, bf16[2,4,128,128]{3,2,0,1:T(8,128)(2,1)S(1)}, u32[]{:S(2)}, u32[]{:S(2)}) collective-permute-start(bf16[2,4,128,128]{3,2,0,1:T(8,128)(2,1)S(1)} %fusion.6), channel_id=1, source_target_pairs={{0,4},{4,8},{8,12},{12,16},{16,20},{20,24},{24,28},{1,5},{5,9},{9,... | collective-permute-start | bytes 786440 | tf_op jit(solution)/shard_map/ppermute | solution.py:14
  144.2 2.3 collective-permute-done.8
  146.5 4.3 %collective-permute-start.9 = (bf16[2,4,128,128]{3,2,1,0:T(8,128)(2,1)S(1)}, bf16[2,4,128,128]{3,2,1,0:T(8,128)(2,1)S(1)}, u32[]{:S(2)}, u32[]{:S(2)}) collective-permute-start(bf16[2,4,128,128]{3,2,1,0:T(8,128)(2,1)S(1)} %collective-permute-done.8), channel_id=1, source_target_pairs={{0,4},{4,8},{8,12},{12,16},{16,20},{20,24},{24,28},{1,5},{5,9},{9,... | collective-permute-start | bytes 786440 | tf_op jit(solution)/shard_map/ppermute | solution.py:14
  152.4 4.4 %collective-permute-start.3 = (bf16[2,4,128,128]{3,2,0,1:T(8,128)(2,1)S(1)}, bf16[2,4,128,128]{3,2,0,1:T(8,128)(2,1)S(1)}, u32[]{:S(2)}, u32[]{:S(2)}) collective-permute-start(bf16[2,4,128,128]{3,2,0,1:T(8,128)(2,1)S(1)} %fusion.7), channel_id=1, source_target_pairs={{0,4},{4,8},{8,12},{12,16},{16,20},{20,24},{24,28},{1,5},{5,9},{9,... | collective-permute-start | bytes 786440 | tf_op jit(solution)/shard_map/ppermute | solution.py:14
  157.6 4.4 %collective-permute-start.10 = (bf16[2,4,128,128]{3,2,1,0:T(8,128)(2,1)S(1)}, bf16[2,4,128,128]{3,2,1,0:T(8,128)(2,1)S(1)}, u32[]{:S(2)}, u32[]{:S(2)}) collective-permute-start(bf16[2,4,128,128]{3,2,1,0:T(8,128)(2,1)S(1)} %collective-permute-done.9), channel_id=1, source_target_pairs={{0,4},{4,8},{8,12},{12,16},{16,20},{20,24},{24,28},{1,5},{5,9},{9,... | collective-permute-start | bytes 786440 | tf_op jit(solution)/shard_map/ppermute | solution.py:14
  163.9 4.4 %collective-permute-start.4 = (bf16[2,4,128,128]{3,2,0,1:T(8,128)(2,1)S(1)}, bf16[2,4,128,128]{3,2,0,1:T(8,128)(2,1)S(1)}, u32[]{:S(2)}, u32[]{:S(2)}) collective-permute-start(bf16[2,4,128,128]{3,2,0,1:T(8,128)(2,1)S(1)} %fusion.8), channel_id=1, source_target_pairs={{0,4},{4,8},{8,12},{12,16},{16,20},{20,24},{24,28},{1,5},{5,9},{9,... | collective-permute-start | bytes 786440 | tf_op jit(solution)/shard_map/ppermute | solution.py:14
  169.2 4.8 %collective-permute-start.11 = (bf16[2,4,128,128]{3,2,1,0:T(8,128)(2,1)S(1)}, bf16[2,4,128,128]{3,2,1,0:T(8,128)(2,1)S(1)}, u32[]{:S(2)}, u32[]{:S(2)}) collective-permute-start(bf16[2,4,128,128]{3,2,1,0:T(8,128)(2,1)S(1)} %collective-permute-done.10), channel_id=1, source_target_pairs={{0,4},{4,8},{8,12},{12,16},{16,20},{20,24},{24,28},{1,5},{5,9},{9,... | collective-permute-start | bytes 786440 | tf_op jit(solution)/shard_map/ppermute | solution.py:14
  175.4 4.4 %collective-permute-start.5 = (bf16[2,4,128,128]{3,2,0,1:T(8,128)(2,1)S(1)}, bf16[2,4,128,128]{3,2,0,1:T(8,128)(2,1)S(1)}, u32[]{:S(2)}, u32[]{:S(2)}) collective-permute-start(bf16[2,4,128,128]{3,2,0,1:T(8,128)(2,1)S(1)} %fusion.9), channel_id=1, source_target_pairs={{0,4},{4,8},{8,12},{12,16},{16,20},{20,24},{24,28},{1,5},{5,9},{9,... | collective-permute-start | bytes 786440 | tf_op jit(solution)/shard_map/ppermute | solution.py:14
  180.8 4.6 %collective-permute-start.12 = (bf16[2,4,128,128]{3,2,1,0:T(8,128)(2,1)S(1)}, bf16[2,4,128,128]{3,2,1,0:T(8,128)(2,1)S(1)}, u32[]{:S(2)}, u32[]{:S(2)}) collective-permute-start(bf16[2,4,128,128]{3,2,1,0:T(8,128)(2,1)S(1)} %collective-permute-done.11), channel_id=1, source_target_pairs={{0,4},{4,8},{8,12},{12,16},{16,20},{20,24},{24,28},{1,5},{5,9},{9,... | collective-permute-start | bytes 786440 | tf_op jit(solution)/shard_map/ppermute | solution.py:14
  187.0 4.4 %collective-permute-start.6 = (bf16[2,4,128,128]{3,2,0,1:T(8,128)(2,1)S(1)}, bf16[2,4,128,128]{3,2,0,1:T(8,128)(2,1)S(1)}, u32[]{:S(2)}, u32[]{:S(2)}) collective-permute-start(bf16[2,4,128,128]{3,2,0,1:T(8,128)(2,1)S(1)} %fusion.10), channel_id=1, source_target_pairs={{0,4},{4,8},{8,12},{12,16},{16,20},{20,24},{24,28},{1,5},{5,9},{9,... | collective-permute-start | bytes 786440 | tf_op jit(solution)/shard_map/ppermute | solution.py:14
  192.2 4.6 %collective-permute-start.13 = (bf16[2,4,128,128]{3,2,1,0:T(8,128)(2,1)S(1)}, bf16[2,4,128,128]{3,2,1,0:T(8,128)(2,1)S(1)}, u32[]{:S(2)}, u32[]{:S(2)}) collective-permute-start(bf16[2,4,128,128]{3,2,1,0:T(8,128)(2,1)S(1)} %collective-permute-done.12), channel_id=1, source_target_pairs={{0,4},{4,8},{8,12},{12,16},{16,20},{20,24},{24,28},{1,5},{5,9},{9,... | collective-permute-start | bytes 786440 | tf_op jit(solution)/shard_map/ppermute | solution.py:14
  210.5 1.7 convolution_convert_fusion
  212.2 26.5 %reduce-scatter.2.cloned.1.call-done = bf16[256,512]{1,0:T(8,128)(2,1)} async-done(((bf16[256,2048]{1,0:T(8,128)(2,1)}), bf16[256,512]{1,0:T(8,128)(2,1)}) %reduce-scatter.2.cloned.1.call-update) | async-done | bytes 262160 | tf_op jit(solution)/shard_map/reduce_scatter | solution.py:164
  (163 shorter events, 50.8 us)
Async XLA Ops:
  6.5 203.9 %copy-start = (bf16[512,2048]{1,0:T(8,128)(2,1)S(1)}, bf16[512,2048]{1,0:T(8,128)(2,1)}, u32[]{:S(2)}) copy-start(bf16[512,2048]{1,0:T(8,128)(2,1)} %param.13) | copy-start | bytes 6291460
  6.5 84.4 %copy-start.13 = (f32[4,256]{1,0:T(4,128)S(1)}, f32[4,256]{1,0:T(4,128)}, u32[]{:S(2)}) copy-start(f32[4,256]{1,0:T(4,128)} %param.11) | copy-start | bytes 12292
  6.5 232.2 %reduce-scatter.2.cloned.1.call-start = ((), (), s32[]{:S(2)}) async-start(), calls=%async_computation.1 | async-start | bytes 1310720 | tf_op jit(solution)/shard_map/reduce_scatter | solution.py:164
  93.8 3.3 %copy-start.1 = (f32[2,4,128,128]{3,2,1,0:T(8,128)}, f32[2,4,128,128]{3,2,1,0:T(8,128)S(1)}, u32[]{:S(2)}) copy-start(f32[2,4,128,128]{3,2,1,0:T(8,128)S(1)} %convolution_multiply_fusion.8) | copy-start | bytes 1572868
  96.1 3.1 %copy-start.10 = (f32[4,128,128]{2,1,0:T(8,128)}, f32[4,128,128]{2,1,0:T(8,128)S(1)}, u32[]{:S(2)}) copy-start(f32[4,128,128]{2,1,0:T(8,128)S(1)} %fusion.38) | copy-start | bytes 786436
  100.0 29.1 %collective-permute-start = (bf16[2,4,128,128]{3,2,1,0:T(8,128)(2,1)}, bf16[2,4,128,128]{3,2,1,0:T(8,128)(2,1)}, u32[]{:S(2)}, u32[]{:S(2)}) collective-permute-start(bf16[2,4,128,128]{3,2,1,0:T(8,128)(2,1)} %pad_maximum_fusion), channel_id=1, source_target_pairs={{0,4},{4,8},{8,12},{12,16},{16,20},{20,24},{24,28},{1,5},{5,9},{9,... | collective-permute-start | bytes 786440 | tf_op jit(solution)/shard_map/ppermute | solution.py:14
  109.0 26.1 %collective-permute-start.7 = (bf16[2,4,128,128]{3,2,1,0:T(8,128)(2,1)}, bf16[2,4,128,128]{3,2,1,0:T(8,128)(2,1)}, u32[]{:S(2)}, u32[]{:S(2)}) collective-permute-start(bf16[2,4,128,128]{3,2,1,0:T(8,128)(2,1)} %bitcast.449), channel_id=1, source_target_pairs={{0,4},{4,8},{8,12},{12,16},{16,20},{20,24},{24,28},{1,5},{5,9},{9,... | collective-permute-start | bytes 786440 | tf_op jit(solution)/shard_map/ppermute | solution.py:14
  116.3 3.5 %copy-start.5 = (f32[2,4,128,128]{3,2,1,0:T(8,128)S(1)}, f32[2,4,128,128]{3,2,1,0:T(8,128)}, u32[]{:S(2)}) copy-start(f32[2,4,128,128]{3,2,1,0:T(8,128)} %copy-done.4) | copy-start | bytes 1572868
  118.0 3.7 %copy-start.11 = (f32[4,128,128]{2,1,0:T(8,128)S(1)}, f32[4,128,128]{2,1,0:T(8,128)}, u32[]{:S(2)}) copy-start(f32[4,128,128]{2,1,0:T(8,128)} %copy-done.10) | copy-start | bytes 786436
  119.0 3.0 %copy-start.2 = (f32[2,4,128,128]{3,2,1,0:T(8,128)S(1)}, f32[2,4,128,128]{3,2,1,0:T(8,128)}, u32[]{:S(2)}) copy-start(f32[2,4,128,128]{3,2,1,0:T(8,128)} %copy-done.1) | copy-start | bytes 1572868
  119.8 3.4 %copy-start.14 = (s32[2,4]{1,0:T(2,128)S(1)}, s32[2,4]{1,0:T(2,128)}, u32[]{:S(2)}) copy-start(s32[2,4]{1,0:T(2,128)} %param.12) | copy-start | bytes 100
  122.1 5.8 %copy-start.7 = (f32[2,4,128,128]{3,2,1,0:T(8,128)S(1)}, f32[2,4,128,128]{3,2,1,0:T(8,128)}, u32[]{:S(2)}) copy-start(f32[2,4,128,128]{3,2,1,0:T(8,128)} %copy-done.6) | copy-start | bytes 1572868
  130.4 9.2 %collective-permute-start.1 = (bf16[2,4,128,128]{3,2,0,1:T(8,128)(2,1)S(1)}, bf16[2,4,128,128]{3,2,0,1:T(8,128)(2,1)S(1)}, u32[]{:S(2)}, u32[]{:S(2)}) collective-permute-start(bf16[2,4,128,128]{3,2,0,1:T(8,128)(2,1)S(1)} %fusion.5), channel_id=1, source_target_pairs={{0,4},{4,8},{8,12},{12,16},{16,20},{20,24},{24,28},{1,5},{5,9},{9,... | collective-permute-start | bytes 786440 | tf_op jit(solution)/shard_map/ppermute | solution.py:14
  136.0 10.5 %collective-permute-start.8 = (bf16[2,4,128,128]{3,2,1,0:T(8,128)(2,1)}, bf16[2,4,128,128]{3,2,1,0:T(8,128)(2,1)S(1)}, u32[]{:S(2)}, u32[]{:S(2)}) collective-permute-start(bf16[2,4,128,128]{3,2,1,0:T(8,128)(2,1)} %collective-permute-done.7), channel_id=1, source_target_pairs={{0,4},{4,8},{8,12},{12,16},{16,20},{20,24},{24,28},{1,5},{5,9},{9,... | collective-permute-start | bytes 786440 | tf_op jit(solution)/shard_map/ppermute | solution.py:14
  140.1 11.9 %collective-permute-start.2 = (bf16[2,4,128,128]{3,2,0,1:T(8,128)(2,1)S(1)}, bf16[2,4,128,128]{3,2,0,1:T(8,128)(2,1)S(1)}, u32[]{:S(2)}, u32[]{:S(2)}) collective-permute-start(bf16[2,4,128,128]{3,2,0,1:T(8,128)(2,1)S(1)} %fusion.6), channel_id=1, source_target_pairs={{0,4},{4,8},{8,12},{12,16},{16,20},{20,24},{24,28},{1,5},{5,9},{9,... | collective-permute-start | bytes 786440 | tf_op jit(solution)/shard_map/ppermute | solution.py:14
  146.5 11.1 %collective-permute-start.9 = (bf16[2,4,128,128]{3,2,1,0:T(8,128)(2,1)S(1)}, bf16[2,4,128,128]{3,2,1,0:T(8,128)(2,1)S(1)}, u32[]{:S(2)}, u32[]{:S(2)}) collective-permute-start(bf16[2,4,128,128]{3,2,1,0:T(8,128)(2,1)S(1)} %collective-permute-done.8), channel_id=1, source_target_pairs={{0,4},{4,8},{8,12},{12,16},{16,20},{20,24},{24,28},{1,5},{5,9},{9,... | collective-permute-start | bytes 786440 | tf_op jit(solution)/shard_map/ppermute | solution.py:14
  152.4 11.1 %collective-permute-start.3 = (bf16[2,4,128,128]{3,2,0,1:T(8,128)(2,1)S(1)}, bf16[2,4,128,128]{3,2,0,1:T(8,128)(2,1)S(1)}, u32[]{:S(2)}, u32[]{:S(2)}) collective-permute-start(bf16[2,4,128,128]{3,2,0,1:T(8,128)(2,1)S(1)} %fusion.7), channel_id=1, source_target_pairs={{0,4},{4,8},{8,12},{12,16},{16,20},{20,24},{24,28},{1,5},{5,9},{9,... | collective-permute-start | bytes 786440 | tf_op jit(solution)/shard_map/ppermute | solution.py:14
  157.6 11.5 %collective-permute-start.10 = (bf16[2,4,128,128]{3,2,1,0:T(8,128)(2,1)S(1)}, bf16[2,4,128,128]{3,2,1,0:T(8,128)(2,1)S(1)}, u32[]{:S(2)}, u32[]{:S(2)}) collective-permute-start(bf16[2,4,128,128]{3,2,1,0:T(8,128)(2,1)S(1)} %collective-permute-done.9), channel_id=1, source_target_pairs={{0,4},{4,8},{8,12},{12,16},{16,20},{20,24},{24,28},{1,5},{5,9},{9,... | collective-permute-start | bytes 786440 | tf_op jit(solution)/shard_map/ppermute | solution.py:14
  163.9 11.1 %collective-permute-start.4 = (bf16[2,4,128,128]{3,2,0,1:T(8,128)(2,1)S(1)}, bf16[2,4,128,128]{3,2,0,1:T(8,128)(2,1)S(1)}, u32[]{:S(2)}, u32[]{:S(2)}) collective-permute-start(bf16[2,4,128,128]{3,2,0,1:T(8,128)(2,1)S(1)} %fusion.8), channel_id=1, source_target_pairs={{0,4},{4,8},{8,12},{12,16},{16,20},{20,24},{24,28},{1,5},{5,9},{9,... | collective-permute-start | bytes 786440 | tf_op jit(solution)/shard_map/ppermute | solution.py:14
  169.2 11.6 %collective-permute-start.11 = (bf16[2,4,128,128]{3,2,1,0:T(8,128)(2,1)S(1)}, bf16[2,4,128,128]{3,2,1,0:T(8,128)(2,1)S(1)}, u32[]{:S(2)}, u32[]{:S(2)}) collective-permute-start(bf16[2,4,128,128]{3,2,1,0:T(8,128)(2,1)S(1)} %collective-permute-done.10), channel_id=1, source_target_pairs={{0,4},{4,8},{8,12},{12,16},{16,20},{20,24},{24,28},{1,5},{5,9},{9,... | collective-permute-start | bytes 786440 | tf_op jit(solution)/shard_map/ppermute | solution.py:14
  175.4 11.1 %collective-permute-start.5 = (bf16[2,4,128,128]{3,2,0,1:T(8,128)(2,1)S(1)}, bf16[2,4,128,128]{3,2,0,1:T(8,128)(2,1)S(1)}, u32[]{:S(2)}, u32[]{:S(2)}) collective-permute-start(bf16[2,4,128,128]{3,2,0,1:T(8,128)(2,1)S(1)} %fusion.9), channel_id=1, source_target_pairs={{0,4},{4,8},{8,12},{12,16},{16,20},{20,24},{24,28},{1,5},{5,9},{9,... | collective-permute-start | bytes 786440 | tf_op jit(solution)/shard_map/ppermute | solution.py:14
  180.8 11.4 %collective-permute-start.12 = (bf16[2,4,128,128]{3,2,1,0:T(8,128)(2,1)S(1)}, bf16[2,4,128,128]{3,2,1,0:T(8,128)(2,1)S(1)}, u32[]{:S(2)}, u32[]{:S(2)}) collective-permute-start(bf16[2,4,128,128]{3,2,1,0:T(8,128)(2,1)S(1)} %collective-permute-done.11), channel_id=1, source_target_pairs={{0,4},{4,8},{8,12},{12,16},{16,20},{20,24},{24,28},{1,5},{5,9},{9,... | collective-permute-start | bytes 786440 | tf_op jit(solution)/shard_map/ppermute | solution.py:14
  187.0 10.7 %collective-permute-start.6 = (bf16[2,4,128,128]{3,2,0,1:T(8,128)(2,1)S(1)}, bf16[2,4,128,128]{3,2,0,1:T(8,128)(2,1)S(1)}, u32[]{:S(2)}, u32[]{:S(2)}) collective-permute-start(bf16[2,4,128,128]{3,2,0,1:T(8,128)(2,1)S(1)} %fusion.10), channel_id=1, source_target_pairs={{0,4},{4,8},{8,12},{12,16},{16,20},{20,24},{24,28},{1,5},{5,9},{9,... | collective-permute-start | bytes 786440 | tf_op jit(solution)/shard_map/ppermute | solution.py:14
  192.2 12.0 %collective-permute-start.13 = (bf16[2,4,128,128]{3,2,1,0:T(8,128)(2,1)S(1)}, bf16[2,4,128,128]{3,2,1,0:T(8,128)(2,1)S(1)}, u32[]{:S(2)}, u32[]{:S(2)}) collective-permute-start(bf16[2,4,128,128]{3,2,1,0:T(8,128)(2,1)S(1)} %collective-permute-done.12), channel_id=1, source_target_pairs={{0,4},{4,8},{8,12},{12,16},{16,20},{20,24},{24,28},{1,5},{5,9},{9,... | collective-permute-start | bytes 786440 | tf_op jit(solution)/shard_map/ppermute | solution.py:14
  (6 other events, 13.6 us)
Sparse Core Ops, SparseCore 0:
  212.3 26.3 reduce-scatter.1
where the time goes:
time: 246 us
  other arithmetic  88.5 us (36%)
  starting transfers between devices  59.2 us (24%)
  matrix products  37.2 us (15%)
  waiting for transfers between devices  34 us (14%)
  between operations  14.3 us (6%)
  local copies, waits for them, and re-layouts  12.3 us (5%)
    another operation x1, other arithmetic, block_terms(): lax.linalg.triangular_solve(lower_matrix, rate_part[..., :, None] * ident...  79.2 us
    ppermute x14, starting transfers between devices, shifted(): return lax.ppermute(value, axis, pairs)  59.2 us
    reduce_scatter x1, waiting for transfers between devices, body(): lax.psum_scatter(partial_value, 'head', scatter_dimension=1, tiled=True)  26.5 us
    dot_general x30, matrix products, product(): return jnp.matmul(left, right, precision=lax.Precision.HIGHEST)  24.6 us
    dot_general x17, matrix products, body(): jnp.einsum('hqk,hke->hqe', weights, entry[2], preferred_element_type=jnp....  8.66 us
    ppermute x14, waiting for transfers between devices, shifted(): return lax.ppermute(value, axis, pairs)  7.53 us
    reshape x4, local copies, waits for them, and re-layouts, blocked(): array.reshape(blocks_here, BLOCK, heads_here, HEAD_DIM)  6.17 us
  transfers between devices with their start and end apart: 15, of which 11 were waited for; matrix products, arithmetic and copies ran while one was open for 15% of the time, Pallas kernels for 0%

commit v1 on v0

v1 whole, which is shorter than its diff:
```python
import functools

import jax
import jax.numpy as jnp
from jax import lax
from jax.experimental import pallas as pl
from jax.experimental.pallas import tpu as pltpu
from jax.sharding import PartitionSpec as P

HEAD_DIM = 128
BLOCK = 128
LOOK = 7
BASE = 16
EXTRA = 16
BF16 = jnp.bfloat16
F32 = jnp.float32
VMEM = pl.BlockSpec(memory_space=pltpu.VMEM)
SMEM = pl.BlockSpec(memory_space=pltpu.SMEM)
PARAMS = pltpu.CompilerParams(vmem_limit_bytes=32 * 1024 * 1024)


def dot(left, right, left_dim, right_dim):
    return lax.dot_general(
        left, right, (((left_dim,), (right_dim,)), ((), ())), preferred_element_type=F32
    )


def nn(left, right):
    return dot(left, right, 1, 0)


def nt(left, right):
    return dot(left, right, 1, 1)


def tn(left, right):
    return dot(left, right, 0, 0)


def split(value):
    high = value.astype(BF16)
    return high, (value - high.astype(F32)).astype(BF16)


def triple(product, left, right):
    return product(left[0], right[0]) + (product(left[0], right[1]) + product(left[1], right[0]))


def square_iotas():
    rows = lax.broadcasted_iota(jnp.int32, (BLOCK, BLOCK), 0)
    columns = lax.broadcasted_iota(jnp.int32, (BLOCK, BLOCK), 1)
    return rows, columns


def pack_kernel(head_axis, ctx_axis, q_ref, k_ref, v_ref, d_ref, rates_ref, selected_ref,
                keep_d, send_d, keep_rest, send_rest):
    heads = q_ref.shape[1] // HEAD_DIM
    blocks = q_ref.shape[0] // BLOCK
    core = lax.rem(lax.axis_index(head_axis), 2)
    first_block = lax.axis_index(ctx_axis) * blocks
    row = lax.broadcasted_iota(jnp.int32, (EXTRA, HEAD_DIM), 0)
    lane = lax.broadcasted_iota(jnp.int32, (EXTRA, HEAD_DIM), 1)
    for parity, d_out, rest_out in ((core, keep_d, keep_rest), (1 - core, send_d, send_rest)):
        rows = pl.ds(pl.multiple_of(parity * BLOCK, BLOCK), BLOCK)
        rate = rates_ref[:, rows]
        rate_1 = rate.astype(BF16).astype(F32)
        rate_2 = (rate - rate_1).astype(BF16).astype(F32)
        rate_3 = (rate - rate_1) - rate_2
        away = jnp.zeros((EXTRA, HEAD_DIM), jnp.int32)
        for entry in range(selected_ref.shape[1]):
            distance = first_block + parity - selected_ref[parity, entry]
            away = jnp.where(lane == entry, distance, away)
        away = away.astype(F32)
        for head in range(heads):
            columns = slice(head * HEAD_DIM, (head + 1) * HEAD_DIM)
            d_out[head, :BLOCK] = d_ref[rows, columns]
            extra = jnp.where(row == 0, rate_1[head:head + 1], 0.0)
            extra = jnp.where(row == 1, rate_2[head:head + 1], extra)
            extra = jnp.where(row == 2, rate_3[head:head + 1], extra)
            extra = jnp.where(row == 3, away, extra)
            d_out[head, BLOCK:] = extra.astype(BF16)
            rest_out[head, 0] = k_ref[rows, columns]
            rest_out[head, 1] = q_ref[rows, columns]
            rest_out[head, 2] = v_ref[rows, columns]


def base_inverse(strict):
    count = BLOCK // BASE
    moved = [
        pltpu.roll(strict[b * BASE:(b + 1) * BASE], (BLOCK - b * BASE) % BLOCK, 1)
        if b else strict[:BASE]
        for b in range(count)
    ]
    lanes = lax.broadcasted_iota(jnp.int32, (BASE // 2, BLOCK), 1)
    rows = lax.broadcasted_iota(jnp.int32, (BASE // 2, BLOCK), 0)
    half = BASE // 2
    parts = []
    for b in range(count):
        upper = (lanes == rows + b * BASE).astype(F32)
        lower = (lanes == rows + b * BASE + half).astype(F32)
        for step in range(BASE - 1):
            if step < half:
                source = upper[step:step + 1]
                if step < half - 1:
                    upper = upper - moved[b][:half, step:step + 1] * source
            else:
                source = lower[step - half:step - half + 1]
            lower = lower - moved[b][half:, step:step + 1] * source
        parts += [upper, lower]
    return jnp.concatenate(parts, 0)


def halves(value, size):
    parts = value.reshape(BLOCK // (2 * size), 2, size, BLOCK)
    return parts[:, 0].reshape(BLOCK // 2, BLOCK), parts[:, 1].reshape(BLOCK // 2, BLOCK)


def joined(first, second, size):
    shape = (BLOCK // (2 * size), 1, size, BLOCK)
    return jnp.concatenate([first.reshape(shape), second.reshape(shape)], 1).reshape(BLOCK, BLOCK)


def mixing_kernel(d_ref, mixing_ref):
    units = d_ref.shape[0]
    rows, columns = square_iotas()
    diagonal = rows == columns
    strict, inverse, scales = [], [], []
    for unit in range(units):
        direction = d_ref[unit, :BLOCK]
        extra = d_ref[unit, BLOCK:].astype(F32)
        rate = extra[0:1] + extra[1:2] + extra[2:3]
        gram = nt(direction, direction)
        squares = jnp.sum(jnp.where(diagonal, gram, 0.0), 0, keepdims=True)
        scale = lax.rsqrt(squares + 1e-06)
        scaled_rate = rate * scale
        scale_column = jnp.sum(jnp.where(diagonal, scale, 0.0), 1, keepdims=True)
        rate_column = jnp.sum(jnp.where(diagonal, scaled_rate, 0.0), 1, keepdims=True)
        strict.append(jnp.where(rows > columns, rate_column * gram * scale, 0.0))
        scales.append((scale_column, scaled_rate))
    for unit in range(units):
        inverse.append(base_inverse(strict[unit]))
    size = BASE
    while size < BLOCK:
        row = lax.broadcasted_iota(jnp.int32, (BLOCK // 2, BLOCK), 0)
        column = lax.broadcasted_iota(jnp.int32, (BLOCK // 2, BLOCK), 1)
        inside = (row // size == column // (2 * size)) & (lax.rem(column, 2 * size) < size)
        below = []
        for unit in range(units):
            corner = jnp.where(inside, halves(strict[unit], size)[1], 0.0)
            below.append(triple(nn, split(corner), split(inverse[unit])))
        for unit in range(units):
            first, second = halves(inverse[unit], size)
            padded = joined(jnp.zeros_like(below[unit]), below[unit], size)
            second = second - triple(nn, split(second), split(padded))
            inverse[unit] = joined(first, second, size)
        size *= 2
    for unit in range(units):
        mixing_ref[unit] = scales[unit][0] * inverse[unit] * scales[unit][1]


def terms_kernel(d_ref, mixing_ref, rest_ref, start_ref, inner_ref, share_ref):
    rows, columns = square_iotas()
    identity = (rows == columns).astype(F32)
    for unit in range(d_ref.shape[0]):
        direction = d_ref[unit, :BLOCK]
        key = rest_ref[unit, 0]
        query = rest_ref[unit, 1]
        every = nt(
            jnp.concatenate([direction, query], 0), jnp.concatenate([direction, key], 0)
        )
        key_proj = split(jnp.where(rows > columns, every[:BLOCK, BLOCK:], 0.0))
        query_proj = split(jnp.where(rows >= columns, every[BLOCK:, :BLOCK], 0.0))
        mixing = split(mixing_ref[unit])
        right = jnp.concatenate([direction, key_proj[0]], 1)
        mixed = nn(mixing[0], right) + nn(mixing[1], right)
        mixed = jnp.concatenate(
            [mixed[:, :BLOCK], mixed[:, BLOCK:] + nn(mixing[0], key_proj[1])], 1
        )
        mixed = split(mixed)
        ahead = triple(nn, query_proj, mixed)
        start = split(query.astype(F32) - ahead[:, :HEAD_DIM])
        start_ref[unit, 0] = start[0]
        start_ref[unit, 1] = start[1]
        inner_ref[unit] = every[BLOCK:, BLOCK:] - ahead[:, HEAD_DIM:]
        behind = tn(mixed[0], direction) + tn(mixed[1], direction)
        end = split(key.astype(F32) - behind[BLOCK:])
        block_map = split(identity - behind[:BLOCK])
        share_ref[unit, 0] = end[0]
        share_ref[unit, 1] = end[1]
        share_ref[unit, 2] = block_map[0]
        share_ref[unit, 3] = block_map[1]


def attend_kernel(head_axis, before, away_ref, start_ref, inner_ref, *refs):
    shares = refs[:2 + 2 * (before > 0)]
    values = refs[len(shares):2 * len(shares)]
    out_ref, ends, maps, tails, moving, value_table = refs[2 * len(shares):]
    units = start_ref.shape[0]
    core = lax.rem(lax.axis_index(head_axis), 2)
    pairs = before + units
    for group in range(len(shares) // 2):
        share_own, share_other = shares[2 * group:2 * group + 2]
        value_own, value_other = values[2 * group:2 * group + 2]
        base = 0 if group else before
        for unit in range(units):
            for parity, share, value in (
                (core, share_own, value_own), (1 - core, share_other, value_other)
            ):
                place = 2 * (base + unit) + parity
                ends[place, 0] = share[unit, 0]
                ends[place, 1] = share[unit, 1]
                maps[place, 0] = share[unit, 2]
                maps[place, 1] = share[unit, 3]
                value_table[place] = value[unit]

    pair_maps = []
    for pair in range(pairs):
        odd = (maps[2 * pair + 1, 0], maps[2 * pair + 1, 1])
        left = tuple(
            jnp.concatenate([ends[2 * pair, part], maps[2 * pair, part]], 0) for part in range(2)
        )
        both = split(triple(nn, left, odd))
        for part in range(2):
            tails[2 * pair, part] = both[part][:BLOCK]
            tails[2 * pair + 1, part] = ends[2 * pair + 1, part]
        pair_maps.append((both[0][BLOCK:], both[1][BLOCK:]))

    current = []
    for unit in range(units):
        pair = before + unit
        start = (start_ref[unit, 0], start_ref[unit, 1])
        passed = triple(nt, start, (maps[2 * pair, 0], maps[2 * pair, 1]))
        whole = start[0].astype(F32) + start[1].astype(F32)
        front = split(jnp.where(core == 1, passed, whole))
        current.append(front)
        for part in range(2):
            moving[unit, 0, part] = start[part]
            moving[unit, 1, part] = front[part]
    for step in range(2, LOOK + 1):
        for unit in range(units):
            pair = before + unit - step
            if pair >= 0:
                current[unit] = split(triple(nt, current[unit], pair_maps[pair + 1]))
                for part in range(2):
                    moving[unit, step, part] = current[unit][part]

    rows, columns = square_iotas()
    scale = HEAD_DIM ** (-0.5)
    entries = away_ref.shape[1]
    for unit in range(units):
        block = 2 * (before + unit) + core
        score_list = [jnp.where(rows >= columns, inner_ref[unit] * scale, -1e30)]
        value_list = [value_table[block]]
        for entry in range(1, entries):
            away = away_ref[unit, entry]
            new = away > 0
            for other in range(1, entry):
                new = new & (away_ref[unit, other] != away)
            source = jnp.clip(block - away, 0, 2 * pairs - 1)
            step = jnp.clip(before + unit - source // 2, 0, LOOK)
            same = step == 0
            query = (moving[unit, step, 0], moving[unit, step, 1])
            key = tuple(
                jnp.where(same, ends[source, part], tails[source, part]) for part in range(2)
            )
            score_list.append(jnp.where(new, triple(nt, query, key) * scale, -1e30))
            value_list.append(value_table[source])
        scores = jnp.concatenate(score_list, 1)
        expos = jnp.exp(scores - jnp.max(scores, 1, keepdims=True))
        weights = (expos / jnp.sum(expos, 1, keepdims=True)).astype(BF16)
        out_ref[unit] = nn(weights, jnp.concatenate(value_list, 0)).astype(BF16)


def project_kernel(head_axis, offset, planes, attended_ref, own_ref, other_ref, out_ref):
    index = lax.axis_index(head_axis)
    core = lax.rem(index, 2)
    plane = lax.rem(index // 2 + offset, planes)
    width = out_ref.shape[1]
    columns = pl.ds(pl.multiple_of(plane * width, width), width)
    heads = own_ref.shape[0] // HEAD_DIM

    def group(which):
        return jnp.concatenate([attended_ref[which * heads + head] for head in range(heads)], 1)

    total = nn(group(core), own_ref[:, columns]) + nn(group(1 - core), other_ref[:, columns])
    out_ref[...] = total.astype(out_ref.dtype)


def call(kernel, outs, specs, flops, scratch=()):
    many = isinstance(outs, (list, tuple))
    return pl.pallas_call(
        kernel,
        out_shape=outs,
        in_specs=specs,
        out_specs=[VMEM] * len(outs) if many else VMEM,
        scratch_shapes=list(scratch),
        compiler_params=PARAMS,
        cost_estimate=pl.CostEstimate(flops=flops, bytes_accessed=2 ** 21, transcendentals=0),
    )


def body(ctx_size, head_size, queries, keys, values, directions, rates, selected, out_weight):
    heads = queries.shape[1] // HEAD_DIM
    group = 2 * heads
    planes = head_size // 2
    groups = ctx_size // group
    core = lax.rem(lax.axis_index("head"), 2)
    partners = [(g, g + 1 - 2 * (g % 2)) for g in range(head_size)]
    cubes = 2 * BLOCK ** 3

    def partner(value):
        return lax.ppermute(value, "head", partners)

    def exchange(value):
        members = None
        if groups > 1:
            members = [[a * group + b for b in range(group)] for a in range(groups)]
        return lax.all_to_all(value, "ctx", 0, 0, axis_index_groups=members, tiled=True)

    def ordered(own, other):
        return jnp.where(
            core == 0, jnp.concatenate([own, other], 0), jnp.concatenate([other, own], 0)
        )

    def array(shape, kind=BF16):
        return jax.ShapeDtypeStruct(shape, kind)

    d_shape = array((heads, BLOCK + EXTRA, HEAD_DIM))
    rest_shape = array((heads, 3, BLOCK, HEAD_DIM))
    keep_d, send_d, keep_rest, send_rest = call(
        functools.partial(pack_kernel, "head", "ctx"),
        [d_shape, d_shape, rest_shape, rest_shape],
        [VMEM] * 5 + [SMEM],
        cubes,
    )(queries, keys, values, directions, rates, selected)
    got_d = partner(send_d)
    got_rest = partner(send_rest)
    weight_other = partner(out_weight)
    unit_d = exchange(ordered(keep_d, got_d))
    unit_rest = exchange(ordered(keep_rest, got_rest))
    away = unit_d[:, BLOCK + 3, :selected.shape[1]].astype(jnp.int32)

    mixing = call(
        mixing_kernel, array((group, BLOCK, BLOCK), F32), [VMEM], 200 * cubes
    )(unit_d)
    value_own = unit_rest[:, 2]
    value_other = partner(value_own)
    start, inner, share = call(
        terms_kernel,
        [
            array((group, 2, BLOCK, HEAD_DIM)),
            array((group, BLOCK, BLOCK), F32),
            array((group, 4, BLOCK, HEAD_DIM)),
        ],
        [VMEM] * 3,
        200 * cubes,
    )(unit_d, mixing, unit_rest)
    share_other = partner(share)
    shares = [share, share_other]
    value_parts = [value_own, value_other]
    before = 0
    if groups > 1:
        before = group
        onward = [(i, i + group) for i in range(ctx_size - group)]
        shares += [lax.ppermute(part, "ctx", onward) for part in shares]
        value_parts += [lax.ppermute(part, "ctx", onward) for part in value_parts]
    pairs = before + group
    attended = call(
        functools.partial(attend_kernel, "head", before),
        array((group, BLOCK, HEAD_DIM)),
        [SMEM] + [VMEM] * (2 + 2 * len(shares)),
        200 * cubes,
        [
            pltpu.VMEM((2 * pairs, 2, BLOCK, HEAD_DIM), BF16),
            pltpu.VMEM((2 * pairs, 2, BLOCK, HEAD_DIM), BF16),
            pltpu.VMEM((2 * pairs, 2, BLOCK, HEAD_DIM), BF16),
            pltpu.VMEM((group, LOOK + 1, 2, BLOCK, HEAD_DIM), BF16),
            pltpu.VMEM((2 * pairs, BLOCK, HEAD_DIM), BF16),
        ],
    )(away, start, inner, *shares, *value_parts)

    local = exchange(attended)
    width = out_weight.shape[1] // planes

    def projected(offset, kind):
        return call(
            functools.partial(project_kernel, "head", offset, planes),
            array((BLOCK, width), kind),
            [VMEM] * 3,
            64 * cubes,
        )(local, out_weight, weight_other)

    arrived = []
    for offset in range(1, planes):
        pairs_of = [(g, (g + 2 * offset) % head_size) for g in range(head_size)]
        arrived.append(lax.ppermute(projected(offset, BF16), "head", pairs_of))
    total = projected(0, F32)
    for part in arrived:
        total = total + part.astype(F32)
    total = total.astype(BF16)
    half = width // 2
    mine = lax.dynamic_slice_in_dim(total, core * half, half, 1)
    theirs = lax.dynamic_slice_in_dim(total, (1 - core) * half, half, 1)
    return ordered(mine, partner(theirs))


def solution(mesh):
    in_specs = (
        P("ctx", "head"),
        P("ctx", "head"),
        P("ctx", "head"),
        P("ctx", "head"),
        P("head", "ctx"),
        P("ctx", None),
        P("head", None),
    )
    out_specs = P("ctx", "head")
    return jax.shard_map(
        functools.partial(body, mesh.shape["ctx"], mesh.shape["head"]),
        mesh=mesh,
        in_specs=in_specs,
        out_specs=out_specs,
        check_vma=False,
    )
```

time: 246 us -> 91.3 us (0.37)
  other arithmetic: 88.5 us -> 3.69 us
  starting transfers between devices: 59.2 us -> 17.4 us
  matrix products: 37.2 us -> 0 us
  Pallas kernels: 0 us -> 22.8 us
  between operations: 14.3 us -> 0.12 us
  waiting for transfers between devices: 34 us -> 39.5 us
  local copies, waits for them, and re-layouts: 12.3 us -> 7.05 us
    another operation x2 -> x0, other arithmetic: 80 us -> none  [the longest x1 79.2 us: block_terms(): lax.linalg.triangular_solve(lower_matrix, rate_part[..., :, None] * ident...]
    ppermute x14 -> x7, starting transfers between devices: 59.2 us -> 2.84 us  [the longest x1 1.56 us: body(): arrived.append(lax.ppermute(projected(offset, BF16), 'head', pairs_of))]
    dot_general x48 -> x0, matrix products: 35 us -> none  [the longest x30 24.6 us: product(): return jnp.matmul(left, right, precision=lax.Precision.HIGHEST)]
    all_to_all x0 -> x3, waiting for transfers between devices: none -> 31.7 us  [exchange(): lax.all_to_all(value, 'ctx', 0, 0, axis_index_groups=members, tiled=True)]
    reduce_scatter x1 -> x0, waiting for transfers between devices: 26.5 us -> none  [body(): lax.psum_scatter(partial_value, 'head', scatter_dimension=1, tiled=True)]
    pallas_call x0 -> x6, Pallas kernels: none -> 22.8 us  [the longest x1 8.79 us: body(): call(functools.partial(attend_kernel, 'head', before), array((group, BLOC...]
    all_to_all x0 -> x3, starting transfers between devices: none -> 14.5 us  [exchange(): lax.all_to_all(value, 'ctx', 0, 0, axis_index_groups=members, tiled=True)]
    unnamed x30 -> x18, local copies, waits for them, and re-layouts: 0.06 us -> 7 us
  transfers between devices with their start and end apart: 15 -> 10, of which waited for: 11 -> 7; matrix products, arithmetic and copies ran while one was open for 15% -> 3% of each run, Pallas kernels for 0% -> 21%
where the time goes in v1:
time: 91.3 us; the launch traced here: 90.6 us
  waiting for transfers between devices  39.5 us (43%)
  Pallas kernels  22.8 us (25%)
  starting transfers between devices  17.4 us (19%)
  local copies, waits for them, and re-layouts  7.05 us (8%)
  other arithmetic  3.69 us (4%)
    all_to_all x3, waiting for transfers between devices, exchange(): lax.all_to_all(value, 'ctx', 0, 0, axis_index_groups=members, tiled=True)  31.7 us
    all_to_all x3, starting transfers between devices, exchange(): lax.all_to_all(value, 'ctx', 0, 0, axis_index_groups=members, tiled=True)  14.5 us
    pallas_call x1, Pallas kernels, body(): call(functools.partial(attend_kernel, 'head', before), array((group, BLOC...  8.79 us
    unnamed x18, local copies, waits for them, and re-layouts  7 us
    ppermute x6, waiting for transfers between devices, partner(): return lax.ppermute(value, 'head', partners)  4.72 us
    pallas_call x1, Pallas kernels, body(): call(mixing_kernel, array((group, BLOCK, BLOCK), F32), [VMEM], 200 * cubes)  4.64 us
    pallas_call x2, Pallas kernels, projected(): call(functools.partial(project_kernel, 'head', offset, planes), array((BL...  4.08 us
    pallas_call x1, Pallas kernels, body(): call(terms_kernel, [array((group, 2, BLOCK, HEAD_DIM)), array((group, BLO...  3.8 us
  transfers between devices with their start and end apart: 10, of which 7 were waited for; matrix products, arithmetic and copies ran while one was open for 3% of the time, Pallas kernels for 21%

profile of v1, /device:TPU:0, one launch (start us, length us, event | category | flops | bytes accessed | tf_op | source)
XLA Modules:
  0.0 90.6 jit_solution(10717593659006365233)
XLA Ops:
  0.0 0.9 %copy-done.1 = bf16[256,512]{1,0:T(8,128)(2,1)S(1)} copy-done((bf16[256,512]{1,0:T(8,128)(2,1)S(1)}, bf16[256,512]{1,0:T(8,128)(2,1)}, u32[]{:S(2)}) %copy-start.1) | copy-done | bytes 262168
  1.0 0.9 %copy-done.2 = bf16[256,512]{1,0:T(8,128)(2,1)S(1)} copy-done((bf16[256,512]{1,0:T(8,128)(2,1)S(1)}, bf16[256,512]{1,0:T(8,128)(2,1)}, u32[]{:S(2)}) %copy-start.2) | copy-done | bytes 262168
  1.9 0.9 %copy-done.3 = bf16[256,512]{1,0:T(8,128)(2,1)S(1)} copy-done((bf16[256,512]{1,0:T(8,128)(2,1)S(1)}, bf16[256,512]{1,0:T(8,128)(2,1)}, u32[]{:S(2)}) %copy-start.3) | copy-done | bytes 262168
  2.9 0.9 %copy-done.4 = bf16[256,512]{1,0:T(8,128)(2,1)S(1)} copy-done((bf16[256,512]{1,0:T(8,128)(2,1)S(1)}, bf16[256,512]{1,0:T(8,128)(2,1)}, u32[]{:S(2)}) %copy-start.4) | copy-done | bytes 262168
  5.2 1.5 %shard_map.73 = (bf16[4,144,128]{2,1,0:T(8,128)(2,1)S(1)}, bf16[4,144,128]{2,1,0:T(8,128)(2,1)S(1)}, bf16[4,3,128,128]{3,2,1,0:T(8,128)(2,1)S(1)}, bf16[4,3,128,128]{3,2,1,0:T(8,128)(2,1)}) custom-call(bf16[256,512]{1,0:T(8,128)(2,1)S(1)} %copy-done.1, bf16[256,512]{1,0:T(8,128)(2,1)S(1)} %copy-done.2, bf16[256,512]{1,0:T(8,128)(2,1)S(1)} %copy-done.3, ...), custom_call_target="tpu_custom_call" | custom-call | flops 4194304 | bytes 2097152 | tf_op jit(solution)/shard_map/pallas_call | solution.py:330
  7.2 0.9 %collective-permute-done = bf16[4,144,128]{2,1,0:T(8,128)(2,1)S(1)} collective-permute-done((bf16[4,144,128]{2,1,0:T(8,128)(2,1)S(1)}, bf16[4,144,128]{2,1,0:T(8,128)(2,1)S(1)}, u32[]{:S(2)}, u32[]{:S(2)}) %collective-permute-start) | collective-permute-done | bytes 147488 | tf_op jit(solution)/shard_map/ppermute | solution.py:312
  8.9 7.4 %all-to-all-start = ((bf16[8,144,128]{2,1,0:T(8,128)(2,1)}), bf16[8,144,128]{2,1,0:T(8,128)(2,1)S(1)}, u32[]{:S(2)}, u32[]{:S(2)}) async-start(bf16[8,144,128]{2,1,0:T(8,128)(2,1)} %maximum_select_fusion.1), calls=%async_computation | async-start | bytes 589824 | tf_op jit(solution)/shard_map/all_to_all | solution.py:318
  16.2 2.1 %maximum_select_fusion = bf16[8,3,128,128]{3,2,1,0:T(8,128)(2,1)} fusion(bf16[4,3,128,128]{3,2,1,0:T(8,128)(2,1)} %collective-permute-done.1, bf16[4,3,128,128]{3,2,1,0:T(8,128)(2,1)S(1)} %get-tuple-element.14, pred[]{:T(512)S(6)} %eq.2), kind=kLoop, calls=%fused_computation | loop fusion | flops 1179648 | bytes 1572865 | tf_op jit(solution)/shard_map/jit(_where)/select_n | solution.py:321
  18.4 7.7 %all-to-all-done.d_ref = bf16[8,144,128]{2,1,0:T(8,128)(2,1)S(1)} async-done(((bf16[8,144,128]{2,1,0:T(8,128)(2,1)}), bf16[8,144,128]{2,1,0:T(8,128)(2,1)S(1)}, u32[]{:S(2)}, u32[]{:S(2)}) %all-to-all-start) | async-done | bytes 294944 | tf_op jit(solution)/shard_map/all_to_all | solution.py:318
  26.1 3.6 %all-to-all-start.1 = ((bf16[8,3,128,128]{3,2,1,0:T(8,128)(2,1)}), bf16[8,3,128,128]{3,2,1,0:T(8,128)(2,1)S(1)}, u32[]{:S(2)}, u32[]{:S(2)}) async-start(bf16[8,3,128,128]{3,2,1,0:T(8,128)(2,1)} %maximum_select_fusion), calls=%async_computation.1 | async-start | bytes 1572864 | tf_op jit(solution)/shard_map/all_to_all | solution.py:318
  29.8 4.6 %shard_map.74.mixing_ref = f32[8,128,128]{2,1,0:T(8,128)S(1)} custom-call(bf16[8,144,128]{2,1,0:T(8,128)(2,1)S(1)} %all-to-all-done.d_ref), custom_call_target="tpu_custom_call" | custom-call | flops 838860800 | bytes 2097152 | tf_op jit(solution)/shard_map/pallas_call | solution.py:343
  34.5 0.8 copy-done.7
  35.3 14.6 %all-to-all-done.1.rest_ref = bf16[8,3,128,128]{3,2,1,0:T(8,128)(2,1)S(1)} async-done(((bf16[8,3,128,128]{3,2,1,0:T(8,128)(2,1)}), bf16[8,3,128,128]{3,2,1,0:T(8,128)(2,1)S(1)}, u32[]{:S(2)}, u32[]{:S(2)}) %all-to-all-start.1) | async-done | bytes 786464 | tf_op jit(solution)/shard_map/all_to_all | solution.py:318
  49.9 1.0 %copy-done.8 = f32[8,128,128]{2,1,0:T(8,128)S(1)} copy-done((f32[8,128,128]{2,1,0:T(8,128)S(1)}, f32[8,128,128]{2,1,0:T(8,128)}, u32[]{:S(2)}) %copy-start.8) | copy-done | bytes 524312
  51.0 3.8 %shard_map.75 = (bf16[8,2,128,128]{3,2,1,0:T(8,128)(2,1)S(1)}, f32[8,128,128]{2,1,0:T(8,128)S(1)}, bf16[8,4,128,128]{3,2,1,0:T(8,128)(2,1)S(1)}) custom-call(bf16[8,144,128]{2,1,0:T(8,128)(2,1)S(1)} %all-to-all-done.d_ref, f32[8,128,128]{2,1,0:T(8,128)S(1)} %copy-done.8, bf16[8,3,128,128]{3,2,1,0:T(8,128)(2,1)S(1)} %all-to-all-done.1.rest_ref), custom_call_target="tpu_custom_call" | custom-call | flops 838860800 | bytes 2097152 | tf_op jit(solution)/shard_map/pallas_call | solution.py:348
  55.4 2.4 %collective-permute-done.3.refs_3_ = bf16[8,128,128]{2,1,0:T(8,128)(2,1)S(1)} collective-permute-done((bf16[8,128,128]{2,1,0:T(8,128)(2,1)S(1)}, bf16[8,128,128]{2,1,0:T(8,128)(2,1)S(1)}, u32[]{:S(2)}, u32[]{:S(2)}) %collective-permute-start.3) | collective-permute-done | bytes 262176 | tf_op jit(solution)/shard_map/ppermute | solution.py:312
  57.9 8.8 %shard_map.76 = bf16[8,128,128]{2,1,0:T(8,128)(2,1)} custom-call(s32[8,4]{1,0:T(8,128)S(1)} %bitcast.5, bf16[8,2,128,128]{3,2,1,0:T(8,128)(2,1)S(1)} %get-tuple-element.16.start_ref, f32[8,128,128]{2,1,0:T(8,128)S(1)} %get-tuple-element.17.inner_ref, bf16[8,4,128,128]{3,2,1,0:T(8,128)(2,1)S(1)} %get-tuple-element.18.refs_0_, ...), custom_call_target="tpu_custom_call" | custom-call | flops 838860800 | bytes 2097152 | tf_op jit(solution)/shard_map/pallas_call | solution.py:368
  66.7 3.5 %all-to-all-start.2 = ((bf16[8,128,128]{2,1,0:T(8,128)(2,1)}), bf16[8,128,128]{2,1,0:T(8,128)(2,1)S(1)}, u32[]{:S(2)}, u32[]{:S(2)}) async-start(bf16[8,128,128]{2,1,0:T(8,128)(2,1)} %shard_map.76), calls=%async_computation.2 | async-start | bytes 524288 | tf_op jit(solution)/shard_map/all_to_all | solution.py:318
  70.2 9.3 %all-to-all-done.2.attended_ref = bf16[8,128,128]{2,1,0:T(8,128)(2,1)S(1)} async-done(((bf16[8,128,128]{2,1,0:T(8,128)(2,1)}), bf16[8,128,128]{2,1,0:T(8,128)(2,1)S(1)}, u32[]{:S(2)}, u32[]{:S(2)}) %all-to-all-start.2) | async-done | bytes 262176 | tf_op jit(solution)/shard_map/all_to_all | solution.py:318
  79.5 2.0 %shard_map.78 = bf16[128,1024]{1,0:T(8,128)(2,1)S(1)} custom-call(bf16[8,128,128]{2,1,0:T(8,128)(2,1)S(1)} %all-to-all-done.2.attended_ref, bf16[512,2048]{1,0:T(8,128)(2,1)S(1)} %copy-done, bf16[512,2048]{1,0:T(8,128)(2,1)} %collective-permute-done.4.other_ref), custom_call_target="tpu_custom_call" | custom-call | flops 268435456 | bytes 2097152 | tf_op jit(solution)/shard_map/pallas_call | solution.py:386
  81.6 1.6 %collective-permute-start.5 = (bf16[128,1024]{1,0:T(8,128)(2,1)S(1)}, bf16[128,1024]{1,0:T(8,128)(2,1)S(1)}, u32[]{:S(2)}, u32[]{:S(2)}) collective-permute-start(bf16[128,1024]{1,0:T(8,128)(2,1)S(1)} %shard_map.78), channel_id=1, source_target_pairs={{0,2},{1,3},{2,0},{3,1},{4,6},{5,7},{6,4},{7,5},{8,10},{9,11},{10,... | collective-permute-start | bytes 786440 | tf_op jit(solution)/shard_map/ppermute | solution.py:396
  83.1 2.0 %shard_map.77 = f32[128,1024]{1,0:T(8,128)S(1)} custom-call(bf16[8,128,128]{2,1,0:T(8,128)(2,1)S(1)} %all-to-all-done.2.attended_ref, bf16[512,2048]{1,0:T(8,128)(2,1)S(1)} %copy-done, bf16[512,2048]{1,0:T(8,128)(2,1)} %collective-permute-done.4.other_ref), custom_call_target="tpu_custom_call" | custom-call | flops 268435456 | bytes 2097152 | tf_op jit(solution)/shard_map/pallas_call | solution.py:386
  85.2 3.1 %collective-permute-done.5 = bf16[128,1024]{1,0:T(8,128)(2,1)S(1)} collective-permute-done((bf16[128,1024]{1,0:T(8,128)(2,1)S(1)}, bf16[128,1024]{1,0:T(8,128)(2,1)S(1)}, u32[]{:S(2)}, u32[]{:S(2)}) %collective-permute-start.5) | collective-permute-done | bytes 262176 | tf_op jit(solution)/shard_map/ppermute | solution.py:396
  88.5 1.3 %collective-permute-done.6 = bf16[128,512]{1,0:T(8,128)(2,1)S(1)} collective-permute-done((bf16[128,512]{1,0:T(8,128)(2,1)S(1)}, bf16[128,512]{1,0:T(8,128)(2,1)S(1)}, u32[]{:S(2)}, u32[]{:S(2)}) %collective-permute-start.6) | collective-permute-done | bytes 131104 | tf_op jit(solution)/shard_map/ppermute | solution.py:312
  (27 shorter events, 4.3 us)
Async XLA Ops:
  0.0 0.9 %copy-start.1 = (bf16[256,512]{1,0:T(8,128)(2,1)S(1)}, bf16[256,512]{1,0:T(8,128)(2,1)}, u32[]{:S(2)}) copy-start(bf16[256,512]{1,0:T(8,128)(2,1)} %q_ref.1) | copy-start | bytes 786436
  1.0 0.9 %copy-start.2 = (bf16[256,512]{1,0:T(8,128)(2,1)S(1)}, bf16[256,512]{1,0:T(8,128)(2,1)}, u32[]{:S(2)}) copy-start(bf16[256,512]{1,0:T(8,128)(2,1)} %k_ref.1) | copy-start | bytes 786436
  1.9 0.9 %copy-start.3 = (bf16[256,512]{1,0:T(8,128)(2,1)S(1)}, bf16[256,512]{1,0:T(8,128)(2,1)}, u32[]{:S(2)}) copy-start(bf16[256,512]{1,0:T(8,128)(2,1)} %v_ref.1) | copy-start | bytes 786436
  2.9 0.9 %copy-start.4 = (bf16[256,512]{1,0:T(8,128)(2,1)S(1)}, bf16[256,512]{1,0:T(8,128)(2,1)}, u32[]{:S(2)}) copy-start(bf16[256,512]{1,0:T(8,128)(2,1)} %d_ref.1) | copy-start | bytes 786436
  3.8 0.7 copy-start.5
  4.5 0.7 copy-start.6
  6.7 1.5 %collective-permute-start = (bf16[4,144,128]{2,1,0:T(8,128)(2,1)S(1)}, bf16[4,144,128]{2,1,0:T(8,128)(2,1)S(1)}, u32[]{:S(2)}, u32[]{:S(2)}) collective-permute-start(bf16[4,144,128]{2,1,0:T(8,128)(2,1)S(1)} %get-tuple-element.13), channel_id=1, source_target_pairs={{0,1},{1,0},{2,3},{3,2},{4,5},{5,4},{6,7},{7,6},{8,9},{9,8},{10,11... | collective-permute-start | bytes 442376 | tf_op jit(solution)/shard_map/ppermute | solution.py:312
  7.1 9.1 %collective-permute-start.1 = (bf16[4,3,128,128]{3,2,1,0:T(8,128)(2,1)}, bf16[4,3,128,128]{3,2,1,0:T(8,128)(2,1)}, u32[]{:S(2)}, u32[]{:S(2)}) collective-permute-start(bf16[4,3,128,128]{3,2,1,0:T(8,128)(2,1)} %get-tuple-element.15), channel_id=1, source_target_pairs={{0,1},{1,0},{2,3},{3,2},{4,5},{5,4},{6,7},{7,6},{8,9},{9,8},{10,11... | collective-permute-start | bytes 1179656 | tf_op jit(solution)/shard_map/ppermute | solution.py:312
  8.1 21.6 %copy-start = (bf16[512,2048]{1,0:T(8,128)(2,1)S(1)}, bf16[512,2048]{1,0:T(8,128)(2,1)}, u32[]{:S(2)}) copy-start(bf16[512,2048]{1,0:T(8,128)(2,1)} %own_ref.3) | copy-start | bytes 6291460
  8.9 17.2 %all-to-all-start = ((bf16[8,144,128]{2,1,0:T(8,128)(2,1)}), bf16[8,144,128]{2,1,0:T(8,128)(2,1)S(1)}, u32[]{:S(2)}, u32[]{:S(2)}) async-start(bf16[8,144,128]{2,1,0:T(8,128)(2,1)} %maximum_select_fusion.1), calls=%async_computation | async-start | bytes 589824 | tf_op jit(solution)/shard_map/all_to_all | solution.py:318
  26.1 23.8 %all-to-all-start.1 = ((bf16[8,3,128,128]{3,2,1,0:T(8,128)(2,1)}), bf16[8,3,128,128]{3,2,1,0:T(8,128)(2,1)S(1)}, u32[]{:S(2)}, u32[]{:S(2)}) async-start(bf16[8,3,128,128]{3,2,1,0:T(8,128)(2,1)} %maximum_select_fusion), calls=%async_computation.1 | async-start | bytes 1572864 | tf_op jit(solution)/shard_map/all_to_all | solution.py:318
  29.8 40.4 %collective-permute-start.4 = (bf16[512,2048]{1,0:T(8,128)(2,1)S(1)}, bf16[512,2048]{1,0:T(8,128)(2,1)}, u32[]{:S(2)}, u32[]{:S(2)}) collective-permute-start(bf16[512,2048]{1,0:T(8,128)(2,1)S(1)} %copy-done), channel_id=1, source_target_pairs={{0,1},{1,0},{2,3},{3,2},{4,5},{5,4},{6,7},{7,6},{8,9},{9,8},{10,11... | collective-permute-start | bytes 6291464 | tf_op jit(solution)/shard_map/ppermute | solution.py:312
  34.5 0.8 copy-start.7
  49.9 1.0 %copy-start.8 = (f32[8,128,128]{2,1,0:T(8,128)S(1)}, f32[8,128,128]{2,1,0:T(8,128)}, u32[]{:S(2)}) copy-start(f32[8,128,128]{2,1,0:T(8,128)} %copy-done.7) | copy-start | bytes 1572868
  54.8 3.1 %collective-permute-start.2 = (bf16[8,4,128,128]{3,2,1,0:T(8,128)(2,1)S(1)}, bf16[8,4,128,128]{3,2,1,0:T(8,128)(2,1)S(1)}, u32[]{:S(2)}, u32[]{:S(2)}) collective-permute-start(bf16[8,4,128,128]{3,2,1,0:T(8,128)(2,1)S(1)} %get-tuple-element.18.refs_0_), channel_id=1, source_target_pairs={{0,1},{1,0},{2,3},{3,2},{4,5},{5,4},{6,7},{7,6},{8,9},{9,8},{10,11... | collective-permute-start | bytes 3145736 | tf_op jit(solution)/shard_map/ppermute | solution.py:312
  54.9 3.0 %collective-permute-start.3 = (bf16[8,128,128]{2,1,0:T(8,128)(2,1)S(1)}, bf16[8,128,128]{2,1,0:T(8,128)(2,1)S(1)}, u32[]{:S(2)}, u32[]{:S(2)}) collective-permute-start(bf16[8,128,128]{2,1,0:T(8,128)(2,1)S(1)} %slice_bitcast_fusion.refs_2_), channel_id=1, source_target_pairs={{0,1},{1,0},{2,3},{3,2},{4,5},{5,4},{6,7},{7,6},{8,9},{9,8},{10,11... | collective-permute-start | bytes 786440 | tf_op jit(solution)/shard_map/ppermute | solution.py:312
  66.7 12.8 %all-to-all-start.2 = ((bf16[8,128,128]{2,1,0:T(8,128)(2,1)}), bf16[8,128,128]{2,1,0:T(8,128)(2,1)S(1)}, u32[]{:S(2)}, u32[]{:S(2)}) async-start(bf16[8,128,128]{2,1,0:T(8,128)(2,1)} %shard_map.76), calls=%async_computation.2 | async-start | bytes 524288 | tf_op jit(solution)/shard_map/all_to_all | solution.py:318
  81.6 6.7 %collective-permute-start.5 = (bf16[128,1024]{1,0:T(8,128)(2,1)S(1)}, bf16[128,1024]{1,0:T(8,128)(2,1)S(1)}, u32[]{:S(2)}, u32[]{:S(2)}) collective-permute-start(bf16[128,1024]{1,0:T(8,128)(2,1)S(1)} %shard_map.78), channel_id=1, source_target_pairs={{0,2},{1,3},{2,0},{3,1},{4,6},{5,7},{6,4},{7,5},{8,10},{9,11},{10,... | collective-permute-start | bytes 786440 | tf_op jit(solution)/shard_map/ppermute | solution.py:396
  88.4 1.4 %collective-permute-start.6 = (bf16[128,512]{1,0:T(8,128)(2,1)S(1)}, bf16[128,512]{1,0:T(8,128)(2,1)S(1)}, u32[]{:S(2)}, u32[]{:S(2)}) collective-permute-start(bf16[128,512]{1,0:T(8,128)(2,1)S(1)} %get-tuple-element.20), channel_id=1, source_target_pairs={{0,1},{1,0},{2,3},{3,2},{4,5},{5,4},{6,7},{7,6},{8,9},{9,8},{10,11... | collective-permute-start | bytes 393224 | tf_op jit(solution)/shard_map/ppermute | solution.py:312

commit v2 on v1

v2 whole, which is shorter than its diff:
```python
import functools

import jax
import jax.numpy as jnp
from jax import lax
from jax.experimental import pallas as pl
from jax.experimental.pallas import tpu as pltpu
from jax.sharding import PartitionSpec as P

HEAD_DIM = 128
BLOCK = 128
LOOK = 7
TOPK = 4
BASE = 16
EXTRA = 16
BF16 = jnp.bfloat16
F32 = jnp.float32
VMEM = pl.BlockSpec(memory_space=pltpu.VMEM)
SMEM = pl.BlockSpec(memory_space=pltpu.SMEM)
ANY = pl.BlockSpec(memory_space=pl.ANY)
HBM = pl.BlockSpec(memory_space=pltpu.HBM)
PARAMS = pltpu.CompilerParams(vmem_limit_bytes=32 * 1024 * 1024)


def dot(left, right, left_dim, right_dim):
    return lax.dot_general(
        left, right, (((left_dim,), (right_dim,)), ((), ())), preferred_element_type=F32
    )


def nn(left, right):
    return dot(left, right, 1, 0)


def nt(left, right):
    return dot(left, right, 1, 1)


def tn(left, right):
    return dot(left, right, 0, 0)


def split(value):
    high = value.astype(BF16)
    return high, (value - high.astype(F32)).astype(BF16)


def triple_nn(left, right):
    width = right[0].shape[1]
    row = jnp.concatenate(right, 1)
    both = nn(jnp.concatenate(left, 1), jnp.concatenate([row, row], 0))
    return both[:, :width] + both[:, width:]


def triple_nt(left, right):
    width = right[0].shape[0]
    column = jnp.concatenate(right, 0)
    both = nt(jnp.concatenate(left, 1), jnp.concatenate([column, column], 1))
    return both[:, :width] + both[:, width:]


def square_iotas():
    rows = lax.broadcasted_iota(jnp.int32, (BLOCK, BLOCK), 0)
    columns = lax.broadcasted_iota(jnp.int32, (BLOCK, BLOCK), 1)
    return rows, columns


def unit_slices(place, turn, blocks):
    unit = lax.bitwise_xor(place, turn)
    head, parity = unit // blocks, lax.rem(unit, blocks)
    rows = pl.ds(pl.multiple_of(parity * BLOCK, BLOCK), BLOCK)
    columns = pl.ds(pl.multiple_of(head * HEAD_DIM, HEAD_DIM), HEAD_DIM)
    return head, parity, rows, columns


def pack_kernel(axes, group, d_ref, rates_ref, selected_ref, *refs):
    outs = refs[:group]
    extra_ref, sems = refs[group:]
    blocks = d_ref.shape[0] // BLOCK
    device = lax.axis_index(axes[0])
    place = lax.rem(device, group)
    copies = []
    for turn in range(group):
        head, parity, rows, columns = unit_slices(place, turn, blocks)
        copies.append(
            pltpu.make_async_copy(
                d_ref.at[rows, columns], outs[turn].at[pl.ds(0, BLOCK)], sems.at[0, turn]
            )
        )
        copies[-1].start()
    row = lax.broadcasted_iota(jnp.int32, (EXTRA, HEAD_DIM), 0)
    lane = lax.broadcasted_iota(jnp.int32, (EXTRA, HEAD_DIM), 1)
    for turn in range(group):
        head, parity, rows, columns = unit_slices(place, turn, blocks)
        rate = rates_ref[:, rows]
        which = lax.broadcasted_iota(jnp.int32, rate.shape, 0)
        rate = jnp.sum(jnp.where(which == head, rate, 0.0), 0, keepdims=True)
        rate_1 = rate.astype(BF16).astype(F32)
        rate_2 = (rate - rate_1).astype(BF16).astype(F32)
        away = jnp.zeros((EXTRA, HEAD_DIM), jnp.int32)
        for entry in range(TOPK):
            distance = device * blocks + parity - selected_ref[parity, entry]
            away = jnp.where(lane == entry, distance, away)
        extra = jnp.where(row == 3, away.astype(F32), 0.0)
        extra = jnp.where(row == 2, (rate - rate_1) - rate_2, extra)
        extra = jnp.where(row == 1, rate_2, extra)
        extra = jnp.where(row == 0, rate_1, extra)
        extra_ref[turn] = extra.astype(BF16)
        copies.append(
            pltpu.make_async_copy(
                extra_ref.at[turn], outs[turn].at[pl.ds(BLOCK, EXTRA)], sems.at[1, turn]
            )
        )
        copies[-1].start()
    for copy in copies:
        copy.wait()


def pack_rest_kernel(axes, group, k_ref, q_ref, after, *refs):
    outs, sems = refs[:group], refs[group]
    blocks = k_ref.shape[0] // BLOCK
    place = lax.rem(lax.axis_index(axes[0]), group)
    copies = []
    for turn in range(group):
        head, parity, rows, columns = unit_slices(place, turn, blocks)
        for part, source in enumerate((k_ref, q_ref)):
            copies.append(
                pltpu.make_async_copy(
                    source.at[rows, columns], outs[turn].at[part], sems.at[part, turn]
                )
            )
            copies[-1].start()
    for copy in copies:
        copy.wait()


def fetched(sources, targets, sems):
    copies = []
    for index, (source, target) in enumerate(zip(sources, targets)):
        copies.append(pltpu.make_async_copy(source, target, sems.at[index]))
        copies[-1].start()
    return copies


def base_inverse(strict):
    count = BLOCK // BASE
    moved = [
        pltpu.roll(strict[b * BASE:(b + 1) * BASE], (BLOCK - b * BASE) % BLOCK, 1)
        if b else strict[:BASE]
        for b in range(count)
    ]
    lanes = lax.broadcasted_iota(jnp.int32, (BASE // 2, BLOCK), 1)
    rows = lax.broadcasted_iota(jnp.int32, (BASE // 2, BLOCK), 0)
    half = BASE // 2
    parts = []
    for b in range(count):
        upper = (lanes == rows + b * BASE).astype(F32)
        lower = (lanes == rows + b * BASE + half).astype(F32)
        for step in range(BASE - 1):
            if step < half:
                source = upper[step:step + 1]
                if step < half - 1:
                    upper = upper - moved[b][:half, step:step + 1] * source
            else:
                source = lower[step - half:step - half + 1]
            lower = lower - moved[b][half:, step:step + 1] * source
        parts += [upper, lower]
    return jnp.concatenate(parts, 0)


def halves(value, size):
    parts = value.reshape(BLOCK // (2 * size), 2, size, BLOCK)
    return parts[:, 0].reshape(BLOCK // 2, BLOCK), parts[:, 1].reshape(BLOCK // 2, BLOCK)


def joined(first, second, size):
    shape = (BLOCK // (2 * size), 1, size, BLOCK)
    return jnp.concatenate([first.reshape(shape), second.reshape(shape)], 1).reshape(BLOCK, BLOCK)


def mixing_kernel(axes, group, *refs):
    v_ref = refs[group]
    mixing_ref, away_ref = refs[group + 1:group + 3]
    v_outs = refs[group + 3:2 * group + 3]
    d_ref, sems, v_sems = refs[2 * group + 3:]
    units = group
    blocks = v_ref.shape[0] // BLOCK
    place = lax.rem(lax.axis_index(axes[0]), group)
    v_copies = []
    for turn in range(group):
        head, parity, v_rows, v_columns = unit_slices(place, turn, blocks)
        v_copies.append(
            pltpu.make_async_copy(v_ref.at[v_rows, v_columns], v_outs[turn], v_sems.at[turn])
        )
        v_copies[-1].start()
    copies = fetched(refs[:group], [d_ref.at[unit] for unit in range(units)], sems)
    rows, columns = square_iotas()
    diagonal = rows == columns
    strict, inverse, scales = [], [], []
    for unit in range(units):
        copies[unit].wait()
        direction = d_ref[unit, :BLOCK]
        extra = d_ref[unit, BLOCK:].astype(F32)
        rate = extra[0:1] + extra[1:2] + extra[2:3]
        away_ref[unit:unit + 1] = extra[3:4].astype(jnp.int32)
        gram = nt(direction, direction)
        squares = jnp.sum(jnp.where(diagonal, gram, 0.0), 0, keepdims=True)
        scale = lax.rsqrt(squares + 1e-06)
        scaled_rate = rate * scale
        scale_column = jnp.sum(jnp.where(diagonal, scale, 0.0), 1, keepdims=True)
        rate_column = jnp.sum(jnp.where(diagonal, scaled_rate, 0.0), 1, keepdims=True)
        strict.append(jnp.where(rows > columns, rate_column * gram * scale, 0.0))
        scales.append((scale_column, scaled_rate))
    for unit in range(units):
        inverse.append(base_inverse(strict[unit]))
    size = BASE
    while size < BLOCK:
        row = lax.broadcasted_iota(jnp.int32, (BLOCK // 2, BLOCK), 0)
        column = lax.broadcasted_iota(jnp.int32, (BLOCK // 2, BLOCK), 1)
        inside = (row // size == column // (2 * size)) & (lax.rem(column, 2 * size) < size)
        below = []
        for unit in range(units):
            corner = jnp.where(inside, halves(strict[unit], size)[1], 0.0)
            below.append(triple_nn(split(corner), split(inverse[unit])))
        for unit in range(units):
            first, second = halves(inverse[unit], size)
            padded = joined(jnp.zeros_like(below[unit]), below[unit], size)
            second = second - triple_nn(split(second), split(padded))
            inverse[unit] = joined(first, second, size)
        size *= 2
    for unit in range(units):
        mixing_ref[unit] = scales[unit][0] * inverse[unit] * scales[unit][1]
    for copy in v_copies:
        copy.wait()


def terms_kernel(group, *refs):
    start_ref, inner_ref, share_ref, d_ref, rest_ref, sems = refs[2 * group + 1:]
    mixing_ref = refs[2 * group]
    d_copies = fetched(
        [ref.at[pl.ds(0, BLOCK)] for ref in refs[:group]],
        [d_ref.at[unit] for unit in range(group)],
        sems.at[0],
    )
    rest_copies = fetched(
        refs[group:2 * group], [rest_ref.at[unit] for unit in range(group)], sems.at[1]
    )
    rows, columns = square_iotas()
    identity = (rows == columns).astype(F32)
    for unit in range(group):
        d_copies[unit].wait()
        rest_copies[unit].wait()
        direction = d_ref[unit]
        key = rest_ref[unit, 0]
        query = rest_ref[unit, 1]
        every = nt(
            jnp.concatenate([direction, query], 0), jnp.concatenate([direction, key], 0)
        )
        key_proj = split(jnp.where(rows > columns, every[:BLOCK, BLOCK:], 0.0))
        query_proj = split(jnp.where(rows >= columns, every[BLOCK:, :BLOCK], 0.0))
        mixing = jnp.concatenate(split(mixing_ref[unit]), 1)
        right = jnp.concatenate([direction, key_proj[0], key_proj[1]], 1)
        mixed = nn(mixing, jnp.concatenate([right, right], 0))
        mixed = split(
            jnp.concatenate(
                [mixed[:, :BLOCK], mixed[:, BLOCK:2 * BLOCK] + mixed[:, 2 * BLOCK:]], 1
            )
        )
        ahead = triple_nn(query_proj, mixed)
        start = split(query.astype(F32) - ahead[:, :HEAD_DIM])
        start_ref[unit, 0] = start[0]
        start_ref[unit, 1] = start[1]
        inner_ref[unit] = every[BLOCK:, BLOCK:] - ahead[:, HEAD_DIM:]
        behind = tn(jnp.concatenate(mixed, 0), jnp.concatenate([direction, direction], 0))
        end = split(key.astype(F32) - behind[BLOCK:])
        block_map = split(identity - behind[:BLOCK])
        share_ref[unit, 0] = end[0]
        share_ref[unit, 1] = end[1]
        share_ref[unit, 2] = block_map[0]
        share_ref[unit, 3] = block_map[1]


def attend_kernel(axes, before, units, away_ref, start_hbm, inner_hbm, *refs):
    count = 2 + 2 * (before > 0)
    shares, values = refs[:count], refs[count:count * (1 + units)]
    outs = refs[count * (1 + units):count * (1 + units) + units]
    (start_ref, inner_ref, ends, maps, tails, moving, value_table, results, own_sems,
     table_sems) = refs[count * (1 + units) + units:]
    core = lax.rem(lax.axis_index(axes[1]), 2)
    owner = lax.rem(lax.axis_index(axes[0]), units)
    mine = lax.rem(owner, units // 2) * 2 + core
    pairs = before + units
    copies, late_copies = [], []
    for side in range(count):
        base = 0 if side >= 2 else before
        for turn in range(units):
            unit = lax.bitwise_xor(mine, turn ^ (side % 2))
            place = 2 * (base + unit) + (core if side % 2 == 0 else 1 - core)
            index = side * units + turn
            for kind, (source, table, waiting) in enumerate((
                (shares[side].at[turn, pl.ds(0, 2)], ends, copies),
                (shares[side].at[turn, pl.ds(2, 2)], maps, copies),
                (values[index], value_table, late_copies),
            )):
                waiting.append(
                    pltpu.make_async_copy(source, table.at[place], table_sems.at[kind, index])
                )
                waiting[-1].start()
    for unit in range(units):
        turn = lax.bitwise_xor(mine, unit)
        for kind, (source, target, waiting) in enumerate((
            (start_hbm, start_ref, copies), (inner_hbm, inner_ref, late_copies)
        )):
            waiting.append(
                pltpu.make_async_copy(source.at[turn], target.at[unit], own_sems.at[kind, unit])
            )
            waiting[-1].start()
    for copy in copies:
        copy.wait()

    pair_maps = []
    for pair in range(pairs - 1):
        odd = (maps[2 * pair + 1, 0], maps[2 * pair + 1, 1])
        left = tuple(
            jnp.concatenate([ends[2 * pair, part], maps[2 * pair, part]], 0) for part in range(2)
        )
        both = split(triple_nn(left, odd))
        for part in range(2):
            tails[2 * pair, part] = both[part][:BLOCK]
            tails[2 * pair + 1, part] = ends[2 * pair + 1, part]
        pair_maps.append((both[0][BLOCK:], both[1][BLOCK:]))

    current = []
    for unit in range(units):
        pair = before + unit
        start = (start_ref[unit, 0], start_ref[unit, 1])
        passed = triple_nt(start, (maps[2 * pair, 0], maps[2 * pair, 1]))
        whole = start[0].astype(F32) + start[1].astype(F32)
        front = split(jnp.where(core == 1, passed, whole))
        current.append(front)
        for part in range(2):
            moving[unit, 0, part] = start[part]
            moving[unit, 1, part] = front[part]
    for step in range(2, LOOK + 1):
        for unit in range(units):
            pair = before + unit - step
            if pair >= 0:
                current[unit] = split(triple_nt(current[unit], pair_maps[pair + 1]))
                for part in range(2):
                    moving[unit, step, part] = current[unit][part]

    for copy in late_copies:
        copy.wait()
    rows, columns = square_iotas()
    scale = HEAD_DIM ** (-0.5)
    for unit in range(units):
        block = 2 * (before + unit) + core
        turn = lax.bitwise_xor(mine, unit)
        score_list = [jnp.where(rows >= columns, inner_ref[unit] * scale, -1e30)]
        value_list = [value_table[block]]
        for entry in range(1, TOPK):
            away = away_ref[turn, entry]
            new = away > 0
            for other in range(1, entry):
                new = new & (away_ref[turn, other] != away)
            source = jnp.clip(block - away, 0, 2 * pairs - 1)
            step = jnp.clip(before + unit - source // 2, 0, LOOK)
            same = step == 0
            query = (moving[unit, step, 0], moving[unit, step, 1])
            key = tuple(
                jnp.where(same, ends[source, part], tails[source, part]) for part in range(2)
            )
            score_list.append(jnp.where(new, triple_nt(query, key) * scale, -1e30))
            value_list.append(value_table[source])
        scores = jnp.concatenate(score_list, 1)
        expos = jnp.exp(scores - jnp.max(scores, 1, keepdims=True))
        weights = (expos / jnp.sum(expos, 1, keepdims=True)).astype(BF16)
        results[unit] = nn(weights, jnp.concatenate(value_list, 0)).astype(BF16)
    for turn in range(units):
        outs[turn][...] = results[lax.bitwise_xor(owner, turn)]


def project_kernel(axes, offset, planes, group, *refs):
    own_ref, other_ref, out_ref, attended_ref, own, other, sems = refs[group:]
    index = lax.axis_index(axes[1])
    owner = lax.rem(lax.axis_index(axes[0]), group)
    core = lax.rem(index, 2)
    plane = lax.rem(index // 2 + offset, planes)
    width = out_ref.shape[1]
    columns = pl.ds(pl.multiple_of(plane * width, width), width)
    copies = fetched(
        [own_ref.at[:, columns], other_ref.at[:, columns]], [own, other], sems
    )
    for turn in range(group):
        attended_ref[lax.bitwise_xor(owner, turn)] = refs[turn][...]
    heads = group // 2

    def half(which):
        return jnp.concatenate([attended_ref[which * heads + head] for head in range(heads)], 1)

    copies[0].wait()
    total = nn(half(core), own[...])
    copies[1].wait()
    total = total + nn(half(1 - core), other[...])
    out_ref[...] = total.astype(out_ref.dtype)


def call(kernel, outs, specs, flops, scratch=(), places=None):
    if places is None:
        places = [VMEM] * len(outs) if isinstance(outs, list) else VMEM
    return pl.pallas_call(
        kernel,
        out_shape=outs,
        in_specs=specs,
        out_specs=places,
        scratch_shapes=list(scratch),
        compiler_params=PARAMS,
        cost_estimate=pl.CostEstimate(flops=flops, bytes_accessed=2 ** 21, transcendentals=0),
    )


def body(ctx_size, head_size, queries, keys, values, directions, rates, selected, out_weight):
    heads = queries.shape[1] // HEAD_DIM
    blocks = queries.shape[0] // BLOCK
    group = blocks * heads
    planes = head_size // blocks
    groups = ctx_size // group
    axes = ("ctx", "head")
    core = lax.rem(lax.axis_index("head"), blocks)
    partners = [(g, g + 1 - 2 * (g % 2)) for g in range(head_size)]
    cubes = 2 * BLOCK ** 3

    def outward(value, turn):
        pairs = []
        for ctx in range(ctx_size):
            place = ctx % group
            unit = place ^ turn
            for g in range(head_size):
                c = g % blocks
                owner = ctx - place + heads * c + unit // blocks
                pairs.append((ctx * head_size + g, owner * head_size + g - c + unit % blocks))
        return lax.ppermute(value, axes, pairs)

    def homeward(value, turn):
        if turn == 0:
            return value
        pairs = [(i, i - i % group + (i % group ^ turn)) for i in range(ctx_size)]
        return lax.ppermute(value, "ctx", pairs)

    def partner(value):
        return lax.ppermute(value, "head", partners)

    def array(shape, kind=BF16):
        return jax.ShapeDtypeStruct(shape, kind)

    turns = range(group)
    tile = (BLOCK, HEAD_DIM)
    packed_d = call(
        functools.partial(pack_kernel, axes, group),
        [array((BLOCK + EXTRA, HEAD_DIM))] * group,
        [HBM, VMEM, SMEM],
        cubes,
        [pltpu.VMEM((group, EXTRA, HEAD_DIM), BF16), pltpu.SemaphoreType.DMA((2, group))],
        [ANY] * group,
    )(directions, rates, selected)
    unit_d = [outward(packed_d[turn], turn) for turn in turns]
    packed_rest = call(
        functools.partial(pack_rest_kernel, axes, group),
        [array((2, *tile))] * group,
        [HBM, HBM, ANY],
        cubes,
        [pltpu.SemaphoreType.DMA((2, group))],
        [ANY] * group,
    )(keys, queries, unit_d[1])
    unit_rest = [outward(packed_rest[turn], turn) for turn in turns]
    weight_other = partner(out_weight)

    mixing, away, *packed_v = call(
        functools.partial(mixing_kernel, axes, group),
        [array((group, BLOCK, BLOCK), F32), array((group, HEAD_DIM), jnp.int32)]
        + [array(tile)] * group,
        [ANY] * group + [HBM],
        200 * cubes,
        [
            pltpu.VMEM((group, BLOCK + EXTRA, HEAD_DIM), BF16),
            pltpu.SemaphoreType.DMA((group,)),
            pltpu.SemaphoreType.DMA((group,)),
        ],
        [VMEM] * 2 + [ANY] * group,
    )(*unit_d, values)
    unit_v = [outward(packed_v[turn], turn) for turn in turns]
    start, inner, share = call(
        functools.partial(terms_kernel, group),
        [
            array((group, 2, *tile)),
            array((group, BLOCK, BLOCK), F32),
            array((group, 4, *tile)),
        ],
        [ANY] * (2 * group) + [VMEM],
        200 * cubes,
        [
            pltpu.VMEM((group, *tile), BF16),
            pltpu.VMEM((group, 2, *tile), BF16),
            pltpu.SemaphoreType.DMA((2, group)),
        ],
    )(*unit_d, *unit_rest, mixing)
    share_other = partner(share)
    shares = [share, share_other]
    value_parts = unit_v + [partner(part) for part in unit_v]
    before = 0
    if groups > 1:
        before = group
        onward = [(i, i + group) for i in range(ctx_size - group)]
        shares += [lax.ppermute(part, "ctx", onward) for part in shares]
        value_parts += [lax.ppermute(part, "ctx", onward) for part in value_parts]
    pairs = before + group
    attended = call(
        functools.partial(attend_kernel, axes, before, group),
        [array(tile)] * group,
        [SMEM] + [ANY] * (2 + len(shares) + len(value_parts)),
        200 * cubes,
        [
            pltpu.VMEM((group, 2, *tile), BF16),
            pltpu.VMEM((group, BLOCK, BLOCK), F32),
            pltpu.VMEM((2 * pairs, 2, *tile), BF16),
            pltpu.VMEM((2 * pairs, 2, *tile), BF16),
            pltpu.VMEM((2 * pairs, 2, *tile), BF16),
            pltpu.VMEM((group, LOOK + 1, 2, *tile), BF16),
            pltpu.VMEM((2 * pairs, *tile), BF16),
            pltpu.VMEM((group, *tile), BF16),
            pltpu.SemaphoreType.DMA((2, group)),
            pltpu.SemaphoreType.DMA((3, 2 * pairs)),
        ],
    )(away, start, inner, *shares, *value_parts)

    local = [homeward(attended[turn], turn) for turn in turns]
    width = out_weight.shape[1] // planes

    def projected(offset, kind):
        return call(
            functools.partial(project_kernel, axes, offset, planes, group),
            array((BLOCK, width), kind),
            [VMEM] * group + [HBM] * 2,
            64 * cubes,
            [
                pltpu.VMEM((group, *tile), BF16),
                pltpu.VMEM((out_weight.shape[0], width), BF16),
                pltpu.VMEM((out_weight.shape[0], width), BF16),
                pltpu.SemaphoreType.DMA((2,)),
            ],
        )(*local, out_weight, weight_other)

    arrived = []
    for offset in range(1, planes):
        pairs_of = [(g, (g + blocks * offset) % head_size) for g in range(head_size)]
        arrived.append(lax.ppermute(projected(offset, BF16), "head", pairs_of))
    total = projected(0, F32)
    for part in arrived:
        total = total + part.astype(F32)
    total = total.astype(BF16)
    half = width // blocks
    mine = lax.dynamic_slice_in_dim(total, core * half, half, 1)
    theirs = partner(lax.dynamic_slice_in_dim(total, (1 - core) * half, half, 1))
    return jnp.where(
        core == 0,
        jnp.concatenate([mine, theirs], 0),
        jnp.concatenate([theirs, mine], 0),
    )


def solution(mesh):
    in_specs = (
        P("ctx", "head"),
        P("ctx", "head"),
        P("ctx", "head"),
        P("ctx", "head"),
        P("head", "ctx"),
        P("ctx", None),
        P("head", None),
    )
    out_specs = P("ctx", "head")
    return jax.shard_map(
        functools.partial(body, mesh.shape["ctx"], mesh.shape["head"]),
        mesh=mesh,
        in_specs=in_specs,
        out_specs=out_specs,
        check_vma=False,
    )
```

time: 91.3 us -> 125 us (1.37)
  starting transfers between devices: 17.4 us -> 73.5 us
  waiting for transfers between devices: 39.5 us -> 14.5 us
  Pallas kernels: 22.8 us -> 28.4 us
  other arithmetic: 3.69 us -> 0.81 us
    ppermute x0 -> x31, starting transfers between devices: none -> 67.4 us  [the longest x24 56.2 us: outward(): return lax.ppermute(value, axes, pairs)]
    all_to_all x3 -> x0, waiting for transfers between devices: 31.7 us -> none  [exchange(): lax.all_to_all(value, 'ctx', 0, 0, axis_index_groups=members, tiled=True)]
    all_to_all x3 -> x0, starting transfers between devices: 14.5 us -> none  [exchange(): lax.all_to_all(value, 'ctx', 0, 0, axis_index_groups=members, tiled=True)]
    ppermute x0 -> x31, waiting for transfers between devices: none -> 9.23 us  [the longest x7 5.07 us: homeward(): return lax.ppermute(value, 'ctx', pairs)]
    pallas_call x6 -> x7, Pallas kernels: 22.8 us -> 28.4 us  [the longest x1 12.1 us: body(): call(functools.partial(attend_kernel, axes, before, group), [array(tile)]...]
    ppermute x6 -> x11, starting transfers between devices: 1.28 us -> 4.61 us  [partner(): return lax.ppermute(value, 'head', partners)]
    select_n x3 -> x1, other arithmetic: 3.63 us -> 0.76 us  [body(): jnp.where(core == 0, jnp.concatenate([mine, theirs], 0), jnp.concatenate(...]
    ppermute x6 -> x11, waiting for transfers between devices: 4.72 us -> 2.92 us  [partner(): return lax.ppermute(value, 'head', partners)]
  transfers between devices with their start and end apart: 10 -> 43, of which waited for: 7 -> 11; matrix products, arithmetic and copies ran while one was open for 3% -> 0% of each run, Pallas kernels for 21% -> 22%
where the time goes in v2:
time: 125 us
  starting transfers between devices  73.5 us (59%)
  Pallas kernels  28.4 us (23%)
  waiting for transfers between devices  14.5 us (12%)
  local copies, waits for them, and re-layouts  7.14 us (6%)
    ppermute x24, starting transfers between devices, outward(): return lax.ppermute(value, axes, pairs)  56.2 us
    pallas_call x1, Pallas kernels, body(): call(functools.partial(attend_kernel, axes, before, group), [array(tile)]...  12.1 us
    ppermute x7, starting transfers between devices, homeward(): return lax.ppermute(value, 'ctx', pairs)  11.2 us
    unnamed x18, local copies, waits for them, and re-layouts  7.11 us
    pallas_call x1, Pallas kernels, body(): call(functools.partial(mixing_kernel, axes, group), [array((group, BLOCK,...  6.86 us
    pallas_call x1, Pallas kernels, body(): call(functools.partial(terms_kernel, group), [array((group, 2, *tile)), a...  6.1 us
    ppermute x7, waiting for transfers between devices, homeward(): return lax.ppermute(value, 'ctx', pairs)  5.07 us
    ppermute x11, starting transfers between devices, partner(): return lax.ppermute(value, 'head', partners)  4.61 us
  transfers between devices with their start and end apart: 43, of which 11 were waited for; matrix products, arithmetic and copies ran while one was open for 0% of the time, Pallas kernels for 22%

profile of v2, /device:TPU:0, one launch (start us, length us, event | category | flops | bytes accessed | tf_op | source)
XLA Modules:
  0.0 124.7 jit_solution(6689665616743859610)
XLA Ops:
  4.6 6.7 %collective-permute-start.2 = (bf16[144,128]{1,0:T(8,128)(2,1)S(1)}, bf16[144,128]{1,0:T(8,128)(2,1)S(1)}, u32[]{:S(2)}, u32[]{:S(2)}) collective-permute-start(bf16[144,128]{1,0:T(8,128)(2,1)S(1)} %get-tuple-element.44), channel_id=1, source_target_pairs={{0,4},{1,20},{2,6},{3,22},{4,5},{5,21},{6,7},{7,23},{8,0},{9,16},{... | collective-permute-start | bytes 110600 | tf_op jit(solution)/shard_map/ppermute | solution.py:442
  11.3 3.9 %collective-permute-start.3 = (bf16[144,128]{1,0:T(8,128)(2,1)S(1)}, bf16[144,128]{1,0:T(8,128)(2,1)S(1)}, u32[]{:S(2)}, u32[]{:S(2)}) collective-permute-start(bf16[144,128]{1,0:T(8,128)(2,1)S(1)} %get-tuple-element.45), channel_id=1, source_target_pairs={{0,5},{1,21},{2,7},{3,23},{4,4},{5,20},{6,6},{7,22},{8,1},{9,17},{... | collective-permute-start | bytes 110600 | tf_op jit(solution)/shard_map/ppermute | solution.py:442
  16.9 1.9 %collective-permute-start.5 = (bf16[144,128]{1,0:T(8,128)(2,1)S(1)}, bf16[144,128]{1,0:T(8,128)(2,1)S(1)}, u32[]{:S(2)}, u32[]{:S(2)}) collective-permute-start(bf16[144,128]{1,0:T(8,128)(2,1)S(1)} %get-tuple-element.47), channel_id=1, source_target_pairs={{0,9},{1,25},{2,11},{3,27},{4,8},{5,24},{6,10},{7,26},{8,13},{9,29... | collective-permute-start | bytes 110600 | tf_op jit(solution)/shard_map/ppermute | solution.py:442
  18.8 1.9 %collective-permute-start.6 = (bf16[144,128]{1,0:T(8,128)(2,1)S(1)}, bf16[144,128]{1,0:T(8,128)(2,1)S(1)}, u32[]{:S(2)}, u32[]{:S(2)}) collective-permute-start(bf16[144,128]{1,0:T(8,128)(2,1)S(1)} %get-tuple-element.48), channel_id=1, source_target_pairs={{0,12},{1,28},{2,14},{3,30},{4,13},{5,29},{6,15},{7,31},{8,8},{9,2... | collective-permute-start | bytes 110600 | tf_op jit(solution)/shard_map/ppermute | solution.py:442
  20.7 2.4 %collective-permute-start.7 = (bf16[144,128]{1,0:T(8,128)(2,1)S(1)}, bf16[144,128]{1,0:T(8,128)(2,1)S(1)}, u32[]{:S(2)}, u32[]{:S(2)}) collective-permute-start(bf16[144,128]{1,0:T(8,128)(2,1)S(1)} %get-tuple-element.49), channel_id=1, source_target_pairs={{0,13},{1,29},{2,15},{3,31},{4,12},{5,28},{6,14},{7,30},{8,9},{9,2... | collective-permute-start | bytes 110600 | tf_op jit(solution)/shard_map/ppermute | solution.py:442
  26.3 3.8 %collective-permute-start.11 = (bf16[2,128,128]{2,1,0:T(8,128)(2,1)S(1)}, bf16[2,128,128]{2,1,0:T(8,128)(2,1)S(1)}, u32[]{:S(2)}, u32[]{:S(2)}) collective-permute-start(bf16[2,128,128]{2,1,0:T(8,128)(2,1)S(1)} %get-tuple-element.54), channel_id=1, source_target_pairs={{0,5},{1,21},{2,7},{3,23},{4,4},{5,20},{6,6},{7,22},{8,1},{9,17},{... | collective-permute-start | bytes 196616 | tf_op jit(solution)/shard_map/ppermute | solution.py:442
  30.2 1.9 %collective-permute-start.12 = (bf16[2,128,128]{2,1,0:T(8,128)(2,1)S(1)}, bf16[2,128,128]{2,1,0:T(8,128)(2,1)S(1)}, u32[]{:S(2)}, u32[]{:S(2)}) collective-permute-start(bf16[2,128,128]{2,1,0:T(8,128)(2,1)S(1)} %get-tuple-element.55), channel_id=1, source_target_pairs={{0,8},{1,24},{2,10},{3,26},{4,9},{5,25},{6,11},{7,27},{8,12},{9,28... | collective-permute-start | bytes 196616 | tf_op jit(solution)/shard_map/ppermute | solution.py:442
  32.1 2.8 %collective-permute-start.13 = (bf16[2,128,128]{2,1,0:T(8,128)(2,1)S(1)}, bf16[2,128,128]{2,1,0:T(8,128)(2,1)S(1)}, u32[]{:S(2)}, u32[]{:S(2)}) collective-permute-start(bf16[2,128,128]{2,1,0:T(8,128)(2,1)S(1)} %get-tuple-element.56), channel_id=1, source_target_pairs={{0,9},{1,25},{2,11},{3,27},{4,8},{5,24},{6,10},{7,26},{8,13},{9,29... | collective-permute-start | bytes 196616 | tf_op jit(solution)/shard_map/ppermute | solution.py:442
  34.9 1.9 %collective-permute-start.14 = (bf16[2,128,128]{2,1,0:T(8,128)(2,1)S(1)}, bf16[2,128,128]{2,1,0:T(8,128)(2,1)S(1)}, u32[]{:S(2)}, u32[]{:S(2)}) collective-permute-start(bf16[2,128,128]{2,1,0:T(8,128)(2,1)S(1)} %get-tuple-element.57), channel_id=1, source_target_pairs={{0,12},{1,28},{2,14},{3,30},{4,13},{5,29},{6,15},{7,31},{8,8},{9,2... | collective-permute-start | bytes 196616 | tf_op jit(solution)/shard_map/ppermute | solution.py:442
  36.8 2.5 %collective-permute-start.15 = (bf16[2,128,128]{2,1,0:T(8,128)(2,1)S(1)}, bf16[2,128,128]{2,1,0:T(8,128)(2,1)S(1)}, u32[]{:S(2)}, u32[]{:S(2)}) collective-permute-start(bf16[2,128,128]{2,1,0:T(8,128)(2,1)S(1)} %get-tuple-element.58), channel_id=1, source_target_pairs={{0,13},{1,29},{2,15},{3,31},{4,12},{5,28},{6,14},{7,30},{8,9},{9,2... | collective-permute-start | bytes 196616 | tf_op jit(solution)/shard_map/ppermute | solution.py:442
  40.6 4.0 %collective-permute-start.9 = (bf16[2,128,128]{2,1,0:T(8,128)(2,1)S(1)}, bf16[2,128,128]{2,1,0:T(8,128)(2,1)S(1)}, u32[]{:S(2)}, u32[]{:S(2)}) collective-permute-start(bf16[2,128,128]{2,1,0:T(8,128)(2,1)S(1)} %get-tuple-element.52), channel_id=1, source_target_pairs={{0,1},{1,17},{2,3},{3,19},{4,0},{5,16},{6,2},{7,18},{8,5},{9,21},{... | collective-permute-start | bytes 196616 | tf_op jit(solution)/shard_map/ppermute | solution.py:442
  45.6 6.9 %shard_map.74 = (f32[8,128,128]{2,1,0:T(8,128)S(1)}, s32[8,128]{1,0:T(8,128)S(1)}, bf16[128,128]{1,0:T(8,128)(2,1)S(1)}, bf16[128,128]{1,0:T(8,128)(2,1)S(1)}, b...) custom-call(bf16[144,128]{1,0:T(8,128)(2,1)S(1)} %collective-permute, ...), custom_call_target="tpu_custom_call" | custom-call | flops 838860800 | bytes 2097152 | tf_op jit(solution)/shard_map/pallas_call | solution.py:478
  52.5 6.1 %shard_map.76 = (bf16[8,2,128,128]{3,2,1,0:T(8,128)(2,1)S(1)}, f32[8,128,128]{2,1,0:T(8,128)S(1)}, bf16[8,4,128,128]{3,2,1,0:T(8,128)(2,1)S(1)}) custom-call(bf16[144,128]{1,0:T(8,128)(2,1)S(1)} %collective-permute-done.refs_0_, bf16[144,128]{1,0:T(8,128)(2,1)S(1)} %collective-permute-done.1.refs_1_.after, ...), custom_call_target="tpu_custom_call" | custom-call | flops 838860800 | bytes 2097152 | tf_op jit(solution)/shard_map/pallas_call | solution.py:492
  60.3 2.0 %collective-permute-start.18 = (bf16[128,128]{1,0:T(8,128)(2,1)S(1)}, bf16[128,128]{1,0:T(8,128)(2,1)S(1)}, u32[]{:S(2)}, u32[]{:S(2)}) collective-permute-start(bf16[128,128]{1,0:T(8,128)(2,1)S(1)} %get-tuple-element.64), channel_id=1, source_target_pairs={{0,1},{1,17},{2,3},{3,19},{4,0},{5,16},{6,2},{7,18},{8,5},{9,21},{... | collective-permute-start | bytes 98312 | tf_op jit(solution)/shard_map/ppermute | solution.py:442
  63.4 4.8 %collective-permute-start.20 = (bf16[128,128]{1,0:T(8,128)(2,1)S(1)}, bf16[128,128]{1,0:T(8,128)(2,1)S(1)}, u32[]{:S(2)}, u32[]{:S(2)}) collective-permute-start(bf16[128,128]{1,0:T(8,128)(2,1)S(1)} %get-tuple-element.66), channel_id=1, source_target_pairs={{0,5},{1,21},{2,7},{3,23},{4,4},{5,20},{6,6},{7,22},{8,1},{9,17},{... | collective-permute-start | bytes 98312 | tf_op jit(solution)/shard_map/ppermute | solution.py:442
  69.7 3.6 %collective-permute-start.22 = (bf16[128,128]{1,0:T(8,128)(2,1)S(1)}, bf16[128,128]{1,0:T(8,128)(2,1)S(1)}, u32[]{:S(2)}, u32[]{:S(2)}) collective-permute-start(bf16[128,128]{1,0:T(8,128)(2,1)S(1)} %get-tuple-element.68), channel_id=1, source_target_pairs={{0,9},{1,25},{2,11},{3,27},{4,8},{5,24},{6,10},{7,26},{8,13},{9,29... | collective-permute-start | bytes 98312 | tf_op jit(solution)/shard_map/ppermute | solution.py:442
  73.3 2.6 %collective-permute-start.23 = (bf16[128,128]{1,0:T(8,128)(2,1)S(1)}, bf16[128,128]{1,0:T(8,128)(2,1)S(1)}, u32[]{:S(2)}, u32[]{:S(2)}) collective-permute-start(bf16[128,128]{1,0:T(8,128)(2,1)S(1)} %get-tuple-element.69), channel_id=1, source_target_pairs={{0,12},{1,28},{2,14},{3,30},{4,13},{5,29},{6,15},{7,31},{8,8},{9,2... | collective-permute-start | bytes 98312 | tf_op jit(solution)/shard_map/ppermute | solution.py:442
  75.9 2.2 %collective-permute-start.24 = (bf16[128,128]{1,0:T(8,128)(2,1)S(1)}, bf16[128,128]{1,0:T(8,128)(2,1)S(1)}, u32[]{:S(2)}, u32[]{:S(2)}) collective-permute-start(bf16[128,128]{1,0:T(8,128)(2,1)S(1)} %get-tuple-element.70), channel_id=1, source_target_pairs={{0,13},{1,29},{2,15},{3,31},{4,12},{5,28},{6,14},{7,30},{8,9},{9,2... | collective-permute-start | bytes 98312 | tf_op jit(solution)/shard_map/ppermute | solution.py:442
  78.1 2.9 %collective-permute-done.23.refs_8_ = bf16[128,128]{1,0:T(8,128)(2,1)S(1)} collective-permute-done((bf16[128,128]{1,0:T(8,128)(2,1)S(1)}, bf16[128,128]{1,0:T(8,128)(2,1)S(1)}, u32[]{:S(2)}, u32[]{:S(2)}) %collective-permute-start.23) | collective-permute-done | bytes 32800 | tf_op jit(solution)/shard_map/ppermute | solution.py:442
  86.3 12.1 %shard_map.77 = (bf16[128,128]{1,0:T(8,128)(2,1)S(1)}, bf16[128,128]{1,0:T(8,128)(2,1)S(1)}, bf16[128,128]{1,0:T(8,128)(2,1)S(1)}, bf16[128,128]{1,0:T(8,128)(2,...) custom-call(s32[8,128]{1,0:T(8,128)S(1)} %get-tuple-element.50.away_, ...), custom_call_target="tpu_custom_call" | custom-call | flops 838860800 | bytes 2097152 | tf_op jit(solution)/shard_map/pallas_call | solution.py:517
  98.6 3.4 %collective-permute-start.35 = (bf16[128,128]{1,0:T(8,128)(2,1)S(1)}, bf16[128,128]{1,0:T(8,128)(2,1)S(1)}, u32[]{:S(2)}, u32[]{:S(2)}) collective-permute-start(bf16[128,128]{1,0:T(8,128)(2,1)S(1)} %get-tuple-element.74), channel_id=1, source_target_pairs={{0,12},{4,8},{8,4},{12,0},{16,28},{20,24},{24,20},{28,16},{1,13},{... | collective-permute-start | bytes 98312 | tf_op jit(solution)/shard_map/ppermute | solution.py:448
  104.4 3.7 %collective-permute-start.38 = (bf16[128,128]{1,0:T(8,128)(2,1)S(1)}, bf16[128,128]{1,0:T(8,128)(2,1)S(1)}, u32[]{:S(2)}, u32[]{:S(2)}) collective-permute-start(bf16[128,128]{1,0:T(8,128)(2,1)S(1)} %get-tuple-element.77), channel_id=1, source_target_pairs={{0,24},{4,28},{8,16},{12,20},{16,8},{20,12},{24,0},{28,4},{1,25},{... | collective-permute-start | bytes 98312 | tf_op jit(solution)/shard_map/ppermute | solution.py:448
  110.3 4.4 %collective-permute-done.39.refs_7_ = bf16[128,128]{1,0:T(8,128)(2,1)S(1)} collective-permute-done((bf16[128,128]{1,0:T(8,128)(2,1)S(1)}, bf16[128,128]{1,0:T(8,128)(2,1)S(1)}, u32[]{:S(2)}, u32[]{:S(2)}) %collective-permute-start.39) | collective-permute-done | bytes 32800 | tf_op jit(solution)/shard_map/ppermute | solution.py:448
  120.1 2.3 %collective-permute-done.41 = bf16[128,1024]{1,0:T(8,128)(2,1)S(1)} collective-permute-done((bf16[128,1024]{1,0:T(8,128)(2,1)S(1)}, bf16[128,1024]{1,0:T(8,128)(2,1)S(1)}, u32[]{:S(2)}, u32[]{:S(2)}) %collective-permute-start.41) | collective-permute-done | bytes 262176 | tf_op jit(solution)/shard_map/ppermute | solution.py:556
  (90 shorter events, 33.7 us)
Async XLA Ops:
  0.0 114.7 %collective-permute-start.40 = (bf16[512,2048]{1,0:T(8,128)(2,1)}, bf16[512,2048]{1,0:T(8,128)(2,1)S(1)}, u32[]{:S(2)}, u32[]{:S(2)}) collective-permute-start(bf16[512,2048]{1,0:T(8,128)(2,1)} %refs_8_.5), channel_id=1, source_target_pairs={{0,1},{1,0},{2,3},{3,2},{4,5},{5,4},{6,7},{7,6},{8,9},{9,8},{10,11... | collective-permute-start | bytes 6291464 | tf_op jit(solution)/shard_map/ppermute | solution.py:451
  3.8 11.3 %collective-permute-start.1 = (bf16[144,128]{1,0:T(8,128)(2,1)S(1)}, bf16[144,128]{1,0:T(8,128)(2,1)S(1)}, u32[]{:S(2)}, u32[]{:S(2)}) collective-permute-start(bf16[144,128]{1,0:T(8,128)(2,1)S(1)} %get-tuple-element.43), channel_id=1, source_target_pairs={{0,1},{1,17},{2,3},{3,19},{4,0},{5,16},{6,2},{7,18},{8,5},{9,21},{... | collective-permute-start | bytes 110600 | tf_op jit(solution)/shard_map/ppermute | solution.py:442
  3.9 12.9 %collective-permute-start = (bf16[144,128]{1,0:T(8,128)(2,1)S(1)}, bf16[144,128]{1,0:T(8,128)(2,1)S(1)}, u32[]{:S(2)}, u32[]{:S(2)}) collective-permute-start(bf16[144,128]{1,0:T(8,128)(2,1)S(1)} %get-tuple-element.42), channel_id=1, source_target_pairs={{0,0},{1,16},{2,2},{3,18},{4,1},{5,17},{6,3},{7,19},{8,4},{9,20},{... | collective-permute-start | bytes 110600 | tf_op jit(solution)/shard_map/ppermute | solution.py:442
  4.6 14.2 %collective-permute-start.2 = (bf16[144,128]{1,0:T(8,128)(2,1)S(1)}, bf16[144,128]{1,0:T(8,128)(2,1)S(1)}, u32[]{:S(2)}, u32[]{:S(2)}) collective-permute-start(bf16[144,128]{1,0:T(8,128)(2,1)S(1)} %get-tuple-element.44), channel_id=1, source_target_pairs={{0,4},{1,20},{2,6},{3,22},{4,5},{5,21},{6,7},{7,23},{8,0},{9,16},{... | collective-permute-start | bytes 110600 | tf_op jit(solution)/shard_map/ppermute | solution.py:442
  11.3 9.4 %collective-permute-start.3 = (bf16[144,128]{1,0:T(8,128)(2,1)S(1)}, bf16[144,128]{1,0:T(8,128)(2,1)S(1)}, u32[]{:S(2)}, u32[]{:S(2)}) collective-permute-start(bf16[144,128]{1,0:T(8,128)(2,1)S(1)} %get-tuple-element.45), channel_id=1, source_target_pairs={{0,5},{1,21},{2,7},{3,23},{4,4},{5,20},{6,6},{7,22},{8,1},{9,17},{... | collective-permute-start | bytes 110600 | tf_op jit(solution)/shard_map/ppermute | solution.py:442
  15.2 10.2 %collective-permute-start.4 = (bf16[144,128]{1,0:T(8,128)(2,1)S(1)}, bf16[144,128]{1,0:T(8,128)(2,1)S(1)}, u32[]{:S(2)}, u32[]{:S(2)}) collective-permute-start(bf16[144,128]{1,0:T(8,128)(2,1)S(1)} %get-tuple-element.46), channel_id=1, source_target_pairs={{0,8},{1,24},{2,10},{3,26},{4,9},{5,25},{6,11},{7,27},{8,12},{9,28... | collective-permute-start | bytes 110600 | tf_op jit(solution)/shard_map/ppermute | solution.py:442
  16.9 9.4 %collective-permute-start.5 = (bf16[144,128]{1,0:T(8,128)(2,1)S(1)}, bf16[144,128]{1,0:T(8,128)(2,1)S(1)}, u32[]{:S(2)}, u32[]{:S(2)}) collective-permute-start(bf16[144,128]{1,0:T(8,128)(2,1)S(1)} %get-tuple-element.47), channel_id=1, source_target_pairs={{0,9},{1,25},{2,11},{3,27},{4,8},{5,24},{6,10},{7,26},{8,13},{9,29... | collective-permute-start | bytes 110600 | tf_op jit(solution)/shard_map/ppermute | solution.py:442
  18.8 11.3 %collective-permute-start.6 = (bf16[144,128]{1,0:T(8,128)(2,1)S(1)}, bf16[144,128]{1,0:T(8,128)(2,1)S(1)}, u32[]{:S(2)}, u32[]{:S(2)}) collective-permute-start(bf16[144,128]{1,0:T(8,128)(2,1)S(1)} %get-tuple-element.48), channel_id=1, source_target_pairs={{0,12},{1,28},{2,14},{3,30},{4,13},{5,29},{6,15},{7,31},{8,8},{9,2... | collective-permute-start | bytes 110600 | tf_op jit(solution)/shard_map/ppermute | solution.py:442
  20.7 11.3 %collective-permute-start.7 = (bf16[144,128]{1,0:T(8,128)(2,1)S(1)}, bf16[144,128]{1,0:T(8,128)(2,1)S(1)}, u32[]{:S(2)}, u32[]{:S(2)}) collective-permute-start(bf16[144,128]{1,0:T(8,128)(2,1)S(1)} %get-tuple-element.49), channel_id=1, source_target_pairs={{0,13},{1,29},{2,15},{3,31},{4,12},{5,28},{6,14},{7,30},{8,9},{9,2... | collective-permute-start | bytes 110600 | tf_op jit(solution)/shard_map/ppermute | solution.py:442
  25.4 9.5 %collective-permute-start.10 = (bf16[2,128,128]{2,1,0:T(8,128)(2,1)S(1)}, bf16[2,128,128]{2,1,0:T(8,128)(2,1)S(1)}, u32[]{:S(2)}, u32[]{:S(2)}) collective-permute-start(bf16[2,128,128]{2,1,0:T(8,128)(2,1)S(1)} %get-tuple-element.53), channel_id=1, source_target_pairs={{0,4},{1,20},{2,6},{3,22},{4,5},{5,21},{6,7},{7,23},{8,0},{9,16},{... | collective-permute-start | bytes 196616 | tf_op jit(solution)/shard_map/ppermute | solution.py:442
  26.3 10.5 %collective-permute-start.11 = (bf16[2,128,128]{2,1,0:T(8,128)(2,1)S(1)}, bf16[2,128,128]{2,1,0:T(8,128)(2,1)S(1)}, u32[]{:S(2)}, u32[]{:S(2)}) collective-permute-start(bf16[2,128,128]{2,1,0:T(8,128)(2,1)S(1)} %get-tuple-element.54), channel_id=1, source_target_pairs={{0,5},{1,21},{2,7},{3,23},{4,4},{5,20},{6,6},{7,22},{8,1},{9,17},{... | collective-permute-start | bytes 196616 | tf_op jit(solution)/shard_map/ppermute | solution.py:442
  30.2 9.1 %collective-permute-start.12 = (bf16[2,128,128]{2,1,0:T(8,128)(2,1)S(1)}, bf16[2,128,128]{2,1,0:T(8,128)(2,1)S(1)}, u32[]{:S(2)}, u32[]{:S(2)}) collective-permute-start(bf16[2,128,128]{2,1,0:T(8,128)(2,1)S(1)} %get-tuple-element.55), channel_id=1, source_target_pairs={{0,8},{1,24},{2,10},{3,26},{4,9},{5,25},{6,11},{7,27},{8,12},{9,28... | collective-permute-start | bytes 196616 | tf_op jit(solution)/shard_map/ppermute | solution.py:442
  32.1 8.6 %collective-permute-start.13 = (bf16[2,128,128]{2,1,0:T(8,128)(2,1)S(1)}, bf16[2,128,128]{2,1,0:T(8,128)(2,1)S(1)}, u32[]{:S(2)}, u32[]{:S(2)}) collective-permute-start(bf16[2,128,128]{2,1,0:T(8,128)(2,1)S(1)} %get-tuple-element.56), channel_id=1, source_target_pairs={{0,9},{1,25},{2,11},{3,27},{4,8},{5,24},{6,10},{7,26},{8,13},{9,29... | collective-permute-start | bytes 196616 | tf_op jit(solution)/shard_map/ppermute | solution.py:442
  34.9 17.6 %collective-permute-start.14 = (bf16[2,128,128]{2,1,0:T(8,128)(2,1)S(1)}, bf16[2,128,128]{2,1,0:T(8,128)(2,1)S(1)}, u32[]{:S(2)}, u32[]{:S(2)}) collective-permute-start(bf16[2,128,128]{2,1,0:T(8,128)(2,1)S(1)} %get-tuple-element.57), channel_id=1, source_target_pairs={{0,12},{1,28},{2,14},{3,30},{4,13},{5,29},{6,15},{7,31},{8,8},{9,2... | collective-permute-start | bytes 196616 | tf_op jit(solution)/shard_map/ppermute | solution.py:442
  36.8 15.7 %collective-permute-start.15 = (bf16[2,128,128]{2,1,0:T(8,128)(2,1)S(1)}, bf16[2,128,128]{2,1,0:T(8,128)(2,1)S(1)}, u32[]{:S(2)}, u32[]{:S(2)}) collective-permute-start(bf16[2,128,128]{2,1,0:T(8,128)(2,1)S(1)} %get-tuple-element.58), channel_id=1, source_target_pairs={{0,13},{1,29},{2,15},{3,31},{4,12},{5,28},{6,14},{7,30},{8,9},{9,2... | collective-permute-start | bytes 196616 | tf_op jit(solution)/shard_map/ppermute | solution.py:442
  39.3 13.2 %collective-permute-start.8 = (bf16[2,128,128]{2,1,0:T(8,128)(2,1)S(1)}, bf16[2,128,128]{2,1,0:T(8,128)(2,1)S(1)}, u32[]{:S(2)}, u32[]{:S(2)}) collective-permute-start(bf16[2,128,128]{2,1,0:T(8,128)(2,1)S(1)} %get-tuple-element.51), channel_id=1, source_target_pairs={{0,0},{1,16},{2,2},{3,18},{4,1},{5,17},{6,3},{7,19},{8,4},{9,20},{... | collective-permute-start | bytes 196616 | tf_op jit(solution)/shard_map/ppermute | solution.py:442
  40.6 11.9 %collective-permute-start.9 = (bf16[2,128,128]{2,1,0:T(8,128)(2,1)S(1)}, bf16[2,128,128]{2,1,0:T(8,128)(2,1)S(1)}, u32[]{:S(2)}, u32[]{:S(2)}) collective-permute-start(bf16[2,128,128]{2,1,0:T(8,128)(2,1)S(1)} %get-tuple-element.52), channel_id=1, source_target_pairs={{0,1},{1,17},{2,3},{3,19},{4,0},{5,16},{6,2},{7,18},{8,5},{9,21},{... | collective-permute-start | bytes 196616 | tf_op jit(solution)/shard_map/ppermute | solution.py:442
  58.6 27.6 %collective-permute-start.16 = (bf16[8,4,128,128]{3,2,1,0:T(8,128)(2,1)S(1)}, bf16[8,4,128,128]{3,2,1,0:T(8,128)(2,1)S(1)}, u32[]{:S(2)}, u32[]{:S(2)}) collective-permute-start(bf16[8,4,128,128]{3,2,1,0:T(8,128)(2,1)S(1)} %get-tuple-element.62.refs_0_), channel_id=1, source_target_pairs={{0,1},{1,0},{2,3},{3,2},{4,5},{5,4},{6,7},{7,6},{8,9},{9,8},{10,11... | collective-permute-start | bytes 3145736 | tf_op jit(solution)/shard_map/ppermute | solution.py:451
  60.3 8.0 %collective-permute-start.18 = (bf16[128,128]{1,0:T(8,128)(2,1)S(1)}, bf16[128,128]{1,0:T(8,128)(2,1)S(1)}, u32[]{:S(2)}, u32[]{:S(2)}) collective-permute-start(bf16[128,128]{1,0:T(8,128)(2,1)S(1)} %get-tuple-element.64), channel_id=1, source_target_pairs={{0,1},{1,17},{2,3},{3,19},{4,0},{5,16},{6,2},{7,18},{8,5},{9,21},{... | collective-permute-start | bytes 98312 | tf_op jit(solution)/shard_map/ppermute | solution.py:442
  63.4 9.9 %collective-permute-start.20 = (bf16[128,128]{1,0:T(8,128)(2,1)S(1)}, bf16[128,128]{1,0:T(8,128)(2,1)S(1)}, u32[]{:S(2)}, u32[]{:S(2)}) collective-permute-start(bf16[128,128]{1,0:T(8,128)(2,1)S(1)} %get-tuple-element.66), channel_id=1, source_target_pairs={{0,5},{1,21},{2,7},{3,23},{4,4},{5,20},{6,6},{7,22},{8,1},{9,17},{... | collective-permute-start | bytes 98312 | tf_op jit(solution)/shard_map/ppermute | solution.py:442
  69.7 8.4 %collective-permute-start.22 = (bf16[128,128]{1,0:T(8,128)(2,1)S(1)}, bf16[128,128]{1,0:T(8,128)(2,1)S(1)}, u32[]{:S(2)}, u32[]{:S(2)}) collective-permute-start(bf16[128,128]{1,0:T(8,128)(2,1)S(1)} %get-tuple-element.68), channel_id=1, source_target_pairs={{0,9},{1,25},{2,11},{3,27},{4,8},{5,24},{6,10},{7,26},{8,13},{9,29... | collective-permute-start | bytes 98312 | tf_op jit(solution)/shard_map/ppermute | solution.py:442
  73.3 7.7 %collective-permute-start.23 = (bf16[128,128]{1,0:T(8,128)(2,1)S(1)}, bf16[128,128]{1,0:T(8,128)(2,1)S(1)}, u32[]{:S(2)}, u32[]{:S(2)}) collective-permute-start(bf16[128,128]{1,0:T(8,128)(2,1)S(1)} %get-tuple-element.69), channel_id=1, source_target_pairs={{0,12},{1,28},{2,14},{3,30},{4,13},{5,29},{6,15},{7,31},{8,8},{9,2... | collective-permute-start | bytes 98312 | tf_op jit(solution)/shard_map/ppermute | solution.py:442
  98.6 9.5 %collective-permute-start.35 = (bf16[128,128]{1,0:T(8,128)(2,1)S(1)}, bf16[128,128]{1,0:T(8,128)(2,1)S(1)}, u32[]{:S(2)}, u32[]{:S(2)}) collective-permute-start(bf16[128,128]{1,0:T(8,128)(2,1)S(1)} %get-tuple-element.74), channel_id=1, source_target_pairs={{0,12},{4,8},{8,4},{12,0},{16,28},{20,24},{24,20},{28,16},{1,13},{... | collective-permute-start | bytes 98312 | tf_op jit(solution)/shard_map/ppermute | solution.py:448
  102.0 7.7 %collective-permute-start.36 = (bf16[128,128]{1,0:T(8,128)(2,1)S(1)}, bf16[128,128]{1,0:T(8,128)(2,1)S(1)}, u32[]{:S(2)}, u32[]{:S(2)}) collective-permute-start(bf16[128,128]{1,0:T(8,128)(2,1)S(1)} %get-tuple-element.75), channel_id=1, source_target_pairs={{0,16},{4,20},{8,24},{12,28},{16,0},{20,4},{24,8},{28,12},{1,17},{... | collective-permute-start | bytes 98312 | tf_op jit(solution)/shard_map/ppermute | solution.py:448
  (28 other events, 143.4 us)

commit v3 on v1

v3 whole, which is shorter than its diff:
```python
import functools

import jax
import jax.numpy as jnp
from jax import lax
from jax.experimental import pallas as pl
from jax.experimental.pallas import tpu as pltpu
from jax.sharding import PartitionSpec as P

HEAD_DIM = 128
BLOCK = 128
LOOK = 7
TOPK = 4
BASE = 16
EXTRA = 16
KEY_ROW = BLOCK + EXTRA
QUERY_ROW = KEY_ROW + BLOCK
VALUE_ROW = QUERY_ROW + BLOCK
UNIT_ROWS = VALUE_ROW + BLOCK
BF16 = jnp.bfloat16
F32 = jnp.float32
VMEM = pl.BlockSpec(memory_space=pltpu.VMEM)
SMEM = pl.BlockSpec(memory_space=pltpu.SMEM)
ANY = pl.BlockSpec(memory_space=pl.ANY)
PARAMS = pltpu.CompilerParams(vmem_limit_bytes=56 * 1024 * 1024)


def dot(left, right, left_dim, right_dim):
    return lax.dot_general(
        left, right, (((left_dim,), (right_dim,)), ((), ())), preferred_element_type=F32
    )


def nn(left, right):
    return dot(left, right, 1, 0)


def nt(left, right):
    return dot(left, right, 1, 1)


def tn(left, right):
    return dot(left, right, 0, 0)


def split(value):
    high = value.astype(BF16)
    return high, (value - high.astype(F32)).astype(BF16)


def triple(product, left, right):
    rows = left[0].shape[0]
    first = product(jnp.concatenate(left, 0), right[0])
    return first[:rows] + (first[rows:] + product(left[0], right[1]))


def square_iotas():
    rows = lax.broadcasted_iota(jnp.int32, (BLOCK, BLOCK), 0)
    columns = lax.broadcasted_iota(jnp.int32, (BLOCK, BLOCK), 1)
    return rows, columns


def pack_kernel(axes, d_ref, k_ref, q_ref, v_ref, rates_ref, selected_ref, whole, send,
                extra_ref, sems):
    heads = d_ref.shape[1] // HEAD_DIM
    blocks = d_ref.shape[0] // BLOCK
    device = lax.axis_index(axes[0])
    core = lax.rem(lax.axis_index(axes[1]), blocks)
    copies = []
    targets = []
    for side, parity in enumerate((core, 1 - core)):
        rows = pl.ds(pl.multiple_of(parity * BLOCK, BLOCK), BLOCK)
        for head in range(heads):
            target = send.at[head] if side else whole.at[core * heads + head]
            targets.append((parity, head, target))
            columns = pl.ds(head * HEAD_DIM, HEAD_DIM)
            for kind, (source, place) in enumerate((
                (d_ref, 0), (k_ref, KEY_ROW), (q_ref, QUERY_ROW), (v_ref, VALUE_ROW)
            )):
                copies.append(
                    pltpu.make_async_copy(
                        source.at[rows, columns],
                        target.at[pl.ds(place, BLOCK)],
                        sems.at[side * heads + head, kind],
                    )
                )
                copies[-1].start()
    row = lax.broadcasted_iota(jnp.int32, (EXTRA, HEAD_DIM), 0)
    lane = lax.broadcasted_iota(jnp.int32, (EXTRA, HEAD_DIM), 1)
    for index, (parity, head, target) in enumerate(targets):
        rate = rates_ref[:, pl.ds(pl.multiple_of(parity * BLOCK, BLOCK), BLOCK)][head:head + 1]
        rate_1 = rate.astype(BF16).astype(F32)
        rate_2 = (rate - rate_1).astype(BF16).astype(F32)
        away = jnp.zeros((EXTRA, HEAD_DIM), jnp.int32)
        for entry in range(TOPK):
            distance = device * blocks + parity - selected_ref[parity, entry]
            away = jnp.where(lane == entry, distance, away)
        extra = jnp.where(row == 3, away.astype(F32), 0.0)
        extra = jnp.where(row == 2, (rate - rate_1) - rate_2, extra)
        extra = jnp.where(row == 1, rate_2, extra)
        extra = jnp.where(row == 0, rate_1, extra)
        extra_ref[index] = extra.astype(BF16)
        copies.append(
            pltpu.make_async_copy(
                extra_ref.at[index], target.at[pl.ds(BLOCK, EXTRA)], sems.at[index, 4]
            )
        )
        copies[-1].start()
    for copy in copies:
        copy.wait()


def place_kernel(axes, partial, got, whole, sems):
    heads = got.shape[0]
    core = lax.rem(lax.axis_index(axes[1]), 2)
    copies = []
    for head in range(heads):
        copies.append(
            pltpu.make_async_copy(
                got.at[head], whole.at[(1 - core) * heads + head], sems.at[head]
            )
        )
        copies[-1].start()
    for copy in copies:
        copy.wait()


def fetched(sources, targets, sems):
    copies = []
    for index, (source, target) in enumerate(zip(sources, targets)):
        copies.append(pltpu.make_async_copy(source, target, sems.at[index]))
        copies[-1].start()
    return copies


def base_inverse(strict):
    count = BLOCK // BASE
    moved = [
        pltpu.roll(strict[b * BASE:(b + 1) * BASE], (BLOCK - b * BASE) % BLOCK, 1)
        if b else strict[:BASE]
        for b in range(count)
    ]
    lanes = lax.broadcasted_iota(jnp.int32, (BASE // 2, BLOCK), 1)
    rows = lax.broadcasted_iota(jnp.int32, (BASE // 2, BLOCK), 0)
    half = BASE // 2
    parts = []
    for b in range(count):
        upper = (lanes == rows + b * BASE).astype(F32)
        lower = (lanes == rows + b * BASE + half).astype(F32)
        for step in range(BASE - 1):
            if step < half:
                source = upper[step:step + 1]
                if step < half - 1:
                    upper = upper - moved[b][:half, step:step + 1] * source
            else:
                source = lower[step - half:step - half + 1]
            lower = lower - moved[b][half:, step:step + 1] * source
        parts += [upper, lower]
    return jnp.concatenate(parts, 0)


def halves(value, size):
    parts = value.reshape(BLOCK // (2 * size), 2, size, BLOCK)
    return parts[:, 0].reshape(BLOCK // 2, BLOCK), parts[:, 1].reshape(BLOCK // 2, BLOCK)


def joined(first, second, size):
    shape = (BLOCK // (2 * size), 1, size, BLOCK)
    return jnp.concatenate([first.reshape(shape), second.reshape(shape)], 1).reshape(BLOCK, BLOCK)


def terms_kernel(units_ref, start_ref, inner_ref, share_ref, away_ref, unit_ref, sems):
    units = units_ref.shape[0]
    copies = fetched(
        [units_ref.at[unit] for unit in range(units)],
        [unit_ref.at[unit] for unit in range(units)],
        sems,
    )
    rows, columns = square_iotas()
    diagonal = rows == columns
    identity = diagonal.astype(F32)
    strict, inverse, scales, query_projs = [], [], [], []
    for unit in range(units):
        copies[unit].wait()
        direction = unit_ref[unit, :BLOCK]
        query = unit_ref[unit, QUERY_ROW:QUERY_ROW + BLOCK]
        extra = unit_ref[unit, BLOCK:KEY_ROW].astype(F32)
        rate = extra[0:1] + extra[1:2] + extra[2:3]
        away_ref[unit:unit + 1] = extra[3:4].astype(jnp.int32)
        over = nt(jnp.concatenate([direction, query], 0), direction)
        gram = over[:BLOCK]
        query_projs.append(jnp.where(rows >= columns, over[BLOCK:], 0.0))
        squares = jnp.sum(jnp.where(diagonal, gram, 0.0), 0, keepdims=True)
        scale = lax.rsqrt(squares + 1e-06)
        scaled_rate = rate * scale
        scale_column = jnp.sum(jnp.where(diagonal, scale, 0.0), 1, keepdims=True)
        rate_column = jnp.sum(jnp.where(diagonal, scaled_rate, 0.0), 1, keepdims=True)
        strict.append(jnp.where(rows > columns, rate_column * gram * scale, 0.0))
        scales.append((scale_column, scaled_rate))
    for unit in range(units):
        inverse.append(base_inverse(strict[unit]))
    size = BASE
    while size < BLOCK:
        row = lax.broadcasted_iota(jnp.int32, (BLOCK // 2, BLOCK), 0)
        column = lax.broadcasted_iota(jnp.int32, (BLOCK // 2, BLOCK), 1)
        inside = (row // size == column // (2 * size)) & (lax.rem(column, 2 * size) < size)
        below = []
        for unit in range(units):
            corner = jnp.where(inside, halves(strict[unit], size)[1], 0.0)
            below.append(triple(nn, split(corner), split(inverse[unit])))
        for unit in range(units):
            first, second = halves(inverse[unit], size)
            padded = joined(jnp.zeros_like(below[unit]), below[unit], size)
            second = second - triple(nn, split(second), split(padded))
            inverse[unit] = joined(first, second, size)
        size *= 2
    for unit in range(units):
        direction = unit_ref[unit, :BLOCK]
        key = unit_ref[unit, KEY_ROW:KEY_ROW + BLOCK]
        query = unit_ref[unit, QUERY_ROW:QUERY_ROW + BLOCK]
        over = nt(jnp.concatenate([direction, query], 0), key)
        key_proj = jnp.where(rows > columns, over[:BLOCK], 0.0).astype(BF16)
        mixing = split(scales[unit][0] * inverse[unit] * scales[unit][1])
        mixed = nn(jnp.concatenate(mixing, 0), jnp.concatenate([direction, key_proj], 1))
        mixed = split(mixed[:BLOCK] + mixed[BLOCK:])
        query_proj = split(query_projs[unit])
        ahead = nn(jnp.concatenate(query_proj, 0), mixed[0])
        ahead = ahead[:BLOCK] + ahead[BLOCK:]
        start = split(query.astype(F32) - ahead[:, :HEAD_DIM])
        start_ref[unit, 0] = start[0]
        start_ref[unit, 1] = start[1]
        inner_ref[unit] = over[BLOCK:] - ahead[:, HEAD_DIM:]
        behind = tn(jnp.concatenate([mixed[0], mixed[1][:, :BLOCK]], 1), direction)
        block_map = split(identity - (behind[:BLOCK] + behind[2 * BLOCK:]))
        share_ref[unit, 0] = (key.astype(F32) - behind[BLOCK:2 * BLOCK]).astype(BF16)
        share_ref[unit, 1] = block_map[0]
        share_ref[unit, 2] = block_map[1]
        share_ref[unit, 3] = unit_ref[unit, VALUE_ROW:VALUE_ROW + BLOCK]


def attend_kernel(axes, before, units, away_ref, start_ref, inner_ref, *refs):
    count = 2 + 2 * (before > 0)
    shares = refs[:count]
    out_ref, table, tails, moving, sems = refs[count:]
    core = lax.rem(lax.axis_index(axes[1]), 2)
    pairs = before + units
    copies = []
    for side in range(count):
        base = 0 if side >= 2 else before
        parity = core if side % 2 == 0 else 1 - core
        for unit in range(units):
            copies.append(
                pltpu.make_async_copy(
                    shares[side].at[unit],
                    table.at[2 * (base + unit) + parity],
                    sems.at[side, unit],
                )
            )
            copies[-1].start()
    for copy in copies:
        copy.wait()

    pair_maps = []
    for pair in range(pairs - 1):
        even, odd = 2 * pair, 2 * pair + 1
        both = nn(
            jnp.concatenate([table[even, 0], table[even, 1], table[even, 2]], 0), table[odd, 1]
        )
        tails[even] = both[:BLOCK].astype(BF16)
        tails[odd] = table[odd, 0]
        pair_maps.append(
            split(both[BLOCK:2 * BLOCK] + (both[2 * BLOCK:] + nn(table[even, 1], table[odd, 2])))
        )

    current = []
    for unit in range(units):
        pair = before + unit
        start = (start_ref[unit, 0], start_ref[unit, 1])
        passed = triple(nt, start, (table[2 * pair, 1], table[2 * pair, 2]))
        whole = start[0].astype(F32) + start[1].astype(F32)
        current.append(split(jnp.where(core == 1, passed, whole)))
        moving[unit, 0] = start[0]
        moving[unit, 1] = current[unit][0]
    for step in range(2, LOOK + 1):
        for unit in range(units):
            pair = before + unit - step
            if pair >= 0:
                current[unit] = split(triple(nt, current[unit], pair_maps[pair + 1]))
                moving[unit, step] = current[unit][0]

    rows, columns = square_iotas()
    scale = HEAD_DIM ** (-0.5)
    for unit in range(units):
        block = 2 * (before + unit) + core
        score_list = [jnp.where(rows >= columns, inner_ref[unit] * scale, -1e30)]
        value_list = [table[block, 3]]
        for entry in range(1, TOPK):
            away = away_ref[unit, entry]
            new = away > 0
            for other in range(1, entry):
                new = new & (away_ref[unit, other] != away)
            source = jnp.clip(block - away, 0, 2 * pairs - 1)
            step = jnp.clip(before + unit - source // 2, 0, LOOK)
            key = jnp.where(step == 0, table[source, 0], tails[source])
            score = nt(moving[unit, step], key) * scale
            score_list.append(jnp.where(new, score, -1e30))
            value_list.append(table[source, 3])
        scores = jnp.concatenate(score_list, 1)
        expos = jnp.exp(scores - jnp.max(scores, 1, keepdims=True))
        weights = (expos / jnp.sum(expos, 1, keepdims=True)).astype(BF16)
        out_ref[unit] = nn(weights, jnp.concatenate(value_list, 0)).astype(BF16)


def project_kernel(axes, offset, planes, attended_ref, own_ref, other_ref, out_ref, own, other,
                   sems):
    index = lax.axis_index(axes[1])
    core = lax.rem(index, 2)
    plane = lax.rem(index // 2 + offset, planes)
    width = out_ref.shape[1]
    columns = pl.ds(pl.multiple_of(plane * width, width), width)
    copies = fetched(
        [own_ref.at[:, columns], other_ref.at[:, columns]], [own, other], sems
    )
    heads = attended_ref.shape[0] // 2

    def half(which):
        return jnp.concatenate([attended_ref[which * heads + head] for head in range(heads)], 1)

    copies[0].wait()
    total = nn(half(core), own[...])
    copies[1].wait()
    total = total + nn(half(1 - core), other[...])
    out_ref[...] = total.astype(out_ref.dtype)


def call(kernel, outs, specs, flops, scratch=(), places=None, aliases=None):
    if places is None:
        places = [VMEM] * len(outs) if isinstance(outs, list) else VMEM
    return pl.pallas_call(
        kernel,
        out_shape=outs,
        in_specs=specs,
        out_specs=places,
        scratch_shapes=list(scratch),
        input_output_aliases=aliases or {},
        compiler_params=PARAMS,
        cost_estimate=pl.CostEstimate(flops=flops, bytes_accessed=2 ** 21, transcendentals=0),
    )


def body(ctx_size, head_size, queries, keys, values, directions, rates, selected, out_weight):
    heads = queries.shape[1] // HEAD_DIM
    blocks = queries.shape[0] // BLOCK
    group = blocks * heads
    planes = head_size // blocks
    groups = ctx_size // group
    axes = ("ctx", "head")
    core = lax.rem(lax.axis_index("head"), blocks)
    partners = [(g, g + 1 - 2 * (g % 2)) for g in range(head_size)]
    cubes = 2 * BLOCK ** 3

    def exchange(value):
        members = None
        if groups > 1:
            members = [[a * group + b for b in range(group)] for a in range(groups)]
        return lax.all_to_all(value, "ctx", 0, 0, axis_index_groups=members, tiled=True)

    def partner(value):
        return lax.ppermute(value, "head", partners)

    def array(shape, kind=BF16):
        return jax.ShapeDtypeStruct(shape, kind)

    tile = (BLOCK, HEAD_DIM)
    whole_shape = array((group, UNIT_ROWS, HEAD_DIM))
    whole, send = call(
        functools.partial(pack_kernel, axes),
        [whole_shape, array((heads, UNIT_ROWS, HEAD_DIM))],
        [ANY] * 4 + [VMEM, SMEM],
        cubes,
        [pltpu.VMEM((group, EXTRA, HEAD_DIM), BF16), pltpu.SemaphoreType.DMA((group, 5))],
        [ANY] * 2,
    )(directions, keys, queries, values, rates, selected)
    whole = call(
        functools.partial(place_kernel, axes),
        whole_shape,
        [ANY] * 2,
        cubes,
        [pltpu.SemaphoreType.DMA((heads,))],
        ANY,
        {0: 0},
    )(whole, partner(send))
    unit_arrays = exchange(whole)
    weight_other = partner(out_weight)

    start, inner, share, away = call(
        terms_kernel,
        [
            array((group, 2, *tile)),
            array((group, BLOCK, BLOCK), F32),
            array((group, 4, *tile)),
            array((group, HEAD_DIM), jnp.int32),
        ],
        [ANY],
        400 * cubes,
        [
            pltpu.VMEM((group, UNIT_ROWS, HEAD_DIM), BF16),
            pltpu.SemaphoreType.DMA((group,)),
        ],
    )(unit_arrays)
    shares = [share, partner(share)]
    before = 0
    if groups > 1:
        before = group
        onward = [(i, i + group) for i in range(ctx_size - group)]
        shares += [lax.ppermute(part, "ctx", onward) for part in shares]
    pairs = before + group
    attended = call(
        functools.partial(attend_kernel, axes, before, group),
        array((group, *tile)),
        [SMEM, VMEM, VMEM] + [ANY] * len(shares),
        400 * cubes,
        [
            pltpu.VMEM((2 * pairs, 4, *tile), BF16),
            pltpu.VMEM((2 * pairs, *tile), BF16),
            pltpu.VMEM((group, LOOK + 1, *tile), BF16),
            pltpu.SemaphoreType.DMA((len(shares), group)),
        ],
    )(away, start, inner, *shares)

    local = exchange(attended)
    width = out_weight.shape[1] // planes

    def projected(offset, kind):
        return call(
            functools.partial(project_kernel, axes, offset, planes),
            array((BLOCK, width), kind),
            [VMEM, ANY, ANY],
            64 * cubes,
            [
                pltpu.VMEM((out_weight.shape[0], width), BF16),
                pltpu.VMEM((out_weight.shape[0], width), BF16),
                pltpu.SemaphoreType.DMA((2,)),
            ],
        )(local, out_weight, weight_other)

    arrived = []
    for offset in range(1, planes):
        pairs_of = [(g, (g + blocks * offset) % head_size) for g in range(head_size)]
        arrived.append(lax.ppermute(projected(offset, BF16), "head", pairs_of))
    total = projected(0, F32)
    for part in arrived:
        total = total + part.astype(F32)
    total = total.astype(BF16)
    half = width // blocks
    mine = lax.dynamic_slice_in_dim(total, core * half, half, 1)
    theirs = partner(lax.dynamic_slice_in_dim(total, (1 - core) * half, half, 1))
    return jnp.where(
        core == 0,
        jnp.concatenate([mine, theirs], 0),
        jnp.concatenate([theirs, mine], 0),
    )


def solution(mesh):
    in_specs = (
        P("ctx", "head"),
        P("ctx", "head"),
        P("ctx", "head"),
        P("ctx", "head"),
        P("head", "ctx"),
        P("ctx", None),
        P("head", None),
    )
    out_specs = P("ctx", "head")
    return jax.shard_map(
        functools.partial(body, mesh.shape["ctx"], mesh.shape["head"]),
        mesh=mesh,
        in_specs=in_specs,
        out_specs=out_specs,
        check_vma=False,
    )
```

time: 91.3 us -> 141 us (1.54)
  Pallas kernels: 22.8 us -> 78.8 us
  starting transfers between devices: 17.4 us -> 13.3 us
  waiting for transfers between devices: 39.5 us -> 43.4 us
  local copies, waits for them, and re-layouts: 7.05 us -> 3.48 us
  other arithmetic: 3.69 us -> 1.85 us
    pallas_call x6, Pallas kernels: 22.8 us -> 78.8 us  [the longest x1 34.1 us: body(): call(functools.partial(pack_kernel, axes), [whole_shape, array((heads, UN...]
    all_to_all x3 -> x2, waiting for transfers between devices: 31.7 us -> 35.9 us  [exchange(): lax.all_to_all(value, 'ctx', 0, 0, axis_index_groups=members, tiled=True)]
    all_to_all x3 -> x2, starting transfers between devices: 14.5 us -> 11 us  [exchange(): lax.all_to_all(value, 'ctx', 0, 0, axis_index_groups=members, tiled=True)]
    unnamed x18 -> x10, local copies, waits for them, and re-layouts: 7 us -> 3.45 us
    select_n x3 -> x1, other arithmetic: 3.63 us -> 0.76 us  [body(): jnp.where(core == 0, jnp.concatenate([mine, theirs], 0), jnp.concatenate(...]
    ppermute x1, waiting for transfers between devices: 3.12 us -> 1.5 us  [body(): arrived.append(lax.ppermute(projected(offset, BF16), 'head', pairs_of))]
    ppermute x6 -> x4, waiting for transfers between devices: 4.72 us -> 5.96 us  [partner(): return lax.ppermute(value, 'head', partners)]
  transfers between devices with their start and end apart: 10 -> 7, of which waited for: 7 -> 6; matrix products, arithmetic and copies ran while one was open for 3% -> 0% of each run, Pallas kernels for 21% -> 17%
where the time goes in v3:
time: 141 us
  Pallas kernels  78.8 us (56%)
  waiting for transfers between devices  43.4 us (31%)
  starting transfers between devices  13.3 us (9%)
  local copies, waits for them, and re-layouts  3.48 us (2%)
  other arithmetic  1.85 us (1%)
    all_to_all x2, waiting for transfers between devices, exchange(): lax.all_to_all(value, 'ctx', 0, 0, axis_index_groups=members, tiled=True)  35.9 us
    pallas_call x1, Pallas kernels, body(): call(functools.partial(pack_kernel, axes), [whole_shape, array((heads, UN...  34.1 us
    pallas_call x1, Pallas kernels, body(): call(functools.partial(place_kernel, axes), whole_shape, [ANY] * 2, cubes...  17.5 us
    pallas_call x1, Pallas kernels, body(): call(terms_kernel, [array((group, 2, *tile)), array((group, BLOCK, BLOCK)...  11.2 us
    all_to_all x2, starting transfers between devices, exchange(): lax.all_to_all(value, 'ctx', 0, 0, axis_index_groups=members, tiled=True)  11 us
    pallas_call x1, Pallas kernels, body(): call(functools.partial(attend_kernel, axes, before, group), array((group,...  8.54 us
    pallas_call x2, Pallas kernels, projected(): call(functools.partial(project_kernel, axes, offset, planes), array((BLOC...  7.47 us
    ppermute x4, waiting for transfers between devices, partner(): return lax.ppermute(value, 'head', partners)  5.96 us
  transfers between devices with their start and end apart: 7, of which 6 were waited for; matrix products, arithmetic and copies ran while one was open for 0% of the time, Pallas kernels for 17%

profile of v3, /device:TPU:0, one launch (start us, length us, event | category | flops | bytes accessed | tf_op | source)
XLA Modules:
  0.0 140.9 jit_solution(10243289201258937530)
XLA Ops:
  0.0 34.1 %shard_map.73 = (bf16[8,528,128]{2,1,0:T(8,128)(2,1)}, bf16[4,528,128]{2,1,0:T(8,128)(2,1)}) custom-call(bf16[256,512]{1,0:T(8,128)(2,1)} %d_ref.1, bf16[256,512]{1,0:T(8,128)(2,1)} %k_ref.1, bf16[256,512]{1,0:T(8,128)(2,1)} %q_ref.1, bf16[256,512]{1,0:T(8,128)(2,1)} %v_ref.1, f32[4,256]{1,0:T(4,128)} %rates_ref.1, s32[2,4]{1,0:T(2,128)} %selected_ref.1), custom_call_target="tpu_custom_call" | custom-call | flops 4194304 | bytes 2097152 | tf_op jit(solution)/shard_map/pallas_call | solution.py:376
  34.1 0.5 collective-permute-start
  34.6 1.8 %collective-permute-done.got = bf16[4,528,128]{2,1,0:T(8,128)(2,1)S(1)} collective-permute-done((bf16[4,528,128]{2,1,0:T(8,128)(2,1)}, bf16[4,528,128]{2,1,0:T(8,128)(2,1)S(1)}, u32[]{:S(2)}, u32[]{:S(2)}) %collective-permute-start) | collective-permute-done | bytes 540704 | tf_op jit(solution)/shard_map/ppermute | solution.py:369
  36.4 0.8 copy-done.3
  37.2 17.5 %shard_map.74 = bf16[8,528,128]{2,1,0:T(8,128)(2,1)} custom-call(bf16[8,528,128]{2,1,0:T(8,128)(2,1)} %get-tuple-element.11.partial, bf16[4,528,128]{2,1,0:T(8,128)(2,1)} %copy-done.3), custom_call_target="tpu_custom_call", output_to_operand_aliasing={{}: (0, {})} | custom-call | flops 4194304 | bytes 2097152 | tf_op jit(solution)/shard_map/pallas_call | solution.py:384
  54.7 7.3 %all-to-all-start = ((bf16[8,528,128]{2,1,0:T(8,128)(2,1)}), bf16[8,528,128]{2,1,0:T(8,128)(2,1)S(1)}, u32[]{:S(2)}, u32[]{:S(2)}) async-start(bf16[8,528,128]{2,1,0:T(8,128)(2,1)} %shard_map.74), calls=%async_computation | async-start | bytes 2162688 | tf_op jit(solution)/shard_map/all_to_all | solution.py:366
  62.0 0.1 collective-permute-start.2
  62.1 26.7 %all-to-all-done.units_ref = bf16[8,528,128]{2,1,0:T(8,128)(2,1)S(1)} async-done(((bf16[8,528,128]{2,1,0:T(8,128)(2,1)}), bf16[8,528,128]{2,1,0:T(8,128)(2,1)S(1)}, u32[]{:S(2)}, u32[]{:S(2)}) %all-to-all-start) | async-done | bytes 1081376 | tf_op jit(solution)/shard_map/all_to_all | solution.py:366
  88.8 1.0 copy-done.2
  89.8 11.2 %shard_map.75 = (bf16[8,2,128,128]{3,2,1,0:T(8,128)(2,1)}, f32[8,128,128]{2,1,0:T(8,128)}, bf16[8,4,128,128]{3,2,1,0:T(8,128)(2,1)}, s32[8,128]{1,0:T(8,128)}) custom-call(bf16[8,528,128]{2,1,0:T(8,128)(2,1)} %copy-done.2), custom_call_target="tpu_custom_call" | custom-call | flops 1677721600 | bytes 2097152 | tf_op jit(solution)/shard_map/pallas_call | solution.py:396
  101.1 2.9 %collective-permute-done.1.refs_1_ = bf16[8,4,128,128]{3,2,1,0:T(8,128)(2,1)S(1)} collective-permute-done((bf16[8,4,128,128]{3,2,1,0:T(8,128)(2,1)}, bf16[8,4,128,128]{3,2,1,0:T(8,128)(2,1)S(1)}, u32[]{:S(2)}, u32[]{:S(2)}) %collective-permute-start.1) | collective-permute-done | bytes 1048608 | tf_op jit(solution)/shard_map/ppermute | solution.py:369
  104.0 1.0 copy-done.4
  104.9 8.5 %shard_map.76 = bf16[8,128,128]{2,1,0:T(8,128)(2,1)} custom-call(s32[8,128]{1,0:T(8,128)} %get-tuple-element.13.away_ref, bf16[8,2,128,128]{3,2,1,0:T(8,128)(2,1)} %get-tuple-element.14.start_ref, f32[8,128,128]{2,1,0:T(8,128)} %get-tuple-element.15.inner_ref, bf16[8,4,128,128]{3,2,1,0:T(8,128)(2,1)} %get-tuple-element.16.refs_0_, ...), custom_call_target="tpu_custom_call" | custom-call | flops 1677721600 | bytes 2097152 | tf_op jit(solution)/shard_map/pallas_call | solution.py:418
  113.5 3.6 %all-to-all-start.1 = ((bf16[8,128,128]{2,1,0:T(8,128)(2,1)}), bf16[8,128,128]{2,1,0:T(8,128)(2,1)S(1)}, u32[]{:S(2)}, u32[]{:S(2)}) async-start(bf16[8,128,128]{2,1,0:T(8,128)(2,1)} %shard_map.76), calls=%async_computation.1 | async-start | bytes 524288 | tf_op jit(solution)/shard_map/all_to_all | solution.py:366
  117.1 9.2 %all-to-all-done.1.attended_ref = bf16[8,128,128]{2,1,0:T(8,128)(2,1)S(1)} async-done(((bf16[8,128,128]{2,1,0:T(8,128)(2,1)}), bf16[8,128,128]{2,1,0:T(8,128)(2,1)S(1)}, u32[]{:S(2)}, u32[]{:S(2)}) %all-to-all-start.1) | async-done | bytes 262176 | tf_op jit(solution)/shard_map/all_to_all | solution.py:366
  126.4 0.7 copy-done.1
  127.1 3.7 %shard_map.78 = bf16[128,1024]{1,0:T(8,128)(2,1)} custom-call(bf16[8,128,128]{2,1,0:T(8,128)(2,1)} %copy-done.1, bf16[512,2048]{1,0:T(8,128)(2,1)} %own_ref.3, bf16[512,2048]{1,0:T(8,128)(2,1)} %collective-permute-done.2.other_ref), custom_call_target="tpu_custom_call" | custom-call | flops 268435456 | bytes 2097152 | tf_op jit(solution)/shard_map/pallas_call | solution.py:435
  130.8 1.6 %collective-permute-start.3 = (bf16[128,1024]{1,0:T(8,128)(2,1)}, bf16[128,1024]{1,0:T(8,128)(2,1)S(1)}, u32[]{:S(2)}, u32[]{:S(2)}) collective-permute-start(bf16[128,1024]{1,0:T(8,128)(2,1)} %shard_map.78), channel_id=1, source_target_pairs={{0,2},{1,3},{2,0},{3,1},{4,6},{5,7},{6,4},{7,5},{8,10},{9,11},{10,... | collective-permute-start | bytes 786440 | tf_op jit(solution)/shard_map/ppermute | solution.py:450
  132.3 3.8 %shard_map.77 = f32[128,1024]{1,0:T(8,128)} custom-call(bf16[8,128,128]{2,1,0:T(8,128)(2,1)} %copy-done.1, bf16[512,2048]{1,0:T(8,128)(2,1)} %own_ref.3, bf16[512,2048]{1,0:T(8,128)(2,1)} %collective-permute-done.2.other_ref), custom_call_target="tpu_custom_call" | custom-call | flops 268435456 | bytes 2097152 | tf_op jit(solution)/shard_map/pallas_call | solution.py:435
  136.1 1.5 %collective-permute-done.3 = bf16[128,1024]{1,0:T(8,128)(2,1)S(1)} collective-permute-done((bf16[128,1024]{1,0:T(8,128)(2,1)}, bf16[128,1024]{1,0:T(8,128)(2,1)S(1)}, u32[]{:S(2)}, u32[]{:S(2)}) %collective-permute-start.3) | collective-permute-done | bytes 262176 | tf_op jit(solution)/shard_map/ppermute | solution.py:450
  137.6 1.1 add_convert_fusion
  138.7 0.1 collective-permute-start.4
  138.8 1.3 collective-permute-done.4
  140.1 0.8 maximum_select_fusion
  (9 shorter events, 0.1 us)
Async XLA Ops:
  34.1 2.3 %collective-permute-start = (bf16[4,528,128]{2,1,0:T(8,128)(2,1)}, bf16[4,528,128]{2,1,0:T(8,128)(2,1)S(1)}, u32[]{:S(2)}, u32[]{:S(2)}) collective-permute-start(bf16[4,528,128]{2,1,0:T(8,128)(2,1)} %get-tuple-element.12), channel_id=1, source_target_pairs={{0,1},{1,0},{2,3},{3,2},{4,5},{5,4},{6,7},{7,6},{8,9},{9,8},{10,11... | collective-permute-start | bytes 1622024 | tf_op jit(solution)/shard_map/ppermute | solution.py:369
  36.4 0.8 copy-start.3
  54.7 7.4 %copy-start = (bf16[512,2048]{1,0:T(8,128)(2,1)S(1)}, bf16[512,2048]{1,0:T(8,128)(2,1)}, u32[]{:S(2)}) copy-start(bf16[512,2048]{1,0:T(8,128)(2,1)} %own_ref.3) | copy-start | bytes 6291460
  54.7 34.1 %all-to-all-start = ((bf16[8,528,128]{2,1,0:T(8,128)(2,1)}), bf16[8,528,128]{2,1,0:T(8,128)(2,1)S(1)}, u32[]{:S(2)}, u32[]{:S(2)}) async-start(bf16[8,528,128]{2,1,0:T(8,128)(2,1)} %shard_map.74), calls=%async_computation | async-start | bytes 2162688 | tf_op jit(solution)/shard_map/all_to_all | solution.py:366
  62.0 55.1 %collective-permute-start.2 = (bf16[512,2048]{1,0:T(8,128)(2,1)S(1)}, bf16[512,2048]{1,0:T(8,128)(2,1)}, u32[]{:S(2)}, u32[]{:S(2)}) collective-permute-start(bf16[512,2048]{1,0:T(8,128)(2,1)S(1)} %copy-done), channel_id=1, source_target_pairs={{0,1},{1,0},{2,3},{3,2},{4,5},{5,4},{6,7},{7,6},{8,9},{9,8},{10,11... | collective-permute-start | bytes 6291464 | tf_op jit(solution)/shard_map/ppermute | solution.py:369
  88.8 1.0 copy-start.2
  101.0 2.9 %collective-permute-start.1 = (bf16[8,4,128,128]{3,2,1,0:T(8,128)(2,1)}, bf16[8,4,128,128]{3,2,1,0:T(8,128)(2,1)S(1)}, u32[]{:S(2)}, u32[]{:S(2)}) collective-permute-start(bf16[8,4,128,128]{3,2,1,0:T(8,128)(2,1)} %get-tuple-element.16.refs_0_), channel_id=1, source_target_pairs={{0,1},{1,0},{2,3},{3,2},{4,5},{5,4},{6,7},{7,6},{8,9},{9,8},{10,11... | collective-permute-start | bytes 3145736 | tf_op jit(solution)/shard_map/ppermute | solution.py:369
  104.0 1.0 copy-start.4
  113.5 12.9 %all-to-all-start.1 = ((bf16[8,128,128]{2,1,0:T(8,128)(2,1)}), bf16[8,128,128]{2,1,0:T(8,128)(2,1)S(1)}, u32[]{:S(2)}, u32[]{:S(2)}) async-start(bf16[8,128,128]{2,1,0:T(8,128)(2,1)} %shard_map.76), calls=%async_computation.1 | async-start | bytes 524288 | tf_op jit(solution)/shard_map/all_to_all | solution.py:366
  126.4 0.7 copy-start.1
  130.8 6.8 %collective-permute-start.3 = (bf16[128,1024]{1,0:T(8,128)(2,1)}, bf16[128,1024]{1,0:T(8,128)(2,1)S(1)}, u32[]{:S(2)}, u32[]{:S(2)}) collective-permute-start(bf16[128,1024]{1,0:T(8,128)(2,1)} %shard_map.78), channel_id=1, source_target_pairs={{0,2},{1,3},{2,0},{3,1},{4,6},{5,7},{6,4},{7,5},{8,10},{9,11},{10,... | collective-permute-start | bytes 786440 | tf_op jit(solution)/shard_map/ppermute | solution.py:450
  138.7 1.4 %collective-permute-start.4 = (bf16[128,512]{1,0:T(8,128)(2,1)S(1)}, bf16[128,512]{1,0:T(8,128)(2,1)S(1)}, u32[]{:S(2)}, u32[]{:S(2)}) collective-permute-start(bf16[128,512]{1,0:T(8,128)(2,1)S(1)} %get-tuple-element.18), channel_id=1, source_target_pairs={{0,1},{1,0},{2,3},{3,2},{4,5},{5,4},{6,7},{7,6},{8,9},{9,8},{10,11... | collective-permute-start | bytes 393224 | tf_op jit(solution)/shard_map/ppermute | solution.py:369

commit v4 on v3

--- a/solution.py
+++ b/solution.py
@@ -22,7 +22,6 @@
 VMEM = pl.BlockSpec(memory_space=pltpu.VMEM)
 SMEM = pl.BlockSpec(memory_space=pltpu.SMEM)
 ANY = pl.BlockSpec(memory_space=pl.ANY)
-PARAMS = pltpu.CompilerParams(vmem_limit_bytes=56 * 1024 * 1024)
 
 
 def dot(left, right, left_dim, right_dim):
@@ -60,19 +59,17 @@
     return rows, columns
 
 
-def pack_kernel(axes, d_ref, k_ref, q_ref, v_ref, rates_ref, selected_ref, whole, send,
-                extra_ref, sems):
+def pack_kernel(axes, d_ref, k_ref, q_ref, v_ref, rates_ref, selected_ref, keep, send,
+                units_ref, sems, out_sems):
     heads = d_ref.shape[1] // HEAD_DIM
     blocks = d_ref.shape[0] // BLOCK
     device = lax.axis_index(axes[0])
     core = lax.rem(lax.axis_index(axes[1]), blocks)
     copies = []
-    targets = []
-    for side, parity in enumerate((core, 1 - core)):
+    sides = (1 - core, core)
+    for side, parity in enumerate(sides):
         rows = pl.ds(pl.multiple_of(parity * BLOCK, BLOCK), BLOCK)
         for head in range(heads):
-            target = send.at[head] if side else whole.at[core * heads + head]
-            targets.append((parity, head, target))
             columns = pl.ds(head * HEAD_DIM, HEAD_DIM)
             for kind, (source, place) in enumerate((
                 (d_ref, 0), (k_ref, KEY_ROW), (q_ref, QUERY_ROW), (v_ref, VALUE_ROW)
@@ -80,47 +77,56 @@
                 copies.append(
                     pltpu.make_async_copy(
                         source.at[rows, columns],
-                        target.at[pl.ds(place, BLOCK)],
+                        units_ref.at[side, head, pl.ds(place, BLOCK)],
                         sems.at[side * heads + head, kind],
                     )
                 )
                 copies[-1].start()
     row = lax.broadcasted_iota(jnp.int32, (EXTRA, HEAD_DIM), 0)
     lane = lax.broadcasted_iota(jnp.int32, (EXTRA, HEAD_DIM), 1)
-    for index, (parity, head, target) in enumerate(targets):
-        rate = rates_ref[:, pl.ds(pl.multiple_of(parity * BLOCK, BLOCK), BLOCK)][head:head + 1]
-        rate_1 = rate.astype(BF16).astype(F32)
-        rate_2 = (rate - rate_1).astype(BF16).astype(F32)
+    for side, parity in enumerate(sides):
+        rates = rates_ref[:, pl.ds(pl.multiple_of(parity * BLOCK, BLOCK), BLOCK)]
         away = jnp.zeros((EXTRA, HEAD_DIM), jnp.int32)
         for entry in range(TOPK):
             distance = device * blocks + parity - selected_ref[parity, entry]
             away = jnp.where(lane == entry, distance, away)
-        extra = jnp.where(row == 3, away.astype(F32), 0.0)
-        extra = jnp.where(row == 2, (rate - rate_1) - rate_2, extra)
-        extra = jnp.where(row == 1, rate_2, extra)
-        extra = jnp.where(row == 0, rate_1, extra)
-        extra_ref[index] = extra.astype(BF16)
-        copies.append(
-            pltpu.make_async_copy(
-                extra_ref.at[index], target.at[pl.ds(BLOCK, EXTRA)], sems.at[index, 4]
+        away = jnp.where(row == 3, away.astype(F32), 0.0)
+        rates_1 = rates.astype(BF16).astype(F32)
+        rates_2 = (rates - rates_1).astype(BF16).astype(F32)
+        rates_3 = (rates - rates_1) - rates_2
+        for head in range(heads):
+            extra = jnp.where(row == 2, rates_3[head:head + 1], away)
+            extra = jnp.where(row == 1, rates_2[head:head + 1], extra)
+            extra = jnp.where(row == 0, rates_1[head:head + 1], extra)
+            units_ref[side, head, BLOCK:KEY_ROW] = extra.astype(BF16)
+    out_copies = []
+    for side, target in enumerate((send, keep)):
+        for head in range(heads):
+            index = side * heads + head
+            for copy in copies[4 * index:4 * index + 4]:
+                copy.wait()
+            out_copies.append(
+                pltpu.make_async_copy(
+                    units_ref.at[side, head], target.at[head], out_sems.at[index]
+                )
             )
-        )
-        copies[-1].start()
-    for copy in copies:
+            out_copies[-1].start()
+    for copy in out_copies:
         copy.wait()
 
 
-def place_kernel(axes, partial, got, whole, sems):
+def place_kernel(axes, keep, got, whole, sems):
     heads = got.shape[0]
     core = lax.rem(lax.axis_index(axes[1]), 2)
     copies = []
-    for head in range(heads):
-        copies.append(
-            pltpu.make_async_copy(
-                got.at[head], whole.at[(1 - core) * heads + head], sems.at[head]
+    for side, (source, owner) in enumerate(((keep, core), (got, 1 - core))):
+        for head in range(heads):
+            copies.append(
+                pltpu.make_async_copy(
+                    source.at[head], whole.at[owner * heads + head], sems.at[side, head]
+                )
             )
-        )
-        copies[-1].start()
+            copies[-1].start()
     for copy in copies:
         copy.wait()
 
@@ -169,19 +175,13 @@
     return jnp.concatenate([first.reshape(shape), second.reshape(shape)], 1).reshape(BLOCK, BLOCK)
 
 
-def terms_kernel(units_ref, start_ref, inner_ref, share_ref, away_ref, unit_ref, sems):
-    units = units_ref.shape[0]
-    copies = fetched(
-        [units_ref.at[unit] for unit in range(units)],
-        [unit_ref.at[unit] for unit in range(units)],
-        sems,
-    )
+def terms_kernel(unit_ref, start_ref, inner_ref, share_ref, away_ref):
+    units = unit_ref.shape[0]
     rows, columns = square_iotas()
     diagonal = rows == columns
     identity = diagonal.astype(F32)
     strict, inverse, scales, query_projs = [], [], [], []
     for unit in range(units):
-        copies[unit].wait()
         direction = unit_ref[unit, :BLOCK]
         query = unit_ref[unit, QUERY_ROW:QUERY_ROW + BLOCK]
         extra = unit_ref[unit, BLOCK:KEY_ROW].astype(F32)
@@ -238,49 +238,52 @@
         share_ref[unit, 3] = unit_ref[unit, VALUE_ROW:VALUE_ROW + BLOCK]
 
 
-def attend_kernel(axes, before, units, away_ref, start_ref, inner_ref, *refs):
+def attend_kernel(axes, before, units, *refs):
+    core = lax.rem(lax.axis_index(axes[1]), 2)
+    for parity in range(2):
+        pl.when(core == parity)(functools.partial(attend, before, units, parity, *refs))
+
+
+def attend(before, units, parity, away_ref, start_ref, inner_ref, *refs):
     count = 2 + 2 * (before > 0)
-    shares = refs[:count]
-    out_ref, table, tails, moving, sems = refs[count:]
-    core = lax.rem(lax.axis_index(axes[1]), 2)
+    tails, moving = refs[count + 1:]
+    out_ref = refs[count]
     pairs = before + units
-    copies = []
-    for side in range(count):
-        base = 0 if side >= 2 else before
-        parity = core if side % 2 == 0 else 1 - core
-        for unit in range(units):
-            copies.append(
-                pltpu.make_async_copy(
-                    shares[side].at[unit],
-                    table.at[2 * (base + unit) + parity],
-                    sems.at[side, unit],
-                )
-            )
-            copies[-1].start()
-    for copy in copies:
-        copy.wait()
+    sides = [(refs[2 * group + parity], refs[2 * group + 1 - parity]) for group in range(count // 2)]
+
+    def fixed(odd, pair, part):
+        if pair < before:
+            return sides[1][odd][pair, part]
+        return sides[0][odd][pair - before, part]
+
+    def listed(odd, pair, part):
+        if not before:
+            return sides[0][odd][pair, part]
+        return jnp.where(
+            pair < before,
+            sides[1][odd][jnp.minimum(pair, before - 1), part],
+            sides[0][odd][jnp.maximum(pair - before, 0), part],
+        )
 
     pair_maps = []
     for pair in range(pairs - 1):
-        even, odd = 2 * pair, 2 * pair + 1
         both = nn(
-            jnp.concatenate([table[even, 0], table[even, 1], table[even, 2]], 0), table[odd, 1]
+            jnp.concatenate([fixed(0, pair, 0), fixed(0, pair, 1), fixed(0, pair, 2)], 0),
+            fixed(1, pair, 1),
         )
-        tails[even] = both[:BLOCK].astype(BF16)
-        tails[odd] = table[odd, 0]
-        pair_maps.append(
-            split(both[BLOCK:2 * BLOCK] + (both[2 * BLOCK:] + nn(table[even, 1], table[odd, 2])))
-        )
+        tails[pair] = both[:BLOCK].astype(BF16)
+        low = both[2 * BLOCK:] + nn(fixed(0, pair, 1), fixed(1, pair, 2))
+        pair_maps.append(split(both[BLOCK:2 * BLOCK] + low))
 
     current = []
     for unit in range(units):
-        pair = before + unit
-        start = (start_ref[unit, 0], start_ref[unit, 1])
-        passed = triple(nt, start, (table[2 * pair, 1], table[2 * pair, 2]))
-        whole = start[0].astype(F32) + start[1].astype(F32)
-        current.append(split(jnp.where(core == 1, passed, whole)))
-        moving[unit, 0] = start[0]
-        moving[unit, 1] = current[unit][0]
+        front = (start_ref[unit, 0], start_ref[unit, 1])
+        moving[unit, 0] = front[0]
+        if parity:
+            pair = before + unit
+            front = split(triple(nt, front, (fixed(0, pair, 1), fixed(0, pair, 2))))
+        moving[unit, 1] = front[0]
+        current.append(front)
     for step in range(2, LOOK + 1):
         for unit in range(units):
             pair = before + unit - step
@@ -291,20 +294,23 @@
     rows, columns = square_iotas()
     scale = HEAD_DIM ** (-0.5)
     for unit in range(units):
-        block = 2 * (before + unit) + core
+        block = 2 * (before + unit) + parity
         score_list = [jnp.where(rows >= columns, inner_ref[unit] * scale, -1e30)]
-        value_list = [table[block, 3]]
+        value_list = [fixed(parity, before + unit, 3)]
         for entry in range(1, TOPK):
             away = away_ref[unit, entry]
             new = away > 0
             for other in range(1, entry):
                 new = new & (away_ref[unit, other] != away)
             source = jnp.clip(block - away, 0, 2 * pairs - 1)
-            step = jnp.clip(before + unit - source // 2, 0, LOOK)
-            key = jnp.where(step == 0, table[source, 0], tails[source])
+            pair, odd = source // 2, lax.rem(source, 2) == 1
+            step = jnp.clip(before + unit - pair, 0, LOOK)
+            key = jnp.where(odd, listed(1, pair, 0), tails[pair])
+            if parity:
+                key = jnp.where(step == 0, fixed(0, before + unit, 0), key)
             score = nt(moving[unit, step], key) * scale
             score_list.append(jnp.where(new, score, -1e30))
-            value_list.append(table[source, 3])
+            value_list.append(jnp.where(odd, listed(1, pair, 3), listed(0, pair, 3)))
         scores = jnp.concatenate(score_list, 1)
         expos = jnp.exp(scores - jnp.max(scores, 1, keepdims=True))
         weights = (expos / jnp.sum(expos, 1, keepdims=True)).astype(BF16)
@@ -333,7 +339,7 @@
     out_ref[...] = total.astype(out_ref.dtype)
 
 
-def call(kernel, outs, specs, flops, scratch=(), places=None, aliases=None):
+def call(kernel, outs, specs, flops, scratch=(), places=None, space=32):
     if places is None:
         places = [VMEM] * len(outs) if isinstance(outs, list) else VMEM
     return pl.pallas_call(
@@ -342,8 +348,7 @@
         in_specs=specs,
         out_specs=places,
         scratch_shapes=list(scratch),
-        input_output_aliases=aliases or {},
-        compiler_params=PARAMS,
+        compiler_params=pltpu.CompilerParams(vmem_limit_bytes=space * 2 ** 20),
         cost_estimate=pl.CostEstimate(flops=flops, bytes_accessed=2 ** 21, transcendentals=0),
     )
 
@@ -373,23 +378,28 @@
 
     tile = (BLOCK, HEAD_DIM)
     whole_shape = array((group, UNIT_ROWS, HEAD_DIM))
-    whole, send = call(
+    half_shape = array((heads, UNIT_ROWS, HEAD_DIM))
+    keep, send = call(
         functools.partial(pack_kernel, axes),
-        [whole_shape, array((heads, UNIT_ROWS, HEAD_DIM))],
+        [half_shape] * 2,
         [ANY] * 4 + [VMEM, SMEM],
         cubes,
-        [pltpu.VMEM((group, EXTRA, HEAD_DIM), BF16), pltpu.SemaphoreType.DMA((group, 5))],
+        [
+            pltpu.VMEM((2, heads, UNIT_ROWS, HEAD_DIM), BF16),
+            pltpu.SemaphoreType.DMA((group, 4)),
+            pltpu.SemaphoreType.DMA((group,)),
+        ],
         [ANY] * 2,
+        56,
     )(directions, keys, queries, values, rates, selected)
     whole = call(
         functools.partial(place_kernel, axes),
-        whole_shape,
-        [ANY] * 2,
+        array((group, UNIT_ROWS, HEAD_DIM)),
+        [VMEM] * 2,
         cubes,
-        [pltpu.SemaphoreType.DMA((heads,))],
+        [pltpu.SemaphoreType.DMA((2, heads))],
         ANY,
-        {0: 0},
-    )(whole, partner(send))
+    )(keep, partner(send))
     unit_arrays = exchange(whole)
     weight_other = partner(out_weight)
 
@@ -401,12 +411,8 @@
             array((group, 4, *tile)),
             array((group, HEAD_DIM), jnp.int32),
         ],
-        [ANY],
+        [VMEM],
         400 * cubes,
-        [
-            pltpu.VMEM((group, UNIT_ROWS, HEAD_DIM), BF16),
-            pltpu.SemaphoreType.DMA((group,)),
-        ],
     )(unit_arrays)
     shares = [share, partner(share)]
     before = 0
@@ -418,13 +424,11 @@
     attended = call(
         functools.partial(attend_kernel, axes, before, group),
         array((group, *tile)),
-        [SMEM, VMEM, VMEM] + [ANY] * len(shares),
+        [SMEM] + [VMEM] * (2 + len(shares)),
         400 * cubes,
         [
-            pltpu.VMEM((2 * pairs, 4, *tile), BF16),
-            pltpu.VMEM((2 * pairs, *tile), BF16),
+            pltpu.VMEM((pairs, *tile), BF16),
             pltpu.VMEM((group, LOOK + 1, *tile), BF16),
-            pltpu.SemaphoreType.DMA((len(shares), group)),
         ],
     )(away, start, inner, *shares)
 

time: 141 us -> 82.8 us (0.59)
  Pallas kernels: 78.8 us -> 21.5 us
  local copies, waits for them, and re-layouts: 3.48 us -> 1.08 us
  waiting for transfers between devices: 43.4 us -> 45.6 us
    pallas_call x2, Pallas kernels: 51.6 us -> 4.1 us  [the longest x1 3.05 us: body(): call(functools.partial(pack_kernel, axes), [half_shape] * 2, [ANY] * 4 +...]
    pallas_call x2, Pallas kernels: 7.47 us -> 3.78 us  [projected(): call(functools.partial(project_kernel, axes, offset, planes), array((BLOC...]
    pallas_call x1, Pallas kernels: 11.2 us -> 7.74 us  [body(): call(terms_kernel, [array((group, 2, *tile)), array((group, BLOCK, BLOCK)...]
    pallas_call x1, Pallas kernels: 8.54 us -> 5.93 us  [body(): call(functools.partial(attend_kernel, axes, before, group), array((group,...]
    unnamed x10 -> x4, local copies, waits for them, and re-layouts: 3.45 us -> 1.05 us
    ppermute x1, waiting for transfers between devices: 1.5 us -> 3.6 us  [body(): arrived.append(lax.ppermute(projected(offset, BF16), 'head', pairs_of))]
  transfers between devices with their start and end apart: 7 -> 7, of which waited for: 6 -> 6; matrix products, arithmetic and copies ran while one was open for 0% -> 0% of each run, Pallas kernels for 17% -> 19%
where the time goes in v4:
time: 82.8 us; the launch traced here: 82.2 us
  waiting for transfers between devices  45.6 us (55%)
  Pallas kernels  21.5 us (26%)
  starting transfers between devices  13.1 us (16%)
  local copies, waits for them, and re-layouts  1.08 us (1%)
    all_to_all x2, waiting for transfers between devices, exchange(): lax.all_to_all(value, 'ctx', 0, 0, axis_index_groups=members, tiled=True)  36.2 us
    all_to_all x2, starting transfers between devices, exchange(): lax.all_to_all(value, 'ctx', 0, 0, axis_index_groups=members, tiled=True)  10.9 us
    pallas_call x1, Pallas kernels, body(): call(terms_kernel, [array((group, 2, *tile)), array((group, BLOCK, BLOCK)...  7.74 us
    pallas_call x1, Pallas kernels, body(): call(functools.partial(attend_kernel, axes, before, group), array((group,...  5.93 us
    ppermute x4, waiting for transfers between devices, partner(): return lax.ppermute(value, 'head', partners)  5.75 us
    pallas_call x2, Pallas kernels, projected(): call(functools.partial(project_kernel, axes, offset, planes), array((BLOC...  3.78 us
    ppermute x1, waiting for transfers between devices, body(): arrived.append(lax.ppermute(projected(offset, BF16), 'head', pairs_of))  3.6 us
    pallas_call x1, Pallas kernels, body(): call(functools.partial(pack_kernel, axes), [half_shape] * 2, [ANY] * 4 +...  3.05 us
  transfers between devices with their start and end apart: 7, of which 6 were waited for; matrix products, arithmetic and copies ran while one was open for 0% of the time, Pallas kernels for 19%

profile of v4, /device:TPU:0, one launch (start us, length us, event | category | flops | bytes accessed | tf_op | source)
XLA Modules:
  0.0 82.2 jit_solution(10627208351493018231)
XLA Ops:
  0.0 3.0 %shard_map.73 = (bf16[4,528,128]{2,1,0:T(8,128)(2,1)}, bf16[4,528,128]{2,1,0:T(8,128)(2,1)}) custom-call(bf16[256,512]{1,0:T(8,128)(2,1)} %d_ref.1, bf16[256,512]{1,0:T(8,128)(2,1)} %k_ref.1, bf16[256,512]{1,0:T(8,128)(2,1)} %q_ref.1, bf16[256,512]{1,0:T(8,128)(2,1)} %v_ref.1, f32[4,256]{1,0:T(4,128)} %rates_ref.1, s32[2,4]{1,0:T(2,128)} %selected_ref.1), custom_call_target="tpu_custom_call" | custom-call | flops 4194304 | bytes 2097152 | tf_op jit(solution)/shard_map/pallas_call | solution.py:382
  3.1 0.5 collective-permute-start
  3.6 1.8 %collective-permute-done.got = bf16[4,528,128]{2,1,0:T(8,128)(2,1)S(1)} collective-permute-done((bf16[4,528,128]{2,1,0:T(8,128)(2,1)}, bf16[4,528,128]{2,1,0:T(8,128)(2,1)S(1)}, u32[]{:S(2)}, u32[]{:S(2)}) %collective-permute-start) | collective-permute-done | bytes 540704 | tf_op jit(solution)/shard_map/ppermute | solution.py:374
  5.3 1.0 %copy-done.1 = bf16[4,528,128]{2,1,0:T(8,128)(2,1)S(1)} copy-done((bf16[4,528,128]{2,1,0:T(8,128)(2,1)S(1)}, bf16[4,528,128]{2,1,0:T(8,128)(2,1)}, u32[]{:S(2)}) %copy-start.1) | copy-done | bytes 540696
  6.4 1.1 %shard_map.74 = bf16[8,528,128]{2,1,0:T(8,128)(2,1)} custom-call(bf16[4,528,128]{2,1,0:T(8,128)(2,1)S(1)} %copy-done.1, bf16[4,528,128]{2,1,0:T(8,128)(2,1)S(1)} %collective-permute-done.got), custom_call_target="tpu_custom_call" | custom-call | flops 4194304 | bytes 2097152 | tf_op jit(solution)/shard_map/pallas_call | solution.py:395
  7.5 7.2 %all-to-all-start = ((bf16[8,528,128]{2,1,0:T(8,128)(2,1)}), bf16[8,528,128]{2,1,0:T(8,128)(2,1)S(1)}, u32[]{:S(2)}, u32[]{:S(2)}) async-start(bf16[8,528,128]{2,1,0:T(8,128)(2,1)} %shard_map.74), calls=%async_computation | async-start | bytes 2162688 | tf_op jit(solution)/shard_map/all_to_all | solution.py:371
  14.7 0.0 copy-done
  14.7 0.1 collective-permute-start.2
  14.8 26.7 %all-to-all-done.unit_ref = bf16[8,528,128]{2,1,0:T(8,128)(2,1)S(1)} async-done(((bf16[8,528,128]{2,1,0:T(8,128)(2,1)}), bf16[8,528,128]{2,1,0:T(8,128)(2,1)S(1)}, u32[]{:S(2)}, u32[]{:S(2)}) %all-to-all-start) | async-done | bytes 1081376 | tf_op jit(solution)/shard_map/all_to_all | solution.py:371
  41.4 7.7 %shard_map.75 = (bf16[8,2,128,128]{3,2,1,0:T(8,128)(2,1)S(1)}, f32[8,128,128]{2,1,0:T(8,128)S(1)}, bf16[8,4,128,128]{3,2,1,0:T(8,128)(2,1)S(1)}, s32[8,128]{1,0:T(8,128)S(1)}) custom-call(bf16[8,528,128]{2,1,0:T(8,128)(2,1)S(1)} %all-to-all-done.unit_ref), custom_call_target="tpu_custom_call" | custom-call | flops 1677721600 | bytes 2097152 | tf_op jit(solution)/shard_map/pallas_call | solution.py:406
  49.2 0.1 collective-permute-start.1
  49.3 2.6 %collective-permute-done.1.refs_4_ = bf16[8,4,128,128]{3,2,1,0:T(8,128)(2,1)S(1)} collective-permute-done((bf16[8,4,128,128]{3,2,1,0:T(8,128)(2,1)S(1)}, bf16[8,4,128,128]{3,2,1,0:T(8,128)(2,1)S(1)}, u32[]{:S(2)}, u32[]{:S(2)}) %collective-permute-start.1) | collective-permute-done | bytes 1048608 | tf_op jit(solution)/shard_map/ppermute | solution.py:374
  51.9 5.9 %shard_map.76 = bf16[8,128,128]{2,1,0:T(8,128)(2,1)} custom-call(s32[8,128]{1,0:T(8,128)S(1)} %get-tuple-element.13.refs_0_, bf16[8,2,128,128]{3,2,1,0:T(8,128)(2,1)S(1)} %get-tuple-element.14.refs_1_, f32[8,128,128]{2,1,0:T(8,128)S(1)} %get-tuple-element.15.refs_2_, bf16[8,4,128,128]{3,2,1,0:T(8,128)(2,1)S(1)} %get-tuple-element.16.refs_3_, ...), custom_call_target="tpu_custom_call" | custom-call | flops 1677721600 | bytes 2097152 | tf_op jit(solution)/shard_map/pallas_call | solution.py:424
  57.8 3.6 %all-to-all-start.1 = ((bf16[8,128,128]{2,1,0:T(8,128)(2,1)}), bf16[8,128,128]{2,1,0:T(8,128)(2,1)S(1)}, u32[]{:S(2)}, u32[]{:S(2)}) async-start(bf16[8,128,128]{2,1,0:T(8,128)(2,1)} %shard_map.76), calls=%async_computation.1 | async-start | bytes 524288 | tf_op jit(solution)/shard_map/all_to_all | solution.py:371
  61.5 0.0 collective-permute-done.2.other_ref
  61.5 9.5 %all-to-all-done.1.attended_ref = bf16[8,128,128]{2,1,0:T(8,128)(2,1)S(1)} async-done(((bf16[8,128,128]{2,1,0:T(8,128)(2,1)}), bf16[8,128,128]{2,1,0:T(8,128)(2,1)S(1)}, u32[]{:S(2)}, u32[]{:S(2)}) %all-to-all-start.1) | async-done | bytes 262176 | tf_op jit(solution)/shard_map/all_to_all | solution.py:371
  71.0 1.9 %shard_map.78 = bf16[128,1024]{1,0:T(8,128)(2,1)S(1)} custom-call(bf16[8,128,128]{2,1,0:T(8,128)(2,1)S(1)} %all-to-all-done.1.attended_ref, bf16[512,2048]{1,0:T(8,128)(2,1)S(1)} %copy-done, bf16[512,2048]{1,0:T(8,128)(2,1)} %collective-permute-done.2.other_ref), custom_call_target="tpu_custom_call" | custom-call | flops 268435456 | bytes 2097152 | tf_op jit(solution)/shard_map/pallas_call | solution.py:439
  72.9 1.6 %collective-permute-start.3 = (bf16[128,1024]{1,0:T(8,128)(2,1)S(1)}, bf16[128,1024]{1,0:T(8,128)(2,1)S(1)}, u32[]{:S(2)}, u32[]{:S(2)}) collective-permute-start(bf16[128,1024]{1,0:T(8,128)(2,1)S(1)} %shard_map.78), channel_id=1, source_target_pairs={{0,2},{1,3},{2,0},{3,1},{4,6},{5,7},{6,4},{7,5},{8,10},{9,11},{10,... | collective-permute-start | bytes 786440 | tf_op jit(solution)/shard_map/ppermute | solution.py:454
  74.5 1.9 %shard_map.77 = f32[128,1024]{1,0:T(8,128)S(1)} custom-call(bf16[8,128,128]{2,1,0:T(8,128)(2,1)S(1)} %all-to-all-done.1.attended_ref, bf16[512,2048]{1,0:T(8,128)(2,1)S(1)} %copy-done, bf16[512,2048]{1,0:T(8,128)(2,1)} %collective-permute-done.2.other_ref), custom_call_target="tpu_custom_call" | custom-call | flops 268435456 | bytes 2097152 | tf_op jit(solution)/shard_map/pallas_call | solution.py:439
  76.4 3.6 %collective-permute-done.3 = bf16[128,1024]{1,0:T(8,128)(2,1)S(1)} collective-permute-done((bf16[128,1024]{1,0:T(8,128)(2,1)S(1)}, bf16[128,1024]{1,0:T(8,128)(2,1)S(1)}, u32[]{:S(2)}, u32[]{:S(2)}) %collective-permute-start.3) | collective-permute-done | bytes 262176 | tf_op jit(solution)/shard_map/ppermute | solution.py:454
  80.0 0.1 add_convert_fusion
  80.1 0.1 collective-permute-start.4
  80.1 1.3 %collective-permute-done.4 = bf16[128,512]{1,0:T(8,128)(2,1)S(1)} collective-permute-done((bf16[128,512]{1,0:T(8,128)(2,1)S(1)}, bf16[128,512]{1,0:T(8,128)(2,1)S(1)}, u32[]{:S(2)}, u32[]{:S(2)}) %collective-permute-start.4) | collective-permute-done | bytes 131104 | tf_op jit(solution)/shard_map/ppermute | solution.py:374
  81.5 0.8 maximum_select_fusion
  (3 shorter events, 0.0 us)
Async XLA Ops:
  3.1 2.3 %collective-permute-start = (bf16[4,528,128]{2,1,0:T(8,128)(2,1)}, bf16[4,528,128]{2,1,0:T(8,128)(2,1)S(1)}, u32[]{:S(2)}, u32[]{:S(2)}) collective-permute-start(bf16[4,528,128]{2,1,0:T(8,128)(2,1)} %get-tuple-element.12), channel_id=1, source_target_pairs={{0,1},{1,0},{2,3},{3,2},{4,5},{5,4},{6,7},{7,6},{8,9},{9,8},{10,11... | collective-permute-start | bytes 1622024 | tf_op jit(solution)/shard_map/ppermute | solution.py:374
  5.3 1.0 %copy-start.1 = (bf16[4,528,128]{2,1,0:T(8,128)(2,1)S(1)}, bf16[4,528,128]{2,1,0:T(8,128)(2,1)}, u32[]{:S(2)}) copy-start(bf16[4,528,128]{2,1,0:T(8,128)(2,1)} %get-tuple-element.11.keep) | copy-start | bytes 1622020
  6.4 8.3 %copy-start = (bf16[512,2048]{1,0:T(8,128)(2,1)S(1)}, bf16[512,2048]{1,0:T(8,128)(2,1)}, u32[]{:S(2)}) copy-start(bf16[512,2048]{1,0:T(8,128)(2,1)} %own_ref.3) | copy-start | bytes 6291460
  7.5 34.0 %all-to-all-start = ((bf16[8,528,128]{2,1,0:T(8,128)(2,1)}), bf16[8,528,128]{2,1,0:T(8,128)(2,1)S(1)}, u32[]{:S(2)}, u32[]{:S(2)}) async-start(bf16[8,528,128]{2,1,0:T(8,128)(2,1)} %shard_map.74), calls=%async_computation | async-start | bytes 2162688 | tf_op jit(solution)/shard_map/all_to_all | solution.py:371
  14.7 46.8 %collective-permute-start.2 = (bf16[512,2048]{1,0:T(8,128)(2,1)S(1)}, bf16[512,2048]{1,0:T(8,128)(2,1)}, u32[]{:S(2)}, u32[]{:S(2)}) collective-permute-start(bf16[512,2048]{1,0:T(8,128)(2,1)S(1)} %copy-done), channel_id=1, source_target_pairs={{0,1},{1,0},{2,3},{3,2},{4,5},{5,4},{6,7},{7,6},{8,9},{9,8},{10,11... | collective-permute-start | bytes 6291464 | tf_op jit(solution)/shard_map/ppermute | solution.py:374
  49.2 2.7 %collective-permute-start.1 = (bf16[8,4,128,128]{3,2,1,0:T(8,128)(2,1)S(1)}, bf16[8,4,128,128]{3,2,1,0:T(8,128)(2,1)S(1)}, u32[]{:S(2)}, u32[]{:S(2)}) collective-permute-start(bf16[8,4,128,128]{3,2,1,0:T(8,128)(2,1)S(1)} %get-tuple-element.16.refs_3_), channel_id=1, source_target_pairs={{0,1},{1,0},{2,3},{3,2},{4,5},{5,4},{6,7},{7,6},{8,9},{9,8},{10,11... | collective-permute-start | bytes 3145736 | tf_op jit(solution)/shard_map/ppermute | solution.py:374
  57.8 13.2 %all-to-all-start.1 = ((bf16[8,128,128]{2,1,0:T(8,128)(2,1)}), bf16[8,128,128]{2,1,0:T(8,128)(2,1)S(1)}, u32[]{:S(2)}, u32[]{:S(2)}) async-start(bf16[8,128,128]{2,1,0:T(8,128)(2,1)} %shard_map.76), calls=%async_computation.1 | async-start | bytes 524288 | tf_op jit(solution)/shard_map/all_to_all | solution.py:371
  72.9 7.1 %collective-permute-start.3 = (bf16[128,1024]{1,0:T(8,128)(2,1)S(1)}, bf16[128,1024]{1,0:T(8,128)(2,1)S(1)}, u32[]{:S(2)}, u32[]{:S(2)}) collective-permute-start(bf16[128,1024]{1,0:T(8,128)(2,1)S(1)} %shard_map.78), channel_id=1, source_target_pairs={{0,2},{1,3},{2,0},{3,1},{4,6},{5,7},{6,4},{7,5},{8,10},{9,11},{10,... | collective-permute-start | bytes 786440 | tf_op jit(solution)/shard_map/ppermute | solution.py:454
  80.1 1.4 %collective-permute-start.4 = (bf16[128,512]{1,0:T(8,128)(2,1)S(1)}, bf16[128,512]{1,0:T(8,128)(2,1)S(1)}, u32[]{:S(2)}, u32[]{:S(2)}) collective-permute-start(bf16[128,512]{1,0:T(8,128)(2,1)S(1)} %get-tuple-element.18), channel_id=1, source_target_pairs={{0,1},{1,0},{2,3},{3,2},{4,5},{5,4},{6,7},{7,6},{8,9},{9,8},{10,11... | collective-permute-start | bytes 393224 | tf_op jit(solution)/shard_map/ppermute | solution.py:374

commit v5 on v1

v5 whole, which is shorter than its diff:
```python
import functools

import jax
import jax.numpy as jnp
from jax import lax
from jax.experimental import pallas as pl
from jax.experimental.pallas import tpu as pltpu
from jax.sharding import PartitionSpec as P

HEAD_DIM = 128
BLOCK = 128
LOOK = 7
TOPK = 4
BASE = 16
EXTRA = 16
TERMS = 3
BF16 = jnp.bfloat16
F32 = jnp.float32
VMEM = pl.BlockSpec(memory_space=pltpu.VMEM)
SMEM = pl.BlockSpec(memory_space=pltpu.SMEM)
ANY = pl.BlockSpec(memory_space=pl.ANY)


def dot(left, right, left_dim, right_dim):
    return lax.dot_general(
        left, right, (((left_dim,), (right_dim,)), ((), ())), preferred_element_type=F32
    )


def nn(left, right):
    return dot(left, right, 1, 0)


def nt(left, right):
    return dot(left, right, 1, 1)


def tn(left, right):
    return dot(left, right, 0, 0)


def split(value):
    high = value.astype(BF16)
    return high, (value - high.astype(F32)).astype(BF16)


def triple(product, left, right):
    rows = left[0].shape[0]
    first = product(jnp.concatenate(left, 0), right[0])
    return first[:rows] + (first[rows:] + product(left[0], right[1]))


def square_iotas():
    rows = lax.broadcasted_iota(jnp.int32, (BLOCK, BLOCK), 0)
    columns = lax.broadcasted_iota(jnp.int32, (BLOCK, BLOCK), 1)
    return rows, columns


def pack_kernel(axes, d_ref, k_ref, q_ref, v_ref, rates_ref, selected_ref, out_ref, parts_ref,
                sems, out_sems):
    tokens = d_ref.shape[0]
    heads = d_ref.shape[1] // HEAD_DIM
    blocks = tokens // BLOCK
    first_block = lax.axis_index(axes[0]) * blocks
    copies = []
    for head in range(heads):
        columns = pl.ds(head * HEAD_DIM, HEAD_DIM)
        for kind, source in enumerate((d_ref, k_ref, q_ref, v_ref)):
            copies.append(
                pltpu.make_async_copy(
                    source.at[:, columns],
                    parts_ref.at[head, pl.ds(kind * tokens, tokens)],
                    sems.at[head, kind],
                )
            )
            copies[-1].start()
    row = lax.broadcasted_iota(jnp.int32, (EXTRA, HEAD_DIM), 0)
    lane = lax.broadcasted_iota(jnp.int32, (EXTRA, HEAD_DIM), 1)
    away = jnp.zeros((EXTRA, HEAD_DIM), jnp.int32)
    for block in range(blocks):
        for entry in range(TOPK):
            distance = first_block + block - selected_ref[block, entry]
            away = jnp.where((row == TERMS * blocks + block) & (lane == entry), distance, away)
    away = away.astype(F32)
    terms = []
    rest = rates_ref[...]
    for _ in range(TERMS):
        terms.append(rest.astype(BF16).astype(F32))
        rest = rest - terms[-1]
    out_copies = []
    for head in range(heads):
        extra = away
        for block in range(blocks):
            for index, term in enumerate(terms):
                piece = term[head:head + 1, block * BLOCK:(block + 1) * BLOCK]
                extra = jnp.where(row == TERMS * block + index, piece, extra)
        parts_ref[head, 4 * tokens:] = extra.astype(BF16)
        for copy in copies[4 * head:4 * head + 4]:
            copy.wait()
        out_copies.append(
            pltpu.make_async_copy(parts_ref.at[head], out_ref.at[head], out_sems.at[head])
        )
        out_copies[-1].start()
    for copy in out_copies:
        copy.wait()


def rows_of(ref, blocks, unit, kind):
    start = (kind * blocks + unit % blocks) * BLOCK
    return ref[unit // blocks, start:start + BLOCK]


def base_inverse(strict):
    count = BLOCK // BASE
    moved = [
        pltpu.roll(strict[b * BASE:(b + 1) * BASE], (BLOCK - b * BASE) % BLOCK, 1)
        if b else strict[:BASE]
        for b in range(count)
    ]
    lanes = lax.broadcasted_iota(jnp.int32, (BASE // 2, BLOCK), 1)
    rows = lax.broadcasted_iota(jnp.int32, (BASE // 2, BLOCK), 0)
    half = BASE // 2
    parts = []
    for b in range(count):
        upper = (lanes == rows + b * BASE).astype(F32)
        lower = (lanes == rows + b * BASE + half).astype(F32)
        for step in range(BASE - 1):
            if step < half:
                source = upper[step:step + 1]
                if step < half - 1:
                    upper = upper - moved[b][:half, step:step + 1] * source
            else:
                source = lower[step - half:step - half + 1]
            lower = lower - moved[b][half:, step:step + 1] * source
        parts += [upper, lower]
    return jnp.concatenate(parts, 0)


def halves(value, size):
    parts = value.reshape(BLOCK // (2 * size), 2, size, BLOCK)
    return parts[:, 0].reshape(BLOCK // 2, BLOCK), parts[:, 1].reshape(BLOCK // 2, BLOCK)


def joined(first, second, size):
    shape = (BLOCK // (2 * size), 1, size, BLOCK)
    return jnp.concatenate([first.reshape(shape), second.reshape(shape)], 1).reshape(BLOCK, BLOCK)


def keys_kernel(blocks, part_ref, end_ref, tail_ref, far_ref, even_ref, pair_ref, group_ref,
                mixed_ref, away_ref):
    units = part_ref.shape[0] * blocks
    rows, columns = square_iotas()
    diagonal = rows == columns
    identity = diagonal.astype(F32)
    strict, inverse, scales = [], [], []
    for unit in range(units):
        direction = rows_of(part_ref, blocks, unit, 0)
        extra = part_ref[unit // blocks, 4 * blocks * BLOCK:].astype(F32)
        first = TERMS * (unit % blocks)
        rate = extra[first:first + 1] + extra[first + 1:first + 2] + extra[first + 2:first + 3]
        listed = TERMS * blocks + unit % blocks
        away_ref[unit:unit + 1] = extra[listed:listed + 1].astype(jnp.int32)
        gram = nt(direction, direction)
        squares = jnp.sum(jnp.where(diagonal, gram, 0.0), 0, keepdims=True)
        scale = lax.rsqrt(squares + 1e-06)
        scaled_rate = rate * scale
        scale_column = jnp.sum(jnp.where(diagonal, scale, 0.0), 1, keepdims=True)
        rate_column = jnp.sum(jnp.where(diagonal, scaled_rate, 0.0), 1, keepdims=True)
        strict.append(jnp.where(rows > columns, rate_column * gram * scale, 0.0))
        scales.append((scale_column, scaled_rate))
    for unit in range(units):
        inverse.append(base_inverse(strict[unit]))
    size = BASE
    while size < BLOCK:
        row = lax.broadcasted_iota(jnp.int32, (BLOCK // 2, BLOCK), 0)
        column = lax.broadcasted_iota(jnp.int32, (BLOCK // 2, BLOCK), 1)
        inside = (row // size == column // (2 * size)) & (lax.rem(column, 2 * size) < size)
        below = []
        for unit in range(units):
            corner = jnp.where(inside, halves(strict[unit], size)[1], 0.0)
            below.append(triple(nn, split(corner), split(inverse[unit])))
        for unit in range(units):
            first, second = halves(inverse[unit], size)
            padded = joined(jnp.zeros_like(below[unit]), below[unit], size)
            second = second - triple(nn, split(second), split(padded))
            inverse[unit] = joined(first, second, size)
        size *= 2
    ends, maps = [], []
    for unit in range(units):
        direction = rows_of(part_ref, blocks, unit, 0)
        key = rows_of(part_ref, blocks, unit, 1)
        key_proj = jnp.where(rows > columns, nt(direction, key), 0.0).astype(BF16)
        mixing = split(scales[unit][0] * inverse[unit] * scales[unit][1])
        mixed = nn(jnp.concatenate(mixing, 0), jnp.concatenate([direction, key_proj], 1))
        mixed = split(mixed[:BLOCK] + mixed[BLOCK:])
        mixed_ref[unit] = mixed[0]
        behind = tn(jnp.concatenate([mixed[0], mixed[1][:, :BLOCK]], 1), direction)
        ends.append(key.astype(F32) - behind[BLOCK:2 * BLOCK])
        maps.append(split(identity - (behind[:BLOCK] + behind[2 * BLOCK:])))
        end_ref[unit] = ends[unit].astype(BF16)
    pair_keys, pair_maps = [], []
    for pair in range(units // 2):
        even, odd = 2 * pair, 2 * pair + 1
        even_ref[pair, 0] = maps[even][0]
        even_ref[pair, 1] = maps[even][1]
        end = split(ends[even])
        left = tuple(jnp.concatenate([end[part], maps[even][part]], 0) for part in range(2))
        both = triple(nn, left, maps[odd])
        tail_ref[even] = both[:BLOCK].astype(BF16)
        tail_ref[odd] = ends[odd].astype(BF16)
        pair_keys.append(jnp.concatenate([both[:BLOCK], ends[odd]], 0))
        pair_maps.append(split(both[BLOCK:]))
        pair_ref[pair, 0] = pair_maps[pair][0]
        pair_ref[pair, 1] = pair_maps[pair][1]
    onward = None
    for pair in reversed(range(units // 2)):
        far = pair_keys[pair]
        if onward is None:
            onward = pair_maps[pair]
        else:
            far = triple(nn, split(far), onward)
            onward = split(triple(nn, pair_maps[pair], onward))
        far_ref[2 * pair] = far[:BLOCK].astype(BF16)
        far_ref[2 * pair + 1] = far[BLOCK:].astype(BF16)
    group_ref[0] = onward[0]
    group_ref[1] = onward[1]


def queries_kernel(blocks, part_ref, mixed_ref, even_ref, pair_ref, *refs):
    inner_ref, moving_ref = refs[-2:]
    units = part_ref.shape[0] * blocks
    rows, columns = square_iotas()
    current = []
    for unit in range(units):
        direction = rows_of(part_ref, blocks, unit, 0)
        key = rows_of(part_ref, blocks, unit, 1)
        query = rows_of(part_ref, blocks, unit, 2)
        query_proj = split(jnp.where(rows >= columns, nt(query, direction), 0.0))
        ahead = nn(jnp.concatenate(query_proj, 0), mixed_ref[unit])
        ahead = ahead[:BLOCK] + ahead[BLOCK:]
        inner_ref[unit] = nt(query, key) - ahead[:, HEAD_DIM:]
        start = split(query.astype(F32) - ahead[:, :HEAD_DIM])
        moving_ref[unit, 0] = start[0]
        if unit % 2:
            pair = unit // 2
            start = split(triple(nt, start, (even_ref[pair, 0], even_ref[pair, 1])))
        moving_ref[unit, 1] = start[0]
        current.append(start)
    pairs = units // 2
    current = [
        tuple(jnp.concatenate([current[2 * pair][part], current[2 * pair + 1][part]], 0)
              for part in range(2))
        for pair in range(pairs)
    ]
    for step in range(2, pairs + 1):
        for pair in range(step - 1, pairs):
            passed = pair - step + 1
            current[pair] = split(
                triple(nt, current[pair], (pair_ref[passed, 0], pair_ref[passed, 1]))
            )
            moving_ref[2 * pair, step] = current[pair][0][:BLOCK]
            moving_ref[2 * pair + 1, step] = current[pair][0][BLOCK:]


def attend_kernel(before, away_ref, moving_ref, inner_ref, end_ref, tail_ref, *refs):
    values, far_keys = refs[:before + 1], refs[before + 1:2 * before + 1]
    group_maps = refs[2 * before + 1:3 * before]
    out_ref = refs[max(3 * before, 1)]
    units = inner_ref.shape[0]
    rows, columns = square_iotas()
    scale = HEAD_DIM ** (-0.5)
    for unit in range(units):
        pair = unit // 2
        fronts = [moving_ref[unit, pair + 1]]
        for group_map in group_maps:
            passed = nt(fronts[-1], group_map[0]) + nt(fronts[-1], group_map[1])
            fronts.append(passed.astype(BF16))
        score_list = [jnp.where(rows >= columns, inner_ref[unit] * scale, -1e30)]
        value_list = [values[0][unit]]
        for entry in range(1, TOPK):
            away = away_ref[unit, entry]
            new = away > 0
            for other in range(1, entry):
                new = new & (away_ref[unit, other] != away)
            source = unit - away
            inside = jnp.maximum(source, 0)
            step = jnp.maximum(pair - inside // 2, 0)
            query = moving_ref[unit, step]
            key = jnp.where(step == 0, end_ref[inside], tail_ref[inside])
            value = values[0][inside]
            for ahead in range(1, before + 1):
                here = source < (1 - ahead) * units
                place = jnp.clip(source + ahead * units, 0, units - 1)
                query = jnp.where(here, fronts[ahead - 1], query)
                key = jnp.where(here, far_keys[ahead - 1][place], key)
                value = jnp.where(here, values[ahead][place], value)
            score_list.append(jnp.where(new, nt(query, key) * scale, -1e30))
            value_list.append(value)
        scores = jnp.concatenate(score_list, 1)
        expos = jnp.exp(scores - jnp.max(scores, 1, keepdims=True))
        weights = (expos / jnp.sum(expos, 1, keepdims=True)).astype(BF16)
        out_ref[unit] = nn(weights, jnp.concatenate(value_list, 0)).astype(BF16)


def project_kernel(axes, other, blocks, attended_ref, weight_ref, out_ref):
    planes, _, width = out_ref.shape
    cores = weight_ref.shape[1] // (planes * width)
    core = lax.rem(lax.axis_index(axes[1]) + other, cores)
    heads = attended_ref.shape[0] // blocks
    attended = jnp.concatenate(
        [
            jnp.concatenate([attended_ref[head * blocks + block] for head in range(heads)], 1)
            for block in range(blocks)
        ],
        0,
    )
    for plane in range(planes):
        start = pl.multiple_of((plane * cores + core) * width, width)
        total = nn(attended, weight_ref[:, pl.ds(start, width)])
        out_ref[plane] = total.astype(out_ref.dtype)


def call(kernel, outs, specs, flops, scratch=(), places=None, space=32):
    if places is None:
        places = [VMEM] * len(outs) if isinstance(outs, list) else VMEM
    return pl.pallas_call(
        kernel,
        out_shape=outs,
        in_specs=specs,
        out_specs=places,
        scratch_shapes=list(scratch),
        compiler_params=pltpu.CompilerParams(vmem_limit_bytes=space * 2 ** 20),
        cost_estimate=pl.CostEstimate(flops=flops, bytes_accessed=2 ** 21, transcendentals=0),
    )


def body(ctx_size, head_size, queries, keys, values, directions, rates, selected, out_weight):
    tokens = queries.shape[0]
    blocks = tokens // BLOCK
    heads = queries.shape[1] // HEAD_DIM
    units = heads * blocks
    pairs = units // 2
    groups = ctx_size // heads
    before = min(groups - 1, -(-LOOK // heads))
    cores = 2
    planes = head_size // cores
    axes = ("ctx", "head")
    members = [[group * heads + place for place in range(heads)] for group in range(groups)]
    partners = [(g, g + 1 - 2 * (g % cores)) for g in range(head_size)]
    cubes = 2 * BLOCK ** 3
    tile = (BLOCK, HEAD_DIM)

    def exchange(value):
        return lax.all_to_all(value, "ctx", 0, 0, axis_index_groups=members, tiled=True)

    def onward(value, by):
        shift = by * heads
        return lax.ppermute(value, "ctx", [(i, i + shift) for i in range(ctx_size - shift)])

    def array(shape, kind=BF16):
        return jax.ShapeDtypeStruct(shape, kind)

    part_shape = (heads, 4 * tokens + EXTRA, HEAD_DIM)
    packed = call(
        functools.partial(pack_kernel, axes),
        array(part_shape),
        [ANY] * 4 + [VMEM, SMEM],
        cubes,
        [
            pltpu.VMEM(part_shape, BF16),
            pltpu.SemaphoreType.DMA((heads, 4)),
            pltpu.SemaphoreType.DMA((heads,)),
        ],
        ANY,
        56,
    )(directions, keys, queries, values, rates, selected)
    parts = exchange(packed)
    own_values = parts[:, 3 * tokens:4 * tokens].reshape(units, *tile)
    value_parts = [own_values] + [onward(own_values, by) for by in range(1, before + 1)]

    end, tail, far, even, pair_map, group_map, mixed, away = call(
        functools.partial(keys_kernel, blocks),
        [
            array((units, *tile)),
            array((units, *tile)),
            array((units, *tile)),
            array((pairs, 2, *tile)),
            array((pairs, 2, *tile)),
            array((2, *tile)),
            array((units, BLOCK, 2 * BLOCK)),
            array((units, HEAD_DIM), jnp.int32),
        ],
        [VMEM],
        400 * cubes,
    )(parts)
    far_parts = [onward(far, by) for by in range(1, before + 1)]
    map_parts = [onward(group_map, by) for by in range(1, before)]
    inner, moving = call(
        functools.partial(queries_kernel, blocks),
        [array((units, BLOCK, BLOCK), F32), array((units, pairs + 1, *tile))],
        [VMEM] * 4 + [ANY] * before,
        200 * cubes,
    )(parts, mixed, even, pair_map, *value_parts[1:])
    attended = call(
        functools.partial(attend_kernel, before),
        array((units, *tile)),
        [SMEM] + [VMEM] * (4 + max(3 * before, 1)),
        200 * cubes,
    )(away, moving, inner, end, tail, *value_parts, *far_parts, *map_parts)

    local = exchange(attended)
    width = out_weight.shape[1] // head_size

    def projected(other, kind):
        return call(
            functools.partial(project_kernel, axes, other, blocks),
            array((planes, tokens, width), kind),
            [VMEM] * 2,
            128 * cubes,
        )(local, out_weight)

    arrived = lax.ppermute(projected(1, BF16), "head", partners)
    total = projected(0, F32) + arrived.astype(F32)
    plane = lax.axis_index("head") // cores
    result = lax.dynamic_index_in_dim(total, plane, 0, False)
    for offset in range(1, planes):
        part = lax.dynamic_index_in_dim(total, lax.rem(plane + offset, planes), 0, False)
        turned = [(g, (g + cores * offset) % head_size) for g in range(head_size)]
        result = result + lax.ppermute(part.astype(BF16), "head", turned).astype(F32)
    return result.astype(BF16)


def solution(mesh):
    in_specs = (
        P("ctx", "head"),
        P("ctx", "head"),
        P("ctx", "head"),
        P("ctx", "head"),
        P("head", "ctx"),
        P("ctx", None),
        P("head", None),
    )
    out_specs = P("ctx", "head")
    return jax.shard_map(
        functools.partial(body, mesh.shape["ctx"], mesh.shape["head"]),
        mesh=mesh,
        in_specs=in_specs,
        out_specs=out_specs,
        check_vma=False,
    )
```

time: 91.3 us -> 72.1 us (0.79)
  blocking collectives: 0 us -> 34.2 us
  waiting for transfers between devices: 39.5 us -> 10.3 us
  starting transfers between devices: 17.4 us -> 7.42 us
  local copies, waits for them, and re-layouts: 7.05 us -> 0.06 us
  Pallas kernels: 22.8 us -> 18.7 us
  other arithmetic: 3.69 us -> 0.94 us
    all_to_all x0 -> x2, blocking collectives: none -> 34.2 us  [exchange(): lax.all_to_all(value, 'ctx', 0, 0, axis_index_groups=members, tiled=True)]
    all_to_all x3 -> x0, waiting for transfers between devices: 31.7 us -> none  [exchange(): lax.all_to_all(value, 'ctx', 0, 0, axis_index_groups=members, tiled=True)]
    all_to_all x3 -> x0, starting transfers between devices: 14.5 us -> none  [exchange(): lax.all_to_all(value, 'ctx', 0, 0, axis_index_groups=members, tiled=True)]
    unnamed x18 -> x2, local copies, waits for them, and re-layouts: 7 us -> 0.01 us
    ppermute x7 -> x4, starting transfers between devices: 2.84 us -> 7.42 us  [the longest x2 5.8 us: onward(): lax.ppermute(value, 'ctx', [(i, i + shift) for i in range(ctx_size - shif...]
    pallas_call x6, Pallas kernels: 22.8 us -> 18.7 us  [the longest x1 8.94 us: body(): call(functools.partial(keys_kernel, blocks), [array((units, *tile)), arra...]
    select_n x3 -> x0, other arithmetic: 3.63 us -> none  [ordered(): jnp.where(core == 0, jnp.concatenate([own, other], 0), jnp.concatenate([o...]
    ppermute x7 -> x4, waiting for transfers between devices: 7.83 us -> 10.3 us  [the longest x1 6.87 us: body(): lax.ppermute(part.astype(BF16), 'head', turned).astype(F32)]
  transfers between devices with their start and end apart: 10 -> 4, of which waited for: 7 -> 3; matrix products, arithmetic and copies ran while one was open for 3% -> 0% of each run, Pallas kernels for 21% -> 16%
where the time goes in v5:
time: 72.1 us; the launch traced here: 71.7 us
  blocking collectives  34.2 us (47%)
  Pallas kernels  18.7 us (26%)
  waiting for transfers between devices  10.3 us (14%)
  starting transfers between devices  7.42 us (10%)
  other arithmetic  0.94 us (1%)
    all_to_all x2, blocking collectives, exchange(): lax.all_to_all(value, 'ctx', 0, 0, axis_index_groups=members, tiled=True)  34.2 us
    pallas_call x1, Pallas kernels, body(): call(functools.partial(keys_kernel, blocks), [array((units, *tile)), arra...  8.94 us
    ppermute x1, waiting for transfers between devices, body(): lax.ppermute(part.astype(BF16), 'head', turned).astype(F32)  6.87 us
    ppermute x2, starting transfers between devices, onward(): lax.ppermute(value, 'ctx', [(i, i + shift) for i in range(ctx_size - shif...  5.8 us
    pallas_call x1, Pallas kernels, body(): call(functools.partial(attend_kernel, before), array((units, *tile)), [SM...  3.88 us
    pallas_call x1, Pallas kernels, body(): call(functools.partial(pack_kernel, axes), array(part_shape), [ANY] * 4 +...  2.96 us
    pallas_call x1, Pallas kernels, body(): call(functools.partial(queries_kernel, blocks), [array((units, BLOCK, BLO...  2.02 us
    ppermute x2, waiting for transfers between devices, onward(): lax.ppermute(value, 'ctx', [(i, i + shift) for i in range(ctx_size - shif...  2.01 us
  transfers between devices with their start and end apart: 4, of which 3 were waited for; matrix products, arithmetic and copies ran while one was open for 0% of the time, Pallas kernels for 16%

profile of v5, /device:TPU:0, one launch (start us, length us, event | category | flops | bytes accessed | tf_op | source)
XLA Modules:
  0.0 71.7 jit_solution(2957559963137313109)
XLA Ops:
  0.0 3.0 %shard_map.73 = bf16[4,1040,128]{2,1,0:T(8,128)(2,1)} custom-call(bf16[256,512]{1,0:T(8,128)(2,1)} %d_ref.1, bf16[256,512]{1,0:T(8,128)(2,1)} %k_ref.1, bf16[256,512]{1,0:T(8,128)(2,1)} %q_ref.1, bf16[256,512]{1,0:T(8,128)(2,1)} %v_ref.1, f32[4,256]{1,0:T(4,128)} %rates_ref.1, s32[2,4]{1,0:T(2,128)} %selected_ref.1), custom_call_target="tpu_custom_call" | custom-call | flops 4194304 | bytes 2097152 | tf_op jit(solution)/shard_map/pallas_call | solution.py:364
  3.0 19.9 %all_to_all.10.part_ref = bf16[4,1040,128]{2,1,0:T(8,128)(2,1)S(1)} all-to-all(bf16[4,1040,128]{2,1,0:T(8,128)(2,1)} %shard_map.73), channel_id=1, replica_groups={{0,4,8,12},{16,20,24,28},{1,5,9,13},{17,21,25,29},{2,6,10,14},{18,22,26..., dimensions={0} | all-to-all | bytes 2129920 | tf_op jit(solution)/shard_map/all_to_all | solution.py:354
  22.9 4.5 %collective-permute-start = (bf16[8,128,128]{2,1,0:T(8,128)(2,1)S(1)}, bf16[8,128,128]{2,1,0:T(8,128)(2,1)S(1)}, u32[]{:S(2)}, u32[]{:S(2)}) collective-permute-start(bf16[8,128,128]{2,1,0:T(8,128)(2,1)S(1)} %bitcast.7), channel_id=1, source_target_pairs={{0,16},{4,20},{8,24},{12,28},{1,17},{5,21},{9,25},{13,29},{2,18},{... | collective-permute-start | bytes 786440 | tf_op jit(solution)/shard_map/ppermute | solution.py:358
  27.4 8.9 %shard_map.74 = (bf16[8,128,128]{2,1,0:T(8,128)(2,1)S(1)}, bf16[8,128,128]{2,1,0:T(8,128)(2,1)S(1)}, bf16[8,128,128]{2,1,0:T(8,128)(2,1)S(1)}, bf16[4,2,128,128]...) custom-call(bf16[4,1040,128]{2,1,0:T(8,128)(2,1)S(1)} %all_to_all.10, ...), custom_call_target="tpu_custom_call" | custom-call | flops 1677721600 | bytes 2097152 | tf_op jit(solution)/shard_map/pallas_call | solution.py:381
  36.3 1.3 %collective-permute-start.1 = (bf16[8,128,128]{2,1,0:T(8,128)(2,1)S(1)}, bf16[8,128,128]{2,1,0:T(8,128)(2,1)S(1)}, u32[]{:S(2)}, u32[]{:S(2)}) collective-permute-start(bf16[8,128,128]{2,1,0:T(8,128)(2,1)S(1)} %get-tuple-element.22), channel_id=1, source_target_pairs={{0,16},{4,20},{8,24},{12,28},{1,17},{5,21},{9,25},{13,29},{2,18},{... | collective-permute-start | bytes 786440 | tf_op jit(solution)/shard_map/ppermute | solution.py:358
  37.6 0.0 collective-permute-done.refs_0_.refs_1_
  37.6 2.0 %shard_map.75 = (f32[8,128,128]{2,1,0:T(8,128)S(1)}, bf16[8,5,128,128]{3,2,1,0:T(8,128)(2,1)S(1)}) custom-call(bf16[4,1040,128]{2,1,0:T(8,128)(2,1)S(1)} %all_to_all.10.part_ref, bf16[8,128,256]{2,1,0:T(8,128)(2,1)S(1)} %get-tuple-element.15.mixed_ref, bf16[4,2,128,128]{3,2,1,0:T(8,128)(2,1)S(1)} %get-tuple-element.16.even_ref, ...), custom_call_target="tpu_custom_call" | custom-call | flops 838860800 | bytes 2097152 | tf_op jit(solution)/shard_map/pallas_call | solution.py:398
  39.7 2.0 %collective-permute-done.1.refs_2_ = bf16[8,128,128]{2,1,0:T(8,128)(2,1)S(1)} collective-permute-done((bf16[8,128,128]{2,1,0:T(8,128)(2,1)S(1)}, bf16[8,128,128]{2,1,0:T(8,128)(2,1)S(1)}, u32[]{:S(2)}, u32[]{:S(2)}) %collective-permute-start.1) | collective-permute-done | bytes 262176 | tf_op jit(solution)/shard_map/ppermute | solution.py:358
  41.7 0.0 copy-start
  41.7 3.9 %shard_map.76 = bf16[8,128,128]{2,1,0:T(8,128)(2,1)S(1)} custom-call(s32[8,128]{1,0:T(8,128)S(1)} %get-tuple-element.14.away_ref, bf16[8,5,128,128]{3,2,1,0:T(8,128)(2,1)S(1)} %get-tuple-element.18.moving_ref, f32[8,128,128]{2,1,0:T(8,128)S(1)} %get-tuple-element.19.inner_ref, bf16[8,128,128]{2,1,0:T(8,128)(2,1)S(1)} %get-tuple-element.20.end_ref, ...), custom_call_target="tpu_custom_call" | custom-call | flops 838860800 | bytes 2097152 | tf_op jit(solution)/shard_map/pallas_call | solution.py:404
  45.6 14.3 %all_to_all.11.attended_ref = bf16[8,128,128]{2,1,0:T(8,128)(2,1)S(1)} all-to-all(bf16[8,128,128]{2,1,0:T(8,128)(2,1)S(1)} %shard_map.76), channel_id=1, replica_groups={{0,4,8,12},{16,20,24,28},{1,5,9,13},{17,21,25,29},{2,6,10,14},{18,22,26..., dimensions={0} | all-to-all | bytes 524288 | tf_op jit(solution)/shard_map/all_to_all | solution.py:354
  59.9 0.0 copy-done
  59.9 0.5 shard_map.78
  60.4 0.1 collective-permute-start.2
  60.5 0.4 shard_map.77
  60.9 1.4 %collective-permute-done.2 = bf16[2,256,512]{2,1,0:T(8,128)(2,1)S(1)} collective-permute-done((bf16[2,256,512]{2,1,0:T(8,128)(2,1)S(1)}, bf16[2,256,512]{2,1,0:T(8,128)(2,1)S(1)}, u32[]{:S(2)}, u32[]{:S(2)}) %collective-permute-start.2) | collective-permute-done | bytes 524320 | tf_op jit(solution)/shard_map/ppermute | solution.py:422
  62.3 0.2 convert_add_fusion
  62.6 1.5 %collective-permute-start.3 = (bf16[256,512]{1,0:T(8,128)(2,1)S(1)}, bf16[256,512]{1,0:T(8,128)(2,1)S(1)}, u32[]{:S(2)}, u32[]{:S(2)}) collective-permute-start(bf16[256,512]{1,0:T(8,128)(2,1)S(1)} %fusion.1), channel_id=1, source_target_pairs={{0,2},{1,3},{2,0},{3,1},{4,6},{5,7},{6,4},{7,5},{8,10},{9,11},{10,... | collective-permute-start | bytes 786440 | tf_op jit(solution)/shard_map/ppermute | solution.py:429
  64.1 6.9 %collective-permute-done.3 = bf16[256,512]{1,0:T(8,128)(2,1)S(1)} collective-permute-done((bf16[256,512]{1,0:T(8,128)(2,1)S(1)}, bf16[256,512]{1,0:T(8,128)(2,1)S(1)}, u32[]{:S(2)}, u32[]{:S(2)}) %collective-permute-start.3) | collective-permute-done | bytes 262176 | tf_op jit(solution)/shard_map/ppermute | solution.py:429
  71.0 0.8 %fusion = bf16[256,512]{1,0:T(8,128)(2,1)} fusion(bf16[256,512]{1,0:T(8,128)(2,1)S(1)} %collective-permute-done.3, f32[2,256,512]{2,1,0:T(8,128)S(1)} %convert_add_fusion, s32[]{:T(128)S(6)} %select_n.13), kind=kLoop, calls=%fused_computation.2 | loop fusion | flops 393216 | bytes 1048580 | tf_op jit(solution)/shard_map/convert_element_type | solution.py:430
  (2 shorter events, 0.1 us)
Async XLA Ops:
  22.9 14.8 %collective-permute-start = (bf16[8,128,128]{2,1,0:T(8,128)(2,1)S(1)}, bf16[8,128,128]{2,1,0:T(8,128)(2,1)S(1)}, u32[]{:S(2)}, u32[]{:S(2)}) collective-permute-start(bf16[8,128,128]{2,1,0:T(8,128)(2,1)S(1)} %bitcast.7), channel_id=1, source_target_pairs={{0,16},{4,20},{8,24},{12,28},{1,17},{5,21},{9,25},{13,29},{2,18},{... | collective-permute-start | bytes 786440 | tf_op jit(solution)/shard_map/ppermute | solution.py:358
  36.3 5.3 %collective-permute-start.1 = (bf16[8,128,128]{2,1,0:T(8,128)(2,1)S(1)}, bf16[8,128,128]{2,1,0:T(8,128)(2,1)S(1)}, u32[]{:S(2)}, u32[]{:S(2)}) collective-permute-start(bf16[8,128,128]{2,1,0:T(8,128)(2,1)S(1)} %get-tuple-element.22), channel_id=1, source_target_pairs={{0,16},{4,20},{8,24},{12,28},{1,17},{5,21},{9,25},{13,29},{2,18},{... | collective-permute-start | bytes 786440 | tf_op jit(solution)/shard_map/ppermute | solution.py:358
  41.7 18.2 %copy-start = (bf16[512,2048]{1,0:T(8,128)(2,1)S(1)}, bf16[512,2048]{1,0:T(8,128)(2,1)}, u32[]{:S(2)}) copy-start(bf16[512,2048]{1,0:T(8,128)(2,1)} %weight_ref.3) | copy-start | bytes 6291460
  60.4 2.0 %collective-permute-start.2 = (bf16[2,256,512]{2,1,0:T(8,128)(2,1)S(1)}, bf16[2,256,512]{2,1,0:T(8,128)(2,1)S(1)}, u32[]{:S(2)}, u32[]{:S(2)}) collective-permute-start(bf16[2,256,512]{2,1,0:T(8,128)(2,1)S(1)} %shard_map.78), channel_id=1, source_target_pairs={{0,1},{1,0},{2,3},{3,2},{4,5},{5,4},{6,7},{7,6},{8,9},{9,8},{10,11... | collective-permute-start | bytes 1572872 | tf_op jit(solution)/shard_map/ppermute | solution.py:422
  62.6 8.4 %collective-permute-start.3 = (bf16[256,512]{1,0:T(8,128)(2,1)S(1)}, bf16[256,512]{1,0:T(8,128)(2,1)S(1)}, u32[]{:S(2)}, u32[]{:S(2)}) collective-permute-start(bf16[256,512]{1,0:T(8,128)(2,1)S(1)} %fusion.1), channel_id=1, source_target_pairs={{0,2},{1,3},{2,0},{3,1},{4,6},{5,7},{6,4},{7,5},{8,10},{9,11},{10,... | collective-permute-start | bytes 786440 | tf_op jit(solution)/shard_map/ppermute | solution.py:429

commit v6 on v5

--- a/solution.py
+++ b/solution.py
@@ -146,58 +146,71 @@
     return jnp.concatenate([first.reshape(shape), second.reshape(shape)], 1).reshape(BLOCK, BLOCK)
 
 
+def interleaved(steps, lag):
+    running = list(steps)
+    tick = 0
+    while any(step is not None for step in running):
+        for index, step in enumerate(running):
+            if step is not None and tick >= index * lag:
+                try:
+                    next(step)
+                except StopIteration:
+                    running[index] = None
+        tick += 1
+
+
 def keys_kernel(blocks, part_ref, end_ref, tail_ref, far_ref, even_ref, pair_ref, group_ref,
                 mixed_ref, away_ref):
     units = part_ref.shape[0] * blocks
     rows, columns = square_iotas()
     diagonal = rows == columns
     identity = diagonal.astype(F32)
-    strict, inverse, scales = [], [], []
-    for unit in range(units):
+    row = lax.broadcasted_iota(jnp.int32, (BLOCK // 2, BLOCK), 0)
+    column = lax.broadcasted_iota(jnp.int32, (BLOCK // 2, BLOCK), 1)
+    ends, maps = [None] * units, [None] * units
+
+    def terms(unit):
         direction = rows_of(part_ref, blocks, unit, 0)
+        key = rows_of(part_ref, blocks, unit, 1)
         extra = part_ref[unit // blocks, 4 * blocks * BLOCK:].astype(F32)
         first = TERMS * (unit % blocks)
         rate = extra[first:first + 1] + extra[first + 1:first + 2] + extra[first + 2:first + 3]
         listed = TERMS * blocks + unit % blocks
         away_ref[unit:unit + 1] = extra[listed:listed + 1].astype(jnp.int32)
         gram = nt(direction, direction)
+        key_proj = jnp.where(rows > columns, nt(direction, key), 0.0).astype(BF16)
         squares = jnp.sum(jnp.where(diagonal, gram, 0.0), 0, keepdims=True)
         scale = lax.rsqrt(squares + 1e-06)
         scaled_rate = rate * scale
         scale_column = jnp.sum(jnp.where(diagonal, scale, 0.0), 1, keepdims=True)
         rate_column = jnp.sum(jnp.where(diagonal, scaled_rate, 0.0), 1, keepdims=True)
-        strict.append(jnp.where(rows > columns, rate_column * gram * scale, 0.0))
-        scales.append((scale_column, scaled_rate))
-    for unit in range(units):
-        inverse.append(base_inverse(strict[unit]))
-    size = BASE
-    while size < BLOCK:
-        row = lax.broadcasted_iota(jnp.int32, (BLOCK // 2, BLOCK), 0)
-        column = lax.broadcasted_iota(jnp.int32, (BLOCK // 2, BLOCK), 1)
-        inside = (row // size == column // (2 * size)) & (lax.rem(column, 2 * size) < size)
-        below = []
-        for unit in range(units):
-            corner = jnp.where(inside, halves(strict[unit], size)[1], 0.0)
-            below.append(triple(nn, split(corner), split(inverse[unit])))
-        for unit in range(units):
-            first, second = halves(inverse[unit], size)
-            padded = joined(jnp.zeros_like(below[unit]), below[unit], size)
+        strict = jnp.where(rows > columns, rate_column * gram * scale, 0.0)
+        yield
+        inverse = base_inverse(strict)
+        yield
+        size = BASE
+        while size < BLOCK:
+            inside = (row // size == column // (2 * size)) & (lax.rem(column, 2 * size) < size)
+            corner = jnp.where(inside, halves(strict, size)[1], 0.0)
+            below = triple(nn, split(corner), split(inverse))
+            yield
+            first_half, second = halves(inverse, size)
+            padded = joined(jnp.zeros_like(below), below, size)
             second = second - triple(nn, split(second), split(padded))
-            inverse[unit] = joined(first, second, size)
-        size *= 2
-    ends, maps = [], []
-    for unit in range(units):
-        direction = rows_of(part_ref, blocks, unit, 0)
-        key = rows_of(part_ref, blocks, unit, 1)
-        key_proj = jnp.where(rows > columns, nt(direction, key), 0.0).astype(BF16)
-        mixing = split(scales[unit][0] * inverse[unit] * scales[unit][1])
+            inverse = joined(first_half, second, size)
+            size *= 2
+            yield
+        mixing = split(scale_column * inverse * scaled_rate)
         mixed = nn(jnp.concatenate(mixing, 0), jnp.concatenate([direction, key_proj], 1))
         mixed = split(mixed[:BLOCK] + mixed[BLOCK:])
         mixed_ref[unit] = mixed[0]
+        yield
         behind = tn(jnp.concatenate([mixed[0], mixed[1][:, :BLOCK]], 1), direction)
-        ends.append(key.astype(F32) - behind[BLOCK:2 * BLOCK])
-        maps.append(split(identity - (behind[:BLOCK] + behind[2 * BLOCK:])))
+        ends[unit] = key.astype(F32) - behind[BLOCK:2 * BLOCK]
+        maps[unit] = split(identity - (behind[:BLOCK] + behind[2 * BLOCK:]))
         end_ref[unit] = ends[unit].astype(BF16)
+
+    interleaved([terms(unit) for unit in range(units)], 1)
     pair_keys, pair_maps = [], []
     for pair in range(units // 2):
         even, odd = 2 * pair, 2 * pair + 1
@@ -227,8 +240,10 @@
 
 
 def queries_kernel(blocks, part_ref, mixed_ref, even_ref, pair_ref, *refs):
-    inner_ref, moving_ref = refs[-2:]
+    inner_ref, moving_ref, late_ref = refs[-3:]
     units = part_ref.shape[0] * blocks
+    for unit in range(units // 2, units):
+        late_ref[unit - units // 2] = rows_of(part_ref, blocks, unit, 3)
     rows, columns = square_iotas()
     current = []
     for unit in range(units):
@@ -262,10 +277,21 @@
             moving_ref[2 * pair + 1, step] = current[pair][0][BLOCK:]
 
 
-def attend_kernel(before, away_ref, moving_ref, inner_ref, end_ref, tail_ref, *refs):
-    values, far_keys = refs[:before + 1], refs[before + 1:2 * before + 1]
-    group_maps = refs[2 * before + 1:3 * before]
-    out_ref = refs[max(3 * before, 1)]
+def listed_block(away_ref, unit, entry):
+    away = away_ref[unit, entry]
+    new = away > 0
+    for other in range(1, entry):
+        new = new & (away_ref[unit, other] != away)
+    return unit - away, new
+
+
+def earlier(source, ahead, units):
+    return jnp.clip(source + ahead * units, 0, units - 1), source < (1 - ahead) * units
+
+
+def weights_kernel(before, away_ref, moving_ref, inner_ref, end_ref, tail_ref, *refs):
+    far_keys, group_maps = refs[:before], refs[before:-1]
+    weights_ref = refs[-1]
     units = inner_ref.shape[0]
     rows, columns = square_iotas()
     scale = HEAD_DIM ** (-0.5)
@@ -276,48 +302,72 @@
             passed = nt(fronts[-1], group_map[0]) + nt(fronts[-1], group_map[1])
             fronts.append(passed.astype(BF16))
         score_list = [jnp.where(rows >= columns, inner_ref[unit] * scale, -1e30)]
-        value_list = [values[0][unit]]
         for entry in range(1, TOPK):
-            away = away_ref[unit, entry]
-            new = away > 0
-            for other in range(1, entry):
-                new = new & (away_ref[unit, other] != away)
-            source = unit - away
+            source, new = listed_block(away_ref, unit, entry)
             inside = jnp.maximum(source, 0)
             step = jnp.maximum(pair - inside // 2, 0)
             query = moving_ref[unit, step]
             key = jnp.where(step == 0, end_ref[inside], tail_ref[inside])
-            value = values[0][inside]
             for ahead in range(1, before + 1):
-                here = source < (1 - ahead) * units
-                place = jnp.clip(source + ahead * units, 0, units - 1)
+                place, here = earlier(source, ahead, units)
                 query = jnp.where(here, fronts[ahead - 1], query)
                 key = jnp.where(here, far_keys[ahead - 1][place], key)
-                value = jnp.where(here, values[ahead][place], value)
             score_list.append(jnp.where(new, nt(query, key) * scale, -1e30))
-            value_list.append(value)
         scores = jnp.concatenate(score_list, 1)
         expos = jnp.exp(scores - jnp.max(scores, 1, keepdims=True))
-        weights = (expos / jnp.sum(expos, 1, keepdims=True)).astype(BF16)
-        out_ref[unit] = nn(weights, jnp.concatenate(value_list, 0)).astype(BF16)
-
-
-def project_kernel(axes, other, blocks, attended_ref, weight_ref, out_ref):
-    planes, _, width = out_ref.shape
-    cores = weight_ref.shape[1] // (planes * width)
-    core = lax.rem(lax.axis_index(axes[1]) + other, cores)
-    heads = attended_ref.shape[0] // blocks
-    attended = jnp.concatenate(
-        [
-            jnp.concatenate([attended_ref[head * blocks + block] for head in range(heads)], 1)
-            for block in range(blocks)
-        ],
-        0,
-    )
-    for plane in range(planes):
-        start = pl.multiple_of((plane * cores + core) * width, width)
-        total = nn(attended, weight_ref[:, pl.ds(start, width)])
-        out_ref[plane] = total.astype(out_ref.dtype)
+        weights_ref[unit] = (expos / jnp.sum(expos, 1, keepdims=True)).astype(BF16)
+
+
+def blend_kernel(before, blocks, away_ref, weights_ref, part_ref, *refs):
+    early, late, out_ref = refs[:before], refs[before:2 * before], refs[2 * before]
+    units = weights_ref.shape[0]
+    half = units // 2
+    for unit in range(units):
+        value_list = [rows_of(part_ref, blocks, unit, 3)]
+        for entry in range(1, TOPK):
+            source, _ = listed_block(away_ref, unit, entry)
+            inside = jnp.maximum(source, 0)
+            start = pl.multiple_of((3 * blocks + lax.rem(inside, blocks)) * BLOCK, BLOCK)
+            value = part_ref[inside // blocks, pl.ds(start, BLOCK)]
+            for ahead in range(1, before + 1):
+                place, here = earlier(source, ahead, units)
+                value = jnp.where(here, early[ahead - 1][jnp.minimum(place, half - 1)], value)
+                value = jnp.where(
+                    here & (place >= half), late[ahead - 1][jnp.maximum(place - half, 0)], value
+                )
+            value_list.append(value)
+        blended = nn(weights_ref[unit], jnp.concatenate(value_list, 0)).astype(BF16)
+        for plane in range(out_ref.shape[1]):
+            out_ref[unit // blocks, plane, unit % blocks] = blended
+
+
+def project_kernel(axes, other, cores, attended_ref, own_ref, *refs):
+    other_refs, out_ref = refs[:-1], refs[-1]
+    heads, planes, blocks = attended_ref.shape[:3]
+    index = lax.axis_index(axes[1])
+    core, plane = lax.rem(index + other, cores), index // cores
+    width = out_ref.shape[1]
+    total = None
+    for offset in range(planes):
+        source = lax.rem(plane + offset, planes)
+        attended = jnp.concatenate(
+            [
+                jnp.concatenate(
+                    [attended_ref[head, source, block] for head in range(heads)], 1
+                )
+                for block in range(blocks)
+            ],
+            0,
+        )
+        if offset:
+            start = pl.multiple_of(core * width, width)
+            weight = other_refs[offset - 1][:, pl.ds(start, width)]
+        else:
+            start = pl.multiple_of((plane * cores + core) * width, width)
+            weight = own_ref[:, pl.ds(start, width)]
+        product = nn(attended, weight)
+        total = product if total is None else total + product
+    out_ref[...] = total.astype(out_ref.dtype)
 
 
 def call(kernel, outs, specs, flops, scratch=(), places=None, space=32):
@@ -374,9 +424,17 @@
         ANY,
         56,
     )(directions, keys, queries, values, rates, selected)
+    plane = lax.axis_index("head") // cores
+    width = out_weight.shape[1] // planes
+    weight_parts = []
+    for offset in range(1, planes):
+        start = lax.rem(plane + planes - offset, planes) * width
+        turned = [(g, (g + head_size - cores * offset) % head_size) for g in range(head_size)]
+        piece = lax.dynamic_slice_in_dim(out_weight, start, width, 1)
+        weight_parts.append(lax.ppermute(piece, "head", turned))
     parts = exchange(packed)
-    own_values = parts[:, 3 * tokens:4 * tokens].reshape(units, *tile)
-    value_parts = [own_values] + [onward(own_values, by) for by in range(1, before + 1)]
+    early = parts[:heads // 2, 3 * tokens:4 * tokens].reshape(units // 2, *tile)
+    early_parts = [onward(early, by) for by in range(1, before + 1)]
 
     end, tail, far, even, pair_map, group_map, mixed, away = call(
         functools.partial(keys_kernel, blocks),
@@ -395,39 +453,54 @@
     )(parts)
     far_parts = [onward(far, by) for by in range(1, before + 1)]
     map_parts = [onward(group_map, by) for by in range(1, before)]
-    inner, moving = call(
+    inner, moving, late = call(
         functools.partial(queries_kernel, blocks),
-        [array((units, BLOCK, BLOCK), F32), array((units, pairs + 1, *tile))],
-        [VMEM] * 4 + [ANY] * before,
+        [
+            array((units, BLOCK, BLOCK), F32),
+            array((units, pairs + 1, *tile)),
+            array((units - units // 2, *tile)),
+        ],
+        [VMEM] * 4 + [ANY] * (before + len(weight_parts)),
         200 * cubes,
-    )(parts, mixed, even, pair_map, *value_parts[1:])
+    )(parts, mixed, even, pair_map, *early_parts, *weight_parts)
+    late_parts = [onward(late, by) for by in range(1, before + 1)]
+    weights = call(
+        functools.partial(weights_kernel, before),
+        array((units, BLOCK, TOPK * BLOCK)),
+        [SMEM] + [VMEM] * (4 + before + len(map_parts)),
+        100 * cubes,
+    )(away, moving, inner, end, tail, *far_parts, *map_parts)
     attended = call(
-        functools.partial(attend_kernel, before),
-        array((units, *tile)),
-        [SMEM] + [VMEM] * (4 + max(3 * before, 1)),
-        200 * cubes,
-    )(away, moving, inner, end, tail, *value_parts, *far_parts, *map_parts)
-
-    local = exchange(attended)
-    width = out_weight.shape[1] // head_size
+        functools.partial(blend_kernel, before, blocks),
+        array((heads, planes, blocks, *tile)),
+        [SMEM] + [VMEM] * (2 + 2 * before),
+        100 * cubes,
+    )(away, weights, parts, *early_parts, *late_parts)
+
+    returns = [
+        [
+            (group * heads + place) * head_size + p * cores + core
+            for place in range(heads)
+            for p in range(planes)
+        ]
+        for group in range(groups)
+        for core in range(cores)
+    ]
+    local = lax.all_to_all(
+        attended.reshape(heads * planes, blocks, *tile),
+        axes, 0, 0, axis_index_groups=returns, tiled=True,
+    ).reshape(heads, planes, blocks, *tile)
 
     def projected(other, kind):
         return call(
-            functools.partial(project_kernel, axes, other, blocks),
-            array((planes, tokens, width), kind),
-            [VMEM] * 2,
+            functools.partial(project_kernel, axes, other, cores),
+            array((tokens, width // cores), kind),
+            [VMEM] * (1 + planes),
             128 * cubes,
-        )(local, out_weight)
+        )(local, out_weight, *weight_parts)
 
     arrived = lax.ppermute(projected(1, BF16), "head", partners)
-    total = projected(0, F32) + arrived.astype(F32)
-    plane = lax.axis_index("head") // cores
-    result = lax.dynamic_index_in_dim(total, plane, 0, False)
-    for offset in range(1, planes):
-        part = lax.dynamic_index_in_dim(total, lax.rem(plane + offset, planes), 0, False)
-        turned = [(g, (g + cores * offset) % head_size) for g in range(head_size)]
-        result = result + lax.ppermute(part.astype(BF16), "head", turned).astype(F32)
-    return result.astype(BF16)
+    return (projected(0, F32) + arrived.astype(F32)).astype(BF16)
 
 
 def solution(mesh):

time: 72.1 us -> 71.6 us (level)
  blocking collectives: 34.2 us -> 22 us
  starting transfers between devices: 7.42 us -> 15.7 us
  waiting for transfers between devices: 10.3 us -> 12 us
  local copies, waits for them, and re-layouts: 0.06 us -> 1.13 us
    all_to_all x2 -> x1, blocking collectives: 34.2 us -> 22 us  [body(): lax.all_to_all(attended.reshape(heads * planes, blocks, *tile), axes, 0,...]
    all_to_all x0 -> x1, waiting for transfers between devices: none -> 11.2 us  [exchange(): lax.all_to_all(value, 'ctx', 0, 0, axis_index_groups=members, tiled=True)]
    ppermute x1, waiting for transfers between devices: 6.87 us -> 0.01 us  [body(): weight_parts.append(lax.ppermute(piece, 'head', turned))]
    all_to_all x0 -> x1, starting transfers between devices: none -> 5.39 us  [exchange(): lax.all_to_all(value, 'ctx', 0, 0, axis_index_groups=members, tiled=True)]
    ppermute x2 -> x3, starting transfers between devices: 5.8 us -> 8.75 us  [onward(): lax.ppermute(value, 'ctx', [(i, i + shift) for i in range(ctx_size - shif...]
    pallas_call x3 -> x4, Pallas kernels: 4.78 us -> 6.35 us  [the longest x2 3.31 us: projected(): call(functools.partial(project_kernel, axes, other, cores), array((tokens...]
    ppermute x1, waiting for transfers between devices: 1.42 us -> 0.01 us  [body(): arrived = lax.ppermute(projected(1, BF16), 'head', partners)]
    ppermute x2 -> x3, waiting for transfers between devices: 2.01 us -> 0.84 us  [onward(): lax.ppermute(value, 'ctx', [(i, i + shift) for i in range(ctx_size - shif...]
  transfers between devices with their start and end apart: 4 -> 6, of which waited for: 3 -> 2; matrix products, arithmetic and copies ran while one was open for 0% -> 2% of each run, Pallas kernels for 16% -> 19%
where the time goes in v6:
time: 71.6 us; the launch traced here: 71.1 us
  blocking collectives  22 us (31%)
  Pallas kernels  19.3 us (27%)
  starting transfers between devices  15.7 us (22%)
  waiting for transfers between devices  12 us (17%)
  local copies, waits for them, and re-layouts  1.13 us (2%)
  other arithmetic  0.77 us (1%)
    all_to_all x1, blocking collectives, body(): lax.all_to_all(attended.reshape(heads * planes, blocks, *tile), axes, 0,...  22 us
    all_to_all x1, waiting for transfers between devices, exchange(): lax.all_to_all(value, 'ctx', 0, 0, axis_index_groups=members, tiled=True)  11.2 us
    ppermute x3, starting transfers between devices, onward(): lax.ppermute(value, 'ctx', [(i, i + shift) for i in range(ctx_size - shif...  8.75 us
    pallas_call x1, Pallas kernels, body(): call(functools.partial(keys_kernel, blocks), [array((units, *tile)), arra...  7.99 us
    all_to_all x1, starting transfers between devices, exchange(): lax.all_to_all(value, 'ctx', 0, 0, axis_index_groups=members, tiled=True)  5.39 us
    pallas_call x2, Pallas kernels, projected(): call(functools.partial(project_kernel, axes, other, cores), array((tokens...  3.31 us
    pallas_call x1, Pallas kernels, body(): call(functools.partial(pack_kernel, axes), array(part_shape), [ANY] * 4 +...  2.96 us
    pallas_call x1, Pallas kernels, body(): call(functools.partial(queries_kernel, blocks), [array((units, BLOCK, BLO...  2.03 us
  transfers between devices with their start and end apart: 6, of which 2 were waited for; matrix products, arithmetic and copies ran while one was open for 2% of the time, Pallas kernels for 19%

profile of v6, /device:TPU:0, one launch (start us, length us, event | category | flops | bytes accessed | tf_op | source)
XLA Modules:
  0.0 71.1 jit_solution(7544300002598016291)
XLA Ops:
  0.0 3.0 %shard_map.73 = bf16[4,1040,128]{2,1,0:T(8,128)(2,1)} custom-call(bf16[256,512]{1,0:T(8,128)(2,1)} %d_ref.1, bf16[256,512]{1,0:T(8,128)(2,1)} %k_ref.1, bf16[256,512]{1,0:T(8,128)(2,1)} %q_ref.1, bf16[256,512]{1,0:T(8,128)(2,1)} %v_ref.1, f32[4,256]{1,0:T(4,128)} %rates_ref.1, s32[2,4]{1,0:T(2,128)} %selected_ref.1), custom_call_target="tpu_custom_call" | custom-call | flops 4194304 | bytes 2097152 | tf_op jit(solution)/shard_map/pallas_call | solution.py:414
  3.0 0.0 copy-start
  3.0 5.4 %all-to-all-start = ((bf16[4,1040,128]{2,1,0:T(8,128)(2,1)}), bf16[4,1040,128]{2,1,0:T(8,128)(2,1)S(1)}, u32[]{:S(2)}, u32[]{:S(2)}) async-start(bf16[4,1040,128]{2,1,0:T(8,128)(2,1)} %shard_map.73), calls=%async_computation | async-start | bytes 2129920 | tf_op jit(solution)/shard_map/all_to_all | solution.py:404
  8.4 0.0 copy-done
  8.4 1.1 %constant_dynamic-slice_fusion = bf16[512,1024]{1,0:T(8,128)(2,1)} fusion(bf16[512,2048]{1,0:T(8,128)(2,1)S(1)} %copy-done, s32[]{:T(128)S(6)} %select_n.9), kind=kLoop, calls=%fused_computation.1 | loop fusion | bytes 2097156 | tf_op jit(solution)/shard_map/dynamic_slice | solution.py:433
  9.5 1.5 %collective-permute-start.1 = (bf16[512,1024]{1,0:T(8,128)(2,1)}, bf16[512,1024]{1,0:T(8,128)(2,1)}, u32[]{:S(2)}, u32[]{:S(2)}) collective-permute-start(bf16[512,1024]{1,0:T(8,128)(2,1)} %constant_dynamic-slice_fusion), channel_id=1, source_target_pairs={{0,2},{1,3},{2,0},{3,1},{4,6},{5,7},{6,4},{7,5},{8,10},{9,11},{10,... | collective-permute-start | bytes 3145736 | tf_op jit(solution)/shard_map/ppermute | solution.py:434
  11.0 11.2 %all-to-all-done.part_ref = bf16[4,1040,128]{2,1,0:T(8,128)(2,1)S(1)} async-done(((bf16[4,1040,128]{2,1,0:T(8,128)(2,1)}), bf16[4,1040,128]{2,1,0:T(8,128)(2,1)S(1)}, u32[]{:S(2)}, u32[]{:S(2)}) %all-to-all-start) | async-done | bytes 1064992 | tf_op jit(solution)/shard_map/all_to_all | solution.py:404
  22.2 4.5 %collective-permute-start = (bf16[4,128,128]{2,1,0:T(8,128)(2,1)S(1)}, bf16[4,128,128]{2,1,0:T(8,128)(2,1)S(1)}, u32[]{:S(2)}, u32[]{:S(2)}) collective-permute-start(bf16[4,128,128]{2,1,0:T(8,128)(2,1)S(1)} %bitcast.6), channel_id=1, source_target_pairs={{0,16},{4,20},{8,24},{12,28},{1,17},{5,21},{9,25},{13,29},{2,18},{... | collective-permute-start | bytes 393224 | tf_op jit(solution)/shard_map/ppermute | solution.py:408
  26.7 8.0 %shard_map.74 = (bf16[8,128,128]{2,1,0:T(8,128)(2,1)S(1)}, bf16[8,128,128]{2,1,0:T(8,128)(2,1)S(1)}, bf16[8,128,128]{2,1,0:T(8,128)(2,1)S(1)}, bf16[4,2,128,128]...) custom-call(bf16[4,1040,128]{2,1,0:T(8,128)(2,1)S(1)} %all-to-all-do, ...), custom_call_target="tpu_custom_call" | custom-call | flops 1677721600 | bytes 2097152 | tf_op jit(solution)/shard_map/pallas_call | solution.py:439
  34.7 1.3 %collective-permute-start.2 = (bf16[8,128,128]{2,1,0:T(8,128)(2,1)S(1)}, bf16[8,128,128]{2,1,0:T(8,128)(2,1)S(1)}, u32[]{:S(2)}, u32[]{:S(2)}) collective-permute-start(bf16[8,128,128]{2,1,0:T(8,128)(2,1)S(1)} %get-tuple-element.23), channel_id=1, source_target_pairs={{0,16},{4,20},{8,24},{12,28},{1,17},{5,21},{9,25},{13,29},{2,18},{... | collective-permute-start | bytes 786440 | tf_op jit(solution)/shard_map/ppermute | solution.py:408
  36.0 0.0 collective-permute-done.1.refs_1_.refs_0_
  36.0 0.0 collective-permute-done.refs_0_
  36.0 2.0 %shard_map.75 = (f32[8,128,128]{2,1,0:T(8,128)S(1)}, bf16[8,5,128,128]{3,2,1,0:T(8,128)(2,1)S(1)}, bf16[4,128,128]{2,1,0:T(8,128)(2,1)S(1)}) custom-call(bf16[4,1040,128]{2,1,0:T(8,128)(2,1)S(1)} %all-to-all-done.part_ref, bf16[8,128,256]{2,1,0:T(8,128)(2,1)S(1)} %get-tuple-element.16.mixed_ref, bf16[4,2,128,128]{3,2,1,0:T(8,128)(2,1)S(1)} %get-tuple-element.17.even_ref, ...), custom_call_target="tpu_custom_call" | custom-call | flops 838860800 | bytes 2097152 | tf_op jit(solution)/shard_map/pallas_call | solution.py:456
  38.1 3.0 %collective-permute-start.3 = (bf16[4,128,128]{2,1,0:T(8,128)(2,1)S(1)}, bf16[4,128,128]{2,1,0:T(8,128)(2,1)S(1)}, u32[]{:S(2)}, u32[]{:S(2)}) collective-permute-start(bf16[4,128,128]{2,1,0:T(8,128)(2,1)S(1)} %get-tuple-element.24), channel_id=1, source_target_pairs={{0,16},{4,20},{8,24},{12,28},{1,17},{5,21},{9,25},{13,29},{2,18},{... | collective-permute-start | bytes 393224 | tf_op jit(solution)/shard_map/ppermute | solution.py:408
  41.0 0.8 %collective-permute-done.2.refs_0_ = bf16[8,128,128]{2,1,0:T(8,128)(2,1)S(1)} collective-permute-done((bf16[8,128,128]{2,1,0:T(8,128)(2,1)S(1)}, bf16[8,128,128]{2,1,0:T(8,128)(2,1)S(1)}, u32[]{:S(2)}, u32[]{:S(2)}) %collective-permute-start.2) | collective-permute-done | bytes 262176 | tf_op jit(solution)/shard_map/ppermute | solution.py:408
  41.9 1.8 %shard_map.76.weights_ref = bf16[8,128,512]{2,1,0:T(8,128)(2,1)S(1)} custom-call(s32[8,128]{1,0:T(8,128)S(1)} %get-tuple-element.15.away_ref, bf16[8,5,128,128]{3,2,1,0:T(8,128)(2,1)S(1)} %get-tuple-element.19.moving_ref, f32[8,128,128]{2,1,0:T(8,128)S(1)} %get-tuple-element.20.inner_ref, bf16[8,128,128]{2,1,0:T(8,128)(2,1)S(1)} %get-tuple-element.21.end_ref, ...), custom_call_target="tpu_custom_call" | custom-call | flops 419430400 | bytes 2097152 | tf_op jit(solution)/shard_map/pallas_call | solution.py:467
  43.7 0.0 collective-permute-done.3.refs_1_
  43.7 1.2 %shard_map.77 = bf16[4,2,2,128,128]{4,3,2,1,0:T(8,128)(2,1)S(1)} custom-call(s32[8,128]{1,0:T(8,128)S(1)} %get-tuple-element.15.away_ref, bf16[8,128,512]{2,1,0:T(8,128)(2,1)S(1)} %shard_map.76.weights_ref, bf16[4,1040,128]{2,1,0:T(8,128)(2,1)S(1)} %all-to-all-done.part_ref, bf16[4,128,128]{2,1,0:T(8,128)(2,1)S(1)} %collective-permute-done.refs_0_, ...), custom_call_target="tpu_custom_call" | custom-call | flops 419430400 | bytes 2097152 | tf_op jit(solution)/shard_map/pallas_call | solution.py:473
  44.9 22.0 %all_to_all.10 = bf16[8,2,128,128]{3,2,1,0:T(8,128)(2,1)S(1)} all-to-all(bf16[8,2,128,128]{3,2,1,0:T(8,128)(2,1)S(1)} %bitcast.5), channel_id=1, replica_groups={{0,2,4,6,8,10,12,14},{1,3,5,7,9,11,13,15},{16,18,20,22,24,26,28,30},{17..., dimensions={0} | all-to-all | bytes 1048576 | tf_op jit(solution)/shard_map/all_to_all | solution.py:489
  66.9 1.7 %shard_map.79 = bf16[256,512]{1,0:T(8,128)(2,1)S(1)} custom-call(bf16[4,2,2,128,128]{4,3,2,1,0:T(8,128)(2,1)S(1)} %bitcast.3, bf16[512,2048]{1,0:T(8,128)(2,1)S(1)} %copy-done, bf16[512,1024]{1,0:T(8,128)(2,1)} %collective-permute-done.1.refs_1_.refs_0_), custom_call_target="tpu_custom_call" | custom-call | flops 536870912 | bytes 2097152 | tf_op jit(solution)/shard_map/pallas_call | solution.py:495
  68.6 0.1 collective-permute-start.4
  68.6 1.7 %shard_map.78 = f32[256,512]{1,0:T(8,128)S(1)} custom-call(bf16[4,2,2,128,128]{4,3,2,1,0:T(8,128)(2,1)S(1)} %bitcast.4, bf16[512,2048]{1,0:T(8,128)(2,1)S(1)} %copy-done, bf16[512,1024]{1,0:T(8,128)(2,1)} %collective-permute-done.1.refs_1_.refs_0_), custom_call_target="tpu_custom_call" | custom-call | flops 536870912 | bytes 2097152 | tf_op jit(solution)/shard_map/pallas_call | solution.py:495
  70.3 0.0 collective-permute-done.4
  70.3 0.8 %add_convert_fusion = bf16[256,512]{1,0:T(8,128)(2,1)} fusion(f32[256,512]{1,0:T(8,128)S(1)} %shard_map.78, bf16[256,512]{1,0:T(8,128)(2,1)S(1)} %collective-permute-done.4), kind=kLoop, calls=%fused_computation | loop fusion | flops 393216 | bytes 1048576 | tf_op jit(solution)/shard_map/convert_element_type | solution.py:503
  (1 shorter events, 0.0 us)
Async XLA Ops:
  3.0 5.4 %copy-start = (bf16[512,2048]{1,0:T(8,128)(2,1)S(1)}, bf16[512,2048]{1,0:T(8,128)(2,1)}, u32[]{:S(2)}) copy-start(bf16[512,2048]{1,0:T(8,128)(2,1)} %own_ref.3) | copy-start | bytes 6291460
  3.0 19.2 %all-to-all-start = ((bf16[4,1040,128]{2,1,0:T(8,128)(2,1)}), bf16[4,1040,128]{2,1,0:T(8,128)(2,1)S(1)}, u32[]{:S(2)}, u32[]{:S(2)}) async-start(bf16[4,1040,128]{2,1,0:T(8,128)(2,1)} %shard_map.73), calls=%async_computation | async-start | bytes 2129920 | tf_op jit(solution)/shard_map/all_to_all | solution.py:404
  9.5 26.5 %collective-permute-start.1 = (bf16[512,1024]{1,0:T(8,128)(2,1)}, bf16[512,1024]{1,0:T(8,128)(2,1)}, u32[]{:S(2)}, u32[]{:S(2)}) collective-permute-start(bf16[512,1024]{1,0:T(8,128)(2,1)} %constant_dynamic-slice_fusion), channel_id=1, source_target_pairs={{0,2},{1,3},{2,0},{3,1},{4,6},{5,7},{6,4},{7,5},{8,10},{9,11},{10,... | collective-permute-start | bytes 3145736 | tf_op jit(solution)/shard_map/ppermute | solution.py:434
  22.2 13.8 %collective-permute-start = (bf16[4,128,128]{2,1,0:T(8,128)(2,1)S(1)}, bf16[4,128,128]{2,1,0:T(8,128)(2,1)S(1)}, u32[]{:S(2)}, u32[]{:S(2)}) collective-permute-start(bf16[4,128,128]{2,1,0:T(8,128)(2,1)S(1)} %bitcast.6), channel_id=1, source_target_pairs={{0,16},{4,20},{8,24},{12,28},{1,17},{5,21},{9,25},{13,29},{2,18},{... | collective-permute-start | bytes 393224 | tf_op jit(solution)/shard_map/ppermute | solution.py:408
  34.7 7.2 %collective-permute-start.2 = (bf16[8,128,128]{2,1,0:T(8,128)(2,1)S(1)}, bf16[8,128,128]{2,1,0:T(8,128)(2,1)S(1)}, u32[]{:S(2)}, u32[]{:S(2)}) collective-permute-start(bf16[8,128,128]{2,1,0:T(8,128)(2,1)S(1)} %get-tuple-element.23), channel_id=1, source_target_pairs={{0,16},{4,20},{8,24},{12,28},{1,17},{5,21},{9,25},{13,29},{2,18},{... | collective-permute-start | bytes 786440 | tf_op jit(solution)/shard_map/ppermute | solution.py:408
  38.1 5.6 %collective-permute-start.3 = (bf16[4,128,128]{2,1,0:T(8,128)(2,1)S(1)}, bf16[4,128,128]{2,1,0:T(8,128)(2,1)S(1)}, u32[]{:S(2)}, u32[]{:S(2)}) collective-permute-start(bf16[4,128,128]{2,1,0:T(8,128)(2,1)S(1)} %get-tuple-element.24), channel_id=1, source_target_pairs={{0,16},{4,20},{8,24},{12,28},{1,17},{5,21},{9,25},{13,29},{2,18},{... | collective-permute-start | bytes 393224 | tf_op jit(solution)/shard_map/ppermute | solution.py:408
  68.6 1.7 %collective-permute-start.4 = (bf16[256,512]{1,0:T(8,128)(2,1)S(1)}, bf16[256,512]{1,0:T(8,128)(2,1)S(1)}, u32[]{:S(2)}, u32[]{:S(2)}) collective-permute-start(bf16[256,512]{1,0:T(8,128)(2,1)S(1)} %shard_map.79), channel_id=1, source_target_pairs={{0,1},{1,0},{2,3},{3,2},{4,5},{5,4},{6,7},{7,6},{8,9},{9,8},{10,11... | collective-permute-start | bytes 786440 | tf_op jit(solution)/shard_map/ppermute | solution.py:502

commit v7 on v6

--- a/solution.py
+++ b/solution.py
@@ -56,16 +56,26 @@
     return rows, columns
 
 
-def pack_kernel(axes, d_ref, k_ref, q_ref, v_ref, rates_ref, selected_ref, out_ref, parts_ref,
-                sems, out_sems):
+def fetched(sources, targets, sems):
+    copies = []
+    for index, (source, target) in enumerate(zip(sources, targets)):
+        copies.append(pltpu.make_async_copy(source, target, sems.at[index]))
+        copies[-1].start()
+    return copies
+
+
+def pack_kernel(axes, d_ref, k_ref, v_ref, rates_hbm, selected_hbm, out_ref, parts_ref,
+                rates_ref, selected_ref, sems, few_sems, out_sems):
     tokens = d_ref.shape[0]
     heads = d_ref.shape[1] // HEAD_DIM
     blocks = tokens // BLOCK
     first_block = lax.axis_index(axes[0]) * blocks
+    few_copies = fetched([rates_hbm, selected_hbm], [rates_ref, selected_ref], few_sems)
+    sources = (d_ref, k_ref, v_ref)
     copies = []
     for head in range(heads):
         columns = pl.ds(head * HEAD_DIM, HEAD_DIM)
-        for kind, source in enumerate((d_ref, k_ref, q_ref, v_ref)):
+        for kind, source in enumerate(sources):
             copies.append(
                 pltpu.make_async_copy(
                     source.at[:, columns],
@@ -74,6 +84,8 @@
                 )
             )
             copies[-1].start()
+    for copy in few_copies:
+        copy.wait()
     row = lax.broadcasted_iota(jnp.int32, (EXTRA, HEAD_DIM), 0)
     lane = lax.broadcasted_iota(jnp.int32, (EXTRA, HEAD_DIM), 1)
     away = jnp.zeros((EXTRA, HEAD_DIM), jnp.int32)
@@ -94,8 +106,8 @@
             for index, term in enumerate(terms):
                 piece = term[head:head + 1, block * BLOCK:(block + 1) * BLOCK]
                 extra = jnp.where(row == TERMS * block + index, piece, extra)
-        parts_ref[head, 4 * tokens:] = extra.astype(BF16)
-        for copy in copies[4 * head:4 * head + 4]:
+        parts_ref[head, len(sources) * tokens:] = extra.astype(BF16)
+        for copy in copies[len(sources) * head:len(sources) * (head + 1)]:
             copy.wait()
         out_copies.append(
             pltpu.make_async_copy(parts_ref.at[head], out_ref.at[head], out_sems.at[head])
@@ -159,9 +171,15 @@
         tick += 1
 
 
-def keys_kernel(blocks, part_ref, end_ref, tail_ref, far_ref, even_ref, pair_ref, group_ref,
-                mixed_ref, away_ref):
-    units = part_ref.shape[0] * blocks
+def keys_kernel(blocks, part_ref, queries_ref, end_ref, tail_ref, far_ref, even_ref, pair_ref,
+                group_ref, mixed_ref, away_ref, out_ref, cut_ref, sems, out_sems):
+    heads = part_ref.shape[0]
+    units = heads * blocks
+    query_copies = fetched(
+        [queries_ref.at[:, pl.ds(head * HEAD_DIM, HEAD_DIM)] for head in range(heads)],
+        [cut_ref.at[head] for head in range(heads)],
+        sems,
+    )
     rows, columns = square_iotas()
     diagonal = rows == columns
     identity = diagonal.astype(F32)
@@ -172,7 +190,7 @@
     def terms(unit):
         direction = rows_of(part_ref, blocks, unit, 0)
         key = rows_of(part_ref, blocks, unit, 1)
-        extra = part_ref[unit // blocks, 4 * blocks * BLOCK:].astype(F32)
+        extra = part_ref[unit // blocks, 3 * blocks * BLOCK:].astype(F32)
         first = TERMS * (unit % blocks)
         rate = extra[first:first + 1] + extra[first + 1:first + 2] + extra[first + 2:first + 3]
         listed = TERMS * blocks + unit % blocks
@@ -211,6 +229,13 @@
         end_ref[unit] = ends[unit].astype(BF16)
 
     interleaved([terms(unit) for unit in range(units)], 1)
+    out_copies = []
+    for head in range(heads):
+        query_copies[head].wait()
+        out_copies.append(
+            pltpu.make_async_copy(cut_ref.at[head], out_ref.at[head], out_sems.at[head])
+        )
+        out_copies[-1].start()
     pair_keys, pair_maps = [], []
     for pair in range(units // 2):
         even, odd = 2 * pair, 2 * pair + 1
@@ -237,19 +262,20 @@
         far_ref[2 * pair + 1] = far[BLOCK:].astype(BF16)
     group_ref[0] = onward[0]
     group_ref[1] = onward[1]
-
-
-def queries_kernel(blocks, part_ref, mixed_ref, even_ref, pair_ref, *refs):
-    inner_ref, moving_ref, late_ref = refs[-3:]
+    for copy in out_copies:
+        copy.wait()
+
+
+def queries_kernel(blocks, count, part_ref, query_ref, mixed_ref, even_ref, pair_ref, *refs):
+    inner_ref, moving_ref = refs[-3 - count:-1 - count]
     units = part_ref.shape[0] * blocks
-    for unit in range(units // 2, units):
-        late_ref[unit - units // 2] = rows_of(part_ref, blocks, unit, 3)
+    copies = fetched(refs[:count], refs[-1 - count:-1], refs[-1])
     rows, columns = square_iotas()
     current = []
     for unit in range(units):
         direction = rows_of(part_ref, blocks, unit, 0)
         key = rows_of(part_ref, blocks, unit, 1)
-        query = rows_of(part_ref, blocks, unit, 2)
+        query = rows_of(query_ref, blocks, unit, 0)
         query_proj = split(jnp.where(rows >= columns, nt(query, direction), 0.0))
         ahead = nn(jnp.concatenate(query_proj, 0), mixed_ref[unit])
         ahead = ahead[:BLOCK] + ahead[BLOCK:]
@@ -275,6 +301,8 @@
             )
             moving_ref[2 * pair, step] = current[pair][0][:BLOCK]
             moving_ref[2 * pair + 1, step] = current[pair][0][BLOCK:]
+    for copy in copies:
+        copy.wait()
 
 
 def listed_block(away_ref, unit, entry):
@@ -289,56 +317,47 @@
     return jnp.clip(source + ahead * units, 0, units - 1), source < (1 - ahead) * units
 
 
-def weights_kernel(before, away_ref, moving_ref, inner_ref, end_ref, tail_ref, *refs):
-    far_keys, group_maps = refs[:before], refs[before:-1]
-    weights_ref = refs[-1]
+def attend_kernel(before, blocks, away_ref, moving_ref, inner_ref, end_ref, tail_ref, part_ref,
+                  *refs):
+    values, far_keys = refs[:before], refs[before:2 * before]
+    group_maps, out_ref = refs[2 * before:-1], refs[-1]
     units = inner_ref.shape[0]
     rows, columns = square_iotas()
     scale = HEAD_DIM ** (-0.5)
-    for unit in range(units):
+
+    def steps(unit):
         pair = unit // 2
         fronts = [moving_ref[unit, pair + 1]]
         for group_map in group_maps:
             passed = nt(fronts[-1], group_map[0]) + nt(fronts[-1], group_map[1])
             fronts.append(passed.astype(BF16))
         score_list = [jnp.where(rows >= columns, inner_ref[unit] * scale, -1e30)]
+        value_list = [rows_of(part_ref, blocks, unit, 2)]
         for entry in range(1, TOPK):
             source, new = listed_block(away_ref, unit, entry)
             inside = jnp.maximum(source, 0)
             step = jnp.maximum(pair - inside // 2, 0)
+            start = pl.multiple_of((2 * blocks + lax.rem(inside, blocks)) * BLOCK, BLOCK)
             query = moving_ref[unit, step]
             key = jnp.where(step == 0, end_ref[inside], tail_ref[inside])
+            value = part_ref[inside // blocks, pl.ds(start, BLOCK)]
             for ahead in range(1, before + 1):
                 place, here = earlier(source, ahead, units)
                 query = jnp.where(here, fronts[ahead - 1], query)
                 key = jnp.where(here, far_keys[ahead - 1][place], key)
+                value = jnp.where(here, values[ahead - 1][place], value)
             score_list.append(jnp.where(new, nt(query, key) * scale, -1e30))
+            value_list.append(value)
+        yield
         scores = jnp.concatenate(score_list, 1)
         expos = jnp.exp(scores - jnp.max(scores, 1, keepdims=True))
-        weights_ref[unit] = (expos / jnp.sum(expos, 1, keepdims=True)).astype(BF16)
-
-
-def blend_kernel(before, blocks, away_ref, weights_ref, part_ref, *refs):
-    early, late, out_ref = refs[:before], refs[before:2 * before], refs[2 * before]
-    units = weights_ref.shape[0]
-    half = units // 2
-    for unit in range(units):
-        value_list = [rows_of(part_ref, blocks, unit, 3)]
-        for entry in range(1, TOPK):
-            source, _ = listed_block(away_ref, unit, entry)
-            inside = jnp.maximum(source, 0)
-            start = pl.multiple_of((3 * blocks + lax.rem(inside, blocks)) * BLOCK, BLOCK)
-            value = part_ref[inside // blocks, pl.ds(start, BLOCK)]
-            for ahead in range(1, before + 1):
-                place, here = earlier(source, ahead, units)
-                value = jnp.where(here, early[ahead - 1][jnp.minimum(place, half - 1)], value)
-                value = jnp.where(
-                    here & (place >= half), late[ahead - 1][jnp.maximum(place - half, 0)], value
-                )
-            value_list.append(value)
-        blended = nn(weights_ref[unit], jnp.concatenate(value_list, 0)).astype(BF16)
+        weights = (expos / jnp.sum(expos, 1, keepdims=True)).astype(BF16)
+        yield
+        blended = nn(weights, jnp.concatenate(value_list, 0)).astype(BF16)
         for plane in range(out_ref.shape[1]):
             out_ref[unit // blocks, plane, unit % blocks] = blended
+
+    interleaved([steps(unit) for unit in range(units)], 1)
 
 
 def project_kernel(axes, other, cores, attended_ref, own_ref, *refs):
@@ -410,20 +429,23 @@
     def array(shape, kind=BF16):
         return jax.ShapeDtypeStruct(shape, kind)
 
-    part_shape = (heads, 4 * tokens + EXTRA, HEAD_DIM)
+    part_shape = (heads, 3 * tokens + EXTRA, HEAD_DIM)
     packed = call(
         functools.partial(pack_kernel, axes),
         array(part_shape),
-        [ANY] * 4 + [VMEM, SMEM],
+        [ANY] * 5,
         cubes,
         [
             pltpu.VMEM(part_shape, BF16),
-            pltpu.SemaphoreType.DMA((heads, 4)),
+            pltpu.VMEM(rates.shape, F32),
+            pltpu.SMEM(selected.shape, jnp.int32),
+            pltpu.SemaphoreType.DMA((heads, 3)),
+            pltpu.SemaphoreType.DMA((2,)),
             pltpu.SemaphoreType.DMA((heads,)),
         ],
         ANY,
         56,
-    )(directions, keys, queries, values, rates, selected)
+    )(directions, keys, values, rates, selected)
     plane = lax.axis_index("head") // cores
     width = out_weight.shape[1] // planes
     weight_parts = []
@@ -433,10 +455,10 @@
         piece = lax.dynamic_slice_in_dim(out_weight, start, width, 1)
         weight_parts.append(lax.ppermute(piece, "head", turned))
     parts = exchange(packed)
-    early = parts[:heads // 2, 3 * tokens:4 * tokens].reshape(units // 2, *tile)
-    early_parts = [onward(early, by) for by in range(1, before + 1)]
-
-    end, tail, far, even, pair_map, group_map, mixed, away = call(
+    own_values = parts[:, 2 * tokens:3 * tokens].reshape(units, *tile)
+    value_parts = [onward(own_values, by) for by in range(1, before + 1)]
+
+    end, tail, far, even, pair_map, group_map, mixed, away, cut = call(
         functools.partial(keys_kernel, blocks),
         [
             array((units, *tile)),
@@ -447,35 +469,34 @@
             array((2, *tile)),
             array((units, BLOCK, 2 * BLOCK)),
             array((units, HEAD_DIM), jnp.int32),
+            array((heads, tokens, HEAD_DIM)),
         ],
-        [VMEM],
+        [VMEM, ANY],
         400 * cubes,
-    )(parts)
+        [
+            pltpu.VMEM((heads, tokens, HEAD_DIM), BF16),
+            pltpu.SemaphoreType.DMA((heads,)),
+            pltpu.SemaphoreType.DMA((heads,)),
+        ],
+        [VMEM] * 8 + [ANY],
+    )(parts, queries)
     far_parts = [onward(far, by) for by in range(1, before + 1)]
     map_parts = [onward(group_map, by) for by in range(1, before)]
-    inner, moving, late = call(
-        functools.partial(queries_kernel, blocks),
-        [
-            array((units, BLOCK, BLOCK), F32),
-            array((units, pairs + 1, *tile)),
-            array((units - units // 2, *tile)),
-        ],
-        [VMEM] * 4 + [ANY] * (before + len(weight_parts)),
+    query_parts = exchange(cut)
+    inner, moving, *weight_parts = call(
+        functools.partial(queries_kernel, blocks, len(weight_parts)),
+        [array((units, BLOCK, BLOCK), F32), array((units, pairs + 1, *tile))]
+        + [array(part.shape) for part in weight_parts],
+        [VMEM] * 5 + [ANY] * (len(weight_parts) + before),
         200 * cubes,
-    )(parts, mixed, even, pair_map, *early_parts, *weight_parts)
-    late_parts = [onward(late, by) for by in range(1, before + 1)]
-    weights = call(
-        functools.partial(weights_kernel, before),
-        array((units, BLOCK, TOPK * BLOCK)),
-        [SMEM] + [VMEM] * (4 + before + len(map_parts)),
-        100 * cubes,
-    )(away, moving, inner, end, tail, *far_parts, *map_parts)
+        [pltpu.SemaphoreType.DMA((max(len(weight_parts), 1),))],
+    )(parts, query_parts, mixed, even, pair_map, *weight_parts, *value_parts)
     attended = call(
-        functools.partial(blend_kernel, before, blocks),
+        functools.partial(attend_kernel, before, blocks),
         array((heads, planes, blocks, *tile)),
-        [SMEM] + [VMEM] * (2 + 2 * before),
-        100 * cubes,
-    )(away, weights, parts, *early_parts, *late_parts)
+        [SMEM] + [VMEM] * (5 + 2 * before + len(map_parts)),
+        200 * cubes,
+    )(away, moving, inner, end, tail, parts, *value_parts, *far_parts, *map_parts)
 
     returns = [
         [

time: 71.6 us -> 81 us (1.13)
  local copies, waits for them, and re-layouts: 1.13 us -> 8.35 us
  Pallas kernels: 19.3 us -> 15.9 us
  waiting for transfers between devices: 12 us -> 14.3 us
  blocking collectives: 22 us -> 24.2 us
  starting transfers between devices: 15.7 us -> 16.9 us
    unnamed x2 -> x26, local copies, waits for them, and re-layouts: 0.01 us -> 7.26 us
    ppermute x3 -> x2, waiting for transfers between devices: 0.84 us -> 4.78 us  [onward(): lax.ppermute(value, 'ctx', [(i, i + shift) for i in range(ctx_size - shif...]
    all_to_all x1 -> x2, starting transfers between devices: 5.39 us -> 8.8 us  [exchange(): lax.all_to_all(value, 'ctx', 0, 0, axis_index_groups=members, tiled=True)]
    all_to_all x1 -> x2, waiting for transfers between devices: 11.2 us -> 8.45 us  [exchange(): lax.all_to_all(value, 'ctx', 0, 0, axis_index_groups=members, tiled=True)]
    pallas_call x2, Pallas kernels: 3.31 us -> 0.88 us  [projected(): call(functools.partial(project_kernel, axes, other, cores), array((tokens...]
    ppermute x3 -> x2, starting transfers between devices: 8.75 us -> 6.5 us  [onward(): lax.ppermute(value, 'ctx', [(i, i + shift) for i in range(ctx_size - shif...]
    all_to_all x1, blocking collectives: 22 us -> 24.2 us  [body(): lax.all_to_all(attended.reshape(heads * planes, blocks, *tile), axes, 0,...]
    ppermute x1, waiting for transfers between devices: 0.01 us -> 1.07 us  [body(): arrived = lax.ppermute(projected(1, BF16), 'head', partners)]
  transfers between devices with their start and end apart: 6 -> 6, of which waited for: 2 -> 3; matrix products, arithmetic and copies ran while one was open for 2% -> 1% of each run, Pallas kernels for 19% -> 13%
where the time goes in v7:
time: 81 us; the launch traced here: 80.5 us
  blocking collectives  24.2 us (30%)
  starting transfers between devices  16.9 us (21%)
  Pallas kernels  15.9 us (20%)
  waiting for transfers between devices  14.3 us (18%)
  local copies, waits for them, and re-layouts  8.35 us (10%)
    all_to_all x1, blocking collectives, body(): lax.all_to_all(attended.reshape(heads * planes, blocks, *tile), axes, 0,...  24.2 us
    all_to_all x2, starting transfers between devices, exchange(): lax.all_to_all(value, 'ctx', 0, 0, axis_index_groups=members, tiled=True)  8.8 us
    all_to_all x2, waiting for transfers between devices, exchange(): lax.all_to_all(value, 'ctx', 0, 0, axis_index_groups=members, tiled=True)  8.45 us
    pallas_call x1, Pallas kernels, body(): call(functools.partial(keys_kernel, blocks), [array((units, *tile)), arra...  7.92 us
    unnamed x26, local copies, waits for them, and re-layouts  7.26 us
    ppermute x2, starting transfers between devices, onward(): lax.ppermute(value, 'ctx', [(i, i + shift) for i in range(ctx_size - shif...  6.5 us
    ppermute x2, waiting for transfers between devices, onward(): lax.ppermute(value, 'ctx', [(i, i + shift) for i in range(ctx_size - shif...  4.78 us
    pallas_call x1, Pallas kernels, body(): call(functools.partial(attend_kernel, before, blocks), array((heads, plan...  2.85 us
  transfers between devices with their start and end apart: 6, of which 3 were waited for; matrix products, arithmetic and copies ran while one was open for 1% of the time, Pallas kernels for 13%

profile of v7, /device:TPU:0, one launch (start us, length us, event | category | flops | bytes accessed | tf_op | source)
XLA Modules:
  0.0 80.5 jit_solution(4738415372789081812)
XLA Ops:
  0.0 2.2 %shard_map.73 = bf16[4,784,128]{2,1,0:T(8,128)(2,1)} custom-call(bf16[256,512]{1,0:T(8,128)(2,1)} %d_ref.1, bf16[256,512]{1,0:T(8,128)(2,1)} %k_ref.1, bf16[256,512]{1,0:T(8,128)(2,1)} %v_ref.1, f32[4,256]{1,0:T(4,128)} %rates_hbm.1, s32[2,4]{1,0:T(2,128)} %selected_hbm.1), custom_call_target="tpu_custom_call" | custom-call | flops 4194304 | bytes 2097152 | tf_op jit(solution)/shard_map/pallas_call | solution.py:433
  2.2 5.4 %all-to-all-start = ((bf16[4,784,128]{2,1,0:T(8,128)(2,1)}), bf16[4,784,128]{2,1,0:T(8,128)(2,1)S(1)}, u32[]{:S(2)}, u32[]{:S(2)}) async-start(bf16[4,784,128]{2,1,0:T(8,128)(2,1)} %shard_map.73), calls=%async_computation | async-start | bytes 1605632 | tf_op jit(solution)/shard_map/all_to_all | solution.py:423
  7.6 1.1 %constant_dynamic-slice_fusion = bf16[512,1024]{1,0:T(8,128)(2,1)} fusion(bf16[512,2048]{1,0:T(8,128)(2,1)S(1)} %copy-done, s32[]{:T(128)S(6)} %select_n.9), kind=kLoop, calls=%fused_computation.1 | loop fusion | bytes 2097156 | tf_op jit(solution)/shard_map/dynamic_slice | solution.py:455
  8.7 1.5 %collective-permute-start = (bf16[512,1024]{1,0:T(8,128)(2,1)}, bf16[512,1024]{1,0:T(8,128)(2,1)}, u32[]{:S(2)}, u32[]{:S(2)}) collective-permute-start(bf16[512,1024]{1,0:T(8,128)(2,1)} %constant_dynamic-slice_fusion), channel_id=1, source_target_pairs={{0,2},{1,3},{2,0},{3,1},{4,6},{5,7},{6,4},{7,5},{8,10},{9,11},{10,... | collective-permute-start | bytes 3145736 | tf_op jit(solution)/shard_map/ppermute | solution.py:456
  10.2 8.4 %all-to-all-done.part_ref = bf16[4,784,128]{2,1,0:T(8,128)(2,1)S(1)} async-done(((bf16[4,784,128]{2,1,0:T(8,128)(2,1)}), bf16[4,784,128]{2,1,0:T(8,128)(2,1)S(1)}, u32[]{:S(2)}, u32[]{:S(2)}) %all-to-all-start) | async-done | bytes 802848 | tf_op jit(solution)/shard_map/all_to_all | solution.py:423
  18.6 7.9 %shard_map.74 = (bf16[8,128,128]{2,1,0:T(8,128)(2,1)S(1)}, bf16[8,128,128]{2,1,0:T(8,128)(2,1)S(1)}, bf16[8,128,128]{2,1,0:T(8,128)(2,1)S(1)}, bf16[4,2,128,128]...) custom-call(bf16[4,784,128]{2,1,0:T(8,128)(2,1)S(1)} %all-to-all-don, ...), custom_call_target="tpu_custom_call" | custom-call | flops 1677721600 | bytes 2097152 | tf_op jit(solution)/shard_map/pallas_call | solution.py:461
  26.6 0.8 copy-done.1
  27.4 0.7 copy-done.3
  28.1 0.7 copy-done.5
  28.8 0.7 copy-done.7
  29.5 0.7 copy-done.9
  30.2 0.7 copy-done.12
  30.9 3.4 %all-to-all-start.1 = ((bf16[4,256,128]{2,1,0:T(8,128)(2,1)}), bf16[4,256,128]{2,1,0:T(8,128)(2,1)S(1)}, u32[]{:S(2)}, u32[]{:S(2)}) async-start(bf16[4,256,128]{2,1,0:T(8,128)(2,1)} %get-tuple-element.17), calls=%async_computation.1 | async-start | bytes 524288 | tf_op jit(solution)/shard_map/all_to_all | solution.py:423
  34.3 4.5 %collective-permute-start.1 = (bf16[8,128,128]{2,1,0:T(8,128)(2,1)S(1)}, bf16[8,128,128]{2,1,0:T(8,128)(2,1)S(1)}, u32[]{:S(2)}, u32[]{:S(2)}) collective-permute-start(bf16[8,128,128]{2,1,0:T(8,128)(2,1)S(1)} %bitcast.6), channel_id=1, source_target_pairs={{0,16},{4,20},{8,24},{12,28},{1,17},{5,21},{9,25},{13,29},{2,18},{... | collective-permute-start | bytes 786440 | tf_op jit(solution)/shard_map/ppermute | solution.py:427
  38.8 2.0 %collective-permute-start.2 = (bf16[8,128,128]{2,1,0:T(8,128)(2,1)}, bf16[8,128,128]{2,1,0:T(8,128)(2,1)}, u32[]{:S(2)}, u32[]{:S(2)}) collective-permute-start(bf16[8,128,128]{2,1,0:T(8,128)(2,1)} %copy-done.12), channel_id=1, source_target_pairs={{0,16},{4,20},{8,24},{12,28},{1,17},{5,21},{9,25},{13,29},{2,18},{... | collective-permute-start | bytes 786440 | tf_op jit(solution)/shard_map/ppermute | solution.py:427
  40.8 4.8 %collective-permute-done.1.refs_1_.refs_0_ = bf16[8,128,128]{2,1,0:T(8,128)(2,1)S(1)} collective-permute-done((bf16[8,128,128]{2,1,0:T(8,128)(2,1)S(1)}, bf16[8,128,128]{2,1,0:T(8,128)(2,1)S(1)}, u32[]{:S(2)}, u32[]{:S(2)}) %collective-permute-start.1) | collective-permute-done | bytes 262176 | tf_op jit(solution)/shard_map/ppermute | solution.py:427
  45.6 1.0 %copy-done.2 = bf16[8,128,256]{2,1,0:T(8,128)(2,1)S(1)} copy-done((bf16[8,128,256]{2,1,0:T(8,128)(2,1)S(1)}, bf16[8,128,256]{2,1,0:T(8,128)(2,1)}, u32[]{:S(2)}) %copy-start.2) | copy-done | bytes 524312
  46.7 0.9 %copy-done.8 = bf16[4,2,128,128]{3,2,1,0:T(8,128)(2,1)S(1)} copy-done((bf16[4,2,128,128]{3,2,1,0:T(8,128)(2,1)S(1)}, bf16[4,2,128,128]{3,2,1,0:T(8,128)(2,1)}, u32[]{:S(2)}) %copy-start.8) | copy-done | bytes 262168
  47.6 0.9 %copy-done.10 = bf16[4,2,128,128]{3,2,1,0:T(8,128)(2,1)S(1)} copy-done((bf16[4,2,128,128]{3,2,1,0:T(8,128)(2,1)S(1)}, bf16[4,2,128,128]{3,2,1,0:T(8,128)(2,1)}, u32[]{:S(2)}) %copy-start.10) | copy-done | bytes 262168
  48.6 2.0 %shard_map.75 = (f32[8,128,128]{2,1,0:T(8,128)S(1)}, bf16[8,5,128,128]{3,2,1,0:T(8,128)(2,1)S(1)}, bf16[512,1024]{1,0:T(8,128)(2,1)S(1)}) custom-call(bf16[4,784,128]{2,1,0:T(8,128)(2,1)S(1)} %all-to-all-done.part_ref, bf16[4,256,128]{2,1,0:T(8,128)(2,1)S(1)} %all-to-all-done.1.query_ref, bf16[8,128,256]{2,1,0:T(8,128)(2,1)S(1)} %copy-done.2, ...), custom_call_target="tpu_custom_call" | custom-call | flops 838860800 | bytes 2097152 | tf_op jit(solution)/shard_map/pallas_call | solution.py:486
  50.6 2.8 %shard_map.76 = bf16[4,2,2,128,128]{4,3,2,1,0:T(8,128)(2,1)S(1)} custom-call(s32[8,128]{1,0:T(8,128)S(1)} %get-tuple-element.16.away_ref, bf16[8,5,128,128]{3,2,1,0:T(8,128)(2,1)S(1)} %get-tuple-element.21.moving_ref, f32[8,128,128]{2,1,0:T(8,128)S(1)} %get-tuple-element.22.inner_ref, bf16[8,128,128]{2,1,0:T(8,128)(2,1)S(1)} %copy-done.4, ...), custom_call_target="tpu_custom_call" | custom-call | flops 838860800 | bytes 2097152 | tf_op jit(solution)/shard_map/pallas_call | solution.py:494
  53.5 24.2 %all_to_all.15 = bf16[8,2,128,128]{3,2,1,0:T(8,128)(2,1)S(1)} all-to-all(bf16[8,2,128,128]{3,2,1,0:T(8,128)(2,1)S(1)} %bitcast.5), channel_id=1, replica_groups={{0,2,4,6,8,10,12,14},{1,3,5,7,9,11,13,15},{16,18,20,22,24,26,28,30},{17..., dimensions={0} | all-to-all | bytes 1048576 | tf_op jit(solution)/shard_map/all_to_all | solution.py:510
  78.7 1.1 %collective-permute-done.3 = bf16[256,512]{1,0:T(8,128)(2,1)S(1)} collective-permute-done((bf16[256,512]{1,0:T(8,128)(2,1)S(1)}, bf16[256,512]{1,0:T(8,128)(2,1)S(1)}, u32[]{:S(2)}, u32[]{:S(2)}) %collective-permute-start.3) | collective-permute-done | bytes 262176 | tf_op jit(solution)/shard_map/ppermute | solution.py:523
  79.8 0.8 add_convert_fusion
  (24 shorter events, 1.0 us)
Async XLA Ops:
  0.0 7.6 %copy-start = (bf16[512,2048]{1,0:T(8,128)(2,1)S(1)}, bf16[512,2048]{1,0:T(8,128)(2,1)}, u32[]{:S(2)}) copy-start(bf16[512,2048]{1,0:T(8,128)(2,1)} %own_ref.3) | copy-start | bytes 6291460
  2.2 16.4 %copy-start.11 = (bf16[256,512]{1,0:T(8,128)(2,1)S(1)}, bf16[256,512]{1,0:T(8,128)(2,1)}, u32[]{:S(2)}) copy-start(bf16[256,512]{1,0:T(8,128)(2,1)} %queries_ref.1) | copy-start | bytes 786436
  2.2 16.4 %all-to-all-start = ((bf16[4,784,128]{2,1,0:T(8,128)(2,1)}), bf16[4,784,128]{2,1,0:T(8,128)(2,1)S(1)}, u32[]{:S(2)}, u32[]{:S(2)}) async-start(bf16[4,784,128]{2,1,0:T(8,128)(2,1)} %shard_map.73), calls=%async_computation | async-start | bytes 1605632 | tf_op jit(solution)/shard_map/all_to_all | solution.py:423
  8.7 32.1 %collective-permute-start = (bf16[512,1024]{1,0:T(8,128)(2,1)}, bf16[512,1024]{1,0:T(8,128)(2,1)}, u32[]{:S(2)}, u32[]{:S(2)}) collective-permute-start(bf16[512,1024]{1,0:T(8,128)(2,1)} %constant_dynamic-slice_fusion), channel_id=1, source_target_pairs={{0,2},{1,3},{2,0},{3,1},{4,6},{5,7},{6,4},{7,5},{8,10},{9,11},{10,... | collective-permute-start | bytes 3145736 | tf_op jit(solution)/shard_map/ppermute | solution.py:456
  26.6 0.8 copy-start.1
  27.4 0.7 copy-start.3
  28.1 0.7 copy-start.5
  28.8 0.7 copy-start.7
  29.5 0.7 copy-start.9
  30.2 0.7 copy-start.12
  30.9 14.7 %all-to-all-start.1 = ((bf16[4,256,128]{2,1,0:T(8,128)(2,1)}), bf16[4,256,128]{2,1,0:T(8,128)(2,1)S(1)}, u32[]{:S(2)}, u32[]{:S(2)}) async-start(bf16[4,256,128]{2,1,0:T(8,128)(2,1)} %get-tuple-element.17), calls=%async_computation.1 | async-start | bytes 524288 | tf_op jit(solution)/shard_map/all_to_all | solution.py:423
  34.3 11.3 %collective-permute-start.1 = (bf16[8,128,128]{2,1,0:T(8,128)(2,1)S(1)}, bf16[8,128,128]{2,1,0:T(8,128)(2,1)S(1)}, u32[]{:S(2)}, u32[]{:S(2)}) collective-permute-start(bf16[8,128,128]{2,1,0:T(8,128)(2,1)S(1)} %bitcast.6), channel_id=1, source_target_pairs={{0,16},{4,20},{8,24},{12,28},{1,17},{5,21},{9,25},{13,29},{2,18},{... | collective-permute-start | bytes 786440 | tf_op jit(solution)/shard_map/ppermute | solution.py:427
  38.8 11.8 %collective-permute-start.2 = (bf16[8,128,128]{2,1,0:T(8,128)(2,1)}, bf16[8,128,128]{2,1,0:T(8,128)(2,1)}, u32[]{:S(2)}, u32[]{:S(2)}) collective-permute-start(bf16[8,128,128]{2,1,0:T(8,128)(2,1)} %copy-done.12), channel_id=1, source_target_pairs={{0,16},{4,20},{8,24},{12,28},{1,17},{5,21},{9,25},{13,29},{2,18},{... | collective-permute-start | bytes 786440 | tf_op jit(solution)/shard_map/ppermute | solution.py:427
  45.6 1.0 %copy-start.2 = (bf16[8,128,256]{2,1,0:T(8,128)(2,1)S(1)}, bf16[8,128,256]{2,1,0:T(8,128)(2,1)}, u32[]{:S(2)}) copy-start(bf16[8,128,256]{2,1,0:T(8,128)(2,1)} %copy-done.1) | copy-start | bytes 1572868
  46.7 0.9 %copy-start.8 = (bf16[4,2,128,128]{3,2,1,0:T(8,128)(2,1)S(1)}, bf16[4,2,128,128]{3,2,1,0:T(8,128)(2,1)}, u32[]{:S(2)}) copy-start(bf16[4,2,128,128]{3,2,1,0:T(8,128)(2,1)} %copy-done.7) | copy-start | bytes 786436
  47.6 0.9 %copy-start.10 = (bf16[4,2,128,128]{3,2,1,0:T(8,128)(2,1)S(1)}, bf16[4,2,128,128]{3,2,1,0:T(8,128)(2,1)}, u32[]{:S(2)}) copy-start(bf16[4,2,128,128]{3,2,1,0:T(8,128)(2,1)} %copy-done.9) | copy-start | bytes 786436
  48.6 2.1 %copy-start.4 = (bf16[8,128,128]{2,1,0:T(8,128)(2,1)S(1)}, bf16[8,128,128]{2,1,0:T(8,128)(2,1)}, u32[]{:S(2)}) copy-start(bf16[8,128,128]{2,1,0:T(8,128)(2,1)} %copy-done.3) | copy-start | bytes 786436
  48.6 2.1 %copy-start.6 = (bf16[8,128,128]{2,1,0:T(8,128)(2,1)S(1)}, bf16[8,128,128]{2,1,0:T(8,128)(2,1)}, u32[]{:S(2)}) copy-start(bf16[8,128,128]{2,1,0:T(8,128)(2,1)} %copy-done.5) | copy-start | bytes 786436
  78.2 1.6 %collective-permute-start.3 = (bf16[256,512]{1,0:T(8,128)(2,1)S(1)}, bf16[256,512]{1,0:T(8,128)(2,1)S(1)}, u32[]{:S(2)}, u32[]{:S(2)}) collective-permute-start(bf16[256,512]{1,0:T(8,128)(2,1)S(1)} %shard_map.78), channel_id=1, source_target_pairs={{0,1},{1,0},{2,3},{3,2},{4,5},{5,4},{6,7},{7,6},{8,9},{9,8},{10,11... | collective-permute-start | bytes 786440 | tf_op jit(solution)/shard_map/ppermute | solution.py:523

commit v8 on v7

--- a/solution.py
+++ b/solution.py
@@ -171,13 +171,19 @@
         tick += 1
 
 
-def keys_kernel(blocks, part_ref, queries_ref, end_ref, tail_ref, far_ref, even_ref, pair_ref,
-                group_ref, mixed_ref, away_ref, out_ref, cut_ref, sems, out_sems):
+def keys_kernel(axes, blocks, part_ref, queries_ref, end_ref, tail_ref, far_ref, even_ref,
+                pair_ref, group_ref, mixed_ref, away_ref, *refs):
     heads = part_ref.shape[0]
     units = heads * blocks
+    out_refs = refs[:heads]
+    cut_ref, sems, out_sems = refs[heads:]
+    place = lax.rem(lax.axis_index(axes[0]), heads)
+    cuts = [
+        pl.multiple_of(lax.bitwise_xor(place, turn) * HEAD_DIM, HEAD_DIM) for turn in range(heads)
+    ]
     query_copies = fetched(
-        [queries_ref.at[:, pl.ds(head * HEAD_DIM, HEAD_DIM)] for head in range(heads)],
-        [cut_ref.at[head] for head in range(heads)],
+        [queries_ref.at[:, pl.ds(cut, HEAD_DIM)] for cut in cuts],
+        [cut_ref.at[turn] for turn in range(heads)],
         sems,
     )
     rows, columns = square_iotas()
@@ -230,10 +236,10 @@
 
     interleaved([terms(unit) for unit in range(units)], 1)
     out_copies = []
-    for head in range(heads):
-        query_copies[head].wait()
+    for turn in range(heads):
+        query_copies[turn].wait()
         out_copies.append(
-            pltpu.make_async_copy(cut_ref.at[head], out_ref.at[head], out_sems.at[head])
+            pltpu.make_async_copy(cut_ref.at[turn], out_refs[turn], out_sems.at[turn])
         )
         out_copies[-1].start()
     pair_keys, pair_maps = [], []
@@ -266,10 +272,21 @@
         copy.wait()
 
 
-def queries_kernel(blocks, count, part_ref, query_ref, mixed_ref, even_ref, pair_ref, *refs):
-    inner_ref, moving_ref = refs[-3 - count:-1 - count]
-    units = part_ref.shape[0] * blocks
-    copies = fetched(refs[:count], refs[-1 - count:-1], refs[-1])
+def queries_kernel(axes, blocks, count, part_ref, mixed_ref, even_ref, pair_ref, *refs):
+    heads = part_ref.shape[0]
+    units = heads * blocks
+    arrived, weights = refs[:heads], refs[heads:heads + count]
+    inner_ref, moving_ref, *weight_refs = refs[-5 - count:-3]
+    query_ref, sems, query_sems = refs[-3:]
+    place = lax.rem(lax.axis_index(axes[0]), heads)
+    query_copies = fetched(
+        arrived,
+        [query_ref.at[lax.bitwise_xor(place, turn)] for turn in range(heads)],
+        query_sems,
+    )
+    copies = fetched(weights, weight_refs, sems)
+    for copy in query_copies:
+        copy.wait()
     rows, columns = square_iotas()
     current = []
     for unit in range(units):
@@ -426,6 +443,10 @@
         shift = by * heads
         return lax.ppermute(value, "ctx", [(i, i + shift) for i in range(ctx_size - shift)])
 
+    def crossed(value, turn):
+        pairs = [(i, i - i % heads + (i % heads ^ turn)) for i in range(ctx_size)]
+        return lax.ppermute(value, "ctx", pairs) if turn else value
+
     def array(shape, kind=BF16):
         return jax.ShapeDtypeStruct(shape, kind)
 
@@ -458,8 +479,8 @@
     own_values = parts[:, 2 * tokens:3 * tokens].reshape(units, *tile)
     value_parts = [onward(own_values, by) for by in range(1, before + 1)]
 
-    end, tail, far, even, pair_map, group_map, mixed, away, cut = call(
-        functools.partial(keys_kernel, blocks),
+    end, tail, far, even, pair_map, group_map, mixed, away, *cut = call(
+        functools.partial(keys_kernel, axes, blocks),
         [
             array((units, *tile)),
             array((units, *tile)),
@@ -469,8 +490,8 @@
             array((2, *tile)),
             array((units, BLOCK, 2 * BLOCK)),
             array((units, HEAD_DIM), jnp.int32),
-            array((heads, tokens, HEAD_DIM)),
-        ],
+        ]
+        + [array((tokens, HEAD_DIM))] * heads,
         [VMEM, ANY],
         400 * cubes,
         [
@@ -478,19 +499,23 @@
             pltpu.SemaphoreType.DMA((heads,)),
             pltpu.SemaphoreType.DMA((heads,)),
         ],
-        [VMEM] * 8 + [ANY],
+        [VMEM] * 8 + [ANY] * heads,
     )(parts, queries)
     far_parts = [onward(far, by) for by in range(1, before + 1)]
     map_parts = [onward(group_map, by) for by in range(1, before)]
-    query_parts = exchange(cut)
+    query_parts = [crossed(cut[turn], turn) for turn in range(heads)]
     inner, moving, *weight_parts = call(
-        functools.partial(queries_kernel, blocks, len(weight_parts)),
+        functools.partial(queries_kernel, axes, blocks, len(weight_parts)),
         [array((units, BLOCK, BLOCK), F32), array((units, pairs + 1, *tile))]
         + [array(part.shape) for part in weight_parts],
-        [VMEM] * 5 + [ANY] * (len(weight_parts) + before),
+        [VMEM] * 4 + [ANY] * (heads + len(weight_parts) + before),
         200 * cubes,
-        [pltpu.SemaphoreType.DMA((max(len(weight_parts), 1),))],
-    )(parts, query_parts, mixed, even, pair_map, *weight_parts, *value_parts)
+        [
+            pltpu.VMEM((heads, tokens, HEAD_DIM), BF16),
+            pltpu.SemaphoreType.DMA((max(len(weight_parts), 1),)),
+            pltpu.SemaphoreType.DMA((heads,)),
+        ],
+    )(parts, mixed, even, pair_map, *query_parts, *weight_parts, *value_parts)
     attended = call(
         functools.partial(attend_kernel, before, blocks),
         array((heads, planes, blocks, *tile)),

time: 81 us -> 64.1 us (0.79)
  blocking collectives: 24.2 us -> 15.6 us
  local copies, waits for them, and re-layouts: 8.35 us -> 1.1 us
    all_to_all x1, blocking collectives: 24.2 us -> 15.6 us  [body(): lax.all_to_all(attended.reshape(heads * planes, blocks, *tile), axes, 0,...]
    unnamed x26 -> x4, local copies, waits for them, and re-layouts: 7.26 us -> 0.01 us
    ppermute x2, waiting for transfers between devices: 4.78 us -> 0.01 us  [onward(): lax.ppermute(value, 'ctx', [(i, i + shift) for i in range(ctx_size - shif...]
    ppermute x0 -> x3, waiting for transfers between devices: none -> 4.12 us  [crossed(): return lax.ppermute(value, 'ctx', pairs) if turn else value]
    ppermute x0 -> x3, starting transfers between devices: none -> 3.55 us  [crossed(): return lax.ppermute(value, 'ctx', pairs) if turn else value]
    all_to_all x2 -> x1, starting transfers between devices: 8.8 us -> 5.39 us  [exchange(): lax.all_to_all(value, 'ctx', 0, 0, axis_index_groups=members, tiled=True)]
    all_to_all x2 -> x1, waiting for transfers between devices: 8.45 us -> 8.44 us  [exchange(): lax.all_to_all(value, 'ctx', 0, 0, axis_index_groups=members, tiled=True)]
  transfers between devices with their start and end apart: 6 -> 8, of which waited for: 3 -> 5; matrix products, arithmetic and copies ran while one was open for 1% -> 2% of each run, Pallas kernels for 13% -> 17%
where the time goes in v8:
time: 64.1 us; the launch traced here: 63.8 us
  Pallas kernels  16.3 us (25%)
  starting transfers between devices  16.3 us (25%)
  blocking collectives  15.6 us (24%)
  waiting for transfers between devices  13.6 us (21%)
  local copies, waits for them, and re-layouts  1.1 us (2%)
  other arithmetic  0.77 us (1%)
    all_to_all x1, blocking collectives, body(): lax.all_to_all(attended.reshape(heads * planes, blocks, *tile), axes, 0,...  15.6 us
    all_to_all x1, waiting for transfers between devices, exchange(): lax.all_to_all(value, 'ctx', 0, 0, axis_index_groups=members, tiled=True)  8.44 us
    pallas_call x1, Pallas kernels, body(): call(functools.partial(keys_kernel, axes, blocks), [array((units, *tile))...  8.29 us
    ppermute x2, starting transfers between devices, onward(): lax.ppermute(value, 'ctx', [(i, i + shift) for i in range(ctx_size - shif...  5.81 us
    all_to_all x1, starting transfers between devices, exchange(): lax.all_to_all(value, 'ctx', 0, 0, axis_index_groups=members, tiled=True)  5.39 us
    ppermute x3, waiting for transfers between devices, crossed(): return lax.ppermute(value, 'ctx', pairs) if turn else value  4.12 us
    ppermute x3, starting transfers between devices, crossed(): return lax.ppermute(value, 'ctx', pairs) if turn else value  3.55 us
    pallas_call x1, Pallas kernels, body(): call(functools.partial(attend_kernel, before, blocks), array((heads, plan...  2.5 us
  transfers between devices with their start and end apart: 8, of which 5 were waited for; matrix products, arithmetic and copies ran while one was open for 2% of the time, Pallas kernels for 17%

profile of v8, /device:TPU:0, one launch (start us, length us, event | category | flops | bytes accessed | tf_op | source)
XLA Modules:
  0.0 63.8 jit_solution(11971647475531667304)
XLA Ops:
  0.0 2.2 %shard_map.73 = bf16[4,784,128]{2,1,0:T(8,128)(2,1)} custom-call(bf16[256,512]{1,0:T(8,128)(2,1)} %d_ref.1, bf16[256,512]{1,0:T(8,128)(2,1)} %k_ref.1, bf16[256,512]{1,0:T(8,128)(2,1)} %v_ref.1, f32[4,256]{1,0:T(4,128)} %rates_hbm.1, s32[2,4]{1,0:T(2,128)} %selected_hbm.1), custom_call_target="tpu_custom_call" | custom-call | flops 4194304 | bytes 2097152 | tf_op jit(solution)/shard_map/pallas_call | solution.py:454
  2.2 0.0 copy-start.1
  2.3 5.4 %all-to-all-start = ((bf16[4,784,128]{2,1,0:T(8,128)(2,1)}), bf16[4,784,128]{2,1,0:T(8,128)(2,1)S(1)}, u32[]{:S(2)}, u32[]{:S(2)}) async-start(bf16[4,784,128]{2,1,0:T(8,128)(2,1)} %shard_map.73), calls=%async_computation | async-start | bytes 1605632 | tf_op jit(solution)/shard_map/all_to_all | solution.py:440
  7.7 1.1 %constant_dynamic-slice_fusion = bf16[512,1024]{1,0:T(8,128)(2,1)} fusion(bf16[512,2048]{1,0:T(8,128)(2,1)S(1)} %copy-done, s32[]{:T(128)S(6)} %select_n.9), kind=kLoop, calls=%fused_computation.1 | loop fusion | bytes 2097156 | tf_op jit(solution)/shard_map/dynamic_slice | solution.py:476
  8.7 1.5 %collective-permute-start.3 = (bf16[512,1024]{1,0:T(8,128)(2,1)}, bf16[512,1024]{1,0:T(8,128)(2,1)}, u32[]{:S(2)}, u32[]{:S(2)}) collective-permute-start(bf16[512,1024]{1,0:T(8,128)(2,1)} %constant_dynamic-slice_fusion), channel_id=1, source_target_pairs={{0,2},{1,3},{2,0},{3,1},{4,6},{5,7},{6,4},{7,5},{8,10},{9,11},{10,... | collective-permute-start | bytes 3145736 | tf_op jit(solution)/shard_map/ppermute | solution.py:477
  10.2 8.4 %all-to-all-done.part_ref = bf16[4,784,128]{2,1,0:T(8,128)(2,1)S(1)} async-done(((bf16[4,784,128]{2,1,0:T(8,128)(2,1)}), bf16[4,784,128]{2,1,0:T(8,128)(2,1)S(1)}, u32[]{:S(2)}, u32[]{:S(2)}) %all-to-all-start) | async-done | bytes 802848 | tf_op jit(solution)/shard_map/all_to_all | solution.py:440
  18.7 4.5 %collective-permute-start.4 = (bf16[8,128,128]{2,1,0:T(8,128)(2,1)S(1)}, bf16[8,128,128]{2,1,0:T(8,128)(2,1)S(1)}, u32[]{:S(2)}, u32[]{:S(2)}) collective-permute-start(bf16[8,128,128]{2,1,0:T(8,128)(2,1)S(1)} %bitcast.6), channel_id=1, source_target_pairs={{0,16},{4,20},{8,24},{12,28},{1,17},{5,21},{9,25},{13,29},{2,18},{... | collective-permute-start | bytes 786440 | tf_op jit(solution)/shard_map/ppermute | solution.py:444
  23.2 8.3 %shard_map.74 = (bf16[8,128,128]{2,1,0:T(8,128)(2,1)S(1)}, bf16[8,128,128]{2,1,0:T(8,128)(2,1)S(1)}, bf16[8,128,128]{2,1,0:T(8,128)(2,1)S(1)}, bf16[4,2,128,128]...) custom-call(bf16[4,784,128]{2,1,0:T(8,128)(2,1)S(1)} %all-to-all-don, ...), custom_call_target="tpu_custom_call" | custom-call | flops 1677721600 | bytes 2097152 | tf_op jit(solution)/shard_map/pallas_call | solution.py:482
  31.5 1.3 %collective-permute-start.5 = (bf16[8,128,128]{2,1,0:T(8,128)(2,1)S(1)}, bf16[8,128,128]{2,1,0:T(8,128)(2,1)S(1)}, u32[]{:S(2)}, u32[]{:S(2)}) collective-permute-start(bf16[8,128,128]{2,1,0:T(8,128)(2,1)S(1)} %get-tuple-element.31), channel_id=1, source_target_pairs={{0,16},{4,20},{8,24},{12,28},{1,17},{5,21},{9,25},{13,29},{2,18},{... | collective-permute-start | bytes 786440 | tf_op jit(solution)/shard_map/ppermute | solution.py:444
  32.8 1.5 %collective-permute-start = (bf16[256,128]{1,0:T(8,128)(2,1)S(1)}, bf16[256,128]{1,0:T(8,128)(2,1)S(1)}, u32[]{:S(2)}, u32[]{:S(2)}) collective-permute-start(bf16[256,128]{1,0:T(8,128)(2,1)S(1)} %get-tuple-element.24), channel_id=1, source_target_pairs={{0,4},{4,0},{8,12},{12,8},{16,20},{20,16},{24,28},{28,24},{1,5},{5... | collective-permute-start | bytes 196616 | tf_op jit(solution)/shard_map/ppermute | solution.py:448
  34.3 0.6 collective-permute-start.1
  34.9 1.5 %collective-permute-start.2 = (bf16[256,128]{1,0:T(8,128)(2,1)S(1)}, bf16[256,128]{1,0:T(8,128)(2,1)S(1)}, u32[]{:S(2)}, u32[]{:S(2)}) collective-permute-start(bf16[256,128]{1,0:T(8,128)(2,1)S(1)} %get-tuple-element.26), channel_id=1, source_target_pairs={{0,12},{4,8},{8,4},{12,0},{16,28},{20,24},{24,20},{28,16},{1,13},{... | collective-permute-start | bytes 196616 | tf_op jit(solution)/shard_map/ppermute | solution.py:448
  36.4 0.8 %collective-permute-done.refs_1_ = bf16[256,128]{1,0:T(8,128)(2,1)S(1)} collective-permute-done((bf16[256,128]{1,0:T(8,128)(2,1)S(1)}, bf16[256,128]{1,0:T(8,128)(2,1)S(1)}, u32[]{:S(2)}, u32[]{:S(2)}) %collective-permute-start) | collective-permute-done | bytes 65568 | tf_op jit(solution)/shard_map/ppermute | solution.py:448
  37.1 2.6 %collective-permute-done.1.refs_2_ = bf16[256,128]{1,0:T(8,128)(2,1)S(1)} collective-permute-done((bf16[256,128]{1,0:T(8,128)(2,1)S(1)}, bf16[256,128]{1,0:T(8,128)(2,1)S(1)}, u32[]{:S(2)}, u32[]{:S(2)}) %collective-permute-start.1) | collective-permute-done | bytes 65568 | tf_op jit(solution)/shard_map/ppermute | solution.py:448
  39.8 0.7 %collective-permute-done.2.refs_3_ = bf16[256,128]{1,0:T(8,128)(2,1)S(1)} collective-permute-done((bf16[256,128]{1,0:T(8,128)(2,1)S(1)}, bf16[256,128]{1,0:T(8,128)(2,1)S(1)}, u32[]{:S(2)}, u32[]{:S(2)}) %collective-permute-start.2) | collective-permute-done | bytes 65568 | tf_op jit(solution)/shard_map/ppermute | solution.py:448
  40.5 0.0 collective-permute-done.4.refs_5_.refs_0_
  40.5 2.4 %shard_map.75 = (f32[8,128,128]{2,1,0:T(8,128)S(1)}, bf16[8,5,128,128]{3,2,1,0:T(8,128)(2,1)S(1)}, bf16[512,1024]{1,0:T(8,128)(2,1)S(1)}) custom-call(bf16[4,784,128]{2,1,0:T(8,128)(2,1)S(1)} %all-to-all-done.part_ref, bf16[8,128,256]{2,1,0:T(8,128)(2,1)S(1)} %get-tuple-element.20.mixed_ref, bf16[4,2,128,128]{3,2,1,0:T(8,128)(2,1)S(1)} %get-tuple-element.21.even_ref, ...), custom_call_target="tpu_custom_call" | custom-call | flops 838860800 | bytes 2097152 | tf_op jit(solution)/shard_map/pallas_call | solution.py:507
  42.9 2.5 %shard_map.76 = bf16[4,2,2,128,128]{4,3,2,1,0:T(8,128)(2,1)S(1)} custom-call(s32[8,128]{1,0:T(8,128)S(1)} %get-tuple-element.19.away_ref, bf16[8,5,128,128]{3,2,1,0:T(8,128)(2,1)S(1)} %get-tuple-element.27.moving_ref, f32[8,128,128]{2,1,0:T(8,128)S(1)} %get-tuple-element.28.inner_ref, bf16[8,128,128]{2,1,0:T(8,128)(2,1)S(1)} %get-tuple-element.29.end_ref, ...), custom_call_target="tpu_custom_call" | custom-call | flops 838860800 | bytes 2097152 | tf_op jit(solution)/shard_map/pallas_call | solution.py:519
  45.4 15.6 %all_to_all.10 = bf16[8,2,128,128]{3,2,1,0:T(8,128)(2,1)S(1)} all-to-all(bf16[8,2,128,128]{3,2,1,0:T(8,128)(2,1)S(1)} %bitcast.5), channel_id=1, replica_groups={{0,2,4,6,8,10,12,14},{1,3,5,7,9,11,13,15},{16,18,20,22,24,26,28,30},{17..., dimensions={0} | all-to-all | bytes 1048576 | tf_op jit(solution)/shard_map/all_to_all | solution.py:535
  61.0 0.4 shard_map.78
  61.4 0.1 collective-permute-start.6
  61.5 0.4 shard_map.77
  62.0 1.1 %collective-permute-done.6 = bf16[256,512]{1,0:T(8,128)(2,1)S(1)} collective-permute-done((bf16[256,512]{1,0:T(8,128)(2,1)S(1)}, bf16[256,512]{1,0:T(8,128)(2,1)S(1)}, u32[]{:S(2)}, u32[]{:S(2)}) %collective-permute-start.6) | collective-permute-done | bytes 262176 | tf_op jit(solution)/shard_map/ppermute | solution.py:548
  63.0 0.8 %add_convert_fusion = bf16[256,512]{1,0:T(8,128)(2,1)} fusion(f32[256,512]{1,0:T(8,128)S(1)} %shard_map.77, bf16[256,512]{1,0:T(8,128)(2,1)S(1)} %collective-permute-done.6), kind=kLoop, calls=%fused_computation | loop fusion | flops 393216 | bytes 1048576 | tf_op jit(solution)/shard_map/convert_element_type | solution.py:549
  (6 shorter events, 0.0 us)
Async XLA Ops:
  0.0 7.7 %copy-start = (bf16[512,2048]{1,0:T(8,128)(2,1)S(1)}, bf16[512,2048]{1,0:T(8,128)(2,1)}, u32[]{:S(2)}) copy-start(bf16[512,2048]{1,0:T(8,128)(2,1)} %own_ref.3) | copy-start | bytes 6291460
  2.2 21.0 %copy-start.1 = (bf16[256,512]{1,0:T(8,128)(2,1)S(1)}, bf16[256,512]{1,0:T(8,128)(2,1)}, u32[]{:S(2)}) copy-start(bf16[256,512]{1,0:T(8,128)(2,1)} %queries_ref.1) | copy-start | bytes 786436
  2.3 16.4 %all-to-all-start = ((bf16[4,784,128]{2,1,0:T(8,128)(2,1)}), bf16[4,784,128]{2,1,0:T(8,128)(2,1)S(1)}, u32[]{:S(2)}, u32[]{:S(2)}) async-start(bf16[4,784,128]{2,1,0:T(8,128)(2,1)} %shard_map.73), calls=%async_computation | async-start | bytes 1605632 | tf_op jit(solution)/shard_map/all_to_all | solution.py:440
  8.7 26.2 %collective-permute-start.3 = (bf16[512,1024]{1,0:T(8,128)(2,1)}, bf16[512,1024]{1,0:T(8,128)(2,1)}, u32[]{:S(2)}, u32[]{:S(2)}) collective-permute-start(bf16[512,1024]{1,0:T(8,128)(2,1)} %constant_dynamic-slice_fusion), channel_id=1, source_target_pairs={{0,2},{1,3},{2,0},{3,1},{4,6},{5,7},{6,4},{7,5},{8,10},{9,11},{10,... | collective-permute-start | bytes 3145736 | tf_op jit(solution)/shard_map/ppermute | solution.py:477
  18.7 21.8 %collective-permute-start.4 = (bf16[8,128,128]{2,1,0:T(8,128)(2,1)S(1)}, bf16[8,128,128]{2,1,0:T(8,128)(2,1)S(1)}, u32[]{:S(2)}, u32[]{:S(2)}) collective-permute-start(bf16[8,128,128]{2,1,0:T(8,128)(2,1)S(1)} %bitcast.6), channel_id=1, source_target_pairs={{0,16},{4,20},{8,24},{12,28},{1,17},{5,21},{9,25},{13,29},{2,18},{... | collective-permute-start | bytes 786440 | tf_op jit(solution)/shard_map/ppermute | solution.py:444
  31.5 11.4 %collective-permute-start.5 = (bf16[8,128,128]{2,1,0:T(8,128)(2,1)S(1)}, bf16[8,128,128]{2,1,0:T(8,128)(2,1)S(1)}, u32[]{:S(2)}, u32[]{:S(2)}) collective-permute-start(bf16[8,128,128]{2,1,0:T(8,128)(2,1)S(1)} %get-tuple-element.31), channel_id=1, source_target_pairs={{0,16},{4,20},{8,24},{12,28},{1,17},{5,21},{9,25},{13,29},{2,18},{... | collective-permute-start | bytes 786440 | tf_op jit(solution)/shard_map/ppermute | solution.py:444
  32.8 4.3 %collective-permute-start = (bf16[256,128]{1,0:T(8,128)(2,1)S(1)}, bf16[256,128]{1,0:T(8,128)(2,1)S(1)}, u32[]{:S(2)}, u32[]{:S(2)}) collective-permute-start(bf16[256,128]{1,0:T(8,128)(2,1)S(1)} %get-tuple-element.24), channel_id=1, source_target_pairs={{0,4},{4,0},{8,12},{12,8},{16,20},{20,16},{24,28},{28,24},{1,5},{5... | collective-permute-start | bytes 196616 | tf_op jit(solution)/shard_map/ppermute | solution.py:448
  34.3 5.4 %collective-permute-start.1 = (bf16[256,128]{1,0:T(8,128)(2,1)S(1)}, bf16[256,128]{1,0:T(8,128)(2,1)S(1)}, u32[]{:S(2)}, u32[]{:S(2)}) collective-permute-start(bf16[256,128]{1,0:T(8,128)(2,1)S(1)} %get-tuple-element.25), channel_id=1, source_target_pairs={{0,8},{4,12},{8,0},{12,4},{16,24},{20,28},{24,16},{28,20},{1,9},{5... | collective-permute-start | bytes 196616 | tf_op jit(solution)/shard_map/ppermute | solution.py:448
  34.9 5.6 %collective-permute-start.2 = (bf16[256,128]{1,0:T(8,128)(2,1)S(1)}, bf16[256,128]{1,0:T(8,128)(2,1)S(1)}, u32[]{:S(2)}, u32[]{:S(2)}) collective-permute-start(bf16[256,128]{1,0:T(8,128)(2,1)S(1)} %get-tuple-element.26), channel_id=1, source_target_pairs={{0,12},{4,8},{8,4},{12,0},{16,28},{20,24},{24,20},{28,16},{1,13},{... | collective-permute-start | bytes 196616 | tf_op jit(solution)/shard_map/ppermute | solution.py:448
  61.4 1.6 %collective-permute-start.6 = (bf16[256,512]{1,0:T(8,128)(2,1)S(1)}, bf16[256,512]{1,0:T(8,128)(2,1)S(1)}, u32[]{:S(2)}, u32[]{:S(2)}) collective-permute-start(bf16[256,512]{1,0:T(8,128)(2,1)S(1)} %shard_map.78), channel_id=1, source_target_pairs={{0,1},{1,0},{2,3},{3,2},{4,5},{5,4},{6,7},{7,6},{8,9},{9,8},{10,11... | collective-permute-start | bytes 786440 | tf_op jit(solution)/shard_map/ppermute | solution.py:548

commit v9 on v8

--- a/solution.py
+++ b/solution.py
@@ -64,14 +64,14 @@
     return copies
 
 
-def pack_kernel(axes, d_ref, k_ref, v_ref, rates_hbm, selected_hbm, out_ref, parts_ref,
+def pack_kernel(axes, d_ref, k_ref, rates_hbm, selected_hbm, out_ref, parts_ref,
                 rates_ref, selected_ref, sems, few_sems, out_sems):
     tokens = d_ref.shape[0]
     heads = d_ref.shape[1] // HEAD_DIM
     blocks = tokens // BLOCK
     first_block = lax.axis_index(axes[0]) * blocks
     few_copies = fetched([rates_hbm, selected_hbm], [rates_ref, selected_ref], few_sems)
-    sources = (d_ref, k_ref, v_ref)
+    sources = (d_ref, k_ref)
     copies = []
     for head in range(heads):
         columns = pl.ds(head * HEAD_DIM, HEAD_DIM)
@@ -117,6 +117,62 @@
         copy.wait()
 
 
+def early_kernel(axes, cores, weight_ref, values_ref, after, *refs):
+    count = (len(refs) - 5) // 2 + 1
+    weight_outs, values_out = refs[:count], refs[count]
+    weight_bufs, values_buf = refs[count + 1:2 * count + 1], refs[2 * count + 1]
+    sems, out_sems = refs[2 * count + 2:]
+    width = weight_outs[0].shape[1]
+    planes = weight_ref.shape[1] // width
+    plane = lax.axis_index(axes[1]) // cores
+    sources = [values_ref]
+    for offset in range(1, planes):
+        start = lax.rem(plane + planes - offset, planes) * width
+        sources.append(weight_ref.at[:, pl.ds(pl.multiple_of(start, width), width)])
+    buffers = [values_buf, *weight_bufs]
+    copies = fetched(sources, buffers, sems)
+    out_copies = []
+    for index, target in enumerate([values_out, *weight_outs]):
+        copies[index].wait()
+        out_copies += fetched([buffers[index]], [target], out_sems.at[pl.ds(index, 1)])
+    for copy in out_copies:
+        copy.wait()
+
+
+def cut_kernel(axes, *refs):
+    sems = refs[-1]
+    parts = refs[-1 - sems.shape[0]:-1]
+    sources = refs[:sems.shape[1]]
+    heads = sems.shape[0]
+    place = lax.rem(lax.axis_index(axes[0]), heads)
+    copies = []
+    for turn in range(heads):
+        cut = pl.multiple_of(lax.bitwise_xor(place, turn) * HEAD_DIM, HEAD_DIM)
+        copies += fetched(
+            [source.at[:, pl.ds(cut, HEAD_DIM)] for source in sources],
+            [parts[turn].at[kind] for kind in range(len(sources))],
+            sems.at[turn],
+        )
+    for copy in copies:
+        copy.wait()
+
+
+def order_kernel(axes, *refs):
+    values_ref, sems = refs[-2:]
+    kinds, heads = values_ref.shape[:2]
+    place = lax.rem(lax.axis_index(axes[0]), heads)
+    copies = []
+    for turn in range(heads):
+        source = lax.bitwise_xor(place, turn)
+        parts = [refs[turn].at[1]]
+        parts += [refs[heads + turn].at[kind] for kind in range(kinds - 1)]
+        copies += fetched(
+            parts, [values_ref.at[kind, source] for kind in range(kinds)], sems.at[turn]
+        )
+    for copy in copies:
+        copy.wait()
+
+
 def rows_of(ref, blocks, unit, kind):
     start = (kind * blocks + unit % blocks) * BLOCK
     return ref[unit // blocks, start:start + BLOCK]
@@ -171,7 +227,7 @@
         tick += 1
 
 
-def keys_kernel(axes, blocks, part_ref, queries_ref, end_ref, tail_ref, far_ref, even_ref,
+def keys_kernel(axes, blocks, part_ref, queries_ref, values_ref, end_ref, tail_ref, far_ref, even_ref,
                 pair_ref, group_ref, mixed_ref, away_ref, *refs):
     heads = part_ref.shape[0]
     units = heads * blocks
@@ -181,11 +237,14 @@
     cuts = [
         pl.multiple_of(lax.bitwise_xor(place, turn) * HEAD_DIM, HEAD_DIM) for turn in range(heads)
     ]
-    query_copies = fetched(
-        [queries_ref.at[:, pl.ds(cut, HEAD_DIM)] for cut in cuts],
-        [cut_ref.at[turn] for turn in range(heads)],
-        sems,
-    )
+    cut_copies = [
+        fetched(
+            [ref.at[:, pl.ds(cut, HEAD_DIM)] for ref in (queries_ref, values_ref)],
+            [cut_ref.at[turn, 0], cut_ref.at[turn, 1]],
+            sems.at[turn],
+        )
+        for turn, cut in enumerate(cuts)
+    ]
     rows, columns = square_iotas()
     diagonal = rows == columns
     identity = diagonal.astype(F32)
@@ -196,7 +255,7 @@
     def terms(unit):
         direction = rows_of(part_ref, blocks, unit, 0)
         key = rows_of(part_ref, blocks, unit, 1)
-        extra = part_ref[unit // blocks, 3 * blocks * BLOCK:].astype(F32)
+        extra = part_ref[unit // blocks, 2 * blocks * BLOCK:].astype(F32)
         first = TERMS * (unit % blocks)
         rate = extra[first:first + 1] + extra[first + 1:first + 2] + extra[first + 2:first + 3]
         listed = TERMS * blocks + unit % blocks
@@ -237,23 +296,21 @@
     interleaved([terms(unit) for unit in range(units)], 1)
     out_copies = []
     for turn in range(heads):
-        query_copies[turn].wait()
-        out_copies.append(
-            pltpu.make_async_copy(cut_ref.at[turn], out_refs[turn], out_sems.at[turn])
-        )
-        out_copies[-1].start()
+        for copy in cut_copies[turn]:
+            copy.wait()
+        out_copies += fetched([cut_ref.at[turn]], [out_refs[turn]], out_sems.at[pl.ds(turn, 1)])
     pair_keys, pair_maps = [], []
     for pair in range(units // 2):
         even, odd = 2 * pair, 2 * pair + 1
         even_ref[pair, 0] = maps[even][0]
         even_ref[pair, 1] = maps[even][1]
-        end = split(ends[even])
-        left = tuple(jnp.concatenate([end[part], maps[even][part]], 0) for part in range(2))
-        both = triple(nn, left, maps[odd])
+        left = jnp.concatenate([ends[even].astype(BF16), *maps[even]], 0)
+        both = nn(left, maps[odd][0])
         tail_ref[even] = both[:BLOCK].astype(BF16)
         tail_ref[odd] = ends[odd].astype(BF16)
         pair_keys.append(jnp.concatenate([both[:BLOCK], ends[odd]], 0))
-        pair_maps.append(split(both[BLOCK:]))
+        low = both[2 * BLOCK:] + nn(maps[even][0], maps[odd][1])
+        pair_maps.append(split(both[BLOCK:2 * BLOCK] + low))
         pair_ref[pair, 0] = pair_maps[pair][0]
         pair_ref[pair, 1] = pair_maps[pair][1]
     onward = None
@@ -262,7 +319,7 @@
         if onward is None:
             onward = pair_maps[pair]
         else:
-            far = triple(nn, split(far), onward)
+            far = nn(far.astype(BF16), onward[0])
             onward = split(triple(nn, pair_maps[pair], onward))
         far_ref[2 * pair] = far[:BLOCK].astype(BF16)
         far_ref[2 * pair + 1] = far[BLOCK:].astype(BF16)
@@ -276,11 +333,11 @@
     heads = part_ref.shape[0]
     units = heads * blocks
     arrived, weights = refs[:heads], refs[heads:heads + count]
-    inner_ref, moving_ref, *weight_refs = refs[-5 - count:-3]
+    inner_ref, moving_ref, *weight_refs = refs[heads + count:-3]
     query_ref, sems, query_sems = refs[-3:]
     place = lax.rem(lax.axis_index(axes[0]), heads)
     query_copies = fetched(
-        arrived,
+        [part.at[0] for part in arrived],
         [query_ref.at[lax.bitwise_xor(place, turn)] for turn in range(heads)],
         query_sems,
     )
@@ -334,10 +391,9 @@
     return jnp.clip(source + ahead * units, 0, units - 1), source < (1 - ahead) * units
 
 
-def attend_kernel(before, blocks, away_ref, moving_ref, inner_ref, end_ref, tail_ref, part_ref,
-                  *refs):
-    values, far_keys = refs[:before], refs[before:2 * before]
-    group_maps, out_ref = refs[2 * before:-1], refs[-1]
+def attend_kernel(before, blocks, away_ref, moving_ref, inner_ref, end_ref, tail_ref,
+                  values_ref, *refs):
+    far_keys, group_maps, out_ref = refs[:before], refs[before:-1], refs[-1]
     units = inner_ref.shape[0]
     rows, columns = square_iotas()
     scale = HEAD_DIM ** (-0.5)
@@ -349,20 +405,19 @@
             passed = nt(fronts[-1], group_map[0]) + nt(fronts[-1], group_map[1])
             fronts.append(passed.astype(BF16))
         score_list = [jnp.where(rows >= columns, inner_ref[unit] * scale, -1e30)]
-        value_list = [rows_of(part_ref, blocks, unit, 2)]
+        value_list = [values_ref[0, unit]]
         for entry in range(1, TOPK):
             source, new = listed_block(away_ref, unit, entry)
             inside = jnp.maximum(source, 0)
             step = jnp.maximum(pair - inside // 2, 0)
-            start = pl.multiple_of((2 * blocks + lax.rem(inside, blocks)) * BLOCK, BLOCK)
             query = moving_ref[unit, step]
             key = jnp.where(step == 0, end_ref[inside], tail_ref[inside])
-            value = part_ref[inside // blocks, pl.ds(start, BLOCK)]
+            value = values_ref[0, inside]
             for ahead in range(1, before + 1):
                 place, here = earlier(source, ahead, units)
                 query = jnp.where(here, fronts[ahead - 1], query)
                 key = jnp.where(here, far_keys[ahead - 1][place], key)
-                value = jnp.where(here, values[ahead - 1][place], value)
+                value = jnp.where(here, values_ref[ahead, place], value)
             score_list.append(jnp.where(new, nt(query, key) * scale, -1e30))
             value_list.append(value)
         yield
@@ -450,34 +505,41 @@
     def array(shape, kind=BF16):
         return jax.ShapeDtypeStruct(shape, kind)
 
-    part_shape = (heads, 3 * tokens + EXTRA, HEAD_DIM)
+    part_shape = (heads, 2 * tokens + EXTRA, HEAD_DIM)
     packed = call(
         functools.partial(pack_kernel, axes),
         array(part_shape),
-        [ANY] * 5,
+        [ANY] * 4,
         cubes,
         [
             pltpu.VMEM(part_shape, BF16),
             pltpu.VMEM(rates.shape, F32),
             pltpu.SMEM(selected.shape, jnp.int32),
-            pltpu.SemaphoreType.DMA((heads, 3)),
+            pltpu.SemaphoreType.DMA((heads, 2)),
             pltpu.SemaphoreType.DMA((2,)),
             pltpu.SemaphoreType.DMA((heads,)),
         ],
         ANY,
         56,
-    )(directions, keys, values, rates, selected)
-    plane = lax.axis_index("head") // cores
+    )(directions, keys, rates, selected)
     width = out_weight.shape[1] // planes
+    early_shapes = [(out_weight.shape[0], width)] * (planes - 1) + [values.shape]
+    *pieces, raw_values = call(
+        functools.partial(early_kernel, axes, cores),
+        [array(shape) for shape in early_shapes],
+        [ANY] * 3,
+        cubes,
+        [pltpu.VMEM(shape, BF16) for shape in early_shapes]
+        + [pltpu.SemaphoreType.DMA((planes,))] * 2,
+        [ANY] * planes,
+        56,
+    )(out_weight, values, packed)
     weight_parts = []
     for offset in range(1, planes):
-        start = lax.rem(plane + planes - offset, planes) * width
         turned = [(g, (g + head_size - cores * offset) % head_size) for g in range(head_size)]
-        piece = lax.dynamic_slice_in_dim(out_weight, start, width, 1)
-        weight_parts.append(lax.ppermute(piece, "head", turned))
+        weight_parts.append(lax.ppermute(pieces[offset - 1], "head", turned))
+    value_parts = [onward(raw_values, by) for by in range(1, before + 1)]
     parts = exchange(packed)
-    own_values = parts[:, 2 * tokens:3 * tokens].reshape(units, *tile)
-    value_parts = [onward(own_values, by) for by in range(1, before + 1)]
 
     end, tail, far, even, pair_map, group_map, mixed, away, *cut = call(
         functools.partial(keys_kernel, axes, blocks),
@@ -491,37 +553,54 @@
             array((units, BLOCK, 2 * BLOCK)),
             array((units, HEAD_DIM), jnp.int32),
         ]
-        + [array((tokens, HEAD_DIM))] * heads,
-        [VMEM, ANY],
+        + [array((2, tokens, HEAD_DIM))] * heads,
+        [VMEM, ANY, ANY],
         400 * cubes,
         [
-            pltpu.VMEM((heads, tokens, HEAD_DIM), BF16),
-            pltpu.SemaphoreType.DMA((heads,)),
+            pltpu.VMEM((heads, 2, tokens, HEAD_DIM), BF16),
+            pltpu.SemaphoreType.DMA((heads, 2)),
             pltpu.SemaphoreType.DMA((heads,)),
         ],
         [VMEM] * 8 + [ANY] * heads,
-    )(parts, queries)
+    )(parts, queries, values)
     far_parts = [onward(far, by) for by in range(1, before + 1)]
     map_parts = [onward(group_map, by) for by in range(1, before)]
-    query_parts = [crossed(cut[turn], turn) for turn in range(heads)]
+    arrived = [crossed(cut[turn], turn) for turn in range(heads)]
+    arrived_values = []
+    if before:
+        cut = call(
+            functools.partial(cut_kernel, axes),
+            [array((before, tokens, HEAD_DIM))] * heads,
+            [ANY] * (before + 1),
+            1000 * cubes,
+            [pltpu.SemaphoreType.DMA((heads, before))],
+        )(*value_parts, away)
+        arrived_values = [crossed(cut[turn], turn) for turn in range(heads)]
     inner, moving, *weight_parts = call(
         functools.partial(queries_kernel, axes, blocks, len(weight_parts)),
         [array((units, BLOCK, BLOCK), F32), array((units, pairs + 1, *tile))]
         + [array(part.shape) for part in weight_parts],
-        [VMEM] * 4 + [ANY] * (heads + len(weight_parts) + before),
+        [VMEM] * 4 + [ANY] * (heads + len(weight_parts)),
         200 * cubes,
         [
             pltpu.VMEM((heads, tokens, HEAD_DIM), BF16),
             pltpu.SemaphoreType.DMA((max(len(weight_parts), 1),)),
             pltpu.SemaphoreType.DMA((heads,)),
         ],
-    )(parts, mixed, even, pair_map, *query_parts, *weight_parts, *value_parts)
+    )(parts, mixed, even, pair_map, *arrived, *weight_parts)
+    all_values = call(
+        functools.partial(order_kernel, axes),
+        array((1 + before, heads, tokens, HEAD_DIM)),
+        [ANY] * (heads + len(arrived_values)),
+        0,
+        [pltpu.SemaphoreType.DMA((heads, 1 + before))],
+    )(*arrived, *arrived_values).reshape(1 + before, units, *tile)
     attended = call(
         functools.partial(attend_kernel, before, blocks),
         array((heads, planes, blocks, *tile)),
-        [SMEM] + [VMEM] * (5 + 2 * before + len(map_parts)),
+        [SMEM] + [VMEM] * (5 + before + len(map_parts)),
         200 * cubes,
-    )(away, moving, inner, end, tail, parts, *value_parts, *far_parts, *map_parts)
+    )(away, moving, inner, end, tail, all_values, *far_parts, *map_parts)
 
     returns = [
         [

time: 64.1 us -> 67.4 us (1.051)
  starting transfers between devices: 16.3 us -> 25.6 us
  waiting for transfers between devices: 13.6 us -> 8.33 us
  Pallas kernels: 16.3 us -> 19.7 us
  blocking collectives: 15.6 us -> 12.5 us
  local copies, waits for them, and re-layouts: 1.1 us -> 0.02 us
    all_to_all x1, waiting for transfers between devices: 8.44 us -> 0.01 us  [exchange(): lax.all_to_all(value, 'ctx', 0, 0, axis_index_groups=members, tiled=True)]
    ppermute x3 -> x6, starting transfers between devices: 3.55 us -> 8.86 us  [crossed(): return lax.ppermute(value, 'ctx', pairs) if turn else value]
    ppermute x2, starting transfers between devices: 5.81 us -> 9.68 us  [onward(): lax.ppermute(value, 'ctx', [(i, i + shift) for i in range(ctx_size - shif...]
    ppermute x3 -> x6, waiting for transfers between devices: 4.12 us -> 7.25 us  [crossed(): return lax.ppermute(value, 'ctx', pairs) if turn else value]
    all_to_all x1, blocking collectives: 15.6 us -> 12.5 us  [body(): lax.all_to_all(attended.reshape(heads * planes, blocks, *tile), axes, 0,...]
    pallas_call x1 -> x4, Pallas kernels: 2.24 us -> 5.04 us  [the longest x1 2.33 us: body(): call(functools.partial(early_kernel, axes, cores), [array(shape) for shap...]
    dynamic_slice x1 -> x0, local copies, waits for them, and re-layouts: 1.07 us -> none  [body(): piece = lax.dynamic_slice_in_dim(out_weight, start, width, 1)]
  transfers between devices with their start and end apart: 8 -> 11, of which waited for: 5 -> 4; matrix products, arithmetic and copies ran while one was open for 2% -> 0% of each run, Pallas kernels for 17% -> 22%
where the time goes in v9:
time: 67.4 us; the launch traced here: 67.1 us
  starting transfers between devices  25.6 us (38%)
  Pallas kernels  19.7 us (29%)
  blocking collectives  12.5 us (19%)
  waiting for transfers between devices  8.33 us (12%)
  other arithmetic  0.77 us (1%)
    all_to_all x1, blocking collectives, body(): lax.all_to_all(attended.reshape(heads * planes, blocks, *tile), axes, 0,...  12.5 us
    ppermute x2, starting transfers between devices, onward(): lax.ppermute(value, 'ctx', [(i, i + shift) for i in range(ctx_size - shif...  9.68 us
    ppermute x6, starting transfers between devices, crossed(): return lax.ppermute(value, 'ctx', pairs) if turn else value  8.86 us
    pallas_call x1, Pallas kernels, body(): call(functools.partial(keys_kernel, axes, blocks), [array((units, *tile))...  8.8 us
    ppermute x6, waiting for transfers between devices, crossed(): return lax.ppermute(value, 'ctx', pairs) if turn else value  7.25 us
    all_to_all x1, starting transfers between devices, exchange(): lax.all_to_all(value, 'ctx', 0, 0, axis_index_groups=members, tiled=True)  5.39 us
    pallas_call x1, Pallas kernels, body(): call(functools.partial(attend_kernel, before, blocks), array((heads, plan...  2.5 us
    pallas_call x1, Pallas kernels, body(): call(functools.partial(queries_kernel, axes, blocks, len(weight_parts)),...  2.5 us
  transfers between devices with their start and end apart: 11, of which 4 were waited for; matrix products, arithmetic and copies ran while one was open for 0% of the time, Pallas kernels for 22%

profile of v9, /device:TPU:0, one launch (start us, length us, event | category | flops | bytes accessed | tf_op | source)
XLA Modules:
  0.0 67.1 jit_solution(12174571395749990925)
XLA Ops:
  0.0 1.9 %shard_map.73.after = bf16[4,528,128]{2,1,0:T(8,128)(2,1)} custom-call(bf16[256,512]{1,0:T(8,128)(2,1)} %d_ref.1, bf16[256,512]{1,0:T(8,128)(2,1)} %k_ref.1, f32[4,256]{1,0:T(4,128)} %rates_hbm.1, s32[2,4]{1,0:T(2,128)} %selected_hbm.1), custom_call_target="tpu_custom_call" | custom-call | flops 4194304 | bytes 2097152 | tf_op jit(solution)/shard_map/pallas_call | solution.py:509
  1.9 5.4 %all-to-all-start = ((bf16[4,528,128]{2,1,0:T(8,128)(2,1)}), bf16[4,528,128]{2,1,0:T(8,128)(2,1)S(1)}, u32[]{:S(2)}, u32[]{:S(2)}) async-start(bf16[4,528,128]{2,1,0:T(8,128)(2,1)} %shard_map.73.after), calls=%async_computation | async-start | bytes 1081344 | tf_op jit(solution)/shard_map/all_to_all | solution.py:495
  7.3 2.3 %shard_map.75 = (bf16[512,1024]{1,0:T(8,128)(2,1)}, bf16[256,512]{1,0:T(8,128)(2,1)}) custom-call(bf16[512,2048]{1,0:T(8,128)(2,1)} %own_ref.3, bf16[256,512]{1,0:T(8,128)(2,1)} %values_ref.3, bf16[4,528,128]{2,1,0:T(8,128)(2,1)} %shard_map.73.after), custom_call_target="tpu_custom_call" | custom-call | flops 4194304 | bytes 2097152 | tf_op jit(solution)/shard_map/pallas_call | solution.py:527
  9.6 1.6 %collective-permute-start.3 = (bf16[512,1024]{1,0:T(8,128)(2,1)}, bf16[512,1024]{1,0:T(8,128)(2,1)S(1)}, u32[]{:S(2)}, u32[]{:S(2)}) collective-permute-start(bf16[512,1024]{1,0:T(8,128)(2,1)} %get-tuple-element.33), channel_id=1, source_target_pairs={{0,2},{1,3},{2,0},{3,1},{4,6},{5,7},{6,4},{7,5},{8,10},{9,11},{10,... | collective-permute-start | bytes 3145736 | tf_op jit(solution)/shard_map/ppermute | solution.py:540
  11.2 4.5 %collective-permute-start.4 = (bf16[256,512]{1,0:T(8,128)(2,1)}, bf16[256,512]{1,0:T(8,128)(2,1)S(1)}, u32[]{:S(2)}, u32[]{:S(2)}) collective-permute-start(bf16[256,512]{1,0:T(8,128)(2,1)} %get-tuple-element.38), channel_id=1, source_target_pairs={{0,16},{4,20},{8,24},{12,28},{1,17},{5,21},{9,25},{13,29},{2,18},{... | collective-permute-start | bytes 786440 | tf_op jit(solution)/shard_map/ppermute | solution.py:499
  15.7 8.8 %shard_map.74 = (bf16[8,128,128]{2,1,0:T(8,128)(2,1)S(1)}, bf16[8,128,128]{2,1,0:T(8,128)(2,1)S(1)}, bf16[8,128,128]{2,1,0:T(8,128)(2,1)S(1)}, bf16[4,2,128,128]...) custom-call(bf16[4,528,128]{2,1,0:T(8,128)(2,1)S(1)} %all-to-all-don, ...), custom_call_target="tpu_custom_call" | custom-call | flops 1677721600 | bytes 2097152 | tf_op jit(solution)/shard_map/pallas_call | solution.py:544
  24.5 0.1 shard_map.77
  24.7 2.1 %collective-permute-start.5 = (bf16[1,256,128]{2,1,0:T(8,128)(2,1)S(1)}, bf16[1,256,128]{2,1,0:T(8,128)(2,1)S(1)}, u32[]{:S(2)}, u32[]{:S(2)}) collective-permute-start(bf16[1,256,128]{2,1,0:T(8,128)(2,1)S(1)} %get-tuple-element.40), channel_id=1, source_target_pairs={{0,4},{4,0},{8,12},{12,8},{16,20},{20,16},{24,28},{28,24},{1,5},{5... | collective-permute-start | bytes 196616 | tf_op jit(solution)/shard_map/ppermute | solution.py:503
  26.7 3.2 %collective-permute-start.6 = (bf16[1,256,128]{2,1,0:T(8,128)(2,1)S(1)}, bf16[1,256,128]{2,1,0:T(8,128)(2,1)S(1)}, u32[]{:S(2)}, u32[]{:S(2)}) collective-permute-start(bf16[1,256,128]{2,1,0:T(8,128)(2,1)S(1)} %get-tuple-element.41), channel_id=1, source_target_pairs={{0,8},{4,12},{8,0},{12,4},{16,24},{20,28},{24,16},{28,20},{1,9},{5... | collective-permute-start | bytes 196616 | tf_op jit(solution)/shard_map/ppermute | solution.py:503
  30.0 5.2 %collective-permute-start.8 = (bf16[8,128,128]{2,1,0:T(8,128)(2,1)S(1)}, bf16[8,128,128]{2,1,0:T(8,128)(2,1)S(1)}, u32[]{:S(2)}, u32[]{:S(2)}) collective-permute-start(bf16[8,128,128]{2,1,0:T(8,128)(2,1)S(1)} %get-tuple-element.43), channel_id=1, source_target_pairs={{0,16},{4,20},{8,24},{12,28},{1,17},{5,21},{9,25},{13,29},{2,18},{... | collective-permute-start | bytes 786440 | tf_op jit(solution)/shard_map/ppermute | solution.py:499
  35.2 1.5 %collective-permute-start = (bf16[2,256,128]{2,1,0:T(8,128)(2,1)S(1)}, bf16[2,256,128]{2,1,0:T(8,128)(2,1)S(1)}, u32[]{:S(2)}, u32[]{:S(2)}) collective-permute-start(bf16[2,256,128]{2,1,0:T(8,128)(2,1)S(1)} %get-tuple-element.30), channel_id=1, source_target_pairs={{0,4},{4,0},{8,12},{12,8},{16,20},{20,16},{24,28},{28,24},{1,5},{5... | collective-permute-start | bytes 393224 | tf_op jit(solution)/shard_map/ppermute | solution.py:503
  36.7 2.0 %collective-permute-start.1 = (bf16[2,256,128]{2,1,0:T(8,128)(2,1)S(1)}, bf16[2,256,128]{2,1,0:T(8,128)(2,1)S(1)}, u32[]{:S(2)}, u32[]{:S(2)}) collective-permute-start(bf16[2,256,128]{2,1,0:T(8,128)(2,1)S(1)} %get-tuple-element.31), channel_id=1, source_target_pairs={{0,8},{4,12},{8,0},{12,4},{16,24},{20,28},{24,16},{28,20},{1,9},{5... | collective-permute-start | bytes 393224 | tf_op jit(solution)/shard_map/ppermute | solution.py:503
  38.7 1.6 %collective-permute-done.refs_1_ = bf16[2,256,128]{2,1,0:T(8,128)(2,1)S(1)} collective-permute-done((bf16[2,256,128]{2,1,0:T(8,128)(2,1)S(1)}, bf16[2,256,128]{2,1,0:T(8,128)(2,1)S(1)}, u32[]{:S(2)}, u32[]{:S(2)}) %collective-permute-start) | collective-permute-done | bytes 131104 | tf_op jit(solution)/shard_map/ppermute | solution.py:503
  40.4 4.2 %collective-permute-done.1.refs_2_ = bf16[2,256,128]{2,1,0:T(8,128)(2,1)S(1)} collective-permute-done((bf16[2,256,128]{2,1,0:T(8,128)(2,1)S(1)}, bf16[2,256,128]{2,1,0:T(8,128)(2,1)S(1)}, u32[]{:S(2)}, u32[]{:S(2)}) %collective-permute-start.1) | collective-permute-done | bytes 131104 | tf_op jit(solution)/shard_map/ppermute | solution.py:503
  44.6 1.4 %collective-permute-done.2.refs_3_ = bf16[2,256,128]{2,1,0:T(8,128)(2,1)S(1)} collective-permute-done((bf16[2,256,128]{2,1,0:T(8,128)(2,1)S(1)}, bf16[2,256,128]{2,1,0:T(8,128)(2,1)S(1)}, u32[]{:S(2)}, u32[]{:S(2)}) %collective-permute-start.2) | collective-permute-done | bytes 131104 | tf_op jit(solution)/shard_map/ppermute | solution.py:503
  46.0 0.7 %shard_map.78 = bf16[2,4,256,128]{3,2,1,0:T(8,128)(2,1)S(1)} custom-call(bf16[2,256,128]{2,1,0:T(8,128)(2,1)S(1)} %get-tuple-element.29.refs_0_, bf16[2,256,128]{2,1,0:T(8,128)(2,1)S(1)} %collective-permute-done.refs_1_, bf16[2,256,128]{2,1,0:T(8,128)(2,1)S(1)} %collective-permute-done.1.refs_2_, bf16[2,256,128]{2,1,0:T(8,128)(2,1)S(1)} %collective-permute-done.2.refs_3_, ...), custom_call_target="tpu_custom_call" | custom-call | bytes 2097152 | tf_op jit(solution)/shard_map/pallas_call | solution.py:591
  46.7 2.5 %shard_map.76 = (f32[8,128,128]{2,1,0:T(8,128)S(1)}, bf16[8,5,128,128]{3,2,1,0:T(8,128)(2,1)S(1)}, bf16[512,1024]{1,0:T(8,128)(2,1)S(1)}) custom-call(bf16[4,528,128]{2,1,0:T(8,128)(2,1)S(1)} %all-to-all-done.part_ref, bf16[8,128,256]{2,1,0:T(8,128)(2,1)S(1)} %get-tuple-element.26.mixed_ref, bf16[4,2,128,128]{3,2,1,0:T(8,128)(2,1)S(1)} %get-tuple-element.27.even_ref, ...), custom_call_target="tpu_custom_call" | custom-call | flops 838860800 | bytes 2097152 | tf_op jit(solution)/shard_map/pallas_call | solution.py:579
  49.3 2.5 %shard_map.79 = bf16[4,2,2,128,128]{4,3,2,1,0:T(8,128)(2,1)S(1)} custom-call(s32[8,128]{1,0:T(8,128)S(1)} %get-tuple-element.25.refs_1_.away_ref, bf16[8,5,128,128]{3,2,1,0:T(8,128)(2,1)S(1)} %get-tuple-element.34.moving_ref, f32[8,128,128]{2,1,0:T(8,128)S(1)} %get-tuple-element.35.inner_ref, bf16[8,128,128]{2,1,0:T(8,128)(2,1)S(1)} %get-tuple-element.36.end_ref, ...), custom_call_target="tpu_custom_call" | custom-call | flops 838860800 | bytes 2097152 | tf_op jit(solution)/shard_map/pallas_call | solution.py:598
  51.8 12.5 %all_to_all.10 = bf16[8,2,128,128]{3,2,1,0:T(8,128)(2,1)S(1)} all-to-all(bf16[8,2,128,128]{3,2,1,0:T(8,128)(2,1)S(1)} %bitcast.6), channel_id=1, replica_groups={{0,2,4,6,8,10,12,14},{1,3,5,7,9,11,13,15},{16,18,20,22,24,26,28,30},{17..., dimensions={0} | all-to-all | bytes 1048576 | tf_op jit(solution)/shard_map/all_to_all | solution.py:614
  64.2 0.4 shard_map.81
  64.7 0.1 collective-permute-start.9
  64.8 0.4 shard_map.80
  65.2 1.1 %collective-permute-done.9 = bf16[256,512]{1,0:T(8,128)(2,1)S(1)} collective-permute-done((bf16[256,512]{1,0:T(8,128)(2,1)S(1)}, bf16[256,512]{1,0:T(8,128)(2,1)S(1)}, u32[]{:S(2)}, u32[]{:S(2)}) %collective-permute-start.9) | collective-permute-done | bytes 262176 | tf_op jit(solution)/shard_map/ppermute | solution.py:627
  66.3 0.8 %add_convert_fusion = bf16[256,512]{1,0:T(8,128)(2,1)} fusion(f32[256,512]{1,0:T(8,128)S(1)} %shard_map.80, bf16[256,512]{1,0:T(8,128)(2,1)S(1)} %collective-permute-done.9), kind=kLoop, calls=%fused_computation | loop fusion | flops 393216 | bytes 1048576 | tf_op jit(solution)/shard_map/convert_element_type | solution.py:628
  (15 shorter events, 0.0 us)
Async XLA Ops:
  1.9 13.8 %copy-start.1 = (bf16[256,512]{1,0:T(8,128)(2,1)S(1)}, bf16[256,512]{1,0:T(8,128)(2,1)}, u32[]{:S(2)}) copy-start(bf16[256,512]{1,0:T(8,128)(2,1)} %values_ref.3) | copy-start | bytes 786436
  1.9 13.8 %copy-start.2 = (bf16[256,512]{1,0:T(8,128)(2,1)S(1)}, bf16[256,512]{1,0:T(8,128)(2,1)}, u32[]{:S(2)}) copy-start(bf16[256,512]{1,0:T(8,128)(2,1)} %queries_ref.1) | copy-start | bytes 786436
  1.9 13.8 %all-to-all-start = ((bf16[4,528,128]{2,1,0:T(8,128)(2,1)}), bf16[4,528,128]{2,1,0:T(8,128)(2,1)S(1)}, u32[]{:S(2)}, u32[]{:S(2)}) async-start(bf16[4,528,128]{2,1,0:T(8,128)(2,1)} %shard_map.73.after), calls=%async_computation | async-start | bytes 1081344 | tf_op jit(solution)/shard_map/all_to_all | solution.py:495
  9.6 37.1 %collective-permute-start.3 = (bf16[512,1024]{1,0:T(8,128)(2,1)}, bf16[512,1024]{1,0:T(8,128)(2,1)S(1)}, u32[]{:S(2)}, u32[]{:S(2)}) collective-permute-start(bf16[512,1024]{1,0:T(8,128)(2,1)} %get-tuple-element.33), channel_id=1, source_target_pairs={{0,2},{1,3},{2,0},{3,1},{4,6},{5,7},{6,4},{7,5},{8,10},{9,11},{10,... | collective-permute-start | bytes 3145736 | tf_op jit(solution)/shard_map/ppermute | solution.py:540
  11.2 13.3 %collective-permute-start.4 = (bf16[256,512]{1,0:T(8,128)(2,1)}, bf16[256,512]{1,0:T(8,128)(2,1)S(1)}, u32[]{:S(2)}, u32[]{:S(2)}) collective-permute-start(bf16[256,512]{1,0:T(8,128)(2,1)} %get-tuple-element.38), channel_id=1, source_target_pairs={{0,16},{4,20},{8,24},{12,28},{1,17},{5,21},{9,25},{13,29},{2,18},{... | collective-permute-start | bytes 786440 | tf_op jit(solution)/shard_map/ppermute | solution.py:499
  24.7 10.5 %collective-permute-start.5 = (bf16[1,256,128]{2,1,0:T(8,128)(2,1)S(1)}, bf16[1,256,128]{2,1,0:T(8,128)(2,1)S(1)}, u32[]{:S(2)}, u32[]{:S(2)}) collective-permute-start(bf16[1,256,128]{2,1,0:T(8,128)(2,1)S(1)} %get-tuple-element.40), channel_id=1, source_target_pairs={{0,4},{4,0},{8,12},{12,8},{16,20},{20,16},{24,28},{28,24},{1,5},{5... | collective-permute-start | bytes 196616 | tf_op jit(solution)/shard_map/ppermute | solution.py:503
  26.7 10.0 %collective-permute-start.6 = (bf16[1,256,128]{2,1,0:T(8,128)(2,1)S(1)}, bf16[1,256,128]{2,1,0:T(8,128)(2,1)S(1)}, u32[]{:S(2)}, u32[]{:S(2)}) collective-permute-start(bf16[1,256,128]{2,1,0:T(8,128)(2,1)S(1)} %get-tuple-element.41), channel_id=1, source_target_pairs={{0,8},{4,12},{8,0},{12,4},{16,24},{20,28},{24,16},{28,20},{1,9},{5... | collective-permute-start | bytes 196616 | tf_op jit(solution)/shard_map/ppermute | solution.py:503
  30.0 8.8 %collective-permute-start.7 = (bf16[1,256,128]{2,1,0:T(8,128)(2,1)S(1)}, bf16[1,256,128]{2,1,0:T(8,128)(2,1)S(1)}, u32[]{:S(2)}, u32[]{:S(2)}) collective-permute-start(bf16[1,256,128]{2,1,0:T(8,128)(2,1)S(1)} %get-tuple-element.42), channel_id=1, source_target_pairs={{0,12},{4,8},{8,4},{12,0},{16,28},{20,24},{24,20},{28,16},{1,13},{... | collective-permute-start | bytes 196616 | tf_op jit(solution)/shard_map/ppermute | solution.py:503
  30.0 19.3 %collective-permute-start.8 = (bf16[8,128,128]{2,1,0:T(8,128)(2,1)S(1)}, bf16[8,128,128]{2,1,0:T(8,128)(2,1)S(1)}, u32[]{:S(2)}, u32[]{:S(2)}) collective-permute-start(bf16[8,128,128]{2,1,0:T(8,128)(2,1)S(1)} %get-tuple-element.43), channel_id=1, source_target_pairs={{0,16},{4,20},{8,24},{12,28},{1,17},{5,21},{9,25},{13,29},{2,18},{... | collective-permute-start | bytes 786440 | tf_op jit(solution)/shard_map/ppermute | solution.py:499
  35.2 5.2 %collective-permute-start = (bf16[2,256,128]{2,1,0:T(8,128)(2,1)S(1)}, bf16[2,256,128]{2,1,0:T(8,128)(2,1)S(1)}, u32[]{:S(2)}, u32[]{:S(2)}) collective-permute-start(bf16[2,256,128]{2,1,0:T(8,128)(2,1)S(1)} %get-tuple-element.30), channel_id=1, source_target_pairs={{0,4},{4,0},{8,12},{12,8},{16,20},{20,16},{24,28},{28,24},{1,5},{5... | collective-permute-start | bytes 393224 | tf_op jit(solution)/shard_map/ppermute | solution.py:503
  36.7 7.9 %collective-permute-start.1 = (bf16[2,256,128]{2,1,0:T(8,128)(2,1)S(1)}, bf16[2,256,128]{2,1,0:T(8,128)(2,1)S(1)}, u32[]{:S(2)}, u32[]{:S(2)}) collective-permute-start(bf16[2,256,128]{2,1,0:T(8,128)(2,1)S(1)} %get-tuple-element.31), channel_id=1, source_target_pairs={{0,8},{4,12},{8,0},{12,4},{16,24},{20,28},{24,16},{28,20},{1,9},{5... | collective-permute-start | bytes 393224 | tf_op jit(solution)/shard_map/ppermute | solution.py:503
  38.7 7.2 %collective-permute-start.2 = (bf16[2,256,128]{2,1,0:T(8,128)(2,1)S(1)}, bf16[2,256,128]{2,1,0:T(8,128)(2,1)S(1)}, u32[]{:S(2)}, u32[]{:S(2)}) collective-permute-start(bf16[2,256,128]{2,1,0:T(8,128)(2,1)S(1)} %get-tuple-element.32), channel_id=1, source_target_pairs={{0,12},{4,8},{8,4},{12,0},{16,28},{20,24},{24,20},{28,16},{1,13},{... | collective-permute-start | bytes 393224 | tf_op jit(solution)/shard_map/ppermute | solution.py:503
  49.2 15.0 %copy-start = (bf16[512,2048]{1,0:T(8,128)(2,1)S(1)}, bf16[512,2048]{1,0:T(8,128)(2,1)}, u32[]{:S(2)}) copy-start(bf16[512,2048]{1,0:T(8,128)(2,1)} %own_ref.3) | copy-start | bytes 6291460
  64.7 1.6 %collective-permute-start.9 = (bf16[256,512]{1,0:T(8,128)(2,1)S(1)}, bf16[256,512]{1,0:T(8,128)(2,1)S(1)}, u32[]{:S(2)}, u32[]{:S(2)}) collective-permute-start(bf16[256,512]{1,0:T(8,128)(2,1)S(1)} %shard_map.81), channel_id=1, source_target_pairs={{0,1},{1,0},{2,3},{3,2},{4,5},{5,4},{6,7},{7,6},{8,9},{9,8},{10,11... | collective-permute-start | bytes 786440 | tf_op jit(solution)/shard_map/ppermute | solution.py:627

commit v10 on v9

--- a/solution.py
+++ b/solution.py
@@ -117,22 +117,27 @@
         copy.wait()
 
 
-def early_kernel(axes, cores, weight_ref, values_ref, after, *refs):
-    count = (len(refs) - 5) // 2 + 1
-    weight_outs, values_out = refs[:count], refs[count]
-    weight_bufs, values_buf = refs[count + 1:2 * count + 1], refs[2 * count + 1]
-    sems, out_sems = refs[2 * count + 2:]
-    width = weight_outs[0].shape[1]
+def values_kernel(values_ref, after, out_ref, buffer_ref, sems):
+    for copy in fetched([values_ref], [buffer_ref], sems.at[pl.ds(0, 1)]):
+        copy.wait()
+    for copy in fetched([buffer_ref], [out_ref], sems.at[pl.ds(1, 1)]):
+        copy.wait()
+
+
+def weights_kernel(axes, cores, weight_ref, after, *refs):
+    count = (len(refs) - 2) // 2
+    outs, buffers = refs[:count], refs[count:2 * count]
+    sems, out_sems = refs[2 * count:]
+    width = outs[0].shape[1]
     planes = weight_ref.shape[1] // width
     plane = lax.axis_index(axes[1]) // cores
-    sources = [values_ref]
+    sources = []
     for offset in range(1, planes):
         start = lax.rem(plane + planes - offset, planes) * width
         sources.append(weight_ref.at[:, pl.ds(pl.multiple_of(start, width), width)])
-    buffers = [values_buf, *weight_bufs]
     copies = fetched(sources, buffers, sems)
     out_copies = []
-    for index, target in enumerate([values_out, *weight_outs]):
+    for index, target in enumerate(outs):
         copies[index].wait()
         out_copies += fetched([buffers[index]], [target], out_sems.at[pl.ds(index, 1)])
     for copy in out_copies:
@@ -152,22 +157,6 @@
             [source.at[:, pl.ds(cut, HEAD_DIM)] for source in sources],
             [parts[turn].at[kind] for kind in range(len(sources))],
             sems.at[turn],
-        )
-    for copy in copies:
-        copy.wait()
-
-
-def order_kernel(axes, *refs):
-    values_ref, sems = refs[-2:]
-    kinds, heads = values_ref.shape[:2]
-    place = lax.rem(lax.axis_index(axes[0]), heads)
-    copies = []
-    for turn in range(heads):
-        source = lax.bitwise_xor(place, turn)
-        parts = [refs[turn].at[1]]
-        parts += [refs[heads + turn].at[kind] for kind in range(kinds - 1)]
-        copies += fetched(
-            parts, [values_ref.at[kind, source] for kind in range(kinds)], sems.at[turn]
         )
     for copy in copies:
         copy.wait()
@@ -227,24 +216,9 @@
         tick += 1
 
 
-def keys_kernel(axes, blocks, part_ref, queries_ref, values_ref, end_ref, tail_ref, far_ref, even_ref,
-                pair_ref, group_ref, mixed_ref, away_ref, *refs):
-    heads = part_ref.shape[0]
-    units = heads * blocks
-    out_refs = refs[:heads]
-    cut_ref, sems, out_sems = refs[heads:]
-    place = lax.rem(lax.axis_index(axes[0]), heads)
-    cuts = [
-        pl.multiple_of(lax.bitwise_xor(place, turn) * HEAD_DIM, HEAD_DIM) for turn in range(heads)
-    ]
-    cut_copies = [
-        fetched(
-            [ref.at[:, pl.ds(cut, HEAD_DIM)] for ref in (queries_ref, values_ref)],
-            [cut_ref.at[turn, 0], cut_ref.at[turn, 1]],
-            sems.at[turn],
-        )
-        for turn, cut in enumerate(cuts)
-    ]
+def keys_kernel(blocks, part_ref, end_ref, tail_ref, far_ref, even_ref, pair_ref, group_ref,
+                mixed_ref, away_ref):
+    units = part_ref.shape[0] * blocks
     rows, columns = square_iotas()
     diagonal = rows == columns
     identity = diagonal.astype(F32)
@@ -294,11 +268,6 @@
         end_ref[unit] = ends[unit].astype(BF16)
 
     interleaved([terms(unit) for unit in range(units)], 1)
-    out_copies = []
-    for turn in range(heads):
-        for copy in cut_copies[turn]:
-            copy.wait()
-        out_copies += fetched([cut_ref.at[turn]], [out_refs[turn]], out_sems.at[pl.ds(turn, 1)])
     pair_keys, pair_maps = [], []
     for pair in range(units // 2):
         even, odd = 2 * pair, 2 * pair + 1
@@ -325,23 +294,26 @@
         far_ref[2 * pair + 1] = far[BLOCK:].astype(BF16)
     group_ref[0] = onward[0]
     group_ref[1] = onward[1]
-    for copy in out_copies:
-        copy.wait()
 
 
 def queries_kernel(axes, blocks, count, part_ref, mixed_ref, even_ref, pair_ref, *refs):
     heads = part_ref.shape[0]
     units = heads * blocks
     arrived, weights = refs[:heads], refs[heads:heads + count]
-    inner_ref, moving_ref, *weight_refs = refs[heads + count:-3]
-    query_ref, sems, query_sems = refs[-3:]
+    inner_ref, moving_ref, values_ref, *weight_refs = refs[-7 - count:-4]
+    query_ref, sems, query_sems, value_sems = refs[-4:]
     place = lax.rem(lax.axis_index(axes[0]), heads)
+    sources = [lax.bitwise_xor(place, turn) for turn in range(heads)]
     query_copies = fetched(
-        [part.at[0] for part in arrived],
-        [query_ref.at[lax.bitwise_xor(place, turn)] for turn in range(heads)],
-        query_sems,
+        [part.at[0] for part in arrived], [query_ref.at[source] for source in sources], query_sems
     )
     copies = fetched(weights, weight_refs, sems)
+    for kind in range(values_ref.shape[0]):
+        copies += fetched(
+            [part.at[kind + 1] for part in arrived],
+            [values_ref.at[kind, source] for source in sources],
+            value_sems.at[kind],
+        )
     for copy in query_copies:
         copy.wait()
     rows, columns = square_iotas()
@@ -523,26 +495,36 @@
         56,
     )(directions, keys, rates, selected)
     width = out_weight.shape[1] // planes
-    early_shapes = [(out_weight.shape[0], width)] * (planes - 1) + [values.shape]
-    *pieces, raw_values = call(
-        functools.partial(early_kernel, axes, cores),
-        [array(shape) for shape in early_shapes],
-        [ANY] * 3,
+    raw_values = call(
+        values_kernel,
+        array(values.shape),
+        [ANY] * 2,
         cubes,
-        [pltpu.VMEM(shape, BF16) for shape in early_shapes]
-        + [pltpu.SemaphoreType.DMA((planes,))] * 2,
-        [ANY] * planes,
+        [pltpu.VMEM(values.shape, BF16), pltpu.SemaphoreType.DMA((2,))],
+        ANY,
         56,
-    )(out_weight, values, packed)
+    )(values, packed)
+    value_parts = [onward(raw_values, by) for by in range(1, before + 1)]
     weight_parts = []
+    if planes > 1:
+        piece_shape = (out_weight.shape[0], width)
+        pieces = call(
+            functools.partial(weights_kernel, axes, cores),
+            [array(piece_shape)] * (planes - 1),
+            [ANY] * 2,
+            cubes,
+            [pltpu.VMEM(piece_shape, BF16)] * (planes - 1)
+            + [pltpu.SemaphoreType.DMA((planes - 1,))] * 2,
+            [ANY] * (planes - 1),
+            56,
+        )(out_weight, raw_values)
     for offset in range(1, planes):
         turned = [(g, (g + head_size - cores * offset) % head_size) for g in range(head_size)]
         weight_parts.append(lax.ppermute(pieces[offset - 1], "head", turned))
-    value_parts = [onward(raw_values, by) for by in range(1, before + 1)]
     parts = exchange(packed)
 
-    end, tail, far, even, pair_map, group_map, mixed, away, *cut = call(
-        functools.partial(keys_kernel, axes, blocks),
+    end, tail, far, even, pair_map, group_map, mixed, away = call(
+        functools.partial(keys_kernel, blocks),
         [
             array((units, *tile)),
             array((units, *tile)),
@@ -552,49 +534,39 @@
             array((2, *tile)),
             array((units, BLOCK, 2 * BLOCK)),
             array((units, HEAD_DIM), jnp.int32),
-        ]
-        + [array((2, tokens, HEAD_DIM))] * heads,
-        [VMEM, ANY, ANY],
+        ],
+        [VMEM],
         400 * cubes,
-        [
-            pltpu.VMEM((heads, 2, tokens, HEAD_DIM), BF16),
-            pltpu.SemaphoreType.DMA((heads, 2)),
-            pltpu.SemaphoreType.DMA((heads,)),
-        ],
-        [VMEM] * 8 + [ANY] * heads,
-    )(parts, queries, values)
+    )(parts)
     far_parts = [onward(far, by) for by in range(1, before + 1)]
     map_parts = [onward(group_map, by) for by in range(1, before)]
+    kinds = 2 + before
+    cut = call(
+        functools.partial(cut_kernel, axes),
+        [array((kinds, tokens, HEAD_DIM))] * heads,
+        [ANY] * (kinds + 1),
+        2000 * cubes,
+        [pltpu.SemaphoreType.DMA((heads, kinds))],
+    )(queries, values, *value_parts, away)
     arrived = [crossed(cut[turn], turn) for turn in range(heads)]
-    arrived_values = []
-    if before:
-        cut = call(
-            functools.partial(cut_kernel, axes),
-            [array((before, tokens, HEAD_DIM))] * heads,
-            [ANY] * (before + 1),
-            1000 * cubes,
-            [pltpu.SemaphoreType.DMA((heads, before))],
-        )(*value_parts, away)
-        arrived_values = [crossed(cut[turn], turn) for turn in range(heads)]
-    inner, moving, *weight_parts = call(
+    inner, moving, all_values, *weight_parts = call(
         functools.partial(queries_kernel, axes, blocks, len(weight_parts)),
-        [array((units, BLOCK, BLOCK), F32), array((units, pairs + 1, *tile))]
+        [
+            array((units, BLOCK, BLOCK), F32),
+            array((units, pairs + 1, *tile)),
+            array((1 + before, heads, tokens, HEAD_DIM)),
+        ]
         + [array(part.shape) for part in weight_parts],
         [VMEM] * 4 + [ANY] * (heads + len(weight_parts)),
-        200 * cubes,
+        0,
         [
             pltpu.VMEM((heads, tokens, HEAD_DIM), BF16),
             pltpu.SemaphoreType.DMA((max(len(weight_parts), 1),)),
             pltpu.SemaphoreType.DMA((heads,)),
+            pltpu.SemaphoreType.DMA((1 + before, heads)),
         ],
     )(parts, mixed, even, pair_map, *arrived, *weight_parts)
-    all_values = call(
-        functools.partial(order_kernel, axes),
-        array((1 + before, heads, tokens, HEAD_DIM)),
-        [ANY] * (heads + len(arrived_values)),
-        0,
-        [pltpu.SemaphoreType.DMA((heads, 1 + before))],
-    )(*arrived, *arrived_values).reshape(1 + before, units, *tile)
+    all_values = all_values.reshape(1 + before, units, *tile)
     attended = call(
         functools.partial(attend_kernel, before, blocks),
         array((heads, planes, blocks, *tile)),

time: 67.4 us -> 64.2 us (0.953)
  the two profiles are of different devices: /device:TPU:0 before, /device:TPU:17 now
where the time goes in v10:
time: 64.2 us; the launch traced here: 63.8 us
  Pallas kernels  20.7 us (32%)
  starting transfers between devices  15.2 us (24%)
  waiting for transfers between devices  14.7 us (23%)
  blocking collectives  12.3 us (19%)
  other arithmetic  0.77 us (1%)
    ppermute x3, waiting for transfers between devices, crossed(): return lax.ppermute(value, 'ctx', pairs) if turn else value  13.2 us
    all_to_all x1, blocking collectives, body(): lax.all_to_all(attended.reshape(heads * planes, blocks, *tile), axes, 0,...  12.3 us
    pallas_call x1, Pallas kernels, body(): call(functools.partial(keys_kernel, blocks), [array((units, *tile)), arra...  8.02 us
    ppermute x3, starting transfers between devices, crossed(): return lax.ppermute(value, 'ctx', pairs) if turn else value  4.55 us
    all_to_all x1, starting transfers between devices, exchange(): lax.all_to_all(value, 'ctx', 0, 0, axis_index_groups=members, tiled=True)  3.53 us
    ppermute x1, starting transfers between devices, body(): arrived = lax.ppermute(projected(1, BF16), 'head', partners)  3.26 us
    pallas_call x1, Pallas kernels, body(): call(functools.partial(queries_kernel, axes, blocks, len(weight_parts)),...  3.23 us
    ppermute x2, starting transfers between devices, onward(): lax.ppermute(value, 'ctx', [(i, i + shift) for i in range(ctx_size - shif...  2.57 us
  transfers between devices with their start and end apart: 8, of which 5 were waited for; matrix products, arithmetic and copies ran while one was open for 0% of the time, Pallas kernels for 25%

profile of v10, /device:TPU:17, one launch (start us, length us, event | category | flops | bytes accessed | tf_op | source)
XLA Modules:
  0.0 63.8 jit_solution(1753037339262923703)
XLA Ops:
  0.0 1.9 %shard_map.73.after = bf16[4,528,128]{2,1,0:T(8,128)(2,1)} custom-call(bf16[256,512]{1,0:T(8,128)(2,1)} %d_ref.1, bf16[256,512]{1,0:T(8,128)(2,1)} %k_ref.1, f32[4,256]{1,0:T(4,128)} %rates_hbm.1, s32[2,4]{1,0:T(2,128)} %selected_hbm.1), custom_call_target="tpu_custom_call" | custom-call | flops 4194304 | bytes 2097152 | tf_op jit(solution)/shard_map/pallas_call | solution.py:481
  1.9 3.5 %all-to-all-start = ((bf16[4,528,128]{2,1,0:T(8,128)(2,1)}), bf16[4,528,128]{2,1,0:T(8,128)(2,1)S(1)}, u32[]{:S(2)}, u32[]{:S(2)}) async-start(bf16[4,528,128]{2,1,0:T(8,128)(2,1)} %shard_map.73.after), calls=%async_computation | async-start | bytes 1081344 | tf_op jit(solution)/shard_map/all_to_all | solution.py:467
  5.4 1.7 %shard_map.75.after = bf16[256,512]{1,0:T(8,128)(2,1)} custom-call(bf16[256,512]{1,0:T(8,128)(2,1)} %refs_1_.1, bf16[4,528,128]{2,1,0:T(8,128)(2,1)} %shard_map.73.after), custom_call_target="tpu_custom_call" | custom-call | flops 4194304 | bytes 2097152 | tf_op jit(solution)/shard_map/pallas_call | solution.py:498
  7.1 1.3 %collective-permute-start = (bf16[256,512]{1,0:T(8,128)(2,1)}, bf16[256,512]{1,0:T(8,128)(2,1)S(1)}, u32[]{:S(2)}, u32[]{:S(2)}) collective-permute-start(bf16[256,512]{1,0:T(8,128)(2,1)} %shard_map.75.after), channel_id=1, source_target_pairs={{0,16},{4,20},{8,24},{12,28},{1,17},{5,21},{9,25},{13,29},{2,18},{... | collective-permute-start | bytes 786440 | tf_op jit(solution)/shard_map/ppermute | solution.py:471
  8.4 2.2 %shard_map.77 = bf16[512,1024]{1,0:T(8,128)(2,1)} custom-call(bf16[512,2048]{1,0:T(8,128)(2,1)} %own_ref.3, bf16[256,512]{1,0:T(8,128)(2,1)} %shard_map.75.after), custom_call_target="tpu_custom_call" | custom-call | flops 4194304 | bytes 2097152 | tf_op jit(solution)/shard_map/pallas_call | solution.py:511
  10.6 0.0 copy-start.1
  10.7 1.3 %collective-permute-start.4 = (bf16[512,1024]{1,0:T(8,128)(2,1)}, bf16[512,1024]{1,0:T(8,128)(2,1)S(1)}, u32[]{:S(2)}, u32[]{:S(2)}) collective-permute-start(bf16[512,1024]{1,0:T(8,128)(2,1)} %shard_map.77), channel_id=1, source_target_pairs={{0,2},{1,3},{2,0},{3,1},{4,6},{5,7},{6,4},{7,5},{8,10},{9,11},{10,... | collective-permute-start | bytes 3145736 | tf_op jit(solution)/shard_map/ppermute | solution.py:523
  11.9 0.8 %all-to-all-done.part_ref = bf16[4,528,128]{2,1,0:T(8,128)(2,1)S(1)} async-done(((bf16[4,528,128]{2,1,0:T(8,128)(2,1)}), bf16[4,528,128]{2,1,0:T(8,128)(2,1)S(1)}, u32[]{:S(2)}, u32[]{:S(2)}) %all-to-all-start) | async-done | bytes 540704 | tf_op jit(solution)/shard_map/all_to_all | solution.py:467
  12.7 8.0 %shard_map.74 = (bf16[8,128,128]{2,1,0:T(8,128)(2,1)S(1)}, bf16[8,128,128]{2,1,0:T(8,128)(2,1)S(1)}, bf16[8,128,128]{2,1,0:T(8,128)(2,1)S(1)}, bf16[4,2,128,128]...) custom-call(bf16[4,528,128]{2,1,0:T(8,128)(2,1)S(1)} %all-to-all-don, ...), custom_call_target="tpu_custom_call" | custom-call | flops 1677721600 | bytes 2097152 | tf_op jit(solution)/shard_map/pallas_call | solution.py:526
  20.8 1.3 %collective-permute-start.5 = (bf16[8,128,128]{2,1,0:T(8,128)(2,1)S(1)}, bf16[8,128,128]{2,1,0:T(8,128)(2,1)S(1)}, u32[]{:S(2)}, u32[]{:S(2)}) collective-permute-start(bf16[8,128,128]{2,1,0:T(8,128)(2,1)S(1)} %get-tuple-element.33), channel_id=1, source_target_pairs={{0,16},{4,20},{8,24},{12,28},{1,17},{5,21},{9,25},{13,29},{2,18},{... | collective-permute-start | bytes 786440 | tf_op jit(solution)/shard_map/ppermute | solution.py:471
  22.1 0.3 shard_map.76
  22.4 1.2 %collective-permute-start.1 = (bf16[3,256,128]{2,1,0:T(8,128)(2,1)S(1)}, bf16[3,256,128]{2,1,0:T(8,128)(2,1)S(1)}, u32[]{:S(2)}, u32[]{:S(2)}) collective-permute-start(bf16[3,256,128]{2,1,0:T(8,128)(2,1)S(1)} %get-tuple-element.25), channel_id=1, source_target_pairs={{0,4},{4,0},{8,12},{12,8},{16,20},{20,16},{24,28},{28,24},{1,5},{5... | collective-permute-start | bytes 589832 | tf_op jit(solution)/shard_map/ppermute | solution.py:475
  23.6 3.3 %collective-permute-start.2 = (bf16[3,256,128]{2,1,0:T(8,128)(2,1)S(1)}, bf16[3,256,128]{2,1,0:T(8,128)(2,1)S(1)}, u32[]{:S(2)}, u32[]{:S(2)}) collective-permute-start(bf16[3,256,128]{2,1,0:T(8,128)(2,1)S(1)} %get-tuple-element.26), channel_id=1, source_target_pairs={{0,8},{4,12},{8,0},{12,4},{16,24},{20,28},{24,16},{28,20},{1,9},{5... | collective-permute-start | bytes 589832 | tf_op jit(solution)/shard_map/ppermute | solution.py:475
  26.9 0.3 collective-permute-done.1.refs_1_
  27.3 4.4 %collective-permute-done.2.refs_2_ = bf16[3,256,128]{2,1,0:T(8,128)(2,1)S(1)} collective-permute-done((bf16[3,256,128]{2,1,0:T(8,128)(2,1)S(1)}, bf16[3,256,128]{2,1,0:T(8,128)(2,1)S(1)}, u32[]{:S(2)}, u32[]{:S(2)}) %collective-permute-start.2) | collective-permute-done | bytes 196640 | tf_op jit(solution)/shard_map/ppermute | solution.py:475
  31.7 8.5 %collective-permute-done.3.refs_3_ = bf16[3,256,128]{2,1,0:T(8,128)(2,1)S(1)} collective-permute-done((bf16[3,256,128]{2,1,0:T(8,128)(2,1)S(1)}, bf16[3,256,128]{2,1,0:T(8,128)(2,1)S(1)}, u32[]{:S(2)}, u32[]{:S(2)}) %collective-permute-start.3) | collective-permute-done | bytes 196640 | tf_op jit(solution)/shard_map/ppermute | solution.py:475
  40.2 3.2 %shard_map.78 = (f32[8,128,128]{2,1,0:T(8,128)S(1)}, bf16[8,5,128,128]{3,2,1,0:T(8,128)(2,1)S(1)}, bf16[2,4,256,128]{3,2,1,0:T(8,128)(2,1)S(1)}, bf16[512,1024]{1,0:T(8,128)(2,1)S(1)}) custom-call(bf16[4,528,128]{2,1,0:T(8,128)(2,1)S(1)} %all-to-all-done.part_ref, bf16[8,128,256]{2,1,0:T(8,128)(2,1)S(1)} %get-tuple-element.21.mixed_ref, ...), custom_call_target="tpu_custom_call" | custom-call | bytes 2097152 | tf_op jit(solution)/shard_map/pallas_call | solution.py:552
  43.4 2.5 %shard_map.79 = bf16[4,2,2,128,128]{4,3,2,1,0:T(8,128)(2,1)S(1)} custom-call(s32[8,128]{1,0:T(8,128)S(1)} %get-tuple-element.20.refs_3_.away_ref, bf16[8,5,128,128]{3,2,1,0:T(8,128)(2,1)S(1)} %get-tuple-element.28.moving_ref, f32[8,128,128]{2,1,0:T(8,128)S(1)} %get-tuple-element.29.inner_ref, bf16[8,128,128]{2,1,0:T(8,128)(2,1)S(1)} %get-tuple-element.30.end_ref, ...), custom_call_target="tpu_custom_call" | custom-call | flops 838860800 | bytes 2097152 | tf_op jit(solution)/shard_map/pallas_call | solution.py:570
  45.9 12.3 %all_to_all.10 = bf16[8,2,128,128]{3,2,1,0:T(8,128)(2,1)S(1)} all-to-all(bf16[8,2,128,128]{3,2,1,0:T(8,128)(2,1)S(1)} %bitcast.5), channel_id=1, replica_groups={{0,2,4,6,8,10,12,14},{1,3,5,7,9,11,13,15},{16,18,20,22,24,26,28,30},{17..., dimensions={0} | all-to-all | bytes 1048576 | tf_op jit(solution)/shard_map/all_to_all | solution.py:586
  58.2 0.4 shard_map.81
  58.6 3.3 %collective-permute-start.6 = (bf16[256,512]{1,0:T(8,128)(2,1)S(1)}, bf16[256,512]{1,0:T(8,128)(2,1)S(1)}, u32[]{:S(2)}, u32[]{:S(2)}) collective-permute-start(bf16[256,512]{1,0:T(8,128)(2,1)S(1)} %shard_map.81), channel_id=1, source_target_pairs={{0,1},{1,0},{2,3},{3,2},{4,5},{5,4},{6,7},{7,6},{8,9},{9,8},{10,11... | collective-permute-start | bytes 786440 | tf_op jit(solution)/shard_map/ppermute | solution.py:599
  61.9 0.4 shard_map.80
  62.4 0.7 %collective-permute-done.6 = bf16[256,512]{1,0:T(8,128)(2,1)S(1)} collective-permute-done((bf16[256,512]{1,0:T(8,128)(2,1)S(1)}, bf16[256,512]{1,0:T(8,128)(2,1)S(1)}, u32[]{:S(2)}, u32[]{:S(2)}) %collective-permute-start.6) | collective-permute-done | bytes 262176 | tf_op jit(solution)/shard_map/ppermute | solution.py:599
  63.1 0.8 %add_convert_fusion = bf16[256,512]{1,0:T(8,128)(2,1)} fusion(f32[256,512]{1,0:T(8,128)S(1)} %shard_map.80, bf16[256,512]{1,0:T(8,128)(2,1)S(1)} %collective-permute-done.6), kind=kLoop, calls=%fused_computation | loop fusion | flops 393216 | bytes 1048576 | tf_op jit(solution)/shard_map/convert_element_type | solution.py:600
  (9 shorter events, 0.0 us)
Async XLA Ops:
  1.9 10.9 %all-to-all-start = ((bf16[4,528,128]{2,1,0:T(8,128)(2,1)}), bf16[4,528,128]{2,1,0:T(8,128)(2,1)S(1)}, u32[]{:S(2)}, u32[]{:S(2)}) async-start(bf16[4,528,128]{2,1,0:T(8,128)(2,1)} %shard_map.73.after), calls=%async_computation | async-start | bytes 1081344 | tf_op jit(solution)/shard_map/all_to_all | solution.py:467
  7.1 15.0 %collective-permute-start = (bf16[256,512]{1,0:T(8,128)(2,1)}, bf16[256,512]{1,0:T(8,128)(2,1)S(1)}, u32[]{:S(2)}, u32[]{:S(2)}) collective-permute-start(bf16[256,512]{1,0:T(8,128)(2,1)} %shard_map.75.after), channel_id=1, source_target_pairs={{0,16},{4,20},{8,24},{12,28},{1,17},{5,21},{9,25},{13,29},{2,18},{... | collective-permute-start | bytes 786440 | tf_op jit(solution)/shard_map/ppermute | solution.py:471
  10.6 11.4 %copy-start.1 = (bf16[256,512]{1,0:T(8,128)(2,1)S(1)}, bf16[256,512]{1,0:T(8,128)(2,1)}, u32[]{:S(2)}) copy-start(bf16[256,512]{1,0:T(8,128)(2,1)} %refs_1_.1) | copy-start | bytes 786436
  10.7 11.4 %copy-start.2 = (bf16[256,512]{1,0:T(8,128)(2,1)S(1)}, bf16[256,512]{1,0:T(8,128)(2,1)}, u32[]{:S(2)}) copy-start(bf16[256,512]{1,0:T(8,128)(2,1)} %refs_0_.1) | copy-start | bytes 786436
  10.7 29.5 %collective-permute-start.4 = (bf16[512,1024]{1,0:T(8,128)(2,1)}, bf16[512,1024]{1,0:T(8,128)(2,1)S(1)}, u32[]{:S(2)}, u32[]{:S(2)}) collective-permute-start(bf16[512,1024]{1,0:T(8,128)(2,1)} %shard_map.77), channel_id=1, source_target_pairs={{0,2},{1,3},{2,0},{3,1},{4,6},{5,7},{6,4},{7,5},{8,10},{9,11},{10,... | collective-permute-start | bytes 3145736 | tf_op jit(solution)/shard_map/ppermute | solution.py:523
  20.8 22.6 %collective-permute-start.5 = (bf16[8,128,128]{2,1,0:T(8,128)(2,1)S(1)}, bf16[8,128,128]{2,1,0:T(8,128)(2,1)S(1)}, u32[]{:S(2)}, u32[]{:S(2)}) collective-permute-start(bf16[8,128,128]{2,1,0:T(8,128)(2,1)S(1)} %get-tuple-element.33), channel_id=1, source_target_pairs={{0,16},{4,20},{8,24},{12,28},{1,17},{5,21},{9,25},{13,29},{2,18},{... | collective-permute-start | bytes 786440 | tf_op jit(solution)/shard_map/ppermute | solution.py:471
  22.4 4.9 %collective-permute-start.1 = (bf16[3,256,128]{2,1,0:T(8,128)(2,1)S(1)}, bf16[3,256,128]{2,1,0:T(8,128)(2,1)S(1)}, u32[]{:S(2)}, u32[]{:S(2)}) collective-permute-start(bf16[3,256,128]{2,1,0:T(8,128)(2,1)S(1)} %get-tuple-element.25), channel_id=1, source_target_pairs={{0,4},{4,0},{8,12},{12,8},{16,20},{20,16},{24,28},{28,24},{1,5},{5... | collective-permute-start | bytes 589832 | tf_op jit(solution)/shard_map/ppermute | solution.py:475
  23.6 8.0 %collective-permute-start.2 = (bf16[3,256,128]{2,1,0:T(8,128)(2,1)S(1)}, bf16[3,256,128]{2,1,0:T(8,128)(2,1)S(1)}, u32[]{:S(2)}, u32[]{:S(2)}) collective-permute-start(bf16[3,256,128]{2,1,0:T(8,128)(2,1)S(1)} %get-tuple-element.26), channel_id=1, source_target_pairs={{0,8},{4,12},{8,0},{12,4},{16,24},{20,28},{24,16},{28,20},{1,9},{5... | collective-permute-start | bytes 589832 | tf_op jit(solution)/shard_map/ppermute | solution.py:475
  26.9 13.2 %collective-permute-start.3 = (bf16[3,256,128]{2,1,0:T(8,128)(2,1)S(1)}, bf16[3,256,128]{2,1,0:T(8,128)(2,1)S(1)}, u32[]{:S(2)}, u32[]{:S(2)}) collective-permute-start(bf16[3,256,128]{2,1,0:T(8,128)(2,1)S(1)} %get-tuple-element.27), channel_id=1, source_target_pairs={{0,12},{4,8},{8,4},{12,0},{16,28},{20,24},{24,20},{28,16},{1,13},{... | collective-permute-start | bytes 589832 | tf_op jit(solution)/shard_map/ppermute | solution.py:475
  43.4 14.8 %copy-start = (bf16[512,2048]{1,0:T(8,128)(2,1)S(1)}, bf16[512,2048]{1,0:T(8,128)(2,1)}, u32[]{:S(2)}) copy-start(bf16[512,2048]{1,0:T(8,128)(2,1)} %own_ref.3) | copy-start | bytes 6291460
  58.6 4.4 %collective-permute-start.6 = (bf16[256,512]{1,0:T(8,128)(2,1)S(1)}, bf16[256,512]{1,0:T(8,128)(2,1)S(1)}, u32[]{:S(2)}, u32[]{:S(2)}) collective-permute-start(bf16[256,512]{1,0:T(8,128)(2,1)S(1)} %shard_map.81), channel_id=1, source_target_pairs={{0,1},{1,0},{2,3},{3,2},{4,5},{5,4},{6,7},{7,6},{8,9},{9,8},{10,11... | collective-permute-start | bytes 786440 | tf_op jit(solution)/shard_map/ppermute | solution.py:599

commit v11 on v10

--- a/solution.py
+++ b/solution.py
@@ -64,12 +64,20 @@
     return copies
 
 
-def pack_kernel(axes, d_ref, k_ref, rates_hbm, selected_hbm, out_ref, parts_ref,
-                rates_ref, selected_ref, sems, few_sems, out_sems):
+def pack_kernel(axes, cores, d_ref, k_ref, rates_hbm, selected_hbm, values_ref, weight_ref,
+                *refs):
     tokens = d_ref.shape[0]
     heads = d_ref.shape[1] // HEAD_DIM
     blocks = tokens // BLOCK
-    first_block = lax.axis_index(axes[0]) * blocks
+    (parts_ref, rates_ref, selected_ref, cut_ref, piece_ref, sems, few_sems, out_sems, cut_sems,
+     cut_out_sems, piece_sems) = refs[-11:]
+    out_ref, cut_outs, piece_outs = refs[0], refs[1:1 + heads], refs[1 + heads:-11]
+    planes = len(piece_outs) + 1
+    width = weight_ref.shape[1] // planes
+    device = lax.axis_index(axes[0])
+    place = lax.rem(device, heads)
+    plane = lax.axis_index(axes[1]) // cores
+    first_block = device * blocks
     few_copies = fetched([rates_hbm, selected_hbm], [rates_ref, selected_ref], few_sems)
     sources = (d_ref, k_ref)
     copies = []
@@ -84,6 +92,22 @@
                 )
             )
             copies[-1].start()
+    cuts = [
+        pl.multiple_of(lax.bitwise_xor(place, turn) * HEAD_DIM, HEAD_DIM) for turn in range(heads)
+    ]
+    cut_copies = fetched(
+        [values_ref.at[:, pl.ds(cut, HEAD_DIM)] for cut in cuts],
+        [cut_ref.at[turn] for turn in range(heads)],
+        cut_sems,
+    )
+    piece_copies = []
+    for offset in range(1, planes):
+        start = pl.multiple_of(lax.rem(plane + planes - offset, planes) * width, width)
+        piece_copies += fetched(
+            [weight_ref.at[:, pl.ds(start, width)]],
+            [piece_ref.at[offset - 1]],
+            piece_sems.at[0, pl.ds(offset - 1, 1)],
+        )
     for copy in few_copies:
         copy.wait()
     row = lax.broadcasted_iota(jnp.int32, (EXTRA, HEAD_DIM), 0)
@@ -113,33 +137,16 @@
             pltpu.make_async_copy(parts_ref.at[head], out_ref.at[head], out_sems.at[head])
         )
         out_copies[-1].start()
-    for copy in out_copies:
+    for turn in range(heads):
+        cut_copies[turn].wait()
+        out_copies += fetched(
+            [cut_ref.at[turn]], [cut_outs[turn]], cut_out_sems.at[pl.ds(turn, 1)]
+        )
+    for index, copy in enumerate(piece_copies):
         copy.wait()
-
-
-def values_kernel(values_ref, after, out_ref, buffer_ref, sems):
-    for copy in fetched([values_ref], [buffer_ref], sems.at[pl.ds(0, 1)]):
-        copy.wait()
-    for copy in fetched([buffer_ref], [out_ref], sems.at[pl.ds(1, 1)]):
-        copy.wait()
-
-
-def weights_kernel(axes, cores, weight_ref, after, *refs):
-    count = (len(refs) - 2) // 2
-    outs, buffers = refs[:count], refs[count:2 * count]
-    sems, out_sems = refs[2 * count:]
-    width = outs[0].shape[1]
-    planes = weight_ref.shape[1] // width
-    plane = lax.axis_index(axes[1]) // cores
-    sources = []
-    for offset in range(1, planes):
-        start = lax.rem(plane + planes - offset, planes) * width
-        sources.append(weight_ref.at[:, pl.ds(pl.multiple_of(start, width), width)])
-    copies = fetched(sources, buffers, sems)
-    out_copies = []
-    for index, target in enumerate(outs):
-        copies[index].wait()
-        out_copies += fetched([buffers[index]], [target], out_sems.at[pl.ds(index, 1)])
+        out_copies += fetched(
+            [piece_ref.at[index]], [piece_outs[index]], piece_sems.at[1, pl.ds(index, 1)]
+        )
     for copy in out_copies:
         copy.wait()
 
@@ -308,9 +315,10 @@
         [part.at[0] for part in arrived], [query_ref.at[source] for source in sources], query_sems
     )
     copies = fetched(weights, weight_refs, sems)
+    straight = refs[heads + count:-7 - count]
     for kind in range(values_ref.shape[0]):
         copies += fetched(
-            [part.at[kind + 1] for part in arrived],
+            straight[(kind - 1) * heads:kind * heads] if kind else [part.at[1] for part in arrived],
             [values_ref.at[kind, source] for source in sources],
             value_sems.at[kind],
         )
@@ -474,50 +482,45 @@
         pairs = [(i, i - i % heads + (i % heads ^ turn)) for i in range(ctx_size)]
         return lax.ppermute(value, "ctx", pairs) if turn else value
 
+    def straight(value, turn, by):
+        shift = by * heads
+        pairs = [(i, i - i % heads + (i % heads ^ turn) + shift) for i in range(ctx_size - shift)]
+        return lax.ppermute(value, "ctx", pairs)
+
     def array(shape, kind=BF16):
         return jax.ShapeDtypeStruct(shape, kind)
 
     part_shape = (heads, 2 * tokens + EXTRA, HEAD_DIM)
-    packed = call(
-        functools.partial(pack_kernel, axes),
-        array(part_shape),
-        [ANY] * 4,
+    width = out_weight.shape[1] // planes
+    piece_shape = (out_weight.shape[0], width)
+    packed, *rest = call(
+        functools.partial(pack_kernel, axes, cores),
+        [array(part_shape)]
+        + [array((tokens, HEAD_DIM))] * heads
+        + [array(piece_shape)] * (planes - 1),
+        [ANY] * 6,
         cubes,
         [
             pltpu.VMEM(part_shape, BF16),
             pltpu.VMEM(rates.shape, F32),
             pltpu.SMEM(selected.shape, jnp.int32),
+            pltpu.VMEM((heads, tokens, HEAD_DIM), BF16),
+            pltpu.VMEM((max(planes - 1, 1), *piece_shape), BF16),
             pltpu.SemaphoreType.DMA((heads, 2)),
             pltpu.SemaphoreType.DMA((2,)),
             pltpu.SemaphoreType.DMA((heads,)),
+            pltpu.SemaphoreType.DMA((heads,)),
+            pltpu.SemaphoreType.DMA((heads,)),
+            pltpu.SemaphoreType.DMA((2, planes)),
         ],
-        ANY,
+        [ANY] * (heads + planes),
         56,
-    )(directions, keys, rates, selected)
-    width = out_weight.shape[1] // planes
-    raw_values = call(
-        values_kernel,
-        array(values.shape),
-        [ANY] * 2,
-        cubes,
-        [pltpu.VMEM(values.shape, BF16), pltpu.SemaphoreType.DMA((2,))],
-        ANY,
-        56,
-    )(values, packed)
-    value_parts = [onward(raw_values, by) for by in range(1, before + 1)]
+    )(directions, keys, rates, selected, values, out_weight)
+    value_cuts, pieces = rest[:heads], rest[heads:]
+    value_parts = [
+        straight(value_cuts[turn], turn, by) for by in range(1, before + 1) for turn in range(heads)
+    ]
     weight_parts = []
-    if planes > 1:
-        piece_shape = (out_weight.shape[0], width)
-        pieces = call(
-            functools.partial(weights_kernel, axes, cores),
-            [array(piece_shape)] * (planes - 1),
-            [ANY] * 2,
-            cubes,
-            [pltpu.VMEM(piece_shape, BF16)] * (planes - 1)
-            + [pltpu.SemaphoreType.DMA((planes - 1,))] * 2,
-            [ANY] * (planes - 1),
-            56,
-        )(out_weight, raw_values)
     for offset in range(1, planes):
         turned = [(g, (g + head_size - cores * offset) % head_size) for g in range(head_size)]
         weight_parts.append(lax.ppermute(pieces[offset - 1], "head", turned))
@@ -540,11 +543,11 @@
     )(parts)
     far_parts = [onward(far, by) for by in range(1, before + 1)]
     map_parts = [onward(group_map, by) for by in range(1, before)]
-    kinds = 2 + before
+    kinds = 2
     cut = call(
         functools.partial(cut_kernel, axes),
         [array((kinds, tokens, HEAD_DIM))] * heads,
-        [ANY] * (kinds + 1),
+        [ANY] * (kinds + len(value_parts) + 1),
         2000 * cubes,
         [pltpu.SemaphoreType.DMA((heads, kinds))],
     )(queries, values, *value_parts, away)
@@ -557,7 +560,7 @@
             array((1 + before, heads, tokens, HEAD_DIM)),
         ]
         + [array(part.shape) for part in weight_parts],
-        [VMEM] * 4 + [ANY] * (heads + len(weight_parts)),
+        [VMEM] * 4 + [ANY] * (heads + len(weight_parts) + len(value_parts)),
         0,
         [
             pltpu.VMEM((heads, tokens, HEAD_DIM), BF16),
@@ -565,7 +568,7 @@
             pltpu.SemaphoreType.DMA((heads,)),
             pltpu.SemaphoreType.DMA((1 + before, heads)),
         ],
-    )(parts, mixed, even, pair_map, *arrived, *weight_parts)
+    )(parts, mixed, even, pair_map, *arrived, *weight_parts, *value_parts)
     all_values = all_values.reshape(1 + before, units, *tile)
     attended = call(
         functools.partial(attend_kernel, before, blocks),

time: 64.2 us -> 62.7 us (0.977)
  the two profiles are of different devices: /device:TPU:17 before, /device:TPU:0 now
where the time goes in v11:
time: 62.7 us; the launch traced here: 62.4 us
  starting transfers between devices  22.5 us (36%)
  Pallas kernels  17.7 us (28%)
  waiting for transfers between devices  10.7 us (17%)
  blocking collectives  10.6 us (17%)
  other arithmetic  0.77 us (1%)
    ppermute x4, starting transfers between devices, straight(): return lax.ppermute(value, 'ctx', pairs)  10.7 us
    all_to_all x1, blocking collectives, body(): lax.all_to_all(attended.reshape(heads * planes, blocks, *tile), axes, 0,...  10.6 us
    pallas_call x1, Pallas kernels, body(): call(functools.partial(keys_kernel, blocks), [array((units, *tile)), arra...  8.03 us
    ppermute x3, waiting for transfers between devices, crossed(): return lax.ppermute(value, 'ctx', pairs) if turn else value  6.53 us
    all_to_all x1, starting transfers between devices, exchange(): lax.all_to_all(value, 'ctx', 0, 0, axis_index_groups=members, tiled=True)  5.26 us
    ppermute x3, starting transfers between devices, crossed(): return lax.ppermute(value, 'ctx', pairs) if turn else value  3.55 us
    pallas_call x1, Pallas kernels, body(): call(functools.partial(queries_kernel, axes, blocks, len(weight_parts)),...  3.22 us
    ppermute x1, waiting for transfers between devices, body(): weight_parts.append(lax.ppermute(pieces[offset - 1], 'head', turned))  3.09 us
  transfers between devices with their start and end apart: 11, of which 5 were waited for; matrix products, arithmetic and copies ran while one was open for 0% of the time, Pallas kernels for 19%

profile of v11, /device:TPU:0, one launch (start us, length us, event | category | flops | bytes accessed | tf_op | source)
XLA Modules:
  0.0 62.4 jit_solution(10665336070856976937)
XLA Ops:
  0.0 2.8 %shard_map.73 = (bf16[4,528,128]{2,1,0:T(8,128)(2,1)}, bf16[256,128]{1,0:T(8,128)(2,1)}, bf16[256,128]{1,0:T(8,128)(2,1)}, bf16[256,128]{1,0:T(8,128)(2,1)}, bf1...) custom-call(bf16[256,512]{1,0:T(8,128)(2,1)} %d_ref.1, bf16[256,512]{1,0:T(8,128)(2,1)} %k_ref.1, f32[4,256]{1,0:T(4,128)} %rates_hbm.1, ...), custom_call_target="tpu_custom_call" | custom-call | flops 4194304 | bytes 2097152 | tf_op jit(solution)/shard_map/pallas_call | solution.py:496
  2.8 5.3 %all-to-all-start = ((bf16[4,528,128]{2,1,0:T(8,128)(2,1)}), bf16[4,528,128]{2,1,0:T(8,128)(2,1)S(1)}, u32[]{:S(2)}, u32[]{:S(2)}) async-start(bf16[4,528,128]{2,1,0:T(8,128)(2,1)} %get-tuple-element.26), calls=%async_computation | async-start | bytes 1081344 | tf_op jit(solution)/shard_map/all_to_all | solution.py:475
  8.1 4.5 %collective-permute-start = (bf16[256,128]{1,0:T(8,128)(2,1)}, bf16[256,128]{1,0:T(8,128)(2,1)S(1)}, u32[]{:S(2)}, u32[]{:S(2)}) collective-permute-start(bf16[256,128]{1,0:T(8,128)(2,1)} %get-tuple-element.31), channel_id=1, source_target_pairs={{0,16},{4,20},{8,24},{12,28},{1,17},{5,21},{9,25},{13,29},{2,18},{... | collective-permute-start | bytes 196616 | tf_op jit(solution)/shard_map/ppermute | solution.py:488
  12.6 2.8 %collective-permute-start.1 = (bf16[256,128]{1,0:T(8,128)(2,1)}, bf16[256,128]{1,0:T(8,128)(2,1)S(1)}, u32[]{:S(2)}, u32[]{:S(2)}) collective-permute-start(bf16[256,128]{1,0:T(8,128)(2,1)} %get-tuple-element.32), channel_id=1, source_target_pairs={{0,20},{4,16},{8,28},{12,24},{1,21},{5,17},{9,29},{13,25},{2,22},{... | collective-permute-start | bytes 196616 | tf_op jit(solution)/shard_map/ppermute | solution.py:488
  15.4 1.3 %collective-permute-start.2 = (bf16[256,128]{1,0:T(8,128)(2,1)}, bf16[256,128]{1,0:T(8,128)(2,1)S(1)}, u32[]{:S(2)}, u32[]{:S(2)}) collective-permute-start(bf16[256,128]{1,0:T(8,128)(2,1)} %get-tuple-element.33), channel_id=1, source_target_pairs={{0,24},{4,28},{8,16},{12,20},{1,25},{5,29},{9,17},{13,21},{2,26},{... | collective-permute-start | bytes 196616 | tf_op jit(solution)/shard_map/ppermute | solution.py:488
  16.7 2.2 %collective-permute-start.3 = (bf16[256,128]{1,0:T(8,128)(2,1)}, bf16[256,128]{1,0:T(8,128)(2,1)S(1)}, u32[]{:S(2)}, u32[]{:S(2)}) collective-permute-start(bf16[256,128]{1,0:T(8,128)(2,1)} %get-tuple-element.34), channel_id=1, source_target_pairs={{0,28},{4,24},{8,20},{12,16},{1,29},{5,25},{9,21},{13,17},{2,30},{... | collective-permute-start | bytes 196616 | tf_op jit(solution)/shard_map/ppermute | solution.py:488
  18.9 1.6 %collective-permute-start.7 = (bf16[512,1024]{1,0:T(8,128)(2,1)}, bf16[512,1024]{1,0:T(8,128)(2,1)S(1)}, u32[]{:S(2)}, u32[]{:S(2)}) collective-permute-start(bf16[512,1024]{1,0:T(8,128)(2,1)} %get-tuple-element.39), channel_id=1, source_target_pairs={{0,2},{1,3},{2,0},{3,1},{4,6},{5,7},{6,4},{7,5},{8,10},{9,11},{10,... | collective-permute-start | bytes 3145736 | tf_op jit(solution)/shard_map/ppermute | solution.py:526
  20.4 8.0 %shard_map.74 = (bf16[8,128,128]{2,1,0:T(8,128)(2,1)S(1)}, bf16[8,128,128]{2,1,0:T(8,128)(2,1)S(1)}, bf16[8,128,128]{2,1,0:T(8,128)(2,1)S(1)}, bf16[4,2,128,128]...) custom-call(bf16[4,528,128]{2,1,0:T(8,128)(2,1)S(1)} %all-to-all-don, ...), custom_call_target="tpu_custom_call" | custom-call | flops 1677721600 | bytes 2097152 | tf_op jit(solution)/shard_map/pallas_call | solution.py:529
  28.5 1.3 %collective-permute-start.8 = (bf16[8,128,128]{2,1,0:T(8,128)(2,1)S(1)}, bf16[8,128,128]{2,1,0:T(8,128)(2,1)S(1)}, u32[]{:S(2)}, u32[]{:S(2)}) collective-permute-start(bf16[8,128,128]{2,1,0:T(8,128)(2,1)S(1)} %get-tuple-element.45), channel_id=1, source_target_pairs={{0,16},{4,20},{8,24},{12,28},{1,17},{5,21},{9,25},{13,29},{2,18},{... | collective-permute-start | bytes 786440 | tf_op jit(solution)/shard_map/ppermute | solution.py:479
  29.8 0.2 shard_map.75
  30.0 0.6 %collective-permute-start.4 = (bf16[2,256,128]{2,1,0:T(8,128)(2,1)S(1)}, bf16[2,256,128]{2,1,0:T(8,128)(2,1)S(1)}, u32[]{:S(2)}, u32[]{:S(2)}) collective-permute-start(bf16[2,256,128]{2,1,0:T(8,128)(2,1)S(1)} %get-tuple-element.36), channel_id=1, source_target_pairs={{0,4},{4,0},{8,12},{12,8},{16,20},{20,16},{24,28},{28,24},{1,5},{5... | collective-permute-start | bytes 393224 | tf_op jit(solution)/shard_map/ppermute | solution.py:483
  30.7 2.2 %collective-permute-start.5 = (bf16[2,256,128]{2,1,0:T(8,128)(2,1)S(1)}, bf16[2,256,128]{2,1,0:T(8,128)(2,1)S(1)}, u32[]{:S(2)}, u32[]{:S(2)}) collective-permute-start(bf16[2,256,128]{2,1,0:T(8,128)(2,1)S(1)} %get-tuple-element.37), channel_id=1, source_target_pairs={{0,8},{4,12},{8,0},{12,4},{16,24},{20,28},{24,16},{28,20},{1,9},{5... | collective-permute-start | bytes 393224 | tf_op jit(solution)/shard_map/ppermute | solution.py:483
  32.8 0.8 %collective-permute-start.6 = (bf16[2,256,128]{2,1,0:T(8,128)(2,1)S(1)}, bf16[2,256,128]{2,1,0:T(8,128)(2,1)S(1)}, u32[]{:S(2)}, u32[]{:S(2)}) collective-permute-start(bf16[2,256,128]{2,1,0:T(8,128)(2,1)S(1)} %get-tuple-element.38), channel_id=1, source_target_pairs={{0,12},{4,8},{8,4},{12,0},{16,28},{20,24},{24,20},{28,16},{1,13},{... | collective-permute-start | bytes 393224 | tf_op jit(solution)/shard_map/ppermute | solution.py:483
  33.6 2.9 %collective-permute-done.4.refs_1_ = bf16[2,256,128]{2,1,0:T(8,128)(2,1)S(1)} collective-permute-done((bf16[2,256,128]{2,1,0:T(8,128)(2,1)S(1)}, bf16[2,256,128]{2,1,0:T(8,128)(2,1)S(1)}, u32[]{:S(2)}, u32[]{:S(2)}) %collective-permute-start.4) | collective-permute-done | bytes 131104 | tf_op jit(solution)/shard_map/ppermute | solution.py:483
  36.5 2.2 %collective-permute-done.5.refs_2_ = bf16[2,256,128]{2,1,0:T(8,128)(2,1)S(1)} collective-permute-done((bf16[2,256,128]{2,1,0:T(8,128)(2,1)S(1)}, bf16[2,256,128]{2,1,0:T(8,128)(2,1)S(1)}, u32[]{:S(2)}, u32[]{:S(2)}) %collective-permute-start.5) | collective-permute-done | bytes 131104 | tf_op jit(solution)/shard_map/ppermute | solution.py:483
  38.7 1.4 %collective-permute-done.6.refs_3_ = bf16[2,256,128]{2,1,0:T(8,128)(2,1)S(1)} collective-permute-done((bf16[2,256,128]{2,1,0:T(8,128)(2,1)S(1)}, bf16[2,256,128]{2,1,0:T(8,128)(2,1)S(1)}, u32[]{:S(2)}, u32[]{:S(2)}) %collective-permute-start.6) | collective-permute-done | bytes 131104 | tf_op jit(solution)/shard_map/ppermute | solution.py:483
  40.1 3.1 %collective-permute-done.7.refs_4_ = bf16[512,1024]{1,0:T(8,128)(2,1)S(1)} collective-permute-done((bf16[512,1024]{1,0:T(8,128)(2,1)}, bf16[512,1024]{1,0:T(8,128)(2,1)S(1)}, u32[]{:S(2)}, u32[]{:S(2)}) %collective-permute-start.7) | collective-permute-done | bytes 1048608 | tf_op jit(solution)/shard_map/ppermute | solution.py:526
  43.2 3.2 %shard_map.76 = (f32[8,128,128]{2,1,0:T(8,128)S(1)}, bf16[8,5,128,128]{3,2,1,0:T(8,128)(2,1)S(1)}, bf16[2,4,256,128]{3,2,1,0:T(8,128)(2,1)S(1)}, bf16[512,1024]{1,0:T(8,128)(2,1)S(1)}) custom-call(bf16[4,528,128]{2,1,0:T(8,128)(2,1)S(1)} %all-to-all-done.part_ref, bf16[8,128,256]{2,1,0:T(8,128)(2,1)S(1)} %get-tuple-element.28.mixed_ref, ...), custom_call_target="tpu_custom_call" | custom-call | bytes 2097152 | tf_op jit(solution)/shard_map/pallas_call | solution.py:555
  46.5 2.5 %shard_map.77 = bf16[4,2,2,128,128]{4,3,2,1,0:T(8,128)(2,1)S(1)} custom-call(s32[8,128]{1,0:T(8,128)S(1)} %get-tuple-element.27.refs_6_.away_ref, bf16[8,5,128,128]{3,2,1,0:T(8,128)(2,1)S(1)} %get-tuple-element.40.moving_ref, f32[8,128,128]{2,1,0:T(8,128)S(1)} %get-tuple-element.41.inner_ref, bf16[8,128,128]{2,1,0:T(8,128)(2,1)S(1)} %get-tuple-element.42.end_ref, ...), custom_call_target="tpu_custom_call" | custom-call | flops 838860800 | bytes 2097152 | tf_op jit(solution)/shard_map/pallas_call | solution.py:573
  49.0 10.6 %all_to_all.10 = bf16[8,2,128,128]{3,2,1,0:T(8,128)(2,1)S(1)} all-to-all(bf16[8,2,128,128]{3,2,1,0:T(8,128)(2,1)S(1)} %bitcast.5), channel_id=1, replica_groups={{0,2,4,6,8,10,12,14},{1,3,5,7,9,11,13,15},{16,18,20,22,24,26,28,30},{17..., dimensions={0} | all-to-all | bytes 1048576 | tf_op jit(solution)/shard_map/all_to_all | solution.py:589
  59.6 0.4 shard_map.79
  60.1 0.4 shard_map.78
  60.5 1.1 %collective-permute-done.9 = bf16[256,512]{1,0:T(8,128)(2,1)S(1)} collective-permute-done((bf16[256,512]{1,0:T(8,128)(2,1)S(1)}, bf16[256,512]{1,0:T(8,128)(2,1)S(1)}, u32[]{:S(2)}, u32[]{:S(2)}) %collective-permute-start.9) | collective-permute-done | bytes 262176 | tf_op jit(solution)/shard_map/ppermute | solution.py:602
  61.6 0.8 %add_convert_fusion = bf16[256,512]{1,0:T(8,128)(2,1)} fusion(f32[256,512]{1,0:T(8,128)S(1)} %shard_map.78, bf16[256,512]{1,0:T(8,128)(2,1)S(1)} %collective-permute-done.9), kind=kLoop, calls=%fused_computation | loop fusion | flops 393216 | bytes 1048576 | tf_op jit(solution)/shard_map/convert_element_type | solution.py:603
  (13 shorter events, 0.1 us)
Async XLA Ops:
  2.8 17.6 %all-to-all-start = ((bf16[4,528,128]{2,1,0:T(8,128)(2,1)}), bf16[4,528,128]{2,1,0:T(8,128)(2,1)S(1)}, u32[]{:S(2)}, u32[]{:S(2)}) async-start(bf16[4,528,128]{2,1,0:T(8,128)(2,1)} %get-tuple-element.26), calls=%async_computation | async-start | bytes 1081344 | tf_op jit(solution)/shard_map/all_to_all | solution.py:475
  8.1 20.4 %collective-permute-start = (bf16[256,128]{1,0:T(8,128)(2,1)}, bf16[256,128]{1,0:T(8,128)(2,1)S(1)}, u32[]{:S(2)}, u32[]{:S(2)}) collective-permute-start(bf16[256,128]{1,0:T(8,128)(2,1)} %get-tuple-element.31), channel_id=1, source_target_pairs={{0,16},{4,20},{8,24},{12,28},{1,17},{5,21},{9,25},{13,29},{2,18},{... | collective-permute-start | bytes 196616 | tf_op jit(solution)/shard_map/ppermute | solution.py:488
  12.6 17.2 %collective-permute-start.1 = (bf16[256,128]{1,0:T(8,128)(2,1)}, bf16[256,128]{1,0:T(8,128)(2,1)S(1)}, u32[]{:S(2)}, u32[]{:S(2)}) collective-permute-start(bf16[256,128]{1,0:T(8,128)(2,1)} %get-tuple-element.32), channel_id=1, source_target_pairs={{0,20},{4,16},{8,28},{12,24},{1,21},{5,17},{9,29},{13,25},{2,22},{... | collective-permute-start | bytes 196616 | tf_op jit(solution)/shard_map/ppermute | solution.py:488
  15.4 14.4 %collective-permute-start.2 = (bf16[256,128]{1,0:T(8,128)(2,1)}, bf16[256,128]{1,0:T(8,128)(2,1)S(1)}, u32[]{:S(2)}, u32[]{:S(2)}) collective-permute-start(bf16[256,128]{1,0:T(8,128)(2,1)} %get-tuple-element.33), channel_id=1, source_target_pairs={{0,24},{4,28},{8,16},{12,20},{1,25},{5,29},{9,17},{13,21},{2,26},{... | collective-permute-start | bytes 196616 | tf_op jit(solution)/shard_map/ppermute | solution.py:488
  16.7 13.1 %collective-permute-start.3 = (bf16[256,128]{1,0:T(8,128)(2,1)}, bf16[256,128]{1,0:T(8,128)(2,1)S(1)}, u32[]{:S(2)}, u32[]{:S(2)}) collective-permute-start(bf16[256,128]{1,0:T(8,128)(2,1)} %get-tuple-element.34), channel_id=1, source_target_pairs={{0,28},{4,24},{8,20},{12,16},{1,29},{5,25},{9,21},{13,17},{2,30},{... | collective-permute-start | bytes 196616 | tf_op jit(solution)/shard_map/ppermute | solution.py:488
  18.9 11.0 %copy-start.1 = (bf16[256,512]{1,0:T(8,128)(2,1)S(1)}, bf16[256,512]{1,0:T(8,128)(2,1)}, u32[]{:S(2)}) copy-start(bf16[256,512]{1,0:T(8,128)(2,1)} %refs_1_.1) | copy-start | bytes 786436
  18.9 11.0 %copy-start.2 = (bf16[256,512]{1,0:T(8,128)(2,1)S(1)}, bf16[256,512]{1,0:T(8,128)(2,1)}, u32[]{:S(2)}) copy-start(bf16[256,512]{1,0:T(8,128)(2,1)} %refs_0_.1) | copy-start | bytes 786436
  18.9 24.3 %collective-permute-start.7 = (bf16[512,1024]{1,0:T(8,128)(2,1)}, bf16[512,1024]{1,0:T(8,128)(2,1)S(1)}, u32[]{:S(2)}, u32[]{:S(2)}) collective-permute-start(bf16[512,1024]{1,0:T(8,128)(2,1)} %get-tuple-element.39), channel_id=1, source_target_pairs={{0,2},{1,3},{2,0},{3,1},{4,6},{5,7},{6,4},{7,5},{8,10},{9,11},{10,... | collective-permute-start | bytes 3145736 | tf_op jit(solution)/shard_map/ppermute | solution.py:526
  28.5 18.0 %collective-permute-start.8 = (bf16[8,128,128]{2,1,0:T(8,128)(2,1)S(1)}, bf16[8,128,128]{2,1,0:T(8,128)(2,1)S(1)}, u32[]{:S(2)}, u32[]{:S(2)}) collective-permute-start(bf16[8,128,128]{2,1,0:T(8,128)(2,1)S(1)} %get-tuple-element.45), channel_id=1, source_target_pairs={{0,16},{4,20},{8,24},{12,28},{1,17},{5,21},{9,25},{13,29},{2,18},{... | collective-permute-start | bytes 786440 | tf_op jit(solution)/shard_map/ppermute | solution.py:479
  30.0 6.4 %collective-permute-start.4 = (bf16[2,256,128]{2,1,0:T(8,128)(2,1)S(1)}, bf16[2,256,128]{2,1,0:T(8,128)(2,1)S(1)}, u32[]{:S(2)}, u32[]{:S(2)}) collective-permute-start(bf16[2,256,128]{2,1,0:T(8,128)(2,1)S(1)} %get-tuple-element.36), channel_id=1, source_target_pairs={{0,4},{4,0},{8,12},{12,8},{16,20},{20,16},{24,28},{28,24},{1,5},{5... | collective-permute-start | bytes 393224 | tf_op jit(solution)/shard_map/ppermute | solution.py:483
  30.7 8.1 %collective-permute-start.5 = (bf16[2,256,128]{2,1,0:T(8,128)(2,1)S(1)}, bf16[2,256,128]{2,1,0:T(8,128)(2,1)S(1)}, u32[]{:S(2)}, u32[]{:S(2)}) collective-permute-start(bf16[2,256,128]{2,1,0:T(8,128)(2,1)S(1)} %get-tuple-element.37), channel_id=1, source_target_pairs={{0,8},{4,12},{8,0},{12,4},{16,24},{20,28},{24,16},{28,20},{1,9},{5... | collective-permute-start | bytes 393224 | tf_op jit(solution)/shard_map/ppermute | solution.py:483
  32.8 7.3 %collective-permute-start.6 = (bf16[2,256,128]{2,1,0:T(8,128)(2,1)S(1)}, bf16[2,256,128]{2,1,0:T(8,128)(2,1)S(1)}, u32[]{:S(2)}, u32[]{:S(2)}) collective-permute-start(bf16[2,256,128]{2,1,0:T(8,128)(2,1)S(1)} %get-tuple-element.38), channel_id=1, source_target_pairs={{0,12},{4,8},{8,4},{12,0},{16,28},{20,24},{24,20},{28,16},{1,13},{... | collective-permute-start | bytes 393224 | tf_op jit(solution)/shard_map/ppermute | solution.py:483
  46.5 13.1 %copy-start = (bf16[512,2048]{1,0:T(8,128)(2,1)S(1)}, bf16[512,2048]{1,0:T(8,128)(2,1)}, u32[]{:S(2)}) copy-start(bf16[512,2048]{1,0:T(8,128)(2,1)} %own_ref.3) | copy-start | bytes 6291460
  60.0 1.6 %collective-permute-start.9 = (bf16[256,512]{1,0:T(8,128)(2,1)S(1)}, bf16[256,512]{1,0:T(8,128)(2,1)S(1)}, u32[]{:S(2)}, u32[]{:S(2)}) collective-permute-start(bf16[256,512]{1,0:T(8,128)(2,1)S(1)} %shard_map.79), channel_id=1, source_target_pairs={{0,1},{1,0},{2,3},{3,2},{4,5},{5,4},{6,7},{7,6},{8,9},{9,8},{10,11... | collective-permute-start | bytes 786440 | tf_op jit(solution)/shard_map/ppermute | solution.py:602

commit v12 on v11

--- a/solution.py
+++ b/solution.py
@@ -64,8 +64,8 @@
     return copies
 
 
-def pack_kernel(axes, cores, d_ref, k_ref, rates_hbm, selected_hbm, values_ref, weight_ref,
-                *refs):
+def pack_kernel(axes, cores, d_ref, k_ref, q_ref, rates_hbm, selected_hbm, values_ref,
+                weight_ref, *refs):
     tokens = d_ref.shape[0]
     heads = d_ref.shape[1] // HEAD_DIM
     blocks = tokens // BLOCK
@@ -79,7 +79,7 @@
     plane = lax.axis_index(axes[1]) // cores
     first_block = device * blocks
     few_copies = fetched([rates_hbm, selected_hbm], [rates_ref, selected_ref], few_sems)
-    sources = (d_ref, k_ref)
+    sources = (d_ref, k_ref, q_ref)
     copies = []
     for head in range(heads):
         columns = pl.ds(head * HEAD_DIM, HEAD_DIM)
@@ -151,20 +151,16 @@
         copy.wait()
 
 
-def cut_kernel(axes, *refs):
+def cut_kernel(axes, values_ref, *refs):
     sems = refs[-1]
-    parts = refs[-1 - sems.shape[0]:-1]
-    sources = refs[:sems.shape[1]]
     heads = sems.shape[0]
     place = lax.rem(lax.axis_index(axes[0]), heads)
-    copies = []
-    for turn in range(heads):
-        cut = pl.multiple_of(lax.bitwise_xor(place, turn) * HEAD_DIM, HEAD_DIM)
-        copies += fetched(
-            [source.at[:, pl.ds(cut, HEAD_DIM)] for source in sources],
-            [parts[turn].at[kind] for kind in range(len(sources))],
-            sems.at[turn],
-        )
+    cuts = [
+        pl.multiple_of(lax.bitwise_xor(place, turn) * HEAD_DIM, HEAD_DIM) for turn in range(heads)
+    ]
+    copies = fetched(
+        [values_ref.at[:, pl.ds(cut, HEAD_DIM)] for cut in cuts], refs[-1 - heads:-1], sems
+    )
     for copy in copies:
         copy.wait()
 
@@ -236,7 +232,7 @@
     def terms(unit):
         direction = rows_of(part_ref, blocks, unit, 0)
         key = rows_of(part_ref, blocks, unit, 1)
-        extra = part_ref[unit // blocks, 2 * blocks * BLOCK:].astype(F32)
+        extra = part_ref[unit // blocks, 3 * blocks * BLOCK:].astype(F32)
         first = TERMS * (unit % blocks)
         rate = extra[first:first + 1] + extra[first + 1:first + 2] + extra[first + 2:first + 3]
         listed = TERMS * blocks + unit % blocks
@@ -303,33 +299,24 @@
     group_ref[1] = onward[1]
 
 
-def queries_kernel(axes, blocks, count, part_ref, mixed_ref, even_ref, pair_ref, *refs):
+def queries_kernel(axes, blocks, part_ref, mixed_ref, even_ref, pair_ref, *refs):
     heads = part_ref.shape[0]
     units = heads * blocks
-    arrived, weights = refs[:heads], refs[heads:heads + count]
-    inner_ref, moving_ref, values_ref, *weight_refs = refs[-7 - count:-4]
-    query_ref, sems, query_sems, value_sems = refs[-4:]
+    inner_ref, moving_ref, values_ref, sems = refs[-4:]
     place = lax.rem(lax.axis_index(axes[0]), heads)
-    sources = [lax.bitwise_xor(place, turn) for turn in range(heads)]
-    query_copies = fetched(
-        [part.at[0] for part in arrived], [query_ref.at[source] for source in sources], query_sems
-    )
-    copies = fetched(weights, weight_refs, sems)
-    straight = refs[heads + count:-7 - count]
+    copies = []
     for kind in range(values_ref.shape[0]):
         copies += fetched(
-            straight[(kind - 1) * heads:kind * heads] if kind else [part.at[1] for part in arrived],
-            [values_ref.at[kind, source] for source in sources],
-            value_sems.at[kind],
+            refs[kind * heads:(kind + 1) * heads],
+            [values_ref.at[kind, lax.bitwise_xor(place, turn)] for turn in range(heads)],
+            sems.at[kind],
         )
-    for copy in query_copies:
-        copy.wait()
     rows, columns = square_iotas()
     current = []
     for unit in range(units):
         direction = rows_of(part_ref, blocks, unit, 0)
         key = rows_of(part_ref, blocks, unit, 1)
-        query = rows_of(query_ref, blocks, unit, 0)
+        query = rows_of(part_ref, blocks, unit, 2)
         query_proj = split(jnp.where(rows >= columns, nt(query, direction), 0.0))
         ahead = nn(jnp.concatenate(query_proj, 0), mixed_ref[unit])
         ahead = ahead[:BLOCK] + ahead[BLOCK:]
@@ -373,7 +360,11 @@
 
 def attend_kernel(before, blocks, away_ref, moving_ref, inner_ref, end_ref, tail_ref,
                   values_ref, *refs):
-    far_keys, group_maps, out_ref = refs[:before], refs[before:-1], refs[-1]
+    maps = max(before - 1, 0)
+    far_keys, group_maps = refs[:before], refs[before:before + maps]
+    count = (len(refs) - before - maps - 2) // 2
+    out_ref, sems = refs[-2 - count], refs[-1]
+    copies = fetched(refs[before + maps:before + maps + count], refs[-1 - count:-1], sems)
     units = inner_ref.shape[0]
     rows, columns = square_iotas()
     scale = HEAD_DIM ** (-0.5)
@@ -410,6 +401,8 @@
             out_ref[unit // blocks, plane, unit % blocks] = blended
 
     interleaved([steps(unit) for unit in range(units)], 1)
+    for copy in copies:
+        copy.wait()
 
 
 def project_kernel(axes, other, cores, attended_ref, own_ref, *refs):
@@ -490,7 +483,7 @@
     def array(shape, kind=BF16):
         return jax.ShapeDtypeStruct(shape, kind)
 
-    part_shape = (heads, 2 * tokens + EXTRA, HEAD_DIM)
+    part_shape = (heads, 3 * tokens + EXTRA, HEAD_DIM)
     width = out_weight.shape[1] // planes
     piece_shape = (out_weight.shape[0], width)
     packed, *rest = call(
@@ -498,7 +491,7 @@
         [array(part_shape)]
         + [array((tokens, HEAD_DIM))] * heads
         + [array(piece_shape)] * (planes - 1),
-        [ANY] * 6,
+        [ANY] * 7,
         cubes,
         [
             pltpu.VMEM(part_shape, BF16),
@@ -506,7 +499,7 @@
             pltpu.SMEM(selected.shape, jnp.int32),
             pltpu.VMEM((heads, tokens, HEAD_DIM), BF16),
             pltpu.VMEM((max(planes - 1, 1), *piece_shape), BF16),
-            pltpu.SemaphoreType.DMA((heads, 2)),
+            pltpu.SemaphoreType.DMA((heads, 3)),
             pltpu.SemaphoreType.DMA((2,)),
             pltpu.SemaphoreType.DMA((heads,)),
             pltpu.SemaphoreType.DMA((heads,)),
@@ -515,7 +508,7 @@
         ],
         [ANY] * (heads + planes),
         56,
-    )(directions, keys, rates, selected, values, out_weight)
+    )(directions, keys, queries, rates, selected, values, out_weight)
     value_cuts, pieces = rest[:heads], rest[heads:]
     value_parts = [
         straight(value_cuts[turn], turn, by) for by in range(1, before + 1) for turn in range(heads)
@@ -543,39 +536,33 @@
     )(parts)
     far_parts = [onward(far, by) for by in range(1, before + 1)]
     map_parts = [onward(group_map, by) for by in range(1, before)]
-    kinds = 2
     cut = call(
         functools.partial(cut_kernel, axes),
-        [array((kinds, tokens, HEAD_DIM))] * heads,
-        [ANY] * (kinds + len(value_parts) + 1),
+        [array((tokens, HEAD_DIM))] * heads,
+        [ANY] * (len(value_parts) + 2),
         2000 * cubes,
-        [pltpu.SemaphoreType.DMA((heads, kinds))],
-    )(queries, values, *value_parts, away)
-    arrived = [crossed(cut[turn], turn) for turn in range(heads)]
-    inner, moving, all_values, *weight_parts = call(
-        functools.partial(queries_kernel, axes, blocks, len(weight_parts)),
+        [pltpu.SemaphoreType.DMA((heads,))],
+    )(values, *value_parts, away)
+    own_parts = [crossed(cut[turn], turn) for turn in range(heads)]
+    inner, moving, all_values = call(
+        functools.partial(queries_kernel, axes, blocks),
         [
             array((units, BLOCK, BLOCK), F32),
             array((units, pairs + 1, *tile)),
             array((1 + before, heads, tokens, HEAD_DIM)),
-        ]
-        + [array(part.shape) for part in weight_parts],
-        [VMEM] * 4 + [ANY] * (heads + len(weight_parts) + len(value_parts)),
+        ],
+        [VMEM] * 4 + [ANY] * (heads + len(value_parts)),
         0,
-        [
-            pltpu.VMEM((heads, tokens, HEAD_DIM), BF16),
-            pltpu.SemaphoreType.DMA((max(len(weight_parts), 1),)),
-            pltpu.SemaphoreType.DMA((heads,)),
-            pltpu.SemaphoreType.DMA((1 + before, heads)),
-        ],
-    )(parts, mixed, even, pair_map, *arrived, *weight_parts, *value_parts)
+        [pltpu.SemaphoreType.DMA((1 + before, heads))],
+    )(parts, mixed, even, pair_map, *own_parts, *value_parts)
     all_values = all_values.reshape(1 + before, units, *tile)
-    attended = call(
+    attended, *weight_parts = call(
         functools.partial(attend_kernel, before, blocks),
-        array((heads, planes, blocks, *tile)),
-        [SMEM] + [VMEM] * (5 + before + len(map_parts)),
+        [array((heads, planes, blocks, *tile))] + [array(part.shape) for part in weight_parts],
+        [SMEM] + [VMEM] * (5 + before + len(map_parts)) + [ANY] * len(weight_parts),
         200 * cubes,
-    )(away, moving, inner, end, tail, all_values, *far_parts, *map_parts)
+        [pltpu.SemaphoreType.DMA((planes,))],
+    )(away, moving, inner, end, tail, all_values, *far_parts, *map_parts, *weight_parts)
 
     returns = [
         [

time: 62.7 us -> 64.1 us (1.022)
  waiting for transfers between devices: 10.7 us -> 6.25 us
  starting transfers between devices: 22.5 us -> 26 us
  blocking collectives: 10.6 us -> 13.2 us
    ppermute x1, waiting for transfers between devices: 3.09 us -> 0.01 us  [body(): weight_parts.append(lax.ppermute(pieces[offset - 1], 'head', turned))]
    all_to_all x1, blocking collectives: 10.6 us -> 13.2 us  [body(): lax.all_to_all(attended.reshape(heads * planes, blocks, *tile), axes, 0,...]
    ppermute x1, starting transfers between devices: 1.29 us -> 3.3 us  [onward(): lax.ppermute(value, 'ctx', [(i, i + shift) for i in range(ctx_size - shif...]
    ppermute x3, starting transfers between devices: 3.55 us -> 5.01 us  [crossed(): return lax.ppermute(value, 'ctx', pairs) if turn else value]
    ppermute x3, waiting for transfers between devices: 6.53 us -> 5.16 us  [crossed(): return lax.ppermute(value, 'ctx', pairs) if turn else value]
  transfers between devices with their start and end apart: 11 -> 11, of which waited for: 5 -> 3; matrix products, arithmetic and copies ran while one was open for 0% -> 0% of each run, Pallas kernels for 19% -> 18%
where the time goes in v12:
time: 64.1 us; the launch traced here: 63.7 us
  starting transfers between devices  26 us (41%)
  Pallas kernels  17.3 us (27%)
  blocking collectives  13.2 us (21%)
  waiting for transfers between devices  6.25 us (10%)
  other arithmetic  0.77 us (1%)
    all_to_all x1, blocking collectives, body(): lax.all_to_all(attended.reshape(heads * planes, blocks, *tile), axes, 0,...  13.2 us
    ppermute x4, starting transfers between devices, straight(): return lax.ppermute(value, 'ctx', pairs)  10.9 us
    pallas_call x1, Pallas kernels, body(): call(functools.partial(keys_kernel, blocks), [array((units, *tile)), arra...  8.03 us
    all_to_all x1, starting transfers between devices, exchange(): lax.all_to_all(value, 'ctx', 0, 0, axis_index_groups=members, tiled=True)  5.26 us
    ppermute x3, waiting for transfers between devices, crossed(): return lax.ppermute(value, 'ctx', pairs) if turn else value  5.16 us
    ppermute x3, starting transfers between devices, crossed(): return lax.ppermute(value, 'ctx', pairs) if turn else value  5.01 us
    ppermute x1, starting transfers between devices, onward(): lax.ppermute(value, 'ctx', [(i, i + shift) for i in range(ctx_size - shif...  3.3 us
    pallas_call x1, Pallas kernels, body(): call(functools.partial(pack_kernel, axes, cores), [array(part_shape)] + [...  2.94 us
  transfers between devices with their start and end apart: 11, of which 3 were waited for; matrix products, arithmetic and copies ran while one was open for 0% of the time, Pallas kernels for 18%

profile of v12, /device:TPU:0, one launch (start us, length us, event | category | flops | bytes accessed | tf_op | source)
XLA Modules:
  0.0 63.7 jit_solution(3254288602759402923)
XLA Ops:
  0.0 2.9 %shard_map.73 = (bf16[4,784,128]{2,1,0:T(8,128)(2,1)}, bf16[256,128]{1,0:T(8,128)(2,1)}, bf16[256,128]{1,0:T(8,128)(2,1)}, bf16[256,128]{1,0:T(8,128)(2,1)}, bf1...) custom-call(bf16[256,512]{1,0:T(8,128)(2,1)} %d_ref.1, bf16[256,512]{1,0:T(8,128)(2,1)} %k_ref.1, ...), custom_call_target="tpu_custom_call" | custom-call | flops 4194304 | bytes 2097152 | tf_op jit(solution)/shard_map/pallas_call | solution.py:489
  2.9 5.3 %all-to-all-start = ((bf16[4,784,128]{2,1,0:T(8,128)(2,1)}), bf16[4,784,128]{2,1,0:T(8,128)(2,1)S(1)}, u32[]{:S(2)}, u32[]{:S(2)}) async-start(bf16[4,784,128]{2,1,0:T(8,128)(2,1)} %get-tuple-element.27), calls=%async_computation | async-start | bytes 1605632 | tf_op jit(solution)/shard_map/all_to_all | solution.py:468
  8.2 1.5 %collective-permute-start.8 = (bf16[512,1024]{1,0:T(8,128)(2,1)}, bf16[512,1024]{1,0:T(8,128)(2,1)S(1)}, u32[]{:S(2)}, u32[]{:S(2)}) collective-permute-start(bf16[512,1024]{1,0:T(8,128)(2,1)} %get-tuple-element.46), channel_id=1, source_target_pairs={{0,2},{1,3},{2,0},{3,1},{4,6},{5,7},{6,4},{7,5},{8,10},{9,11},{10,... | collective-permute-start | bytes 3145736 | tf_op jit(solution)/shard_map/ppermute | solution.py:519
  9.7 4.5 %collective-permute-start = (bf16[256,128]{1,0:T(8,128)(2,1)}, bf16[256,128]{1,0:T(8,128)(2,1)S(1)}, u32[]{:S(2)}, u32[]{:S(2)}) collective-permute-start(bf16[256,128]{1,0:T(8,128)(2,1)} %get-tuple-element.32), channel_id=1, source_target_pairs={{0,16},{4,20},{8,24},{12,28},{1,17},{5,21},{9,25},{13,29},{2,18},{... | collective-permute-start | bytes 196616 | tf_op jit(solution)/shard_map/ppermute | solution.py:481
  14.2 2.8 %collective-permute-start.1 = (bf16[256,128]{1,0:T(8,128)(2,1)}, bf16[256,128]{1,0:T(8,128)(2,1)S(1)}, u32[]{:S(2)}, u32[]{:S(2)}) collective-permute-start(bf16[256,128]{1,0:T(8,128)(2,1)} %get-tuple-element.33), channel_id=1, source_target_pairs={{0,20},{4,16},{8,28},{12,24},{1,21},{5,17},{9,29},{13,25},{2,22},{... | collective-permute-start | bytes 196616 | tf_op jit(solution)/shard_map/ppermute | solution.py:481
  17.0 1.3 %collective-permute-start.2 = (bf16[256,128]{1,0:T(8,128)(2,1)}, bf16[256,128]{1,0:T(8,128)(2,1)S(1)}, u32[]{:S(2)}, u32[]{:S(2)}) collective-permute-start(bf16[256,128]{1,0:T(8,128)(2,1)} %get-tuple-element.34), channel_id=1, source_target_pairs={{0,24},{4,28},{8,16},{12,20},{1,25},{5,29},{9,17},{13,21},{2,26},{... | collective-permute-start | bytes 196616 | tf_op jit(solution)/shard_map/ppermute | solution.py:481
  18.3 0.0 copy-start.1
  18.3 2.3 %collective-permute-start.3 = (bf16[256,128]{1,0:T(8,128)(2,1)}, bf16[256,128]{1,0:T(8,128)(2,1)S(1)}, u32[]{:S(2)}, u32[]{:S(2)}) collective-permute-start(bf16[256,128]{1,0:T(8,128)(2,1)} %get-tuple-element.35), channel_id=1, source_target_pairs={{0,28},{4,24},{8,20},{12,16},{1,29},{5,25},{9,21},{13,17},{2,30},{... | collective-permute-start | bytes 196616 | tf_op jit(solution)/shard_map/ppermute | solution.py:481
  20.6 8.0 %shard_map.74 = (bf16[8,128,128]{2,1,0:T(8,128)(2,1)S(1)}, bf16[8,128,128]{2,1,0:T(8,128)(2,1)S(1)}, bf16[8,128,128]{2,1,0:T(8,128)(2,1)S(1)}, bf16[4,2,128,128]...) custom-call(bf16[4,784,128]{2,1,0:T(8,128)(2,1)S(1)} %all-to-all-don, ...), custom_call_target="tpu_custom_call" | custom-call | flops 1677721600 | bytes 2097152 | tf_op jit(solution)/shard_map/pallas_call | solution.py:522
  28.6 3.3 %collective-permute-start.7 = (bf16[8,128,128]{2,1,0:T(8,128)(2,1)S(1)}, bf16[8,128,128]{2,1,0:T(8,128)(2,1)S(1)}, u32[]{:S(2)}, u32[]{:S(2)}) collective-permute-start(bf16[8,128,128]{2,1,0:T(8,128)(2,1)S(1)} %get-tuple-element.45), channel_id=1, source_target_pairs={{0,16},{4,20},{8,24},{12,28},{1,17},{5,21},{9,25},{13,29},{2,18},{... | collective-permute-start | bytes 786440 | tf_op jit(solution)/shard_map/ppermute | solution.py:472
  32.0 0.1 shard_map.75
  32.1 2.5 %collective-permute-start.4 = (bf16[256,128]{1,0:T(8,128)(2,1)S(1)}, bf16[256,128]{1,0:T(8,128)(2,1)S(1)}, u32[]{:S(2)}, u32[]{:S(2)}) collective-permute-start(bf16[256,128]{1,0:T(8,128)(2,1)S(1)} %get-tuple-element.37), channel_id=1, source_target_pairs={{0,4},{4,0},{8,12},{12,8},{16,20},{20,16},{24,28},{28,24},{1,5},{5... | collective-permute-start | bytes 196616 | tf_op jit(solution)/shard_map/ppermute | solution.py:476
  34.6 2.5 %collective-permute-start.5 = (bf16[256,128]{1,0:T(8,128)(2,1)S(1)}, bf16[256,128]{1,0:T(8,128)(2,1)S(1)}, u32[]{:S(2)}, u32[]{:S(2)}) collective-permute-start(bf16[256,128]{1,0:T(8,128)(2,1)S(1)} %get-tuple-element.38), channel_id=1, source_target_pairs={{0,8},{4,12},{8,0},{12,4},{16,24},{20,28},{24,16},{28,20},{1,9},{5... | collective-permute-start | bytes 196616 | tf_op jit(solution)/shard_map/ppermute | solution.py:476
  37.1 2.2 %collective-permute-done.5.refs_2_ = bf16[256,128]{1,0:T(8,128)(2,1)S(1)} collective-permute-done((bf16[256,128]{1,0:T(8,128)(2,1)S(1)}, bf16[256,128]{1,0:T(8,128)(2,1)S(1)}, u32[]{:S(2)}, u32[]{:S(2)}) %collective-permute-start.5) | collective-permute-done | bytes 65568 | tf_op jit(solution)/shard_map/ppermute | solution.py:476
  39.4 2.9 %collective-permute-done.6.refs_3_ = bf16[256,128]{1,0:T(8,128)(2,1)S(1)} collective-permute-done((bf16[256,128]{1,0:T(8,128)(2,1)S(1)}, bf16[256,128]{1,0:T(8,128)(2,1)S(1)}, u32[]{:S(2)}, u32[]{:S(2)}) %collective-permute-start.6) | collective-permute-done | bytes 65568 | tf_op jit(solution)/shard_map/ppermute | solution.py:476
  42.3 2.8 %shard_map.76 = (f32[8,128,128]{2,1,0:T(8,128)S(1)}, bf16[8,5,128,128]{3,2,1,0:T(8,128)(2,1)S(1)}, bf16[2,4,256,128]{3,2,1,0:T(8,128)(2,1)S(1)}) custom-call(bf16[4,784,128]{2,1,0:T(8,128)(2,1)S(1)} %all-to-all-done.part_ref, bf16[8,128,256]{2,1,0:T(8,128)(2,1)S(1)} %get-tuple-element.29.mixed_ref, bf16[4,2,128,128]{3,2,1,0:T(8,128)(2,1)S(1)} %get-tuple-element.30.even_ref, ...), custom_call_target="tpu_custom_call" | custom-call | bytes 2097152 | tf_op jit(solution)/shard_map/pallas_call | solution.py:547
  45.1 0.0 copy-start
  45.1 2.6 %shard_map.77 = (bf16[4,2,2,128,128]{4,3,2,1,0:T(8,128)(2,1)S(1)}, bf16[512,1024]{1,0:T(8,128)(2,1)S(1)}) custom-call(s32[8,128]{1,0:T(8,128)S(1)} %get-tuple-element.28.refs_4_.away_ref, bf16[8,5,128,128]{3,2,1,0:T(8,128)(2,1)S(1)} %get-tuple-element.40.moving_ref, f32[8,128,128]{2,1,0:T(8,128)S(1)} %get-tuple-element.41.inner_ref, ...), custom_call_target="tpu_custom_call" | custom-call | flops 838860800 | bytes 2097152 | tf_op jit(solution)/shard_map/pallas_call | solution.py:559
  47.7 13.2 %all_to_all.10 = bf16[8,2,128,128]{3,2,1,0:T(8,128)(2,1)S(1)} all-to-all(bf16[8,2,128,128]{3,2,1,0:T(8,128)(2,1)S(1)} %bitcast.6), channel_id=1, replica_groups={{0,2,4,6,8,10,12,14},{1,3,5,7,9,11,13,15},{16,18,20,22,24,26,28,30},{17..., dimensions={0} | all-to-all | bytes 1048576 | tf_op jit(solution)/shard_map/all_to_all | solution.py:576
  60.9 0.4 shard_map.79
  61.4 0.1 collective-permute-start.9
  61.4 0.4 shard_map.78
  61.9 1.1 %collective-permute-done.9 = bf16[256,512]{1,0:T(8,128)(2,1)S(1)} collective-permute-done((bf16[256,512]{1,0:T(8,128)(2,1)S(1)}, bf16[256,512]{1,0:T(8,128)(2,1)S(1)}, u32[]{:S(2)}, u32[]{:S(2)}) %collective-permute-start.9) | collective-permute-done | bytes 262176 | tf_op jit(solution)/shard_map/ppermute | solution.py:589
  63.0 0.8 %add_convert_fusion = bf16[256,512]{1,0:T(8,128)(2,1)} fusion(f32[256,512]{1,0:T(8,128)S(1)} %shard_map.78, bf16[256,512]{1,0:T(8,128)(2,1)S(1)} %collective-permute-done.9), kind=kLoop, calls=%fused_computation | loop fusion | flops 393216 | bytes 1048576 | tf_op jit(solution)/shard_map/convert_element_type | solution.py:590
  (11 shorter events, 0.0 us)
Async XLA Ops:
  2.9 17.7 %all-to-all-start = ((bf16[4,784,128]{2,1,0:T(8,128)(2,1)}), bf16[4,784,128]{2,1,0:T(8,128)(2,1)S(1)}, u32[]{:S(2)}, u32[]{:S(2)}) async-start(bf16[4,784,128]{2,1,0:T(8,128)(2,1)} %get-tuple-element.27), calls=%async_computation | async-start | bytes 1605632 | tf_op jit(solution)/shard_map/all_to_all | solution.py:468
  8.2 36.8 %collective-permute-start.8 = (bf16[512,1024]{1,0:T(8,128)(2,1)}, bf16[512,1024]{1,0:T(8,128)(2,1)S(1)}, u32[]{:S(2)}, u32[]{:S(2)}) collective-permute-start(bf16[512,1024]{1,0:T(8,128)(2,1)} %get-tuple-element.46), channel_id=1, source_target_pairs={{0,2},{1,3},{2,0},{3,1},{4,6},{5,7},{6,4},{7,5},{8,10},{9,11},{10,... | collective-permute-start | bytes 3145736 | tf_op jit(solution)/shard_map/ppermute | solution.py:519
  9.7 18.9 %collective-permute-start = (bf16[256,128]{1,0:T(8,128)(2,1)}, bf16[256,128]{1,0:T(8,128)(2,1)S(1)}, u32[]{:S(2)}, u32[]{:S(2)}) collective-permute-start(bf16[256,128]{1,0:T(8,128)(2,1)} %get-tuple-element.32), channel_id=1, source_target_pairs={{0,16},{4,20},{8,24},{12,28},{1,17},{5,21},{9,25},{13,29},{2,18},{... | collective-permute-start | bytes 196616 | tf_op jit(solution)/shard_map/ppermute | solution.py:481
  14.2 17.8 %collective-permute-start.1 = (bf16[256,128]{1,0:T(8,128)(2,1)}, bf16[256,128]{1,0:T(8,128)(2,1)S(1)}, u32[]{:S(2)}, u32[]{:S(2)}) collective-permute-start(bf16[256,128]{1,0:T(8,128)(2,1)} %get-tuple-element.33), channel_id=1, source_target_pairs={{0,20},{4,16},{8,28},{12,24},{1,21},{5,17},{9,29},{13,25},{2,22},{... | collective-permute-start | bytes 196616 | tf_op jit(solution)/shard_map/ppermute | solution.py:481
  17.0 15.0 %collective-permute-start.2 = (bf16[256,128]{1,0:T(8,128)(2,1)}, bf16[256,128]{1,0:T(8,128)(2,1)S(1)}, u32[]{:S(2)}, u32[]{:S(2)}) collective-permute-start(bf16[256,128]{1,0:T(8,128)(2,1)} %get-tuple-element.34), channel_id=1, source_target_pairs={{0,24},{4,28},{8,16},{12,20},{1,25},{5,29},{9,17},{13,21},{2,26},{... | collective-permute-start | bytes 196616 | tf_op jit(solution)/shard_map/ppermute | solution.py:481
  18.3 13.7 %copy-start.1 = (bf16[256,512]{1,0:T(8,128)(2,1)S(1)}, bf16[256,512]{1,0:T(8,128)(2,1)}, u32[]{:S(2)}) copy-start(bf16[256,512]{1,0:T(8,128)(2,1)} %values_ref.3) | copy-start | bytes 786436
  18.3 13.7 %collective-permute-start.3 = (bf16[256,128]{1,0:T(8,128)(2,1)}, bf16[256,128]{1,0:T(8,128)(2,1)S(1)}, u32[]{:S(2)}, u32[]{:S(2)}) collective-permute-start(bf16[256,128]{1,0:T(8,128)(2,1)} %get-tuple-element.35), channel_id=1, source_target_pairs={{0,28},{4,24},{8,20},{12,16},{1,29},{5,25},{9,21},{13,17},{2,30},{... | collective-permute-start | bytes 196616 | tf_op jit(solution)/shard_map/ppermute | solution.py:481
  28.6 16.4 %collective-permute-start.7 = (bf16[8,128,128]{2,1,0:T(8,128)(2,1)S(1)}, bf16[8,128,128]{2,1,0:T(8,128)(2,1)S(1)}, u32[]{:S(2)}, u32[]{:S(2)}) collective-permute-start(bf16[8,128,128]{2,1,0:T(8,128)(2,1)S(1)} %get-tuple-element.45), channel_id=1, source_target_pairs={{0,16},{4,20},{8,24},{12,28},{1,17},{5,21},{9,25},{13,29},{2,18},{... | collective-permute-start | bytes 786440 | tf_op jit(solution)/shard_map/ppermute | solution.py:472
  32.1 5.0 %collective-permute-start.4 = (bf16[256,128]{1,0:T(8,128)(2,1)S(1)}, bf16[256,128]{1,0:T(8,128)(2,1)S(1)}, u32[]{:S(2)}, u32[]{:S(2)}) collective-permute-start(bf16[256,128]{1,0:T(8,128)(2,1)S(1)} %get-tuple-element.37), channel_id=1, source_target_pairs={{0,4},{4,0},{8,12},{12,8},{16,20},{20,16},{24,28},{28,24},{1,5},{5... | collective-permute-start | bytes 196616 | tf_op jit(solution)/shard_map/ppermute | solution.py:476
  34.6 4.8 %collective-permute-start.5 = (bf16[256,128]{1,0:T(8,128)(2,1)S(1)}, bf16[256,128]{1,0:T(8,128)(2,1)S(1)}, u32[]{:S(2)}, u32[]{:S(2)}) collective-permute-start(bf16[256,128]{1,0:T(8,128)(2,1)S(1)} %get-tuple-element.38), channel_id=1, source_target_pairs={{0,8},{4,12},{8,0},{12,4},{16,24},{20,28},{24,16},{28,20},{1,9},{5... | collective-permute-start | bytes 196616 | tf_op jit(solution)/shard_map/ppermute | solution.py:476
  37.1 5.2 %collective-permute-start.6 = (bf16[256,128]{1,0:T(8,128)(2,1)S(1)}, bf16[256,128]{1,0:T(8,128)(2,1)S(1)}, u32[]{:S(2)}, u32[]{:S(2)}) collective-permute-start(bf16[256,128]{1,0:T(8,128)(2,1)S(1)} %get-tuple-element.39), channel_id=1, source_target_pairs={{0,12},{4,8},{8,4},{12,0},{16,28},{20,24},{24,20},{28,16},{1,13},{... | collective-permute-start | bytes 196616 | tf_op jit(solution)/shard_map/ppermute | solution.py:476
  45.1 15.9 %copy-start = (bf16[512,2048]{1,0:T(8,128)(2,1)S(1)}, bf16[512,2048]{1,0:T(8,128)(2,1)}, u32[]{:S(2)}) copy-start(bf16[512,2048]{1,0:T(8,128)(2,1)} %own_ref.3) | copy-start | bytes 6291460
  61.4 1.6 %collective-permute-start.9 = (bf16[256,512]{1,0:T(8,128)(2,1)S(1)}, bf16[256,512]{1,0:T(8,128)(2,1)S(1)}, u32[]{:S(2)}, u32[]{:S(2)}) collective-permute-start(bf16[256,512]{1,0:T(8,128)(2,1)S(1)} %shard_map.79), channel_id=1, source_target_pairs={{0,1},{1,0},{2,3},{3,2},{4,5},{5,4},{6,7},{7,6},{8,9},{9,8},{10,11... | collective-permute-start | bytes 786440 | tf_op jit(solution)/shard_map/ppermute | solution.py:589

commit v13 on v12

--- a/solution.py
+++ b/solution.py
@@ -64,8 +64,8 @@
     return copies
 
 
-def pack_kernel(axes, cores, d_ref, k_ref, q_ref, rates_hbm, selected_hbm, values_ref,
-                weight_ref, *refs):
+def pack_kernel(axes, cores, d_ref, k_ref, rates_hbm, selected_hbm, values_ref, weight_ref,
+                *refs):
     tokens = d_ref.shape[0]
     heads = d_ref.shape[1] // HEAD_DIM
     blocks = tokens // BLOCK
@@ -79,7 +79,7 @@
     plane = lax.axis_index(axes[1]) // cores
     first_block = device * blocks
     few_copies = fetched([rates_hbm, selected_hbm], [rates_ref, selected_ref], few_sems)
-    sources = (d_ref, k_ref, q_ref)
+    sources = (d_ref, k_ref)
     copies = []
     for head in range(heads):
         columns = pl.ds(head * HEAD_DIM, HEAD_DIM)
@@ -151,16 +151,36 @@
         copy.wait()
 
 
-def cut_kernel(axes, values_ref, *refs):
+def cut_kernel(axes, queries_ref, values_ref, *refs):
     sems = refs[-1]
-    heads = sems.shape[0]
+    heads = sems.shape[1]
+    outs = refs[-1 - 2 * heads:-1]
     place = lax.rem(lax.axis_index(axes[0]), heads)
     cuts = [
         pl.multiple_of(lax.bitwise_xor(place, turn) * HEAD_DIM, HEAD_DIM) for turn in range(heads)
     ]
-    copies = fetched(
-        [values_ref.at[:, pl.ds(cut, HEAD_DIM)] for cut in cuts], refs[-1 - heads:-1], sems
-    )
+    copies = []
+    for kind, source in enumerate((queries_ref, values_ref)):
+        copies += fetched(
+            [source.at[:, pl.ds(cut, HEAD_DIM)] for cut in cuts],
+            outs[kind * heads:(kind + 1) * heads],
+            sems.at[kind],
+        )
+    for copy in copies:
+        copy.wait()
+
+
+def order_kernel(axes, after, *refs):
+    values_ref, sems = refs[-2:]
+    kinds, heads = values_ref.shape[:2]
+    place = lax.rem(lax.axis_index(axes[0]), heads)
+    copies = []
+    for kind in range(kinds):
+        copies += fetched(
+            refs[kind * heads:(kind + 1) * heads],
+            [values_ref.at[kind, lax.bitwise_xor(place, turn)] for turn in range(heads)],
+            sems.at[kind],
+        )
     for copy in copies:
         copy.wait()
 
@@ -232,7 +252,7 @@
     def terms(unit):
         direction = rows_of(part_ref, blocks, unit, 0)
         key = rows_of(part_ref, blocks, unit, 1)
-        extra = part_ref[unit // blocks, 3 * blocks * BLOCK:].astype(F32)
+        extra = part_ref[unit // blocks, 2 * blocks * BLOCK:].astype(F32)
         first = TERMS * (unit % blocks)
         rate = extra[first:first + 1] + extra[first + 1:first + 2] + extra[first + 2:first + 3]
         listed = TERMS * blocks + unit % blocks
@@ -270,53 +290,61 @@
         maps[unit] = split(identity - (behind[:BLOCK] + behind[2 * BLOCK:]))
         end_ref[unit] = ends[unit].astype(BF16)
 
-    interleaved([terms(unit) for unit in range(units)], 1)
-    pair_keys, pair_maps = [], []
-    for pair in range(units // 2):
+    onward = []
+
+    def pair_terms(pair):
         even, odd = 2 * pair, 2 * pair + 1
+        running = [terms(even), terms(odd)]
+        while running:
+            for step in list(running):
+                if next(step, running) is running:
+                    running.remove(step)
+            yield
         even_ref[pair, 0] = maps[even][0]
         even_ref[pair, 1] = maps[even][1]
         left = jnp.concatenate([ends[even].astype(BF16), *maps[even]], 0)
         both = nn(left, maps[odd][0])
-        tail_ref[even] = both[:BLOCK].astype(BF16)
-        tail_ref[odd] = ends[odd].astype(BF16)
-        pair_keys.append(jnp.concatenate([both[:BLOCK], ends[odd]], 0))
+        tail_even, tail_odd = both[:BLOCK].astype(BF16), ends[odd].astype(BF16)
+        tail_ref[even] = tail_even
+        tail_ref[odd] = tail_odd
         low = both[2 * BLOCK:] + nn(maps[even][0], maps[odd][1])
-        pair_maps.append(split(both[BLOCK:2 * BLOCK] + low))
-        pair_ref[pair, 0] = pair_maps[pair][0]
-        pair_ref[pair, 1] = pair_maps[pair][1]
-    onward = None
-    for pair in reversed(range(units // 2)):
-        far = pair_keys[pair]
-        if onward is None:
-            onward = pair_maps[pair]
+        pair_map = split(both[BLOCK:2 * BLOCK] + low)
+        pair_ref[pair, 0] = pair_map[0]
+        pair_ref[pair, 1] = pair_map[1]
+        yield
+        if onward:
+            far = nn(jnp.concatenate([tail_even, tail_odd], 0), onward[-1][0]).astype(BF16)
+            far_ref[even] = far[:BLOCK]
+            far_ref[odd] = far[BLOCK:]
+            pair_map = split(triple(nn, pair_map, onward[-1]))
         else:
-            far = nn(far.astype(BF16), onward[0])
-            onward = split(triple(nn, pair_maps[pair], onward))
-        far_ref[2 * pair] = far[:BLOCK].astype(BF16)
-        far_ref[2 * pair + 1] = far[BLOCK:].astype(BF16)
-    group_ref[0] = onward[0]
-    group_ref[1] = onward[1]
+            far_ref[even] = tail_even
+            far_ref[odd] = tail_odd
+        onward.append(pair_map)
+
+    interleaved([pair_terms(pair) for pair in reversed(range(units // 2))], 1)
+    group_ref[0] = onward[-1][0]
+    group_ref[1] = onward[-1][1]
 
 
 def queries_kernel(axes, blocks, part_ref, mixed_ref, even_ref, pair_ref, *refs):
     heads = part_ref.shape[0]
     units = heads * blocks
-    inner_ref, moving_ref, values_ref, sems = refs[-4:]
+    inner_ref, moving_ref, query_ref, sems = refs[heads:]
     place = lax.rem(lax.axis_index(axes[0]), heads)
-    copies = []
-    for kind in range(values_ref.shape[0]):
-        copies += fetched(
-            refs[kind * heads:(kind + 1) * heads],
-            [values_ref.at[kind, lax.bitwise_xor(place, turn)] for turn in range(heads)],
-            sems.at[kind],
-        )
+    copies = fetched(
+        refs[:heads],
+        [query_ref.at[lax.bitwise_xor(place, turn)] for turn in range(heads)],
+        sems,
+    )
+    for copy in copies:
+        copy.wait()
     rows, columns = square_iotas()
     current = []
     for unit in range(units):
         direction = rows_of(part_ref, blocks, unit, 0)
         key = rows_of(part_ref, blocks, unit, 1)
-        query = rows_of(part_ref, blocks, unit, 2)
+        query = rows_of(query_ref, blocks, unit, 0)
         query_proj = split(jnp.where(rows >= columns, nt(query, direction), 0.0))
         ahead = nn(jnp.concatenate(query_proj, 0), mixed_ref[unit])
         ahead = ahead[:BLOCK] + ahead[BLOCK:]
@@ -342,8 +370,6 @@
             )
             moving_ref[2 * pair, step] = current[pair][0][:BLOCK]
             moving_ref[2 * pair + 1, step] = current[pair][0][BLOCK:]
-    for copy in copies:
-        copy.wait()
 
 
 def listed_block(away_ref, unit, entry):
@@ -483,7 +509,7 @@
     def array(shape, kind=BF16):
         return jax.ShapeDtypeStruct(shape, kind)
 
-    part_shape = (heads, 3 * tokens + EXTRA, HEAD_DIM)
+    part_shape = (heads, 2 * tokens + EXTRA, HEAD_DIM)
     width = out_weight.shape[1] // planes
     piece_shape = (out_weight.shape[0], width)
     packed, *rest = call(
@@ -491,7 +517,7 @@
         [array(part_shape)]
         + [array((tokens, HEAD_DIM))] * heads
         + [array(piece_shape)] * (planes - 1),
-        [ANY] * 7,
+        [ANY] * 6,
         cubes,
         [
             pltpu.VMEM(part_shape, BF16),
@@ -499,7 +525,7 @@
             pltpu.SMEM(selected.shape, jnp.int32),
             pltpu.VMEM((heads, tokens, HEAD_DIM), BF16),
             pltpu.VMEM((max(planes - 1, 1), *piece_shape), BF16),
-            pltpu.SemaphoreType.DMA((heads, 3)),
+            pltpu.SemaphoreType.DMA((heads, 2)),
             pltpu.SemaphoreType.DMA((2,)),
             pltpu.SemaphoreType.DMA((heads,)),
             pltpu.SemaphoreType.DMA((heads,)),
@@ -508,7 +534,7 @@
         ],
         [ANY] * (heads + planes),
         56,
-    )(directions, keys, queries, rates, selected, values, out_weight)
+    )(directions, keys, rates, selected, values, out_weight)
     value_cuts, pieces = rest[:heads], rest[heads:]
     value_parts = [
         straight(value_cuts[turn], turn, by) for by in range(1, before + 1) for turn in range(heads)
@@ -538,24 +564,27 @@
     map_parts = [onward(group_map, by) for by in range(1, before)]
     cut = call(
         functools.partial(cut_kernel, axes),
-        [array((tokens, HEAD_DIM))] * heads,
-        [ANY] * (len(value_parts) + 2),
+        [array((tokens, HEAD_DIM))] * (2 * heads),
+        [ANY] * (len(value_parts) + 3),
         2000 * cubes,
-        [pltpu.SemaphoreType.DMA((heads,))],
-    )(values, *value_parts, away)
-    own_parts = [crossed(cut[turn], turn) for turn in range(heads)]
-    inner, moving, all_values = call(
+        [pltpu.SemaphoreType.DMA((2, heads))],
+    )(queries, values, *value_parts, away)
+    query_parts = [crossed(cut[turn], turn) for turn in range(heads)]
+    own_parts = [crossed(cut[heads + turn], turn) for turn in range(heads)]
+    inner, moving = call(
         functools.partial(queries_kernel, axes, blocks),
-        [
-            array((units, BLOCK, BLOCK), F32),
-            array((units, pairs + 1, *tile)),
-            array((1 + before, heads, tokens, HEAD_DIM)),
-        ],
-        [VMEM] * 4 + [ANY] * (heads + len(value_parts)),
+        [array((units, BLOCK, BLOCK), F32), array((units, pairs + 1, *tile))],
+        [VMEM] * 4 + [ANY] * heads,
+        0,
+        [pltpu.VMEM((heads, tokens, HEAD_DIM), BF16), pltpu.SemaphoreType.DMA((heads,))],
+    )(parts, mixed, even, pair_map, *query_parts)
+    all_values = call(
+        functools.partial(order_kernel, axes),
+        array((1 + before, heads, tokens, HEAD_DIM)),
+        [ANY] * (1 + heads + len(value_parts)),
         0,
         [pltpu.SemaphoreType.DMA((1 + before, heads))],
-    )(parts, mixed, even, pair_map, *own_parts, *value_parts)
-    all_values = all_values.reshape(1 + before, units, *tile)
+    )(inner, *own_parts, *value_parts).reshape(1 + before, units, *tile)
     attended, *weight_parts = call(
         functools.partial(attend_kernel, before, blocks),
         [array((heads, planes, blocks, *tile))] + [array(part.shape) for part in weight_parts],

time: 64.1 us -> 60.6 us (0.945)
  blocking collectives: 13.2 us -> 11.4 us
  waiting for transfers between devices: 6.25 us -> 4.63 us
  Pallas kernels: 17.3 us -> 16.1 us
  starting transfers between devices: 26 us -> 27.2 us
    ppermute x3 -> x6, starting transfers between devices: 5.01 us -> 8.29 us  [crossed(): return lax.ppermute(value, 'ctx', pairs) if turn else value]
    ppermute x1, starting transfers between devices: 3.3 us -> 1.29 us  [onward(): lax.ppermute(value, 'ctx', [(i, i + shift) for i in range(ctx_size - shif...]
    all_to_all x1, blocking collectives: 13.2 us -> 11.4 us  [body(): lax.all_to_all(attended.reshape(heads * planes, blocks, *tile), axes, 0,...]
    ppermute x3 -> x6, waiting for transfers between devices: 5.16 us -> 3.54 us  [crossed(): return lax.ppermute(value, 'ctx', pairs) if turn else value]
    pallas_call x1, Pallas kernels: 8.03 us -> 6.45 us  [body(): call(functools.partial(keys_kernel, blocks), [array((units, *tile)), arra...]
    pallas_call x1 -> x2, Pallas kernels: 0.11 us -> 0.93 us  [the longest x1 0.73 us: body(): call(functools.partial(order_kernel, axes), array((1 + before, heads, tok...]
  transfers between devices with their start and end apart: 11 -> 14, of which waited for: 3 -> 4; matrix products, arithmetic and copies ran while one was open for 0% -> 0% of each run, Pallas kernels for 18% -> 17%
where the time goes in v13:
time: 60.6 us; the launch traced here: 60.3 us
  starting transfers between devices  27.2 us (45%)
  Pallas kernels  16.1 us (27%)
  blocking collectives  11.4 us (19%)
  waiting for transfers between devices  4.63 us (8%)
  other arithmetic  0.77 us (1%)
    all_to_all x1, blocking collectives, body(): lax.all_to_all(attended.reshape(heads * planes, blocks, *tile), axes, 0,...  11.4 us
    ppermute x4, starting transfers between devices, straight(): return lax.ppermute(value, 'ctx', pairs)  10.7 us
    ppermute x6, starting transfers between devices, crossed(): return lax.ppermute(value, 'ctx', pairs) if turn else value  8.29 us
    pallas_call x1, Pallas kernels, body(): call(functools.partial(keys_kernel, blocks), [array((units, *tile)), arra...  6.45 us
    all_to_all x1, starting transfers between devices, exchange(): lax.all_to_all(value, 'ctx', 0, 0, axis_index_groups=members, tiled=True)  5.26 us
    ppermute x6, waiting for transfers between devices, crossed(): return lax.ppermute(value, 'ctx', pairs) if turn else value  3.54 us
    pallas_call x1, Pallas kernels, body(): call(functools.partial(pack_kernel, axes, cores), [array(part_shape)] + [...  2.85 us
    pallas_call x1, Pallas kernels, body(): call(functools.partial(attend_kernel, before, blocks), [array((heads, pla...  2.6 us
  transfers between devices with their start and end apart: 14, of which 4 were waited for; matrix products, arithmetic and copies ran while one was open for 0% of the time, Pallas kernels for 17%

profile of v13, /device:TPU:0, one launch (start us, length us, event | category | flops | bytes accessed | tf_op | source)
XLA Modules:
  0.0 60.3 jit_solution(17097027638628278773)
XLA Ops:
  0.0 2.8 %shard_map.73 = (bf16[4,528,128]{2,1,0:T(8,128)(2,1)}, bf16[256,128]{1,0:T(8,128)(2,1)}, bf16[256,128]{1,0:T(8,128)(2,1)}, bf16[256,128]{1,0:T(8,128)(2,1)}, bf1...) custom-call(bf16[256,512]{1,0:T(8,128)(2,1)} %d_ref.1, bf16[256,512]{1,0:T(8,128)(2,1)} %k_ref.1, f32[4,256]{1,0:T(4,128)} %rates_hbm.1, ...), custom_call_target="tpu_custom_call" | custom-call | flops 4194304 | bytes 2097152 | tf_op jit(solution)/shard_map/pallas_call | solution.py:515
  2.9 5.3 %all-to-all-start = ((bf16[4,528,128]{2,1,0:T(8,128)(2,1)}), bf16[4,528,128]{2,1,0:T(8,128)(2,1)S(1)}, u32[]{:S(2)}, u32[]{:S(2)}) async-start(bf16[4,528,128]{2,1,0:T(8,128)(2,1)} %get-tuple-element.30), calls=%async_computation | async-start | bytes 1081344 | tf_op jit(solution)/shard_map/all_to_all | solution.py:494
  8.1 4.5 %collective-permute-start = (bf16[256,128]{1,0:T(8,128)(2,1)}, bf16[256,128]{1,0:T(8,128)(2,1)S(1)}, u32[]{:S(2)}, u32[]{:S(2)}) collective-permute-start(bf16[256,128]{1,0:T(8,128)(2,1)} %get-tuple-element.35), channel_id=1, source_target_pairs={{0,16},{4,20},{8,24},{12,28},{1,17},{5,21},{9,25},{13,29},{2,18},{... | collective-permute-start | bytes 196616 | tf_op jit(solution)/shard_map/ppermute | solution.py:507
  12.6 2.8 %collective-permute-start.1 = (bf16[256,128]{1,0:T(8,128)(2,1)}, bf16[256,128]{1,0:T(8,128)(2,1)S(1)}, u32[]{:S(2)}, u32[]{:S(2)}) collective-permute-start(bf16[256,128]{1,0:T(8,128)(2,1)} %get-tuple-element.36), channel_id=1, source_target_pairs={{0,20},{4,16},{8,28},{12,24},{1,21},{5,17},{9,29},{13,25},{2,22},{... | collective-permute-start | bytes 196616 | tf_op jit(solution)/shard_map/ppermute | solution.py:507
  15.4 1.3 %collective-permute-start.2 = (bf16[256,128]{1,0:T(8,128)(2,1)}, bf16[256,128]{1,0:T(8,128)(2,1)S(1)}, u32[]{:S(2)}, u32[]{:S(2)}) collective-permute-start(bf16[256,128]{1,0:T(8,128)(2,1)} %get-tuple-element.37), channel_id=1, source_target_pairs={{0,24},{4,28},{8,16},{12,20},{1,25},{5,29},{9,17},{13,21},{2,26},{... | collective-permute-start | bytes 196616 | tf_op jit(solution)/shard_map/ppermute | solution.py:507
  16.7 2.2 %collective-permute-start.3 = (bf16[256,128]{1,0:T(8,128)(2,1)}, bf16[256,128]{1,0:T(8,128)(2,1)S(1)}, u32[]{:S(2)}, u32[]{:S(2)}) collective-permute-start(bf16[256,128]{1,0:T(8,128)(2,1)} %get-tuple-element.38), channel_id=1, source_target_pairs={{0,28},{4,24},{8,20},{12,16},{1,29},{5,25},{9,21},{13,17},{2,30},{... | collective-permute-start | bytes 196616 | tf_op jit(solution)/shard_map/ppermute | solution.py:507
  18.9 1.6 %collective-permute-start.11 = (bf16[512,1024]{1,0:T(8,128)(2,1)}, bf16[512,1024]{1,0:T(8,128)(2,1)S(1)}, u32[]{:S(2)}, u32[]{:S(2)}) collective-permute-start(bf16[512,1024]{1,0:T(8,128)(2,1)} %get-tuple-element.52), channel_id=1, source_target_pairs={{0,2},{1,3},{2,0},{3,1},{4,6},{5,7},{6,4},{7,5},{8,10},{9,11},{10,... | collective-permute-start | bytes 3145736 | tf_op jit(solution)/shard_map/ppermute | solution.py:545
  20.5 6.4 %shard_map.74 = (bf16[8,128,128]{2,1,0:T(8,128)(2,1)S(1)}, bf16[8,128,128]{2,1,0:T(8,128)(2,1)S(1)}, bf16[8,128,128]{2,1,0:T(8,128)(2,1)S(1)}, bf16[4,2,128,128]...) custom-call(bf16[4,528,128]{2,1,0:T(8,128)(2,1)S(1)} %all-to-all-don, ...), custom_call_target="tpu_custom_call" | custom-call | flops 1677721600 | bytes 2097152 | tf_op jit(solution)/shard_map/pallas_call | solution.py:548
  26.9 1.3 %collective-permute-start.10 = (bf16[8,128,128]{2,1,0:T(8,128)(2,1)S(1)}, bf16[8,128,128]{2,1,0:T(8,128)(2,1)S(1)}, u32[]{:S(2)}, u32[]{:S(2)}) collective-permute-start(bf16[8,128,128]{2,1,0:T(8,128)(2,1)S(1)} %get-tuple-element.51), channel_id=1, source_target_pairs={{0,16},{4,20},{8,24},{12,28},{1,17},{5,21},{9,25},{13,29},{2,18},{... | collective-permute-start | bytes 786440 | tf_op jit(solution)/shard_map/ppermute | solution.py:498
  28.5 0.6 %collective-permute-start.4 = (bf16[256,128]{1,0:T(8,128)(2,1)S(1)}, bf16[256,128]{1,0:T(8,128)(2,1)S(1)}, u32[]{:S(2)}, u32[]{:S(2)}) collective-permute-start(bf16[256,128]{1,0:T(8,128)(2,1)S(1)} %get-tuple-element.40), channel_id=1, source_target_pairs={{0,4},{4,0},{8,12},{12,8},{16,20},{20,16},{24,28},{28,24},{1,5},{5... | collective-permute-start | bytes 196616 | tf_op jit(solution)/shard_map/ppermute | solution.py:502
  29.1 2.2 %collective-permute-start.5 = (bf16[256,128]{1,0:T(8,128)(2,1)S(1)}, bf16[256,128]{1,0:T(8,128)(2,1)S(1)}, u32[]{:S(2)}, u32[]{:S(2)}) collective-permute-start(bf16[256,128]{1,0:T(8,128)(2,1)S(1)} %get-tuple-element.41), channel_id=1, source_target_pairs={{0,8},{4,12},{8,0},{12,4},{16,24},{20,28},{24,16},{28,20},{1,9},{5... | collective-permute-start | bytes 196616 | tf_op jit(solution)/shard_map/ppermute | solution.py:502
  31.3 0.8 %collective-permute-start.6 = (bf16[256,128]{1,0:T(8,128)(2,1)S(1)}, bf16[256,128]{1,0:T(8,128)(2,1)S(1)}, u32[]{:S(2)}, u32[]{:S(2)}) collective-permute-start(bf16[256,128]{1,0:T(8,128)(2,1)S(1)} %get-tuple-element.42), channel_id=1, source_target_pairs={{0,12},{4,8},{8,4},{12,0},{16,28},{20,24},{24,20},{28,16},{1,13},{... | collective-permute-start | bytes 196616 | tf_op jit(solution)/shard_map/ppermute | solution.py:502
  32.0 1.7 %collective-permute-done.4.refs_1_ = bf16[256,128]{1,0:T(8,128)(2,1)S(1)} collective-permute-done((bf16[256,128]{1,0:T(8,128)(2,1)S(1)}, bf16[256,128]{1,0:T(8,128)(2,1)S(1)}, u32[]{:S(2)}, u32[]{:S(2)}) %collective-permute-start.4) | collective-permute-done | bytes 65568 | tf_op jit(solution)/shard_map/ppermute | solution.py:502
  33.7 1.3 %collective-permute-done.5.refs_2_ = bf16[256,128]{1,0:T(8,128)(2,1)S(1)} collective-permute-done((bf16[256,128]{1,0:T(8,128)(2,1)S(1)}, bf16[256,128]{1,0:T(8,128)(2,1)S(1)}, u32[]{:S(2)}, u32[]{:S(2)}) %collective-permute-start.5) | collective-permute-done | bytes 65568 | tf_op jit(solution)/shard_map/ppermute | solution.py:502
  35.1 2.5 %collective-permute-start.8 = (bf16[256,128]{1,0:T(8,128)(2,1)S(1)}, bf16[256,128]{1,0:T(8,128)(2,1)S(1)}, u32[]{:S(2)}, u32[]{:S(2)}) collective-permute-start(bf16[256,128]{1,0:T(8,128)(2,1)S(1)} %get-tuple-element.49), channel_id=1, source_target_pairs={{0,8},{4,12},{8,0},{12,4},{16,24},{20,28},{24,16},{28,20},{1,9},{5... | collective-permute-start | bytes 196616 | tf_op jit(solution)/shard_map/ppermute | solution.py:502
  37.5 2.2 %collective-permute-start.9 = (bf16[256,128]{1,0:T(8,128)(2,1)S(1)}, bf16[256,128]{1,0:T(8,128)(2,1)S(1)}, u32[]{:S(2)}, u32[]{:S(2)}) collective-permute-start(bf16[256,128]{1,0:T(8,128)(2,1)S(1)} %get-tuple-element.50), channel_id=1, source_target_pairs={{0,12},{4,8},{8,4},{12,0},{16,28},{20,24},{24,20},{28,16},{1,13},{... | collective-permute-start | bytes 196616 | tf_op jit(solution)/shard_map/ppermute | solution.py:502
  39.8 2.4 %shard_map.76 = (f32[8,128,128]{2,1,0:T(8,128)S(1)}, bf16[8,5,128,128]{3,2,1,0:T(8,128)(2,1)S(1)}) custom-call(bf16[4,528,128]{2,1,0:T(8,128)(2,1)S(1)} %all-to-all-done.part_ref, bf16[8,128,256]{2,1,0:T(8,128)(2,1)S(1)} %get-tuple-element.32.mixed_ref, bf16[4,2,128,128]{3,2,1,0:T(8,128)(2,1)S(1)} %get-tuple-element.33.even_ref, ...), custom_call_target="tpu_custom_call" | custom-call | bytes 2097152 | tf_op jit(solution)/shard_map/pallas_call | solution.py:574
  42.2 0.5 collective-permute-done.9.refs_3_
  42.7 0.7 %shard_map.77 = bf16[2,4,256,128]{3,2,1,0:T(8,128)(2,1)S(1)} custom-call(f32[8,128,128]{2,1,0:T(8,128)S(1)} %get-tuple-element.44.after.inner_ref, bf16[256,128]{1,0:T(8,128)(2,1)S(1)} %get-tuple-element.47.refs_0_, bf16[256,128]{1,0:T(8,128)(2,1)S(1)} %collective-permute-done.7.refs_1_, bf16[256,128]{1,0:T(8,128)(2,1)S(1)} %collective-permute-done.8.refs_2_, ...), custom_call_target="tpu_custom_call" | custom-call | bytes 2097152 | tf_op jit(solution)/shard_map/pallas_call | solution.py:581
  43.5 2.6 %shard_map.78 = (bf16[4,2,2,128,128]{4,3,2,1,0:T(8,128)(2,1)S(1)}, bf16[512,1024]{1,0:T(8,128)(2,1)S(1)}) custom-call(s32[8,128]{1,0:T(8,128)S(1)} %get-tuple-element.31.refs_4_.away_ref, bf16[8,5,128,128]{3,2,1,0:T(8,128)(2,1)S(1)} %get-tuple-element.43.moving_ref, f32[8,128,128]{2,1,0:T(8,128)S(1)} %get-tuple-element.44.after.inner_ref, ...), custom_call_target="tpu_custom_call" | custom-call | flops 838860800 | bytes 2097152 | tf_op jit(solution)/shard_map/pallas_call | solution.py:588
  46.1 11.4 %all_to_all.10 = bf16[8,2,128,128]{3,2,1,0:T(8,128)(2,1)S(1)} all-to-all(bf16[8,2,128,128]{3,2,1,0:T(8,128)(2,1)S(1)} %bitcast.6), channel_id=1, replica_groups={{0,2,4,6,8,10,12,14},{1,3,5,7,9,11,13,15},{16,18,20,22,24,26,28,30},{17..., dimensions={0} | all-to-all | bytes 1048576 | tf_op jit(solution)/shard_map/all_to_all | solution.py:605
  58.0 0.4 shard_map.79
  58.4 1.1 %collective-permute-done.12 = bf16[256,512]{1,0:T(8,128)(2,1)S(1)} collective-permute-done((bf16[256,512]{1,0:T(8,128)(2,1)S(1)}, bf16[256,512]{1,0:T(8,128)(2,1)S(1)}, u32[]{:S(2)}, u32[]{:S(2)}) %collective-permute-start.12) | collective-permute-done | bytes 262176 | tf_op jit(solution)/shard_map/ppermute | solution.py:618
  59.5 0.8 %add_convert_fusion = bf16[256,512]{1,0:T(8,128)(2,1)} fusion(f32[256,512]{1,0:T(8,128)S(1)} %shard_map.79, bf16[256,512]{1,0:T(8,128)(2,1)S(1)} %collective-permute-done.12), kind=kLoop, calls=%fused_computation | loop fusion | flops 393216 | bytes 1048576 | tf_op jit(solution)/shard_map/convert_element_type | solution.py:619
  (20 shorter events, 0.8 us)
Async XLA Ops:
  2.9 17.6 %all-to-all-start = ((bf16[4,528,128]{2,1,0:T(8,128)(2,1)}), bf16[4,528,128]{2,1,0:T(8,128)(2,1)S(1)}, u32[]{:S(2)}, u32[]{:S(2)}) async-start(bf16[4,528,128]{2,1,0:T(8,128)(2,1)} %get-tuple-element.30), calls=%async_computation | async-start | bytes 1081344 | tf_op jit(solution)/shard_map/all_to_all | solution.py:494
  8.1 18.8 %collective-permute-start = (bf16[256,128]{1,0:T(8,128)(2,1)}, bf16[256,128]{1,0:T(8,128)(2,1)S(1)}, u32[]{:S(2)}, u32[]{:S(2)}) collective-permute-start(bf16[256,128]{1,0:T(8,128)(2,1)} %get-tuple-element.35), channel_id=1, source_target_pairs={{0,16},{4,20},{8,24},{12,28},{1,17},{5,21},{9,25},{13,29},{2,18},{... | collective-permute-start | bytes 196616 | tf_op jit(solution)/shard_map/ppermute | solution.py:507
  12.6 15.6 %collective-permute-start.1 = (bf16[256,128]{1,0:T(8,128)(2,1)}, bf16[256,128]{1,0:T(8,128)(2,1)S(1)}, u32[]{:S(2)}, u32[]{:S(2)}) collective-permute-start(bf16[256,128]{1,0:T(8,128)(2,1)} %get-tuple-element.36), channel_id=1, source_target_pairs={{0,20},{4,16},{8,28},{12,24},{1,21},{5,17},{9,29},{13,25},{2,22},{... | collective-permute-start | bytes 196616 | tf_op jit(solution)/shard_map/ppermute | solution.py:507
  15.4 12.9 %collective-permute-start.2 = (bf16[256,128]{1,0:T(8,128)(2,1)}, bf16[256,128]{1,0:T(8,128)(2,1)S(1)}, u32[]{:S(2)}, u32[]{:S(2)}) collective-permute-start(bf16[256,128]{1,0:T(8,128)(2,1)} %get-tuple-element.37), channel_id=1, source_target_pairs={{0,24},{4,28},{8,16},{12,20},{1,25},{5,29},{9,17},{13,21},{2,26},{... | collective-permute-start | bytes 196616 | tf_op jit(solution)/shard_map/ppermute | solution.py:507
  16.7 11.6 %collective-permute-start.3 = (bf16[256,128]{1,0:T(8,128)(2,1)}, bf16[256,128]{1,0:T(8,128)(2,1)S(1)}, u32[]{:S(2)}, u32[]{:S(2)}) collective-permute-start(bf16[256,128]{1,0:T(8,128)(2,1)} %get-tuple-element.38), channel_id=1, source_target_pairs={{0,28},{4,24},{8,20},{12,16},{1,29},{5,25},{9,21},{13,17},{2,30},{... | collective-permute-start | bytes 196616 | tf_op jit(solution)/shard_map/ppermute | solution.py:507
  18.9 9.4 %copy-start.1 = (bf16[256,512]{1,0:T(8,128)(2,1)S(1)}, bf16[256,512]{1,0:T(8,128)(2,1)}, u32[]{:S(2)}) copy-start(bf16[256,512]{1,0:T(8,128)(2,1)} %values_ref.3) | copy-start | bytes 786436
  18.9 9.4 %copy-start.2 = (bf16[256,512]{1,0:T(8,128)(2,1)S(1)}, bf16[256,512]{1,0:T(8,128)(2,1)}, u32[]{:S(2)}) copy-start(bf16[256,512]{1,0:T(8,128)(2,1)} %queries_ref.1) | copy-start | bytes 786436
  18.9 24.5 %collective-permute-start.11 = (bf16[512,1024]{1,0:T(8,128)(2,1)}, bf16[512,1024]{1,0:T(8,128)(2,1)S(1)}, u32[]{:S(2)}, u32[]{:S(2)}) collective-permute-start(bf16[512,1024]{1,0:T(8,128)(2,1)} %get-tuple-element.52), channel_id=1, source_target_pairs={{0,2},{1,3},{2,0},{3,1},{4,6},{5,7},{6,4},{7,5},{8,10},{9,11},{10,... | collective-permute-start | bytes 3145736 | tf_op jit(solution)/shard_map/ppermute | solution.py:545
  26.9 16.5 %collective-permute-start.10 = (bf16[8,128,128]{2,1,0:T(8,128)(2,1)S(1)}, bf16[8,128,128]{2,1,0:T(8,128)(2,1)S(1)}, u32[]{:S(2)}, u32[]{:S(2)}) collective-permute-start(bf16[8,128,128]{2,1,0:T(8,128)(2,1)S(1)} %get-tuple-element.51), channel_id=1, source_target_pairs={{0,16},{4,20},{8,24},{12,28},{1,17},{5,21},{9,25},{13,29},{2,18},{... | collective-permute-start | bytes 786440 | tf_op jit(solution)/shard_map/ppermute | solution.py:498
  28.5 5.3 %collective-permute-start.4 = (bf16[256,128]{1,0:T(8,128)(2,1)S(1)}, bf16[256,128]{1,0:T(8,128)(2,1)S(1)}, u32[]{:S(2)}, u32[]{:S(2)}) collective-permute-start(bf16[256,128]{1,0:T(8,128)(2,1)S(1)} %get-tuple-element.40), channel_id=1, source_target_pairs={{0,4},{4,0},{8,12},{12,8},{16,20},{20,16},{24,28},{28,24},{1,5},{5... | collective-permute-start | bytes 196616 | tf_op jit(solution)/shard_map/ppermute | solution.py:502
  29.1 5.9 %collective-permute-start.5 = (bf16[256,128]{1,0:T(8,128)(2,1)S(1)}, bf16[256,128]{1,0:T(8,128)(2,1)S(1)}, u32[]{:S(2)}, u32[]{:S(2)}) collective-permute-start(bf16[256,128]{1,0:T(8,128)(2,1)S(1)} %get-tuple-element.41), channel_id=1, source_target_pairs={{0,8},{4,12},{8,0},{12,4},{16,24},{20,28},{24,16},{28,20},{1,9},{5... | collective-permute-start | bytes 196616 | tf_op jit(solution)/shard_map/ppermute | solution.py:502
  31.3 6.3 %collective-permute-start.6 = (bf16[256,128]{1,0:T(8,128)(2,1)S(1)}, bf16[256,128]{1,0:T(8,128)(2,1)S(1)}, u32[]{:S(2)}, u32[]{:S(2)}) collective-permute-start(bf16[256,128]{1,0:T(8,128)(2,1)S(1)} %get-tuple-element.42), channel_id=1, source_target_pairs={{0,12},{4,8},{8,4},{12,0},{16,28},{20,24},{24,20},{28,16},{1,13},{... | collective-permute-start | bytes 196616 | tf_op jit(solution)/shard_map/ppermute | solution.py:502
  33.7 8.4 %collective-permute-start.7 = (bf16[256,128]{1,0:T(8,128)(2,1)S(1)}, bf16[256,128]{1,0:T(8,128)(2,1)S(1)}, u32[]{:S(2)}, u32[]{:S(2)}) collective-permute-start(bf16[256,128]{1,0:T(8,128)(2,1)S(1)} %get-tuple-element.48), channel_id=1, source_target_pairs={{0,4},{4,0},{8,12},{12,8},{16,20},{20,16},{24,28},{28,24},{1,5},{5... | collective-permute-start | bytes 196616 | tf_op jit(solution)/shard_map/ppermute | solution.py:502
  35.1 7.1 %collective-permute-start.8 = (bf16[256,128]{1,0:T(8,128)(2,1)S(1)}, bf16[256,128]{1,0:T(8,128)(2,1)S(1)}, u32[]{:S(2)}, u32[]{:S(2)}) collective-permute-start(bf16[256,128]{1,0:T(8,128)(2,1)S(1)} %get-tuple-element.49), channel_id=1, source_target_pairs={{0,8},{4,12},{8,0},{12,4},{16,24},{20,28},{24,16},{28,20},{1,9},{5... | collective-permute-start | bytes 196616 | tf_op jit(solution)/shard_map/ppermute | solution.py:502
  37.5 5.2 %collective-permute-start.9 = (bf16[256,128]{1,0:T(8,128)(2,1)S(1)}, bf16[256,128]{1,0:T(8,128)(2,1)S(1)}, u32[]{:S(2)}, u32[]{:S(2)}) collective-permute-start(bf16[256,128]{1,0:T(8,128)(2,1)S(1)} %get-tuple-element.50), channel_id=1, source_target_pairs={{0,12},{4,8},{8,4},{12,0},{16,28},{20,24},{24,20},{28,16},{1,13},{... | collective-permute-start | bytes 196616 | tf_op jit(solution)/shard_map/ppermute | solution.py:502
  43.5 14.0 %copy-start = (bf16[512,2048]{1,0:T(8,128)(2,1)S(1)}, bf16[512,2048]{1,0:T(8,128)(2,1)}, u32[]{:S(2)}) copy-start(bf16[512,2048]{1,0:T(8,128)(2,1)} %own_ref.3) | copy-start | bytes 6291460
  57.9 1.6 %collective-permute-start.12 = (bf16[256,512]{1,0:T(8,128)(2,1)S(1)}, bf16[256,512]{1,0:T(8,128)(2,1)S(1)}, u32[]{:S(2)}, u32[]{:S(2)}) collective-permute-start(bf16[256,512]{1,0:T(8,128)(2,1)S(1)} %shard_map.80), channel_id=1, source_target_pairs={{0,1},{1,0},{2,3},{3,2},{4,5},{5,4},{6,7},{7,6},{8,9},{9,8},{10,11... | collective-permute-start | bytes 786440 | tf_op jit(solution)/shard_map/ppermute | solution.py:618

commit v14 on v13

--- a/solution.py
+++ b/solution.py
@@ -170,21 +170,6 @@
         copy.wait()
 
 
-def order_kernel(axes, after, *refs):
-    values_ref, sems = refs[-2:]
-    kinds, heads = values_ref.shape[:2]
-    place = lax.rem(lax.axis_index(axes[0]), heads)
-    copies = []
-    for kind in range(kinds):
-        copies += fetched(
-            refs[kind * heads:(kind + 1) * heads],
-            [values_ref.at[kind, lax.bitwise_xor(place, turn)] for turn in range(heads)],
-            sems.at[kind],
-        )
-    for copy in copies:
-        copy.wait()
-
-
 def rows_of(ref, blocks, unit, kind):
     start = (kind * blocks + unit % blocks) * BLOCK
     return ref[unit // blocks, start:start + BLOCK]
@@ -384,13 +369,8 @@
     return jnp.clip(source + ahead * units, 0, units - 1), source < (1 - ahead) * units
 
 
-def attend_kernel(before, blocks, away_ref, moving_ref, inner_ref, end_ref, tail_ref,
-                  values_ref, *refs):
-    maps = max(before - 1, 0)
-    far_keys, group_maps = refs[:before], refs[before:before + maps]
-    count = (len(refs) - before - maps - 2) // 2
-    out_ref, sems = refs[-2 - count], refs[-1]
-    copies = fetched(refs[before + maps:before + maps + count], refs[-1 - count:-1], sems)
+def weights_kernel(before, away_ref, moving_ref, inner_ref, end_ref, tail_ref, *refs):
+    far_keys, group_maps, weights_ref = refs[:before], refs[before:-1], refs[-1]
     units = inner_ref.shape[0]
     rows, columns = square_iotas()
     scale = HEAD_DIM ** (-0.5)
@@ -402,31 +382,63 @@
             passed = nt(fronts[-1], group_map[0]) + nt(fronts[-1], group_map[1])
             fronts.append(passed.astype(BF16))
         score_list = [jnp.where(rows >= columns, inner_ref[unit] * scale, -1e30)]
-        value_list = [values_ref[0, unit]]
         for entry in range(1, TOPK):
             source, new = listed_block(away_ref, unit, entry)
             inside = jnp.maximum(source, 0)
             step = jnp.maximum(pair - inside // 2, 0)
             query = moving_ref[unit, step]
             key = jnp.where(step == 0, end_ref[inside], tail_ref[inside])
-            value = values_ref[0, inside]
             for ahead in range(1, before + 1):
                 place, here = earlier(source, ahead, units)
                 query = jnp.where(here, fronts[ahead - 1], query)
                 key = jnp.where(here, far_keys[ahead - 1][place], key)
-                value = jnp.where(here, values_ref[ahead, place], value)
             score_list.append(jnp.where(new, nt(query, key) * scale, -1e30))
-            value_list.append(value)
         yield
         scores = jnp.concatenate(score_list, 1)
         expos = jnp.exp(scores - jnp.max(scores, 1, keepdims=True))
-        weights = (expos / jnp.sum(expos, 1, keepdims=True)).astype(BF16)
-        yield
-        blended = nn(weights, jnp.concatenate(value_list, 0)).astype(BF16)
+        weights_ref[unit] = (expos / jnp.sum(expos, 1, keepdims=True)).astype(BF16)
+
+    interleaved([steps(unit) for unit in range(units)], 1)
+
+
+def blend_kernel(axes, before, blocks, away_ref, weights_ref, *refs):
+    units = weights_ref.shape[0]
+    heads = units // blocks
+    count = (len(refs) - 4 - heads * (1 + before)) // 2
+    arrived = refs[:heads * (1 + before)]
+    out_ref, (values_ref, value_sems, sems) = refs[-4 - count], refs[-3:]
+    place = lax.rem(lax.axis_index(axes[0]), heads)
+    value_copies = []
+    for kind in range(1 + before):
+        for turn in range(heads):
+            start = pl.multiple_of(lax.bitwise_xor(place, turn) * blocks * BLOCK, BLOCK)
+            value_copies += fetched(
+                [arrived[kind * heads + turn]],
+                [values_ref.at[kind, pl.ds(start, blocks * BLOCK)]],
+                value_sems.at[kind, pl.ds(turn, 1)],
+            )
+    copies = fetched(
+        refs[heads * (1 + before):heads * (1 + before) + count], refs[-3 - count:-3], sems
+    )
+    for copy in value_copies:
+        copy.wait()
+
+    def value_of(kind, block):
+        return values_ref[kind, pl.ds(pl.multiple_of(block * BLOCK, BLOCK), BLOCK)]
+
+    for unit in range(units):
+        value_list = [value_of(0, unit)]
+        for entry in range(1, TOPK):
+            source, _ = listed_block(away_ref, unit, entry)
+            kind, block = 0, jnp.maximum(source, 0)
+            for ahead in range(1, before + 1):
+                other, here = earlier(source, ahead, units)
+                kind = jnp.where(here, ahead, kind)
+                block = jnp.where(here, other, block)
+            value_list.append(value_of(kind, block))
+        blended = nn(weights_ref[unit], jnp.concatenate(value_list, 0)).astype(BF16)
         for plane in range(out_ref.shape[1]):
             out_ref[unit // blocks, plane, unit % blocks] = blended
-
-    interleaved([steps(unit) for unit in range(units)], 1)
     for copy in copies:
         copy.wait()
 
@@ -578,20 +590,23 @@
         0,
         [pltpu.VMEM((heads, tokens, HEAD_DIM), BF16), pltpu.SemaphoreType.DMA((heads,))],
     )(parts, mixed, even, pair_map, *query_parts)
-    all_values = call(
-        functools.partial(order_kernel, axes),
-        array((1 + before, heads, tokens, HEAD_DIM)),
-        [ANY] * (1 + heads + len(value_parts)),
+    weights = call(
+        functools.partial(weights_kernel, before),
+        array((units, BLOCK, TOPK * BLOCK)),
+        [SMEM] + [VMEM] * (4 + before + len(map_parts)),
         0,
-        [pltpu.SemaphoreType.DMA((1 + before, heads))],
-    )(inner, *own_parts, *value_parts).reshape(1 + before, units, *tile)
+    )(away, moving, inner, end, tail, *far_parts, *map_parts)
     attended, *weight_parts = call(
-        functools.partial(attend_kernel, before, blocks),
+        functools.partial(blend_kernel, axes, before, blocks),
         [array((heads, planes, blocks, *tile))] + [array(part.shape) for part in weight_parts],
-        [SMEM] + [VMEM] * (5 + before + len(map_parts)) + [ANY] * len(weight_parts),
-        200 * cubes,
-        [pltpu.SemaphoreType.DMA((planes,))],
-    )(away, moving, inner, end, tail, all_values, *far_parts, *map_parts, *weight_parts)
+        [SMEM, VMEM] + [ANY] * (heads * (1 + before) + len(weight_parts)),
+        0,
+        [
+            pltpu.VMEM((1 + before, units * BLOCK, HEAD_DIM), BF16),
+            pltpu.SemaphoreType.DMA((1 + before, heads)),
+            pltpu.SemaphoreType.DMA((planes,)),
+        ],
+    )(away, weights, *own_parts, *value_parts, *weight_parts)
 
     returns = [
         [

time: 60.6 us -> 59.6 us (0.983)
  blocking collectives: 11.4 us -> 10.4 us
    all_to_all x1, blocking collectives: 11.4 us -> 10.4 us  [body(): lax.all_to_all(attended.reshape(heads * planes, blocks, *tile), axes, 0,...]
  transfers between devices with their start and end apart: 14 -> 14, of which waited for: 4 -> 3; matrix products, arithmetic and copies ran while one was open for 0% -> 0% of each run, Pallas kernels for 17% -> 19%
where the time goes in v14:
time: 59.6 us; the launch traced here: 59.3 us
  starting transfers between devices  27.2 us (46%)
  Pallas kernels  16.5 us (28%)
  blocking collectives  10.4 us (17%)
  waiting for transfers between devices  4.12 us (7%)
  other arithmetic  0.77 us (1%)
    ppermute x4, starting transfers between devices, straight(): return lax.ppermute(value, 'ctx', pairs)  10.7 us
    all_to_all x1, blocking collectives, body(): lax.all_to_all(attended.reshape(heads * planes, blocks, *tile), axes, 0,...  10.4 us
    ppermute x6, starting transfers between devices, crossed(): return lax.ppermute(value, 'ctx', pairs) if turn else value  8.29 us
    pallas_call x1, Pallas kernels, body(): call(functools.partial(keys_kernel, blocks), [array((units, *tile)), arra...  6.45 us
    all_to_all x1, starting transfers between devices, exchange(): lax.all_to_all(value, 'ctx', 0, 0, axis_index_groups=members, tiled=True)  5.26 us
    ppermute x6, waiting for transfers between devices, crossed(): return lax.ppermute(value, 'ctx', pairs) if turn else value  3.02 us
    pallas_call x1, Pallas kernels, body(): call(functools.partial(pack_kernel, axes, cores), [array(part_shape)] + [...  2.85 us
    pallas_call x1, Pallas kernels, body(): call(functools.partial(queries_kernel, axes, blocks), [array((units, BLOC...  2.37 us
  transfers between devices with their start and end apart: 14, of which 3 were waited for; matrix products, arithmetic and copies ran while one was open for 0% of the time, Pallas kernels for 19%

profile of v14, /device:TPU:0, one launch (start us, length us, event | category | flops | bytes accessed | tf_op | source)
XLA Modules:
  0.0 59.3 jit_solution(10728981735815361544)
XLA Ops:
  0.0 2.8 %shard_map.73 = (bf16[4,528,128]{2,1,0:T(8,128)(2,1)}, bf16[256,128]{1,0:T(8,128)(2,1)}, bf16[256,128]{1,0:T(8,128)(2,1)}, bf16[256,128]{1,0:T(8,128)(2,1)}, bf1...) custom-call(bf16[256,512]{1,0:T(8,128)(2,1)} %d_ref.1, bf16[256,512]{1,0:T(8,128)(2,1)} %k_ref.1, f32[4,256]{1,0:T(4,128)} %rates_hbm.1, ...), custom_call_target="tpu_custom_call" | custom-call | flops 4194304 | bytes 2097152 | tf_op jit(solution)/shard_map/pallas_call | solution.py:527
  2.9 5.3 %all-to-all-start = ((bf16[4,528,128]{2,1,0:T(8,128)(2,1)}), bf16[4,528,128]{2,1,0:T(8,128)(2,1)S(1)}, u32[]{:S(2)}, u32[]{:S(2)}) async-start(bf16[4,528,128]{2,1,0:T(8,128)(2,1)} %get-tuple-element.30), calls=%async_computation | async-start | bytes 1081344 | tf_op jit(solution)/shard_map/all_to_all | solution.py:506
  8.1 4.5 %collective-permute-start = (bf16[256,128]{1,0:T(8,128)(2,1)}, bf16[256,128]{1,0:T(8,128)(2,1)S(1)}, u32[]{:S(2)}, u32[]{:S(2)}) collective-permute-start(bf16[256,128]{1,0:T(8,128)(2,1)} %get-tuple-element.35), channel_id=1, source_target_pairs={{0,16},{4,20},{8,24},{12,28},{1,17},{5,21},{9,25},{13,29},{2,18},{... | collective-permute-start | bytes 196616 | tf_op jit(solution)/shard_map/ppermute | solution.py:519
  12.6 2.8 %collective-permute-start.1 = (bf16[256,128]{1,0:T(8,128)(2,1)}, bf16[256,128]{1,0:T(8,128)(2,1)S(1)}, u32[]{:S(2)}, u32[]{:S(2)}) collective-permute-start(bf16[256,128]{1,0:T(8,128)(2,1)} %get-tuple-element.36), channel_id=1, source_target_pairs={{0,20},{4,16},{8,28},{12,24},{1,21},{5,17},{9,29},{13,25},{2,22},{... | collective-permute-start | bytes 196616 | tf_op jit(solution)/shard_map/ppermute | solution.py:519
  15.4 1.3 %collective-permute-start.2 = (bf16[256,128]{1,0:T(8,128)(2,1)}, bf16[256,128]{1,0:T(8,128)(2,1)S(1)}, u32[]{:S(2)}, u32[]{:S(2)}) collective-permute-start(bf16[256,128]{1,0:T(8,128)(2,1)} %get-tuple-element.37), channel_id=1, source_target_pairs={{0,24},{4,28},{8,16},{12,20},{1,25},{5,29},{9,17},{13,21},{2,26},{... | collective-permute-start | bytes 196616 | tf_op jit(solution)/shard_map/ppermute | solution.py:519
  16.7 2.2 %collective-permute-start.3 = (bf16[256,128]{1,0:T(8,128)(2,1)}, bf16[256,128]{1,0:T(8,128)(2,1)S(1)}, u32[]{:S(2)}, u32[]{:S(2)}) collective-permute-start(bf16[256,128]{1,0:T(8,128)(2,1)} %get-tuple-element.38), channel_id=1, source_target_pairs={{0,28},{4,24},{8,20},{12,16},{1,29},{5,25},{9,21},{13,17},{2,30},{... | collective-permute-start | bytes 196616 | tf_op jit(solution)/shard_map/ppermute | solution.py:519
  18.9 1.6 %collective-permute-start.11 = (bf16[512,1024]{1,0:T(8,128)(2,1)}, bf16[512,1024]{1,0:T(8,128)(2,1)S(1)}, u32[]{:S(2)}, u32[]{:S(2)}) collective-permute-start(bf16[512,1024]{1,0:T(8,128)(2,1)} %get-tuple-element.52), channel_id=1, source_target_pairs={{0,2},{1,3},{2,0},{3,1},{4,6},{5,7},{6,4},{7,5},{8,10},{9,11},{10,... | collective-permute-start | bytes 3145736 | tf_op jit(solution)/shard_map/ppermute | solution.py:557
  20.5 6.5 %shard_map.74 = (bf16[8,128,128]{2,1,0:T(8,128)(2,1)S(1)}, bf16[8,128,128]{2,1,0:T(8,128)(2,1)S(1)}, bf16[8,128,128]{2,1,0:T(8,128)(2,1)S(1)}, bf16[4,2,128,128]...) custom-call(bf16[4,528,128]{2,1,0:T(8,128)(2,1)S(1)} %all-to-all-don, ...), custom_call_target="tpu_custom_call" | custom-call | flops 1677721600 | bytes 2097152 | tf_op jit(solution)/shard_map/pallas_call | solution.py:560
  26.9 1.3 %collective-permute-start.7 = (bf16[8,128,128]{2,1,0:T(8,128)(2,1)S(1)}, bf16[8,128,128]{2,1,0:T(8,128)(2,1)S(1)}, u32[]{:S(2)}, u32[]{:S(2)}) collective-permute-start(bf16[8,128,128]{2,1,0:T(8,128)(2,1)S(1)} %get-tuple-element.47), channel_id=1, source_target_pairs={{0,16},{4,20},{8,24},{12,28},{1,17},{5,21},{9,25},{13,29},{2,18},{... | collective-permute-start | bytes 786440 | tf_op jit(solution)/shard_map/ppermute | solution.py:510
  28.5 0.6 %collective-permute-start.4 = (bf16[256,128]{1,0:T(8,128)(2,1)S(1)}, bf16[256,128]{1,0:T(8,128)(2,1)S(1)}, u32[]{:S(2)}, u32[]{:S(2)}) collective-permute-start(bf16[256,128]{1,0:T(8,128)(2,1)S(1)} %get-tuple-element.40), channel_id=1, source_target_pairs={{0,4},{4,0},{8,12},{12,8},{16,20},{20,16},{24,28},{28,24},{1,5},{5... | collective-permute-start | bytes 196616 | tf_op jit(solution)/shard_map/ppermute | solution.py:514
  29.1 2.2 %collective-permute-start.5 = (bf16[256,128]{1,0:T(8,128)(2,1)S(1)}, bf16[256,128]{1,0:T(8,128)(2,1)S(1)}, u32[]{:S(2)}, u32[]{:S(2)}) collective-permute-start(bf16[256,128]{1,0:T(8,128)(2,1)S(1)} %get-tuple-element.41), channel_id=1, source_target_pairs={{0,8},{4,12},{8,0},{12,4},{16,24},{20,28},{24,16},{28,20},{1,9},{5... | collective-permute-start | bytes 196616 | tf_op jit(solution)/shard_map/ppermute | solution.py:514
  31.3 0.8 %collective-permute-start.6 = (bf16[256,128]{1,0:T(8,128)(2,1)S(1)}, bf16[256,128]{1,0:T(8,128)(2,1)S(1)}, u32[]{:S(2)}, u32[]{:S(2)}) collective-permute-start(bf16[256,128]{1,0:T(8,128)(2,1)S(1)} %get-tuple-element.42), channel_id=1, source_target_pairs={{0,12},{4,8},{8,4},{12,0},{16,28},{20,24},{24,20},{28,16},{1,13},{... | collective-permute-start | bytes 196616 | tf_op jit(solution)/shard_map/ppermute | solution.py:514
  32.0 1.7 %collective-permute-done.4.refs_1_ = bf16[256,128]{1,0:T(8,128)(2,1)S(1)} collective-permute-done((bf16[256,128]{1,0:T(8,128)(2,1)S(1)}, bf16[256,128]{1,0:T(8,128)(2,1)S(1)}, u32[]{:S(2)}, u32[]{:S(2)}) %collective-permute-start.4) | collective-permute-done | bytes 65568 | tf_op jit(solution)/shard_map/ppermute | solution.py:514
  33.7 1.3 %collective-permute-done.5.refs_2_ = bf16[256,128]{1,0:T(8,128)(2,1)S(1)} collective-permute-done((bf16[256,128]{1,0:T(8,128)(2,1)S(1)}, bf16[256,128]{1,0:T(8,128)(2,1)S(1)}, u32[]{:S(2)}, u32[]{:S(2)}) %collective-permute-start.5) | collective-permute-done | bytes 65568 | tf_op jit(solution)/shard_map/ppermute | solution.py:514
  35.0 2.5 %collective-permute-start.9 = (bf16[256,128]{1,0:T(8,128)(2,1)S(1)}, bf16[256,128]{1,0:T(8,128)(2,1)S(1)}, u32[]{:S(2)}, u32[]{:S(2)}) collective-permute-start(bf16[256,128]{1,0:T(8,128)(2,1)S(1)} %get-tuple-element.50), channel_id=1, source_target_pairs={{0,8},{4,12},{8,0},{12,4},{16,24},{20,28},{24,16},{28,20},{1,9},{5... | collective-permute-start | bytes 196616 | tf_op jit(solution)/shard_map/ppermute | solution.py:514
  37.5 2.3 %collective-permute-start.10 = (bf16[256,128]{1,0:T(8,128)(2,1)S(1)}, bf16[256,128]{1,0:T(8,128)(2,1)S(1)}, u32[]{:S(2)}, u32[]{:S(2)}) collective-permute-start(bf16[256,128]{1,0:T(8,128)(2,1)S(1)} %get-tuple-element.51), channel_id=1, source_target_pairs={{0,12},{4,8},{8,4},{12,0},{16,28},{20,24},{24,20},{28,16},{1,13},{... | collective-permute-start | bytes 196616 | tf_op jit(solution)/shard_map/ppermute | solution.py:514
  39.8 2.4 %shard_map.76 = (f32[8,128,128]{2,1,0:T(8,128)S(1)}, bf16[8,5,128,128]{3,2,1,0:T(8,128)(2,1)S(1)}) custom-call(bf16[4,528,128]{2,1,0:T(8,128)(2,1)S(1)} %all-to-all-done.part_ref, bf16[8,128,256]{2,1,0:T(8,128)(2,1)S(1)} %get-tuple-element.32.mixed_ref, bf16[4,2,128,128]{3,2,1,0:T(8,128)(2,1)S(1)} %get-tuple-element.33.even_ref, ...), custom_call_target="tpu_custom_call" | custom-call | bytes 2097152 | tf_op jit(solution)/shard_map/pallas_call | solution.py:586
  42.2 1.8 %shard_map.77.weights_ref = bf16[8,128,512]{2,1,0:T(8,128)(2,1)S(1)} custom-call(s32[8,128]{1,0:T(8,128)S(1)} %get-tuple-element.31.refs_4_.away_ref, bf16[8,5,128,128]{3,2,1,0:T(8,128)(2,1)S(1)} %get-tuple-element.43.moving_ref, f32[8,128,128]{2,1,0:T(8,128)S(1)} %get-tuple-element.44.inner_ref, bf16[8,128,128]{2,1,0:T(8,128)(2,1)S(1)} %get-tuple-element.45.end_ref, ...), custom_call_target="tpu_custom_call" | custom-call | bytes 2097152 | tf_op jit(solution)/shard_map/pallas_call | solution.py:593
  44.1 1.9 %shard_map.78 = (bf16[4,2,2,128,128]{4,3,2,1,0:T(8,128)(2,1)S(1)}, bf16[512,1024]{1,0:T(8,128)(2,1)S(1)}) custom-call(s32[8,128]{1,0:T(8,128)S(1)} %get-tuple-element.31.refs_4_.away_ref, bf16[8,128,512]{2,1,0:T(8,128)(2,1)S(1)} %shard_map.77.weights_ref, bf16[256,128]{1,0:T(8,128)(2,1)S(1)} %get-tuple-element.48.refs_0_, ...), custom_call_target="tpu_custom_call" | custom-call | bytes 2097152 | tf_op jit(solution)/shard_map/pallas_call | solution.py:599
  46.0 10.4 %all_to_all.10 = bf16[8,2,128,128]{3,2,1,0:T(8,128)(2,1)S(1)} all-to-all(bf16[8,2,128,128]{3,2,1,0:T(8,128)(2,1)S(1)} %bitcast.4), channel_id=1, replica_groups={{0,2,4,6,8,10,12,14},{1,3,5,7,9,11,13,15},{16,18,20,22,24,26,28,30},{17..., dimensions={0} | all-to-all | bytes 1048576 | tf_op jit(solution)/shard_map/all_to_all | solution.py:620
  56.4 0.4 shard_map.80
  57.0 0.4 shard_map.79
  57.4 1.1 %collective-permute-done.12 = bf16[256,512]{1,0:T(8,128)(2,1)S(1)} collective-permute-done((bf16[256,512]{1,0:T(8,128)(2,1)S(1)}, bf16[256,512]{1,0:T(8,128)(2,1)S(1)}, u32[]{:S(2)}, u32[]{:S(2)}) %collective-permute-start.12) | collective-permute-done | bytes 262176 | tf_op jit(solution)/shard_map/ppermute | solution.py:633
  58.5 0.8 %add_convert_fusion = bf16[256,512]{1,0:T(8,128)(2,1)} fusion(f32[256,512]{1,0:T(8,128)S(1)} %shard_map.79, bf16[256,512]{1,0:T(8,128)(2,1)S(1)} %collective-permute-done.12), kind=kLoop, calls=%fused_computation | loop fusion | flops 393216 | bytes 1048576 | tf_op jit(solution)/shard_map/convert_element_type | solution.py:634
  (20 shorter events, 0.3 us)
Async XLA Ops:
  2.9 17.6 %all-to-all-start = ((bf16[4,528,128]{2,1,0:T(8,128)(2,1)}), bf16[4,528,128]{2,1,0:T(8,128)(2,1)S(1)}, u32[]{:S(2)}, u32[]{:S(2)}) async-start(bf16[4,528,128]{2,1,0:T(8,128)(2,1)} %get-tuple-element.30), calls=%async_computation | async-start | bytes 1081344 | tf_op jit(solution)/shard_map/all_to_all | solution.py:506
  8.1 18.8 %collective-permute-start = (bf16[256,128]{1,0:T(8,128)(2,1)}, bf16[256,128]{1,0:T(8,128)(2,1)S(1)}, u32[]{:S(2)}, u32[]{:S(2)}) collective-permute-start(bf16[256,128]{1,0:T(8,128)(2,1)} %get-tuple-element.35), channel_id=1, source_target_pairs={{0,16},{4,20},{8,24},{12,28},{1,17},{5,21},{9,25},{13,29},{2,18},{... | collective-permute-start | bytes 196616 | tf_op jit(solution)/shard_map/ppermute | solution.py:519
  12.6 15.6 %collective-permute-start.1 = (bf16[256,128]{1,0:T(8,128)(2,1)}, bf16[256,128]{1,0:T(8,128)(2,1)S(1)}, u32[]{:S(2)}, u32[]{:S(2)}) collective-permute-start(bf16[256,128]{1,0:T(8,128)(2,1)} %get-tuple-element.36), channel_id=1, source_target_pairs={{0,20},{4,16},{8,28},{12,24},{1,21},{5,17},{9,29},{13,25},{2,22},{... | collective-permute-start | bytes 196616 | tf_op jit(solution)/shard_map/ppermute | solution.py:519
  15.4 12.9 %collective-permute-start.2 = (bf16[256,128]{1,0:T(8,128)(2,1)}, bf16[256,128]{1,0:T(8,128)(2,1)S(1)}, u32[]{:S(2)}, u32[]{:S(2)}) collective-permute-start(bf16[256,128]{1,0:T(8,128)(2,1)} %get-tuple-element.37), channel_id=1, source_target_pairs={{0,24},{4,28},{8,16},{12,20},{1,25},{5,29},{9,17},{13,21},{2,26},{... | collective-permute-start | bytes 196616 | tf_op jit(solution)/shard_map/ppermute | solution.py:519
  16.7 11.6 %collective-permute-start.3 = (bf16[256,128]{1,0:T(8,128)(2,1)}, bf16[256,128]{1,0:T(8,128)(2,1)S(1)}, u32[]{:S(2)}, u32[]{:S(2)}) collective-permute-start(bf16[256,128]{1,0:T(8,128)(2,1)} %get-tuple-element.38), channel_id=1, source_target_pairs={{0,28},{4,24},{8,20},{12,16},{1,29},{5,25},{9,21},{13,17},{2,30},{... | collective-permute-start | bytes 196616 | tf_op jit(solution)/shard_map/ppermute | solution.py:519
  18.9 9.4 %copy-start.1 = (bf16[256,512]{1,0:T(8,128)(2,1)S(1)}, bf16[256,512]{1,0:T(8,128)(2,1)}, u32[]{:S(2)}) copy-start(bf16[256,512]{1,0:T(8,128)(2,1)} %values_ref.3) | copy-start | bytes 786436
  18.9 9.4 %copy-start.2 = (bf16[256,512]{1,0:T(8,128)(2,1)S(1)}, bf16[256,512]{1,0:T(8,128)(2,1)}, u32[]{:S(2)}) copy-start(bf16[256,512]{1,0:T(8,128)(2,1)} %queries_ref.1) | copy-start | bytes 786436
  18.9 25.2 %collective-permute-start.11 = (bf16[512,1024]{1,0:T(8,128)(2,1)}, bf16[512,1024]{1,0:T(8,128)(2,1)S(1)}, u32[]{:S(2)}, u32[]{:S(2)}) collective-permute-start(bf16[512,1024]{1,0:T(8,128)(2,1)} %get-tuple-element.52), channel_id=1, source_target_pairs={{0,2},{1,3},{2,0},{3,1},{4,6},{5,7},{6,4},{7,5},{8,10},{9,11},{10,... | collective-permute-start | bytes 3145736 | tf_op jit(solution)/shard_map/ppermute | solution.py:557
  26.9 15.3 %collective-permute-start.7 = (bf16[8,128,128]{2,1,0:T(8,128)(2,1)S(1)}, bf16[8,128,128]{2,1,0:T(8,128)(2,1)S(1)}, u32[]{:S(2)}, u32[]{:S(2)}) collective-permute-start(bf16[8,128,128]{2,1,0:T(8,128)(2,1)S(1)} %get-tuple-element.47), channel_id=1, source_target_pairs={{0,16},{4,20},{8,24},{12,28},{1,17},{5,21},{9,25},{13,29},{2,18},{... | collective-permute-start | bytes 786440 | tf_op jit(solution)/shard_map/ppermute | solution.py:510
  28.5 5.3 %collective-permute-start.4 = (bf16[256,128]{1,0:T(8,128)(2,1)S(1)}, bf16[256,128]{1,0:T(8,128)(2,1)S(1)}, u32[]{:S(2)}, u32[]{:S(2)}) collective-permute-start(bf16[256,128]{1,0:T(8,128)(2,1)S(1)} %get-tuple-element.40), channel_id=1, source_target_pairs={{0,4},{4,0},{8,12},{12,8},{16,20},{20,16},{24,28},{28,24},{1,5},{5... | collective-permute-start | bytes 196616 | tf_op jit(solution)/shard_map/ppermute | solution.py:514
  29.1 5.9 %collective-permute-start.5 = (bf16[256,128]{1,0:T(8,128)(2,1)S(1)}, bf16[256,128]{1,0:T(8,128)(2,1)S(1)}, u32[]{:S(2)}, u32[]{:S(2)}) collective-permute-start(bf16[256,128]{1,0:T(8,128)(2,1)S(1)} %get-tuple-element.41), channel_id=1, source_target_pairs={{0,8},{4,12},{8,0},{12,4},{16,24},{20,28},{24,16},{28,20},{1,9},{5... | collective-permute-start | bytes 196616 | tf_op jit(solution)/shard_map/ppermute | solution.py:514
  31.3 6.3 %collective-permute-start.6 = (bf16[256,128]{1,0:T(8,128)(2,1)S(1)}, bf16[256,128]{1,0:T(8,128)(2,1)S(1)}, u32[]{:S(2)}, u32[]{:S(2)}) collective-permute-start(bf16[256,128]{1,0:T(8,128)(2,1)S(1)} %get-tuple-element.42), channel_id=1, source_target_pairs={{0,12},{4,8},{8,4},{12,0},{16,28},{20,24},{24,20},{28,16},{1,13},{... | collective-permute-start | bytes 196616 | tf_op jit(solution)/shard_map/ppermute | solution.py:514
  33.7 10.3 %collective-permute-start.8 = (bf16[256,128]{1,0:T(8,128)(2,1)S(1)}, bf16[256,128]{1,0:T(8,128)(2,1)S(1)}, u32[]{:S(2)}, u32[]{:S(2)}) collective-permute-start(bf16[256,128]{1,0:T(8,128)(2,1)S(1)} %get-tuple-element.49), channel_id=1, source_target_pairs={{0,4},{4,0},{8,12},{12,8},{16,20},{20,16},{24,28},{28,24},{1,5},{5... | collective-permute-start | bytes 196616 | tf_op jit(solution)/shard_map/ppermute | solution.py:514
  35.0 9.0 %collective-permute-start.9 = (bf16[256,128]{1,0:T(8,128)(2,1)S(1)}, bf16[256,128]{1,0:T(8,128)(2,1)S(1)}, u32[]{:S(2)}, u32[]{:S(2)}) collective-permute-start(bf16[256,128]{1,0:T(8,128)(2,1)S(1)} %get-tuple-element.50), channel_id=1, source_target_pairs={{0,8},{4,12},{8,0},{12,4},{16,24},{20,28},{24,16},{28,20},{1,9},{5... | collective-permute-start | bytes 196616 | tf_op jit(solution)/shard_map/ppermute | solution.py:514
  37.5 6.5 %collective-permute-start.10 = (bf16[256,128]{1,0:T(8,128)(2,1)S(1)}, bf16[256,128]{1,0:T(8,128)(2,1)S(1)}, u32[]{:S(2)}, u32[]{:S(2)}) collective-permute-start(bf16[256,128]{1,0:T(8,128)(2,1)S(1)} %get-tuple-element.51), channel_id=1, source_target_pairs={{0,12},{4,8},{8,4},{12,0},{16,28},{20,24},{24,20},{28,16},{1,13},{... | collective-permute-start | bytes 196616 | tf_op jit(solution)/shard_map/ppermute | solution.py:514
  44.0 12.4 %copy-start = (bf16[512,2048]{1,0:T(8,128)(2,1)S(1)}, bf16[512,2048]{1,0:T(8,128)(2,1)}, u32[]{:S(2)}) copy-start(bf16[512,2048]{1,0:T(8,128)(2,1)} %own_ref.3) | copy-start | bytes 6291460
  56.9 1.6 %collective-permute-start.12 = (bf16[256,512]{1,0:T(8,128)(2,1)S(1)}, bf16[256,512]{1,0:T(8,128)(2,1)S(1)}, u32[]{:S(2)}, u32[]{:S(2)}) collective-permute-start(bf16[256,512]{1,0:T(8,128)(2,1)S(1)} %shard_map.80), channel_id=1, source_target_pairs={{0,1},{1,0},{2,3},{3,2},{4,5},{5,4},{6,7},{7,6},{8,9},{9,8},{10,11... | collective-permute-start | bytes 786440 | tf_op jit(solution)/shard_map/ppermute | solution.py:633

commit v15 on v14

--- a/solution.py
+++ b/solution.py
@@ -71,7 +71,8 @@
     blocks = tokens // BLOCK
     (parts_ref, rates_ref, selected_ref, cut_ref, piece_ref, sems, few_sems, out_sems, cut_sems,
      cut_out_sems, piece_sems) = refs[-11:]
-    out_ref, cut_outs, piece_outs = refs[0], refs[1:1 + heads], refs[1 + heads:-11]
+    rounds = heads // 2
+    out_ref, cut_outs, piece_outs = refs[0], refs[1:1 + rounds], refs[1 + rounds:-11]
     planes = len(piece_outs) + 1
     width = weight_ref.shape[1] // planes
     device = lax.axis_index(axes[0])
@@ -97,7 +98,7 @@
     ]
     cut_copies = fetched(
         [values_ref.at[:, pl.ds(cut, HEAD_DIM)] for cut in cuts],
-        [cut_ref.at[turn] for turn in range(heads)],
+        [cut_ref.at[turn // 2, turn % 2] for turn in range(heads)],
         cut_sems,
     )
     piece_copies = []
@@ -137,8 +138,9 @@
             pltpu.make_async_copy(parts_ref.at[head], out_ref.at[head], out_sems.at[head])
         )
         out_copies[-1].start()
-    for turn in range(heads):
-        cut_copies[turn].wait()
+    for turn in range(rounds):
+        cut_copies[2 * turn].wait()
+        cut_copies[2 * turn + 1].wait()
         out_copies += fetched(
             [cut_ref.at[turn]], [cut_outs[turn]], cut_out_sems.at[pl.ds(turn, 1)]
         )
@@ -152,20 +154,27 @@
 
 
 def cut_kernel(axes, queries_ref, values_ref, *refs):
-    sems = refs[-1]
+    sems, more_sems = refs[-2:]
     heads = sems.shape[1]
-    outs = refs[-1 - 2 * heads:-1]
+    outs = refs[-2 - 2 * heads:-2]
+    come = refs[:-3 - 2 * heads]
     place = lax.rem(lax.axis_index(axes[0]), heads)
     cuts = [
         pl.multiple_of(lax.bitwise_xor(place, turn) * HEAD_DIM, HEAD_DIM) for turn in range(heads)
     ]
     copies = []
     for kind, source in enumerate((queries_ref, values_ref)):
+        targets = list(outs[kind * heads:(kind + 1) * heads])
+        if kind:
+            targets[1] = targets[1].at[0]
         copies += fetched(
-            [source.at[:, pl.ds(cut, HEAD_DIM)] for cut in cuts],
-            outs[kind * heads:(kind + 1) * heads],
-            sems.at[kind],
+            [source.at[:, pl.ds(cut, HEAD_DIM)] for cut in cuts], targets, sems.at[kind]
         )
+    copies += fetched(
+        [part.at[1] for part in come],
+        [outs[heads + 1].at[1 + index] for index in range(len(come))],
+        more_sems,
+    )
     for copy in copies:
         copy.wait()
 
@@ -404,22 +413,31 @@
 def blend_kernel(axes, before, blocks, away_ref, weights_ref, *refs):
     units = weights_ref.shape[0]
     heads = units // blocks
-    count = (len(refs) - 4 - heads * (1 + before)) // 2
-    arrived = refs[:heads * (1 + before)]
+    rounds = heads // 2
+    own, come = refs[:heads], refs[heads:heads + rounds * before]
+    count = (len(refs) - 4 - heads - rounds * before) // 2
     out_ref, (values_ref, value_sems, sems) = refs[-4 - count], refs[-3:]
     place = lax.rem(lax.axis_index(axes[0]), heads)
     value_copies = []
-    for kind in range(1 + before):
-        for turn in range(heads):
-            start = pl.multiple_of(lax.bitwise_xor(place, turn) * blocks * BLOCK, BLOCK)
-            value_copies += fetched(
-                [arrived[kind * heads + turn]],
+
+    def put(source, kind, turn):
+        start = pl.multiple_of(lax.bitwise_xor(place, turn) * blocks * BLOCK, BLOCK)
+        value_copies.extend(
+            fetched(
+                [source],
                 [values_ref.at[kind, pl.ds(start, blocks * BLOCK)]],
                 value_sems.at[kind, pl.ds(turn, 1)],
             )
-    copies = fetched(
-        refs[heads * (1 + before):heads * (1 + before) + count], refs[-3 - count:-3], sems
-    )
+        )
+
+    for turn in range(heads):
+        put(own[turn].at[0] if turn == 1 else own[turn], 0, turn)
+    for index in range(rounds * before):
+        kind, turn = 1 + index // rounds, 2 * (index % rounds)
+        put(come[index].at[0], kind, turn)
+        put(own[1].at[1 + index], kind, turn + 1)
+    start = heads + rounds * before
+    copies = fetched(refs[start:start + count], refs[-3 - count:-3], sems)
     for copy in value_copies:
         copy.wait()
 
@@ -515,7 +533,7 @@
 
     def straight(value, turn, by):
         shift = by * heads
-        pairs = [(i, i - i % heads + (i % heads ^ turn) + shift) for i in range(ctx_size - shift)]
+        pairs = [(i, (i ^ 2 * turn) + shift) for i in range(ctx_size - shift)]
         return lax.ppermute(value, "ctx", pairs)
 
     def array(shape, kind=BF16):
@@ -524,10 +542,11 @@
     part_shape = (heads, 2 * tokens + EXTRA, HEAD_DIM)
     width = out_weight.shape[1] // planes
     piece_shape = (out_weight.shape[0], width)
+    rounds = heads // 2
     packed, *rest = call(
         functools.partial(pack_kernel, axes, cores),
         [array(part_shape)]
-        + [array((tokens, HEAD_DIM))] * heads
+        + [array((2, tokens, HEAD_DIM))] * rounds
         + [array(piece_shape)] * (planes - 1),
         [ANY] * 6,
         cubes,
@@ -535,7 +554,7 @@
             pltpu.VMEM(part_shape, BF16),
             pltpu.VMEM(rates.shape, F32),
             pltpu.SMEM(selected.shape, jnp.int32),
-            pltpu.VMEM((heads, tokens, HEAD_DIM), BF16),
+            pltpu.VMEM((rounds, 2, tokens, HEAD_DIM), BF16),
             pltpu.VMEM((max(planes - 1, 1), *piece_shape), BF16),
             pltpu.SemaphoreType.DMA((heads, 2)),
             pltpu.SemaphoreType.DMA((2,)),
@@ -544,12 +563,14 @@
             pltpu.SemaphoreType.DMA((heads,)),
             pltpu.SemaphoreType.DMA((2, planes)),
         ],
-        [ANY] * (heads + planes),
+        [ANY] * (rounds + planes),
         56,
     )(directions, keys, rates, selected, values, out_weight)
-    value_cuts, pieces = rest[:heads], rest[heads:]
+    value_cuts, pieces = rest[:rounds], rest[rounds:]
     value_parts = [
-        straight(value_cuts[turn], turn, by) for by in range(1, before + 1) for turn in range(heads)
+        straight(value_cuts[turn], turn, by)
+        for by in range(1, before + 1)
+        for turn in range(rounds)
     ]
     weight_parts = []
     for offset in range(1, planes):
@@ -576,10 +597,16 @@
     map_parts = [onward(group_map, by) for by in range(1, before)]
     cut = call(
         functools.partial(cut_kernel, axes),
-        [array((tokens, HEAD_DIM))] * (2 * heads),
+        [
+            array((1 + len(value_parts), tokens, HEAD_DIM) if turn == heads + 1 else (tokens, HEAD_DIM))
+            for turn in range(2 * heads)
+        ],
         [ANY] * (len(value_parts) + 3),
         2000 * cubes,
-        [pltpu.SemaphoreType.DMA((2, heads))],
+        [
+            pltpu.SemaphoreType.DMA((2, heads)),
+            pltpu.SemaphoreType.DMA((max(len(value_parts), 1),)),
+        ],
     )(queries, values, *value_parts, away)
     query_parts = [crossed(cut[turn], turn) for turn in range(heads)]
     own_parts = [crossed(cut[heads + turn], turn) for turn in range(heads)]
@@ -599,7 +626,7 @@
     attended, *weight_parts = call(
         functools.partial(blend_kernel, axes, before, blocks),
         [array((heads, planes, blocks, *tile))] + [array(part.shape) for part in weight_parts],
-        [SMEM, VMEM] + [ANY] * (heads * (1 + before) + len(weight_parts)),
+        [SMEM, VMEM] + [ANY] * (heads + len(value_parts) + len(weight_parts)),
         0,
         [
             pltpu.VMEM((1 + before, units * BLOCK, HEAD_DIM), BF16),

time: 59.6 us -> 61.5 us (1.032)
  starting transfers between devices: 27.2 us -> 29 us
    ppermute x4 -> x2, starting transfers between devices: 10.7 us -> 7.24 us  [straight(): return lax.ppermute(value, 'ctx', pairs)]
    ppermute x6, starting transfers between devices: 8.29 us -> 11 us  [crossed(): return lax.ppermute(value, 'ctx', pairs) if turn else value]
    ppermute x1, starting transfers between devices: 1.29 us -> 3.85 us  [onward(): lax.ppermute(value, 'ctx', [(i, i + shift) for i in range(ctx_size - shif...]
  transfers between devices with their start and end apart: 14 -> 12, of which waited for: 3 -> 3; matrix products, arithmetic and copies ran while one was open for 0% -> 0% of each run, Pallas kernels for 19% -> 19%
where the time goes in v15:
time: 61.5 us; the launch traced here: 61.2 us
  starting transfers between devices  29 us (47%)
  Pallas kernels  16.7 us (27%)
  blocking collectives  10.9 us (18%)
  waiting for transfers between devices  3.68 us (6%)
  other arithmetic  0.77 us (1%)
    ppermute x6, starting transfers between devices, crossed(): return lax.ppermute(value, 'ctx', pairs) if turn else value  11 us
    all_to_all x1, blocking collectives, body(): lax.all_to_all(attended.reshape(heads * planes, blocks, *tile), axes, 0,...  10.9 us
    ppermute x2, starting transfers between devices, straight(): return lax.ppermute(value, 'ctx', pairs)  7.24 us
    pallas_call x1, Pallas kernels, body(): call(functools.partial(keys_kernel, blocks), [array((units, *tile)), arra...  6.44 us
    all_to_all x1, starting transfers between devices, exchange(): lax.all_to_all(value, 'ctx', 0, 0, axis_index_groups=members, tiled=True)  5.26 us
    ppermute x1, starting transfers between devices, onward(): lax.ppermute(value, 'ctx', [(i, i + shift) for i in range(ctx_size - shif...  3.85 us
    pallas_call x1, Pallas kernels, body(): call(functools.partial(pack_kernel, axes, cores), [array(part_shape)] + [...  2.84 us
    ppermute x6, waiting for transfers between devices, crossed(): return lax.ppermute(value, 'ctx', pairs) if turn else value  2.59 us
  transfers between devices with their start and end apart: 12, of which 3 were waited for; matrix products, arithmetic and copies ran while one was open for 0% of the time, Pallas kernels for 19%

profile of v15, /device:TPU:0, one launch (start us, length us, event | category | flops | bytes accessed | tf_op | source)
XLA Modules:
  0.0 61.2 jit_solution(14793644839921706965)
XLA Ops:
  0.0 2.8 %shard_map.73 = (bf16[4,528,128]{2,1,0:T(8,128)(2,1)}, bf16[2,256,128]{2,1,0:T(8,128)(2,1)}, bf16[2,256,128]{2,1,0:T(8,128)(2,1)}, bf16[512,1024]{1,0:T(8,128)(2,1)}) custom-call(bf16[256,512]{1,0:T(8,128)(2,1)} %d_ref.1, bf16[256,512]{1,0:T(8,128)(2,1)} %k_ref.1, f32[4,256]{1,0:T(4,128)} %rates_hbm.1, s32[2,4]{1,0:T(2,128)} %selected_hbm.1, ...), custom_call_target="tpu_custom_call" | custom-call | flops 4194304 | bytes 2097152 | tf_op jit(solution)/shard_map/pallas_call | solution.py:546
  2.8 5.3 %all-to-all-start = ((bf16[4,528,128]{2,1,0:T(8,128)(2,1)}), bf16[4,528,128]{2,1,0:T(8,128)(2,1)S(1)}, u32[]{:S(2)}, u32[]{:S(2)}) async-start(bf16[4,528,128]{2,1,0:T(8,128)(2,1)} %get-tuple-element.28), calls=%async_computation | async-start | bytes 1081344 | tf_op jit(solution)/shard_map/all_to_all | solution.py:524
  8.1 4.5 %collective-permute-start = (bf16[2,256,128]{2,1,0:T(8,128)(2,1)}, bf16[2,256,128]{2,1,0:T(8,128)(2,1)S(1)}, u32[]{:S(2)}, u32[]{:S(2)}) collective-permute-start(bf16[2,256,128]{2,1,0:T(8,128)(2,1)} %get-tuple-element.33), channel_id=1, source_target_pairs={{0,16},{4,20},{8,24},{12,28},{1,17},{5,21},{9,25},{13,29},{2,18},{... | collective-permute-start | bytes 393224 | tf_op jit(solution)/shard_map/ppermute | solution.py:537
  12.6 2.8 %collective-permute-start.1 = (bf16[2,256,128]{2,1,0:T(8,128)(2,1)}, bf16[2,256,128]{2,1,0:T(8,128)(2,1)S(1)}, u32[]{:S(2)}, u32[]{:S(2)}) collective-permute-start(bf16[2,256,128]{2,1,0:T(8,128)(2,1)} %get-tuple-element.34), channel_id=1, source_target_pairs={{0,24},{4,28},{8,16},{12,20},{1,25},{5,29},{9,17},{13,21},{2,26},{... | collective-permute-start | bytes 393224 | tf_op jit(solution)/shard_map/ppermute | solution.py:537
  15.4 1.6 %collective-permute-start.9 = (bf16[512,1024]{1,0:T(8,128)(2,1)}, bf16[512,1024]{1,0:T(8,128)(2,1)S(1)}, u32[]{:S(2)}, u32[]{:S(2)}) collective-permute-start(bf16[512,1024]{1,0:T(8,128)(2,1)} %get-tuple-element.48), channel_id=1, source_target_pairs={{0,2},{1,3},{2,0},{3,1},{4,6},{5,7},{6,4},{7,5},{8,10},{9,11},{10,... | collective-permute-start | bytes 3145736 | tf_op jit(solution)/shard_map/ppermute | solution.py:578
  17.0 6.4 %shard_map.74 = (bf16[8,128,128]{2,1,0:T(8,128)(2,1)S(1)}, bf16[8,128,128]{2,1,0:T(8,128)(2,1)S(1)}, bf16[8,128,128]{2,1,0:T(8,128)(2,1)S(1)}, bf16[4,2,128,128]...) custom-call(bf16[4,528,128]{2,1,0:T(8,128)(2,1)S(1)} %all-to-all-don, ...), custom_call_target="tpu_custom_call" | custom-call | flops 1677721600 | bytes 2097152 | tf_op jit(solution)/shard_map/pallas_call | solution.py:581
  23.4 3.9 %collective-permute-start.5 = (bf16[8,128,128]{2,1,0:T(8,128)(2,1)S(1)}, bf16[8,128,128]{2,1,0:T(8,128)(2,1)S(1)}, u32[]{:S(2)}, u32[]{:S(2)}) collective-permute-start(bf16[8,128,128]{2,1,0:T(8,128)(2,1)S(1)} %get-tuple-element.43), channel_id=1, source_target_pairs={{0,16},{4,20},{8,24},{12,28},{1,17},{5,21},{9,25},{13,29},{2,18},{... | collective-permute-start | bytes 786440 | tf_op jit(solution)/shard_map/ppermute | solution.py:528
  27.3 0.4 shard_map.75
  27.7 1.7 %collective-permute-start.2 = (bf16[256,128]{1,0:T(8,128)(2,1)S(1)}, bf16[256,128]{1,0:T(8,128)(2,1)S(1)}, u32[]{:S(2)}, u32[]{:S(2)}) collective-permute-start(bf16[256,128]{1,0:T(8,128)(2,1)S(1)} %get-tuple-element.36), channel_id=1, source_target_pairs={{0,4},{4,0},{8,12},{12,8},{16,20},{20,16},{24,28},{28,24},{1,5},{5... | collective-permute-start | bytes 196616 | tf_op jit(solution)/shard_map/ppermute | solution.py:532
  29.4 0.4 collective-permute-start.6
  29.8 2.2 %collective-permute-start.3 = (bf16[256,128]{1,0:T(8,128)(2,1)S(1)}, bf16[256,128]{1,0:T(8,128)(2,1)S(1)}, u32[]{:S(2)}, u32[]{:S(2)}) collective-permute-start(bf16[256,128]{1,0:T(8,128)(2,1)S(1)} %get-tuple-element.37), channel_id=1, source_target_pairs={{0,8},{4,12},{8,0},{12,4},{16,24},{20,28},{24,16},{28,20},{1,9},{5... | collective-permute-start | bytes 196616 | tf_op jit(solution)/shard_map/ppermute | solution.py:532
  32.0 0.7 %collective-permute-done.2.refs_1_ = bf16[256,128]{1,0:T(8,128)(2,1)S(1)} collective-permute-done((bf16[256,128]{1,0:T(8,128)(2,1)S(1)}, bf16[256,128]{1,0:T(8,128)(2,1)S(1)}, u32[]{:S(2)}, u32[]{:S(2)}) %collective-permute-start.2) | collective-permute-done | bytes 65568 | tf_op jit(solution)/shard_map/ppermute | solution.py:532
  32.7 2.9 %collective-permute-start.4 = (bf16[256,128]{1,0:T(8,128)(2,1)S(1)}, bf16[256,128]{1,0:T(8,128)(2,1)S(1)}, u32[]{:S(2)}, u32[]{:S(2)}) collective-permute-start(bf16[256,128]{1,0:T(8,128)(2,1)S(1)} %get-tuple-element.38), channel_id=1, source_target_pairs={{0,12},{4,8},{8,4},{12,0},{16,28},{20,24},{24,20},{28,16},{1,13},{... | collective-permute-start | bytes 196616 | tf_op jit(solution)/shard_map/ppermute | solution.py:532
  35.6 0.6 %collective-permute-start.7 = (bf16[256,128]{1,0:T(8,128)(2,1)S(1)}, bf16[256,128]{1,0:T(8,128)(2,1)S(1)}, u32[]{:S(2)}, u32[]{:S(2)}) collective-permute-start(bf16[256,128]{1,0:T(8,128)(2,1)S(1)} %get-tuple-element.46), channel_id=1, source_target_pairs={{0,8},{4,12},{8,0},{12,4},{16,24},{20,28},{24,16},{28,20},{1,9},{5... | collective-permute-start | bytes 196616 | tf_op jit(solution)/shard_map/ppermute | solution.py:532
  36.3 1.8 %collective-permute-done.4.refs_3_ = bf16[256,128]{1,0:T(8,128)(2,1)S(1)} collective-permute-done((bf16[256,128]{1,0:T(8,128)(2,1)S(1)}, bf16[256,128]{1,0:T(8,128)(2,1)S(1)}, u32[]{:S(2)}, u32[]{:S(2)}) %collective-permute-start.4) | collective-permute-done | bytes 65568 | tf_op jit(solution)/shard_map/ppermute | solution.py:532
  38.1 3.2 %collective-permute-start.8 = (bf16[256,128]{1,0:T(8,128)(2,1)S(1)}, bf16[256,128]{1,0:T(8,128)(2,1)S(1)}, u32[]{:S(2)}, u32[]{:S(2)}) collective-permute-start(bf16[256,128]{1,0:T(8,128)(2,1)S(1)} %get-tuple-element.47), channel_id=1, source_target_pairs={{0,12},{4,8},{8,4},{12,0},{16,28},{20,24},{24,20},{28,16},{1,13},{... | collective-permute-start | bytes 196616 | tf_op jit(solution)/shard_map/ppermute | solution.py:532
  41.3 2.4 %shard_map.76 = (f32[8,128,128]{2,1,0:T(8,128)S(1)}, bf16[8,5,128,128]{3,2,1,0:T(8,128)(2,1)S(1)}) custom-call(bf16[4,528,128]{2,1,0:T(8,128)(2,1)S(1)} %all-to-all-done.part_ref, bf16[8,128,256]{2,1,0:T(8,128)(2,1)S(1)} %get-tuple-element.30.mixed_ref, bf16[4,2,128,128]{3,2,1,0:T(8,128)(2,1)S(1)} %get-tuple-element.31.even_ref, ...), custom_call_target="tpu_custom_call" | custom-call | bytes 2097152 | tf_op jit(solution)/shard_map/pallas_call | solution.py:613
  43.7 1.8 %shard_map.77.weights_ref = bf16[8,128,512]{2,1,0:T(8,128)(2,1)S(1)} custom-call(s32[8,128]{1,0:T(8,128)S(1)} %get-tuple-element.29.refs_2_.away_ref, bf16[8,5,128,128]{3,2,1,0:T(8,128)(2,1)S(1)} %get-tuple-element.39.moving_ref, f32[8,128,128]{2,1,0:T(8,128)S(1)} %get-tuple-element.40.inner_ref, bf16[8,128,128]{2,1,0:T(8,128)(2,1)S(1)} %get-tuple-element.41.end_ref, ...), custom_call_target="tpu_custom_call" | custom-call | bytes 2097152 | tf_op jit(solution)/shard_map/pallas_call | solution.py:620
  45.6 1.9 %shard_map.78 = (bf16[4,2,2,128,128]{4,3,2,1,0:T(8,128)(2,1)S(1)}, bf16[512,1024]{1,0:T(8,128)(2,1)S(1)}) custom-call(s32[8,128]{1,0:T(8,128)S(1)} %get-tuple-element.29.refs_2_.away_ref, bf16[8,128,512]{2,1,0:T(8,128)(2,1)S(1)} %shard_map.77.weights_ref, bf16[256,128]{1,0:T(8,128)(2,1)S(1)} %get-tuple-element.44.refs_0_, ...), custom_call_target="tpu_custom_call" | custom-call | bytes 2097152 | tf_op jit(solution)/shard_map/pallas_call | solution.py:626
  47.5 10.9 %all_to_all.10 = bf16[8,2,128,128]{3,2,1,0:T(8,128)(2,1)S(1)} all-to-all(bf16[8,2,128,128]{3,2,1,0:T(8,128)(2,1)S(1)} %bitcast.4), channel_id=1, replica_groups={{0,2,4,6,8,10,12,14},{1,3,5,7,9,11,13,15},{16,18,20,22,24,26,28,30},{17..., dimensions={0} | all-to-all | bytes 1048576 | tf_op jit(solution)/shard_map/all_to_all | solution.py:647
  58.4 0.4 shard_map.80
  58.9 0.4 shard_map.79
  59.4 1.1 %collective-permute-done.10 = bf16[256,512]{1,0:T(8,128)(2,1)S(1)} collective-permute-done((bf16[256,512]{1,0:T(8,128)(2,1)S(1)}, bf16[256,512]{1,0:T(8,128)(2,1)S(1)}, u32[]{:S(2)}, u32[]{:S(2)}) %collective-permute-start.10) | collective-permute-done | bytes 262176 | tf_op jit(solution)/shard_map/ppermute | solution.py:660
  60.5 0.8 %add_convert_fusion = bf16[256,512]{1,0:T(8,128)(2,1)} fusion(f32[256,512]{1,0:T(8,128)S(1)} %shard_map.79, bf16[256,512]{1,0:T(8,128)(2,1)S(1)} %collective-permute-done.10), kind=kLoop, calls=%fused_computation | loop fusion | flops 393216 | bytes 1048576 | tf_op jit(solution)/shard_map/convert_element_type | solution.py:661
  (16 shorter events, 0.1 us)
Async XLA Ops:
  2.8 14.1 %all-to-all-start = ((bf16[4,528,128]{2,1,0:T(8,128)(2,1)}), bf16[4,528,128]{2,1,0:T(8,128)(2,1)S(1)}, u32[]{:S(2)}, u32[]{:S(2)}) async-start(bf16[4,528,128]{2,1,0:T(8,128)(2,1)} %get-tuple-element.28), calls=%async_computation | async-start | bytes 1081344 | tf_op jit(solution)/shard_map/all_to_all | solution.py:524
  8.1 19.1 %collective-permute-start = (bf16[2,256,128]{2,1,0:T(8,128)(2,1)}, bf16[2,256,128]{2,1,0:T(8,128)(2,1)S(1)}, u32[]{:S(2)}, u32[]{:S(2)}) collective-permute-start(bf16[2,256,128]{2,1,0:T(8,128)(2,1)} %get-tuple-element.33), channel_id=1, source_target_pairs={{0,16},{4,20},{8,24},{12,28},{1,17},{5,21},{9,25},{13,29},{2,18},{... | collective-permute-start | bytes 393224 | tf_op jit(solution)/shard_map/ppermute | solution.py:537
  12.6 14.7 %collective-permute-start.1 = (bf16[2,256,128]{2,1,0:T(8,128)(2,1)}, bf16[2,256,128]{2,1,0:T(8,128)(2,1)S(1)}, u32[]{:S(2)}, u32[]{:S(2)}) collective-permute-start(bf16[2,256,128]{2,1,0:T(8,128)(2,1)} %get-tuple-element.34), channel_id=1, source_target_pairs={{0,24},{4,28},{8,16},{12,20},{1,25},{5,29},{9,17},{13,21},{2,26},{... | collective-permute-start | bytes 393224 | tf_op jit(solution)/shard_map/ppermute | solution.py:537
  15.4 11.9 %copy-start.1 = (bf16[256,512]{1,0:T(8,128)(2,1)S(1)}, bf16[256,512]{1,0:T(8,128)(2,1)}, u32[]{:S(2)}) copy-start(bf16[256,512]{1,0:T(8,128)(2,1)} %values_ref.3) | copy-start | bytes 786436
  15.4 11.9 %copy-start.2 = (bf16[256,512]{1,0:T(8,128)(2,1)S(1)}, bf16[256,512]{1,0:T(8,128)(2,1)}, u32[]{:S(2)}) copy-start(bf16[256,512]{1,0:T(8,128)(2,1)} %queries_ref.1) | copy-start | bytes 786436
  15.4 30.2 %collective-permute-start.9 = (bf16[512,1024]{1,0:T(8,128)(2,1)}, bf16[512,1024]{1,0:T(8,128)(2,1)S(1)}, u32[]{:S(2)}, u32[]{:S(2)}) collective-permute-start(bf16[512,1024]{1,0:T(8,128)(2,1)} %get-tuple-element.48), channel_id=1, source_target_pairs={{0,2},{1,3},{2,0},{3,1},{4,6},{5,7},{6,4},{7,5},{8,10},{9,11},{10,... | collective-permute-start | bytes 3145736 | tf_op jit(solution)/shard_map/ppermute | solution.py:578
  23.4 20.3 %collective-permute-start.5 = (bf16[8,128,128]{2,1,0:T(8,128)(2,1)S(1)}, bf16[8,128,128]{2,1,0:T(8,128)(2,1)S(1)}, u32[]{:S(2)}, u32[]{:S(2)}) collective-permute-start(bf16[8,128,128]{2,1,0:T(8,128)(2,1)S(1)} %get-tuple-element.43), channel_id=1, source_target_pairs={{0,16},{4,20},{8,24},{12,28},{1,17},{5,21},{9,25},{13,29},{2,18},{... | collective-permute-start | bytes 786440 | tf_op jit(solution)/shard_map/ppermute | solution.py:528
  27.7 5.0 %collective-permute-start.2 = (bf16[256,128]{1,0:T(8,128)(2,1)S(1)}, bf16[256,128]{1,0:T(8,128)(2,1)S(1)}, u32[]{:S(2)}, u32[]{:S(2)}) collective-permute-start(bf16[256,128]{1,0:T(8,128)(2,1)S(1)} %get-tuple-element.36), channel_id=1, source_target_pairs={{0,4},{4,0},{8,12},{12,8},{16,20},{20,16},{24,28},{28,24},{1,5},{5... | collective-permute-start | bytes 196616 | tf_op jit(solution)/shard_map/ppermute | solution.py:532
  29.4 16.2 %collective-permute-start.6 = (bf16[3,256,128]{2,1,0:T(8,128)(2,1)S(1)}, bf16[3,256,128]{2,1,0:T(8,128)(2,1)S(1)}, u32[]{:S(2)}, u32[]{:S(2)}) collective-permute-start(bf16[3,256,128]{2,1,0:T(8,128)(2,1)S(1)} %get-tuple-element.45), channel_id=1, source_target_pairs={{0,4},{4,0},{8,12},{12,8},{16,20},{20,16},{24,28},{28,24},{1,5},{5... | collective-permute-start | bytes 589832 | tf_op jit(solution)/shard_map/ppermute | solution.py:532
  29.8 5.9 %collective-permute-start.3 = (bf16[256,128]{1,0:T(8,128)(2,1)S(1)}, bf16[256,128]{1,0:T(8,128)(2,1)S(1)}, u32[]{:S(2)}, u32[]{:S(2)}) collective-permute-start(bf16[256,128]{1,0:T(8,128)(2,1)S(1)} %get-tuple-element.37), channel_id=1, source_target_pairs={{0,8},{4,12},{8,0},{12,4},{16,24},{20,28},{24,16},{28,20},{1,9},{5... | collective-permute-start | bytes 196616 | tf_op jit(solution)/shard_map/ppermute | solution.py:532
  32.7 5.4 %collective-permute-start.4 = (bf16[256,128]{1,0:T(8,128)(2,1)S(1)}, bf16[256,128]{1,0:T(8,128)(2,1)S(1)}, u32[]{:S(2)}, u32[]{:S(2)}) collective-permute-start(bf16[256,128]{1,0:T(8,128)(2,1)S(1)} %get-tuple-element.38), channel_id=1, source_target_pairs={{0,12},{4,8},{8,4},{12,0},{16,28},{20,24},{24,20},{28,16},{1,13},{... | collective-permute-start | bytes 196616 | tf_op jit(solution)/shard_map/ppermute | solution.py:532
  35.6 9.9 %collective-permute-start.7 = (bf16[256,128]{1,0:T(8,128)(2,1)S(1)}, bf16[256,128]{1,0:T(8,128)(2,1)S(1)}, u32[]{:S(2)}, u32[]{:S(2)}) collective-permute-start(bf16[256,128]{1,0:T(8,128)(2,1)S(1)} %get-tuple-element.46), channel_id=1, source_target_pairs={{0,8},{4,12},{8,0},{12,4},{16,24},{20,28},{24,16},{28,20},{1,9},{5... | collective-permute-start | bytes 196616 | tf_op jit(solution)/shard_map/ppermute | solution.py:532
  38.1 7.4 %collective-permute-start.8 = (bf16[256,128]{1,0:T(8,128)(2,1)S(1)}, bf16[256,128]{1,0:T(8,128)(2,1)S(1)}, u32[]{:S(2)}, u32[]{:S(2)}) collective-permute-start(bf16[256,128]{1,0:T(8,128)(2,1)S(1)} %get-tuple-element.47), channel_id=1, source_target_pairs={{0,12},{4,8},{8,4},{12,0},{16,28},{20,24},{24,20},{28,16},{1,13},{... | collective-permute-start | bytes 196616 | tf_op jit(solution)/shard_map/ppermute | solution.py:532
  45.5 12.9 %copy-start = (bf16[512,2048]{1,0:T(8,128)(2,1)S(1)}, bf16[512,2048]{1,0:T(8,128)(2,1)}, u32[]{:S(2)}) copy-start(bf16[512,2048]{1,0:T(8,128)(2,1)} %own_ref.3) | copy-start | bytes 6291460
  58.9 1.6 %collective-permute-start.10 = (bf16[256,512]{1,0:T(8,128)(2,1)S(1)}, bf16[256,512]{1,0:T(8,128)(2,1)S(1)}, u32[]{:S(2)}, u32[]{:S(2)}) collective-permute-start(bf16[256,512]{1,0:T(8,128)(2,1)S(1)} %shard_map.80), channel_id=1, source_target_pairs={{0,1},{1,0},{2,3},{3,2},{4,5},{5,4},{6,7},{7,6},{8,9},{9,8},{10,11... | collective-permute-start | bytes 786440 | tf_op jit(solution)/shard_map/ppermute | solution.py:660

commit v16 on v15

--- a/solution.py
+++ b/solution.py
@@ -72,7 +72,8 @@
     (parts_ref, rates_ref, selected_ref, cut_ref, piece_ref, sems, few_sems, out_sems, cut_sems,
      cut_out_sems, piece_sems) = refs[-11:]
     rounds = heads // 2
-    out_ref, cut_outs, piece_outs = refs[0], refs[1:1 + rounds], refs[1 + rounds:-11]
+    out_ref, cut_outs = refs[0], refs[1:1 + rounds]
+    inner_outs, piece_outs = refs[1 + rounds:rounds + heads - 1], refs[rounds + heads - 1:-11]
     planes = len(piece_outs) + 1
     width = weight_ref.shape[1] // planes
     device = lax.axis_index(axes[0])
@@ -142,8 +143,11 @@
         cut_copies[2 * turn].wait()
         cut_copies[2 * turn + 1].wait()
         out_copies += fetched(
-            [cut_ref.at[turn]], [cut_outs[turn]], cut_out_sems.at[pl.ds(turn, 1)]
+            [cut_ref.at[turn]], [cut_outs[turn]], cut_out_sems.at[0, pl.ds(turn, 1)]
         )
+    out_copies += fetched(
+        [cut_ref.at[turn // 2, turn % 2] for turn in range(2, heads)], inner_outs, cut_out_sems.at[1]
+    )
     for index, copy in enumerate(piece_copies):
         copy.wait()
         out_copies += fetched(
@@ -153,27 +157,19 @@
         copy.wait()
 
 
-def cut_kernel(axes, queries_ref, values_ref, *refs):
-    sems, more_sems = refs[-2:]
-    heads = sems.shape[1]
-    outs = refs[-2 - 2 * heads:-2]
-    come = refs[:-3 - 2 * heads]
+def cut_kernel(axes, heads, count, queries_ref, values_ref, *refs):
+    come, (stay_ref, hand_ref, sems, hand_sems) = refs[:count], refs[-4:]
+    outs = refs[-4 - heads:-4]
     place = lax.rem(lax.axis_index(axes[0]), heads)
     cuts = [
         pl.multiple_of(lax.bitwise_xor(place, turn) * HEAD_DIM, HEAD_DIM) for turn in range(heads)
     ]
-    copies = []
-    for kind, source in enumerate((queries_ref, values_ref)):
-        targets = list(outs[kind * heads:(kind + 1) * heads])
-        if kind:
-            targets[1] = targets[1].at[0]
-        copies += fetched(
-            [source.at[:, pl.ds(cut, HEAD_DIM)] for cut in cuts], targets, sems.at[kind]
-        )
+    copies = fetched([queries_ref.at[:, pl.ds(cut, HEAD_DIM)] for cut in cuts], outs, sems)
     copies += fetched(
-        [part.at[1] for part in come],
-        [outs[heads + 1].at[1 + index] for index in range(len(come))],
-        more_sems,
+        [values_ref.at[:, pl.ds(cut, HEAD_DIM)] for cut in cuts[:2]]
+        + [part.at[1] for part in come],
+        [stay_ref] + [hand_ref.at[index] for index in range(1 + count)],
+        hand_sems,
     )
     for copy in copies:
         copy.wait()
@@ -547,6 +543,7 @@
         functools.partial(pack_kernel, axes, cores),
         [array(part_shape)]
         + [array((2, tokens, HEAD_DIM))] * rounds
+        + [array((tokens, HEAD_DIM))] * (heads - 2)
         + [array(piece_shape)] * (planes - 1),
         [ANY] * 6,
         cubes,
@@ -560,13 +557,15 @@
             pltpu.SemaphoreType.DMA((2,)),
             pltpu.SemaphoreType.DMA((heads,)),
             pltpu.SemaphoreType.DMA((heads,)),
-            pltpu.SemaphoreType.DMA((heads,)),
+            pltpu.SemaphoreType.DMA((2, heads)),
             pltpu.SemaphoreType.DMA((2, planes)),
         ],
-        [ANY] * (rounds + planes),
+        [ANY] * (rounds + heads - 2 + planes),
         56,
     )(directions, keys, rates, selected, values, out_weight)
-    value_cuts, pieces = rest[:rounds], rest[rounds:]
+    value_cuts, inner_cuts = rest[:rounds], rest[rounds:rounds + heads - 2]
+    pieces = rest[rounds + heads - 2:]
+    own_parts = [crossed(part, 2 + index) for index, part in enumerate(inner_cuts)]
     value_parts = [
         straight(value_cuts[turn], turn, by)
         for by in range(1, before + 1)
@@ -595,21 +594,19 @@
     )(parts)
     far_parts = [onward(far, by) for by in range(1, before + 1)]
     map_parts = [onward(group_map, by) for by in range(1, before)]
-    cut = call(
-        functools.partial(cut_kernel, axes),
-        [
-            array((1 + len(value_parts), tokens, HEAD_DIM) if turn == heads + 1 else (tokens, HEAD_DIM))
-            for turn in range(2 * heads)
-        ],
-        [ANY] * (len(value_parts) + 3),
+    *cut, stay, hand = call(
+        functools.partial(cut_kernel, axes, heads, len(value_parts)),
+        [array((tokens, HEAD_DIM))] * (heads + 1)
+        + [array((1 + len(value_parts), tokens, HEAD_DIM))],
+        [ANY] * (2 + len(value_parts) + len(own_parts) + 1),
         2000 * cubes,
         [
-            pltpu.SemaphoreType.DMA((2, heads)),
-            pltpu.SemaphoreType.DMA((max(len(value_parts), 1),)),
+            pltpu.SemaphoreType.DMA((heads,)),
+            pltpu.SemaphoreType.DMA((2 + len(value_parts),)),
         ],
-    )(queries, values, *value_parts, away)
+    )(queries, values, *value_parts, *own_parts, away)
     query_parts = [crossed(cut[turn], turn) for turn in range(heads)]
-    own_parts = [crossed(cut[heads + turn], turn) for turn in range(heads)]
+    own_parts = [stay, crossed(hand, 1), *own_parts]
     inner, moving = call(
         functools.partial(queries_kernel, axes, blocks),
         [array((units, BLOCK, BLOCK), F32), array((units, pairs + 1, *tile))],

time: 61.5 us -> 63.8 us (1.037)
  waiting for transfers between devices: 3.68 us -> 6.68 us
  starting transfers between devices: 29 us -> 26.3 us
  blocking collectives: 10.9 us -> 12.9 us
    ppermute x6, waiting for transfers between devices: 2.59 us -> 5.59 us  [crossed(): return lax.ppermute(value, 'ctx', pairs) if turn else value]
    all_to_all x1, blocking collectives: 10.9 us -> 12.9 us  [body(): lax.all_to_all(attended.reshape(heads * planes, blocks, *tile), axes, 0,...]
    ppermute x1, starting transfers between devices: 3.85 us -> 2.33 us  [onward(): lax.ppermute(value, 'ctx', [(i, i + shift) for i in range(ctx_size - shif...]
    ppermute x6, starting transfers between devices: 11 us -> 10.4 us  [crossed(): return lax.ppermute(value, 'ctx', pairs) if turn else value]
  transfers between devices with their start and end apart: 12 -> 12, of which waited for: 3 -> 3; matrix products, arithmetic and copies ran while one was open for 0% -> 0% of each run, Pallas kernels for 19% -> 18%
where the time goes in v16:
time: 63.8 us; the launch traced here: 63.5 us
  starting transfers between devices  26.3 us (41%)
  Pallas kernels  16.7 us (26%)
  blocking collectives  12.9 us (20%)
  waiting for transfers between devices  6.68 us (10%)
  other arithmetic  0.78 us (1%)
    all_to_all x1, blocking collectives, body(): lax.all_to_all(attended.reshape(heads * planes, blocks, *tile), axes, 0,...  12.9 us
    ppermute x6, starting transfers between devices, crossed(): return lax.ppermute(value, 'ctx', pairs) if turn else value  10.4 us
    ppermute x2, starting transfers between devices, straight(): return lax.ppermute(value, 'ctx', pairs)  6.68 us
    pallas_call x1, Pallas kernels, body(): call(functools.partial(keys_kernel, blocks), [array((units, *tile)), arra...  6.44 us
    ppermute x6, waiting for transfers between devices, crossed(): return lax.ppermute(value, 'ctx', pairs) if turn else value  5.59 us
    all_to_all x1, starting transfers between devices, exchange(): lax.all_to_all(value, 'ctx', 0, 0, axis_index_groups=members, tiled=True)  5.26 us
    pallas_call x1, Pallas kernels, body(): call(functools.partial(pack_kernel, axes, cores), [array(part_shape)] + [...  2.87 us
    pallas_call x1, Pallas kernels, body(): call(functools.partial(queries_kernel, axes, blocks), [array((units, BLOC...  2.37 us
  transfers between devices with their start and end apart: 12, of which 3 were waited for; matrix products, arithmetic and copies ran while one was open for 0% of the time, Pallas kernels for 18%

profile of v16, /device:TPU:0, one launch (start us, length us, event | category | flops | bytes accessed | tf_op | source)
XLA Modules:
  0.0 63.5 jit_solution(5574445188567948809)
XLA Ops:
  0.0 2.9 %shard_map.73 = (bf16[4,528,128]{2,1,0:T(8,128)(2,1)}, bf16[2,256,128]{2,1,0:T(8,128)(2,1)}, bf16[2,256,128]{2,1,0:T(8,128)(2,1)}, bf16[256,128]{1,0:T(8,128)(2,...) custom-call(bf16[256,512]{1,0:T(8,128)(2,1)} %d_ref.1, bf16[256,512]{1,0:T(8,128)(2,1)} %k_ref.1, ...), custom_call_target="tpu_custom_call" | custom-call | flops 4194304 | bytes 2097152 | tf_op jit(solution)/shard_map/pallas_call | solution.py:542
  2.9 5.3 %all-to-all-start = ((bf16[4,528,128]{2,1,0:T(8,128)(2,1)}), bf16[4,528,128]{2,1,0:T(8,128)(2,1)S(1)}, u32[]{:S(2)}, u32[]{:S(2)}) async-start(bf16[4,528,128]{2,1,0:T(8,128)(2,1)} %get-tuple-element.28), calls=%async_computation | async-start | bytes 1081344 | tf_op jit(solution)/shard_map/all_to_all | solution.py:520
  8.1 2.0 %collective-permute-start.2 = (bf16[256,128]{1,0:T(8,128)(2,1)}, bf16[256,128]{1,0:T(8,128)(2,1)S(1)}, u32[]{:S(2)}, u32[]{:S(2)}) collective-permute-start(bf16[256,128]{1,0:T(8,128)(2,1)} %get-tuple-element.35), channel_id=1, source_target_pairs={{0,8},{4,12},{8,0},{12,4},{16,24},{20,28},{24,16},{28,20},{1,9},{5... | collective-permute-start | bytes 196616 | tf_op jit(solution)/shard_map/ppermute | solution.py:528
  10.2 1.5 %collective-permute-start.3 = (bf16[256,128]{1,0:T(8,128)(2,1)}, bf16[256,128]{1,0:T(8,128)(2,1)S(1)}, u32[]{:S(2)}, u32[]{:S(2)}) collective-permute-start(bf16[256,128]{1,0:T(8,128)(2,1)} %get-tuple-element.36), channel_id=1, source_target_pairs={{0,12},{4,8},{8,4},{12,0},{16,28},{20,24},{24,20},{28,16},{1,13},{... | collective-permute-start | bytes 196616 | tf_op jit(solution)/shard_map/ppermute | solution.py:528
  11.6 4.5 %collective-permute-start = (bf16[2,256,128]{2,1,0:T(8,128)(2,1)}, bf16[2,256,128]{2,1,0:T(8,128)(2,1)S(1)}, u32[]{:S(2)}, u32[]{:S(2)}) collective-permute-start(bf16[2,256,128]{2,1,0:T(8,128)(2,1)} %get-tuple-element.33), channel_id=1, source_target_pairs={{0,16},{4,20},{8,24},{12,28},{1,17},{5,21},{9,25},{13,29},{2,18},{... | collective-permute-start | bytes 393224 | tf_op jit(solution)/shard_map/ppermute | solution.py:533
  16.1 2.2 %collective-permute-start.1 = (bf16[2,256,128]{2,1,0:T(8,128)(2,1)}, bf16[2,256,128]{2,1,0:T(8,128)(2,1)S(1)}, u32[]{:S(2)}, u32[]{:S(2)}) collective-permute-start(bf16[2,256,128]{2,1,0:T(8,128)(2,1)} %get-tuple-element.34), channel_id=1, source_target_pairs={{0,24},{4,28},{8,16},{12,20},{1,25},{5,29},{9,17},{13,21},{2,26},{... | collective-permute-start | bytes 393224 | tf_op jit(solution)/shard_map/ppermute | solution.py:533
  18.4 1.6 %collective-permute-start.9 = (bf16[512,1024]{1,0:T(8,128)(2,1)}, bf16[512,1024]{1,0:T(8,128)(2,1)S(1)}, u32[]{:S(2)}, u32[]{:S(2)}) collective-permute-start(bf16[512,1024]{1,0:T(8,128)(2,1)} %get-tuple-element.48), channel_id=1, source_target_pairs={{0,2},{1,3},{2,0},{3,1},{4,6},{5,7},{6,4},{7,5},{8,10},{9,11},{10,... | collective-permute-start | bytes 3145736 | tf_op jit(solution)/shard_map/ppermute | solution.py:577
  19.9 6.4 %shard_map.74 = (bf16[8,128,128]{2,1,0:T(8,128)(2,1)S(1)}, bf16[8,128,128]{2,1,0:T(8,128)(2,1)S(1)}, bf16[8,128,128]{2,1,0:T(8,128)(2,1)S(1)}, bf16[4,2,128,128]...) custom-call(bf16[4,528,128]{2,1,0:T(8,128)(2,1)S(1)} %all-to-all-don, ...), custom_call_target="tpu_custom_call" | custom-call | flops 1677721600 | bytes 2097152 | tf_op jit(solution)/shard_map/pallas_call | solution.py:580
  26.4 2.3 %collective-permute-start.7 = (bf16[8,128,128]{2,1,0:T(8,128)(2,1)S(1)}, bf16[8,128,128]{2,1,0:T(8,128)(2,1)S(1)}, u32[]{:S(2)}, u32[]{:S(2)}) collective-permute-start(bf16[8,128,128]{2,1,0:T(8,128)(2,1)S(1)} %get-tuple-element.45), channel_id=1, source_target_pairs={{0,16},{4,20},{8,24},{12,28},{1,17},{5,21},{9,25},{13,29},{2,18},{... | collective-permute-start | bytes 786440 | tf_op jit(solution)/shard_map/ppermute | solution.py:524
  28.7 0.3 shard_map.75
  29.1 1.5 %collective-permute-start.8 = (bf16[3,256,128]{2,1,0:T(8,128)(2,1)S(1)}, bf16[3,256,128]{2,1,0:T(8,128)(2,1)S(1)}, u32[]{:S(2)}, u32[]{:S(2)}) collective-permute-start(bf16[3,256,128]{2,1,0:T(8,128)(2,1)S(1)} %get-tuple-element.47), channel_id=1, source_target_pairs={{0,4},{4,0},{8,12},{12,8},{16,20},{20,16},{24,28},{28,24},{1,5},{5... | collective-permute-start | bytes 589832 | tf_op jit(solution)/shard_map/ppermute | solution.py:528
  30.6 0.6 collective-permute-start.4
  31.2 1.7 %collective-permute-start.5 = (bf16[256,128]{1,0:T(8,128)(2,1)S(1)}, bf16[256,128]{1,0:T(8,128)(2,1)S(1)}, u32[]{:S(2)}, u32[]{:S(2)}) collective-permute-start(bf16[256,128]{1,0:T(8,128)(2,1)S(1)} %get-tuple-element.39), channel_id=1, source_target_pairs={{0,8},{4,12},{8,0},{12,4},{16,24},{20,28},{24,16},{28,20},{1,9},{5... | collective-permute-start | bytes 196616 | tf_op jit(solution)/shard_map/ppermute | solution.py:528
  32.9 3.3 %collective-permute-done.4.refs_1_ = bf16[256,128]{1,0:T(8,128)(2,1)S(1)} collective-permute-done((bf16[256,128]{1,0:T(8,128)(2,1)S(1)}, bf16[256,128]{1,0:T(8,128)(2,1)S(1)}, u32[]{:S(2)}, u32[]{:S(2)}) %collective-permute-start.4) | collective-permute-done | bytes 65568 | tf_op jit(solution)/shard_map/ppermute | solution.py:528
  36.2 3.1 %collective-permute-start.6 = (bf16[256,128]{1,0:T(8,128)(2,1)S(1)}, bf16[256,128]{1,0:T(8,128)(2,1)S(1)}, u32[]{:S(2)}, u32[]{:S(2)}) collective-permute-start(bf16[256,128]{1,0:T(8,128)(2,1)S(1)} %get-tuple-element.40), channel_id=1, source_target_pairs={{0,12},{4,8},{8,4},{12,0},{16,28},{20,24},{24,20},{28,16},{1,13},{... | collective-permute-start | bytes 196616 | tf_op jit(solution)/shard_map/ppermute | solution.py:528
  39.3 2.2 %collective-permute-done.6.refs_3_ = bf16[256,128]{1,0:T(8,128)(2,1)S(1)} collective-permute-done((bf16[256,128]{1,0:T(8,128)(2,1)S(1)}, bf16[256,128]{1,0:T(8,128)(2,1)S(1)}, u32[]{:S(2)}, u32[]{:S(2)}) %collective-permute-start.6) | collective-permute-done | bytes 65568 | tf_op jit(solution)/shard_map/ppermute | solution.py:528
  41.6 2.4 %shard_map.76 = (f32[8,128,128]{2,1,0:T(8,128)S(1)}, bf16[8,5,128,128]{3,2,1,0:T(8,128)(2,1)S(1)}) custom-call(bf16[4,528,128]{2,1,0:T(8,128)(2,1)S(1)} %all-to-all-done.part_ref, bf16[8,128,256]{2,1,0:T(8,128)(2,1)S(1)} %get-tuple-element.30.mixed_ref, bf16[4,2,128,128]{3,2,1,0:T(8,128)(2,1)S(1)} %get-tuple-element.31.even_ref, ...), custom_call_target="tpu_custom_call" | custom-call | bytes 2097152 | tf_op jit(solution)/shard_map/pallas_call | solution.py:610
  44.0 1.8 %shard_map.77.weights_ref = bf16[8,128,512]{2,1,0:T(8,128)(2,1)S(1)} custom-call(s32[8,128]{1,0:T(8,128)S(1)} %get-tuple-element.29.refs_4_.away_ref, bf16[8,5,128,128]{3,2,1,0:T(8,128)(2,1)S(1)} %get-tuple-element.41.moving_ref, f32[8,128,128]{2,1,0:T(8,128)S(1)} %get-tuple-element.42.inner_ref, bf16[8,128,128]{2,1,0:T(8,128)(2,1)S(1)} %get-tuple-element.43.end_ref, ...), custom_call_target="tpu_custom_call" | custom-call | bytes 2097152 | tf_op jit(solution)/shard_map/pallas_call | solution.py:617
  45.8 1.9 %shard_map.78 = (bf16[4,2,2,128,128]{4,3,2,1,0:T(8,128)(2,1)S(1)}, bf16[512,1024]{1,0:T(8,128)(2,1)S(1)}) custom-call(s32[8,128]{1,0:T(8,128)S(1)} %get-tuple-element.29.refs_4_.away_ref, bf16[8,128,512]{2,1,0:T(8,128)(2,1)S(1)} %shard_map.77.weights_ref, bf16[256,128]{1,0:T(8,128)(2,1)S(1)} %get-tuple-element.46.refs_0_, ...), custom_call_target="tpu_custom_call" | custom-call | bytes 2097152 | tf_op jit(solution)/shard_map/pallas_call | solution.py:623
  47.8 12.9 %all_to_all.10 = bf16[8,2,128,128]{3,2,1,0:T(8,128)(2,1)S(1)} all-to-all(bf16[8,2,128,128]{3,2,1,0:T(8,128)(2,1)S(1)} %bitcast.4), channel_id=1, replica_groups={{0,2,4,6,8,10,12,14},{1,3,5,7,9,11,13,15},{16,18,20,22,24,26,28,30},{17..., dimensions={0} | all-to-all | bytes 1048576 | tf_op jit(solution)/shard_map/all_to_all | solution.py:644
  60.7 0.4 shard_map.80
  61.2 0.4 shard_map.79
  61.7 1.1 %collective-permute-done.10 = bf16[256,512]{1,0:T(8,128)(2,1)S(1)} collective-permute-done((bf16[256,512]{1,0:T(8,128)(2,1)S(1)}, bf16[256,512]{1,0:T(8,128)(2,1)S(1)}, u32[]{:S(2)}, u32[]{:S(2)}) %collective-permute-start.10) | collective-permute-done | bytes 262176 | tf_op jit(solution)/shard_map/ppermute | solution.py:657
  62.8 0.8 %add_convert_fusion = bf16[256,512]{1,0:T(8,128)(2,1)} fusion(f32[256,512]{1,0:T(8,128)S(1)} %shard_map.79, bf16[256,512]{1,0:T(8,128)(2,1)S(1)} %collective-permute-done.10), kind=kLoop, calls=%fused_computation | loop fusion | flops 393216 | bytes 1048576 | tf_op jit(solution)/shard_map/convert_element_type | solution.py:658
  (16 shorter events, 0.1 us)
Async XLA Ops:
  2.9 17.0 %all-to-all-start = ((bf16[4,528,128]{2,1,0:T(8,128)(2,1)}), bf16[4,528,128]{2,1,0:T(8,128)(2,1)S(1)}, u32[]{:S(2)}, u32[]{:S(2)}) async-start(bf16[4,528,128]{2,1,0:T(8,128)(2,1)} %get-tuple-element.28), calls=%async_computation | async-start | bytes 1081344 | tf_op jit(solution)/shard_map/all_to_all | solution.py:520
  8.1 18.2 %collective-permute-start.2 = (bf16[256,128]{1,0:T(8,128)(2,1)}, bf16[256,128]{1,0:T(8,128)(2,1)S(1)}, u32[]{:S(2)}, u32[]{:S(2)}) collective-permute-start(bf16[256,128]{1,0:T(8,128)(2,1)} %get-tuple-element.35), channel_id=1, source_target_pairs={{0,8},{4,12},{8,0},{12,4},{16,24},{20,28},{24,16},{28,20},{1,9},{5... | collective-permute-start | bytes 196616 | tf_op jit(solution)/shard_map/ppermute | solution.py:528
  10.2 18.5 %collective-permute-start.3 = (bf16[256,128]{1,0:T(8,128)(2,1)}, bf16[256,128]{1,0:T(8,128)(2,1)S(1)}, u32[]{:S(2)}, u32[]{:S(2)}) collective-permute-start(bf16[256,128]{1,0:T(8,128)(2,1)} %get-tuple-element.36), channel_id=1, source_target_pairs={{0,12},{4,8},{8,4},{12,0},{16,28},{20,24},{24,20},{28,16},{1,13},{... | collective-permute-start | bytes 196616 | tf_op jit(solution)/shard_map/ppermute | solution.py:528
  11.6 17.1 %collective-permute-start = (bf16[2,256,128]{2,1,0:T(8,128)(2,1)}, bf16[2,256,128]{2,1,0:T(8,128)(2,1)S(1)}, u32[]{:S(2)}, u32[]{:S(2)}) collective-permute-start(bf16[2,256,128]{2,1,0:T(8,128)(2,1)} %get-tuple-element.33), channel_id=1, source_target_pairs={{0,16},{4,20},{8,24},{12,28},{1,17},{5,21},{9,25},{13,29},{2,18},{... | collective-permute-start | bytes 393224 | tf_op jit(solution)/shard_map/ppermute | solution.py:533
  16.1 12.6 %collective-permute-start.1 = (bf16[2,256,128]{2,1,0:T(8,128)(2,1)}, bf16[2,256,128]{2,1,0:T(8,128)(2,1)S(1)}, u32[]{:S(2)}, u32[]{:S(2)}) collective-permute-start(bf16[2,256,128]{2,1,0:T(8,128)(2,1)} %get-tuple-element.34), channel_id=1, source_target_pairs={{0,24},{4,28},{8,16},{12,20},{1,25},{5,29},{9,17},{13,21},{2,26},{... | collective-permute-start | bytes 393224 | tf_op jit(solution)/shard_map/ppermute | solution.py:533
  18.3 10.4 %copy-start.1 = (bf16[256,512]{1,0:T(8,128)(2,1)S(1)}, bf16[256,512]{1,0:T(8,128)(2,1)}, u32[]{:S(2)}) copy-start(bf16[256,512]{1,0:T(8,128)(2,1)} %values_ref.3) | copy-start | bytes 786436
  18.3 10.4 %copy-start.2 = (bf16[256,512]{1,0:T(8,128)(2,1)S(1)}, bf16[256,512]{1,0:T(8,128)(2,1)}, u32[]{:S(2)}) copy-start(bf16[256,512]{1,0:T(8,128)(2,1)} %queries_ref.1) | copy-start | bytes 786436
  18.4 27.5 %collective-permute-start.9 = (bf16[512,1024]{1,0:T(8,128)(2,1)}, bf16[512,1024]{1,0:T(8,128)(2,1)S(1)}, u32[]{:S(2)}, u32[]{:S(2)}) collective-permute-start(bf16[512,1024]{1,0:T(8,128)(2,1)} %get-tuple-element.48), channel_id=1, source_target_pairs={{0,2},{1,3},{2,0},{3,1},{4,6},{5,7},{6,4},{7,5},{8,10},{9,11},{10,... | collective-permute-start | bytes 3145736 | tf_op jit(solution)/shard_map/ppermute | solution.py:577
  26.4 17.6 %collective-permute-start.7 = (bf16[8,128,128]{2,1,0:T(8,128)(2,1)S(1)}, bf16[8,128,128]{2,1,0:T(8,128)(2,1)S(1)}, u32[]{:S(2)}, u32[]{:S(2)}) collective-permute-start(bf16[8,128,128]{2,1,0:T(8,128)(2,1)S(1)} %get-tuple-element.45), channel_id=1, source_target_pairs={{0,16},{4,20},{8,24},{12,28},{1,17},{5,21},{9,25},{13,29},{2,18},{... | collective-permute-start | bytes 786440 | tf_op jit(solution)/shard_map/ppermute | solution.py:524
  29.1 16.7 %collective-permute-start.8 = (bf16[3,256,128]{2,1,0:T(8,128)(2,1)S(1)}, bf16[3,256,128]{2,1,0:T(8,128)(2,1)S(1)}, u32[]{:S(2)}, u32[]{:S(2)}) collective-permute-start(bf16[3,256,128]{2,1,0:T(8,128)(2,1)S(1)} %get-tuple-element.47), channel_id=1, source_target_pairs={{0,4},{4,0},{8,12},{12,8},{16,20},{20,16},{24,28},{28,24},{1,5},{5... | collective-permute-start | bytes 589832 | tf_op jit(solution)/shard_map/ppermute | solution.py:528
  30.6 5.6 %collective-permute-start.4 = (bf16[256,128]{1,0:T(8,128)(2,1)S(1)}, bf16[256,128]{1,0:T(8,128)(2,1)S(1)}, u32[]{:S(2)}, u32[]{:S(2)}) collective-permute-start(bf16[256,128]{1,0:T(8,128)(2,1)S(1)} %get-tuple-element.38), channel_id=1, source_target_pairs={{0,4},{4,0},{8,12},{12,8},{16,20},{20,16},{24,28},{28,24},{1,5},{5... | collective-permute-start | bytes 196616 | tf_op jit(solution)/shard_map/ppermute | solution.py:528
  31.2 8.1 %collective-permute-start.5 = (bf16[256,128]{1,0:T(8,128)(2,1)S(1)}, bf16[256,128]{1,0:T(8,128)(2,1)S(1)}, u32[]{:S(2)}, u32[]{:S(2)}) collective-permute-start(bf16[256,128]{1,0:T(8,128)(2,1)S(1)} %get-tuple-element.39), channel_id=1, source_target_pairs={{0,8},{4,12},{8,0},{12,4},{16,24},{20,28},{24,16},{28,20},{1,9},{5... | collective-permute-start | bytes 196616 | tf_op jit(solution)/shard_map/ppermute | solution.py:528
  36.2 5.3 %collective-permute-start.6 = (bf16[256,128]{1,0:T(8,128)(2,1)S(1)}, bf16[256,128]{1,0:T(8,128)(2,1)S(1)}, u32[]{:S(2)}, u32[]{:S(2)}) collective-permute-start(bf16[256,128]{1,0:T(8,128)(2,1)S(1)} %get-tuple-element.40), channel_id=1, source_target_pairs={{0,12},{4,8},{8,4},{12,0},{16,28},{20,24},{24,20},{28,16},{1,13},{... | collective-permute-start | bytes 196616 | tf_op jit(solution)/shard_map/ppermute | solution.py:528
  45.8 14.9 %copy-start = (bf16[512,2048]{1,0:T(8,128)(2,1)S(1)}, bf16[512,2048]{1,0:T(8,128)(2,1)}, u32[]{:S(2)}) copy-start(bf16[512,2048]{1,0:T(8,128)(2,1)} %own_ref.3) | copy-start | bytes 6291460
  61.2 1.6 %collective-permute-start.10 = (bf16[256,512]{1,0:T(8,128)(2,1)S(1)}, bf16[256,512]{1,0:T(8,128)(2,1)S(1)}, u32[]{:S(2)}, u32[]{:S(2)}) collective-permute-start(bf16[256,512]{1,0:T(8,128)(2,1)S(1)} %shard_map.80), channel_id=1, source_target_pairs={{0,1},{1,0},{2,3},{3,2},{4,5},{5,4},{6,7},{7,6},{8,9},{9,8},{10,11... | collective-permute-start | bytes 786440 | tf_op jit(solution)/shard_map/ppermute | solution.py:657

commit v17 on v14

--- a/solution.py
+++ b/solution.py
@@ -224,8 +224,8 @@
         tick += 1
 
 
-def keys_kernel(blocks, part_ref, end_ref, tail_ref, far_ref, even_ref, pair_ref, group_ref,
-                mixed_ref, away_ref):
+def keys_kernel(blocks, part_ref, end_ref, tail_ref, far_ref, even_ref, pair_ref, mixed_ref,
+                away_ref, *group_refs):
     units = part_ref.shape[0] * blocks
     rows, columns = square_iotas()
     diagonal = rows == columns
@@ -266,11 +266,12 @@
             size *= 2
             yield
         mixing = split(scale_column * inverse * scaled_rate)
-        mixed = nn(jnp.concatenate(mixing, 0), jnp.concatenate([direction, key_proj], 1))
-        mixed = split(mixed[:BLOCK] + mixed[BLOCK:])
-        mixed_ref[unit] = mixed[0]
+        mixed = nn(mixing[0], jnp.concatenate([direction, key_proj], 1))
+        mixed_map = split(mixed[:, :BLOCK] + nn(mixing[1], direction))
+        mixed = jnp.concatenate([mixed_map[0], mixed[:, BLOCK:].astype(BF16)], 1)
+        mixed_ref[unit] = mixed
         yield
-        behind = tn(jnp.concatenate([mixed[0], mixed[1][:, :BLOCK]], 1), direction)
+        behind = tn(jnp.concatenate([mixed, mixed_map[1]], 1), direction)
         ends[unit] = key.astype(F32) - behind[BLOCK:2 * BLOCK]
         maps[unit] = split(identity - (behind[:BLOCK] + behind[2 * BLOCK:]))
         end_ref[unit] = ends[unit].astype(BF16)
@@ -301,15 +302,17 @@
             far = nn(jnp.concatenate([tail_even, tail_odd], 0), onward[-1][0]).astype(BF16)
             far_ref[even] = far[:BLOCK]
             far_ref[odd] = far[BLOCK:]
-            pair_map = split(triple(nn, pair_map, onward[-1]))
+            if pair or group_refs:
+                pair_map = split(triple(nn, pair_map, onward[-1]))
         else:
             far_ref[even] = tail_even
             far_ref[odd] = tail_odd
         onward.append(pair_map)
 
     interleaved([pair_terms(pair) for pair in reversed(range(units // 2))], 1)
-    group_ref[0] = onward[-1][0]
-    group_ref[1] = onward[-1][1]
+    for group_ref in group_refs:
+        group_ref[0] = onward[-1][0]
+        group_ref[1] = onward[-1][1]
 
 
 def queries_kernel(axes, blocks, part_ref, mixed_ref, even_ref, pair_ref, *refs):
@@ -396,7 +399,7 @@
         yield
         scores = jnp.concatenate(score_list, 1)
         expos = jnp.exp(scores - jnp.max(scores, 1, keepdims=True))
-        weights_ref[unit] = (expos / jnp.sum(expos, 1, keepdims=True)).astype(BF16)
+        weights_ref[unit] = (expos * (1.0 / jnp.sum(expos, 1, keepdims=True))).astype(BF16)
 
     interleaved([steps(unit) for unit in range(units)], 1)
 
@@ -557,7 +560,7 @@
         weight_parts.append(lax.ppermute(pieces[offset - 1], "head", turned))
     parts = exchange(packed)
 
-    end, tail, far, even, pair_map, group_map, mixed, away = call(
+    end, tail, far, even, pair_map, mixed, away, *group_maps = call(
         functools.partial(keys_kernel, blocks),
         [
             array((units, *tile)),
@@ -565,15 +568,15 @@
             array((units, *tile)),
             array((pairs, 2, *tile)),
             array((pairs, 2, *tile)),
-            array((2, *tile)),
             array((units, BLOCK, 2 * BLOCK)),
             array((units, HEAD_DIM), jnp.int32),
-        ],
+        ]
+        + [array((2, *tile))] * (before > 1),
         [VMEM],
         400 * cubes,
     )(parts)
     far_parts = [onward(far, by) for by in range(1, before + 1)]
-    map_parts = [onward(group_map, by) for by in range(1, before)]
+    map_parts = [onward(group_maps[0], by) for by in range(1, before)]
     cut = call(
         functools.partial(cut_kernel, axes),
         [array((tokens, HEAD_DIM))] * (2 * heads),

time: 59.6 us -> 59 us (0.990)
  Pallas kernels: 16.5 us -> 15.9 us
    pallas_call x1, Pallas kernels: 6.45 us -> 5.82 us  [body(): call(functools.partial(keys_kernel, blocks), [array((units, *tile)), arra...]
  transfers between devices with their start and end apart: 14 -> 14, of which waited for: 3 -> 3; matrix products, arithmetic and copies ran while one was open for 0% -> 0% of each run, Pallas kernels for 19% -> 18%
where the time goes in v17:
time: 59 us; the launch traced here: 58.7 us
  starting transfers between devices  27.2 us (46%)
  Pallas kernels  15.9 us (27%)
  blocking collectives  10.4 us (18%)
  waiting for transfers between devices  4.12 us (7%)
  other arithmetic  0.77 us (1%)
    ppermute x4, starting transfers between devices, straight(): return lax.ppermute(value, 'ctx', pairs)  10.7 us
    all_to_all x1, blocking collectives, body(): lax.all_to_all(attended.reshape(heads * planes, blocks, *tile), axes, 0,...  10.4 us
    ppermute x6, starting transfers between devices, crossed(): return lax.ppermute(value, 'ctx', pairs) if turn else value  8.29 us
    pallas_call x1, Pallas kernels, body(): call(functools.partial(keys_kernel, blocks), [array((units, *tile)), arra...  5.82 us
    all_to_all x1, starting transfers between devices, exchange(): lax.all_to_all(value, 'ctx', 0, 0, axis_index_groups=members, tiled=True)  5.26 us
    ppermute x6, waiting for transfers between devices, crossed(): return lax.ppermute(value, 'ctx', pairs) if turn else value  3.03 us
    pallas_call x1, Pallas kernels, body(): call(functools.partial(pack_kernel, axes, cores), [array(part_shape)] + [...  2.85 us
    pallas_call x1, Pallas kernels, body(): call(functools.partial(queries_kernel, axes, blocks), [array((units, BLOC...  2.37 us
  transfers between devices with their start and end apart: 14, of which 3 were waited for; matrix products, arithmetic and copies ran while one was open for 0% of the time, Pallas kernels for 18%

profile of v17, /device:TPU:0, one launch (start us, length us, event | category | flops | bytes accessed | tf_op | source)
XLA Modules:
  0.0 58.7 jit_solution(1311560455664246094)
XLA Ops:
  0.0 2.8 %shard_map.73 = (bf16[4,528,128]{2,1,0:T(8,128)(2,1)}, bf16[256,128]{1,0:T(8,128)(2,1)}, bf16[256,128]{1,0:T(8,128)(2,1)}, bf16[256,128]{1,0:T(8,128)(2,1)}, bf1...) custom-call(bf16[256,512]{1,0:T(8,128)(2,1)} %d_ref.1, bf16[256,512]{1,0:T(8,128)(2,1)} %k_ref.1, f32[4,256]{1,0:T(4,128)} %rates_hbm.1, ...), custom_call_target="tpu_custom_call" | custom-call | flops 4194304 | bytes 2097152 | tf_op jit(solution)/shard_map/pallas_call | solution.py:530
  2.9 5.3 %all-to-all-start = ((bf16[4,528,128]{2,1,0:T(8,128)(2,1)}), bf16[4,528,128]{2,1,0:T(8,128)(2,1)S(1)}, u32[]{:S(2)}, u32[]{:S(2)}) async-start(bf16[4,528,128]{2,1,0:T(8,128)(2,1)} %get-tuple-element.30), calls=%async_computation | async-start | bytes 1081344 | tf_op jit(solution)/shard_map/all_to_all | solution.py:509
  8.1 4.5 %collective-permute-start = (bf16[256,128]{1,0:T(8,128)(2,1)}, bf16[256,128]{1,0:T(8,128)(2,1)S(1)}, u32[]{:S(2)}, u32[]{:S(2)}) collective-permute-start(bf16[256,128]{1,0:T(8,128)(2,1)} %get-tuple-element.35), channel_id=1, source_target_pairs={{0,16},{4,20},{8,24},{12,28},{1,17},{5,21},{9,25},{13,29},{2,18},{... | collective-permute-start | bytes 196616 | tf_op jit(solution)/shard_map/ppermute | solution.py:522
  12.6 2.8 %collective-permute-start.1 = (bf16[256,128]{1,0:T(8,128)(2,1)}, bf16[256,128]{1,0:T(8,128)(2,1)S(1)}, u32[]{:S(2)}, u32[]{:S(2)}) collective-permute-start(bf16[256,128]{1,0:T(8,128)(2,1)} %get-tuple-element.36), channel_id=1, source_target_pairs={{0,20},{4,16},{8,28},{12,24},{1,21},{5,17},{9,29},{13,25},{2,22},{... | collective-permute-start | bytes 196616 | tf_op jit(solution)/shard_map/ppermute | solution.py:522
  15.4 1.3 %collective-permute-start.2 = (bf16[256,128]{1,0:T(8,128)(2,1)}, bf16[256,128]{1,0:T(8,128)(2,1)S(1)}, u32[]{:S(2)}, u32[]{:S(2)}) collective-permute-start(bf16[256,128]{1,0:T(8,128)(2,1)} %get-tuple-element.37), channel_id=1, source_target_pairs={{0,24},{4,28},{8,16},{12,20},{1,25},{5,29},{9,17},{13,21},{2,26},{... | collective-permute-start | bytes 196616 | tf_op jit(solution)/shard_map/ppermute | solution.py:522
  16.7 2.2 %collective-permute-start.3 = (bf16[256,128]{1,0:T(8,128)(2,1)}, bf16[256,128]{1,0:T(8,128)(2,1)S(1)}, u32[]{:S(2)}, u32[]{:S(2)}) collective-permute-start(bf16[256,128]{1,0:T(8,128)(2,1)} %get-tuple-element.38), channel_id=1, source_target_pairs={{0,28},{4,24},{8,20},{12,16},{1,29},{5,25},{9,21},{13,17},{2,30},{... | collective-permute-start | bytes 196616 | tf_op jit(solution)/shard_map/ppermute | solution.py:522
  18.9 1.6 %collective-permute-start.11 = (bf16[512,1024]{1,0:T(8,128)(2,1)}, bf16[512,1024]{1,0:T(8,128)(2,1)S(1)}, u32[]{:S(2)}, u32[]{:S(2)}) collective-permute-start(bf16[512,1024]{1,0:T(8,128)(2,1)} %get-tuple-element.52), channel_id=1, source_target_pairs={{0,2},{1,3},{2,0},{3,1},{4,6},{5,7},{6,4},{7,5},{8,10},{9,11},{10,... | collective-permute-start | bytes 3145736 | tf_op jit(solution)/shard_map/ppermute | solution.py:560
  20.5 5.8 %shard_map.74 = (bf16[8,128,128]{2,1,0:T(8,128)(2,1)S(1)}, bf16[8,128,128]{2,1,0:T(8,128)(2,1)S(1)}, bf16[8,128,128]{2,1,0:T(8,128)(2,1)S(1)}, bf16[4,2,128,128]...) custom-call(bf16[4,528,128]{2,1,0:T(8,128)(2,1)S(1)} %all-to-all-don, ...), custom_call_target="tpu_custom_call" | custom-call | flops 1677721600 | bytes 2097152 | tf_op jit(solution)/shard_map/pallas_call | solution.py:563
  26.3 1.3 %collective-permute-start.7 = (bf16[8,128,128]{2,1,0:T(8,128)(2,1)S(1)}, bf16[8,128,128]{2,1,0:T(8,128)(2,1)S(1)}, u32[]{:S(2)}, u32[]{:S(2)}) collective-permute-start(bf16[8,128,128]{2,1,0:T(8,128)(2,1)S(1)} %get-tuple-element.47), channel_id=1, source_target_pairs={{0,16},{4,20},{8,24},{12,28},{1,17},{5,21},{9,25},{13,29},{2,18},{... | collective-permute-start | bytes 786440 | tf_op jit(solution)/shard_map/ppermute | solution.py:513
  27.9 0.6 %collective-permute-start.4 = (bf16[256,128]{1,0:T(8,128)(2,1)S(1)}, bf16[256,128]{1,0:T(8,128)(2,1)S(1)}, u32[]{:S(2)}, u32[]{:S(2)}) collective-permute-start(bf16[256,128]{1,0:T(8,128)(2,1)S(1)} %get-tuple-element.40), channel_id=1, source_target_pairs={{0,4},{4,0},{8,12},{12,8},{16,20},{20,16},{24,28},{28,24},{1,5},{5... | collective-permute-start | bytes 196616 | tf_op jit(solution)/shard_map/ppermute | solution.py:517
  28.5 2.2 %collective-permute-start.5 = (bf16[256,128]{1,0:T(8,128)(2,1)S(1)}, bf16[256,128]{1,0:T(8,128)(2,1)S(1)}, u32[]{:S(2)}, u32[]{:S(2)}) collective-permute-start(bf16[256,128]{1,0:T(8,128)(2,1)S(1)} %get-tuple-element.41), channel_id=1, source_target_pairs={{0,8},{4,12},{8,0},{12,4},{16,24},{20,28},{24,16},{28,20},{1,9},{5... | collective-permute-start | bytes 196616 | tf_op jit(solution)/shard_map/ppermute | solution.py:517
  30.7 0.8 %collective-permute-start.6 = (bf16[256,128]{1,0:T(8,128)(2,1)S(1)}, bf16[256,128]{1,0:T(8,128)(2,1)S(1)}, u32[]{:S(2)}, u32[]{:S(2)}) collective-permute-start(bf16[256,128]{1,0:T(8,128)(2,1)S(1)} %get-tuple-element.42), channel_id=1, source_target_pairs={{0,12},{4,8},{8,4},{12,0},{16,28},{20,24},{24,20},{28,16},{1,13},{... | collective-permute-start | bytes 196616 | tf_op jit(solution)/shard_map/ppermute | solution.py:517
  31.4 1.7 %collective-permute-done.4.refs_1_ = bf16[256,128]{1,0:T(8,128)(2,1)S(1)} collective-permute-done((bf16[256,128]{1,0:T(8,128)(2,1)S(1)}, bf16[256,128]{1,0:T(8,128)(2,1)S(1)}, u32[]{:S(2)}, u32[]{:S(2)}) %collective-permute-start.4) | collective-permute-done | bytes 65568 | tf_op jit(solution)/shard_map/ppermute | solution.py:517
  33.1 1.3 %collective-permute-done.5.refs_2_ = bf16[256,128]{1,0:T(8,128)(2,1)S(1)} collective-permute-done((bf16[256,128]{1,0:T(8,128)(2,1)S(1)}, bf16[256,128]{1,0:T(8,128)(2,1)S(1)}, u32[]{:S(2)}, u32[]{:S(2)}) %collective-permute-start.5) | collective-permute-done | bytes 65568 | tf_op jit(solution)/shard_map/ppermute | solution.py:517
  34.5 2.5 %collective-permute-start.9 = (bf16[256,128]{1,0:T(8,128)(2,1)S(1)}, bf16[256,128]{1,0:T(8,128)(2,1)S(1)}, u32[]{:S(2)}, u32[]{:S(2)}) collective-permute-start(bf16[256,128]{1,0:T(8,128)(2,1)S(1)} %get-tuple-element.50), channel_id=1, source_target_pairs={{0,8},{4,12},{8,0},{12,4},{16,24},{20,28},{24,16},{28,20},{1,9},{5... | collective-permute-start | bytes 196616 | tf_op jit(solution)/shard_map/ppermute | solution.py:517
  36.9 2.2 %collective-permute-start.10 = (bf16[256,128]{1,0:T(8,128)(2,1)S(1)}, bf16[256,128]{1,0:T(8,128)(2,1)S(1)}, u32[]{:S(2)}, u32[]{:S(2)}) collective-permute-start(bf16[256,128]{1,0:T(8,128)(2,1)S(1)} %get-tuple-element.51), channel_id=1, source_target_pairs={{0,12},{4,8},{8,4},{12,0},{16,28},{20,24},{24,20},{28,16},{1,13},{... | collective-permute-start | bytes 196616 | tf_op jit(solution)/shard_map/ppermute | solution.py:517
  39.2 2.4 %shard_map.76 = (f32[8,128,128]{2,1,0:T(8,128)S(1)}, bf16[8,5,128,128]{3,2,1,0:T(8,128)(2,1)S(1)}) custom-call(bf16[4,528,128]{2,1,0:T(8,128)(2,1)S(1)} %all-to-all-done.part_ref, bf16[8,128,256]{2,1,0:T(8,128)(2,1)S(1)} %get-tuple-element.32.mixed_ref, bf16[4,2,128,128]{3,2,1,0:T(8,128)(2,1)S(1)} %get-tuple-element.33.even_ref, ...), custom_call_target="tpu_custom_call" | custom-call | bytes 2097152 | tf_op jit(solution)/shard_map/pallas_call | solution.py:589
  41.6 1.8 %shard_map.77.weights_ref = bf16[8,128,512]{2,1,0:T(8,128)(2,1)S(1)} custom-call(s32[8,128]{1,0:T(8,128)S(1)} %get-tuple-element.31.refs_4_.away_ref, bf16[8,5,128,128]{3,2,1,0:T(8,128)(2,1)S(1)} %get-tuple-element.43.moving_ref, f32[8,128,128]{2,1,0:T(8,128)S(1)} %get-tuple-element.44.inner_ref, bf16[8,128,128]{2,1,0:T(8,128)(2,1)S(1)} %get-tuple-element.45.end_ref, ...), custom_call_target="tpu_custom_call" | custom-call | bytes 2097152 | tf_op jit(solution)/shard_map/pallas_call | solution.py:596
  43.5 1.9 %shard_map.78 = (bf16[4,2,2,128,128]{4,3,2,1,0:T(8,128)(2,1)S(1)}, bf16[512,1024]{1,0:T(8,128)(2,1)S(1)}) custom-call(s32[8,128]{1,0:T(8,128)S(1)} %get-tuple-element.31.refs_4_.away_ref, bf16[8,128,512]{2,1,0:T(8,128)(2,1)S(1)} %shard_map.77.weights_ref, bf16[256,128]{1,0:T(8,128)(2,1)S(1)} %get-tuple-element.48.refs_0_, ...), custom_call_target="tpu_custom_call" | custom-call | bytes 2097152 | tf_op jit(solution)/shard_map/pallas_call | solution.py:602
  45.4 10.4 %all_to_all.10 = bf16[8,2,128,128]{3,2,1,0:T(8,128)(2,1)S(1)} all-to-all(bf16[8,2,128,128]{3,2,1,0:T(8,128)(2,1)S(1)} %bitcast.4), channel_id=1, replica_groups={{0,2,4,6,8,10,12,14},{1,3,5,7,9,11,13,15},{16,18,20,22,24,26,28,30},{17..., dimensions={0} | all-to-all | bytes 1048576 | tf_op jit(solution)/shard_map/all_to_all | solution.py:623
  55.8 0.4 shard_map.80
  56.4 0.4 shard_map.79
  56.8 1.1 %collective-permute-done.12 = bf16[256,512]{1,0:T(8,128)(2,1)S(1)} collective-permute-done((bf16[256,512]{1,0:T(8,128)(2,1)S(1)}, bf16[256,512]{1,0:T(8,128)(2,1)S(1)}, u32[]{:S(2)}, u32[]{:S(2)}) %collective-permute-start.12) | collective-permute-done | bytes 262176 | tf_op jit(solution)/shard_map/ppermute | solution.py:636
  57.9 0.8 %add_convert_fusion = bf16[256,512]{1,0:T(8,128)(2,1)} fusion(f32[256,512]{1,0:T(8,128)S(1)} %shard_map.79, bf16[256,512]{1,0:T(8,128)(2,1)S(1)} %collective-permute-done.12), kind=kLoop, calls=%fused_computation | loop fusion | flops 393216 | bytes 1048576 | tf_op jit(solution)/shard_map/convert_element_type | solution.py:637
  (20 shorter events, 0.3 us)
Async XLA Ops:
  2.9 17.6 %all-to-all-start = ((bf16[4,528,128]{2,1,0:T(8,128)(2,1)}), bf16[4,528,128]{2,1,0:T(8,128)(2,1)S(1)}, u32[]{:S(2)}, u32[]{:S(2)}) async-start(bf16[4,528,128]{2,1,0:T(8,128)(2,1)} %get-tuple-element.30), calls=%async_computation | async-start | bytes 1081344 | tf_op jit(solution)/shard_map/all_to_all | solution.py:509
  8.1 18.2 %collective-permute-start = (bf16[256,128]{1,0:T(8,128)(2,1)}, bf16[256,128]{1,0:T(8,128)(2,1)S(1)}, u32[]{:S(2)}, u32[]{:S(2)}) collective-permute-start(bf16[256,128]{1,0:T(8,128)(2,1)} %get-tuple-element.35), channel_id=1, source_target_pairs={{0,16},{4,20},{8,24},{12,28},{1,17},{5,21},{9,25},{13,29},{2,18},{... | collective-permute-start | bytes 196616 | tf_op jit(solution)/shard_map/ppermute | solution.py:522
  12.6 15.0 %collective-permute-start.1 = (bf16[256,128]{1,0:T(8,128)(2,1)}, bf16[256,128]{1,0:T(8,128)(2,1)S(1)}, u32[]{:S(2)}, u32[]{:S(2)}) collective-permute-start(bf16[256,128]{1,0:T(8,128)(2,1)} %get-tuple-element.36), channel_id=1, source_target_pairs={{0,20},{4,16},{8,28},{12,24},{1,21},{5,17},{9,29},{13,25},{2,22},{... | collective-permute-start | bytes 196616 | tf_op jit(solution)/shard_map/ppermute | solution.py:522
  15.4 12.2 %collective-permute-start.2 = (bf16[256,128]{1,0:T(8,128)(2,1)}, bf16[256,128]{1,0:T(8,128)(2,1)S(1)}, u32[]{:S(2)}, u32[]{:S(2)}) collective-permute-start(bf16[256,128]{1,0:T(8,128)(2,1)} %get-tuple-element.37), channel_id=1, source_target_pairs={{0,24},{4,28},{8,16},{12,20},{1,25},{5,29},{9,17},{13,21},{2,26},{... | collective-permute-start | bytes 196616 | tf_op jit(solution)/shard_map/ppermute | solution.py:522
  16.7 11.0 %collective-permute-start.3 = (bf16[256,128]{1,0:T(8,128)(2,1)}, bf16[256,128]{1,0:T(8,128)(2,1)S(1)}, u32[]{:S(2)}, u32[]{:S(2)}) collective-permute-start(bf16[256,128]{1,0:T(8,128)(2,1)} %get-tuple-element.38), channel_id=1, source_target_pairs={{0,28},{4,24},{8,20},{12,16},{1,29},{5,25},{9,21},{13,17},{2,30},{... | collective-permute-start | bytes 196616 | tf_op jit(solution)/shard_map/ppermute | solution.py:522
  18.9 8.8 %copy-start.1 = (bf16[256,512]{1,0:T(8,128)(2,1)S(1)}, bf16[256,512]{1,0:T(8,128)(2,1)}, u32[]{:S(2)}) copy-start(bf16[256,512]{1,0:T(8,128)(2,1)} %values_ref.3) | copy-start | bytes 786436
  18.9 8.8 %copy-start.2 = (bf16[256,512]{1,0:T(8,128)(2,1)S(1)}, bf16[256,512]{1,0:T(8,128)(2,1)}, u32[]{:S(2)}) copy-start(bf16[256,512]{1,0:T(8,128)(2,1)} %queries_ref.1) | copy-start | bytes 786436
  18.9 24.6 %collective-permute-start.11 = (bf16[512,1024]{1,0:T(8,128)(2,1)}, bf16[512,1024]{1,0:T(8,128)(2,1)S(1)}, u32[]{:S(2)}, u32[]{:S(2)}) collective-permute-start(bf16[512,1024]{1,0:T(8,128)(2,1)} %get-tuple-element.52), channel_id=1, source_target_pairs={{0,2},{1,3},{2,0},{3,1},{4,6},{5,7},{6,4},{7,5},{8,10},{9,11},{10,... | collective-permute-start | bytes 3145736 | tf_op jit(solution)/shard_map/ppermute | solution.py:560
  26.3 15.3 %collective-permute-start.7 = (bf16[8,128,128]{2,1,0:T(8,128)(2,1)S(1)}, bf16[8,128,128]{2,1,0:T(8,128)(2,1)S(1)}, u32[]{:S(2)}, u32[]{:S(2)}) collective-permute-start(bf16[8,128,128]{2,1,0:T(8,128)(2,1)S(1)} %get-tuple-element.47), channel_id=1, source_target_pairs={{0,16},{4,20},{8,24},{12,28},{1,17},{5,21},{9,25},{13,29},{2,18},{... | collective-permute-start | bytes 786440 | tf_op jit(solution)/shard_map/ppermute | solution.py:513
  27.9 5.3 %collective-permute-start.4 = (bf16[256,128]{1,0:T(8,128)(2,1)S(1)}, bf16[256,128]{1,0:T(8,128)(2,1)S(1)}, u32[]{:S(2)}, u32[]{:S(2)}) collective-permute-start(bf16[256,128]{1,0:T(8,128)(2,1)S(1)} %get-tuple-element.40), channel_id=1, source_target_pairs={{0,4},{4,0},{8,12},{12,8},{16,20},{20,16},{24,28},{28,24},{1,5},{5... | collective-permute-start | bytes 196616 | tf_op jit(solution)/shard_map/ppermute | solution.py:517
  28.5 5.9 %collective-permute-start.5 = (bf16[256,128]{1,0:T(8,128)(2,1)S(1)}, bf16[256,128]{1,0:T(8,128)(2,1)S(1)}, u32[]{:S(2)}, u32[]{:S(2)}) collective-permute-start(bf16[256,128]{1,0:T(8,128)(2,1)S(1)} %get-tuple-element.41), channel_id=1, source_target_pairs={{0,8},{4,12},{8,0},{12,4},{16,24},{20,28},{24,16},{28,20},{1,9},{5... | collective-permute-start | bytes 196616 | tf_op jit(solution)/shard_map/ppermute | solution.py:517
  30.7 6.3 %collective-permute-start.6 = (bf16[256,128]{1,0:T(8,128)(2,1)S(1)}, bf16[256,128]{1,0:T(8,128)(2,1)S(1)}, u32[]{:S(2)}, u32[]{:S(2)}) collective-permute-start(bf16[256,128]{1,0:T(8,128)(2,1)S(1)} %get-tuple-element.42), channel_id=1, source_target_pairs={{0,12},{4,8},{8,4},{12,0},{16,28},{20,24},{24,20},{28,16},{1,13},{... | collective-permute-start | bytes 196616 | tf_op jit(solution)/shard_map/ppermute | solution.py:517
  33.1 10.3 %collective-permute-start.8 = (bf16[256,128]{1,0:T(8,128)(2,1)S(1)}, bf16[256,128]{1,0:T(8,128)(2,1)S(1)}, u32[]{:S(2)}, u32[]{:S(2)}) collective-permute-start(bf16[256,128]{1,0:T(8,128)(2,1)S(1)} %get-tuple-element.49), channel_id=1, source_target_pairs={{0,4},{4,0},{8,12},{12,8},{16,20},{20,16},{24,28},{28,24},{1,5},{5... | collective-permute-start | bytes 196616 | tf_op jit(solution)/shard_map/ppermute | solution.py:517
  34.5 9.0 %collective-permute-start.9 = (bf16[256,128]{1,0:T(8,128)(2,1)S(1)}, bf16[256,128]{1,0:T(8,128)(2,1)S(1)}, u32[]{:S(2)}, u32[]{:S(2)}) collective-permute-start(bf16[256,128]{1,0:T(8,128)(2,1)S(1)} %get-tuple-element.50), channel_id=1, source_target_pairs={{0,8},{4,12},{8,0},{12,4},{16,24},{20,28},{24,16},{28,20},{1,9},{5... | collective-permute-start | bytes 196616 | tf_op jit(solution)/shard_map/ppermute | solution.py:517
  36.9 6.5 %collective-permute-start.10 = (bf16[256,128]{1,0:T(8,128)(2,1)S(1)}, bf16[256,128]{1,0:T(8,128)(2,1)S(1)}, u32[]{:S(2)}, u32[]{:S(2)}) collective-permute-start(bf16[256,128]{1,0:T(8,128)(2,1)S(1)} %get-tuple-element.51), channel_id=1, source_target_pairs={{0,12},{4,8},{8,4},{12,0},{16,28},{20,24},{24,20},{28,16},{1,13},{... | collective-permute-start | bytes 196616 | tf_op jit(solution)/shard_map/ppermute | solution.py:517
  43.4 12.4 %copy-start = (bf16[512,2048]{1,0:T(8,128)(2,1)S(1)}, bf16[512,2048]{1,0:T(8,128)(2,1)}, u32[]{:S(2)}) copy-start(bf16[512,2048]{1,0:T(8,128)(2,1)} %own_ref.3) | copy-start | bytes 6291460
  56.3 1.6 %collective-permute-start.12 = (bf16[256,512]{1,0:T(8,128)(2,1)S(1)}, bf16[256,512]{1,0:T(8,128)(2,1)S(1)}, u32[]{:S(2)}, u32[]{:S(2)}) collective-permute-start(bf16[256,512]{1,0:T(8,128)(2,1)S(1)} %shard_map.80), channel_id=1, source_target_pairs={{0,1},{1,0},{2,3},{3,2},{4,5},{5,4},{6,7},{7,6},{8,9},{9,8},{10,11... | collective-permute-start | bytes 786440 | tf_op jit(solution)/shard_map/ppermute | solution.py:636

commit v18 on v17

--- a/solution.py
+++ b/solution.py
@@ -309,7 +309,7 @@
             far_ref[odd] = tail_odd
         onward.append(pair_map)
 
-    interleaved([pair_terms(pair) for pair in reversed(range(units // 2))], 1)
+    interleaved([pair_terms(pair) for pair in reversed(range(units // 2))], 2)
     for group_ref in group_refs:
         group_ref[0] = onward[-1][0]
         group_ref[1] = onward[-1][1]
@@ -372,11 +372,34 @@
     return jnp.clip(source + ahead * units, 0, units - 1), source < (1 - ahead) * units
 
 
-def weights_kernel(before, away_ref, moving_ref, inner_ref, end_ref, tail_ref, *refs):
-    far_keys, group_maps, weights_ref = refs[:before], refs[before:-1], refs[-1]
+def attend_kernel(axes, before, blocks, away_ref, moving_ref, inner_ref, end_ref, tail_ref,
+                  *refs):
     units = inner_ref.shape[0]
+    heads = units // blocks
+    maps = max(before - 1, 0)
+    far_keys, group_maps = refs[:before], refs[before:before + maps]
+    refs = refs[before + maps:]
+    count = (len(refs) - 4 - heads * (1 + before)) // 2
+    arrived = refs[:heads * (1 + before)]
+    out_ref, (values_ref, value_sems, sems) = refs[-4 - count], refs[-3:]
+    place_here = lax.rem(lax.axis_index(axes[0]), heads)
+    value_copies = []
+    for kind in range(1 + before):
+        for turn in range(heads):
+            start = pl.multiple_of(lax.bitwise_xor(place_here, turn) * blocks * BLOCK, BLOCK)
+            value_copies += fetched(
+                [arrived[kind * heads + turn]],
+                [values_ref.at[kind, pl.ds(start, blocks * BLOCK)]],
+                value_sems.at[kind, pl.ds(turn, 1)],
+            )
+    copies = fetched(
+        refs[heads * (1 + before):heads * (1 + before) + count], refs[-3 - count:-3], sems
+    )
     rows, columns = square_iotas()
     scale = HEAD_DIM ** (-0.5)
+
+    def value_of(kind, block):
+        return values_ref[kind, pl.ds(pl.multiple_of(block * BLOCK, BLOCK), BLOCK)]
 
     def steps(unit):
         pair = unit // 2
@@ -385,63 +408,36 @@
             passed = nt(fronts[-1], group_map[0]) + nt(fronts[-1], group_map[1])
             fronts.append(passed.astype(BF16))
         score_list = [jnp.where(rows >= columns, inner_ref[unit] * scale, -1e30)]
+        sources = [(0, unit)]
         for entry in range(1, TOPK):
             source, new = listed_block(away_ref, unit, entry)
             inside = jnp.maximum(source, 0)
             step = jnp.maximum(pair - inside // 2, 0)
             query = moving_ref[unit, step]
             key = jnp.where(step == 0, end_ref[inside], tail_ref[inside])
+            kind, block = 0, inside
             for ahead in range(1, before + 1):
                 place, here = earlier(source, ahead, units)
                 query = jnp.where(here, fronts[ahead - 1], query)
                 key = jnp.where(here, far_keys[ahead - 1][place], key)
+                kind = jnp.where(here, ahead, kind)
+                block = jnp.where(here, place, block)
             score_list.append(jnp.where(new, nt(query, key) * scale, -1e30))
+            sources.append((kind, block))
         yield
         scores = jnp.concatenate(score_list, 1)
         expos = jnp.exp(scores - jnp.max(scores, 1, keepdims=True))
-        weights_ref[unit] = (expos * (1.0 / jnp.sum(expos, 1, keepdims=True))).astype(BF16)
-
-    interleaved([steps(unit) for unit in range(units)], 1)
-
-
-def blend_kernel(axes, before, blocks, away_ref, weights_ref, *refs):
-    units = weights_ref.shape[0]
-    heads = units // blocks
-    count = (len(refs) - 4 - heads * (1 + before)) // 2
-    arrived = refs[:heads * (1 + before)]
-    out_ref, (values_ref, value_sems, sems) = refs[-4 - count], refs[-3:]
-    place = lax.rem(lax.axis_index(axes[0]), heads)
-    value_copies = []
-    for kind in range(1 + before):
-        for turn in range(heads):
-            start = pl.multiple_of(lax.bitwise_xor(place, turn) * blocks * BLOCK, BLOCK)
-            value_copies += fetched(
-                [arrived[kind * heads + turn]],
-                [values_ref.at[kind, pl.ds(start, blocks * BLOCK)]],
-                value_sems.at[kind, pl.ds(turn, 1)],
-            )
-    copies = fetched(
-        refs[heads * (1 + before):heads * (1 + before) + count], refs[-3 - count:-3], sems
-    )
-    for copy in value_copies:
-        copy.wait()
-
-    def value_of(kind, block):
-        return values_ref[kind, pl.ds(pl.multiple_of(block * BLOCK, BLOCK), BLOCK)]
-
-    for unit in range(units):
-        value_list = [value_of(0, unit)]
-        for entry in range(1, TOPK):
-            source, _ = listed_block(away_ref, unit, entry)
-            kind, block = 0, jnp.maximum(source, 0)
-            for ahead in range(1, before + 1):
-                other, here = earlier(source, ahead, units)
-                kind = jnp.where(here, ahead, kind)
-                block = jnp.where(here, other, block)
-            value_list.append(value_of(kind, block))
-        blended = nn(weights_ref[unit], jnp.concatenate(value_list, 0)).astype(BF16)
+        weights = (expos * (1.0 / jnp.sum(expos, 1, keepdims=True))).astype(BF16)
+        yield
+        if unit == 0:
+            for copy in value_copies:
+                copy.wait()
+        value_list = [value_of(kind, block) for kind, block in sources]
+        blended = nn(weights, jnp.concatenate(value_list, 0)).astype(BF16)
         for plane in range(out_ref.shape[1]):
             out_ref[unit // blocks, plane, unit % blocks] = blended
+
+    interleaved([steps(unit) for unit in range(units)], 1)
     for copy in copies:
         copy.wait()
 
@@ -593,23 +589,22 @@
         0,
         [pltpu.VMEM((heads, tokens, HEAD_DIM), BF16), pltpu.SemaphoreType.DMA((heads,))],
     )(parts, mixed, even, pair_map, *query_parts)
-    weights = call(
-        functools.partial(weights_kernel, before),
-        array((units, BLOCK, TOPK * BLOCK)),
-        [SMEM] + [VMEM] * (4 + before + len(map_parts)),
-        0,
-    )(away, moving, inner, end, tail, *far_parts, *map_parts)
     attended, *weight_parts = call(
-        functools.partial(blend_kernel, axes, before, blocks),
+        functools.partial(attend_kernel, axes, before, blocks),
         [array((heads, planes, blocks, *tile))] + [array(part.shape) for part in weight_parts],
-        [SMEM, VMEM] + [ANY] * (heads * (1 + before) + len(weight_parts)),
+        [SMEM]
+        + [VMEM] * (4 + before + len(map_parts))
+        + [ANY] * (heads * (1 + before) + len(weight_parts)),
         0,
         [
             pltpu.VMEM((1 + before, units * BLOCK, HEAD_DIM), BF16),
             pltpu.SemaphoreType.DMA((1 + before, heads)),
             pltpu.SemaphoreType.DMA((planes,)),
         ],
-    )(away, weights, *own_parts, *value_parts, *weight_parts)
+    )(
+        away, moving, inner, end, tail, *far_parts, *map_parts, *own_parts, *value_parts,
+        *weight_parts,
+    )
 
     returns = [
         [

time: 59 us -> 60.5 us (1.025)
  waiting for transfers between devices: 4.12 us -> 5.35 us
    ppermute x1, waiting for transfers between devices: 0.01 us -> 0.72 us  [body(): weight_parts.append(lax.ppermute(pieces[offset - 1], 'head', turned))]
    pallas_call x2 -> x1, Pallas kernels: 3.76 us -> 3.46 us  [body(): call(functools.partial(attend_kernel, axes, before, blocks), [array((head...]
  transfers between devices with their start and end apart: 14 -> 14, of which waited for: 3 -> 5; matrix products, arithmetic and copies ran while one was open for 0% -> 0% of each run, Pallas kernels for 18% -> 15%
where the time goes in v18:
time: 60.5 us; the launch traced here: 60.2 us
  starting transfers between devices  27.2 us (45%)
  Pallas kernels  16 us (26%)
  blocking collectives  10.7 us (18%)
  waiting for transfers between devices  5.35 us (9%)
  other arithmetic  0.77 us (1%)
    ppermute x4, starting transfers between devices, straight(): return lax.ppermute(value, 'ctx', pairs)  10.7 us
    all_to_all x1, blocking collectives, body(): lax.all_to_all(attended.reshape(heads * planes, blocks, *tile), axes, 0,...  10.7 us
    ppermute x6, starting transfers between devices, crossed(): return lax.ppermute(value, 'ctx', pairs) if turn else value  8.29 us
    pallas_call x1, Pallas kernels, body(): call(functools.partial(keys_kernel, blocks), [array((units, *tile)), arra...  6.23 us
    all_to_all x1, starting transfers between devices, exchange(): lax.all_to_all(value, 'ctx', 0, 0, axis_index_groups=members, tiled=True)  5.26 us
    ppermute x6, waiting for transfers between devices, crossed(): return lax.ppermute(value, 'ctx', pairs) if turn else value  3.55 us
    pallas_call x1, Pallas kernels, body(): call(functools.partial(attend_kernel, axes, before, blocks), [array((head...  3.46 us
    pallas_call x1, Pallas kernels, body(): call(functools.partial(pack_kernel, axes, cores), [array(part_shape)] + [...  2.85 us
  transfers between devices with their start and end apart: 14, of which 5 were waited for; matrix products, arithmetic and copies ran while one was open for 0% of the time, Pallas kernels for 15%

profile of v18, /device:TPU:0, one launch (start us, length us, event | category | flops | bytes accessed | tf_op | source)
XLA Modules:
  0.0 60.2 jit_solution(5728080134894927140)
XLA Ops:
  0.0 2.8 %shard_map.73 = (bf16[4,528,128]{2,1,0:T(8,128)(2,1)}, bf16[256,128]{1,0:T(8,128)(2,1)}, bf16[256,128]{1,0:T(8,128)(2,1)}, bf16[256,128]{1,0:T(8,128)(2,1)}, bf1...) custom-call(bf16[256,512]{1,0:T(8,128)(2,1)} %d_ref.1, bf16[256,512]{1,0:T(8,128)(2,1)} %k_ref.1, f32[4,256]{1,0:T(4,128)} %rates_hbm.1, ...), custom_call_target="tpu_custom_call" | custom-call | flops 4194304 | bytes 2097152 | tf_op jit(solution)/shard_map/pallas_call | solution.py:526
  2.9 5.3 %all-to-all-start = ((bf16[4,528,128]{2,1,0:T(8,128)(2,1)}), bf16[4,528,128]{2,1,0:T(8,128)(2,1)S(1)}, u32[]{:S(2)}, u32[]{:S(2)}) async-start(bf16[4,528,128]{2,1,0:T(8,128)(2,1)} %get-tuple-element.30), calls=%async_computation | async-start | bytes 1081344 | tf_op jit(solution)/shard_map/all_to_all | solution.py:505
  8.1 4.5 %collective-permute-start = (bf16[256,128]{1,0:T(8,128)(2,1)}, bf16[256,128]{1,0:T(8,128)(2,1)S(1)}, u32[]{:S(2)}, u32[]{:S(2)}) collective-permute-start(bf16[256,128]{1,0:T(8,128)(2,1)} %get-tuple-element.35), channel_id=1, source_target_pairs={{0,16},{4,20},{8,24},{12,28},{1,17},{5,21},{9,25},{13,29},{2,18},{... | collective-permute-start | bytes 196616 | tf_op jit(solution)/shard_map/ppermute | solution.py:518
  12.6 2.8 %collective-permute-start.1 = (bf16[256,128]{1,0:T(8,128)(2,1)}, bf16[256,128]{1,0:T(8,128)(2,1)S(1)}, u32[]{:S(2)}, u32[]{:S(2)}) collective-permute-start(bf16[256,128]{1,0:T(8,128)(2,1)} %get-tuple-element.36), channel_id=1, source_target_pairs={{0,20},{4,16},{8,28},{12,24},{1,21},{5,17},{9,29},{13,25},{2,22},{... | collective-permute-start | bytes 196616 | tf_op jit(solution)/shard_map/ppermute | solution.py:518
  15.4 1.3 %collective-permute-start.2 = (bf16[256,128]{1,0:T(8,128)(2,1)}, bf16[256,128]{1,0:T(8,128)(2,1)S(1)}, u32[]{:S(2)}, u32[]{:S(2)}) collective-permute-start(bf16[256,128]{1,0:T(8,128)(2,1)} %get-tuple-element.37), channel_id=1, source_target_pairs={{0,24},{4,28},{8,16},{12,20},{1,25},{5,29},{9,17},{13,21},{2,26},{... | collective-permute-start | bytes 196616 | tf_op jit(solution)/shard_map/ppermute | solution.py:518
  16.7 2.2 %collective-permute-start.3 = (bf16[256,128]{1,0:T(8,128)(2,1)}, bf16[256,128]{1,0:T(8,128)(2,1)S(1)}, u32[]{:S(2)}, u32[]{:S(2)}) collective-permute-start(bf16[256,128]{1,0:T(8,128)(2,1)} %get-tuple-element.38), channel_id=1, source_target_pairs={{0,28},{4,24},{8,20},{12,16},{1,29},{5,25},{9,21},{13,17},{2,30},{... | collective-permute-start | bytes 196616 | tf_op jit(solution)/shard_map/ppermute | solution.py:518
  18.9 1.6 %collective-permute-start.11 = (bf16[512,1024]{1,0:T(8,128)(2,1)}, bf16[512,1024]{1,0:T(8,128)(2,1)S(1)}, u32[]{:S(2)}, u32[]{:S(2)}) collective-permute-start(bf16[512,1024]{1,0:T(8,128)(2,1)} %get-tuple-element.52), channel_id=1, source_target_pairs={{0,2},{1,3},{2,0},{3,1},{4,6},{5,7},{6,4},{7,5},{8,10},{9,11},{10,... | collective-permute-start | bytes 3145736 | tf_op jit(solution)/shard_map/ppermute | solution.py:556
  20.5 6.2 %shard_map.74 = (bf16[8,128,128]{2,1,0:T(8,128)(2,1)S(1)}, bf16[8,128,128]{2,1,0:T(8,128)(2,1)S(1)}, bf16[8,128,128]{2,1,0:T(8,128)(2,1)S(1)}, bf16[4,2,128,128]...) custom-call(bf16[4,528,128]{2,1,0:T(8,128)(2,1)S(1)} %all-to-all-don, ...), custom_call_target="tpu_custom_call" | custom-call | flops 1677721600 | bytes 2097152 | tf_op jit(solution)/shard_map/pallas_call | solution.py:559
  26.7 1.3 %collective-permute-start.7 = (bf16[8,128,128]{2,1,0:T(8,128)(2,1)S(1)}, bf16[8,128,128]{2,1,0:T(8,128)(2,1)S(1)}, u32[]{:S(2)}, u32[]{:S(2)}) collective-permute-start(bf16[8,128,128]{2,1,0:T(8,128)(2,1)S(1)} %get-tuple-element.47), channel_id=1, source_target_pairs={{0,16},{4,20},{8,24},{12,28},{1,17},{5,21},{9,25},{13,29},{2,18},{... | collective-permute-start | bytes 786440 | tf_op jit(solution)/shard_map/ppermute | solution.py:509
  28.3 0.6 %collective-permute-start.4 = (bf16[256,128]{1,0:T(8,128)(2,1)S(1)}, bf16[256,128]{1,0:T(8,128)(2,1)S(1)}, u32[]{:S(2)}, u32[]{:S(2)}) collective-permute-start(bf16[256,128]{1,0:T(8,128)(2,1)S(1)} %get-tuple-element.40), channel_id=1, source_target_pairs={{0,4},{4,0},{8,12},{12,8},{16,20},{20,16},{24,28},{28,24},{1,5},{5... | collective-permute-start | bytes 196616 | tf_op jit(solution)/shard_map/ppermute | solution.py:513
  28.9 2.2 %collective-permute-start.5 = (bf16[256,128]{1,0:T(8,128)(2,1)S(1)}, bf16[256,128]{1,0:T(8,128)(2,1)S(1)}, u32[]{:S(2)}, u32[]{:S(2)}) collective-permute-start(bf16[256,128]{1,0:T(8,128)(2,1)S(1)} %get-tuple-element.41), channel_id=1, source_target_pairs={{0,8},{4,12},{8,0},{12,4},{16,24},{20,28},{24,16},{28,20},{1,9},{5... | collective-permute-start | bytes 196616 | tf_op jit(solution)/shard_map/ppermute | solution.py:513
  31.1 0.8 %collective-permute-start.6 = (bf16[256,128]{1,0:T(8,128)(2,1)S(1)}, bf16[256,128]{1,0:T(8,128)(2,1)S(1)}, u32[]{:S(2)}, u32[]{:S(2)}) collective-permute-start(bf16[256,128]{1,0:T(8,128)(2,1)S(1)} %get-tuple-element.42), channel_id=1, source_target_pairs={{0,12},{4,8},{8,4},{12,0},{16,28},{20,24},{24,20},{28,16},{1,13},{... | collective-permute-start | bytes 196616 | tf_op jit(solution)/shard_map/ppermute | solution.py:513
  31.8 1.7 %collective-permute-done.4.refs_1_ = bf16[256,128]{1,0:T(8,128)(2,1)S(1)} collective-permute-done((bf16[256,128]{1,0:T(8,128)(2,1)S(1)}, bf16[256,128]{1,0:T(8,128)(2,1)S(1)}, u32[]{:S(2)}, u32[]{:S(2)}) %collective-permute-start.4) | collective-permute-done | bytes 65568 | tf_op jit(solution)/shard_map/ppermute | solution.py:513
  33.5 1.3 %collective-permute-done.5.refs_2_ = bf16[256,128]{1,0:T(8,128)(2,1)S(1)} collective-permute-done((bf16[256,128]{1,0:T(8,128)(2,1)S(1)}, bf16[256,128]{1,0:T(8,128)(2,1)S(1)}, u32[]{:S(2)}, u32[]{:S(2)}) %collective-permute-start.5) | collective-permute-done | bytes 65568 | tf_op jit(solution)/shard_map/ppermute | solution.py:513
  34.9 2.5 %collective-permute-start.9 = (bf16[256,128]{1,0:T(8,128)(2,1)S(1)}, bf16[256,128]{1,0:T(8,128)(2,1)S(1)}, u32[]{:S(2)}, u32[]{:S(2)}) collective-permute-start(bf16[256,128]{1,0:T(8,128)(2,1)S(1)} %get-tuple-element.50), channel_id=1, source_target_pairs={{0,8},{4,12},{8,0},{12,4},{16,24},{20,28},{24,16},{28,20},{1,9},{5... | collective-permute-start | bytes 196616 | tf_op jit(solution)/shard_map/ppermute | solution.py:513
  37.3 2.2 %collective-permute-start.10 = (bf16[256,128]{1,0:T(8,128)(2,1)S(1)}, bf16[256,128]{1,0:T(8,128)(2,1)S(1)}, u32[]{:S(2)}, u32[]{:S(2)}) collective-permute-start(bf16[256,128]{1,0:T(8,128)(2,1)S(1)} %get-tuple-element.51), channel_id=1, source_target_pairs={{0,12},{4,8},{8,4},{12,0},{16,28},{20,24},{24,20},{28,16},{1,13},{... | collective-permute-start | bytes 196616 | tf_op jit(solution)/shard_map/ppermute | solution.py:513
  39.6 2.4 %shard_map.76 = (f32[8,128,128]{2,1,0:T(8,128)S(1)}, bf16[8,5,128,128]{3,2,1,0:T(8,128)(2,1)S(1)}) custom-call(bf16[4,528,128]{2,1,0:T(8,128)(2,1)S(1)} %all-to-all-done.part_ref, bf16[8,128,256]{2,1,0:T(8,128)(2,1)S(1)} %get-tuple-element.32.mixed_ref, bf16[4,2,128,128]{3,2,1,0:T(8,128)(2,1)S(1)} %get-tuple-element.33.even_ref, ...), custom_call_target="tpu_custom_call" | custom-call | bytes 2097152 | tf_op jit(solution)/shard_map/pallas_call | solution.py:585
  42.0 0.5 collective-permute-done.10.refs_4_
  42.5 0.7 %collective-permute-done.11.refs_9_ = bf16[512,1024]{1,0:T(8,128)(2,1)S(1)} collective-permute-done((bf16[512,1024]{1,0:T(8,128)(2,1)}, bf16[512,1024]{1,0:T(8,128)(2,1)S(1)}, u32[]{:S(2)}, u32[]{:S(2)}) %collective-permute-start.11) | collective-permute-done | bytes 1048608 | tf_op jit(solution)/shard_map/ppermute | solution.py:556
  43.2 3.5 %shard_map.77 = (bf16[4,2,2,128,128]{4,3,2,1,0:T(8,128)(2,1)S(1)}, bf16[512,1024]{1,0:T(8,128)(2,1)S(1)}) custom-call(s32[8,128]{1,0:T(8,128)S(1)} %get-tuple-element.31.refs_4_.away_ref, bf16[8,5,128,128]{3,2,1,0:T(8,128)(2,1)S(1)} %get-tuple-element.43.moving_ref, f32[8,128,128]{2,1,0:T(8,128)S(1)} %get-tuple-element.44.inner_ref, ...), custom_call_target="tpu_custom_call" | custom-call | bytes 2097152 | tf_op jit(solution)/shard_map/pallas_call | solution.py:592
  46.7 10.7 %all_to_all.10 = bf16[8,2,128,128]{3,2,1,0:T(8,128)(2,1)S(1)} all-to-all(bf16[8,2,128,128]{3,2,1,0:T(8,128)(2,1)S(1)} %bitcast.4), channel_id=1, replica_groups={{0,2,4,6,8,10,12,14},{1,3,5,7,9,11,13,15},{16,18,20,22,24,26,28,30},{17..., dimensions={0} | all-to-all | bytes 1048576 | tf_op jit(solution)/shard_map/all_to_all | solution.py:618
  57.9 0.4 shard_map.78
  58.4 1.1 %collective-permute-done.12 = bf16[256,512]{1,0:T(8,128)(2,1)S(1)} collective-permute-done((bf16[256,512]{1,0:T(8,128)(2,1)S(1)}, bf16[256,512]{1,0:T(8,128)(2,1)S(1)}, u32[]{:S(2)}, u32[]{:S(2)}) %collective-permute-start.12) | collective-permute-done | bytes 262176 | tf_op jit(solution)/shard_map/ppermute | solution.py:631
  59.4 0.8 %add_convert_fusion = bf16[256,512]{1,0:T(8,128)(2,1)} fusion(f32[256,512]{1,0:T(8,128)S(1)} %shard_map.78, bf16[256,512]{1,0:T(8,128)(2,1)S(1)} %collective-permute-done.12), kind=kLoop, calls=%fused_computation | loop fusion | flops 393216 | bytes 1048576 | tf_op jit(solution)/shard_map/convert_element_type | solution.py:632
  (19 shorter events, 0.8 us)
Async XLA Ops:
  2.9 17.6 %all-to-all-start = ((bf16[4,528,128]{2,1,0:T(8,128)(2,1)}), bf16[4,528,128]{2,1,0:T(8,128)(2,1)S(1)}, u32[]{:S(2)}, u32[]{:S(2)}) async-start(bf16[4,528,128]{2,1,0:T(8,128)(2,1)} %get-tuple-element.30), calls=%async_computation | async-start | bytes 1081344 | tf_op jit(solution)/shard_map/all_to_all | solution.py:505
  8.1 18.6 %collective-permute-start = (bf16[256,128]{1,0:T(8,128)(2,1)}, bf16[256,128]{1,0:T(8,128)(2,1)S(1)}, u32[]{:S(2)}, u32[]{:S(2)}) collective-permute-start(bf16[256,128]{1,0:T(8,128)(2,1)} %get-tuple-element.35), channel_id=1, source_target_pairs={{0,16},{4,20},{8,24},{12,28},{1,17},{5,21},{9,25},{13,29},{2,18},{... | collective-permute-start | bytes 196616 | tf_op jit(solution)/shard_map/ppermute | solution.py:518
  12.6 15.4 %collective-permute-start.1 = (bf16[256,128]{1,0:T(8,128)(2,1)}, bf16[256,128]{1,0:T(8,128)(2,1)S(1)}, u32[]{:S(2)}, u32[]{:S(2)}) collective-permute-start(bf16[256,128]{1,0:T(8,128)(2,1)} %get-tuple-element.36), channel_id=1, source_target_pairs={{0,20},{4,16},{8,28},{12,24},{1,21},{5,17},{9,29},{13,25},{2,22},{... | collective-permute-start | bytes 196616 | tf_op jit(solution)/shard_map/ppermute | solution.py:518
  15.4 12.7 %collective-permute-start.2 = (bf16[256,128]{1,0:T(8,128)(2,1)}, bf16[256,128]{1,0:T(8,128)(2,1)S(1)}, u32[]{:S(2)}, u32[]{:S(2)}) collective-permute-start(bf16[256,128]{1,0:T(8,128)(2,1)} %get-tuple-element.37), channel_id=1, source_target_pairs={{0,24},{4,28},{8,16},{12,20},{1,25},{5,29},{9,17},{13,21},{2,26},{... | collective-permute-start | bytes 196616 | tf_op jit(solution)/shard_map/ppermute | solution.py:518
  16.7 11.4 %collective-permute-start.3 = (bf16[256,128]{1,0:T(8,128)(2,1)}, bf16[256,128]{1,0:T(8,128)(2,1)S(1)}, u32[]{:S(2)}, u32[]{:S(2)}) collective-permute-start(bf16[256,128]{1,0:T(8,128)(2,1)} %get-tuple-element.38), channel_id=1, source_target_pairs={{0,28},{4,24},{8,20},{12,16},{1,29},{5,25},{9,21},{13,17},{2,30},{... | collective-permute-start | bytes 196616 | tf_op jit(solution)/shard_map/ppermute | solution.py:518
  18.9 9.2 %copy-start.1 = (bf16[256,512]{1,0:T(8,128)(2,1)S(1)}, bf16[256,512]{1,0:T(8,128)(2,1)}, u32[]{:S(2)}) copy-start(bf16[256,512]{1,0:T(8,128)(2,1)} %values_ref.3) | copy-start | bytes 786436
  18.9 9.2 %copy-start.2 = (bf16[256,512]{1,0:T(8,128)(2,1)S(1)}, bf16[256,512]{1,0:T(8,128)(2,1)}, u32[]{:S(2)}) copy-start(bf16[256,512]{1,0:T(8,128)(2,1)} %queries_ref.1) | copy-start | bytes 786436
  18.9 24.3 %collective-permute-start.11 = (bf16[512,1024]{1,0:T(8,128)(2,1)}, bf16[512,1024]{1,0:T(8,128)(2,1)S(1)}, u32[]{:S(2)}, u32[]{:S(2)}) collective-permute-start(bf16[512,1024]{1,0:T(8,128)(2,1)} %get-tuple-element.52), channel_id=1, source_target_pairs={{0,2},{1,3},{2,0},{3,1},{4,6},{5,7},{6,4},{7,5},{8,10},{9,11},{10,... | collective-permute-start | bytes 3145736 | tf_op jit(solution)/shard_map/ppermute | solution.py:556
  26.7 16.5 %collective-permute-start.7 = (bf16[8,128,128]{2,1,0:T(8,128)(2,1)S(1)}, bf16[8,128,128]{2,1,0:T(8,128)(2,1)S(1)}, u32[]{:S(2)}, u32[]{:S(2)}) collective-permute-start(bf16[8,128,128]{2,1,0:T(8,128)(2,1)S(1)} %get-tuple-element.47), channel_id=1, source_target_pairs={{0,16},{4,20},{8,24},{12,28},{1,17},{5,21},{9,25},{13,29},{2,18},{... | collective-permute-start | bytes 786440 | tf_op jit(solution)/shard_map/ppermute | solution.py:509
  28.3 5.3 %collective-permute-start.4 = (bf16[256,128]{1,0:T(8,128)(2,1)S(1)}, bf16[256,128]{1,0:T(8,128)(2,1)S(1)}, u32[]{:S(2)}, u32[]{:S(2)}) collective-permute-start(bf16[256,128]{1,0:T(8,128)(2,1)S(1)} %get-tuple-element.40), channel_id=1, source_target_pairs={{0,4},{4,0},{8,12},{12,8},{16,20},{20,16},{24,28},{28,24},{1,5},{5... | collective-permute-start | bytes 196616 | tf_op jit(solution)/shard_map/ppermute | solution.py:513
  28.9 5.9 %collective-permute-start.5 = (bf16[256,128]{1,0:T(8,128)(2,1)S(1)}, bf16[256,128]{1,0:T(8,128)(2,1)S(1)}, u32[]{:S(2)}, u32[]{:S(2)}) collective-permute-start(bf16[256,128]{1,0:T(8,128)(2,1)S(1)} %get-tuple-element.41), channel_id=1, source_target_pairs={{0,8},{4,12},{8,0},{12,4},{16,24},{20,28},{24,16},{28,20},{1,9},{5... | collective-permute-start | bytes 196616 | tf_op jit(solution)/shard_map/ppermute | solution.py:513
  31.1 6.3 %collective-permute-start.6 = (bf16[256,128]{1,0:T(8,128)(2,1)S(1)}, bf16[256,128]{1,0:T(8,128)(2,1)S(1)}, u32[]{:S(2)}, u32[]{:S(2)}) collective-permute-start(bf16[256,128]{1,0:T(8,128)(2,1)S(1)} %get-tuple-element.42), channel_id=1, source_target_pairs={{0,12},{4,8},{8,4},{12,0},{16,28},{20,24},{24,20},{28,16},{1,13},{... | collective-permute-start | bytes 196616 | tf_op jit(solution)/shard_map/ppermute | solution.py:513
  33.5 8.4 %collective-permute-start.8 = (bf16[256,128]{1,0:T(8,128)(2,1)S(1)}, bf16[256,128]{1,0:T(8,128)(2,1)S(1)}, u32[]{:S(2)}, u32[]{:S(2)}) collective-permute-start(bf16[256,128]{1,0:T(8,128)(2,1)S(1)} %get-tuple-element.49), channel_id=1, source_target_pairs={{0,4},{4,0},{8,12},{12,8},{16,20},{20,16},{24,28},{28,24},{1,5},{5... | collective-permute-start | bytes 196616 | tf_op jit(solution)/shard_map/ppermute | solution.py:513
  34.9 7.1 %collective-permute-start.9 = (bf16[256,128]{1,0:T(8,128)(2,1)S(1)}, bf16[256,128]{1,0:T(8,128)(2,1)S(1)}, u32[]{:S(2)}, u32[]{:S(2)}) collective-permute-start(bf16[256,128]{1,0:T(8,128)(2,1)S(1)} %get-tuple-element.50), channel_id=1, source_target_pairs={{0,8},{4,12},{8,0},{12,4},{16,24},{20,28},{24,16},{28,20},{1,9},{5... | collective-permute-start | bytes 196616 | tf_op jit(solution)/shard_map/ppermute | solution.py:513
  37.3 5.2 %collective-permute-start.10 = (bf16[256,128]{1,0:T(8,128)(2,1)S(1)}, bf16[256,128]{1,0:T(8,128)(2,1)S(1)}, u32[]{:S(2)}, u32[]{:S(2)}) collective-permute-start(bf16[256,128]{1,0:T(8,128)(2,1)S(1)} %get-tuple-element.51), channel_id=1, source_target_pairs={{0,12},{4,8},{8,4},{12,0},{16,28},{20,24},{24,20},{28,16},{1,13},{... | collective-permute-start | bytes 196616 | tf_op jit(solution)/shard_map/ppermute | solution.py:513
  43.2 14.1 %copy-start = (bf16[512,2048]{1,0:T(8,128)(2,1)S(1)}, bf16[512,2048]{1,0:T(8,128)(2,1)}, u32[]{:S(2)}) copy-start(bf16[512,2048]{1,0:T(8,128)(2,1)} %own_ref.3) | copy-start | bytes 6291460
  57.8 1.6 %collective-permute-start.12 = (bf16[256,512]{1,0:T(8,128)(2,1)S(1)}, bf16[256,512]{1,0:T(8,128)(2,1)S(1)}, u32[]{:S(2)}, u32[]{:S(2)}) collective-permute-start(bf16[256,512]{1,0:T(8,128)(2,1)S(1)} %shard_map.79), channel_id=1, source_target_pairs={{0,1},{1,0},{2,3},{3,2},{4,5},{5,4},{6,7},{7,6},{8,9},{9,8},{10,11... | collective-permute-start | bytes 786440 | tf_op jit(solution)/shard_map/ppermute | solution.py:631

commit v19 on v17

--- a/solution.py
+++ b/solution.py
@@ -151,20 +151,22 @@
         copy.wait()
 
 
-def cut_kernel(axes, queries_ref, values_ref, *refs):
+def cut_kernel(axes, heads, queries_ref, values_ref, *refs):
     sems = refs[-1]
-    heads = sems.shape[1]
-    outs = refs[-1 - 2 * heads:-1]
+    first, outs = refs[-2 * heads], refs[1 - 2 * heads:-1]
+    query_outs, value_outs = list(outs[:heads - 1]), list(outs[heads - 1:])
+    query_outs.insert(1, first.at[0])
+    value_outs.insert(1, first.at[1])
     place = lax.rem(lax.axis_index(axes[0]), heads)
     cuts = [
         pl.multiple_of(lax.bitwise_xor(place, turn) * HEAD_DIM, HEAD_DIM) for turn in range(heads)
     ]
     copies = []
-    for kind, source in enumerate((queries_ref, values_ref)):
+    for kind, (source, targets) in enumerate(
+        ((queries_ref, query_outs), (values_ref, value_outs))
+    ):
         copies += fetched(
-            [source.at[:, pl.ds(cut, HEAD_DIM)] for cut in cuts],
-            outs[kind * heads:(kind + 1) * heads],
-            sems.at[kind],
+            [source.at[:, pl.ds(cut, HEAD_DIM)] for cut in cuts], targets, sems.at[kind]
         )
     for copy in copies:
         copy.wait()
@@ -321,7 +323,7 @@
     inner_ref, moving_ref, query_ref, sems = refs[heads:]
     place = lax.rem(lax.axis_index(axes[0]), heads)
     copies = fetched(
-        refs[:heads],
+        [refs[turn].at[0] if turn == 1 else refs[turn] for turn in range(heads)],
         [query_ref.at[lax.bitwise_xor(place, turn)] for turn in range(heads)],
         sems,
     )
@@ -415,8 +417,9 @@
     for kind in range(1 + before):
         for turn in range(heads):
             start = pl.multiple_of(lax.bitwise_xor(place, turn) * blocks * BLOCK, BLOCK)
+            source = arrived[kind * heads + turn]
             value_copies += fetched(
-                [arrived[kind * heads + turn]],
+                [source if kind or turn != 1 else source.at[1]],
                 [values_ref.at[kind, pl.ds(start, blocks * BLOCK)]],
                 value_sems.at[kind, pl.ds(turn, 1)],
             )
@@ -577,15 +580,19 @@
     )(parts)
     far_parts = [onward(far, by) for by in range(1, before + 1)]
     map_parts = [onward(group_maps[0], by) for by in range(1, before)]
-    cut = call(
-        functools.partial(cut_kernel, axes),
-        [array((tokens, HEAD_DIM))] * (2 * heads),
+    first, *cut = call(
+        functools.partial(cut_kernel, axes, heads),
+        [array((2, tokens, HEAD_DIM))] + [array((tokens, HEAD_DIM))] * (2 * heads - 2),
         [ANY] * (len(value_parts) + 3),
         2000 * cubes,
         [pltpu.SemaphoreType.DMA((2, heads))],
     )(queries, values, *value_parts, away)
-    query_parts = [crossed(cut[turn], turn) for turn in range(heads)]
-    own_parts = [crossed(cut[heads + turn], turn) for turn in range(heads)]
+    first = crossed(first, 1)
+    turns = [0, *range(2, heads)]
+    query_parts = [crossed(part, turn) for part, turn in zip(cut[:heads - 1], turns)]
+    own_parts = [crossed(part, turn) for part, turn in zip(cut[heads - 1:], turns)]
+    query_parts.insert(1, first)
+    own_parts.insert(1, first)
     inner, moving = call(
         functools.partial(queries_kernel, axes, blocks),
         [array((units, BLOCK, BLOCK), F32), array((units, pairs + 1, *tile))],

time: 59 us -> 59 us (level)
    ppermute x6 -> x5, waiting for transfers between devices: 3.03 us -> 3.03 us  [crossed(): return lax.ppermute(value, 'ctx', pairs) if turn else value]
    ppermute x6 -> x5, starting transfers between devices: 8.29 us -> 8.28 us  [crossed(): return lax.ppermute(value, 'ctx', pairs) if turn else value]
  transfers between devices with their start and end apart: 14 -> 13, of which waited for: 3 -> 2; matrix products, arithmetic and copies ran while one was open for 0% -> 0% of each run, Pallas kernels for 18% -> 18%
where the time goes in v19:
time: 59 us; the launch traced here: 58.7 us
  starting transfers between devices  27.2 us (46%)
  Pallas kernels  15.9 us (27%)
  blocking collectives  10.4 us (18%)
  waiting for transfers between devices  4.13 us (7%)
  other arithmetic  0.78 us (1%)
    ppermute x4, starting transfers between devices, straight(): return lax.ppermute(value, 'ctx', pairs)  10.7 us
    all_to_all x1, blocking collectives, body(): lax.all_to_all(attended.reshape(heads * planes, blocks, *tile), axes, 0,...  10.4 us
    ppermute x5, starting transfers between devices, crossed(): return lax.ppermute(value, 'ctx', pairs) if turn else value  8.28 us
    pallas_call x1, Pallas kernels, body(): call(functools.partial(keys_kernel, blocks), [array((units, *tile)), arra...  5.82 us
    all_to_all x1, starting transfers between devices, exchange(): lax.all_to_all(value, 'ctx', 0, 0, axis_index_groups=members, tiled=True)  5.26 us
    ppermute x5, waiting for transfers between devices, crossed(): return lax.ppermute(value, 'ctx', pairs) if turn else value  3.03 us
    pallas_call x1, Pallas kernels, body(): call(functools.partial(pack_kernel, axes, cores), [array(part_shape)] + [...  2.83 us
    pallas_call x1, Pallas kernels, body(): call(functools.partial(queries_kernel, axes, blocks), [array((units, BLOC...  2.38 us
  transfers between devices with their start and end apart: 13, of which 2 were waited for; matrix products, arithmetic and copies ran while one was open for 0% of the time, Pallas kernels for 18%

profile of v19, /device:TPU:0, one launch (start us, length us, event | category | flops | bytes accessed | tf_op | source)
XLA Modules:
  0.0 58.7 jit_solution(11991305082349002917)
XLA Ops:
  0.0 2.8 %shard_map.73 = (bf16[4,528,128]{2,1,0:T(8,128)(2,1)}, bf16[256,128]{1,0:T(8,128)(2,1)}, bf16[256,128]{1,0:T(8,128)(2,1)}, bf16[256,128]{1,0:T(8,128)(2,1)}, bf1...) custom-call(bf16[256,512]{1,0:T(8,128)(2,1)} %d_ref.1, bf16[256,512]{1,0:T(8,128)(2,1)} %k_ref.1, f32[4,256]{1,0:T(4,128)} %rates_hbm.1, ...), custom_call_target="tpu_custom_call" | custom-call | flops 4194304 | bytes 2097152 | tf_op jit(solution)/shard_map/pallas_call | solution.py:533
  2.8 5.3 %all-to-all-start = ((bf16[4,528,128]{2,1,0:T(8,128)(2,1)}), bf16[4,528,128]{2,1,0:T(8,128)(2,1)S(1)}, u32[]{:S(2)}, u32[]{:S(2)}) async-start(bf16[4,528,128]{2,1,0:T(8,128)(2,1)} %get-tuple-element.29), calls=%async_computation | async-start | bytes 1081344 | tf_op jit(solution)/shard_map/all_to_all | solution.py:512
  8.1 4.5 %collective-permute-start = (bf16[256,128]{1,0:T(8,128)(2,1)}, bf16[256,128]{1,0:T(8,128)(2,1)S(1)}, u32[]{:S(2)}, u32[]{:S(2)}) collective-permute-start(bf16[256,128]{1,0:T(8,128)(2,1)} %get-tuple-element.34), channel_id=1, source_target_pairs={{0,16},{4,20},{8,24},{12,28},{1,17},{5,21},{9,25},{13,29},{2,18},{... | collective-permute-start | bytes 196616 | tf_op jit(solution)/shard_map/ppermute | solution.py:525
  12.6 2.8 %collective-permute-start.1 = (bf16[256,128]{1,0:T(8,128)(2,1)}, bf16[256,128]{1,0:T(8,128)(2,1)S(1)}, u32[]{:S(2)}, u32[]{:S(2)}) collective-permute-start(bf16[256,128]{1,0:T(8,128)(2,1)} %get-tuple-element.35), channel_id=1, source_target_pairs={{0,20},{4,16},{8,28},{12,24},{1,21},{5,17},{9,29},{13,25},{2,22},{... | collective-permute-start | bytes 196616 | tf_op jit(solution)/shard_map/ppermute | solution.py:525
  15.4 1.3 %collective-permute-start.2 = (bf16[256,128]{1,0:T(8,128)(2,1)}, bf16[256,128]{1,0:T(8,128)(2,1)S(1)}, u32[]{:S(2)}, u32[]{:S(2)}) collective-permute-start(bf16[256,128]{1,0:T(8,128)(2,1)} %get-tuple-element.36), channel_id=1, source_target_pairs={{0,24},{4,28},{8,16},{12,20},{1,25},{5,29},{9,17},{13,21},{2,26},{... | collective-permute-start | bytes 196616 | tf_op jit(solution)/shard_map/ppermute | solution.py:525
  16.7 2.2 %collective-permute-start.3 = (bf16[256,128]{1,0:T(8,128)(2,1)}, bf16[256,128]{1,0:T(8,128)(2,1)S(1)}, u32[]{:S(2)}, u32[]{:S(2)}) collective-permute-start(bf16[256,128]{1,0:T(8,128)(2,1)} %get-tuple-element.37), channel_id=1, source_target_pairs={{0,28},{4,24},{8,20},{12,16},{1,29},{5,25},{9,21},{13,17},{2,30},{... | collective-permute-start | bytes 196616 | tf_op jit(solution)/shard_map/ppermute | solution.py:525
  18.9 1.6 %collective-permute-start.10 = (bf16[512,1024]{1,0:T(8,128)(2,1)}, bf16[512,1024]{1,0:T(8,128)(2,1)S(1)}, u32[]{:S(2)}, u32[]{:S(2)}) collective-permute-start(bf16[512,1024]{1,0:T(8,128)(2,1)} %get-tuple-element.50), channel_id=1, source_target_pairs={{0,2},{1,3},{2,0},{3,1},{4,6},{5,7},{6,4},{7,5},{8,10},{9,11},{10,... | collective-permute-start | bytes 3145736 | tf_op jit(solution)/shard_map/ppermute | solution.py:563
  20.4 5.8 %shard_map.74 = (bf16[8,128,128]{2,1,0:T(8,128)(2,1)S(1)}, bf16[8,128,128]{2,1,0:T(8,128)(2,1)S(1)}, bf16[8,128,128]{2,1,0:T(8,128)(2,1)S(1)}, bf16[4,2,128,128]...) custom-call(bf16[4,528,128]{2,1,0:T(8,128)(2,1)S(1)} %all-to-all-don, ...), custom_call_target="tpu_custom_call" | custom-call | flops 1677721600 | bytes 2097152 | tf_op jit(solution)/shard_map/pallas_call | solution.py:566
  26.3 1.3 %collective-permute-start.7 = (bf16[8,128,128]{2,1,0:T(8,128)(2,1)S(1)}, bf16[8,128,128]{2,1,0:T(8,128)(2,1)S(1)}, u32[]{:S(2)}, u32[]{:S(2)}) collective-permute-start(bf16[8,128,128]{2,1,0:T(8,128)(2,1)S(1)} %get-tuple-element.46), channel_id=1, source_target_pairs={{0,16},{4,20},{8,24},{12,28},{1,17},{5,21},{9,25},{13,29},{2,18},{... | collective-permute-start | bytes 786440 | tf_op jit(solution)/shard_map/ppermute | solution.py:516
  27.6 0.2 shard_map.75
  27.9 0.6 %collective-permute-start.4 = (bf16[2,256,128]{2,1,0:T(8,128)(2,1)S(1)}, bf16[2,256,128]{2,1,0:T(8,128)(2,1)S(1)}, u32[]{:S(2)}, u32[]{:S(2)}) collective-permute-start(bf16[2,256,128]{2,1,0:T(8,128)(2,1)S(1)} %get-tuple-element.39), channel_id=1, source_target_pairs={{0,4},{4,0},{8,12},{12,8},{16,20},{20,16},{24,28},{28,24},{1,5},{5... | collective-permute-start | bytes 393224 | tf_op jit(solution)/shard_map/ppermute | solution.py:520
  28.5 2.2 %collective-permute-start.5 = (bf16[256,128]{1,0:T(8,128)(2,1)S(1)}, bf16[256,128]{1,0:T(8,128)(2,1)S(1)}, u32[]{:S(2)}, u32[]{:S(2)}) collective-permute-start(bf16[256,128]{1,0:T(8,128)(2,1)S(1)} %get-tuple-element.40), channel_id=1, source_target_pairs={{0,8},{4,12},{8,0},{12,4},{16,24},{20,28},{24,16},{28,20},{1,9},{5... | collective-permute-start | bytes 196616 | tf_op jit(solution)/shard_map/ppermute | solution.py:520
  30.7 0.8 %collective-permute-start.6 = (bf16[256,128]{1,0:T(8,128)(2,1)S(1)}, bf16[256,128]{1,0:T(8,128)(2,1)S(1)}, u32[]{:S(2)}, u32[]{:S(2)}) collective-permute-start(bf16[256,128]{1,0:T(8,128)(2,1)S(1)} %get-tuple-element.41), channel_id=1, source_target_pairs={{0,12},{4,8},{8,4},{12,0},{16,28},{20,24},{24,20},{28,16},{1,13},{... | collective-permute-start | bytes 196616 | tf_op jit(solution)/shard_map/ppermute | solution.py:520
  31.4 3.0 %collective-permute-done.5.refs_2_ = bf16[256,128]{1,0:T(8,128)(2,1)S(1)} collective-permute-done((bf16[256,128]{1,0:T(8,128)(2,1)S(1)}, bf16[256,128]{1,0:T(8,128)(2,1)S(1)}, u32[]{:S(2)}, u32[]{:S(2)}) %collective-permute-start.5) | collective-permute-done | bytes 65568 | tf_op jit(solution)/shard_map/ppermute | solution.py:520
  34.4 2.5 %collective-permute-start.8 = (bf16[256,128]{1,0:T(8,128)(2,1)S(1)}, bf16[256,128]{1,0:T(8,128)(2,1)S(1)}, u32[]{:S(2)}, u32[]{:S(2)}) collective-permute-start(bf16[256,128]{1,0:T(8,128)(2,1)S(1)} %get-tuple-element.48), channel_id=1, source_target_pairs={{0,8},{4,12},{8,0},{12,4},{16,24},{20,28},{24,16},{28,20},{1,9},{5... | collective-permute-start | bytes 196616 | tf_op jit(solution)/shard_map/ppermute | solution.py:520
  36.9 2.2 %collective-permute-start.9 = (bf16[256,128]{1,0:T(8,128)(2,1)S(1)}, bf16[256,128]{1,0:T(8,128)(2,1)S(1)}, u32[]{:S(2)}, u32[]{:S(2)}) collective-permute-start(bf16[256,128]{1,0:T(8,128)(2,1)S(1)} %get-tuple-element.49), channel_id=1, source_target_pairs={{0,12},{4,8},{8,4},{12,0},{16,28},{20,24},{24,20},{28,16},{1,13},{... | collective-permute-start | bytes 196616 | tf_op jit(solution)/shard_map/ppermute | solution.py:520
  39.2 2.4 %shard_map.76 = (f32[8,128,128]{2,1,0:T(8,128)S(1)}, bf16[8,5,128,128]{3,2,1,0:T(8,128)(2,1)S(1)}) custom-call(bf16[4,528,128]{2,1,0:T(8,128)(2,1)S(1)} %all-to-all-done.part_ref, bf16[8,128,256]{2,1,0:T(8,128)(2,1)S(1)} %get-tuple-element.31.mixed_ref, bf16[4,2,128,128]{3,2,1,0:T(8,128)(2,1)S(1)} %get-tuple-element.32.even_ref, ...), custom_call_target="tpu_custom_call" | custom-call | bytes 2097152 | tf_op jit(solution)/shard_map/pallas_call | solution.py:596
  41.6 1.8 %shard_map.77.weights_ref = bf16[8,128,512]{2,1,0:T(8,128)(2,1)S(1)} custom-call(s32[8,128]{1,0:T(8,128)S(1)} %get-tuple-element.30.refs_4_.away_ref, bf16[8,5,128,128]{3,2,1,0:T(8,128)(2,1)S(1)} %get-tuple-element.42.moving_ref, f32[8,128,128]{2,1,0:T(8,128)S(1)} %get-tuple-element.43.inner_ref, bf16[8,128,128]{2,1,0:T(8,128)(2,1)S(1)} %get-tuple-element.44.end_ref, ...), custom_call_target="tpu_custom_call" | custom-call | bytes 2097152 | tf_op jit(solution)/shard_map/pallas_call | solution.py:603
  43.5 1.9 %shard_map.78 = (bf16[4,2,2,128,128]{4,3,2,1,0:T(8,128)(2,1)S(1)}, bf16[512,1024]{1,0:T(8,128)(2,1)S(1)}) custom-call(s32[8,128]{1,0:T(8,128)S(1)} %get-tuple-element.30.refs_4_.away_ref, bf16[8,128,512]{2,1,0:T(8,128)(2,1)S(1)} %shard_map.77.weights_ref, bf16[256,128]{1,0:T(8,128)(2,1)S(1)} %get-tuple-element.47.refs_0_, ...), custom_call_target="tpu_custom_call" | custom-call | bytes 2097152 | tf_op jit(solution)/shard_map/pallas_call | solution.py:609
  45.4 10.4 %all_to_all.10 = bf16[8,2,128,128]{3,2,1,0:T(8,128)(2,1)S(1)} all-to-all(bf16[8,2,128,128]{3,2,1,0:T(8,128)(2,1)S(1)} %bitcast.4), channel_id=1, replica_groups={{0,2,4,6,8,10,12,14},{1,3,5,7,9,11,13,15},{16,18,20,22,24,26,28,30},{17..., dimensions={0} | all-to-all | bytes 1048576 | tf_op jit(solution)/shard_map/all_to_all | solution.py:630
  55.8 0.4 shard_map.80
  56.3 0.4 shard_map.79
  56.8 1.1 %collective-permute-done.11 = bf16[256,512]{1,0:T(8,128)(2,1)S(1)} collective-permute-done((bf16[256,512]{1,0:T(8,128)(2,1)S(1)}, bf16[256,512]{1,0:T(8,128)(2,1)S(1)}, u32[]{:S(2)}, u32[]{:S(2)}) %collective-permute-start.11) | collective-permute-done | bytes 262176 | tf_op jit(solution)/shard_map/ppermute | solution.py:643
  57.9 0.8 %add_convert_fusion = bf16[256,512]{1,0:T(8,128)(2,1)} fusion(f32[256,512]{1,0:T(8,128)S(1)} %shard_map.79, bf16[256,512]{1,0:T(8,128)(2,1)S(1)} %collective-permute-done.11), kind=kLoop, calls=%fused_computation | loop fusion | flops 393216 | bytes 1048576 | tf_op jit(solution)/shard_map/convert_element_type | solution.py:644
  (18 shorter events, 0.1 us)
Async XLA Ops:
  2.8 17.6 %all-to-all-start = ((bf16[4,528,128]{2,1,0:T(8,128)(2,1)}), bf16[4,528,128]{2,1,0:T(8,128)(2,1)S(1)}, u32[]{:S(2)}, u32[]{:S(2)}) async-start(bf16[4,528,128]{2,1,0:T(8,128)(2,1)} %get-tuple-element.29), calls=%async_computation | async-start | bytes 1081344 | tf_op jit(solution)/shard_map/all_to_all | solution.py:512
  8.1 18.2 %collective-permute-start = (bf16[256,128]{1,0:T(8,128)(2,1)}, bf16[256,128]{1,0:T(8,128)(2,1)S(1)}, u32[]{:S(2)}, u32[]{:S(2)}) collective-permute-start(bf16[256,128]{1,0:T(8,128)(2,1)} %get-tuple-element.34), channel_id=1, source_target_pairs={{0,16},{4,20},{8,24},{12,28},{1,17},{5,21},{9,25},{13,29},{2,18},{... | collective-permute-start | bytes 196616 | tf_op jit(solution)/shard_map/ppermute | solution.py:525
  12.6 15.0 %collective-permute-start.1 = (bf16[256,128]{1,0:T(8,128)(2,1)}, bf16[256,128]{1,0:T(8,128)(2,1)S(1)}, u32[]{:S(2)}, u32[]{:S(2)}) collective-permute-start(bf16[256,128]{1,0:T(8,128)(2,1)} %get-tuple-element.35), channel_id=1, source_target_pairs={{0,20},{4,16},{8,28},{12,24},{1,21},{5,17},{9,29},{13,25},{2,22},{... | collective-permute-start | bytes 196616 | tf_op jit(solution)/shard_map/ppermute | solution.py:525
  15.4 12.2 %collective-permute-start.2 = (bf16[256,128]{1,0:T(8,128)(2,1)}, bf16[256,128]{1,0:T(8,128)(2,1)S(1)}, u32[]{:S(2)}, u32[]{:S(2)}) collective-permute-start(bf16[256,128]{1,0:T(8,128)(2,1)} %get-tuple-element.36), channel_id=1, source_target_pairs={{0,24},{4,28},{8,16},{12,20},{1,25},{5,29},{9,17},{13,21},{2,26},{... | collective-permute-start | bytes 196616 | tf_op jit(solution)/shard_map/ppermute | solution.py:525
  16.7 11.0 %collective-permute-start.3 = (bf16[256,128]{1,0:T(8,128)(2,1)}, bf16[256,128]{1,0:T(8,128)(2,1)S(1)}, u32[]{:S(2)}, u32[]{:S(2)}) collective-permute-start(bf16[256,128]{1,0:T(8,128)(2,1)} %get-tuple-element.37), channel_id=1, source_target_pairs={{0,28},{4,24},{8,20},{12,16},{1,29},{5,25},{9,21},{13,17},{2,30},{... | collective-permute-start | bytes 196616 | tf_op jit(solution)/shard_map/ppermute | solution.py:525
  18.9 8.8 %copy-start.1 = (bf16[256,512]{1,0:T(8,128)(2,1)S(1)}, bf16[256,512]{1,0:T(8,128)(2,1)}, u32[]{:S(2)}) copy-start(bf16[256,512]{1,0:T(8,128)(2,1)} %values_ref.3) | copy-start | bytes 786436
  18.9 8.8 %copy-start.2 = (bf16[256,512]{1,0:T(8,128)(2,1)S(1)}, bf16[256,512]{1,0:T(8,128)(2,1)}, u32[]{:S(2)}) copy-start(bf16[256,512]{1,0:T(8,128)(2,1)} %queries_ref.1) | copy-start | bytes 786436
  18.9 24.6 %collective-permute-start.10 = (bf16[512,1024]{1,0:T(8,128)(2,1)}, bf16[512,1024]{1,0:T(8,128)(2,1)S(1)}, u32[]{:S(2)}, u32[]{:S(2)}) collective-permute-start(bf16[512,1024]{1,0:T(8,128)(2,1)} %get-tuple-element.50), channel_id=1, source_target_pairs={{0,2},{1,3},{2,0},{3,1},{4,6},{5,7},{6,4},{7,5},{8,10},{9,11},{10,... | collective-permute-start | bytes 3145736 | tf_op jit(solution)/shard_map/ppermute | solution.py:563
  26.3 15.3 %collective-permute-start.7 = (bf16[8,128,128]{2,1,0:T(8,128)(2,1)S(1)}, bf16[8,128,128]{2,1,0:T(8,128)(2,1)S(1)}, u32[]{:S(2)}, u32[]{:S(2)}) collective-permute-start(bf16[8,128,128]{2,1,0:T(8,128)(2,1)S(1)} %get-tuple-element.46), channel_id=1, source_target_pairs={{0,16},{4,20},{8,24},{12,28},{1,17},{5,21},{9,25},{13,29},{2,18},{... | collective-permute-start | bytes 786440 | tf_op jit(solution)/shard_map/ppermute | solution.py:516
  27.9 11.3 %collective-permute-start.4 = (bf16[2,256,128]{2,1,0:T(8,128)(2,1)S(1)}, bf16[2,256,128]{2,1,0:T(8,128)(2,1)S(1)}, u32[]{:S(2)}, u32[]{:S(2)}) collective-permute-start(bf16[2,256,128]{2,1,0:T(8,128)(2,1)S(1)} %get-tuple-element.39), channel_id=1, source_target_pairs={{0,4},{4,0},{8,12},{12,8},{16,20},{20,16},{24,28},{28,24},{1,5},{5... | collective-permute-start | bytes 393224 | tf_op jit(solution)/shard_map/ppermute | solution.py:520
  28.5 5.9 %collective-permute-start.5 = (bf16[256,128]{1,0:T(8,128)(2,1)S(1)}, bf16[256,128]{1,0:T(8,128)(2,1)S(1)}, u32[]{:S(2)}, u32[]{:S(2)}) collective-permute-start(bf16[256,128]{1,0:T(8,128)(2,1)S(1)} %get-tuple-element.40), channel_id=1, source_target_pairs={{0,8},{4,12},{8,0},{12,4},{16,24},{20,28},{24,16},{28,20},{1,9},{5... | collective-permute-start | bytes 196616 | tf_op jit(solution)/shard_map/ppermute | solution.py:520
  30.7 6.3 %collective-permute-start.6 = (bf16[256,128]{1,0:T(8,128)(2,1)S(1)}, bf16[256,128]{1,0:T(8,128)(2,1)S(1)}, u32[]{:S(2)}, u32[]{:S(2)}) collective-permute-start(bf16[256,128]{1,0:T(8,128)(2,1)S(1)} %get-tuple-element.41), channel_id=1, source_target_pairs={{0,12},{4,8},{8,4},{12,0},{16,28},{20,24},{24,20},{28,16},{1,13},{... | collective-permute-start | bytes 196616 | tf_op jit(solution)/shard_map/ppermute | solution.py:520
  34.4 9.0 %collective-permute-start.8 = (bf16[256,128]{1,0:T(8,128)(2,1)S(1)}, bf16[256,128]{1,0:T(8,128)(2,1)S(1)}, u32[]{:S(2)}, u32[]{:S(2)}) collective-permute-start(bf16[256,128]{1,0:T(8,128)(2,1)S(1)} %get-tuple-element.48), channel_id=1, source_target_pairs={{0,8},{4,12},{8,0},{12,4},{16,24},{20,28},{24,16},{28,20},{1,9},{5... | collective-permute-start | bytes 196616 | tf_op jit(solution)/shard_map/ppermute | solution.py:520
  36.9 6.5 %collective-permute-start.9 = (bf16[256,128]{1,0:T(8,128)(2,1)S(1)}, bf16[256,128]{1,0:T(8,128)(2,1)S(1)}, u32[]{:S(2)}, u32[]{:S(2)}) collective-permute-start(bf16[256,128]{1,0:T(8,128)(2,1)S(1)} %get-tuple-element.49), channel_id=1, source_target_pairs={{0,12},{4,8},{8,4},{12,0},{16,28},{20,24},{24,20},{28,16},{1,13},{... | collective-permute-start | bytes 196616 | tf_op jit(solution)/shard_map/ppermute | solution.py:520
  43.4 12.4 %copy-start = (bf16[512,2048]{1,0:T(8,128)(2,1)S(1)}, bf16[512,2048]{1,0:T(8,128)(2,1)}, u32[]{:S(2)}) copy-start(bf16[512,2048]{1,0:T(8,128)(2,1)} %own_ref.3) | copy-start | bytes 6291460
  56.3 1.6 %collective-permute-start.11 = (bf16[256,512]{1,0:T(8,128)(2,1)S(1)}, bf16[256,512]{1,0:T(8,128)(2,1)S(1)}, u32[]{:S(2)}, u32[]{:S(2)}) collective-permute-start(bf16[256,512]{1,0:T(8,128)(2,1)S(1)} %shard_map.80), channel_id=1, source_target_pairs={{0,1},{1,0},{2,3},{3,2},{4,5},{5,4},{6,7},{7,6},{8,9},{9,8},{10,11... | collective-permute-start | bytes 786440 | tf_op jit(solution)/shard_map/ppermute | solution.py:643

commit v20 on v19

--- a/solution.py
+++ b/solution.py
@@ -374,9 +374,16 @@
     return jnp.clip(source + ahead * units, 0, units - 1), source < (1 - ahead) * units
 
 
+def softmax(scores):
+    expos = jnp.exp(scores - jnp.max(scores, 1, keepdims=True))
+    return (expos * (1.0 / jnp.sum(expos, 1, keepdims=True))).astype(BF16)
+
+
 def weights_kernel(before, away_ref, moving_ref, inner_ref, end_ref, tail_ref, *refs):
-    far_keys, group_maps, weights_ref = refs[:before], refs[before:-1], refs[-1]
+    far_keys, group_maps = refs[:before], refs[before:-2]
+    weights_ref, scores_ref = refs[-2:]
     units = inner_ref.shape[0]
+    ready = weights_ref.shape[0]
     rows, columns = square_iotas()
     scale = HEAD_DIM ** (-0.5)
 
@@ -400,14 +407,17 @@
             score_list.append(jnp.where(new, nt(query, key) * scale, -1e30))
         yield
         scores = jnp.concatenate(score_list, 1)
-        expos = jnp.exp(scores - jnp.max(scores, 1, keepdims=True))
-        weights_ref[unit] = (expos * (1.0 / jnp.sum(expos, 1, keepdims=True))).astype(BF16)
+        if unit < ready:
+            weights_ref[unit] = softmax(scores)
+        else:
+            scores_ref[unit - ready] = scores
 
     interleaved([steps(unit) for unit in range(units)], 1)
 
 
-def blend_kernel(axes, before, blocks, away_ref, weights_ref, *refs):
-    units = weights_ref.shape[0]
+def blend_kernel(axes, before, blocks, away_ref, weights_ref, scores_ref, *refs):
+    ready, late = weights_ref.shape[0], scores_ref.shape[0]
+    units = ready + late
     heads = units // blocks
     count = (len(refs) - 4 - heads * (1 + before)) // 2
     arrived = refs[:heads * (1 + before)]
@@ -426,6 +436,7 @@
     copies = fetched(
         refs[heads * (1 + before):heads * (1 + before) + count], refs[-3 - count:-3], sems
     )
+    late_weights = [softmax(scores_ref[unit]) for unit in range(late)]
     for copy in value_copies:
         copy.wait()
 
@@ -442,7 +453,8 @@
                 kind = jnp.where(here, ahead, kind)
                 block = jnp.where(here, other, block)
             value_list.append(value_of(kind, block))
-        blended = nn(weights_ref[unit], jnp.concatenate(value_list, 0)).astype(BF16)
+        weights = weights_ref[unit] if unit < ready else late_weights[unit - ready]
+        blended = nn(weights, jnp.concatenate(value_list, 0)).astype(BF16)
         for plane in range(out_ref.shape[1]):
             out_ref[unit // blocks, plane, unit % blocks] = blended
     for copy in copies:
@@ -600,23 +612,26 @@
         0,
         [pltpu.VMEM((heads, tokens, HEAD_DIM), BF16), pltpu.SemaphoreType.DMA((heads,))],
     )(parts, mixed, even, pair_map, *query_parts)
-    weights = call(
+    weights, scores = call(
         functools.partial(weights_kernel, before),
-        array((units, BLOCK, TOPK * BLOCK)),
+        [
+            array((units - units // 2, BLOCK, TOPK * BLOCK)),
+            array((units // 2, BLOCK, TOPK * BLOCK), F32),
+        ],
         [SMEM] + [VMEM] * (4 + before + len(map_parts)),
         0,
     )(away, moving, inner, end, tail, *far_parts, *map_parts)
     attended, *weight_parts = call(
         functools.partial(blend_kernel, axes, before, blocks),
         [array((heads, planes, blocks, *tile))] + [array(part.shape) for part in weight_parts],
-        [SMEM, VMEM] + [ANY] * (heads * (1 + before) + len(weight_parts)),
+        [SMEM, VMEM, VMEM] + [ANY] * (heads * (1 + before) + len(weight_parts)),
         0,
         [
             pltpu.VMEM((1 + before, units * BLOCK, HEAD_DIM), BF16),
             pltpu.SemaphoreType.DMA((1 + before, heads)),
             pltpu.SemaphoreType.DMA((planes,)),
         ],
-    )(away, weights, *own_parts, *value_parts, *weight_parts)
+    )(away, weights, scores, *own_parts, *value_parts, *weight_parts)
 
     returns = [
         [

time: 59 us -> 59.2 us (level)
  no operation moved by 1% of the time
where the time goes in v20:
time: 59.2 us; the launch traced here: 58.9 us
  starting transfers between devices  27.2 us (46%)
  Pallas kernels  15.9 us (27%)
  blocking collectives  10.6 us (18%)
  waiting for transfers between devices  4.14 us (7%)
  other arithmetic  0.77 us (1%)
    ppermute x4, starting transfers between devices, straight(): return lax.ppermute(value, 'ctx', pairs)  10.7 us
    all_to_all x1, blocking collectives, body(): lax.all_to_all(attended.reshape(heads * planes, blocks, *tile), axes, 0,...  10.6 us
    ppermute x5, starting transfers between devices, crossed(): return lax.ppermute(value, 'ctx', pairs) if turn else value  8.28 us
    pallas_call x1, Pallas kernels, body(): call(functools.partial(keys_kernel, blocks), [array((units, *tile)), arra...  5.82 us
    all_to_all x1, starting transfers between devices, exchange(): lax.all_to_all(value, 'ctx', 0, 0, axis_index_groups=members, tiled=True)  5.26 us
    ppermute x5, waiting for transfers between devices, crossed(): return lax.ppermute(value, 'ctx', pairs) if turn else value  3.03 us
    pallas_call x1, Pallas kernels, body(): call(functools.partial(pack_kernel, axes, cores), [array(part_shape)] + [...  2.85 us
    pallas_call x1, Pallas kernels, body(): call(functools.partial(queries_kernel, axes, blocks), [array((units, BLOC...  2.38 us
  transfers between devices with their start and end apart: 13, of which 2 were waited for; matrix products, arithmetic and copies ran while one was open for 0% of the time, Pallas kernels for 18%

profile of v20, /device:TPU:0, one launch (start us, length us, event | category | flops | bytes accessed | tf_op | source)
XLA Modules:
  0.0 58.9 jit_solution(15782120418147553133)
XLA Ops:
  0.0 2.8 %shard_map.73 = (bf16[4,528,128]{2,1,0:T(8,128)(2,1)}, bf16[256,128]{1,0:T(8,128)(2,1)}, bf16[256,128]{1,0:T(8,128)(2,1)}, bf16[256,128]{1,0:T(8,128)(2,1)}, bf1...) custom-call(bf16[256,512]{1,0:T(8,128)(2,1)} %d_ref.1, bf16[256,512]{1,0:T(8,128)(2,1)} %k_ref.1, f32[4,256]{1,0:T(4,128)} %rates_hbm.1, ...), custom_call_target="tpu_custom_call" | custom-call | flops 4194304 | bytes 2097152 | tf_op jit(solution)/shard_map/pallas_call | solution.py:545
  2.9 5.3 %all-to-all-start = ((bf16[4,528,128]{2,1,0:T(8,128)(2,1)}), bf16[4,528,128]{2,1,0:T(8,128)(2,1)S(1)}, u32[]{:S(2)}, u32[]{:S(2)}) async-start(bf16[4,528,128]{2,1,0:T(8,128)(2,1)} %get-tuple-element.31), calls=%async_computation | async-start | bytes 1081344 | tf_op jit(solution)/shard_map/all_to_all | solution.py:524
  8.1 4.5 %collective-permute-start = (bf16[256,128]{1,0:T(8,128)(2,1)}, bf16[256,128]{1,0:T(8,128)(2,1)S(1)}, u32[]{:S(2)}, u32[]{:S(2)}) collective-permute-start(bf16[256,128]{1,0:T(8,128)(2,1)} %get-tuple-element.36), channel_id=1, source_target_pairs={{0,16},{4,20},{8,24},{12,28},{1,17},{5,21},{9,25},{13,29},{2,18},{... | collective-permute-start | bytes 196616 | tf_op jit(solution)/shard_map/ppermute | solution.py:537
  12.6 2.8 %collective-permute-start.1 = (bf16[256,128]{1,0:T(8,128)(2,1)}, bf16[256,128]{1,0:T(8,128)(2,1)S(1)}, u32[]{:S(2)}, u32[]{:S(2)}) collective-permute-start(bf16[256,128]{1,0:T(8,128)(2,1)} %get-tuple-element.37), channel_id=1, source_target_pairs={{0,20},{4,16},{8,28},{12,24},{1,21},{5,17},{9,29},{13,25},{2,22},{... | collective-permute-start | bytes 196616 | tf_op jit(solution)/shard_map/ppermute | solution.py:537
  15.4 1.3 %collective-permute-start.2 = (bf16[256,128]{1,0:T(8,128)(2,1)}, bf16[256,128]{1,0:T(8,128)(2,1)S(1)}, u32[]{:S(2)}, u32[]{:S(2)}) collective-permute-start(bf16[256,128]{1,0:T(8,128)(2,1)} %get-tuple-element.38), channel_id=1, source_target_pairs={{0,24},{4,28},{8,16},{12,20},{1,25},{5,29},{9,17},{13,21},{2,26},{... | collective-permute-start | bytes 196616 | tf_op jit(solution)/shard_map/ppermute | solution.py:537
  16.7 2.2 %collective-permute-start.3 = (bf16[256,128]{1,0:T(8,128)(2,1)}, bf16[256,128]{1,0:T(8,128)(2,1)S(1)}, u32[]{:S(2)}, u32[]{:S(2)}) collective-permute-start(bf16[256,128]{1,0:T(8,128)(2,1)} %get-tuple-element.39), channel_id=1, source_target_pairs={{0,28},{4,24},{8,20},{12,16},{1,29},{5,25},{9,21},{13,17},{2,30},{... | collective-permute-start | bytes 196616 | tf_op jit(solution)/shard_map/ppermute | solution.py:537
  18.9 1.6 %collective-permute-start.10 = (bf16[512,1024]{1,0:T(8,128)(2,1)}, bf16[512,1024]{1,0:T(8,128)(2,1)S(1)}, u32[]{:S(2)}, u32[]{:S(2)}) collective-permute-start(bf16[512,1024]{1,0:T(8,128)(2,1)} %get-tuple-element.54), channel_id=1, source_target_pairs={{0,2},{1,3},{2,0},{3,1},{4,6},{5,7},{6,4},{7,5},{8,10},{9,11},{10,... | collective-permute-start | bytes 3145736 | tf_op jit(solution)/shard_map/ppermute | solution.py:575
  20.5 5.8 %shard_map.74 = (bf16[8,128,128]{2,1,0:T(8,128)(2,1)S(1)}, bf16[8,128,128]{2,1,0:T(8,128)(2,1)S(1)}, bf16[8,128,128]{2,1,0:T(8,128)(2,1)S(1)}, bf16[4,2,128,128]...) custom-call(bf16[4,528,128]{2,1,0:T(8,128)(2,1)S(1)} %all-to-all-don, ...), custom_call_target="tpu_custom_call" | custom-call | flops 1677721600 | bytes 2097152 | tf_op jit(solution)/shard_map/pallas_call | solution.py:578
  26.3 1.3 %collective-permute-start.7 = (bf16[8,128,128]{2,1,0:T(8,128)(2,1)S(1)}, bf16[8,128,128]{2,1,0:T(8,128)(2,1)S(1)}, u32[]{:S(2)}, u32[]{:S(2)}) collective-permute-start(bf16[8,128,128]{2,1,0:T(8,128)(2,1)S(1)} %get-tuple-element.48), channel_id=1, source_target_pairs={{0,16},{4,20},{8,24},{12,28},{1,17},{5,21},{9,25},{13,29},{2,18},{... | collective-permute-start | bytes 786440 | tf_op jit(solution)/shard_map/ppermute | solution.py:528
  27.7 0.2 shard_map.75
  27.9 0.6 %collective-permute-start.4 = (bf16[2,256,128]{2,1,0:T(8,128)(2,1)S(1)}, bf16[2,256,128]{2,1,0:T(8,128)(2,1)S(1)}, u32[]{:S(2)}, u32[]{:S(2)}) collective-permute-start(bf16[2,256,128]{2,1,0:T(8,128)(2,1)S(1)} %get-tuple-element.41), channel_id=1, source_target_pairs={{0,4},{4,0},{8,12},{12,8},{16,20},{20,16},{24,28},{28,24},{1,5},{5... | collective-permute-start | bytes 393224 | tf_op jit(solution)/shard_map/ppermute | solution.py:532
  28.5 2.2 %collective-permute-start.5 = (bf16[256,128]{1,0:T(8,128)(2,1)S(1)}, bf16[256,128]{1,0:T(8,128)(2,1)S(1)}, u32[]{:S(2)}, u32[]{:S(2)}) collective-permute-start(bf16[256,128]{1,0:T(8,128)(2,1)S(1)} %get-tuple-element.42), channel_id=1, source_target_pairs={{0,8},{4,12},{8,0},{12,4},{16,24},{20,28},{24,16},{28,20},{1,9},{5... | collective-permute-start | bytes 196616 | tf_op jit(solution)/shard_map/ppermute | solution.py:532
  30.7 0.8 %collective-permute-start.6 = (bf16[256,128]{1,0:T(8,128)(2,1)S(1)}, bf16[256,128]{1,0:T(8,128)(2,1)S(1)}, u32[]{:S(2)}, u32[]{:S(2)}) collective-permute-start(bf16[256,128]{1,0:T(8,128)(2,1)S(1)} %get-tuple-element.43), channel_id=1, source_target_pairs={{0,12},{4,8},{8,4},{12,0},{16,28},{20,24},{24,20},{28,16},{1,13},{... | collective-permute-start | bytes 196616 | tf_op jit(solution)/shard_map/ppermute | solution.py:532
  31.4 3.0 %collective-permute-done.5.refs_2_ = bf16[256,128]{1,0:T(8,128)(2,1)S(1)} collective-permute-done((bf16[256,128]{1,0:T(8,128)(2,1)S(1)}, bf16[256,128]{1,0:T(8,128)(2,1)S(1)}, u32[]{:S(2)}, u32[]{:S(2)}) %collective-permute-start.5) | collective-permute-done | bytes 65568 | tf_op jit(solution)/shard_map/ppermute | solution.py:532
  34.4 2.5 %collective-permute-start.8 = (bf16[256,128]{1,0:T(8,128)(2,1)S(1)}, bf16[256,128]{1,0:T(8,128)(2,1)S(1)}, u32[]{:S(2)}, u32[]{:S(2)}) collective-permute-start(bf16[256,128]{1,0:T(8,128)(2,1)S(1)} %get-tuple-element.52), channel_id=1, source_target_pairs={{0,8},{4,12},{8,0},{12,4},{16,24},{20,28},{24,16},{28,20},{1,9},{5... | collective-permute-start | bytes 196616 | tf_op jit(solution)/shard_map/ppermute | solution.py:532
  36.9 2.2 %collective-permute-start.9 = (bf16[256,128]{1,0:T(8,128)(2,1)S(1)}, bf16[256,128]{1,0:T(8,128)(2,1)S(1)}, u32[]{:S(2)}, u32[]{:S(2)}) collective-permute-start(bf16[256,128]{1,0:T(8,128)(2,1)S(1)} %get-tuple-element.53), channel_id=1, source_target_pairs={{0,12},{4,8},{8,4},{12,0},{16,28},{20,24},{24,20},{28,16},{1,13},{... | collective-permute-start | bytes 196616 | tf_op jit(solution)/shard_map/ppermute | solution.py:532
  39.2 2.4 %shard_map.76 = (f32[8,128,128]{2,1,0:T(8,128)S(1)}, bf16[8,5,128,128]{3,2,1,0:T(8,128)(2,1)S(1)}) custom-call(bf16[4,528,128]{2,1,0:T(8,128)(2,1)S(1)} %all-to-all-done.part_ref, bf16[8,128,256]{2,1,0:T(8,128)(2,1)S(1)} %get-tuple-element.33.mixed_ref, bf16[4,2,128,128]{3,2,1,0:T(8,128)(2,1)S(1)} %get-tuple-element.34.even_ref, ...), custom_call_target="tpu_custom_call" | custom-call | bytes 2097152 | tf_op jit(solution)/shard_map/pallas_call | solution.py:608
  41.6 1.6 %shard_map.77 = (bf16[4,128,512]{2,1,0:T(8,128)(2,1)S(1)}, f32[4,128,512]{2,1,0:T(8,128)S(1)}) custom-call(s32[8,128]{1,0:T(8,128)S(1)} %get-tuple-element.32.refs_4_.away_ref, bf16[8,5,128,128]{3,2,1,0:T(8,128)(2,1)S(1)} %get-tuple-element.44.moving_ref, f32[8,128,128]{2,1,0:T(8,128)S(1)} %get-tuple-element.45.inner_ref, ...), custom_call_target="tpu_custom_call" | custom-call | bytes 2097152 | tf_op jit(solution)/shard_map/pallas_call | solution.py:615
  43.2 2.2 %shard_map.78 = (bf16[4,2,2,128,128]{4,3,2,1,0:T(8,128)(2,1)S(1)}, bf16[512,1024]{1,0:T(8,128)(2,1)S(1)}) custom-call(s32[8,128]{1,0:T(8,128)S(1)} %get-tuple-element.32.refs_4_.away_ref, bf16[4,128,512]{2,1,0:T(8,128)(2,1)S(1)} %get-tuple-element.49.weights_ref, f32[4,128,512]{2,1,0:T(8,128)S(1)} %get-tuple-element.50.scores_ref, ...), custom_call_target="tpu_custom_call" | custom-call | bytes 2097152 | tf_op jit(solution)/shard_map/pallas_call | solution.py:624
  45.5 10.6 %all_to_all.10 = bf16[8,2,128,128]{3,2,1,0:T(8,128)(2,1)S(1)} all-to-all(bf16[8,2,128,128]{3,2,1,0:T(8,128)(2,1)S(1)} %bitcast.4), channel_id=1, replica_groups={{0,2,4,6,8,10,12,14},{1,3,5,7,9,11,13,15},{16,18,20,22,24,26,28,30},{17..., dimensions={0} | all-to-all | bytes 1048576 | tf_op jit(solution)/shard_map/all_to_all | solution.py:645
  56.0 0.4 shard_map.80
  56.6 0.4 shard_map.79
  57.0 1.1 %collective-permute-done.11 = bf16[256,512]{1,0:T(8,128)(2,1)S(1)} collective-permute-done((bf16[256,512]{1,0:T(8,128)(2,1)S(1)}, bf16[256,512]{1,0:T(8,128)(2,1)S(1)}, u32[]{:S(2)}, u32[]{:S(2)}) %collective-permute-start.11) | collective-permute-done | bytes 262176 | tf_op jit(solution)/shard_map/ppermute | solution.py:658
  58.1 0.8 %add_convert_fusion = bf16[256,512]{1,0:T(8,128)(2,1)} fusion(f32[256,512]{1,0:T(8,128)S(1)} %shard_map.79, bf16[256,512]{1,0:T(8,128)(2,1)S(1)} %collective-permute-done.11), kind=kLoop, calls=%fused_computation | loop fusion | flops 393216 | bytes 1048576 | tf_op jit(solution)/shard_map/convert_element_type | solution.py:659
  (18 shorter events, 0.1 us)
Async XLA Ops:
  2.9 17.6 %all-to-all-start = ((bf16[4,528,128]{2,1,0:T(8,128)(2,1)}), bf16[4,528,128]{2,1,0:T(8,128)(2,1)S(1)}, u32[]{:S(2)}, u32[]{:S(2)}) async-start(bf16[4,528,128]{2,1,0:T(8,128)(2,1)} %get-tuple-element.31), calls=%async_computation | async-start | bytes 1081344 | tf_op jit(solution)/shard_map/all_to_all | solution.py:524
  8.1 18.2 %collective-permute-start = (bf16[256,128]{1,0:T(8,128)(2,1)}, bf16[256,128]{1,0:T(8,128)(2,1)S(1)}, u32[]{:S(2)}, u32[]{:S(2)}) collective-permute-start(bf16[256,128]{1,0:T(8,128)(2,1)} %get-tuple-element.36), channel_id=1, source_target_pairs={{0,16},{4,20},{8,24},{12,28},{1,17},{5,21},{9,25},{13,29},{2,18},{... | collective-permute-start | bytes 196616 | tf_op jit(solution)/shard_map/ppermute | solution.py:537
  12.6 15.0 %collective-permute-start.1 = (bf16[256,128]{1,0:T(8,128)(2,1)}, bf16[256,128]{1,0:T(8,128)(2,1)S(1)}, u32[]{:S(2)}, u32[]{:S(2)}) collective-permute-start(bf16[256,128]{1,0:T(8,128)(2,1)} %get-tuple-element.37), channel_id=1, source_target_pairs={{0,20},{4,16},{8,28},{12,24},{1,21},{5,17},{9,29},{13,25},{2,22},{... | collective-permute-start | bytes 196616 | tf_op jit(solution)/shard_map/ppermute | solution.py:537
  15.4 12.2 %collective-permute-start.2 = (bf16[256,128]{1,0:T(8,128)(2,1)}, bf16[256,128]{1,0:T(8,128)(2,1)S(1)}, u32[]{:S(2)}, u32[]{:S(2)}) collective-permute-start(bf16[256,128]{1,0:T(8,128)(2,1)} %get-tuple-element.38), channel_id=1, source_target_pairs={{0,24},{4,28},{8,16},{12,20},{1,25},{5,29},{9,17},{13,21},{2,26},{... | collective-permute-start | bytes 196616 | tf_op jit(solution)/shard_map/ppermute | solution.py:537
  16.7 11.0 %collective-permute-start.3 = (bf16[256,128]{1,0:T(8,128)(2,1)}, bf16[256,128]{1,0:T(8,128)(2,1)S(1)}, u32[]{:S(2)}, u32[]{:S(2)}) collective-permute-start(bf16[256,128]{1,0:T(8,128)(2,1)} %get-tuple-element.39), channel_id=1, source_target_pairs={{0,28},{4,24},{8,20},{12,16},{1,29},{5,25},{9,21},{13,17},{2,30},{... | collective-permute-start | bytes 196616 | tf_op jit(solution)/shard_map/ppermute | solution.py:537
  18.9 8.8 %copy-start.1 = (bf16[256,512]{1,0:T(8,128)(2,1)S(1)}, bf16[256,512]{1,0:T(8,128)(2,1)}, u32[]{:S(2)}) copy-start(bf16[256,512]{1,0:T(8,128)(2,1)} %values_ref.3) | copy-start | bytes 786436
  18.9 8.8 %copy-start.2 = (bf16[256,512]{1,0:T(8,128)(2,1)S(1)}, bf16[256,512]{1,0:T(8,128)(2,1)}, u32[]{:S(2)}) copy-start(bf16[256,512]{1,0:T(8,128)(2,1)} %queries_ref.1) | copy-start | bytes 786436
  18.9 24.3 %collective-permute-start.10 = (bf16[512,1024]{1,0:T(8,128)(2,1)}, bf16[512,1024]{1,0:T(8,128)(2,1)S(1)}, u32[]{:S(2)}, u32[]{:S(2)}) collective-permute-start(bf16[512,1024]{1,0:T(8,128)(2,1)} %get-tuple-element.54), channel_id=1, source_target_pairs={{0,2},{1,3},{2,0},{3,1},{4,6},{5,7},{6,4},{7,5},{8,10},{9,11},{10,... | collective-permute-start | bytes 3145736 | tf_op jit(solution)/shard_map/ppermute | solution.py:575
  26.3 15.3 %collective-permute-start.7 = (bf16[8,128,128]{2,1,0:T(8,128)(2,1)S(1)}, bf16[8,128,128]{2,1,0:T(8,128)(2,1)S(1)}, u32[]{:S(2)}, u32[]{:S(2)}) collective-permute-start(bf16[8,128,128]{2,1,0:T(8,128)(2,1)S(1)} %get-tuple-element.48), channel_id=1, source_target_pairs={{0,16},{4,20},{8,24},{12,28},{1,17},{5,21},{9,25},{13,29},{2,18},{... | collective-permute-start | bytes 786440 | tf_op jit(solution)/shard_map/ppermute | solution.py:528
  27.9 11.3 %collective-permute-start.4 = (bf16[2,256,128]{2,1,0:T(8,128)(2,1)S(1)}, bf16[2,256,128]{2,1,0:T(8,128)(2,1)S(1)}, u32[]{:S(2)}, u32[]{:S(2)}) collective-permute-start(bf16[2,256,128]{2,1,0:T(8,128)(2,1)S(1)} %get-tuple-element.41), channel_id=1, source_target_pairs={{0,4},{4,0},{8,12},{12,8},{16,20},{20,16},{24,28},{28,24},{1,5},{5... | collective-permute-start | bytes 393224 | tf_op jit(solution)/shard_map/ppermute | solution.py:532
  28.5 5.9 %collective-permute-start.5 = (bf16[256,128]{1,0:T(8,128)(2,1)S(1)}, bf16[256,128]{1,0:T(8,128)(2,1)S(1)}, u32[]{:S(2)}, u32[]{:S(2)}) collective-permute-start(bf16[256,128]{1,0:T(8,128)(2,1)S(1)} %get-tuple-element.42), channel_id=1, source_target_pairs={{0,8},{4,12},{8,0},{12,4},{16,24},{20,28},{24,16},{28,20},{1,9},{5... | collective-permute-start | bytes 196616 | tf_op jit(solution)/shard_map/ppermute | solution.py:532
  30.7 6.3 %collective-permute-start.6 = (bf16[256,128]{1,0:T(8,128)(2,1)S(1)}, bf16[256,128]{1,0:T(8,128)(2,1)S(1)}, u32[]{:S(2)}, u32[]{:S(2)}) collective-permute-start(bf16[256,128]{1,0:T(8,128)(2,1)S(1)} %get-tuple-element.43), channel_id=1, source_target_pairs={{0,12},{4,8},{8,4},{12,0},{16,28},{20,24},{24,20},{28,16},{1,13},{... | collective-permute-start | bytes 196616 | tf_op jit(solution)/shard_map/ppermute | solution.py:532
  34.4 8.7 %collective-permute-start.8 = (bf16[256,128]{1,0:T(8,128)(2,1)S(1)}, bf16[256,128]{1,0:T(8,128)(2,1)S(1)}, u32[]{:S(2)}, u32[]{:S(2)}) collective-permute-start(bf16[256,128]{1,0:T(8,128)(2,1)S(1)} %get-tuple-element.52), channel_id=1, source_target_pairs={{0,8},{4,12},{8,0},{12,4},{16,24},{20,28},{24,16},{28,20},{1,9},{5... | collective-permute-start | bytes 196616 | tf_op jit(solution)/shard_map/ppermute | solution.py:532
  36.9 6.3 %collective-permute-start.9 = (bf16[256,128]{1,0:T(8,128)(2,1)S(1)}, bf16[256,128]{1,0:T(8,128)(2,1)S(1)}, u32[]{:S(2)}, u32[]{:S(2)}) collective-permute-start(bf16[256,128]{1,0:T(8,128)(2,1)S(1)} %get-tuple-element.53), channel_id=1, source_target_pairs={{0,12},{4,8},{8,4},{12,0},{16,28},{20,24},{24,20},{28,16},{1,13},{... | collective-permute-start | bytes 196616 | tf_op jit(solution)/shard_map/ppermute | solution.py:532
  43.2 12.8 %copy-start = (bf16[512,2048]{1,0:T(8,128)(2,1)S(1)}, bf16[512,2048]{1,0:T(8,128)(2,1)}, u32[]{:S(2)}) copy-start(bf16[512,2048]{1,0:T(8,128)(2,1)} %own_ref.3) | copy-start | bytes 6291460
  56.5 1.6 %collective-permute-start.11 = (bf16[256,512]{1,0:T(8,128)(2,1)S(1)}, bf16[256,512]{1,0:T(8,128)(2,1)S(1)}, u32[]{:S(2)}, u32[]{:S(2)}) collective-permute-start(bf16[256,512]{1,0:T(8,128)(2,1)S(1)} %shard_map.80), channel_id=1, source_target_pairs={{0,1},{1,0},{2,3},{3,2},{4,5},{5,4},{6,7},{7,6},{8,9},{9,8},{10,11... | collective-permute-start | bytes 786440 | tf_op jit(solution)/shard_map/ppermute | solution.py:658

commit v21 on v19

--- a/solution.py
+++ b/solution.py
@@ -330,36 +330,38 @@
     for copy in copies:
         copy.wait()
     rows, columns = square_iotas()
-    current = []
-    for unit in range(units):
-        direction = rows_of(part_ref, blocks, unit, 0)
-        key = rows_of(part_ref, blocks, unit, 1)
-        query = rows_of(query_ref, blocks, unit, 0)
-        query_proj = split(jnp.where(rows >= columns, nt(query, direction), 0.0))
-        ahead = nn(jnp.concatenate(query_proj, 0), mixed_ref[unit])
-        ahead = ahead[:BLOCK] + ahead[BLOCK:]
-        inner_ref[unit] = nt(query, key) - ahead[:, HEAD_DIM:]
-        start = split(query.astype(F32) - ahead[:, :HEAD_DIM])
-        moving_ref[unit, 0] = start[0]
-        if unit % 2:
-            pair = unit // 2
-            start = split(triple(nt, start, (even_ref[pair, 0], even_ref[pair, 1])))
-        moving_ref[unit, 1] = start[0]
-        current.append(start)
-    pairs = units // 2
-    current = [
-        tuple(jnp.concatenate([current[2 * pair][part], current[2 * pair + 1][part]], 0)
-              for part in range(2))
-        for pair in range(pairs)
-    ]
-    for step in range(2, pairs + 1):
-        for pair in range(step - 1, pairs):
-            passed = pair - step + 1
-            current[pair] = split(
-                triple(nt, current[pair], (pair_ref[passed, 0], pair_ref[passed, 1]))
-            )
-            moving_ref[2 * pair, step] = current[pair][0][:BLOCK]
-            moving_ref[2 * pair + 1, step] = current[pair][0][BLOCK:]
+
+    def pair_steps(pair):
+        projs, fronts = [], []
+        for unit in (2 * pair, 2 * pair + 1):
+            direction = rows_of(part_ref, blocks, unit, 0)
+            query = rows_of(query_ref, blocks, unit, 0)
+            projs.append(split(jnp.where(rows >= columns, nt(query, direction), 0.0)))
+        yield
+        for unit in (2 * pair, 2 * pair + 1):
+            key = rows_of(part_ref, blocks, unit, 1)
+            query = rows_of(query_ref, blocks, unit, 0)
+            ahead = nn(jnp.concatenate(projs[unit % 2], 0), mixed_ref[unit])
+            ahead = ahead[:BLOCK] + ahead[BLOCK:]
+            inner_ref[unit] = nt(query, key) - ahead[:, HEAD_DIM:]
+            fronts.append(split(query.astype(F32) - ahead[:, :HEAD_DIM]))
+            moving_ref[unit, 0] = fronts[-1][0]
+        yield
+        fronts[1] = split(triple(nt, fronts[1], (even_ref[pair, 0], even_ref[pair, 1])))
+        current = tuple(
+            jnp.concatenate([fronts[0][part], fronts[1][part]], 0) for part in range(2)
+        )
+        for step in range(1, pair + 2):
+            if step > 1:
+                passed = pair - step + 1
+                current = split(
+                    triple(nt, current, (pair_ref[passed, 0], pair_ref[passed, 1]))
+                )
+            moving_ref[2 * pair, step] = current[0][:BLOCK]
+            moving_ref[2 * pair + 1, step] = current[0][BLOCK:]
+            yield
+
+    interleaved([pair_steps(pair) for pair in reversed(range(units // 2))], 1)
 
 
 def listed_block(away_ref, unit, entry):

time: 59 us -> 58.9 us (level)
  Pallas kernels: 15.9 us -> 15.2 us
    pallas_call x1, Pallas kernels: 2.38 us -> 1.73 us  [body(): call(functools.partial(queries_kernel, axes, blocks), [array((units, BLOC...]
  transfers between devices with their start and end apart: 13 -> 13, of which waited for: 2 -> 3; matrix products, arithmetic and copies ran while one was open for 0% -> 0% of each run, Pallas kernels for 18% -> 17%
where the time goes in v21:
time: 58.9 us; the launch traced here: 58.6 us
  starting transfers between devices  27.2 us (46%)
  Pallas kernels  15.2 us (26%)
  blocking collectives  10.6 us (18%)
  waiting for transfers between devices  4.54 us (8%)
  other arithmetic  0.78 us (1%)
    ppermute x4, starting transfers between devices, straight(): return lax.ppermute(value, 'ctx', pairs)  10.7 us
    all_to_all x1, blocking collectives, body(): lax.all_to_all(attended.reshape(heads * planes, blocks, *tile), axes, 0,...  10.6 us
    ppermute x5, starting transfers between devices, crossed(): return lax.ppermute(value, 'ctx', pairs) if turn else value  8.28 us
    pallas_call x1, Pallas kernels, body(): call(functools.partial(keys_kernel, blocks), [array((units, *tile)), arra...  5.82 us
    all_to_all x1, starting transfers between devices, exchange(): lax.all_to_all(value, 'ctx', 0, 0, axis_index_groups=members, tiled=True)  5.26 us
    ppermute x5, waiting for transfers between devices, crossed(): return lax.ppermute(value, 'ctx', pairs) if turn else value  3.03 us
    pallas_call x1, Pallas kernels, body(): call(functools.partial(pack_kernel, axes, cores), [array(part_shape)] + [...  2.83 us
    pallas_call x1, Pallas kernels, body(): call(functools.partial(blend_kernel, axes, before, blocks), [array((heads...  1.92 us
  transfers between devices with their start and end apart: 13, of which 3 were waited for; matrix products, arithmetic and copies ran while one was open for 0% of the time, Pallas kernels for 17%

profile of v21, /device:TPU:0, one launch (start us, length us, event | category | flops | bytes accessed | tf_op | source)
XLA Modules:
  0.0 58.6 jit_solution(3390908831352883881)
XLA Ops:
  0.0 2.8 %shard_map.73 = (bf16[4,528,128]{2,1,0:T(8,128)(2,1)}, bf16[256,128]{1,0:T(8,128)(2,1)}, bf16[256,128]{1,0:T(8,128)(2,1)}, bf16[256,128]{1,0:T(8,128)(2,1)}, bf1...) custom-call(bf16[256,512]{1,0:T(8,128)(2,1)} %d_ref.1, bf16[256,512]{1,0:T(8,128)(2,1)} %k_ref.1, f32[4,256]{1,0:T(4,128)} %rates_hbm.1, ...), custom_call_target="tpu_custom_call" | custom-call | flops 4194304 | bytes 2097152 | tf_op jit(solution)/shard_map/pallas_call | solution.py:535
  2.8 5.3 %all-to-all-start = ((bf16[4,528,128]{2,1,0:T(8,128)(2,1)}), bf16[4,528,128]{2,1,0:T(8,128)(2,1)S(1)}, u32[]{:S(2)}, u32[]{:S(2)}) async-start(bf16[4,528,128]{2,1,0:T(8,128)(2,1)} %get-tuple-element.29), calls=%async_computation | async-start | bytes 1081344 | tf_op jit(solution)/shard_map/all_to_all | solution.py:514
  8.1 4.5 %collective-permute-start = (bf16[256,128]{1,0:T(8,128)(2,1)}, bf16[256,128]{1,0:T(8,128)(2,1)S(1)}, u32[]{:S(2)}, u32[]{:S(2)}) collective-permute-start(bf16[256,128]{1,0:T(8,128)(2,1)} %get-tuple-element.34), channel_id=1, source_target_pairs={{0,16},{4,20},{8,24},{12,28},{1,17},{5,21},{9,25},{13,29},{2,18},{... | collective-permute-start | bytes 196616 | tf_op jit(solution)/shard_map/ppermute | solution.py:527
  12.6 2.8 %collective-permute-start.1 = (bf16[256,128]{1,0:T(8,128)(2,1)}, bf16[256,128]{1,0:T(8,128)(2,1)S(1)}, u32[]{:S(2)}, u32[]{:S(2)}) collective-permute-start(bf16[256,128]{1,0:T(8,128)(2,1)} %get-tuple-element.35), channel_id=1, source_target_pairs={{0,20},{4,16},{8,28},{12,24},{1,21},{5,17},{9,29},{13,25},{2,22},{... | collective-permute-start | bytes 196616 | tf_op jit(solution)/shard_map/ppermute | solution.py:527
  15.4 1.3 %collective-permute-start.2 = (bf16[256,128]{1,0:T(8,128)(2,1)}, bf16[256,128]{1,0:T(8,128)(2,1)S(1)}, u32[]{:S(2)}, u32[]{:S(2)}) collective-permute-start(bf16[256,128]{1,0:T(8,128)(2,1)} %get-tuple-element.36), channel_id=1, source_target_pairs={{0,24},{4,28},{8,16},{12,20},{1,25},{5,29},{9,17},{13,21},{2,26},{... | collective-permute-start | bytes 196616 | tf_op jit(solution)/shard_map/ppermute | solution.py:527
  16.7 2.2 %collective-permute-start.3 = (bf16[256,128]{1,0:T(8,128)(2,1)}, bf16[256,128]{1,0:T(8,128)(2,1)S(1)}, u32[]{:S(2)}, u32[]{:S(2)}) collective-permute-start(bf16[256,128]{1,0:T(8,128)(2,1)} %get-tuple-element.37), channel_id=1, source_target_pairs={{0,28},{4,24},{8,20},{12,16},{1,29},{5,25},{9,21},{13,17},{2,30},{... | collective-permute-start | bytes 196616 | tf_op jit(solution)/shard_map/ppermute | solution.py:527
  18.9 1.6 %collective-permute-start.10 = (bf16[512,1024]{1,0:T(8,128)(2,1)}, bf16[512,1024]{1,0:T(8,128)(2,1)S(1)}, u32[]{:S(2)}, u32[]{:S(2)}) collective-permute-start(bf16[512,1024]{1,0:T(8,128)(2,1)} %get-tuple-element.50), channel_id=1, source_target_pairs={{0,2},{1,3},{2,0},{3,1},{4,6},{5,7},{6,4},{7,5},{8,10},{9,11},{10,... | collective-permute-start | bytes 3145736 | tf_op jit(solution)/shard_map/ppermute | solution.py:565
  20.4 5.8 %shard_map.74 = (bf16[8,128,128]{2,1,0:T(8,128)(2,1)S(1)}, bf16[8,128,128]{2,1,0:T(8,128)(2,1)S(1)}, bf16[8,128,128]{2,1,0:T(8,128)(2,1)S(1)}, bf16[4,2,128,128]...) custom-call(bf16[4,528,128]{2,1,0:T(8,128)(2,1)S(1)} %all-to-all-don, ...), custom_call_target="tpu_custom_call" | custom-call | flops 1677721600 | bytes 2097152 | tf_op jit(solution)/shard_map/pallas_call | solution.py:568
  26.3 1.3 %collective-permute-start.7 = (bf16[8,128,128]{2,1,0:T(8,128)(2,1)S(1)}, bf16[8,128,128]{2,1,0:T(8,128)(2,1)S(1)}, u32[]{:S(2)}, u32[]{:S(2)}) collective-permute-start(bf16[8,128,128]{2,1,0:T(8,128)(2,1)S(1)} %get-tuple-element.46), channel_id=1, source_target_pairs={{0,16},{4,20},{8,24},{12,28},{1,17},{5,21},{9,25},{13,29},{2,18},{... | collective-permute-start | bytes 786440 | tf_op jit(solution)/shard_map/ppermute | solution.py:518
  27.9 0.6 %collective-permute-start.4 = (bf16[2,256,128]{2,1,0:T(8,128)(2,1)S(1)}, bf16[2,256,128]{2,1,0:T(8,128)(2,1)S(1)}, u32[]{:S(2)}, u32[]{:S(2)}) collective-permute-start(bf16[2,256,128]{2,1,0:T(8,128)(2,1)S(1)} %get-tuple-element.39), channel_id=1, source_target_pairs={{0,4},{4,0},{8,12},{12,8},{16,20},{20,16},{24,28},{28,24},{1,5},{5... | collective-permute-start | bytes 393224 | tf_op jit(solution)/shard_map/ppermute | solution.py:522
  28.5 2.2 %collective-permute-start.5 = (bf16[256,128]{1,0:T(8,128)(2,1)S(1)}, bf16[256,128]{1,0:T(8,128)(2,1)S(1)}, u32[]{:S(2)}, u32[]{:S(2)}) collective-permute-start(bf16[256,128]{1,0:T(8,128)(2,1)S(1)} %get-tuple-element.40), channel_id=1, source_target_pairs={{0,8},{4,12},{8,0},{12,4},{16,24},{20,28},{24,16},{28,20},{1,9},{5... | collective-permute-start | bytes 196616 | tf_op jit(solution)/shard_map/ppermute | solution.py:522
  30.7 0.8 %collective-permute-start.6 = (bf16[256,128]{1,0:T(8,128)(2,1)S(1)}, bf16[256,128]{1,0:T(8,128)(2,1)S(1)}, u32[]{:S(2)}, u32[]{:S(2)}) collective-permute-start(bf16[256,128]{1,0:T(8,128)(2,1)S(1)} %get-tuple-element.41), channel_id=1, source_target_pairs={{0,12},{4,8},{8,4},{12,0},{16,28},{20,24},{24,20},{28,16},{1,13},{... | collective-permute-start | bytes 196616 | tf_op jit(solution)/shard_map/ppermute | solution.py:522
  31.4 3.0 %collective-permute-done.5.refs_2_ = bf16[256,128]{1,0:T(8,128)(2,1)S(1)} collective-permute-done((bf16[256,128]{1,0:T(8,128)(2,1)S(1)}, bf16[256,128]{1,0:T(8,128)(2,1)S(1)}, u32[]{:S(2)}, u32[]{:S(2)}) %collective-permute-start.5) | collective-permute-done | bytes 65568 | tf_op jit(solution)/shard_map/ppermute | solution.py:522
  34.4 2.5 %collective-permute-start.8 = (bf16[256,128]{1,0:T(8,128)(2,1)S(1)}, bf16[256,128]{1,0:T(8,128)(2,1)S(1)}, u32[]{:S(2)}, u32[]{:S(2)}) collective-permute-start(bf16[256,128]{1,0:T(8,128)(2,1)S(1)} %get-tuple-element.48), channel_id=1, source_target_pairs={{0,8},{4,12},{8,0},{12,4},{16,24},{20,28},{24,16},{28,20},{1,9},{5... | collective-permute-start | bytes 196616 | tf_op jit(solution)/shard_map/ppermute | solution.py:522
  36.9 2.2 %collective-permute-start.9 = (bf16[256,128]{1,0:T(8,128)(2,1)S(1)}, bf16[256,128]{1,0:T(8,128)(2,1)S(1)}, u32[]{:S(2)}, u32[]{:S(2)}) collective-permute-start(bf16[256,128]{1,0:T(8,128)(2,1)S(1)} %get-tuple-element.49), channel_id=1, source_target_pairs={{0,12},{4,8},{8,4},{12,0},{16,28},{20,24},{24,20},{28,16},{1,13},{... | collective-permute-start | bytes 196616 | tf_op jit(solution)/shard_map/ppermute | solution.py:522
  39.2 1.7 %shard_map.76 = (f32[8,128,128]{2,1,0:T(8,128)S(1)}, bf16[8,5,128,128]{3,2,1,0:T(8,128)(2,1)S(1)}) custom-call(bf16[4,528,128]{2,1,0:T(8,128)(2,1)S(1)} %all-to-all-done.part_ref, bf16[8,128,256]{2,1,0:T(8,128)(2,1)S(1)} %get-tuple-element.31.mixed_ref, bf16[4,2,128,128]{3,2,1,0:T(8,128)(2,1)S(1)} %get-tuple-element.32.even_ref, ...), custom_call_target="tpu_custom_call" | custom-call | bytes 2097152 | tf_op jit(solution)/shard_map/pallas_call | solution.py:598
  40.9 1.8 %shard_map.77.weights_ref = bf16[8,128,512]{2,1,0:T(8,128)(2,1)S(1)} custom-call(s32[8,128]{1,0:T(8,128)S(1)} %get-tuple-element.30.refs_4_.away_ref, bf16[8,5,128,128]{3,2,1,0:T(8,128)(2,1)S(1)} %get-tuple-element.42.moving_ref, f32[8,128,128]{2,1,0:T(8,128)S(1)} %get-tuple-element.43.inner_ref, bf16[8,128,128]{2,1,0:T(8,128)(2,1)S(1)} %get-tuple-element.44.end_ref, ...), custom_call_target="tpu_custom_call" | custom-call | bytes 2097152 | tf_op jit(solution)/shard_map/pallas_call | solution.py:605
  42.8 0.4 collective-permute-done.10.refs_8_
  43.2 1.9 %shard_map.78 = (bf16[4,2,2,128,128]{4,3,2,1,0:T(8,128)(2,1)S(1)}, bf16[512,1024]{1,0:T(8,128)(2,1)S(1)}) custom-call(s32[8,128]{1,0:T(8,128)S(1)} %get-tuple-element.30.refs_4_.away_ref, bf16[8,128,512]{2,1,0:T(8,128)(2,1)S(1)} %shard_map.77.weights_ref, bf16[256,128]{1,0:T(8,128)(2,1)S(1)} %get-tuple-element.47.refs_0_, ...), custom_call_target="tpu_custom_call" | custom-call | bytes 2097152 | tf_op jit(solution)/shard_map/pallas_call | solution.py:611
  45.1 10.6 %all_to_all.10 = bf16[8,2,128,128]{3,2,1,0:T(8,128)(2,1)S(1)} all-to-all(bf16[8,2,128,128]{3,2,1,0:T(8,128)(2,1)S(1)} %bitcast.4), channel_id=1, replica_groups={{0,2,4,6,8,10,12,14},{1,3,5,7,9,11,13,15},{16,18,20,22,24,26,28,30},{17..., dimensions={0} | all-to-all | bytes 1048576 | tf_op jit(solution)/shard_map/all_to_all | solution.py:632
  55.7 0.4 shard_map.80
  56.3 0.4 shard_map.79
  56.7 1.1 %collective-permute-done.11 = bf16[256,512]{1,0:T(8,128)(2,1)S(1)} collective-permute-done((bf16[256,512]{1,0:T(8,128)(2,1)S(1)}, bf16[256,512]{1,0:T(8,128)(2,1)S(1)}, u32[]{:S(2)}, u32[]{:S(2)}) %collective-permute-start.11) | collective-permute-done | bytes 262176 | tf_op jit(solution)/shard_map/ppermute | solution.py:645
  57.8 0.8 %add_convert_fusion = bf16[256,512]{1,0:T(8,128)(2,1)} fusion(f32[256,512]{1,0:T(8,128)S(1)} %shard_map.79, bf16[256,512]{1,0:T(8,128)(2,1)S(1)} %collective-permute-done.11), kind=kLoop, calls=%fused_computation | loop fusion | flops 393216 | bytes 1048576 | tf_op jit(solution)/shard_map/convert_element_type | solution.py:646
  (18 shorter events, 0.3 us)
Async XLA Ops:
  2.8 17.6 %all-to-all-start = ((bf16[4,528,128]{2,1,0:T(8,128)(2,1)}), bf16[4,528,128]{2,1,0:T(8,128)(2,1)S(1)}, u32[]{:S(2)}, u32[]{:S(2)}) async-start(bf16[4,528,128]{2,1,0:T(8,128)(2,1)} %get-tuple-element.29), calls=%async_computation | async-start | bytes 1081344 | tf_op jit(solution)/shard_map/all_to_all | solution.py:514
  8.1 18.2 %collective-permute-start = (bf16[256,128]{1,0:T(8,128)(2,1)}, bf16[256,128]{1,0:T(8,128)(2,1)S(1)}, u32[]{:S(2)}, u32[]{:S(2)}) collective-permute-start(bf16[256,128]{1,0:T(8,128)(2,1)} %get-tuple-element.34), channel_id=1, source_target_pairs={{0,16},{4,20},{8,24},{12,28},{1,17},{5,21},{9,25},{13,29},{2,18},{... | collective-permute-start | bytes 196616 | tf_op jit(solution)/shard_map/ppermute | solution.py:527
  12.6 15.0 %collective-permute-start.1 = (bf16[256,128]{1,0:T(8,128)(2,1)}, bf16[256,128]{1,0:T(8,128)(2,1)S(1)}, u32[]{:S(2)}, u32[]{:S(2)}) collective-permute-start(bf16[256,128]{1,0:T(8,128)(2,1)} %get-tuple-element.35), channel_id=1, source_target_pairs={{0,20},{4,16},{8,28},{12,24},{1,21},{5,17},{9,29},{13,25},{2,22},{... | collective-permute-start | bytes 196616 | tf_op jit(solution)/shard_map/ppermute | solution.py:527
  15.4 12.2 %collective-permute-start.2 = (bf16[256,128]{1,0:T(8,128)(2,1)}, bf16[256,128]{1,0:T(8,128)(2,1)S(1)}, u32[]{:S(2)}, u32[]{:S(2)}) collective-permute-start(bf16[256,128]{1,0:T(8,128)(2,1)} %get-tuple-element.36), channel_id=1, source_target_pairs={{0,24},{4,28},{8,16},{12,20},{1,25},{5,29},{9,17},{13,21},{2,26},{... | collective-permute-start | bytes 196616 | tf_op jit(solution)/shard_map/ppermute | solution.py:527
  16.7 11.0 %collective-permute-start.3 = (bf16[256,128]{1,0:T(8,128)(2,1)}, bf16[256,128]{1,0:T(8,128)(2,1)S(1)}, u32[]{:S(2)}, u32[]{:S(2)}) collective-permute-start(bf16[256,128]{1,0:T(8,128)(2,1)} %get-tuple-element.37), channel_id=1, source_target_pairs={{0,28},{4,24},{8,20},{12,16},{1,29},{5,25},{9,21},{13,17},{2,30},{... | collective-permute-start | bytes 196616 | tf_op jit(solution)/shard_map/ppermute | solution.py:527
  18.9 8.8 %copy-start.1 = (bf16[256,512]{1,0:T(8,128)(2,1)S(1)}, bf16[256,512]{1,0:T(8,128)(2,1)}, u32[]{:S(2)}) copy-start(bf16[256,512]{1,0:T(8,128)(2,1)} %values_ref.3) | copy-start | bytes 786436
  18.9 8.8 %copy-start.2 = (bf16[256,512]{1,0:T(8,128)(2,1)S(1)}, bf16[256,512]{1,0:T(8,128)(2,1)}, u32[]{:S(2)}) copy-start(bf16[256,512]{1,0:T(8,128)(2,1)} %queries_ref.1) | copy-start | bytes 786436
  18.9 24.3 %collective-permute-start.10 = (bf16[512,1024]{1,0:T(8,128)(2,1)}, bf16[512,1024]{1,0:T(8,128)(2,1)S(1)}, u32[]{:S(2)}, u32[]{:S(2)}) collective-permute-start(bf16[512,1024]{1,0:T(8,128)(2,1)} %get-tuple-element.50), channel_id=1, source_target_pairs={{0,2},{1,3},{2,0},{3,1},{4,6},{5,7},{6,4},{7,5},{8,10},{9,11},{10,... | collective-permute-start | bytes 3145736 | tf_op jit(solution)/shard_map/ppermute | solution.py:565
  26.3 14.6 %collective-permute-start.7 = (bf16[8,128,128]{2,1,0:T(8,128)(2,1)S(1)}, bf16[8,128,128]{2,1,0:T(8,128)(2,1)S(1)}, u32[]{:S(2)}, u32[]{:S(2)}) collective-permute-start(bf16[8,128,128]{2,1,0:T(8,128)(2,1)S(1)} %get-tuple-element.46), channel_id=1, source_target_pairs={{0,16},{4,20},{8,24},{12,28},{1,17},{5,21},{9,25},{13,29},{2,18},{... | collective-permute-start | bytes 786440 | tf_op jit(solution)/shard_map/ppermute | solution.py:518
  27.9 11.3 %collective-permute-start.4 = (bf16[2,256,128]{2,1,0:T(8,128)(2,1)S(1)}, bf16[2,256,128]{2,1,0:T(8,128)(2,1)S(1)}, u32[]{:S(2)}, u32[]{:S(2)}) collective-permute-start(bf16[2,256,128]{2,1,0:T(8,128)(2,1)S(1)} %get-tuple-element.39), channel_id=1, source_target_pairs={{0,4},{4,0},{8,12},{12,8},{16,20},{20,16},{24,28},{28,24},{1,5},{5... | collective-permute-start | bytes 393224 | tf_op jit(solution)/shard_map/ppermute | solution.py:522
  28.5 5.9 %collective-permute-start.5 = (bf16[256,128]{1,0:T(8,128)(2,1)S(1)}, bf16[256,128]{1,0:T(8,128)(2,1)S(1)}, u32[]{:S(2)}, u32[]{:S(2)}) collective-permute-start(bf16[256,128]{1,0:T(8,128)(2,1)S(1)} %get-tuple-element.40), channel_id=1, source_target_pairs={{0,8},{4,12},{8,0},{12,4},{16,24},{20,28},{24,16},{28,20},{1,9},{5... | collective-permute-start | bytes 196616 | tf_op jit(solution)/shard_map/ppermute | solution.py:522
  30.7 6.3 %collective-permute-start.6 = (bf16[256,128]{1,0:T(8,128)(2,1)S(1)}, bf16[256,128]{1,0:T(8,128)(2,1)S(1)}, u32[]{:S(2)}, u32[]{:S(2)}) collective-permute-start(bf16[256,128]{1,0:T(8,128)(2,1)S(1)} %get-tuple-element.41), channel_id=1, source_target_pairs={{0,12},{4,8},{8,4},{12,0},{16,28},{20,24},{24,20},{28,16},{1,13},{... | collective-permute-start | bytes 196616 | tf_op jit(solution)/shard_map/ppermute | solution.py:522
  34.4 8.3 %collective-permute-start.8 = (bf16[256,128]{1,0:T(8,128)(2,1)S(1)}, bf16[256,128]{1,0:T(8,128)(2,1)S(1)}, u32[]{:S(2)}, u32[]{:S(2)}) collective-permute-start(bf16[256,128]{1,0:T(8,128)(2,1)S(1)} %get-tuple-element.48), channel_id=1, source_target_pairs={{0,8},{4,12},{8,0},{12,4},{16,24},{20,28},{24,16},{28,20},{1,9},{5... | collective-permute-start | bytes 196616 | tf_op jit(solution)/shard_map/ppermute | solution.py:522
  36.9 5.9 %collective-permute-start.9 = (bf16[256,128]{1,0:T(8,128)(2,1)S(1)}, bf16[256,128]{1,0:T(8,128)(2,1)S(1)}, u32[]{:S(2)}, u32[]{:S(2)}) collective-permute-start(bf16[256,128]{1,0:T(8,128)(2,1)S(1)} %get-tuple-element.49), channel_id=1, source_target_pairs={{0,12},{4,8},{8,4},{12,0},{16,28},{20,24},{24,20},{28,16},{1,13},{... | collective-permute-start | bytes 196616 | tf_op jit(solution)/shard_map/ppermute | solution.py:522
  42.8 13.0 %copy-start = (bf16[512,2048]{1,0:T(8,128)(2,1)S(1)}, bf16[512,2048]{1,0:T(8,128)(2,1)}, u32[]{:S(2)}) copy-start(bf16[512,2048]{1,0:T(8,128)(2,1)} %own_ref.3) | copy-start | bytes 6291460
  56.2 1.6 %collective-permute-start.11 = (bf16[256,512]{1,0:T(8,128)(2,1)S(1)}, bf16[256,512]{1,0:T(8,128)(2,1)S(1)}, u32[]{:S(2)}, u32[]{:S(2)}) collective-permute-start(bf16[256,512]{1,0:T(8,128)(2,1)S(1)} %shard_map.80), channel_id=1, source_target_pairs={{0,1},{1,0},{2,3},{3,2},{4,5},{5,4},{6,7},{7,6},{8,9},{9,8},{10,11... | collective-permute-start | bytes 786440 | tf_op jit(solution)/shard_map/ppermute | solution.py:645

commit v22 on v21

--- a/solution.py
+++ b/solution.py
@@ -320,15 +320,10 @@
 def queries_kernel(axes, blocks, part_ref, mixed_ref, even_ref, pair_ref, *refs):
     heads = part_ref.shape[0]
     units = heads * blocks
-    inner_ref, moving_ref, query_ref, sems = refs[heads:]
+    inner_ref, moving_ref, query_ref = refs[heads:]
     place = lax.rem(lax.axis_index(axes[0]), heads)
-    copies = fetched(
-        [refs[turn].at[0] if turn == 1 else refs[turn] for turn in range(heads)],
-        [query_ref.at[lax.bitwise_xor(place, turn)] for turn in range(heads)],
-        sems,
-    )
-    for copy in copies:
-        copy.wait()
+    for turn in range(heads):
+        query_ref[lax.bitwise_xor(place, turn)] = refs[1][0] if turn == 1 else refs[turn][...]
     rows, columns = square_iotas()
 
     def pair_steps(pair):
@@ -411,25 +406,20 @@
 def blend_kernel(axes, before, blocks, away_ref, weights_ref, *refs):
     units = weights_ref.shape[0]
     heads = units // blocks
-    count = (len(refs) - 4 - heads * (1 + before)) // 2
+    count = (len(refs) - 3 - heads * (1 + before)) // 2
     arrived = refs[:heads * (1 + before)]
-    out_ref, (values_ref, value_sems, sems) = refs[-4 - count], refs[-3:]
+    out_ref, (values_ref, sems) = refs[-3 - count], refs[-2:]
+    copies = fetched(
+        refs[heads * (1 + before):heads * (1 + before) + count], refs[-2 - count:-2], sems
+    )
     place = lax.rem(lax.axis_index(axes[0]), heads)
-    value_copies = []
     for kind in range(1 + before):
         for turn in range(heads):
             start = pl.multiple_of(lax.bitwise_xor(place, turn) * blocks * BLOCK, BLOCK)
             source = arrived[kind * heads + turn]
-            value_copies += fetched(
-                [source if kind or turn != 1 else source.at[1]],
-                [values_ref.at[kind, pl.ds(start, blocks * BLOCK)]],
-                value_sems.at[kind, pl.ds(turn, 1)],
+            values_ref[kind, pl.ds(start, blocks * BLOCK)] = (
+                source[...] if kind or turn != 1 else source[1]
             )
-    copies = fetched(
-        refs[heads * (1 + before):heads * (1 + before) + count], refs[-3 - count:-3], sems
-    )
-    for copy in value_copies:
-        copy.wait()
 
     def value_of(kind, block):
         return values_ref[kind, pl.ds(pl.multiple_of(block * BLOCK, BLOCK), BLOCK)]
@@ -598,9 +588,9 @@
     inner, moving = call(
         functools.partial(queries_kernel, axes, blocks),
         [array((units, BLOCK, BLOCK), F32), array((units, pairs + 1, *tile))],
-        [VMEM] * 4 + [ANY] * heads,
+        [VMEM] * (4 + heads),
         0,
-        [pltpu.VMEM((heads, tokens, HEAD_DIM), BF16), pltpu.SemaphoreType.DMA((heads,))],
+        [pltpu.VMEM((heads, tokens, HEAD_DIM), BF16)],
     )(parts, mixed, even, pair_map, *query_parts)
     weights = call(
         functools.partial(weights_kernel, before),
@@ -611,11 +601,10 @@
     attended, *weight_parts = call(
         functools.partial(blend_kernel, axes, before, blocks),
         [array((heads, planes, blocks, *tile))] + [array(part.shape) for part in weight_parts],
-        [SMEM, VMEM] + [ANY] * (heads * (1 + before) + len(weight_parts)),
+        [SMEM] + [VMEM] * (1 + heads * (1 + before)) + [ANY] * len(weight_parts),
         0,
         [
             pltpu.VMEM((1 + before, units * BLOCK, HEAD_DIM), BF16),
-            pltpu.SemaphoreType.DMA((1 + before, heads)),
             pltpu.SemaphoreType.DMA((planes,)),
         ],
     )(away, weights, *own_parts, *value_parts, *weight_parts)

time: 58.9 us -> 58.1 us (0.986)
  Pallas kernels: 15.2 us -> 14.1 us
    pallas_call x1, Pallas kernels: 1.92 us -> 1.17 us  [body(): call(functools.partial(blend_kernel, axes, before, blocks), [array((heads...]
where the time goes in v22:
time: 58.1 us; the launch traced here: 57.8 us
  starting transfers between devices  27.2 us (47%)
  Pallas kernels  14.1 us (24%)
  blocking collectives  10.6 us (18%)
  waiting for transfers between devices  4.92 us (8%)
  other arithmetic  0.78 us (1%)
    ppermute x4, starting transfers between devices, straight(): return lax.ppermute(value, 'ctx', pairs)  10.7 us
    all_to_all x1, blocking collectives, body(): lax.all_to_all(attended.reshape(heads * planes, blocks, *tile), axes, 0,...  10.6 us
    ppermute x5, starting transfers between devices, crossed(): return lax.ppermute(value, 'ctx', pairs) if turn else value  8.28 us
    pallas_call x1, Pallas kernels, body(): call(functools.partial(keys_kernel, blocks), [array((units, *tile)), arra...  5.82 us
    all_to_all x1, starting transfers between devices, exchange(): lax.all_to_all(value, 'ctx', 0, 0, axis_index_groups=members, tiled=True)  5.26 us
    ppermute x5, waiting for transfers between devices, crossed(): return lax.ppermute(value, 'ctx', pairs) if turn else value  3.03 us
    pallas_call x1, Pallas kernels, body(): call(functools.partial(pack_kernel, axes, cores), [array(part_shape)] + [...  2.83 us
    pallas_call x1, Pallas kernels, body(): call(functools.partial(weights_kernel, before), array((units, BLOCK, TOPK...  1.84 us
  transfers between devices with their start and end apart: 13, of which 3 were waited for; matrix products, arithmetic and copies ran while one was open for 0% of the time, Pallas kernels for 17%

profile of v22, /device:TPU:0, one launch (start us, length us, event | category | flops | bytes accessed | tf_op | source)
XLA Modules:
  0.0 57.8 jit_solution(16042250564894233357)
XLA Ops:
  0.0 2.8 %shard_map.73 = (bf16[4,528,128]{2,1,0:T(8,128)(2,1)}, bf16[256,128]{1,0:T(8,128)(2,1)}, bf16[256,128]{1,0:T(8,128)(2,1)}, bf16[256,128]{1,0:T(8,128)(2,1)}, bf1...) custom-call(bf16[256,512]{1,0:T(8,128)(2,1)} %d_ref.1, bf16[256,512]{1,0:T(8,128)(2,1)} %k_ref.1, f32[4,256]{1,0:T(4,128)} %rates_hbm.1, ...), custom_call_target="tpu_custom_call" | custom-call | flops 4194304 | bytes 2097152 | tf_op jit(solution)/shard_map/pallas_call | solution.py:525
  2.8 5.3 %all-to-all-start = ((bf16[4,528,128]{2,1,0:T(8,128)(2,1)}), bf16[4,528,128]{2,1,0:T(8,128)(2,1)S(1)}, u32[]{:S(2)}, u32[]{:S(2)}) async-start(bf16[4,528,128]{2,1,0:T(8,128)(2,1)} %get-tuple-element.29), calls=%async_computation | async-start | bytes 1081344 | tf_op jit(solution)/shard_map/all_to_all | solution.py:504
  8.1 4.5 %collective-permute-start = (bf16[256,128]{1,0:T(8,128)(2,1)}, bf16[256,128]{1,0:T(8,128)(2,1)S(1)}, u32[]{:S(2)}, u32[]{:S(2)}) collective-permute-start(bf16[256,128]{1,0:T(8,128)(2,1)} %get-tuple-element.34), channel_id=1, source_target_pairs={{0,16},{4,20},{8,24},{12,28},{1,17},{5,21},{9,25},{13,29},{2,18},{... | collective-permute-start | bytes 196616 | tf_op jit(solution)/shard_map/ppermute | solution.py:517
  12.6 2.8 %collective-permute-start.1 = (bf16[256,128]{1,0:T(8,128)(2,1)}, bf16[256,128]{1,0:T(8,128)(2,1)S(1)}, u32[]{:S(2)}, u32[]{:S(2)}) collective-permute-start(bf16[256,128]{1,0:T(8,128)(2,1)} %get-tuple-element.35), channel_id=1, source_target_pairs={{0,20},{4,16},{8,28},{12,24},{1,21},{5,17},{9,29},{13,25},{2,22},{... | collective-permute-start | bytes 196616 | tf_op jit(solution)/shard_map/ppermute | solution.py:517
  15.4 1.3 %collective-permute-start.2 = (bf16[256,128]{1,0:T(8,128)(2,1)}, bf16[256,128]{1,0:T(8,128)(2,1)S(1)}, u32[]{:S(2)}, u32[]{:S(2)}) collective-permute-start(bf16[256,128]{1,0:T(8,128)(2,1)} %get-tuple-element.36), channel_id=1, source_target_pairs={{0,24},{4,28},{8,16},{12,20},{1,25},{5,29},{9,17},{13,21},{2,26},{... | collective-permute-start | bytes 196616 | tf_op jit(solution)/shard_map/ppermute | solution.py:517
  16.7 2.2 %collective-permute-start.3 = (bf16[256,128]{1,0:T(8,128)(2,1)}, bf16[256,128]{1,0:T(8,128)(2,1)S(1)}, u32[]{:S(2)}, u32[]{:S(2)}) collective-permute-start(bf16[256,128]{1,0:T(8,128)(2,1)} %get-tuple-element.37), channel_id=1, source_target_pairs={{0,28},{4,24},{8,20},{12,16},{1,29},{5,25},{9,21},{13,17},{2,30},{... | collective-permute-start | bytes 196616 | tf_op jit(solution)/shard_map/ppermute | solution.py:517
  18.9 1.6 %collective-permute-start.10 = (bf16[512,1024]{1,0:T(8,128)(2,1)}, bf16[512,1024]{1,0:T(8,128)(2,1)S(1)}, u32[]{:S(2)}, u32[]{:S(2)}) collective-permute-start(bf16[512,1024]{1,0:T(8,128)(2,1)} %get-tuple-element.50), channel_id=1, source_target_pairs={{0,2},{1,3},{2,0},{3,1},{4,6},{5,7},{6,4},{7,5},{8,10},{9,11},{10,... | collective-permute-start | bytes 3145736 | tf_op jit(solution)/shard_map/ppermute | solution.py:555
  20.4 5.8 %shard_map.74 = (bf16[8,128,128]{2,1,0:T(8,128)(2,1)S(1)}, bf16[8,128,128]{2,1,0:T(8,128)(2,1)S(1)}, bf16[8,128,128]{2,1,0:T(8,128)(2,1)S(1)}, bf16[4,2,128,128]...) custom-call(bf16[4,528,128]{2,1,0:T(8,128)(2,1)S(1)} %all-to-all-don, ...), custom_call_target="tpu_custom_call" | custom-call | flops 1677721600 | bytes 2097152 | tf_op jit(solution)/shard_map/pallas_call | solution.py:558
  26.3 1.3 %collective-permute-start.7 = (bf16[8,128,128]{2,1,0:T(8,128)(2,1)S(1)}, bf16[8,128,128]{2,1,0:T(8,128)(2,1)S(1)}, u32[]{:S(2)}, u32[]{:S(2)}) collective-permute-start(bf16[8,128,128]{2,1,0:T(8,128)(2,1)S(1)} %get-tuple-element.46), channel_id=1, source_target_pairs={{0,16},{4,20},{8,24},{12,28},{1,17},{5,21},{9,25},{13,29},{2,18},{... | collective-permute-start | bytes 786440 | tf_op jit(solution)/shard_map/ppermute | solution.py:508
  27.9 0.6 %collective-permute-start.4 = (bf16[2,256,128]{2,1,0:T(8,128)(2,1)S(1)}, bf16[2,256,128]{2,1,0:T(8,128)(2,1)S(1)}, u32[]{:S(2)}, u32[]{:S(2)}) collective-permute-start(bf16[2,256,128]{2,1,0:T(8,128)(2,1)S(1)} %get-tuple-element.39), channel_id=1, source_target_pairs={{0,4},{4,0},{8,12},{12,8},{16,20},{20,16},{24,28},{28,24},{1,5},{5... | collective-permute-start | bytes 393224 | tf_op jit(solution)/shard_map/ppermute | solution.py:512
  28.5 2.2 %collective-permute-start.5 = (bf16[256,128]{1,0:T(8,128)(2,1)S(1)}, bf16[256,128]{1,0:T(8,128)(2,1)S(1)}, u32[]{:S(2)}, u32[]{:S(2)}) collective-permute-start(bf16[256,128]{1,0:T(8,128)(2,1)S(1)} %get-tuple-element.40), channel_id=1, source_target_pairs={{0,8},{4,12},{8,0},{12,4},{16,24},{20,28},{24,16},{28,20},{1,9},{5... | collective-permute-start | bytes 196616 | tf_op jit(solution)/shard_map/ppermute | solution.py:512
  30.7 0.8 %collective-permute-start.6 = (bf16[256,128]{1,0:T(8,128)(2,1)S(1)}, bf16[256,128]{1,0:T(8,128)(2,1)S(1)}, u32[]{:S(2)}, u32[]{:S(2)}) collective-permute-start(bf16[256,128]{1,0:T(8,128)(2,1)S(1)} %get-tuple-element.41), channel_id=1, source_target_pairs={{0,12},{4,8},{8,4},{12,0},{16,28},{20,24},{24,20},{28,16},{1,13},{... | collective-permute-start | bytes 196616 | tf_op jit(solution)/shard_map/ppermute | solution.py:512
  31.4 3.0 %collective-permute-done.5.refs_2_ = bf16[256,128]{1,0:T(8,128)(2,1)S(1)} collective-permute-done((bf16[256,128]{1,0:T(8,128)(2,1)S(1)}, bf16[256,128]{1,0:T(8,128)(2,1)S(1)}, u32[]{:S(2)}, u32[]{:S(2)}) %collective-permute-start.5) | collective-permute-done | bytes 65568 | tf_op jit(solution)/shard_map/ppermute | solution.py:512
  34.4 2.5 %collective-permute-start.8 = (bf16[256,128]{1,0:T(8,128)(2,1)S(1)}, bf16[256,128]{1,0:T(8,128)(2,1)S(1)}, u32[]{:S(2)}, u32[]{:S(2)}) collective-permute-start(bf16[256,128]{1,0:T(8,128)(2,1)S(1)} %get-tuple-element.48), channel_id=1, source_target_pairs={{0,8},{4,12},{8,0},{12,4},{16,24},{20,28},{24,16},{28,20},{1,9},{5... | collective-permute-start | bytes 196616 | tf_op jit(solution)/shard_map/ppermute | solution.py:512
  36.9 2.2 %collective-permute-start.9 = (bf16[256,128]{1,0:T(8,128)(2,1)S(1)}, bf16[256,128]{1,0:T(8,128)(2,1)S(1)}, u32[]{:S(2)}, u32[]{:S(2)}) collective-permute-start(bf16[256,128]{1,0:T(8,128)(2,1)S(1)} %get-tuple-element.49), channel_id=1, source_target_pairs={{0,12},{4,8},{8,4},{12,0},{16,28},{20,24},{24,20},{28,16},{1,13},{... | collective-permute-start | bytes 196616 | tf_op jit(solution)/shard_map/ppermute | solution.py:512
  39.2 1.4 %shard_map.76 = (f32[8,128,128]{2,1,0:T(8,128)S(1)}, bf16[8,5,128,128]{3,2,1,0:T(8,128)(2,1)S(1)}) custom-call(bf16[4,528,128]{2,1,0:T(8,128)(2,1)S(1)} %all-to-all-done.part_ref, bf16[8,128,256]{2,1,0:T(8,128)(2,1)S(1)} %get-tuple-element.31.mixed_ref, bf16[4,2,128,128]{3,2,1,0:T(8,128)(2,1)S(1)} %get-tuple-element.32.even_ref, ...), custom_call_target="tpu_custom_call" | custom-call | bytes 2097152 | tf_op jit(solution)/shard_map/pallas_call | solution.py:588
  40.5 1.8 %shard_map.77.weights_ref = bf16[8,128,512]{2,1,0:T(8,128)(2,1)S(1)} custom-call(s32[8,128]{1,0:T(8,128)S(1)} %get-tuple-element.30.refs_4_.away_ref, bf16[8,5,128,128]{3,2,1,0:T(8,128)(2,1)S(1)} %get-tuple-element.42.moving_ref, f32[8,128,128]{2,1,0:T(8,128)S(1)} %get-tuple-element.43.inner_ref, bf16[8,128,128]{2,1,0:T(8,128)(2,1)S(1)} %get-tuple-element.44.end_ref, ...), custom_call_target="tpu_custom_call" | custom-call | bytes 2097152 | tf_op jit(solution)/shard_map/pallas_call | solution.py:595
  42.4 0.8 %collective-permute-done.10.refs_8_ = bf16[512,1024]{1,0:T(8,128)(2,1)S(1)} collective-permute-done((bf16[512,1024]{1,0:T(8,128)(2,1)}, bf16[512,1024]{1,0:T(8,128)(2,1)S(1)}, u32[]{:S(2)}, u32[]{:S(2)}) %collective-permute-start.10) | collective-permute-done | bytes 1048608 | tf_op jit(solution)/shard_map/ppermute | solution.py:555
  43.2 1.2 %shard_map.78 = (bf16[4,2,2,128,128]{4,3,2,1,0:T(8,128)(2,1)S(1)}, bf16[512,1024]{1,0:T(8,128)(2,1)S(1)}) custom-call(s32[8,128]{1,0:T(8,128)S(1)} %get-tuple-element.30.refs_4_.away_ref, bf16[8,128,512]{2,1,0:T(8,128)(2,1)S(1)} %shard_map.77.weights_ref, bf16[256,128]{1,0:T(8,128)(2,1)S(1)} %get-tuple-element.47.refs_0_, ...), custom_call_target="tpu_custom_call" | custom-call | bytes 2097152 | tf_op jit(solution)/shard_map/pallas_call | solution.py:601
  44.4 10.6 %all_to_all.10 = bf16[8,2,128,128]{3,2,1,0:T(8,128)(2,1)S(1)} all-to-all(bf16[8,2,128,128]{3,2,1,0:T(8,128)(2,1)S(1)} %bitcast.4), channel_id=1, replica_groups={{0,2,4,6,8,10,12,14},{1,3,5,7,9,11,13,15},{16,18,20,22,24,26,28,30},{17..., dimensions={0} | all-to-all | bytes 1048576 | tf_op jit(solution)/shard_map/all_to_all | solution.py:621
  55.0 0.4 shard_map.80
  55.5 0.4 shard_map.79
  56.0 1.1 %collective-permute-done.11 = bf16[256,512]{1,0:T(8,128)(2,1)S(1)} collective-permute-done((bf16[256,512]{1,0:T(8,128)(2,1)S(1)}, bf16[256,512]{1,0:T(8,128)(2,1)S(1)}, u32[]{:S(2)}, u32[]{:S(2)}) %collective-permute-start.11) | collective-permute-done | bytes 262176 | tf_op jit(solution)/shard_map/ppermute | solution.py:634
  57.0 0.8 %add_convert_fusion = bf16[256,512]{1,0:T(8,128)(2,1)} fusion(f32[256,512]{1,0:T(8,128)S(1)} %shard_map.79, bf16[256,512]{1,0:T(8,128)(2,1)S(1)} %collective-permute-done.11), kind=kLoop, calls=%fused_computation | loop fusion | flops 393216 | bytes 1048576 | tf_op jit(solution)/shard_map/convert_element_type | solution.py:635
  (18 shorter events, 0.3 us)
Async XLA Ops:
  2.8 17.6 %all-to-all-start = ((bf16[4,528,128]{2,1,0:T(8,128)(2,1)}), bf16[4,528,128]{2,1,0:T(8,128)(2,1)S(1)}, u32[]{:S(2)}, u32[]{:S(2)}) async-start(bf16[4,528,128]{2,1,0:T(8,128)(2,1)} %get-tuple-element.29), calls=%async_computation | async-start | bytes 1081344 | tf_op jit(solution)/shard_map/all_to_all | solution.py:504
  8.1 18.2 %collective-permute-start = (bf16[256,128]{1,0:T(8,128)(2,1)}, bf16[256,128]{1,0:T(8,128)(2,1)S(1)}, u32[]{:S(2)}, u32[]{:S(2)}) collective-permute-start(bf16[256,128]{1,0:T(8,128)(2,1)} %get-tuple-element.34), channel_id=1, source_target_pairs={{0,16},{4,20},{8,24},{12,28},{1,17},{5,21},{9,25},{13,29},{2,18},{... | collective-permute-start | bytes 196616 | tf_op jit(solution)/shard_map/ppermute | solution.py:517
  12.6 15.0 %collective-permute-start.1 = (bf16[256,128]{1,0:T(8,128)(2,1)}, bf16[256,128]{1,0:T(8,128)(2,1)S(1)}, u32[]{:S(2)}, u32[]{:S(2)}) collective-permute-start(bf16[256,128]{1,0:T(8,128)(2,1)} %get-tuple-element.35), channel_id=1, source_target_pairs={{0,20},{4,16},{8,28},{12,24},{1,21},{5,17},{9,29},{13,25},{2,22},{... | collective-permute-start | bytes 196616 | tf_op jit(solution)/shard_map/ppermute | solution.py:517
  15.4 12.2 %collective-permute-start.2 = (bf16[256,128]{1,0:T(8,128)(2,1)}, bf16[256,128]{1,0:T(8,128)(2,1)S(1)}, u32[]{:S(2)}, u32[]{:S(2)}) collective-permute-start(bf16[256,128]{1,0:T(8,128)(2,1)} %get-tuple-element.36), channel_id=1, source_target_pairs={{0,24},{4,28},{8,16},{12,20},{1,25},{5,29},{9,17},{13,21},{2,26},{... | collective-permute-start | bytes 196616 | tf_op jit(solution)/shard_map/ppermute | solution.py:517
  16.7 11.0 %collective-permute-start.3 = (bf16[256,128]{1,0:T(8,128)(2,1)}, bf16[256,128]{1,0:T(8,128)(2,1)S(1)}, u32[]{:S(2)}, u32[]{:S(2)}) collective-permute-start(bf16[256,128]{1,0:T(8,128)(2,1)} %get-tuple-element.37), channel_id=1, source_target_pairs={{0,28},{4,24},{8,20},{12,16},{1,29},{5,25},{9,21},{13,17},{2,30},{... | collective-permute-start | bytes 196616 | tf_op jit(solution)/shard_map/ppermute | solution.py:517
  18.9 8.8 %copy-start.1 = (bf16[256,512]{1,0:T(8,128)(2,1)S(1)}, bf16[256,512]{1,0:T(8,128)(2,1)}, u32[]{:S(2)}) copy-start(bf16[256,512]{1,0:T(8,128)(2,1)} %values_ref.3) | copy-start | bytes 786436
  18.9 8.8 %copy-start.2 = (bf16[256,512]{1,0:T(8,128)(2,1)S(1)}, bf16[256,512]{1,0:T(8,128)(2,1)}, u32[]{:S(2)}) copy-start(bf16[256,512]{1,0:T(8,128)(2,1)} %queries_ref.1) | copy-start | bytes 786436
  18.9 24.3 %collective-permute-start.10 = (bf16[512,1024]{1,0:T(8,128)(2,1)}, bf16[512,1024]{1,0:T(8,128)(2,1)S(1)}, u32[]{:S(2)}, u32[]{:S(2)}) collective-permute-start(bf16[512,1024]{1,0:T(8,128)(2,1)} %get-tuple-element.50), channel_id=1, source_target_pairs={{0,2},{1,3},{2,0},{3,1},{4,6},{5,7},{6,4},{7,5},{8,10},{9,11},{10,... | collective-permute-start | bytes 3145736 | tf_op jit(solution)/shard_map/ppermute | solution.py:555
  26.3 14.3 %collective-permute-start.7 = (bf16[8,128,128]{2,1,0:T(8,128)(2,1)S(1)}, bf16[8,128,128]{2,1,0:T(8,128)(2,1)S(1)}, u32[]{:S(2)}, u32[]{:S(2)}) collective-permute-start(bf16[8,128,128]{2,1,0:T(8,128)(2,1)S(1)} %get-tuple-element.46), channel_id=1, source_target_pairs={{0,16},{4,20},{8,24},{12,28},{1,17},{5,21},{9,25},{13,29},{2,18},{... | collective-permute-start | bytes 786440 | tf_op jit(solution)/shard_map/ppermute | solution.py:508
  27.9 11.3 %collective-permute-start.4 = (bf16[2,256,128]{2,1,0:T(8,128)(2,1)S(1)}, bf16[2,256,128]{2,1,0:T(8,128)(2,1)S(1)}, u32[]{:S(2)}, u32[]{:S(2)}) collective-permute-start(bf16[2,256,128]{2,1,0:T(8,128)(2,1)S(1)} %get-tuple-element.39), channel_id=1, source_target_pairs={{0,4},{4,0},{8,12},{12,8},{16,20},{20,16},{24,28},{28,24},{1,5},{5... | collective-permute-start | bytes 393224 | tf_op jit(solution)/shard_map/ppermute | solution.py:512
  28.5 5.9 %collective-permute-start.5 = (bf16[256,128]{1,0:T(8,128)(2,1)S(1)}, bf16[256,128]{1,0:T(8,128)(2,1)S(1)}, u32[]{:S(2)}, u32[]{:S(2)}) collective-permute-start(bf16[256,128]{1,0:T(8,128)(2,1)S(1)} %get-tuple-element.40), channel_id=1, source_target_pairs={{0,8},{4,12},{8,0},{12,4},{16,24},{20,28},{24,16},{28,20},{1,9},{5... | collective-permute-start | bytes 196616 | tf_op jit(solution)/shard_map/ppermute | solution.py:512
  30.7 6.3 %collective-permute-start.6 = (bf16[256,128]{1,0:T(8,128)(2,1)S(1)}, bf16[256,128]{1,0:T(8,128)(2,1)S(1)}, u32[]{:S(2)}, u32[]{:S(2)}) collective-permute-start(bf16[256,128]{1,0:T(8,128)(2,1)S(1)} %get-tuple-element.41), channel_id=1, source_target_pairs={{0,12},{4,8},{8,4},{12,0},{16,28},{20,24},{24,20},{28,16},{1,13},{... | collective-permute-start | bytes 196616 | tf_op jit(solution)/shard_map/ppermute | solution.py:512
  34.4 8.0 %collective-permute-start.8 = (bf16[256,128]{1,0:T(8,128)(2,1)S(1)}, bf16[256,128]{1,0:T(8,128)(2,1)S(1)}, u32[]{:S(2)}, u32[]{:S(2)}) collective-permute-start(bf16[256,128]{1,0:T(8,128)(2,1)S(1)} %get-tuple-element.48), channel_id=1, source_target_pairs={{0,8},{4,12},{8,0},{12,4},{16,24},{20,28},{24,16},{28,20},{1,9},{5... | collective-permute-start | bytes 196616 | tf_op jit(solution)/shard_map/ppermute | solution.py:512
  36.9 5.5 %collective-permute-start.9 = (bf16[256,128]{1,0:T(8,128)(2,1)S(1)}, bf16[256,128]{1,0:T(8,128)(2,1)S(1)}, u32[]{:S(2)}, u32[]{:S(2)}) collective-permute-start(bf16[256,128]{1,0:T(8,128)(2,1)S(1)} %get-tuple-element.49), channel_id=1, source_target_pairs={{0,12},{4,8},{8,4},{12,0},{16,28},{20,24},{24,20},{28,16},{1,13},{... | collective-permute-start | bytes 196616 | tf_op jit(solution)/shard_map/ppermute | solution.py:512
  42.4 12.6 %copy-start = (bf16[512,2048]{1,0:T(8,128)(2,1)S(1)}, bf16[512,2048]{1,0:T(8,128)(2,1)}, u32[]{:S(2)}) copy-start(bf16[512,2048]{1,0:T(8,128)(2,1)} %own_ref.3) | copy-start | bytes 6291460
  55.4 1.6 %collective-permute-start.11 = (bf16[256,512]{1,0:T(8,128)(2,1)S(1)}, bf16[256,512]{1,0:T(8,128)(2,1)S(1)}, u32[]{:S(2)}, u32[]{:S(2)}) collective-permute-start(bf16[256,512]{1,0:T(8,128)(2,1)S(1)} %shard_map.80), channel_id=1, source_target_pairs={{0,1},{1,0},{2,3},{3,2},{4,5},{5,4},{6,7},{7,6},{8,9},{9,8},{10,11... | collective-permute-start | bytes 786440 | tf_op jit(solution)/shard_map/ppermute | solution.py:634

commit v23 on v22

--- a/solution.py
+++ b/solution.py
@@ -177,7 +177,7 @@
     return ref[unit // blocks, start:start + BLOCK]
 
 
-def base_inverse(strict):
+def base_inverse(strict, first, last):
     count = BLOCK // BASE
     moved = [
         pltpu.roll(strict[b * BASE:(b + 1) * BASE], (BLOCK - b * BASE) % BLOCK, 1)
@@ -188,7 +188,7 @@
     rows = lax.broadcasted_iota(jnp.int32, (BASE // 2, BLOCK), 0)
     half = BASE // 2
     parts = []
-    for b in range(count):
+    for b in range(first, last):
         upper = (lanes == rows + b * BASE).astype(F32)
         lower = (lanes == rows + b * BASE + half).astype(F32)
         for step in range(BASE - 1):
@@ -253,7 +253,10 @@
         rate_column = jnp.sum(jnp.where(diagonal, scaled_rate, 0.0), 1, keepdims=True)
         strict = jnp.where(rows > columns, rate_column * gram * scale, 0.0)
         yield
-        inverse = base_inverse(strict)
+        middle = BLOCK // BASE // 2
+        upper_part = base_inverse(strict, 0, middle)
+        yield
+        inverse = jnp.concatenate([upper_part, base_inverse(strict, middle, 2 * middle)], 0)
         yield
         size = BASE
         while size < BLOCK:
@@ -398,6 +401,7 @@
         yield
         scores = jnp.concatenate(score_list, 1)
         expos = jnp.exp(scores - jnp.max(scores, 1, keepdims=True))
+        yield
         weights_ref[unit] = (expos * (1.0 / jnp.sum(expos, 1, keepdims=True))).astype(BF16)
 
     interleaved([steps(unit) for unit in range(units)], 1)

time: 58.1 us -> 58.1 us (level)
  no operation moved by 1% of the time
where the time goes in v23:
time: 58.1 us; the launch traced here: 57.8 us
  starting transfers between devices  27.2 us (47%)
  Pallas kernels  14.1 us (24%)
  blocking collectives  10.6 us (18%)
  waiting for transfers between devices  4.88 us (8%)
  other arithmetic  0.78 us (1%)
    ppermute x4, starting transfers between devices, straight(): return lax.ppermute(value, 'ctx', pairs)  10.7 us
    all_to_all x1, blocking collectives, body(): lax.all_to_all(attended.reshape(heads * planes, blocks, *tile), axes, 0,...  10.6 us
    ppermute x5, starting transfers between devices, crossed(): return lax.ppermute(value, 'ctx', pairs) if turn else value  8.28 us
    pallas_call x1, Pallas kernels, body(): call(functools.partial(keys_kernel, blocks), [array((units, *tile)), arra...  5.84 us
    all_to_all x1, starting transfers between devices, exchange(): lax.all_to_all(value, 'ctx', 0, 0, axis_index_groups=members, tiled=True)  5.26 us
    ppermute x5, waiting for transfers between devices, crossed(): return lax.ppermute(value, 'ctx', pairs) if turn else value  3.04 us
    pallas_call x1, Pallas kernels, body(): call(functools.partial(pack_kernel, axes, cores), [array(part_shape)] + [...  2.83 us
    pallas_call x1, Pallas kernels, body(): call(functools.partial(weights_kernel, before), array((units, BLOCK, TOPK...  1.84 us
  transfers between devices with their start and end apart: 13, of which 3 were waited for; matrix products, arithmetic and copies ran while one was open for 0% of the time, Pallas kernels for 17%

profile of v23, /device:TPU:0, one launch (start us, length us, event | category | flops | bytes accessed | tf_op | source)
XLA Modules:
  0.0 57.8 jit_solution(4378352996774005960)
XLA Ops:
  0.0 2.8 %shard_map.73 = (bf16[4,528,128]{2,1,0:T(8,128)(2,1)}, bf16[256,128]{1,0:T(8,128)(2,1)}, bf16[256,128]{1,0:T(8,128)(2,1)}, bf16[256,128]{1,0:T(8,128)(2,1)}, bf1...) custom-call(bf16[256,512]{1,0:T(8,128)(2,1)} %d_ref.1, bf16[256,512]{1,0:T(8,128)(2,1)} %k_ref.1, f32[4,256]{1,0:T(4,128)} %rates_hbm.1, ...), custom_call_target="tpu_custom_call" | custom-call | flops 4194304 | bytes 2097152 | tf_op jit(solution)/shard_map/pallas_call | solution.py:529
  2.8 5.3 %all-to-all-start = ((bf16[4,528,128]{2,1,0:T(8,128)(2,1)}), bf16[4,528,128]{2,1,0:T(8,128)(2,1)S(1)}, u32[]{:S(2)}, u32[]{:S(2)}) async-start(bf16[4,528,128]{2,1,0:T(8,128)(2,1)} %get-tuple-element.29), calls=%async_computation | async-start | bytes 1081344 | tf_op jit(solution)/shard_map/all_to_all | solution.py:508
  8.1 4.5 %collective-permute-start = (bf16[256,128]{1,0:T(8,128)(2,1)}, bf16[256,128]{1,0:T(8,128)(2,1)S(1)}, u32[]{:S(2)}, u32[]{:S(2)}) collective-permute-start(bf16[256,128]{1,0:T(8,128)(2,1)} %get-tuple-element.34), channel_id=1, source_target_pairs={{0,16},{4,20},{8,24},{12,28},{1,17},{5,21},{9,25},{13,29},{2,18},{... | collective-permute-start | bytes 196616 | tf_op jit(solution)/shard_map/ppermute | solution.py:521
  12.6 2.8 %collective-permute-start.1 = (bf16[256,128]{1,0:T(8,128)(2,1)}, bf16[256,128]{1,0:T(8,128)(2,1)S(1)}, u32[]{:S(2)}, u32[]{:S(2)}) collective-permute-start(bf16[256,128]{1,0:T(8,128)(2,1)} %get-tuple-element.35), channel_id=1, source_target_pairs={{0,20},{4,16},{8,28},{12,24},{1,21},{5,17},{9,29},{13,25},{2,22},{... | collective-permute-start | bytes 196616 | tf_op jit(solution)/shard_map/ppermute | solution.py:521
  15.4 1.3 %collective-permute-start.2 = (bf16[256,128]{1,0:T(8,128)(2,1)}, bf16[256,128]{1,0:T(8,128)(2,1)S(1)}, u32[]{:S(2)}, u32[]{:S(2)}) collective-permute-start(bf16[256,128]{1,0:T(8,128)(2,1)} %get-tuple-element.36), channel_id=1, source_target_pairs={{0,24},{4,28},{8,16},{12,20},{1,25},{5,29},{9,17},{13,21},{2,26},{... | collective-permute-start | bytes 196616 | tf_op jit(solution)/shard_map/ppermute | solution.py:521
  16.7 2.2 %collective-permute-start.3 = (bf16[256,128]{1,0:T(8,128)(2,1)}, bf16[256,128]{1,0:T(8,128)(2,1)S(1)}, u32[]{:S(2)}, u32[]{:S(2)}) collective-permute-start(bf16[256,128]{1,0:T(8,128)(2,1)} %get-tuple-element.37), channel_id=1, source_target_pairs={{0,28},{4,24},{8,20},{12,16},{1,29},{5,25},{9,21},{13,17},{2,30},{... | collective-permute-start | bytes 196616 | tf_op jit(solution)/shard_map/ppermute | solution.py:521
  18.9 1.6 %collective-permute-start.10 = (bf16[512,1024]{1,0:T(8,128)(2,1)}, bf16[512,1024]{1,0:T(8,128)(2,1)S(1)}, u32[]{:S(2)}, u32[]{:S(2)}) collective-permute-start(bf16[512,1024]{1,0:T(8,128)(2,1)} %get-tuple-element.50), channel_id=1, source_target_pairs={{0,2},{1,3},{2,0},{3,1},{4,6},{5,7},{6,4},{7,5},{8,10},{9,11},{10,... | collective-permute-start | bytes 3145736 | tf_op jit(solution)/shard_map/ppermute | solution.py:559
  20.4 5.8 %shard_map.74 = (bf16[8,128,128]{2,1,0:T(8,128)(2,1)S(1)}, bf16[8,128,128]{2,1,0:T(8,128)(2,1)S(1)}, bf16[8,128,128]{2,1,0:T(8,128)(2,1)S(1)}, bf16[4,2,128,128]...) custom-call(bf16[4,528,128]{2,1,0:T(8,128)(2,1)S(1)} %all-to-all-don, ...), custom_call_target="tpu_custom_call" | custom-call | flops 1677721600 | bytes 2097152 | tf_op jit(solution)/shard_map/pallas_call | solution.py:562
  26.3 1.3 %collective-permute-start.7 = (bf16[8,128,128]{2,1,0:T(8,128)(2,1)S(1)}, bf16[8,128,128]{2,1,0:T(8,128)(2,1)S(1)}, u32[]{:S(2)}, u32[]{:S(2)}) collective-permute-start(bf16[8,128,128]{2,1,0:T(8,128)(2,1)S(1)} %get-tuple-element.46), channel_id=1, source_target_pairs={{0,16},{4,20},{8,24},{12,28},{1,17},{5,21},{9,25},{13,29},{2,18},{... | collective-permute-start | bytes 786440 | tf_op jit(solution)/shard_map/ppermute | solution.py:512
  27.9 0.6 %collective-permute-start.4 = (bf16[2,256,128]{2,1,0:T(8,128)(2,1)S(1)}, bf16[2,256,128]{2,1,0:T(8,128)(2,1)S(1)}, u32[]{:S(2)}, u32[]{:S(2)}) collective-permute-start(bf16[2,256,128]{2,1,0:T(8,128)(2,1)S(1)} %get-tuple-element.39), channel_id=1, source_target_pairs={{0,4},{4,0},{8,12},{12,8},{16,20},{20,16},{24,28},{28,24},{1,5},{5... | collective-permute-start | bytes 393224 | tf_op jit(solution)/shard_map/ppermute | solution.py:516
  28.5 2.2 %collective-permute-start.5 = (bf16[256,128]{1,0:T(8,128)(2,1)S(1)}, bf16[256,128]{1,0:T(8,128)(2,1)S(1)}, u32[]{:S(2)}, u32[]{:S(2)}) collective-permute-start(bf16[256,128]{1,0:T(8,128)(2,1)S(1)} %get-tuple-element.40), channel_id=1, source_target_pairs={{0,8},{4,12},{8,0},{12,4},{16,24},{20,28},{24,16},{28,20},{1,9},{5... | collective-permute-start | bytes 196616 | tf_op jit(solution)/shard_map/ppermute | solution.py:516
  30.7 0.8 %collective-permute-start.6 = (bf16[256,128]{1,0:T(8,128)(2,1)S(1)}, bf16[256,128]{1,0:T(8,128)(2,1)S(1)}, u32[]{:S(2)}, u32[]{:S(2)}) collective-permute-start(bf16[256,128]{1,0:T(8,128)(2,1)S(1)} %get-tuple-element.41), channel_id=1, source_target_pairs={{0,12},{4,8},{8,4},{12,0},{16,28},{20,24},{24,20},{28,16},{1,13},{... | collective-permute-start | bytes 196616 | tf_op jit(solution)/shard_map/ppermute | solution.py:516
  31.4 3.0 %collective-permute-done.5.refs_2_ = bf16[256,128]{1,0:T(8,128)(2,1)S(1)} collective-permute-done((bf16[256,128]{1,0:T(8,128)(2,1)S(1)}, bf16[256,128]{1,0:T(8,128)(2,1)S(1)}, u32[]{:S(2)}, u32[]{:S(2)}) %collective-permute-start.5) | collective-permute-done | bytes 65568 | tf_op jit(solution)/shard_map/ppermute | solution.py:516
  34.5 2.5 %collective-permute-start.8 = (bf16[256,128]{1,0:T(8,128)(2,1)S(1)}, bf16[256,128]{1,0:T(8,128)(2,1)S(1)}, u32[]{:S(2)}, u32[]{:S(2)}) collective-permute-start(bf16[256,128]{1,0:T(8,128)(2,1)S(1)} %get-tuple-element.48), channel_id=1, source_target_pairs={{0,8},{4,12},{8,0},{12,4},{16,24},{20,28},{24,16},{28,20},{1,9},{5... | collective-permute-start | bytes 196616 | tf_op jit(solution)/shard_map/ppermute | solution.py:516
  36.9 2.2 %collective-permute-start.9 = (bf16[256,128]{1,0:T(8,128)(2,1)S(1)}, bf16[256,128]{1,0:T(8,128)(2,1)S(1)}, u32[]{:S(2)}, u32[]{:S(2)}) collective-permute-start(bf16[256,128]{1,0:T(8,128)(2,1)S(1)} %get-tuple-element.49), channel_id=1, source_target_pairs={{0,12},{4,8},{8,4},{12,0},{16,28},{20,24},{24,20},{28,16},{1,13},{... | collective-permute-start | bytes 196616 | tf_op jit(solution)/shard_map/ppermute | solution.py:516
  39.2 1.4 %shard_map.76 = (f32[8,128,128]{2,1,0:T(8,128)S(1)}, bf16[8,5,128,128]{3,2,1,0:T(8,128)(2,1)S(1)}) custom-call(bf16[4,528,128]{2,1,0:T(8,128)(2,1)S(1)} %all-to-all-done.part_ref, bf16[8,128,256]{2,1,0:T(8,128)(2,1)S(1)} %get-tuple-element.31.mixed_ref, bf16[4,2,128,128]{3,2,1,0:T(8,128)(2,1)S(1)} %get-tuple-element.32.even_ref, ...), custom_call_target="tpu_custom_call" | custom-call | bytes 2097152 | tf_op jit(solution)/shard_map/pallas_call | solution.py:592
  40.6 1.8 %shard_map.77.weights_ref = bf16[8,128,512]{2,1,0:T(8,128)(2,1)S(1)} custom-call(s32[8,128]{1,0:T(8,128)S(1)} %get-tuple-element.30.refs_4_.away_ref, bf16[8,5,128,128]{3,2,1,0:T(8,128)(2,1)S(1)} %get-tuple-element.42.moving_ref, f32[8,128,128]{2,1,0:T(8,128)S(1)} %get-tuple-element.43.inner_ref, bf16[8,128,128]{2,1,0:T(8,128)(2,1)S(1)} %get-tuple-element.44.end_ref, ...), custom_call_target="tpu_custom_call" | custom-call | bytes 2097152 | tf_op jit(solution)/shard_map/pallas_call | solution.py:599
  42.5 0.8 %collective-permute-done.10.refs_8_ = bf16[512,1024]{1,0:T(8,128)(2,1)S(1)} collective-permute-done((bf16[512,1024]{1,0:T(8,128)(2,1)}, bf16[512,1024]{1,0:T(8,128)(2,1)S(1)}, u32[]{:S(2)}, u32[]{:S(2)}) %collective-permute-start.10) | collective-permute-done | bytes 1048608 | tf_op jit(solution)/shard_map/ppermute | solution.py:559
  43.2 1.2 %shard_map.78 = (bf16[4,2,2,128,128]{4,3,2,1,0:T(8,128)(2,1)S(1)}, bf16[512,1024]{1,0:T(8,128)(2,1)S(1)}) custom-call(s32[8,128]{1,0:T(8,128)S(1)} %get-tuple-element.30.refs_4_.away_ref, bf16[8,128,512]{2,1,0:T(8,128)(2,1)S(1)} %shard_map.77.weights_ref, bf16[256,128]{1,0:T(8,128)(2,1)S(1)} %get-tuple-element.47.refs_0_, ...), custom_call_target="tpu_custom_call" | custom-call | bytes 2097152 | tf_op jit(solution)/shard_map/pallas_call | solution.py:605
  44.4 10.6 %all_to_all.10 = bf16[8,2,128,128]{3,2,1,0:T(8,128)(2,1)S(1)} all-to-all(bf16[8,2,128,128]{3,2,1,0:T(8,128)(2,1)S(1)} %bitcast.4), channel_id=1, replica_groups={{0,2,4,6,8,10,12,14},{1,3,5,7,9,11,13,15},{16,18,20,22,24,26,28,30},{17..., dimensions={0} | all-to-all | bytes 1048576 | tf_op jit(solution)/shard_map/all_to_all | solution.py:625
  55.0 0.4 shard_map.80
  55.5 0.4 shard_map.79
  56.0 1.1 %collective-permute-done.11 = bf16[256,512]{1,0:T(8,128)(2,1)S(1)} collective-permute-done((bf16[256,512]{1,0:T(8,128)(2,1)S(1)}, bf16[256,512]{1,0:T(8,128)(2,1)S(1)}, u32[]{:S(2)}, u32[]{:S(2)}) %collective-permute-start.11) | collective-permute-done | bytes 262176 | tf_op jit(solution)/shard_map/ppermute | solution.py:638
  57.0 0.8 %add_convert_fusion = bf16[256,512]{1,0:T(8,128)(2,1)} fusion(f32[256,512]{1,0:T(8,128)S(1)} %shard_map.79, bf16[256,512]{1,0:T(8,128)(2,1)S(1)} %collective-permute-done.11), kind=kLoop, calls=%fused_computation | loop fusion | flops 393216 | bytes 1048576 | tf_op jit(solution)/shard_map/convert_element_type | solution.py:639
  (18 shorter events, 0.3 us)
Async XLA Ops:
  2.8 17.6 %all-to-all-start = ((bf16[4,528,128]{2,1,0:T(8,128)(2,1)}), bf16[4,528,128]{2,1,0:T(8,128)(2,1)S(1)}, u32[]{:S(2)}, u32[]{:S(2)}) async-start(bf16[4,528,128]{2,1,0:T(8,128)(2,1)} %get-tuple-element.29), calls=%async_computation | async-start | bytes 1081344 | tf_op jit(solution)/shard_map/all_to_all | solution.py:508
  8.1 18.2 %collective-permute-start = (bf16[256,128]{1,0:T(8,128)(2,1)}, bf16[256,128]{1,0:T(8,128)(2,1)S(1)}, u32[]{:S(2)}, u32[]{:S(2)}) collective-permute-start(bf16[256,128]{1,0:T(8,128)(2,1)} %get-tuple-element.34), channel_id=1, source_target_pairs={{0,16},{4,20},{8,24},{12,28},{1,17},{5,21},{9,25},{13,29},{2,18},{... | collective-permute-start | bytes 196616 | tf_op jit(solution)/shard_map/ppermute | solution.py:521
  12.6 15.0 %collective-permute-start.1 = (bf16[256,128]{1,0:T(8,128)(2,1)}, bf16[256,128]{1,0:T(8,128)(2,1)S(1)}, u32[]{:S(2)}, u32[]{:S(2)}) collective-permute-start(bf16[256,128]{1,0:T(8,128)(2,1)} %get-tuple-element.35), channel_id=1, source_target_pairs={{0,20},{4,16},{8,28},{12,24},{1,21},{5,17},{9,29},{13,25},{2,22},{... | collective-permute-start | bytes 196616 | tf_op jit(solution)/shard_map/ppermute | solution.py:521
  15.4 12.3 %collective-permute-start.2 = (bf16[256,128]{1,0:T(8,128)(2,1)}, bf16[256,128]{1,0:T(8,128)(2,1)S(1)}, u32[]{:S(2)}, u32[]{:S(2)}) collective-permute-start(bf16[256,128]{1,0:T(8,128)(2,1)} %get-tuple-element.36), channel_id=1, source_target_pairs={{0,24},{4,28},{8,16},{12,20},{1,25},{5,29},{9,17},{13,21},{2,26},{... | collective-permute-start | bytes 196616 | tf_op jit(solution)/shard_map/ppermute | solution.py:521
  16.7 11.0 %collective-permute-start.3 = (bf16[256,128]{1,0:T(8,128)(2,1)}, bf16[256,128]{1,0:T(8,128)(2,1)S(1)}, u32[]{:S(2)}, u32[]{:S(2)}) collective-permute-start(bf16[256,128]{1,0:T(8,128)(2,1)} %get-tuple-element.37), channel_id=1, source_target_pairs={{0,28},{4,24},{8,20},{12,16},{1,29},{5,25},{9,21},{13,17},{2,30},{... | collective-permute-start | bytes 196616 | tf_op jit(solution)/shard_map/ppermute | solution.py:521
  18.9 8.8 %copy-start.1 = (bf16[256,512]{1,0:T(8,128)(2,1)S(1)}, bf16[256,512]{1,0:T(8,128)(2,1)}, u32[]{:S(2)}) copy-start(bf16[256,512]{1,0:T(8,128)(2,1)} %values_ref.3) | copy-start | bytes 786436
  18.9 8.8 %copy-start.2 = (bf16[256,512]{1,0:T(8,128)(2,1)S(1)}, bf16[256,512]{1,0:T(8,128)(2,1)}, u32[]{:S(2)}) copy-start(bf16[256,512]{1,0:T(8,128)(2,1)} %queries_ref.1) | copy-start | bytes 786436
  18.9 24.3 %collective-permute-start.10 = (bf16[512,1024]{1,0:T(8,128)(2,1)}, bf16[512,1024]{1,0:T(8,128)(2,1)S(1)}, u32[]{:S(2)}, u32[]{:S(2)}) collective-permute-start(bf16[512,1024]{1,0:T(8,128)(2,1)} %get-tuple-element.50), channel_id=1, source_target_pairs={{0,2},{1,3},{2,0},{3,1},{4,6},{5,7},{6,4},{7,5},{8,10},{9,11},{10,... | collective-permute-start | bytes 3145736 | tf_op jit(solution)/shard_map/ppermute | solution.py:559
  26.3 14.3 %collective-permute-start.7 = (bf16[8,128,128]{2,1,0:T(8,128)(2,1)S(1)}, bf16[8,128,128]{2,1,0:T(8,128)(2,1)S(1)}, u32[]{:S(2)}, u32[]{:S(2)}) collective-permute-start(bf16[8,128,128]{2,1,0:T(8,128)(2,1)S(1)} %get-tuple-element.46), channel_id=1, source_target_pairs={{0,16},{4,20},{8,24},{12,28},{1,17},{5,21},{9,25},{13,29},{2,18},{... | collective-permute-start | bytes 786440 | tf_op jit(solution)/shard_map/ppermute | solution.py:512
  27.9 11.3 %collective-permute-start.4 = (bf16[2,256,128]{2,1,0:T(8,128)(2,1)S(1)}, bf16[2,256,128]{2,1,0:T(8,128)(2,1)S(1)}, u32[]{:S(2)}, u32[]{:S(2)}) collective-permute-start(bf16[2,256,128]{2,1,0:T(8,128)(2,1)S(1)} %get-tuple-element.39), channel_id=1, source_target_pairs={{0,4},{4,0},{8,12},{12,8},{16,20},{20,16},{24,28},{28,24},{1,5},{5... | collective-permute-start | bytes 393224 | tf_op jit(solution)/shard_map/ppermute | solution.py:516
  28.5 5.9 %collective-permute-start.5 = (bf16[256,128]{1,0:T(8,128)(2,1)S(1)}, bf16[256,128]{1,0:T(8,128)(2,1)S(1)}, u32[]{:S(2)}, u32[]{:S(2)}) collective-permute-start(bf16[256,128]{1,0:T(8,128)(2,1)S(1)} %get-tuple-element.40), channel_id=1, source_target_pairs={{0,8},{4,12},{8,0},{12,4},{16,24},{20,28},{24,16},{28,20},{1,9},{5... | collective-permute-start | bytes 196616 | tf_op jit(solution)/shard_map/ppermute | solution.py:516
  30.7 6.3 %collective-permute-start.6 = (bf16[256,128]{1,0:T(8,128)(2,1)S(1)}, bf16[256,128]{1,0:T(8,128)(2,1)S(1)}, u32[]{:S(2)}, u32[]{:S(2)}) collective-permute-start(bf16[256,128]{1,0:T(8,128)(2,1)S(1)} %get-tuple-element.41), channel_id=1, source_target_pairs={{0,12},{4,8},{8,4},{12,0},{16,28},{20,24},{24,20},{28,16},{1,13},{... | collective-permute-start | bytes 196616 | tf_op jit(solution)/shard_map/ppermute | solution.py:516
  34.5 8.0 %collective-permute-start.8 = (bf16[256,128]{1,0:T(8,128)(2,1)S(1)}, bf16[256,128]{1,0:T(8,128)(2,1)S(1)}, u32[]{:S(2)}, u32[]{:S(2)}) collective-permute-start(bf16[256,128]{1,0:T(8,128)(2,1)S(1)} %get-tuple-element.48), channel_id=1, source_target_pairs={{0,8},{4,12},{8,0},{12,4},{16,24},{20,28},{24,16},{28,20},{1,9},{5... | collective-permute-start | bytes 196616 | tf_op jit(solution)/shard_map/ppermute | solution.py:516
  36.9 5.5 %collective-permute-start.9 = (bf16[256,128]{1,0:T(8,128)(2,1)S(1)}, bf16[256,128]{1,0:T(8,128)(2,1)S(1)}, u32[]{:S(2)}, u32[]{:S(2)}) collective-permute-start(bf16[256,128]{1,0:T(8,128)(2,1)S(1)} %get-tuple-element.49), channel_id=1, source_target_pairs={{0,12},{4,8},{8,4},{12,0},{16,28},{20,24},{24,20},{28,16},{1,13},{... | collective-permute-start | bytes 196616 | tf_op jit(solution)/shard_map/ppermute | solution.py:516
  42.4 12.6 %copy-start = (bf16[512,2048]{1,0:T(8,128)(2,1)S(1)}, bf16[512,2048]{1,0:T(8,128)(2,1)}, u32[]{:S(2)}) copy-start(bf16[512,2048]{1,0:T(8,128)(2,1)} %own_ref.3) | copy-start | bytes 6291460
  55.4 1.6 %collective-permute-start.11 = (bf16[256,512]{1,0:T(8,128)(2,1)S(1)}, bf16[256,512]{1,0:T(8,128)(2,1)S(1)}, u32[]{:S(2)}, u32[]{:S(2)}) collective-permute-start(bf16[256,512]{1,0:T(8,128)(2,1)S(1)} %shard_map.80), channel_id=1, source_target_pairs={{0,1},{1,0},{2,3},{3,2},{4,5},{5,4},{6,7},{7,6},{8,9},{9,8},{10,11... | collective-permute-start | bytes 786440 | tf_op jit(solution)/shard_map/ppermute | solution.py:638

commit v24 on v22

--- a/solution.py
+++ b/solution.py
@@ -406,12 +406,8 @@
 def blend_kernel(axes, before, blocks, away_ref, weights_ref, *refs):
     units = weights_ref.shape[0]
     heads = units // blocks
-    count = (len(refs) - 3 - heads * (1 + before)) // 2
     arrived = refs[:heads * (1 + before)]
-    out_ref, (values_ref, sems) = refs[-3 - count], refs[-2:]
-    copies = fetched(
-        refs[heads * (1 + before):heads * (1 + before) + count], refs[-2 - count:-2], sems
-    )
+    out_ref, values_ref = refs[-2:]
     place = lax.rem(lax.axis_index(axes[0]), heads)
     for kind in range(1 + before):
         for turn in range(heads):
@@ -437,8 +433,6 @@
         blended = nn(weights_ref[unit], jnp.concatenate(value_list, 0)).astype(BF16)
         for plane in range(out_ref.shape[1]):
             out_ref[unit // blocks, plane, unit % blocks] = blended
-    for copy in copies:
-        copy.wait()
 
 
 def project_kernel(axes, other, cores, attended_ref, own_ref, *refs):
@@ -598,14 +592,13 @@
         [SMEM] + [VMEM] * (4 + before + len(map_parts)),
         0,
     )(away, moving, inner, end, tail, *far_parts, *map_parts)
-    attended, *weight_parts = call(
+    attended = call(
         functools.partial(blend_kernel, axes, before, blocks),
-        [array((heads, planes, blocks, *tile))] + [array(part.shape) for part in weight_parts],
+        array((heads, planes, blocks, *tile)),
         [SMEM] + [VMEM] * (1 + heads * (1 + before)) + [ANY] * len(weight_parts),
         0,
         [
             pltpu.VMEM((1 + before, units * BLOCK, HEAD_DIM), BF16),
-            pltpu.SemaphoreType.DMA((planes,)),
         ],
     )(away, weights, *own_parts, *value_parts, *weight_parts)
 

time: 58.1 us -> 58.1 us (level)
  no operation moved by 1% of the time
where the time goes in v24:
time: 58.1 us; the launch traced here: 57.7 us
  starting transfers between devices  27.2 us (47%)
  Pallas kernels  14 us (24%)
  blocking collectives  10.6 us (18%)
  waiting for transfers between devices  4.9 us (8%)
  other arithmetic  0.77 us (1%)
    ppermute x4, starting transfers between devices, straight(): return lax.ppermute(value, 'ctx', pairs)  10.7 us
    all_to_all x1, blocking collectives, body(): lax.all_to_all(attended.reshape(heads * planes, blocks, *tile), axes, 0,...  10.6 us
    ppermute x5, starting transfers between devices, crossed(): return lax.ppermute(value, 'ctx', pairs) if turn else value  8.28 us
    pallas_call x1, Pallas kernels, body(): call(functools.partial(keys_kernel, blocks), [array((units, *tile)), arra...  5.82 us
    all_to_all x1, starting transfers between devices, exchange(): lax.all_to_all(value, 'ctx', 0, 0, axis_index_groups=members, tiled=True)  5.26 us
    ppermute x5, waiting for transfers between devices, crossed(): return lax.ppermute(value, 'ctx', pairs) if turn else value  3.03 us
    pallas_call x1, Pallas kernels, body(): call(functools.partial(pack_kernel, axes, cores), [array(part_shape)] + [...  2.84 us
    pallas_call x1, Pallas kernels, body(): call(functools.partial(weights_kernel, before), array((units, BLOCK, TOPK...  1.84 us
  transfers between devices with their start and end apart: 13, of which 3 were waited for; matrix products, arithmetic and copies ran while one was open for 0% of the time, Pallas kernels for 17%

profile of v24, /device:TPU:0, one launch (start us, length us, event | category | flops | bytes accessed | tf_op | source)
XLA Modules:
  0.0 57.7 jit_solution(16847672030483286615)
XLA Ops:
  0.0 2.8 %shard_map.73 = (bf16[4,528,128]{2,1,0:T(8,128)(2,1)}, bf16[256,128]{1,0:T(8,128)(2,1)}, bf16[256,128]{1,0:T(8,128)(2,1)}, bf16[256,128]{1,0:T(8,128)(2,1)}, bf1...) custom-call(bf16[256,512]{1,0:T(8,128)(2,1)} %d_ref.1, bf16[256,512]{1,0:T(8,128)(2,1)} %k_ref.1, f32[4,256]{1,0:T(4,128)} %rates_hbm.1, ...), custom_call_target="tpu_custom_call" | custom-call | flops 4194304 | bytes 2097152 | tf_op jit(solution)/shard_map/pallas_call | solution.py:519
  2.8 5.3 %all-to-all-start = ((bf16[4,528,128]{2,1,0:T(8,128)(2,1)}), bf16[4,528,128]{2,1,0:T(8,128)(2,1)S(1)}, u32[]{:S(2)}, u32[]{:S(2)}) async-start(bf16[4,528,128]{2,1,0:T(8,128)(2,1)} %get-tuple-element.27), calls=%async_computation | async-start | bytes 1081344 | tf_op jit(solution)/shard_map/all_to_all | solution.py:498
  8.1 4.5 %collective-permute-start = (bf16[256,128]{1,0:T(8,128)(2,1)}, bf16[256,128]{1,0:T(8,128)(2,1)S(1)}, u32[]{:S(2)}, u32[]{:S(2)}) collective-permute-start(bf16[256,128]{1,0:T(8,128)(2,1)} %get-tuple-element.32), channel_id=1, source_target_pairs={{0,16},{4,20},{8,24},{12,28},{1,17},{5,21},{9,25},{13,29},{2,18},{... | collective-permute-start | bytes 196616 | tf_op jit(solution)/shard_map/ppermute | solution.py:511
  12.6 2.8 %collective-permute-start.1 = (bf16[256,128]{1,0:T(8,128)(2,1)}, bf16[256,128]{1,0:T(8,128)(2,1)S(1)}, u32[]{:S(2)}, u32[]{:S(2)}) collective-permute-start(bf16[256,128]{1,0:T(8,128)(2,1)} %get-tuple-element.33), channel_id=1, source_target_pairs={{0,20},{4,16},{8,28},{12,24},{1,21},{5,17},{9,29},{13,25},{2,22},{... | collective-permute-start | bytes 196616 | tf_op jit(solution)/shard_map/ppermute | solution.py:511
  15.4 1.3 %collective-permute-start.2 = (bf16[256,128]{1,0:T(8,128)(2,1)}, bf16[256,128]{1,0:T(8,128)(2,1)S(1)}, u32[]{:S(2)}, u32[]{:S(2)}) collective-permute-start(bf16[256,128]{1,0:T(8,128)(2,1)} %get-tuple-element.34), channel_id=1, source_target_pairs={{0,24},{4,28},{8,16},{12,20},{1,25},{5,29},{9,17},{13,21},{2,26},{... | collective-permute-start | bytes 196616 | tf_op jit(solution)/shard_map/ppermute | solution.py:511
  16.7 2.2 %collective-permute-start.3 = (bf16[256,128]{1,0:T(8,128)(2,1)}, bf16[256,128]{1,0:T(8,128)(2,1)S(1)}, u32[]{:S(2)}, u32[]{:S(2)}) collective-permute-start(bf16[256,128]{1,0:T(8,128)(2,1)} %get-tuple-element.35), channel_id=1, source_target_pairs={{0,28},{4,24},{8,20},{12,16},{1,29},{5,25},{9,21},{13,17},{2,30},{... | collective-permute-start | bytes 196616 | tf_op jit(solution)/shard_map/ppermute | solution.py:511
  18.9 1.6 %collective-permute-start.10 = (bf16[512,1024]{1,0:T(8,128)(2,1)}, bf16[512,1024]{1,0:T(8,128)(2,1)S(1)}, u32[]{:S(2)}, u32[]{:S(2)}) collective-permute-start(bf16[512,1024]{1,0:T(8,128)(2,1)} %get-tuple-element.48), channel_id=1, source_target_pairs={{0,2},{1,3},{2,0},{3,1},{4,6},{5,7},{6,4},{7,5},{8,10},{9,11},{10,... | collective-permute-start | bytes 3145736 | tf_op jit(solution)/shard_map/ppermute | solution.py:549
  20.4 5.8 %shard_map.74 = (bf16[8,128,128]{2,1,0:T(8,128)(2,1)S(1)}, bf16[8,128,128]{2,1,0:T(8,128)(2,1)S(1)}, bf16[8,128,128]{2,1,0:T(8,128)(2,1)S(1)}, bf16[4,2,128,128]...) custom-call(bf16[4,528,128]{2,1,0:T(8,128)(2,1)S(1)} %all-to-all-don, ...), custom_call_target="tpu_custom_call" | custom-call | flops 1677721600 | bytes 2097152 | tf_op jit(solution)/shard_map/pallas_call | solution.py:552
  26.3 1.3 %collective-permute-start.7 = (bf16[8,128,128]{2,1,0:T(8,128)(2,1)S(1)}, bf16[8,128,128]{2,1,0:T(8,128)(2,1)S(1)}, u32[]{:S(2)}, u32[]{:S(2)}) collective-permute-start(bf16[8,128,128]{2,1,0:T(8,128)(2,1)S(1)} %get-tuple-element.44), channel_id=1, source_target_pairs={{0,16},{4,20},{8,24},{12,28},{1,17},{5,21},{9,25},{13,29},{2,18},{... | collective-permute-start | bytes 786440 | tf_op jit(solution)/shard_map/ppermute | solution.py:502
  27.9 0.6 %collective-permute-start.4 = (bf16[2,256,128]{2,1,0:T(8,128)(2,1)S(1)}, bf16[2,256,128]{2,1,0:T(8,128)(2,1)S(1)}, u32[]{:S(2)}, u32[]{:S(2)}) collective-permute-start(bf16[2,256,128]{2,1,0:T(8,128)(2,1)S(1)} %get-tuple-element.37), channel_id=1, source_target_pairs={{0,4},{4,0},{8,12},{12,8},{16,20},{20,16},{24,28},{28,24},{1,5},{5... | collective-permute-start | bytes 393224 | tf_op jit(solution)/shard_map/ppermute | solution.py:506
  28.5 2.2 %collective-permute-start.5 = (bf16[256,128]{1,0:T(8,128)(2,1)S(1)}, bf16[256,128]{1,0:T(8,128)(2,1)S(1)}, u32[]{:S(2)}, u32[]{:S(2)}) collective-permute-start(bf16[256,128]{1,0:T(8,128)(2,1)S(1)} %get-tuple-element.38), channel_id=1, source_target_pairs={{0,8},{4,12},{8,0},{12,4},{16,24},{20,28},{24,16},{28,20},{1,9},{5... | collective-permute-start | bytes 196616 | tf_op jit(solution)/shard_map/ppermute | solution.py:506
  30.7 0.8 %collective-permute-start.6 = (bf16[256,128]{1,0:T(8,128)(2,1)S(1)}, bf16[256,128]{1,0:T(8,128)(2,1)S(1)}, u32[]{:S(2)}, u32[]{:S(2)}) collective-permute-start(bf16[256,128]{1,0:T(8,128)(2,1)S(1)} %get-tuple-element.39), channel_id=1, source_target_pairs={{0,12},{4,8},{8,4},{12,0},{16,28},{20,24},{24,20},{28,16},{1,13},{... | collective-permute-start | bytes 196616 | tf_op jit(solution)/shard_map/ppermute | solution.py:506
  31.4 3.0 %collective-permute-done.5.refs_2_ = bf16[256,128]{1,0:T(8,128)(2,1)S(1)} collective-permute-done((bf16[256,128]{1,0:T(8,128)(2,1)S(1)}, bf16[256,128]{1,0:T(8,128)(2,1)S(1)}, u32[]{:S(2)}, u32[]{:S(2)}) %collective-permute-start.5) | collective-permute-done | bytes 65568 | tf_op jit(solution)/shard_map/ppermute | solution.py:506
  34.4 2.5 %collective-permute-start.8 = (bf16[256,128]{1,0:T(8,128)(2,1)S(1)}, bf16[256,128]{1,0:T(8,128)(2,1)S(1)}, u32[]{:S(2)}, u32[]{:S(2)}) collective-permute-start(bf16[256,128]{1,0:T(8,128)(2,1)S(1)} %get-tuple-element.46), channel_id=1, source_target_pairs={{0,8},{4,12},{8,0},{12,4},{16,24},{20,28},{24,16},{28,20},{1,9},{5... | collective-permute-start | bytes 196616 | tf_op jit(solution)/shard_map/ppermute | solution.py:506
  36.9 2.2 %collective-permute-start.9 = (bf16[256,128]{1,0:T(8,128)(2,1)S(1)}, bf16[256,128]{1,0:T(8,128)(2,1)S(1)}, u32[]{:S(2)}, u32[]{:S(2)}) collective-permute-start(bf16[256,128]{1,0:T(8,128)(2,1)S(1)} %get-tuple-element.47), channel_id=1, source_target_pairs={{0,12},{4,8},{8,4},{12,0},{16,28},{20,24},{24,20},{28,16},{1,13},{... | collective-permute-start | bytes 196616 | tf_op jit(solution)/shard_map/ppermute | solution.py:506
  39.2 1.4 %shard_map.76 = (f32[8,128,128]{2,1,0:T(8,128)S(1)}, bf16[8,5,128,128]{3,2,1,0:T(8,128)(2,1)S(1)}) custom-call(bf16[4,528,128]{2,1,0:T(8,128)(2,1)S(1)} %all-to-all-done.part_ref, bf16[8,128,256]{2,1,0:T(8,128)(2,1)S(1)} %get-tuple-element.29.mixed_ref, bf16[4,2,128,128]{3,2,1,0:T(8,128)(2,1)S(1)} %get-tuple-element.30.even_ref, ...), custom_call_target="tpu_custom_call" | custom-call | bytes 2097152 | tf_op jit(solution)/shard_map/pallas_call | solution.py:582
  40.6 1.8 %shard_map.77.weights_ref = bf16[8,128,512]{2,1,0:T(8,128)(2,1)S(1)} custom-call(s32[8,128]{1,0:T(8,128)S(1)} %get-tuple-element.28.refs_4_.away_ref, bf16[8,5,128,128]{3,2,1,0:T(8,128)(2,1)S(1)} %get-tuple-element.40.moving_ref, f32[8,128,128]{2,1,0:T(8,128)S(1)} %get-tuple-element.41.inner_ref, bf16[8,128,128]{2,1,0:T(8,128)(2,1)S(1)} %get-tuple-element.42.end_ref, ...), custom_call_target="tpu_custom_call" | custom-call | bytes 2097152 | tf_op jit(solution)/shard_map/pallas_call | solution.py:589
  42.4 0.8 %collective-permute-done.10.refs_8_.refs_0_ = bf16[512,1024]{1,0:T(8,128)(2,1)S(1)} collective-permute-done((bf16[512,1024]{1,0:T(8,128)(2,1)}, bf16[512,1024]{1,0:T(8,128)(2,1)S(1)}, u32[]{:S(2)}, u32[]{:S(2)}) %collective-permute-start.10) | collective-permute-done | bytes 1048608 | tf_op jit(solution)/shard_map/ppermute | solution.py:549
  43.2 1.1 %shard_map.78 = bf16[4,2,2,128,128]{4,3,2,1,0:T(8,128)(2,1)S(1)} custom-call(s32[8,128]{1,0:T(8,128)S(1)} %get-tuple-element.28.refs_4_.away_ref, bf16[8,128,512]{2,1,0:T(8,128)(2,1)S(1)} %shard_map.77.weights_ref, bf16[256,128]{1,0:T(8,128)(2,1)S(1)} %get-tuple-element.45.refs_0_, bf16[2,256,128]{2,1,0:T(8,128)(2,1)S(1)} %collective-permute-done.4.refs_1_, ...), custom_call_target="tpu_custom_call" | custom-call | bytes 2097152 | tf_op jit(solution)/shard_map/pallas_call | solution.py:595
  44.3 10.6 %all_to_all.10 = bf16[8,2,128,128]{3,2,1,0:T(8,128)(2,1)S(1)} all-to-all(bf16[8,2,128,128]{3,2,1,0:T(8,128)(2,1)S(1)} %bitcast.4), channel_id=1, replica_groups={{0,2,4,6,8,10,12,14},{1,3,5,7,9,11,13,15},{16,18,20,22,24,26,28,30},{17..., dimensions={0} | all-to-all | bytes 1048576 | tf_op jit(solution)/shard_map/all_to_all | solution.py:614
  54.9 0.4 shard_map.80
  55.4 0.4 shard_map.79
  55.9 1.1 %collective-permute-done.11 = bf16[256,512]{1,0:T(8,128)(2,1)S(1)} collective-permute-done((bf16[256,512]{1,0:T(8,128)(2,1)S(1)}, bf16[256,512]{1,0:T(8,128)(2,1)S(1)}, u32[]{:S(2)}, u32[]{:S(2)}) %collective-permute-start.11) | collective-permute-done | bytes 262176 | tf_op jit(solution)/shard_map/ppermute | solution.py:627
  57.0 0.8 %add_convert_fusion = bf16[256,512]{1,0:T(8,128)(2,1)} fusion(f32[256,512]{1,0:T(8,128)S(1)} %shard_map.79, bf16[256,512]{1,0:T(8,128)(2,1)S(1)} %collective-permute-done.11), kind=kLoop, calls=%fused_computation | loop fusion | flops 393216 | bytes 1048576 | tf_op jit(solution)/shard_map/convert_element_type | solution.py:628
  (18 shorter events, 0.3 us)
Async XLA Ops:
  2.8 17.6 %all-to-all-start = ((bf16[4,528,128]{2,1,0:T(8,128)(2,1)}), bf16[4,528,128]{2,1,0:T(8,128)(2,1)S(1)}, u32[]{:S(2)}, u32[]{:S(2)}) async-start(bf16[4,528,128]{2,1,0:T(8,128)(2,1)} %get-tuple-element.27), calls=%async_computation | async-start | bytes 1081344 | tf_op jit(solution)/shard_map/all_to_all | solution.py:498
  8.1 18.2 %collective-permute-start = (bf16[256,128]{1,0:T(8,128)(2,1)}, bf16[256,128]{1,0:T(8,128)(2,1)S(1)}, u32[]{:S(2)}, u32[]{:S(2)}) collective-permute-start(bf16[256,128]{1,0:T(8,128)(2,1)} %get-tuple-element.32), channel_id=1, source_target_pairs={{0,16},{4,20},{8,24},{12,28},{1,17},{5,21},{9,25},{13,29},{2,18},{... | collective-permute-start | bytes 196616 | tf_op jit(solution)/shard_map/ppermute | solution.py:511
  12.6 15.0 %collective-permute-start.1 = (bf16[256,128]{1,0:T(8,128)(2,1)}, bf16[256,128]{1,0:T(8,128)(2,1)S(1)}, u32[]{:S(2)}, u32[]{:S(2)}) collective-permute-start(bf16[256,128]{1,0:T(8,128)(2,1)} %get-tuple-element.33), channel_id=1, source_target_pairs={{0,20},{4,16},{8,28},{12,24},{1,21},{5,17},{9,29},{13,25},{2,22},{... | collective-permute-start | bytes 196616 | tf_op jit(solution)/shard_map/ppermute | solution.py:511
  15.4 12.2 %collective-permute-start.2 = (bf16[256,128]{1,0:T(8,128)(2,1)}, bf16[256,128]{1,0:T(8,128)(2,1)S(1)}, u32[]{:S(2)}, u32[]{:S(2)}) collective-permute-start(bf16[256,128]{1,0:T(8,128)(2,1)} %get-tuple-element.34), channel_id=1, source_target_pairs={{0,24},{4,28},{8,16},{12,20},{1,25},{5,29},{9,17},{13,21},{2,26},{... | collective-permute-start | bytes 196616 | tf_op jit(solution)/shard_map/ppermute | solution.py:511
  16.7 11.0 %collective-permute-start.3 = (bf16[256,128]{1,0:T(8,128)(2,1)}, bf16[256,128]{1,0:T(8,128)(2,1)S(1)}, u32[]{:S(2)}, u32[]{:S(2)}) collective-permute-start(bf16[256,128]{1,0:T(8,128)(2,1)} %get-tuple-element.35), channel_id=1, source_target_pairs={{0,28},{4,24},{8,20},{12,16},{1,29},{5,25},{9,21},{13,17},{2,30},{... | collective-permute-start | bytes 196616 | tf_op jit(solution)/shard_map/ppermute | solution.py:511
  18.9 8.8 %copy-start.1 = (bf16[256,512]{1,0:T(8,128)(2,1)S(1)}, bf16[256,512]{1,0:T(8,128)(2,1)}, u32[]{:S(2)}) copy-start(bf16[256,512]{1,0:T(8,128)(2,1)} %values_ref.3) | copy-start | bytes 786436
  18.9 8.8 %copy-start.2 = (bf16[256,512]{1,0:T(8,128)(2,1)S(1)}, bf16[256,512]{1,0:T(8,128)(2,1)}, u32[]{:S(2)}) copy-start(bf16[256,512]{1,0:T(8,128)(2,1)} %queries_ref.1) | copy-start | bytes 786436
  18.9 24.3 %collective-permute-start.10 = (bf16[512,1024]{1,0:T(8,128)(2,1)}, bf16[512,1024]{1,0:T(8,128)(2,1)S(1)}, u32[]{:S(2)}, u32[]{:S(2)}) collective-permute-start(bf16[512,1024]{1,0:T(8,128)(2,1)} %get-tuple-element.48), channel_id=1, source_target_pairs={{0,2},{1,3},{2,0},{3,1},{4,6},{5,7},{6,4},{7,5},{8,10},{9,11},{10,... | collective-permute-start | bytes 3145736 | tf_op jit(solution)/shard_map/ppermute | solution.py:549
  26.3 14.3 %collective-permute-start.7 = (bf16[8,128,128]{2,1,0:T(8,128)(2,1)S(1)}, bf16[8,128,128]{2,1,0:T(8,128)(2,1)S(1)}, u32[]{:S(2)}, u32[]{:S(2)}) collective-permute-start(bf16[8,128,128]{2,1,0:T(8,128)(2,1)S(1)} %get-tuple-element.44), channel_id=1, source_target_pairs={{0,16},{4,20},{8,24},{12,28},{1,17},{5,21},{9,25},{13,29},{2,18},{... | collective-permute-start | bytes 786440 | tf_op jit(solution)/shard_map/ppermute | solution.py:502
  27.9 11.3 %collective-permute-start.4 = (bf16[2,256,128]{2,1,0:T(8,128)(2,1)S(1)}, bf16[2,256,128]{2,1,0:T(8,128)(2,1)S(1)}, u32[]{:S(2)}, u32[]{:S(2)}) collective-permute-start(bf16[2,256,128]{2,1,0:T(8,128)(2,1)S(1)} %get-tuple-element.37), channel_id=1, source_target_pairs={{0,4},{4,0},{8,12},{12,8},{16,20},{20,16},{24,28},{28,24},{1,5},{5... | collective-permute-start | bytes 393224 | tf_op jit(solution)/shard_map/ppermute | solution.py:506
  28.5 5.9 %collective-permute-start.5 = (bf16[256,128]{1,0:T(8,128)(2,1)S(1)}, bf16[256,128]{1,0:T(8,128)(2,1)S(1)}, u32[]{:S(2)}, u32[]{:S(2)}) collective-permute-start(bf16[256,128]{1,0:T(8,128)(2,1)S(1)} %get-tuple-element.38), channel_id=1, source_target_pairs={{0,8},{4,12},{8,0},{12,4},{16,24},{20,28},{24,16},{28,20},{1,9},{5... | collective-permute-start | bytes 196616 | tf_op jit(solution)/shard_map/ppermute | solution.py:506
  30.7 6.3 %collective-permute-start.6 = (bf16[256,128]{1,0:T(8,128)(2,1)S(1)}, bf16[256,128]{1,0:T(8,128)(2,1)S(1)}, u32[]{:S(2)}, u32[]{:S(2)}) collective-permute-start(bf16[256,128]{1,0:T(8,128)(2,1)S(1)} %get-tuple-element.39), channel_id=1, source_target_pairs={{0,12},{4,8},{8,4},{12,0},{16,28},{20,24},{24,20},{28,16},{1,13},{... | collective-permute-start | bytes 196616 | tf_op jit(solution)/shard_map/ppermute | solution.py:506
  34.4 8.0 %collective-permute-start.8 = (bf16[256,128]{1,0:T(8,128)(2,1)S(1)}, bf16[256,128]{1,0:T(8,128)(2,1)S(1)}, u32[]{:S(2)}, u32[]{:S(2)}) collective-permute-start(bf16[256,128]{1,0:T(8,128)(2,1)S(1)} %get-tuple-element.46), channel_id=1, source_target_pairs={{0,8},{4,12},{8,0},{12,4},{16,24},{20,28},{24,16},{28,20},{1,9},{5... | collective-permute-start | bytes 196616 | tf_op jit(solution)/shard_map/ppermute | solution.py:506
  36.9 5.5 %collective-permute-start.9 = (bf16[256,128]{1,0:T(8,128)(2,1)S(1)}, bf16[256,128]{1,0:T(8,128)(2,1)S(1)}, u32[]{:S(2)}, u32[]{:S(2)}) collective-permute-start(bf16[256,128]{1,0:T(8,128)(2,1)S(1)} %get-tuple-element.47), channel_id=1, source_target_pairs={{0,12},{4,8},{8,4},{12,0},{16,28},{20,24},{24,20},{28,16},{1,13},{... | collective-permute-start | bytes 196616 | tf_op jit(solution)/shard_map/ppermute | solution.py:506
  43.2 11.7 %copy-start = (bf16[512,2048]{1,0:T(8,128)(2,1)S(1)}, bf16[512,2048]{1,0:T(8,128)(2,1)}, u32[]{:S(2)}) copy-start(bf16[512,2048]{1,0:T(8,128)(2,1)} %own_ref.3) | copy-start | bytes 6291460
  55.4 1.6 %collective-permute-start.11 = (bf16[256,512]{1,0:T(8,128)(2,1)S(1)}, bf16[256,512]{1,0:T(8,128)(2,1)S(1)}, u32[]{:S(2)}, u32[]{:S(2)}) collective-permute-start(bf16[256,512]{1,0:T(8,128)(2,1)S(1)} %shard_map.80), channel_id=1, source_target_pairs={{0,1},{1,0},{2,3},{3,2},{4,5},{5,4},{6,7},{7,6},{8,9},{9,8},{10,11... | collective-permute-start | bytes 786440 | tf_op jit(solution)/shard_map/ppermute | solution.py:627
